TPU v7x, 32 devices: a whole 2x2x4 slice. The times are simulated.
32 devices in a mesh: ch: 2 (over core), lat: 4 (over y, x), lon: 4 (over z).
Axes of the slice: x: 2, y: 2, z: 4, core: 2. Of those that a mesh axis runs over, the one named last changes fastest.
Arguments:
- inputs: bfloat16 [512, 4, 16, 192], P('ch', None, 'lat', 'lon'), may hold values from -6 to 6
- weights: bfloat16 [512, 27, 512], P('ch'), may hold values from -0.0546875 to 0.0546875
- out_grad: bfloat16 [512, 4, 16, 192], P('ch', None, 'lat', 'lon'), may hold values from -6 to 6
Outputs:
- input_grad: bfloat16 [512, 4, 16, 192], P('ch', None, 'lat', 'lon')
- weight_grad: float32 [512, 27, 512], P('ch')
All inputs are finite; a program needn't handle non-finite values.
Results may differ from a plain program's by a relative error of at most 0.001.
Values may be sent and summed in bfloat16 or wider, within the bound.
No kernel may reach another device: no remote copies, remote signals or barrier semaphores. Data moves between devices by JAX's collectives and lax.ppermute only.
A program may use at most 320 MiB of HBM per device.

v0:
```python
import math

import jax
import jax.numpy as jnp
from jax import lax
from jax.sharding import PartitionSpec as P


def padded_2(cells, sides, width):
    for axis, dim in sides:
        count = lax.axis_size(axis)
        head = lax.slice_in_dim(cells, 0, width, axis=dim)
        tail = lax.slice_in_dim(cells, cells.shape[dim] - width, cells.shape[dim], axis=dim)
        cells = jnp.concatenate(
            [
                lax.ppermute(tail, axis, [(i, (i + 1) % count) for i in range(count)]),
                cells,
                lax.ppermute(head, axis, [((i + 1) % count, i) for i in range(count)]),
            ],
            axis=dim,
        )
    return cells


def mask_rims(padded):
    count = lax.axis_size("lat")
    where_lat = lax.axis_index("lat")
    lines = jnp.arange(padded.shape[2])
    drop = (lines == 0) & (where_lat == 0) | (lines == padded.shape[2] - 1) & (
        where_lat == count - 1
    )
    return jnp.where(drop[None, None, :, None], jnp.zeros((), padded.dtype), padded)


def pad_levels(field):
    return jnp.pad(field, ((0, 0), (1, 1), (0, 0), (0, 0)))


def body(inputs, weights, out_grad):
    chans, levels, height, width = inputs.shape
    input_pad = pad_levels(mask_rims(padded_2(inputs, (("lat", 2), ("lon", 3)), 1)))
    grad_inner = lax.all_gather(out_grad, "ch", axis=0, tiled=True)
    grad_pad = pad_levels(mask_rims(padded_2(grad_inner, (("lat", 2), ("lon", 3)), 1)))
    filters = grad_pad.shape[0]
    products = jnp.dot(
        weights.reshape(chans * 27, filters),
        grad_pad.reshape(filters, -1),
        preferred_element_type=jnp.float32,
    )
    products = products.reshape((chans, 27) + tuple(grad_pad.shape[1:]))
    total = jnp.zeros((chans, levels, height, width), jnp.float32)
    pieces = []
    for tap in range(27):
        shift_lev = tap // 9 - 1
        shift_lat = tap // 3 % 3 - 1
        shift_lon = tap % 3 - 1
        total = (
            total
            + products[
                :,
                tap,
                1 - shift_lev : 1 - shift_lev + levels,
                1 - shift_lat : 1 - shift_lat + height,
                1 - shift_lon : 1 - shift_lon + width,
            ]
        )
        pieces.append(
            input_pad[
                :,
                1 + shift_lev : 1 + shift_lev + levels,
                1 + shift_lat : 1 + shift_lat + height,
                1 + shift_lon : 1 + shift_lon + width,
            ]
        )
    columns = jnp.stack(pieces, axis=1).reshape(chans * 27, -1)
    partial_grad = lax.dot_general(
        columns,
        grad_inner.reshape(filters, -1),
        (((1,), (1,)), ((), ())),
        preferred_element_type=jnp.float32,
    )
    summed = lax.psum(partial_grad, ("lat", "lon"))
    cells = levels * height * width * lax.axis_size("lat") * lax.axis_size("lon")
    weight_grad = (summed * (1.0 / math.sqrt(cells))).reshape(chans, 27, filters)
    return (total.astype(jnp.bfloat16), weight_grad)


def solution(mesh):
    in_specs = (P("ch", None, "lat", "lon"), P("ch", None, None), P("ch", None, "lat", "lon"))
    out_specs = (P("ch", None, "lat", "lon"), P("ch", None, None))
    return jax.shard_map(body, mesh=mesh, in_specs=in_specs, out_specs=out_specs, check_vma=False)
```

profile of v0, /device:TPU:0, one launch (start us, length us, event | category | flops | bytes accessed | tf_op | source)
XLA Modules:
  0.0 584.8 jit_solution(11194735101973691555)
XLA Ops:
  7.2 1.0 fusion.76
  8.2 3.0 collective-permute-start.4
  11.2 1.0 collective-permute-start.5
  12.2 2.6 all_gather.3
  14.8 0.9 collective-permute-done.4
  15.6 1.0 constant_dynamic-update-slice_fusion.4
  17.3 3.7 collective-permute-start.7
  21.0 1.5 collective-permute-done.7
  22.5 4.1 collective-permute-done.6
  27.9 0.8 fusion.31
  28.7 0.8 fusion.33
  30.3 0.8 fusion.37
  31.1 0.8 fusion.39
  32.7 0.8 fusion.43
  33.6 0.8 fusion.45
  35.1 0.9 fusion.71
  36.0 0.9 fusion.70
  37.7 0.9 fusion.68
  38.5 0.9 fusion.67
  40.2 0.9 fusion.65
  41.0 0.9 fusion.64
  42.7 0.8 fusion.49
  43.5 0.8 fusion.51
  45.1 0.8 fusion.55
  45.9 0.8 fusion.57
  47.5 0.8 fusion.61
  48.4 0.8 fusion.63
  49.2 36.6 %copy.61 = bf16[256,27,4,4,48]{4,3,2,1,0:T(4,128)(2,1)} copy(bf16[256,27,4,4,48]{0,4,3,2,1:T(8,128)(2,1)} %fusion.63) | data formatting | bytes 21233664 | tf_op jit(solution)/shard_map/stack | solution.py:75
  85.7 39.1 %reshape.38 = bf16[6912,768]{1,0:T(8,128)(2,1)} reshape(bf16[256,27,4,4,48]{4,3,2,1,0:T(4,128)(2,1)} %copy.61) | data formatting | bytes 21233664 | tf_op jit(solution)/shard_map/reshape | solution.py:75
  124.8 12.9 %fusion.77 = f32[6912,512]{1,0:T(8,128)} fusion(bf16[6912,768]{1,0:T(8,128)(2,1)} %reshape.38, bf16[512,768]{0,1:T(8,128)(2,1)S(1)} %bitcast.301), kind=kOutput, calls=%fused_computation.142 | convolution fusion | flops 5435817984 | bytes 25559040 | tf_op jit(solution)/shard_map/dot_general | solution.py:76
  137.7 1.6 collective-permute-start
  139.3 1.4 collective-permute-start.1
  140.7 7.5 %collective-permute-done = bf16[512,4,1,48]{0,3,2,1:T(8,128)(2,1)S(1)} collective-permute-done((bf16[512,4,1,48]{0,3,2,1:T(8,128)(2,1)S(1)}, bf16[512,4,1,48]{0,3,2,1:T(8,128)(2,1)S(1)}, u32[]{:S(2)}, u32[]{:S(2)}) %collective-permute-start) | collective-permute-done | bytes 196640 | tf_op jit(solution)/shard_map/ppermute | solution.py:16
  148.2 7.3 %collective-permute-done.1 = bf16[512,4,1,48]{0,3,2,1:T(8,128)(2,1)S(1)} collective-permute-done((bf16[512,4,1,48]{0,3,2,1:T(8,128)(2,1)S(1)}, bf16[512,4,1,48]{0,3,2,1:T(8,128)(2,1)S(1)}, u32[]{:S(2)}, u32[]{:S(2)}) %collective-permute-start.1) | collective-permute-done | bytes 196640 | tf_op jit(solution)/shard_map/ppermute | solution.py:18
  155.7 2.0 collective-permute-start.2
  157.7 10.4 %copy.33 = bf16[256,27,512]{2,1,0:T(8,128)(2,1)} copy(bf16[256,27,512]{2,0,1:T(8,128)(2,1)} %param.4) | data formatting | bytes 14155776 | tf_op args[1]
  168.1 10.7 %reshape.36 = bf16[6912,512]{1,0:T(8,128)(2,1)} reshape(bf16[256,27,512]{2,1,0:T(8,128)(2,1)} %copy.33) | data formatting | bytes 14155776 | tf_op jit(solution)/shard_map/reshape | solution.py:46
  178.8 0.9 maximum_select_fusion
  179.9 2.0 reshape.35
  181.9 24.2 %convolution_bitcast_fusion = f32[6912,1800]{0,1:T(8,128)} fusion(bf16[512,1800]{0,1:T(8,128)(2,1)} %reshape.35, bf16[6912,512]{1,0:T(8,128)(2,1)} %reshape.36), kind=kOutput, calls=%fused_computation | convolution fusion | flops 12740198400 | bytes 58687488 | tf_op jit(solution)/shard_map/dot_general | solution.py:45
  206.1 51.6 %copy.34 = f32[6912,1800]{1,0:T(8,128)} copy(f32[6912,1800]{0,1:T(8,128)} %convolution_bitcast_fusion) | data formatting | bytes 99532800 | tf_op jit(solution)/shard_map/dot_general | solution.py:45
  257.7 122.1 %reshape.37 = f32[256,27,6,6,50]{4,3,2,1,0:T(8,128)} reshape(f32[6912,1800]{1,0:T(8,128)} %copy.34) | data formatting | bytes 99532800 | tf_op jit(solution)/shard_map/reshape | solution.py:50
  379.9 41.6 %fusion.1 = bf16[256,4,4,48]{3,2,1,0:T(4,128)(2,1)S(1)} fusion(f32[256,27,6,6,50]{4,3,2,1,0:T(8,128)} %reshape.37), kind=kLoop, calls=%fused_computation.4 | loop fusion | flops 5308416 | bytes 21626880 | tf_op jit(solution)/shard_map/convert_element_type | solution.py:85
  421.5 1.5 copy.62
  423.0 108.8 %all-reduce.4.cloned.1.call-done = f32[6912,512]{1,0:T(8,128)} async-done(((f32[6912,512]{1,0:T(8,128)}), f32[6912,512]{1,0:T(8,128)}) %all-reduce.4.cloned.1.call-update) | async-done | bytes 14155792 | tf_op jit(solution)/shard_map/psum | solution.py:82
  531.8 12.1 %broadcast_multiply_fusion = f32[6912,512]{1,0:T(8,128)} fusion(f32[6912,512]{1,0:T(8,128)} %all-reduce.4.cloned.1.call-done), kind=kLoop, calls=%fused_computation.1 | loop fusion | flops 3538944 | bytes 28311552 | tf_op jit(solution)/shard_map/mul | solution.py:84
  543.9 14.8 %reshape.40 = f32[256,27,512]{2,1,0:T(8,128)} reshape(f32[6912,512]{1,0:T(8,128)} %broadcast_multiply_fusion) | data formatting | bytes 28311552 | tf_op jit(solution)/shard_map/reshape | solution.py:84
  558.7 19.3 %copy.63 = f32[256,27,512]{2,0,1:T(8,128)} copy(f32[256,27,512]{2,1,0:T(8,128)} %reshape.40) | data formatting | bytes 28311552
  (27 shorter events, 8.6 us)
Async XLA Ops:
  7.2 524.6 %all-reduce.4.cloned.1.call-start = ((), (), s32[]{:S(2)}) async-start(), calls=%async_computation | async-start | bytes 28311552 | tf_op jit(solution)/shard_map/psum | solution.py:82
  8.2 7.4 %collective-permute-start.4 = (bf16[256,4,1,48]{0,3,2,1:T(8,128)(2,1)S(1)}, bf16[256,4,1,48]{0,3,2,1:T(8,128)(2,1)S(1)}, u32[]{:S(2)}, u32[]{:S(2)}) collective-permute-start(bf16[256,4,1,48]{0,3,2,1:T(8,128)(2,1)S(1)} %get-tuple-element.13), channel_id=1, source_target_pairs={{0,4},{4,8},{8,12},{12,0},{1,5},{5,9},{9,13},{13,1},{2,6},{6,10},{... | collective-permute-start | bytes 294920 | tf_op jit(solution)/shard_map/ppermute | solution.py:16
  11.2 6.1 %collective-permute-start.5 = (bf16[256,4,1,48]{0,3,2,1:T(8,128)(2,1)S(1)}, bf16[256,4,1,48]{0,3,2,1:T(8,128)(2,1)S(1)}, u32[]{:S(2)}, u32[]{:S(2)}) collective-permute-start(bf16[256,4,1,48]{0,3,2,1:T(8,128)(2,1)S(1)} %get-tuple-element.12), channel_id=1, source_target_pairs={{4,0},{8,4},{12,8},{0,12},{5,1},{9,5},{13,9},{1,13},{6,2},{10,6},{... | collective-permute-start | bytes 294920 | tf_op jit(solution)/shard_map/ppermute | solution.py:18
  17.3 5.2 collective-permute-start.7
  21.0 5.6 collective-permute-start.6
  137.7 10.4 %collective-permute-start = (bf16[512,4,1,48]{0,3,2,1:T(8,128)(2,1)S(1)}, bf16[512,4,1,48]{0,3,2,1:T(8,128)(2,1)S(1)}, u32[]{:S(2)}, u32[]{:S(2)}) collective-permute-start(bf16[512,4,1,48]{0,3,2,1:T(8,128)(2,1)S(1)} %get-tuple-element.9), channel_id=1, source_target_pairs={{0,4},{4,8},{8,12},{12,0},{1,5},{5,9},{9,13},{13,1},{2,6},{6,10},{... | collective-permute-start | bytes 589832 | tf_op jit(solution)/shard_map/ppermute | solution.py:16
  139.3 16.2 %collective-permute-start.1 = (bf16[512,4,1,48]{0,3,2,1:T(8,128)(2,1)S(1)}, bf16[512,4,1,48]{0,3,2,1:T(8,128)(2,1)S(1)}, u32[]{:S(2)}, u32[]{:S(2)}) collective-permute-start(bf16[512,4,1,48]{0,3,2,1:T(8,128)(2,1)S(1)} %get-tuple-element.8), channel_id=1, source_target_pairs={{4,0},{8,4},{12,8},{0,12},{5,1},{9,5},{13,9},{1,13},{6,2},{10,6},{... | collective-permute-start | bytes 589832 | tf_op jit(solution)/shard_map/ppermute | solution.py:18
  155.6 23.2 %collective-permute-start.3 = (bf16[512,4,6,1]{0,3,2,1:T(2,128)(2,1)S(1)}, bf16[512,4,6,1]{0,3,2,1:T(2,128)(2,1)S(1)}, u32[]{:S(2)}, u32[]{:S(2)}) collective-permute-start(bf16[512,4,6,1]{0,3,2,1:T(2,128)(2,1)S(1)} %get-tuple-element.7), channel_id=1, source_target_pairs={{1,0},{2,1},{3,2},{0,3},{5,4},{6,5},{7,6},{4,7},{9,8},{10,9},{11,1... | collective-permute-start | bytes 73736 | tf_op jit(solution)/shard_map/ppermute | solution.py:18
  155.7 23.1 %collective-permute-start.2 = (bf16[512,4,6,1]{0,3,2,1:T(2,128)(2,1)S(1)}, bf16[512,4,6,1]{0,3,2,1:T(2,128)(2,1)S(1)}, u32[]{:S(2)}, u32[]{:S(2)}) collective-permute-start(bf16[512,4,6,1]{0,3,2,1:T(2,128)(2,1)S(1)} %get-tuple-element.6), channel_id=1, source_target_pairs={{0,1},{1,2},{2,3},{3,0},{4,5},{5,6},{6,7},{7,4},{8,9},{9,10},{10,1... | collective-permute-start | bytes 73736 | tf_op jit(solution)/shard_map/ppermute | solution.py:16
Sparse Core Ops, SparseCore 0:
  137.8 393.9 all-reduce.3
where the time goes:
time: 592 us; the launch traced here: 585 us
  local copies, waits for them, and re-layouts  332 us (56%)
  waiting for transfers between devices  131 us (22%)
  other arithmetic  55.1 us (9%)
  matrix products  37.1 us (6%)
  between operations  14.1 us (2%)
  starting transfers between devices  12.8 us (2%)
    reshape x1, local copies, waits for them, and re-layouts, body(): products = products.reshape((chans, 27) + tuple(grad_pad.shape[1:]))  122 us
    psum x1, waiting for transfers between devices, body(): summed = lax.psum(partial_grad, ('lat', 'lon'))  109 us
    unnamed x33, local copies, waits for them, and re-layouts  53.5 us
    dot_general x1, local copies, waits for them, and re-layouts, body(): jnp.dot(weights.reshape(chans * 27, filters), grad_pad.reshape(filters, -...  51.6 us
    convert_element_type x1, other arithmetic, body(): return (total.astype(jnp.bfloat16), weight_grad)  41.6 us
    reshape x1, local copies, waits for them, and re-layouts, body(): columns = jnp.stack(pieces, axis=1).reshape(chans * 27, -1)  39.1 us
    another operation x2, local copies, waits for them, and re-layouts, body(): columns = jnp.stack(pieces, axis=1).reshape(chans * 27, -1)  37.4 us
    dot_general x1, matrix products, body(): jnp.dot(weights.reshape(chans * 27, filters), grad_pad.reshape(filters, -...  24.2 us
  transfers between devices with their start and end apart: 9, of which 7 were waited for; matrix products, arithmetic and copies ran while one was open for 46% of the time, Pallas kernels for 0%

commit v1 on v0

--- a/solution.py
+++ b/solution.py
@@ -3,7 +3,14 @@
 import jax
 import jax.numpy as jnp
 from jax import lax
+from jax.experimental import pallas as pl
+from jax.experimental.pallas import tpu as pltpu
 from jax.sharding import PartitionSpec as P
+
+VMEM = pltpu.VMEM
+SMEM = pltpu.SMEM
+AXES = ("ch", "lat", "lon")
+LIMIT = 56 * 1024 * 1024
 
 
 def padded_2(cells, sides, width):
@@ -36,7 +43,7 @@
     return jnp.pad(field, ((0, 0), (1, 1), (0, 0), (0, 0)))
 
 
-def body(inputs, weights, out_grad):
+def plain_body(inputs, weights, out_grad):
     chans, levels, height, width = inputs.shape
     input_pad = pad_levels(mask_rims(padded_2(inputs, (("lat", 2), ("lon", 3)), 1)))
     grad_inner = lax.all_gather(out_grad, "ch", axis=0, tiled=True)
@@ -51,25 +58,23 @@
     total = jnp.zeros((chans, levels, height, width), jnp.float32)
     pieces = []
     for tap in range(27):
-        shift_lev = tap // 9 - 1
-        shift_lat = tap // 3 % 3 - 1
-        shift_lon = tap % 3 - 1
+        lev, lat, lon = tap // 9 - 1, tap // 3 % 3 - 1, tap % 3 - 1
         total = (
             total
             + products[
                 :,
                 tap,
-                1 - shift_lev : 1 - shift_lev + levels,
-                1 - shift_lat : 1 - shift_lat + height,
-                1 - shift_lon : 1 - shift_lon + width,
+                1 - lev : 1 - lev + levels,
+                1 - lat : 1 - lat + height,
+                1 - lon : 1 - lon + width,
             ]
         )
         pieces.append(
             input_pad[
                 :,
-                1 + shift_lev : 1 + shift_lev + levels,
-                1 + shift_lat : 1 + shift_lat + height,
-                1 + shift_lon : 1 + shift_lon + width,
+                1 + lev : 1 + lev + levels,
+                1 + lat : 1 + lat + height,
+                1 + lon : 1 + lon + width,
             ]
         )
     columns = jnp.stack(pieces, axis=1).reshape(chans * 27, -1)
@@ -85,6 +90,346 @@
     return (total.astype(jnp.bfloat16), weight_grad)
 
 
+def move(x, target):
+    pairs = []
+    for i in range(32):
+        to = target(i // 16, i // 4 % 4, i % 4)
+        if to is not None:
+            pairs.append((i, (to[0] * 4 + to[1]) * 4 + to[2]))
+    return lax.ppermute(x, AXES, pairs)
+
+
+def lon_by(step):
+    return lambda c, a, o: (c, a, (o + step) % 4)
+
+
+def lat_xor(mask):
+    return lambda c, a, o: (c, a ^ mask, o)
+
+
+def sibling(c, a, o):
+    return (1 - c, a, o)
+
+
+def north(c, a, o):
+    return (c, a + 1, o) if a < 3 else None
+
+
+def south(c, a, o):
+    return (c, a - 1, o) if a > 0 else None
+
+
+def call(kernel, outs, ins, scratch, flops, name, **kw):
+    moved = sum(math.prod(x.shape) * x.dtype.itemsize for x in list(ins[1:]) + list(outs))
+    return pl.pallas_call(
+        kernel,
+        out_shape=outs,
+        in_specs=[pl.BlockSpec(memory_space=SMEM)] + [pl.BlockSpec(memory_space=VMEM)] * (len(ins) - 1),
+        out_specs=[pl.BlockSpec(memory_space=VMEM)] * len(outs),
+        scratch_shapes=scratch,
+        cost_estimate=pl.CostEstimate(flops=flops, bytes_accessed=moved, transcendentals=0),
+        compiler_params=pltpu.CompilerParams(vmem_limit_bytes=LIMIT),
+        name=name,
+    )(*ins)
+
+
+def pack_kernel(pos, x, g, x0, x1, x2, x3, g_same, g_other, rim_lo, rim_hi, held):
+    levels, height, width, chans = x.shape
+    half = levels // 2
+    for block in range(4):
+        at = block * (chans // 4)
+        lo = x[0:half, :, :, at : at + chans // 4]
+        hi = x[half:levels, :, :, at : at + chans // 4]
+        both = jnp.concatenate([lo, hi], axis=-1)
+        held[block] = both.reshape(held.shape[1:])
+    lon = pos[2]
+    for step, out in enumerate((x0, x1, x2, x3)):
+        out[...] = held[lax.rem(lon + step, 4)]
+    right = lax.rem(pos[1], 2)
+    wide = chans // 2
+    g_same[...] = g[:, :, :, pl.ds(pl.multiple_of(right * wide, wide), wide)].reshape(g_same.shape)
+    g_other[...] = g[:, :, :, pl.ds(pl.multiple_of((1 - right) * wide, wide), wide)].reshape(
+        g_other.shape
+    )
+    rim_lo[...] = g[:, 0]
+    rim_hi[...] = g[:, height - 1]
+
+
+def taps_kernel(
+    pos, x_own, x_x, x_y, x_d1, x_d2, g0, g1, g3, g2a, g2b, s0, s1, s3, s2a, s2b, out, xs, gs, gt, acc
+):
+    lat, core = pos[1], pos[0]
+    levels, rows, circle, _ = gs.shape
+    width = circle // 4
+    height = rows // 4
+    half = levels // 2
+    span = 64
+
+    def place(piece, lat_at, lon_at):
+        gs[:, pl.ds(lat_at * height, height), lon_at * width : (lon_at + 1) * width, :] = (
+            piece.reshape(levels, height, width, piece.shape[-1])
+        )
+
+    right = lax.rem(lat, 2)
+    for which, sets in ((core, (g0, g1, g3, g2a, g2b)), (1 - core, (s0, s1, s3, s2a, s2b))):
+        same, other = 2 * which + right, 2 * which + 1 - right
+        for part, lon_at in ((sets[0], 0), (sets[1], 3), (sets[2], 1)):
+            place(part[0], same, lon_at)
+            place(part[1], other, lon_at)
+        place(sets[3][...], same, 2)
+        place(sets[4][...], other, 2)
+    filters = gs.shape[-1]
+
+    @pl.loop(0, levels * (rows // 2))
+    def _(step):
+        lev, pair = step // (rows // 2), lax.rem(step, rows // 2)
+        block = gs[lev, pl.ds(2 * pair, 2)].reshape(2 * circle, filters)
+        gt[
+            pl.ds(pl.multiple_of(lev * filters, filters), filters),
+            pl.ds(pl.multiple_of(pair * 2 * circle, 2 * circle), 2 * circle),
+        ] = block.T
+
+    xs[:, 0] = jnp.zeros_like(xs[:, 0])
+    xs[:, rows + 1] = jnp.zeros_like(xs[:, rows + 1])
+    low = lax.broadcasted_iota(jnp.int32, (circle, 2 * span), 1) < span
+    for tag in range(4):
+        start = (lat ^ tag) * height
+
+        def piece(lon_from, tag=tag):
+            ref, at = ((x_own, lon_from), (x_x, lon_from), (x_y, lon_from), (x_d1, lon_from))[tag]
+            if tag == 3 and lon_from > 1:
+                ref, at = x_d2, lon_from - 2
+            return ref.at[at].reshape(half, height, width, 2 * span)
+
+        strips = [piece((4 - at) % 4) for at in range(4)]
+
+        @pl.loop(0, half * height)
+        def _(step, strips=strips, start=start):
+            lev, row = step // height, lax.rem(step, height)
+            line = jnp.concatenate([s[lev, row] for s in strips], axis=0).astype(jnp.float32)
+            turned = pltpu.roll(line, span, 1)
+            for upper in range(2):
+                same = jnp.where(low, turned, line) if upper else jnp.where(low, line, turned)
+                before = pltpu.roll(same, 1, 0)
+                after = pltpu.roll(same, circle - 1, 0)
+                at = upper * half + lev
+                xs[at, 1 + start + row, :, 0 : 2 * span] = jnp.where(low, before, same).astype(xs.dtype)
+                xs[at, 1 + start + row, :, 2 * span : 4 * span] = after.astype(xs.dtype)
+
+    acc[...] = jnp.zeros_like(acc)
+
+    @pl.loop(0, 3)
+    def _(lat_by):
+        for lev in range(levels):
+            first, last = max(lev - 1, 0), min(lev + 1, levels - 1)
+            to = (first - lev + 1) * filters
+            many = (last - first + 1) * filters
+            acc[lat_by, to : to + many, :] += jnp.dot(
+                gt[first * filters : (last + 1) * filters, :],
+                xs[lev, pl.ds(lat_by, rows)].reshape(rows * circle, 4 * span),
+                preferred_element_type=jnp.float32,
+            )
+
+    scale = 1.0 / math.sqrt(levels * rows * circle)
+    most = jnp.zeros((span, filters), jnp.float32)
+    for lat_by in range(3):
+        for lev_at in range(3):
+            block = acc[lat_by, lev_at * filters : (lev_at + 1) * filters, :].T * scale
+            for lon_by_ in range(3):
+                tap = (2 - lev_at) * 9 + lat_by * 3 + lon_by_
+                value = block[lon_by_ * span : (lon_by_ + 1) * span]
+                out[tap * span : (tap + 1) * span, :] = value
+                most = jnp.maximum(most, jnp.abs(value))
+    top = jnp.maximum(jnp.max(most, axis=(0, 1), keepdims=True), 1e-30)
+    power = jnp.broadcast_to(jnp.ceil(jnp.log(top) * (1.0 / math.log(2.0))), (16, filters))
+    out[27 * span :, :] = power
+    out[0 : 27 * span, :] = out[0 : 27 * span, :] * jnp.exp2(14.0 - power[0:1])
+
+
+def field_kernel(pos, after, mine, theirs, w, out, copies, acc):
+    del after
+    tap = pl.program_id(0)
+    levels, height, width, chans = out.shape
+    many = mine.shape[-1]
+
+    @pl.when(tap == 0)
+    def _():
+        copies[:, 0] = jnp.zeros_like(copies[:, 0])
+        copies[:, levels + 1] = jnp.zeros_like(copies[:, levels + 1])
+        line_at = lax.broadcasted_iota(jnp.int32, (width, many), 0)
+        for which, field in ((pos[0], mine), (1 - pos[0], theirs)):
+            lanes = pl.ds(pl.multiple_of(which * many, many), many)
+            for lev in range(levels):
+                for row in range(height + 2):
+                    line = field[lev, row, 0:width].astype(jnp.float32)
+                    west = field[lev, row, width : width + 1].astype(jnp.float32)
+                    east = field[lev, row, width + 8 : width + 9].astype(jnp.float32)
+                    before = jnp.where(line_at == 0, west, pltpu.roll(line, 1, 0))
+                    later = jnp.where(line_at == width - 1, east, pltpu.roll(line, width - 1, 0))
+                    copies[0, lev + 1, row, :, lanes] = later.astype(copies.dtype)
+                    copies[1, lev + 1, row, :, lanes] = field[lev, row, 0:width]
+                    copies[2, lev + 1, row, :, lanes] = before.astype(copies.dtype)
+        acc[...] = jnp.zeros_like(acc)
+
+    lev_by, lat_by, lon_by_ = tap // 9, lax.rem(tap // 3, 3), lax.rem(tap, 3)
+    cells = copies[lon_by_, pl.ds(2 - lev_by, levels), pl.ds(2 - lat_by, height)]
+    acc[...] += lax.dot_general(
+        cells.reshape(levels * height * width, 2 * many),
+        w[0],
+        (((1,), (1,)), ((), ())),
+        preferred_element_type=jnp.float32,
+    )
+
+    @pl.when(tap == 26)
+    def _():
+        out[...] = acc[...].reshape(out.shape).astype(out.dtype)
+
+
+def blocked_body(inputs, weights, out_grad):
+    chans, levels, height, width = inputs.shape
+    filters = weights.shape[2]
+    bf16, f32 = jnp.bfloat16, jnp.float32
+    lat, lon = lax.axis_index("lat"), lax.axis_index("lon")
+    pos = jnp.stack([lax.axis_index("ch"), lat, lon]).astype(jnp.int32)
+    x_cells = jnp.transpose(inputs, (1, 2, 3, 0))
+    g_cells = jnp.transpose(out_grad, (1, 2, 3, 0))
+    taps = jnp.transpose(weights, (1, 0, 2))
+    cells = levels * height * width
+    span, wide = chans // 4, filters // 4
+    packed = jax.ShapeDtypeStruct((cells // 2, 2 * span), bf16)
+    block = jax.ShapeDtypeStruct((cells, wide), bf16)
+    rim = jax.ShapeDtypeStruct((levels, width, chans), bf16)
+    x0, x1, x2, x3, g_same, g_other, rim_lo, rim_hi = call(
+        pack_kernel,
+        [packed] * 4 + [block] * 2 + [rim] * 2,
+        (pos, x_cells, g_cells),
+        [VMEM((4,) + packed.shape, bf16)],
+        0,
+        "pack",
+    )
+
+    to_same = lambda c, a, o: (a // 2, 2 * c + a % 2, o)
+    to_other = lambda c, a, o: (a // 2, 2 * c + 1 - a % 2, o)
+    g_s = move(g_same, to_same)
+    g_o = move(g_other, to_other)
+    x_r1 = move(x1, lon_by(1))
+    x_r3 = move(x3, lon_by(-1))
+    x_r2 = move(x2, lon_by(2))
+    g0 = jnp.stack([g_s, g_o])
+    g1 = move(g0, lon_by(1))
+    g3 = move(g0, lon_by(-1))
+    s0 = move(g0, sibling)
+    x_own = jnp.stack([x0, x_r1, x_r2, x_r3])
+    x_x = move(x_own, lat_xor(1))
+    x_y = move(x_own, lat_xor(2))
+    x_d1 = move(x_y[0:2], lat_xor(1))
+    x_d2 = move(x_x[2:4], lat_xor(2))
+    g2a = move(g1[0], lon_by(1))
+    g2b = move(g3[1], lon_by(-1))
+    s1 = move(g1, sibling)
+    s3 = move(g3, sibling)
+    s2a = move(g2a, sibling)
+    s2b = move(g2b, sibling)
+
+    from_lo = move(rim_hi, north)
+    from_hi = move(rim_lo, south)
+    tall = jnp.concatenate([from_lo[:, None], g_cells, from_hi[:, None]], axis=1)
+    west = move(tall[:, :, width - 1], lon_by(1))
+    east = move(tall[:, :, 0], lon_by(-1))
+    rims = jnp.stack([jnp.broadcast_to(r[:, :, None], r.shape[:2] + (8,) + r.shape[2:]) for r in (west, east)], 2)
+    mine = jnp.concatenate([tall, rims.reshape(levels, height + 2, 16, chans)], axis=2)
+    theirs = move(mine, sibling)
+
+    rows, circle = 4 * height, 4 * width
+    (grads,) = call(
+        taps_kernel,
+        [jax.ShapeDtypeStruct((27 * span + 16, wide), f32)],
+        (pos, x_own, x_x, x_y, x_d1, x_d2, g0, g1, g3, g2a, g2b, s0, s1, s3, s2a, s2b),
+        [
+            VMEM((levels, rows + 2, circle, 4 * span), bf16),
+            VMEM((levels, rows, circle, wide), bf16),
+            VMEM((levels * wide, rows * circle), bf16),
+            VMEM((3, 3 * wide, 4 * span), f32),
+        ],
+        2 * 27 * span * wide * rows * circle * levels,
+        "taps",
+    )
+    own = grads.astype(jnp.float16)
+
+    weight_grad = jnp.zeros((27, chans, filters), f32)
+    cut = 14 * span
+
+    def put(total, top, bottom, lat_from, lon_from):
+        factor = jnp.exp2(bottom[-1:, :].astype(f32) - 14.0)
+        for piece, first, last in ((top, 0, 14), (bottom, 14, 27)):
+            value = piece[0 : (last - first) * span].reshape(last - first, span, wide)
+            total = lax.dynamic_update_slice(
+                total, value.astype(f32) * factor[None], (first, lon_from * span, lat_from * wide)
+            )
+        return total
+
+    def put_whole(total, piece, lat_from, lon_from):
+        factor = jnp.exp2(piece[-1:, :].astype(f32) - 14.0)
+        value = piece[0 : 27 * span].reshape(27, span, wide).astype(f32) * factor[None]
+        return lax.dynamic_update_slice(total, value, (0, lon_from * span, lat_from * wide))
+
+    from_1 = move(own, lon_by(1))
+    from_3 = move(own, lon_by(-1))
+    shares = {0: own, 3: from_1, 1: from_3}
+    opp_top = move(from_1[:cut], lon_by(1))
+    opp_bottom = move(from_3[cut:], lon_by(-1))
+    for step in (0, 3, 1, 2):
+        share = shares[step] if step != 2 else jnp.concatenate([opp_top, opp_bottom])
+        there = lax.rem(lon + step, 4)
+        weight_grad = put_whole(weight_grad, share, lat, there)
+        by_x = move(share, lat_xor(1))
+        by_y = move(share, lat_xor(2))
+        top = move(by_y[:cut], lat_xor(1))
+        bottom = move(by_x[cut:], lat_xor(2))
+        weight_grad = put_whole(weight_grad, by_x, lat ^ 1, there)
+        weight_grad = put_whole(weight_grad, by_y, lat ^ 2, there)
+        weight_grad = put(weight_grad, top, bottom, lat ^ 3, there)
+
+    whole = lambda t: (0, 0, 0, 0)
+    field = pl.pallas_call(
+        field_kernel,
+        out_shape=jax.ShapeDtypeStruct((levels, height, width, chans), bf16),
+        grid=(27,),
+        in_specs=[
+            pl.BlockSpec(memory_space=SMEM),
+            pl.BlockSpec(memory_space=pl.ANY),
+            pl.BlockSpec(mine.shape, whole),
+            pl.BlockSpec(mine.shape, whole),
+            pl.BlockSpec((1, chans, filters), lambda t: (t, 0, 0)),
+        ],
+        out_specs=pl.BlockSpec((levels, height, width, chans), whole),
+        scratch_shapes=[
+            VMEM((3, levels + 2, height + 2, width, filters), bf16),
+            VMEM((cells, chans), f32),
+        ],
+        cost_estimate=pl.CostEstimate(
+            flops=2 * 27 * chans * filters * cells, bytes_accessed=27 * chans * filters * 2, transcendentals=0
+        ),
+        compiler_params=pltpu.CompilerParams(vmem_limit_bytes=LIMIT),
+        name="field",
+    )(pos, grads, mine, theirs, taps)
+    return (jnp.transpose(field, (3, 0, 1, 2)), jnp.transpose(weight_grad, (1, 0, 2)))
+
+
+def body(inputs, weights, out_grad):
+    chans, levels, height, width = inputs.shape
+    shape = tuple(lax.axis_size(axis) for axis in AXES)
+    fits = (
+        shape == (2, 4, 4)
+        and chans == out_grad.shape[0] == 256
+        and weights.shape[2] == 512
+        and levels % 2 == 0
+        and height % 2 == 0
+        and width % 16 == 0
+    )
+    return (blocked_body if fits else plain_body)(inputs, weights, out_grad)
+
+
 def solution(mesh):
     in_specs = (P("ch", None, "lat", "lon"), P("ch", None, None), P("ch", None, "lat", "lon"))
     out_specs = (P("ch", None, "lat", "lon"), P("ch", None, None))

time: 592 us -> 174 us (0.29); the launches traced: 585 us -> 174 us
  local copies, waits for them, and re-layouts: 332 us -> 12.1 us
  waiting for transfers between devices: 131 us -> 41.9 us
  Pallas kernels: 0 us -> 41.6 us
  starting transfers between devices: 12.8 us -> 53.5 us
  matrix products: 37.1 us -> 0 us
  other arithmetic: 55.1 us -> 23.4 us
  between operations: 14.1 us -> 1.21 us
    reshape x5 -> x0, local copies, waits for them, and re-layouts: 189 us -> none  [the longest x1 122 us: body(): products = products.reshape((chans, 27) + tuple(grad_pad.shape[1:]))]
    psum x1 -> x0, waiting for transfers between devices: 109 us -> none  [body(): summed = lax.psum(partial_grad, ('lat', 'lon'))]
    dot_general x1 -> x0, local copies, waits for them, and re-layouts: 51.6 us -> none  [body(): jnp.dot(weights.reshape(chans * 27, filters), grad_pad.reshape(filters, -...]
    unnamed x33 -> x27, local copies, waits for them, and re-layouts: 53.5 us -> 3.04 us
    pallas_call x0 -> x3, Pallas kernels: none -> 41.6 us  [the longest x1 21.4 us: blocked_body(): pl.pallas_call(field_kernel, out_shape=jax.ShapeDtypeStruct((levels, heig...]
    ppermute x8 -> x43, starting transfers between devices: 12.7 us -> 53.5 us  [move(): return lax.ppermute(x, AXES, pairs)]
    convert_element_type x1, other arithmetic: 41.6 us -> 1.23 us  [blocked_body(): own = grads.astype(jnp.float16)]
    another operation x2, local copies, waits for them, and re-layouts: 37.4 us -> 0.03 us  [blocked_body(): jnp.stack([jnp.broadcast_to(r[:, :, None], r.shape[:2] + (8,) + r.shape[2...]
  transfers between devices with their start and end apart: 9 -> 43, of which waited for: 7 -> 11; matrix products, arithmetic and copies ran while one was open for 46% -> 17% of each run, Pallas kernels for 0% -> 23%
where the time goes in v1:
time: 174 us
  starting transfers between devices  53.5 us (31%)
  waiting for transfers between devices  41.9 us (24%)
  Pallas kernels  41.6 us (24%)
  other arithmetic  23.4 us (13%)
  local copies, waits for them, and re-layouts  12.1 us (7%)
    ppermute x43, starting transfers between devices, move(): return lax.ppermute(x, AXES, pairs)  53.5 us
    ppermute x43, waiting for transfers between devices, move(): return lax.ppermute(x, AXES, pairs)  41.9 us
    pallas_call x1, Pallas kernels, blocked_body(): pl.pallas_call(field_kernel, out_shape=jax.ShapeDtypeStruct((levels, heig...  21.4 us
    pallas_call x2, Pallas kernels, call(): pl.pallas_call(kernel, out_shape=outs, in_specs=[pl.BlockSpec(memory_spac...  20.1 us
    dynamic_update_slice x12, other arithmetic, put_whole(): lax.dynamic_update_slice(total, value, (0, lon_from * span, lat_from * wi...  12 us
    broadcast_in_dim x1, local copies, waits for them, and re-layouts, blocked_body(): weight_grad = jnp.zeros((27, chans, filters), f32)  7.11 us
    dynamic_update_slice x8, other arithmetic, put(): lax.dynamic_update_slice(total, value.astype(f32) * factor[None], (first,...  6.39 us
  transfers between devices with their start and end apart: 43, of which 11 were waited for; matrix products, arithmetic and copies ran while one was open for 17% of the time, Pallas kernels for 23%

profile of v1, /device:TPU:0, one launch (start us, length us, event | category | flops | bytes accessed | tf_op | source)
XLA Modules:
  0.0 173.5 jit_solution(10576259491482879962)
XLA Ops:
  1.3 2.2 %pack.1 = (bf16[384,128]{1,0:T(8,128)(2,1)}, bf16[384,128]{1,0:T(8,128)(2,1)}, bf16[384,128]{1,0:T(8,128)(2,1)}, bf16[384,128]{1,0:T(8,128)(2,1)}, bf16[768,128]...) custom-call(s32[3]{0:T(128)} %pad_add_fusion.pos, ...), custom_call_target="tpu_custom_call" | custom-call | bytes 1769472 | tf_op jit(solution)/shard_map/pack/pallas_call | solution.py:124
  3.5 5.0 %collective-permute-start.2 = (bf16[384,128]{1,0:T(8,128)(2,1)}, bf16[384,128]{1,0:T(8,128)(2,1)S(1)}, u32[]{:S(2)}, u32[]{:S(2)}) collective-permute-start(bf16[384,128]{1,0:T(8,128)(2,1)} %get-tuple-element.13), channel_id=1, source_target_pairs={{0,3},{1,0},{2,1},{3,2},{4,7},{5,4},{6,5},{7,6},{8,11},{9,8},{10,9... | collective-permute-start | bytes 294920 | tf_op jit(solution)/shard_map/ppermute | solution.py:99
  8.5 1.0 collective-permute-start
  9.6 1.5 collective-permute-start.8
  11.0 1.6 collective-permute-start.7
  12.6 4.9 %collective-permute-done.1 = bf16[384,128]{1,0:T(8,128)(2,1)S(1)} collective-permute-done((bf16[384,128]{1,0:T(8,128)(2,1)}, bf16[384,128]{1,0:T(8,128)(2,1)S(1)}, u32[]{:S(2)}, u32[]{:S(2)}) %collective-permute-start.1) | collective-permute-done | bytes 98336 | tf_op jit(solution)/shard_map/ppermute | solution.py:99
  18.5 1.6 collective-permute-start.4
  20.6 1.3 collective-permute-start.19
  21.9 4.6 %collective-permute-start.18 = (bf16[4,48,256]{2,1,0:T(8,128)(2,1)}, bf16[4,48,256]{2,1,0:T(8,128)(2,1)S(1)}, u32[]{:S(2)}, u32[]{:S(2)}) collective-permute-start(bf16[4,48,256]{2,1,0:T(8,128)(2,1)} %get-tuple-element.16), channel_id=1, source_target_pairs={{0,4},{1,5},{2,6},{3,7},{4,8},{5,9},{6,10},{7,11},{8,12},{9,13},{1... | collective-permute-start | bytes 294920 | tf_op jit(solution)/shard_map/ppermute | solution.py:99
  26.5 3.4 %collective-permute-start.10 = (bf16[2,768,128]{2,1,0:T(8,128)(2,1)S(1)}, bf16[2,768,128]{2,1,0:T(8,128)(2,1)S(1)}, u32[]{:S(2)}, u32[]{:S(2)}) collective-permute-start(bf16[2,768,128]{2,1,0:T(8,128)(2,1)S(1)} %pad_maximum_fusion.2.g0), channel_id=1, source_target_pairs={{0,3},{1,0},{2,1},{3,2},{4,7},{5,4},{6,5},{7,6},{8,11},{9,8},{10,9... | collective-permute-start | bytes 1179656 | tf_op jit(solution)/shard_map/ppermute | solution.py:99
  29.9 2.4 %collective-permute-start.3 = (bf16[4,384,128]{2,1,0:T(8,128)(2,1)S(1)}, bf16[4,384,128]{2,1,0:T(8,128)(2,1)S(1)}, u32[]{:S(2)}, u32[]{:S(2)}) collective-permute-start(bf16[4,384,128]{2,1,0:T(8,128)(2,1)S(1)} %pad_maximum_fusion.1.x_own), channel_id=1, source_target_pairs={{0,4},{1,5},{2,6},{3,7},{4,0},{5,1},{6,2},{7,3},{8,12},{9,13},{10,... | collective-permute-start | bytes 1179656 | tf_op jit(solution)/shard_map/ppermute | solution.py:99
  33.2 1.9 %collective-permute-start.21 = (bf16[4,6,256]{2,0,1:T(4,128)(2,1)S(1)}, bf16[4,6,256]{2,0,1:T(4,128)(2,1)S(1)}, u32[]{:S(2)}, u32[]{:S(2)}) collective-permute-start(bf16[4,6,256]{2,0,1:T(4,128)(2,1)S(1)} %bitcast.135), channel_id=1, source_target_pairs={{0,3},{1,0},{2,1},{3,2},{4,7},{5,4},{6,5},{7,6},{8,11},{9,8},{10,9... | collective-permute-start | bytes 36872 | tf_op jit(solution)/shard_map/ppermute | solution.py:99
  35.5 5.6 %collective-permute-done.10.g3 = bf16[2,768,128]{2,1,0:T(8,128)(2,1)S(1)} collective-permute-done((bf16[2,768,128]{2,1,0:T(8,128)(2,1)S(1)}, bf16[2,768,128]{2,1,0:T(8,128)(2,1)S(1)}, u32[]{:S(2)}, u32[]{:S(2)}) %collective-permute-start.10) | collective-permute-done | bytes 393248 | tf_op jit(solution)/shard_map/ppermute | solution.py:99
  41.1 1.3 collective-permute-start.5
  43.1 3.3 %collective-permute-start.12 = (bf16[768,128]{1,0:T(8,128)(2,1)S(1)}, bf16[768,128]{1,0:T(8,128)(2,1)}, u32[]{:S(2)}, u32[]{:S(2)}) collective-permute-start(bf16[768,128]{1,0:T(8,128)(2,1)S(1)} %slice_bitcast_fusion), channel_id=1, source_target_pairs={{0,3},{1,0},{2,1},{3,2},{4,7},{5,4},{6,5},{7,6},{8,11},{9,8},{10,9... | collective-permute-start | bytes 589832 | tf_op jit(solution)/shard_map/ppermute | solution.py:99
  48.2 4.0 %collective-permute-done.11.g2a = bf16[768,128]{1,0:T(8,128)(2,1)} collective-permute-done((bf16[768,128]{1,0:T(8,128)(2,1)S(1)}, bf16[768,128]{1,0:T(8,128)(2,1)}, u32[]{:S(2)}, u32[]{:S(2)}) %collective-permute-start.11) | collective-permute-done | bytes 196640 | tf_op jit(solution)/shard_map/ppermute | solution.py:99
  53.1 1.1 pad_maximum_fusion.mine
  56.2 17.9 %taps.1.after = f32[1744,128]{1,0:T(8,128)} custom-call(s32[3]{0:T(128)} %pad_add_fusion.pos, bf16[4,384,128]{2,1,0:T(8,128)(2,1)} %copy-done.1, bf16[4,384,128]{2,1,0:T(8,128)(2,1)} %copy-done.6, bf16[4,384,128]{2,1,0:T(8,128)(2,1)} %copy-done.3, bf16[2,384,128]{2,1,0:T(8,128)(2,1)} %copy-done.9, bf16[2,384,128]{2,1,0:T(8,128)(2,1)} %copy-done.10, ...), custom_call_target="tpu_custom_call" | custom-call | flops 5435817984 | bytes 5611520 | tf_op jit(solution)/shard_map/taps/pallas_call | solution.py:124
  74.1 1.2 convert_element_type.171
  75.4 1.7 collective-permute-start.23
  77.1 1.7 %collective-permute-start.27 = (f16[1744,128]{1,0:T(8,128)(2,1)S(1)}, f16[1744,128]{1,0:T(8,128)(2,1)S(1)}, u32[]{:S(2)}, u32[]{:S(2)}) collective-permute-start(f16[1744,128]{1,0:T(8,128)(2,1)S(1)} %convert_element_type.171), channel_id=1, source_target_pairs={{0,1},{1,2},{2,3},{3,0},{4,5},{5,6},{6,7},{7,4},{8,9},{9,10},{10,1... | collective-permute-start | bytes 1339400 | tf_op jit(solution)/shard_map/ppermute | solution.py:99
  78.9 2.1 %collective-permute-start.32 = (f16[1744,128]{1,0:T(8,128)(2,1)S(1)}, f16[1744,128]{1,0:T(8,128)(2,1)S(1)}, u32[]{:S(2)}, u32[]{:S(2)}) collective-permute-start(f16[1744,128]{1,0:T(8,128)(2,1)S(1)} %convert_element_type.171), channel_id=1, source_target_pairs={{0,3},{1,0},{2,1},{3,2},{4,7},{5,4},{6,5},{7,6},{8,11},{9,8},{10,9... | collective-permute-start | bytes 1339400 | tf_op jit(solution)/shard_map/ppermute | solution.py:99
  81.0 7.1 %broadcast_in_dim.8 = f32[27,256,512]{2,1,0:T(8,128)} broadcast(f32[]{:T(128)} %constant.50.clone.1), dimensions={} | broadcast | bytes 14155780 | tf_op jit(solution)/shard_map/broadcast_in_dim | solution.py:359
  88.1 1.0 fusion.11
  90.0 21.4 %field.1 = bf16[4,4,48,256]{3,2,1,0:T(8,128)(2,1)} custom-call(s32[3]{0:T(128)} %pad_add_fusion.pos, f32[1744,128]{1,0:T(8,128)} %taps.1.after, bf16[4,6,64,256]{3,2,1,0:T(8,128)(2,1)} %copy-done, bf16[4,6,64,256]{3,2,1,0:T(8,128)(2,1)} %copy-done.7, bf16[27,256,512]{2,1,0:T(8,128)(2,1)} %bitcast.136), custom_call_target="tpu_custom_call" | custom-call | flops 5435817984 | bytes 7077888 | tf_op jit(solution)/shard_map/field/pallas_call | solution.py:394
  111.5 1.4 collective-permute-start.25
  112.9 1.2 collective-permute-start.26
  114.3 4.0 %collective-permute-start.38 = (f16[848,128]{1,0:T(8,128)(2,1)S(1)}, f16[848,128]{1,0:T(8,128)(2,1)S(1)}, u32[]{:S(2)}, u32[]{:S(2)}) collective-permute-start(f16[848,128]{1,0:T(8,128)(2,1)S(1)} %slice.227), channel_id=1, source_target_pairs={{0,3},{1,0},{2,1},{3,2},{4,7},{5,4},{6,5},{7,6},{8,11},{9,8},{10,9... | collective-permute-start | bytes 651272 | tf_op jit(solution)/shard_map/ppermute | solution.py:99
  118.4 1.0 fusion.10
  119.5 1.0 fusion.9
  120.6 1.7 collective-permute-start.28
  122.6 2.7 %collective-permute-done.38 = f16[848,128]{1,0:T(8,128)(2,1)S(1)} collective-permute-done((f16[848,128]{1,0:T(8,128)(2,1)S(1)}, f16[848,128]{1,0:T(8,128)(2,1)S(1)}, u32[]{:S(2)}, u32[]{:S(2)}) %collective-permute-start.38) | collective-permute-done | bytes 217120 | tf_op jit(solution)/shard_map/ppermute | solution.py:99
  125.2 1.5 collective-permute-start.33
  127.4 1.1 collective-permute-start.39
  131.1 4.6 %collective-permute-done.29 = f16[1744,128]{1,0:T(8,128)(2,1)S(1)} collective-permute-done((f16[1744,128]{1,0:T(8,128)(2,1)S(1)}, f16[1744,128]{1,0:T(8,128)(2,1)S(1)}, u32[]{:S(2)}, u32[]{:S(2)}) %collective-permute-start.29) | collective-permute-done | bytes 446496 | tf_op jit(solution)/shard_map/ppermute | solution.py:99
  135.8 1.4 collective-permute-start.30
  137.4 1.0 fusion.7
  138.4 5.0 %collective-permute-done.33 = f16[1744,128]{1,0:T(8,128)(2,1)S(1)} collective-permute-done((f16[1744,128]{1,0:T(8,128)(2,1)S(1)}, f16[1744,128]{1,0:T(8,128)(2,1)S(1)}, u32[]{:S(2)}, u32[]{:S(2)}) %collective-permute-start.33) | collective-permute-done | bytes 446496 | tf_op jit(solution)/shard_map/ppermute | solution.py:99
  144.6 1.0 fusion.6
  145.6 1.1 collective-permute-start.36
  146.8 11.6 %collective-permute-done.31 = f16[848,128]{1,0:T(8,128)(2,1)S(1)} collective-permute-done((f16[848,128]{1,0:T(8,128)(2,1)S(1)}, f16[848,128]{1,0:T(8,128)(2,1)S(1)}, u32[]{:S(2)}, u32[]{:S(2)}) %collective-permute-start.31) | collective-permute-done | bytes 217120 | tf_op jit(solution)/shard_map/ppermute | solution.py:99
  159.0 1.8 %collective-permute-done.36 = f16[848,128]{1,0:T(8,128)(2,1)S(1)} collective-permute-done((f16[848,128]{1,0:T(8,128)(2,1)S(1)}, f16[848,128]{1,0:T(8,128)(2,1)S(1)}, u32[]{:S(2)}, u32[]{:S(2)}) %collective-permute-start.36) | collective-permute-done | bytes 217120 | tf_op jit(solution)/shard_map/ppermute | solution.py:99
  164.3 1.0 fusion.5
  165.3 1.0 fusion.4
  166.3 1.0 fusion.3
  168.9 1.0 fusion.2
  169.9 1.0 fusion.1
  170.9 1.0 fusion
  (149 shorter events, 22.5 us)
Async XLA Ops:
  3.5 9.1 %collective-permute-start.2 = (bf16[384,128]{1,0:T(8,128)(2,1)}, bf16[384,128]{1,0:T(8,128)(2,1)S(1)}, u32[]{:S(2)}, u32[]{:S(2)}) collective-permute-start(bf16[384,128]{1,0:T(8,128)(2,1)} %get-tuple-element.13), channel_id=1, source_target_pairs={{0,3},{1,0},{2,1},{3,2},{4,7},{5,4},{6,5},{7,6},{8,11},{9,8},{10,9... | collective-permute-start | bytes 294920 | tf_op jit(solution)/shard_map/ppermute | solution.py:99
  8.5 9.0 %collective-permute-start.1 = (bf16[384,128]{1,0:T(8,128)(2,1)}, bf16[384,128]{1,0:T(8,128)(2,1)S(1)}, u32[]{:S(2)}, u32[]{:S(2)}) collective-permute-start(bf16[384,128]{1,0:T(8,128)(2,1)} %get-tuple-element.12), channel_id=1, source_target_pairs={{0,2},{1,3},{2,0},{3,1},{4,6},{5,7},{6,4},{7,5},{8,10},{9,11},{10,... | collective-permute-start | bytes 294920 | tf_op jit(solution)/shard_map/ppermute | solution.py:99
  8.5 9.0 %collective-permute-start = (bf16[384,128]{1,0:T(8,128)(2,1)}, bf16[384,128]{1,0:T(8,128)(2,1)S(1)}, u32[]{:S(2)}, u32[]{:S(2)}) collective-permute-start(bf16[384,128]{1,0:T(8,128)(2,1)} %get-tuple-element.11), channel_id=1, source_target_pairs={{0,1},{1,2},{2,3},{3,0},{4,5},{5,6},{6,7},{7,4},{8,9},{9,10},{10,1... | collective-permute-start | bytes 294920 | tf_op jit(solution)/shard_map/ppermute | solution.py:99
  9.6 10.5 %collective-permute-start.8 = (bf16[768,128]{1,0:T(8,128)(2,1)}, bf16[768,128]{1,0:T(8,128)(2,1)S(1)}, u32[]{:S(2)}, u32[]{:S(2)}) collective-permute-start(bf16[768,128]{1,0:T(8,128)(2,1)} %get-tuple-element.15), channel_id=1, source_target_pairs={{0,4},{1,5},{2,6},{3,7},{4,0},{5,1},{6,2},{7,3},{8,20},{9,21},{10,... | collective-permute-start | bytes 589832 | tf_op jit(solution)/shard_map/ppermute | solution.py:99
  11.0 9.0 %collective-permute-start.7 = (bf16[768,128]{1,0:T(8,128)(2,1)}, bf16[768,128]{1,0:T(8,128)(2,1)S(1)}, u32[]{:S(2)}, u32[]{:S(2)}) collective-permute-start(bf16[768,128]{1,0:T(8,128)(2,1)} %get-tuple-element.14), channel_id=1, source_target_pairs={{0,0},{1,1},{2,2},{3,3},{4,4},{5,5},{6,6},{7,7},{8,16},{9,17},{10,... | collective-permute-start | bytes 589832 | tf_op jit(solution)/shard_map/ppermute | solution.py:99
  18.5 36.4 %copy-start.1 = (bf16[4,384,128]{2,1,0:T(8,128)(2,1)}, bf16[4,384,128]{2,1,0:T(8,128)(2,1)S(1)}, u32[]{:S(2)}) copy-start(bf16[4,384,128]{2,1,0:T(8,128)(2,1)S(1)} %pad_maximum_fusion.1.x_own) | copy-start | bytes 1179652
  18.5 16.7 %collective-permute-start.4 = (bf16[4,384,128]{2,1,0:T(8,128)(2,1)S(1)}, bf16[4,384,128]{2,1,0:T(8,128)(2,1)S(1)}, u32[]{:S(2)}, u32[]{:S(2)}) collective-permute-start(bf16[4,384,128]{2,1,0:T(8,128)(2,1)S(1)} %pad_maximum_fusion.1.x_own), channel_id=1, source_target_pairs={{0,8},{1,9},{2,10},{3,11},{4,12},{5,13},{6,14},{7,15},{8,0},{9,1},... | collective-permute-start | bytes 1179656 | tf_op jit(solution)/shard_map/ppermute | solution.py:99
  20.1 34.8 %copy-start.2 = (bf16[2,768,128]{2,1,0:T(8,128)(2,1)}, bf16[2,768,128]{2,1,0:T(8,128)(2,1)S(1)}, u32[]{:S(2)}) copy-start(bf16[2,768,128]{2,1,0:T(8,128)(2,1)S(1)} %pad_maximum_fusion.2.g0) | copy-start | bytes 1179652
  20.1 15.3 %collective-permute-start.9 = (bf16[2,768,128]{2,1,0:T(8,128)(2,1)S(1)}, bf16[2,768,128]{2,1,0:T(8,128)(2,1)S(1)}, u32[]{:S(2)}, u32[]{:S(2)}) collective-permute-start(bf16[2,768,128]{2,1,0:T(8,128)(2,1)S(1)} %pad_maximum_fusion.2.g0), channel_id=1, source_target_pairs={{0,1},{1,2},{2,3},{3,0},{4,5},{5,6},{6,7},{7,4},{8,9},{9,10},{10,1... | collective-permute-start | bytes 1179656 | tf_op jit(solution)/shard_map/ppermute | solution.py:99
  20.6 9.3 %collective-permute-start.19 = (bf16[4,48,256]{2,1,0:T(8,128)(2,1)}, bf16[4,48,256]{2,1,0:T(8,128)(2,1)S(1)}, u32[]{:S(2)}, u32[]{:S(2)}) collective-permute-start(bf16[4,48,256]{2,1,0:T(8,128)(2,1)} %get-tuple-element.17), channel_id=1, source_target_pairs={{4,0},{5,1},{6,2},{7,3},{8,4},{9,5},{10,6},{11,7},{12,8},{13,9},{1... | collective-permute-start | bytes 294920 | tf_op jit(solution)/shard_map/ppermute | solution.py:99
  21.9 10.4 %collective-permute-start.18 = (bf16[4,48,256]{2,1,0:T(8,128)(2,1)}, bf16[4,48,256]{2,1,0:T(8,128)(2,1)S(1)}, u32[]{:S(2)}, u32[]{:S(2)}) collective-permute-start(bf16[4,48,256]{2,1,0:T(8,128)(2,1)} %get-tuple-element.16), channel_id=1, source_target_pairs={{0,4},{1,5},{2,6},{3,7},{4,8},{5,9},{6,10},{7,11},{8,12},{9,13},{1... | collective-permute-start | bytes 294920 | tf_op jit(solution)/shard_map/ppermute | solution.py:99
  26.5 14.6 %collective-permute-start.10 = (bf16[2,768,128]{2,1,0:T(8,128)(2,1)S(1)}, bf16[2,768,128]{2,1,0:T(8,128)(2,1)S(1)}, u32[]{:S(2)}, u32[]{:S(2)}) collective-permute-start(bf16[2,768,128]{2,1,0:T(8,128)(2,1)S(1)} %pad_maximum_fusion.2.g0), channel_id=1, source_target_pairs={{0,3},{1,0},{2,1},{3,2},{4,7},{5,4},{6,5},{7,6},{8,11},{9,8},{10,9... | collective-permute-start | bytes 1179656 | tf_op jit(solution)/shard_map/ppermute | solution.py:99
  29.9 16.4 %collective-permute-start.3 = (bf16[4,384,128]{2,1,0:T(8,128)(2,1)S(1)}, bf16[4,384,128]{2,1,0:T(8,128)(2,1)S(1)}, u32[]{:S(2)}, u32[]{:S(2)}) collective-permute-start(bf16[4,384,128]{2,1,0:T(8,128)(2,1)S(1)} %pad_maximum_fusion.1.x_own), channel_id=1, source_target_pairs={{0,4},{1,5},{2,6},{3,7},{4,0},{5,1},{6,2},{7,3},{8,12},{9,13},{10,... | collective-permute-start | bytes 1179656 | tf_op jit(solution)/shard_map/ppermute | solution.py:99
  33.2 9.2 %collective-permute-start.21 = (bf16[4,6,256]{2,0,1:T(4,128)(2,1)S(1)}, bf16[4,6,256]{2,0,1:T(4,128)(2,1)S(1)}, u32[]{:S(2)}, u32[]{:S(2)}) collective-permute-start(bf16[4,6,256]{2,0,1:T(4,128)(2,1)S(1)} %bitcast.135), channel_id=1, source_target_pairs={{0,3},{1,0},{2,1},{3,2},{4,7},{5,4},{6,5},{7,6},{8,11},{9,8},{10,9... | collective-permute-start | bytes 36872 | tf_op jit(solution)/shard_map/ppermute | solution.py:99
  35.1 19.7 %copy-start.3 = (bf16[4,384,128]{2,1,0:T(8,128)(2,1)}, bf16[4,384,128]{2,1,0:T(8,128)(2,1)S(1)}, u32[]{:S(2)}) copy-start(bf16[4,384,128]{2,1,0:T(8,128)(2,1)S(1)} %collective-permute-done.4.x_y) | copy-start | bytes 1179652
  35.1 7.9 %collective-permute-start.20 = (bf16[4,6,256]{2,0,1:T(4,128)(2,1)S(1)}, bf16[4,6,256]{2,0,1:T(4,128)(2,1)S(1)}, u32[]{:S(2)}, u32[]{:S(2)}) collective-permute-start(bf16[4,6,256]{2,0,1:T(4,128)(2,1)S(1)} %bitcast.134), channel_id=1, source_target_pairs={{0,1},{1,2},{2,3},{3,0},{4,5},{5,6},{6,7},{7,4},{8,9},{9,10},{10,1... | collective-permute-start | bytes 36872 | tf_op jit(solution)/shard_map/ppermute | solution.py:99
  35.4 19.5 %copy-start.4 = (bf16[2,768,128]{2,1,0:T(8,128)(2,1)}, bf16[2,768,128]{2,1,0:T(8,128)(2,1)S(1)}, u32[]{:S(2)}) copy-start(bf16[2,768,128]{2,1,0:T(8,128)(2,1)S(1)} %collective-permute-done.9.g1) | copy-start | bytes 1179652
  35.4 10.9 %collective-permute-start.13 = (bf16[2,768,128]{2,1,0:T(8,128)(2,1)S(1)}, bf16[2,768,128]{2,1,0:T(8,128)(2,1)S(1)}, u32[]{:S(2)}, u32[]{:S(2)}) collective-permute-start(bf16[2,768,128]{2,1,0:T(8,128)(2,1)S(1)} %pad_maximum_fusion.2.g0), channel_id=1, source_target_pairs={{0,16},{1,17},{2,18},{3,19},{4,20},{5,21},{6,22},{7,23},{8,24},{9,... | collective-permute-start | bytes 1179656 | tf_op jit(solution)/shard_map/ppermute | solution.py:99
  41.1 7.0 %collective-permute-start.5 = (bf16[2,384,128]{2,1,0:T(8,128)(2,1)S(1)}, bf16[2,384,128]{2,1,0:T(8,128)(2,1)S(1)}, u32[]{:S(2)}, u32[]{:S(2)}) collective-permute-start(bf16[2,384,128]{2,1,0:T(8,128)(2,1)S(1)} %slice.192), channel_id=1, source_target_pairs={{0,4},{1,5},{2,6},{3,7},{4,0},{5,1},{6,2},{7,3},{8,12},{9,13},{10,... | collective-permute-start | bytes 589832 | tf_op jit(solution)/shard_map/ppermute | solution.py:99
  42.4 9.8 %collective-permute-start.11 = (bf16[768,128]{1,0:T(8,128)(2,1)S(1)}, bf16[768,128]{1,0:T(8,128)(2,1)}, u32[]{:S(2)}, u32[]{:S(2)}) collective-permute-start(bf16[768,128]{1,0:T(8,128)(2,1)S(1)} %slice_bitcast_fusion.1), channel_id=1, source_target_pairs={{0,1},{1,2},{2,3},{3,0},{4,5},{5,6},{6,7},{7,4},{8,9},{9,10},{10,1... | collective-permute-start | bytes 589832 | tf_op jit(solution)/shard_map/ppermute | solution.py:99
  43.1 10.0 %collective-permute-start.12 = (bf16[768,128]{1,0:T(8,128)(2,1)S(1)}, bf16[768,128]{1,0:T(8,128)(2,1)}, u32[]{:S(2)}, u32[]{:S(2)}) collective-permute-start(bf16[768,128]{1,0:T(8,128)(2,1)S(1)} %slice_bitcast_fusion), channel_id=1, source_target_pairs={{0,3},{1,0},{2,1},{3,2},{4,7},{5,4},{6,5},{7,6},{8,11},{9,8},{10,9... | collective-permute-start | bytes 589832 | tf_op jit(solution)/shard_map/ppermute | solution.py:99
  46.3 8.5 %collective-permute-start.14 = (bf16[2,768,128]{2,1,0:T(8,128)(2,1)S(1)}, bf16[2,768,128]{2,1,0:T(8,128)(2,1)}, u32[]{:S(2)}, u32[]{:S(2)}) collective-permute-start(bf16[2,768,128]{2,1,0:T(8,128)(2,1)S(1)} %collective-permute-done.9.g1), channel_id=1, source_target_pairs={{0,16},{1,17},{2,18},{3,19},{4,20},{5,21},{6,22},{7,23},{8,24},{9,... | collective-permute-start | bytes 1179656 | tf_op jit(solution)/shard_map/ppermute | solution.py:99
  47.1 7.7 %collective-permute-start.15 = (bf16[2,768,128]{2,1,0:T(8,128)(2,1)S(1)}, bf16[2,768,128]{2,1,0:T(8,128)(2,1)}, u32[]{:S(2)}, u32[]{:S(2)}) collective-permute-start(bf16[2,768,128]{2,1,0:T(8,128)(2,1)S(1)} %collective-permute-done.10.g3), channel_id=1, source_target_pairs={{0,16},{1,17},{2,18},{3,19},{4,20},{5,21},{6,22},{7,23},{8,24},{9,... | collective-permute-start | bytes 1179656 | tf_op jit(solution)/shard_map/ppermute | solution.py:99
  48.1 6.5 %collective-permute-start.6 = (bf16[2,384,128]{2,1,0:T(8,128)(2,1)S(1)}, bf16[2,384,128]{2,1,0:T(8,128)(2,1)S(1)}, u32[]{:S(2)}, u32[]{:S(2)}) collective-permute-start(bf16[2,384,128]{2,1,0:T(8,128)(2,1)S(1)} %slice.193), channel_id=1, source_target_pairs={{0,8},{1,9},{2,10},{3,11},{4,12},{5,13},{6,14},{7,15},{8,0},{9,1},... | collective-permute-start | bytes 589832 | tf_op jit(solution)/shard_map/ppermute | solution.py:99
  52.2 2.6 %collective-permute-start.16 = (bf16[768,128]{1,0:T(8,128)(2,1)}, bf16[768,128]{1,0:T(8,128)(2,1)S(1)}, u32[]{:S(2)}, u32[]{:S(2)}) collective-permute-start(bf16[768,128]{1,0:T(8,128)(2,1)} %collective-permute-done.11.g2a), channel_id=1, source_target_pairs={{0,16},{1,17},{2,18},{3,19},{4,20},{5,21},{6,22},{7,23},{8,24},{9,... | collective-permute-start | bytes 589832 | tf_op jit(solution)/shard_map/ppermute | solution.py:99
  53.1 1.8 %collective-permute-start.17 = (bf16[768,128]{1,0:T(8,128)(2,1)}, bf16[768,128]{1,0:T(8,128)(2,1)S(1)}, u32[]{:S(2)}, u32[]{:S(2)}) collective-permute-start(bf16[768,128]{1,0:T(8,128)(2,1)} %collective-permute-done.12.g2b), channel_id=1, source_target_pairs={{0,16},{1,17},{2,18},{3,19},{4,20},{5,21},{6,22},{7,23},{8,24},{9,... | collective-permute-start | bytes 589832 | tf_op jit(solution)/shard_map/ppermute | solution.py:99
  54.2 33.8 %copy-start = (bf16[4,6,64,256]{3,2,1,0:T(8,128)(2,1)}, bf16[4,6,64,256]{3,2,1,0:T(8,128)(2,1)S(1)}, u32[]{:S(2)}) copy-start(bf16[4,6,64,256]{3,2,1,0:T(8,128)(2,1)S(1)} %pad_maximum_fusion.mine) | copy-start | bytes 2359300
  54.6 34.5 %collective-permute-start.22 = (bf16[4,6,64,256]{3,2,1,0:T(8,128)(2,1)S(1)}, bf16[4,6,64,256]{3,2,1,0:T(8,128)(2,1)S(1)}, u32[]{:S(2)}, u32[]{:S(2)}) collective-permute-start(bf16[4,6,64,256]{3,2,1,0:T(8,128)(2,1)S(1)} %pad_maximum_fusion.mine), channel_id=1, source_target_pairs={{0,16},{1,17},{2,18},{3,19},{4,20},{5,21},{6,22},{7,23},{8,24},{9,... | collective-permute-start | bytes 2359304 | tf_op jit(solution)/shard_map/ppermute | solution.py:99
  75.4 37.4 %collective-permute-start.23 = (f16[1744,128]{1,0:T(8,128)(2,1)S(1)}, f16[1744,128]{1,0:T(8,128)(2,1)S(1)}, u32[]{:S(2)}, u32[]{:S(2)}) collective-permute-start(f16[1744,128]{1,0:T(8,128)(2,1)S(1)} %convert_element_type.171), channel_id=1, source_target_pairs={{0,4},{1,5},{2,6},{3,7},{4,0},{5,1},{6,2},{7,3},{8,12},{9,13},{10,... | collective-permute-start | bytes 1339400 | tf_op jit(solution)/shard_map/ppermute | solution.py:99
  77.1 34.3 %collective-permute-start.24 = (f16[1744,128]{1,0:T(8,128)(2,1)S(1)}, f16[1744,128]{1,0:T(8,128)(2,1)S(1)}, u32[]{:S(2)}, u32[]{:S(2)}) collective-permute-start(f16[1744,128]{1,0:T(8,128)(2,1)S(1)} %convert_element_type.171), channel_id=1, source_target_pairs={{0,8},{1,9},{2,10},{3,11},{4,12},{5,13},{6,14},{7,15},{8,0},{9,1},... | collective-permute-start | bytes 1339400 | tf_op jit(solution)/shard_map/ppermute | solution.py:99
  77.1 37.0 %collective-permute-start.27 = (f16[1744,128]{1,0:T(8,128)(2,1)S(1)}, f16[1744,128]{1,0:T(8,128)(2,1)S(1)}, u32[]{:S(2)}, u32[]{:S(2)}) collective-permute-start(f16[1744,128]{1,0:T(8,128)(2,1)S(1)} %convert_element_type.171), channel_id=1, source_target_pairs={{0,1},{1,2},{2,3},{3,0},{4,5},{5,6},{6,7},{7,4},{8,9},{9,10},{10,1... | collective-permute-start | bytes 1339400 | tf_op jit(solution)/shard_map/ppermute | solution.py:99
  78.9 35.3 %collective-permute-start.32 = (f16[1744,128]{1,0:T(8,128)(2,1)S(1)}, f16[1744,128]{1,0:T(8,128)(2,1)S(1)}, u32[]{:S(2)}, u32[]{:S(2)}) collective-permute-start(f16[1744,128]{1,0:T(8,128)(2,1)S(1)} %convert_element_type.171), channel_id=1, source_target_pairs={{0,3},{1,0},{2,1},{3,2},{4,7},{5,4},{6,5},{7,6},{8,11},{9,8},{10,9... | collective-permute-start | bytes 1339400 | tf_op jit(solution)/shard_map/ppermute | solution.py:99
  111.5 15.9 %collective-permute-start.25 = (f16[896,128]{1,0:T(8,128)(2,1)S(1)}, f16[896,128]{1,0:T(8,128)(2,1)S(1)}, u32[]{:S(2)}, u32[]{:S(2)}) collective-permute-start(f16[896,128]{1,0:T(8,128)(2,1)S(1)} %slice.202), channel_id=1, source_target_pairs={{0,4},{1,5},{2,6},{3,7},{4,0},{5,1},{6,2},{7,3},{8,12},{9,13},{10,... | collective-permute-start | bytes 688136 | tf_op jit(solution)/shard_map/ppermute | solution.py:99
  112.9 9.5 %collective-permute-start.26 = (f16[848,128]{1,0:T(8,128)(2,1)S(1)}, f16[848,128]{1,0:T(8,128)(2,1)S(1)}, u32[]{:S(2)}, u32[]{:S(2)}) collective-permute-start(f16[848,128]{1,0:T(8,128)(2,1)S(1)} %slice.203), channel_id=1, source_target_pairs={{0,8},{1,9},{2,10},{3,11},{4,12},{5,13},{6,14},{7,15},{8,0},{9,1},... | collective-permute-start | bytes 651272 | tf_op jit(solution)/shard_map/ppermute | solution.py:99
  114.1 12.7 %collective-permute-start.37 = (f16[896,128]{1,0:T(8,128)(2,1)S(1)}, f16[896,128]{1,0:T(8,128)(2,1)S(1)}, u32[]{:S(2)}, u32[]{:S(2)}) collective-permute-start(f16[896,128]{1,0:T(8,128)(2,1)S(1)} %slice.226), channel_id=1, source_target_pairs={{0,1},{1,2},{2,3},{3,0},{4,5},{5,6},{6,7},{7,4},{8,9},{9,10},{10,1... | collective-permute-start | bytes 688136 | tf_op jit(solution)/shard_map/ppermute | solution.py:99
  114.3 11.0 %collective-permute-start.38 = (f16[848,128]{1,0:T(8,128)(2,1)S(1)}, f16[848,128]{1,0:T(8,128)(2,1)S(1)}, u32[]{:S(2)}, u32[]{:S(2)}) collective-permute-start(f16[848,128]{1,0:T(8,128)(2,1)S(1)} %slice.227), channel_id=1, source_target_pairs={{0,3},{1,0},{2,1},{3,2},{4,7},{5,4},{6,5},{7,6},{8,11},{9,8},{10,9... | collective-permute-start | bytes 651272 | tf_op jit(solution)/shard_map/ppermute | solution.py:99
  120.6 15.1 %collective-permute-start.28 = (f16[1744,128]{1,0:T(8,128)(2,1)S(1)}, f16[1744,128]{1,0:T(8,128)(2,1)S(1)}, u32[]{:S(2)}, u32[]{:S(2)}) collective-permute-start(f16[1744,128]{1,0:T(8,128)(2,1)S(1)} %collective-permute-done.27), channel_id=1, source_target_pairs={{0,4},{1,5},{2,6},{3,7},{4,0},{5,1},{6,2},{7,3},{8,12},{9,13},{10,... | collective-permute-start | bytes 1339400 | tf_op jit(solution)/shard_map/ppermute | solution.py:99
  122.4 13.3 %collective-permute-start.29 = (f16[1744,128]{1,0:T(8,128)(2,1)S(1)}, f16[1744,128]{1,0:T(8,128)(2,1)S(1)}, u32[]{:S(2)}, u32[]{:S(2)}) collective-permute-start(f16[1744,128]{1,0:T(8,128)(2,1)S(1)} %collective-permute-done.27), channel_id=1, source_target_pairs={{0,8},{1,9},{2,10},{3,11},{4,12},{5,13},{6,14},{7,15},{8,0},{9,1},... | collective-permute-start | bytes 1339400 | tf_op jit(solution)/shard_map/ppermute | solution.py:99
  125.2 18.2 %collective-permute-start.33 = (f16[1744,128]{1,0:T(8,128)(2,1)S(1)}, f16[1744,128]{1,0:T(8,128)(2,1)S(1)}, u32[]{:S(2)}, u32[]{:S(2)}) collective-permute-start(f16[1744,128]{1,0:T(8,128)(2,1)S(1)} %collective-permute-done.32), channel_id=1, source_target_pairs={{0,4},{1,5},{2,6},{3,7},{4,0},{5,1},{6,2},{7,3},{8,12},{9,13},{10,... | collective-permute-start | bytes 1339400 | tf_op jit(solution)/shard_map/ppermute | solution.py:99
  126.8 18.8 %collective-permute-start.34 = (f16[1744,128]{1,0:T(8,128)(2,1)S(1)}, f16[1744,128]{1,0:T(8,128)(2,1)S(1)}, u32[]{:S(2)}, u32[]{:S(2)}) collective-permute-start(f16[1744,128]{1,0:T(8,128)(2,1)S(1)} %collective-permute-done.32), channel_id=1, source_target_pairs={{0,8},{1,9},{2,10},{3,11},{4,12},{5,13},{6,14},{7,15},{8,0},{9,1},... | collective-permute-start | bytes 1339400 | tf_op jit(solution)/shard_map/ppermute | solution.py:99
  127.4 34.1 %collective-permute-start.39 = (f16[1744,128]{1,0:T(8,128)(2,1)S(1)}, f16[1744,128]{1,0:T(8,128)(2,1)S(1)}, u32[]{:S(2)}, u32[]{:S(2)}) collective-permute-start(f16[1744,128]{1,0:T(8,128)(2,1)S(1)} %constant_dynamic-update-slice_fusion), channel_id=1, source_target_pairs={{0,4},{1,5},{2,6},{3,7},{4,0},{5,1},{6,2},{7,3},{8,12},{9,13},{10,... | collective-permute-start | bytes 1339400 | tf_op jit(solution)/shard_map/ppermute | solution.py:99
  135.7 25.2 %collective-permute-start.40 = (f16[1744,128]{1,0:T(8,128)(2,1)S(1)}, f16[1744,128]{1,0:T(8,128)(2,1)S(1)}, u32[]{:S(2)}, u32[]{:S(2)}) collective-permute-start(f16[1744,128]{1,0:T(8,128)(2,1)S(1)} %constant_dynamic-update-slice_fusion), channel_id=1, source_target_pairs={{0,8},{1,9},{2,10},{3,11},{4,12},{5,13},{6,14},{7,15},{8,0},{9,1},... | collective-permute-start | bytes 1339400 | tf_op jit(solution)/shard_map/ppermute | solution.py:99
  135.8 26.9 %collective-permute-start.30 = (f16[896,128]{1,0:T(8,128)(2,1)S(1)}, f16[896,128]{1,0:T(8,128)(2,1)S(1)}, u32[]{:S(2)}, u32[]{:S(2)}) collective-permute-start(f16[896,128]{1,0:T(8,128)(2,1)S(1)} %slice.212), channel_id=1, source_target_pairs={{0,4},{1,5},{2,6},{3,7},{4,0},{5,1},{6,2},{7,3},{8,12},{9,13},{10,... | collective-permute-start | bytes 688136 | tf_op jit(solution)/shard_map/ppermute | solution.py:99
  143.5 15.0 %collective-permute-start.31 = (f16[848,128]{1,0:T(8,128)(2,1)S(1)}, f16[848,128]{1,0:T(8,128)(2,1)S(1)}, u32[]{:S(2)}, u32[]{:S(2)}) collective-permute-start(f16[848,128]{1,0:T(8,128)(2,1)S(1)} %slice.213), channel_id=1, source_target_pairs={{0,8},{1,9},{2,10},{3,11},{4,12},{5,13},{6,14},{7,15},{8,0},{9,1},... | collective-permute-start | bytes 651272 | tf_op jit(solution)/shard_map/ppermute | solution.py:99
  145.6 15.2 %collective-permute-start.36 = (f16[848,128]{1,0:T(8,128)(2,1)S(1)}, f16[848,128]{1,0:T(8,128)(2,1)S(1)}, u32[]{:S(2)}, u32[]{:S(2)}) collective-permute-start(f16[848,128]{1,0:T(8,128)(2,1)S(1)} %slice.223), channel_id=1, source_target_pairs={{0,8},{1,9},{2,10},{3,11},{4,12},{5,13},{6,14},{7,15},{8,0},{9,1},... | collective-permute-start | bytes 651272 | tf_op jit(solution)/shard_map/ppermute | solution.py:99
  158.4 8.8 %collective-permute-start.35 = (f16[896,128]{1,0:T(8,128)(2,1)S(1)}, f16[896,128]{1,0:T(8,128)(2,1)S(1)}, u32[]{:S(2)}, u32[]{:S(2)}) collective-permute-start(f16[896,128]{1,0:T(8,128)(2,1)S(1)} %slice.222), channel_id=1, source_target_pairs={{0,4},{1,5},{2,6},{3,7},{4,0},{5,1},{6,2},{7,3},{8,12},{9,13},{10,... | collective-permute-start | bytes 688136 | tf_op jit(solution)/shard_map/ppermute | solution.py:99
  160.9 11.0 %collective-permute-start.41 = (f16[896,128]{1,0:T(8,128)(2,1)S(1)}, f16[896,128]{1,0:T(8,128)(2,1)S(1)}, u32[]{:S(2)}, u32[]{:S(2)}) collective-permute-start(f16[896,128]{1,0:T(8,128)(2,1)S(1)} %slice.234), channel_id=1, source_target_pairs={{0,4},{1,5},{2,6},{3,7},{4,0},{5,1},{6,2},{7,3},{8,12},{9,13},{10,... | collective-permute-start | bytes 688136 | tf_op jit(solution)/shard_map/ppermute | solution.py:99
  161.5 10.3 %collective-permute-start.42 = (f16[848,128]{1,0:T(8,128)(2,1)S(1)}, f16[848,128]{1,0:T(8,128)(2,1)S(1)}, u32[]{:S(2)}, u32[]{:S(2)}) collective-permute-start(f16[848,128]{1,0:T(8,128)(2,1)S(1)} %slice.235), channel_id=1, source_target_pairs={{0,8},{1,9},{2,10},{3,11},{4,12},{5,13},{6,14},{7,15},{8,0},{9,1},... | collective-permute-start | bytes 651272 | tf_op jit(solution)/shard_map/ppermute | solution.py:99
  (8 other events, 33.0 us)

commit v2 on v1

v2 whole, which is shorter than its diff:
```python
import math

import jax
import jax.numpy as jnp
from jax import lax
from jax.experimental import pallas as pl
from jax.experimental.pallas import tpu as pltpu
from jax.sharding import PartitionSpec as P

VMEM = pltpu.VMEM
SMEM = pltpu.SMEM
AXES = ("ch", "lat", "lon")


def padded_2(cells, sides, width):
    for axis, dim in sides:
        count = lax.axis_size(axis)
        head = lax.slice_in_dim(cells, 0, width, axis=dim)
        tail = lax.slice_in_dim(cells, cells.shape[dim] - width, cells.shape[dim], axis=dim)
        cells = jnp.concatenate(
            [
                lax.ppermute(tail, axis, [(i, (i + 1) % count) for i in range(count)]),
                cells,
                lax.ppermute(head, axis, [((i + 1) % count, i) for i in range(count)]),
            ],
            axis=dim,
        )
    return cells


def mask_rims(padded):
    count = lax.axis_size("lat")
    where_lat = lax.axis_index("lat")
    lines = jnp.arange(padded.shape[2])
    drop = (lines == 0) & (where_lat == 0) | (lines == padded.shape[2] - 1) & (
        where_lat == count - 1
    )
    return jnp.where(drop[None, None, :, None], jnp.zeros((), padded.dtype), padded)


def pad_levels(field):
    return jnp.pad(field, ((0, 0), (1, 1), (0, 0), (0, 0)))


def plain_body(inputs, weights, out_grad):
    chans, levels, height, width = inputs.shape
    input_pad = pad_levels(mask_rims(padded_2(inputs, (("lat", 2), ("lon", 3)), 1)))
    grad_inner = lax.all_gather(out_grad, "ch", axis=0, tiled=True)
    grad_pad = pad_levels(mask_rims(padded_2(grad_inner, (("lat", 2), ("lon", 3)), 1)))
    filters = grad_pad.shape[0]
    products = jnp.dot(
        weights.reshape(chans * 27, filters),
        grad_pad.reshape(filters, -1),
        preferred_element_type=jnp.float32,
    )
    products = products.reshape((chans, 27) + tuple(grad_pad.shape[1:]))
    total = jnp.zeros((chans, levels, height, width), jnp.float32)
    pieces = []
    for tap in range(27):
        lev, lat, lon = tap // 9 - 1, tap // 3 % 3 - 1, tap % 3 - 1
        total = (
            total
            + products[
                :,
                tap,
                1 - lev : 1 - lev + levels,
                1 - lat : 1 - lat + height,
                1 - lon : 1 - lon + width,
            ]
        )
        pieces.append(
            input_pad[
                :,
                1 + lev : 1 + lev + levels,
                1 + lat : 1 + lat + height,
                1 + lon : 1 + lon + width,
            ]
        )
    columns = jnp.stack(pieces, axis=1).reshape(chans * 27, -1)
    partial_grad = lax.dot_general(
        columns,
        grad_inner.reshape(filters, -1),
        (((1,), (1,)), ((), ())),
        preferred_element_type=jnp.float32,
    )
    summed = lax.psum(partial_grad, ("lat", "lon"))
    cells = levels * height * width * lax.axis_size("lat") * lax.axis_size("lon")
    weight_grad = (summed * (1.0 / math.sqrt(cells))).reshape(chans, 27, filters)
    return (total.astype(jnp.bfloat16), weight_grad)


def move(x, target):
    pairs = []
    for i in range(32):
        to = target(i // 16, i // 4 % 4, i % 4)
        if to is not None:
            pairs.append((i, (to[0] * 4 + to[1]) * 4 + to[2]))
    return lax.ppermute(x, AXES, pairs)


def lon_by(step):
    return lambda c, a, o: (c, a, (o + step) % 4)


def lat_xor(mask):
    return lambda c, a, o: (c, a ^ mask, o)


def sibling(c, a, o):
    return (1 - c, a, o)


def north(c, a, o):
    return (c, a + 1, o) if a < 3 else None


def south(c, a, o):
    return (c, a - 1, o) if a > 0 else None


def call(kernel, outs, ins, scratch, flops, name, limit, held=0):
    read = len(ins) - 1 - held
    moved = sum(math.prod(x.shape) * x.dtype.itemsize for x in list(ins[1 : 1 + read]) + list(outs))
    return pl.pallas_call(
        kernel,
        out_shape=outs,
        in_specs=[pl.BlockSpec(memory_space=SMEM)]
        + [pl.BlockSpec(memory_space=VMEM)] * read
        + [pl.BlockSpec(memory_space=pl.ANY)] * held,
        out_specs=[pl.BlockSpec(memory_space=VMEM)] * len(outs),
        scratch_shapes=scratch,
        cost_estimate=pl.CostEstimate(flops=flops, bytes_accessed=moved, transcendentals=0),
        compiler_params=pltpu.CompilerParams(vmem_limit_bytes=limit * 1024 * 1024),
        name=name,
    )(*ins)


def pack_grad_kernel(pos, g, g_same, g_other):
    right = lax.rem(pos[1], 2)
    wide = g.shape[-1] // 2
    for out, half in ((g_same, right), (g_other, 1 - right)):
        out[...] = g[:, :, :, pl.ds(pl.multiple_of(half * wide, wide), wide)].reshape(out.shape)


def pack_input_kernel(pos, x, g, after, x0, x1, x2, x3, held):
    del after
    levels, height, width, chans = x.shape
    half = levels // 2
    many = x0.shape[0]
    for block in range(4):
        at = block * (chans // 4)
        lo = x[0:half, :, :, at : at + chans // 4]
        hi = x[half:levels, :, :, at : at + chans // 4]
        held[block] = jnp.concatenate([lo, hi], axis=-1).reshape(held.shape[1:])
    lon = pos[2]
    for step, out in enumerate((x0, x1, x2, x3)):
        out[0:many, :] = held[lax.rem(lon + step, 4)]
    wide = chans // 2
    for out, column in ((x1, width - 1), (x3, 0)):
        rim = g[:, :, column, :].reshape(levels * height, chans)
        out[many : many + levels * height, :] = rim[:, 0:wide]
        out[many + levels * height :, :] = rim[:, wide:]


def lines_kernel(pos, x_own, x_x, x_y, x_d, xs, blank):
    del blank
    lat = pos[1]
    levels, rows, circle, lanes = xs.shape
    rows, width, span, half = rows - 2, circle // 4, lanes // 4, levels // 2
    height = rows // 4
    xs[:, 0] = jnp.zeros_like(xs[:, 0])
    xs[:, rows + 1] = jnp.zeros_like(xs[:, rows + 1])
    low = lax.broadcasted_iota(jnp.int32, (circle, 2 * span), 1) < span
    for tag, ref in enumerate((x_own, x_x, x_y, x_d)):
        start = (lat ^ tag) * height
        strips = [ref.at[(4 - at) % 4].reshape(half, height, width, 2 * span) for at in range(4)]

        @pl.loop(0, half * height)
        def _(step, strips=strips, start=start):
            lev, row = step // height, lax.rem(step, height)
            line = jnp.concatenate([s[lev, row] for s in strips], axis=0).astype(jnp.float32)
            turned = pltpu.roll(line, span, 1)
            for upper in range(2):
                same = jnp.where(low, turned, line) if upper else jnp.where(low, line, turned)
                before = pltpu.roll(same, 1, 0)
                after = pltpu.roll(same, circle - 1, 0)
                at = upper * half + lev
                xs[at, 1 + start + row, :, 0 : 2 * span] = jnp.where(low, before, same).astype(xs.dtype)
                xs[at, 1 + start + row, :, 2 * span : 4 * span] = after.astype(xs.dtype)


def turn(gt, slot, core, first, second, levels):
    many, filters = first.shape
    line = many // levels
    for lev in range(levels):
        block = jnp.concatenate([first[lev * line : (lev + 1) * line], second[lev * line : (lev + 1) * line]], axis=0)
        gt[
            lev * filters : (lev + 1) * filters,
            pl.ds(pl.multiple_of((2 * slot + core) * 2 * line, 2 * line), 2 * line),
        ] = block.T


def add_taps(acc, gt, xs, places):
    levels, rows, circle, lanes = xs.shape
    rows, width = rows - 2, circle // 4
    filters = gt.shape[0] // levels
    deep = rows * width

    @pl.loop(0, 3)
    def _(lat_by):
        for lev in range(levels):
            first, last = max(lev - 1, 0), min(lev + 1, levels - 1)
            to = (first - lev + 1) * filters
            many = (last - first + 1) * filters
            total = acc[lat_by, to : to + many, :]
            for slot, place in enumerate(places):
                total += jnp.dot(
                    gt[first * filters : (last + 1) * filters, slot * deep : (slot + 1) * deep],
                    xs[lev, pl.ds(lat_by, rows), place * width : (place + 1) * width].reshape(deep, lanes),
                    preferred_element_type=jnp.float32,
                )
            acc[lat_by, to : to + many, :] = total


def near_kernel(pos, xs, g0, g1, g3, s0, s1, s3, after, acc, gt):
    del after
    levels = xs.shape[0]
    right = lax.rem(pos[1], 2)
    for core, parts in ((pos[0], (g0, g3, g1)), (1 - pos[0], (s0, s3, s1))):
        for slot, part in enumerate(parts):
            turn(gt, slot, core, part[right], part[1 - right], levels)
    acc[...] = jnp.zeros_like(acc)
    add_taps(acc, gt, xs, (0, 1, 3))


def far_kernel(pos, xs, part, g2a, g2b, s2a, s2b, out, gt, acc, *, early):
    levels, rows, circle, lanes = xs.shape
    span = lanes // 4
    filters = out.shape[1]
    right = lax.rem(pos[1], 2) == 0
    for core, same, other in ((pos[0], g2a, g2b), (1 - pos[0], s2a, s2b)):
        one, two = same[...], other[...]
        turn(gt, 0, core, jnp.where(right, one, two), jnp.where(right, two, one), levels)
    acc[...] = part[...]
    add_taps(acc, gt, xs, (2,))
    scale = 1.0 / math.sqrt(levels * (rows - 2) * circle)

    def place(tap):
        return tap * span + (16 if tap >= early else 0)

    most = jnp.zeros((span, filters), jnp.float32)
    for lat_by in range(3):
        for lev_at in range(3):
            block = acc[lat_by, lev_at * filters : (lev_at + 1) * filters, :].T * scale
            for lon_at in range(3):
                at = place((2 - lev_at) * 9 + lat_by * 3 + lon_at)
                value = block[lon_at * span : (lon_at + 1) * span]
                out[at : at + span, :] = value
                most = jnp.maximum(most, jnp.abs(value))
    top = jnp.maximum(jnp.max(most, axis=(0, 1), keepdims=True), 1e-30)
    power = jnp.broadcast_to(jnp.ceil(jnp.log(top) * (1.0 / math.log(2.0))), (16, filters))
    factor = jnp.exp2(14.0 - power[0:1])
    out[0 : early * span, :] = out[0 : early * span, :] * factor
    out[early * span + 16 :, :] = out[early * span + 16 :, :] * factor
    out[early * span : early * span + 16, :] = power


def field_kernel(pos, mine, theirs, w, out, copies, acc):
    step = pl.program_id(0)
    levels, height, width, chans = out.shape
    many = mine.shape[-1]

    @pl.when(step == 0)
    def _():
        copies[:, 0] = jnp.zeros_like(copies[:, 0])
        copies[:, levels + 1] = jnp.zeros_like(copies[:, levels + 1])
        line_at = lax.broadcasted_iota(jnp.int32, (width, many), 0)
        for which, field in ((pos[0], mine), (1 - pos[0], theirs)):
            lanes = pl.ds(pl.multiple_of(which * many, many), many)
            for lev in range(levels):
                for row in range(height + 2):
                    line = field[lev, row, 0:width].astype(jnp.float32)
                    west = field[lev, row, width : width + 1].astype(jnp.float32)
                    east = field[lev, row, width + 8 : width + 9].astype(jnp.float32)
                    before = jnp.where(line_at == 0, west, pltpu.roll(line, 1, 0))
                    later = jnp.where(line_at == width - 1, east, pltpu.roll(line, width - 1, 0))
                    copies[0, lev + 1, row, :, lanes] = later.astype(copies.dtype)
                    copies[1, lev + 1, row, :, lanes] = field[lev, row, 0:width]
                    copies[2, lev + 1, row, :, lanes] = before.astype(copies.dtype)
        acc[...] = jnp.zeros_like(acc)

    lev_by, lat_by = step // 3, lax.rem(step, 3)
    cells = [
        copies[at, pl.ds(2 - lev_by, levels), pl.ds(2 - lat_by, height)].reshape(
            levels * height * width, 2 * many
        )
        for at in range(3)
    ]
    acc[...] += lax.dot_general(
        jnp.concatenate(cells, axis=1),
        jnp.concatenate([w[at] for at in range(3)], axis=1),
        (((1,), (1,)), ((), ())),
        preferred_element_type=jnp.float32,
    )

    @pl.when(step == 8)
    def _():
        out[...] = acc[...].reshape(out.shape).astype(out.dtype)


def blocked_body(inputs, weights, out_grad):
    chans, levels, height, width = inputs.shape
    filters = weights.shape[2]
    bf16, f32 = jnp.bfloat16, jnp.float32
    lat, lon = lax.axis_index("lat"), lax.axis_index("lon")
    pos = jnp.stack([lax.axis_index("ch"), lat, lon]).astype(jnp.int32)
    x_cells = jnp.transpose(inputs, (1, 2, 3, 0))
    g_cells = jnp.transpose(out_grad, (1, 2, 3, 0))
    taps = jnp.transpose(weights, (1, 0, 2))
    cells = levels * height * width
    span, wide = chans // 4, filters // 4
    rows, circle = 4 * height, 4 * width
    edge = levels * height

    to_same = lambda c, a, o: (a // 2, 2 * c + a % 2, o)
    to_other = lambda c, a, o: (a // 2, 2 * c + 1 - a % 2, o)
    g_same, g_other = call(
        pack_grad_kernel, [jax.ShapeDtypeStruct((cells, wide), bf16)] * 2, (pos, g_cells), [], 0, "pack_grad", 16
    )
    g_s = move(g_same, to_same)
    g_o = move(g_other, to_other)
    many = cells // 2
    x0, x1, x2, x3 = call(
        pack_input_kernel,
        [jax.ShapeDtypeStruct((many + extra, 2 * span), bf16) for extra in (0, 2 * edge, 0, 2 * edge)],
        (pos, x_cells, g_cells, g_same),
        [VMEM((4, many, 2 * span), bf16)],
        0,
        "pack_input",
        16,
        held=1,
    )
    x_r1 = move(x1, lon_by(1))
    x_r3 = move(x3, lon_by(-1))
    x_r2 = move(x2, lon_by(2))
    g0 = jnp.stack([g_s, g_o])
    g1 = move(g0, lon_by(1))
    g3 = move(g0, lon_by(-1))

    def column(message):
        rim = message[many:].reshape(2, edge, span * 2)
        rim = jnp.concatenate([rim[0], rim[1]], axis=-1).reshape(levels, height, 1, chans)
        return jnp.broadcast_to(rim, (levels, height, 8, chans))

    broad = jnp.concatenate([g_cells, column(x_r1), column(x_r3)], axis=2)
    from_lo = move(broad[:, height - 1], north)
    from_hi = move(broad[:, 0], south)
    mine = jnp.concatenate([from_lo[:, None], broad, from_hi[:, None]], axis=1)
    theirs = move(mine, sibling)

    s0 = move(g0, sibling)
    x_own = jnp.stack([x0, x_r1[:many], x_r2, x_r3[:many]])
    x_x = move(x_own, lat_xor(1))
    x_y = move(x_own, lat_xor(2))
    x_d = move(x_own, lat_xor(3))
    g2a = move(g1[0], lon_by(1))
    g2b = move(g3[1], lon_by(-1))
    s1 = move(g1, sibling)
    s3 = move(g3, sibling)
    s2a = move(g2a, sibling)
    s2b = move(g2b, sibling)

    xs, total = pl.pallas_call(
        lines_kernel,
        out_shape=[
            jax.ShapeDtypeStruct((levels, rows + 2, circle, 4 * span), bf16),
            jax.ShapeDtypeStruct((27, chans, filters), f32),
        ],
        in_specs=[pl.BlockSpec(memory_space=SMEM)] + [pl.BlockSpec(memory_space=VMEM)] * 4,
        out_specs=[pl.BlockSpec(memory_space=VMEM), pl.BlockSpec(memory_space=pl.ANY)],
        cost_estimate=pl.CostEstimate(flops=0, bytes_accessed=12 * 2**20, transcendentals=0),
        compiler_params=pltpu.CompilerParams(vmem_limit_bytes=24 * 1024 * 1024),
        name="lines",
    )(pos, x_own, x_x, x_y, x_d)

    whole = lambda t: (0, 0, 0, 0)
    field = pl.pallas_call(
        field_kernel,
        out_shape=jax.ShapeDtypeStruct((levels, height, width, chans), bf16),
        grid=(9,),
        in_specs=[
            pl.BlockSpec(memory_space=SMEM),
            pl.BlockSpec(mine.shape, whole),
            pl.BlockSpec(mine.shape, whole),
            pl.BlockSpec((3, chans, filters), lambda t: (t, 0, 0)),
        ],
        out_specs=pl.BlockSpec((levels, height, width, chans), whole),
        scratch_shapes=[
            VMEM((3, levels + 2, height + 2, width, filters), bf16),
            VMEM((cells, chans), f32),
        ],
        cost_estimate=pl.CostEstimate(
            flops=4 * 27 * chans * filters * cells, bytes_accessed=27 * chans * filters * 2, transcendentals=0
        ),
        compiler_params=pltpu.CompilerParams(vmem_limit_bytes=32 * 1024 * 1024),
        name="field",
    )(pos, mine, theirs, taps)

    work = 2 * 27 * span * wide * rows * circle * levels
    (part,) = call(
        near_kernel,
        [jax.ShapeDtypeStruct((3, 3 * wide, 4 * span), f32)],
        (pos, xs, g0, g1, g3, s0, s1, s3, field),
        [VMEM((levels * wide, 3 * rows * width), bf16)],
        work,
        "near",
        28,
        held=1,
    )
    early = 6
    (grads,) = call(
        lambda *refs: far_kernel(*refs, early=early),
        [jax.ShapeDtypeStruct((27 * span + 16, wide), f32)],
        (pos, xs, part, g2a, g2b, s2a, s2b),
        [VMEM((levels * wide, rows * width), bf16), VMEM((3, 3 * wide, 4 * span), f32)],
        work // 3,
        "far",
        28,
    )
    own = grads.astype(jnp.float16)

    front, back = early * span + 16, early * span
    middle = 16 + 10 * span

    def put(total, piece, power, first, last, lat_from, lon_from):
        factor = jnp.exp2(power.astype(f32) - 14.0)
        value = piece.reshape(last - first, span, wide).astype(f32) * factor[None]
        return lax.dynamic_update_slice(total, value, (first, lon_from * span, lat_from * wide))

    def put_late(total, piece, lat_from, lon_from):
        return put(total, piece[16:], piece[0:1], early, 27, lat_from, lon_from)

    def put_split(total, top, bottom, lat_from, lon_from):
        total = put(total, top[16:], top[0:1], early, early + 10, lat_from, lon_from)
        return put(total, bottom, top[0:1], early + 10, 27, lat_from, lon_from)

    def put_whole(total, piece, lat_from, lon_from):
        total = put(total, piece[:back], piece[back : back + 1], 0, early, lat_from, lon_from)
        return put_late(total, piece[back:], lat_from, lon_from)

    late = own[back:]
    from_1 = move(late, lon_by(1))
    from_3 = move(late, lon_by(-1))
    by_x = move(own, lat_xor(1))
    by_y = move(own, lat_xor(2))
    cut = back + middle
    top = move(by_y[:cut], lat_xor(1))
    bottom = move(by_x[cut:], lat_xor(2))
    opp_top = move(from_1[:middle], lon_by(1))
    opp_bottom = move(from_3[middle:], lon_by(-1))

    def exchange(share):
        to_x = move(share, lat_xor(1))
        to_y = move(share, lat_xor(2))
        return to_x, to_y, move(to_y[:middle], lat_xor(1)), move(to_x[middle:], lat_xor(2))

    block = jnp.concatenate([own[:front], by_x[:front], by_y[:front], top[:front]])
    near_1 = exchange(from_1)
    near_3 = exchange(from_3)
    early_1 = move(block, lon_by(1))
    early_3 = move(block, lon_by(-1))
    from_2 = jnp.concatenate([opp_top, opp_bottom])
    across = exchange(from_2)
    early_2a = move(early_1[: 2 * front], lon_by(1))
    early_2b = move(early_3[2 * front :], lon_by(-1))

    total = put_whole(total, own, lat, lon)
    total = put_whole(total, by_x, lat ^ 1, lon)
    total = put_whole(total, by_y, lat ^ 2, lon)
    total = put(total, top[:back], top[back : back + 1], 0, early, lat ^ 3, lon)
    total = put_split(total, top[back:], bottom, lat ^ 3, lon)

    def put_early(total, pieces, tags, lon_from):
        for at, tag in enumerate(tags):
            piece = pieces[at * front : (at + 1) * front]
            total = put(total, piece[:back], piece[back : back + 1], 0, early, lat ^ tag, lon_from)
        return total

    for share, (to_x, to_y, upper, lower), step in ((from_1, near_1, 3), (from_3, near_3, 1)):
        there = lax.rem(lon + step, 4)
        total = put_late(total, share, lat, there)
        total = put_late(total, to_x, lat ^ 1, there)
        total = put_late(total, to_y, lat ^ 2, there)
        total = put_split(total, upper, lower, lat ^ 3, there)
    there = lax.rem(lon + 2, 4)
    total = put_early(total, early_1, (0, 1, 2, 3), lax.rem(lon + 3, 4))
    total = put_early(total, early_3, (0, 1, 2, 3), lax.rem(lon + 1, 4))
    total = put_late(total, from_2, lat, there)
    total = put_late(total, across[0], lat ^ 1, there)
    total = put_late(total, across[1], lat ^ 2, there)
    total = put_early(total, early_2a, (0, 1), there)
    total = put_early(total, early_2b, (2, 3), there)
    total = put_split(total, across[2], across[3], lat ^ 3, there)
    return (jnp.transpose(field, (3, 0, 1, 2)), jnp.transpose(total, (1, 0, 2)))


def body(inputs, weights, out_grad):
    chans, levels, height, width = inputs.shape
    shape = tuple(lax.axis_size(axis) for axis in AXES)
    fits = (
        shape == (2, 4, 4)
        and chans == out_grad.shape[0] == 256
        and weights.shape[2] == 512
        and levels % 2 == 0
        and height % 2 == 0
        and width % 16 == 0
    )
    return (blocked_body if fits else plain_body)(inputs, weights, out_grad)


def solution(mesh):
    in_specs = (P("ch", None, "lat", "lon"), P("ch", None, None), P("ch", None, "lat", "lon"))
    out_specs = (P("ch", None, "lat", "lon"), P("ch", None, None))
    return jax.shard_map(body, mesh=mesh, in_specs=in_specs, out_specs=out_specs, check_vma=False)
```

time: 174 us -> 172 us (0.989)
  waiting for transfers between devices: 41.9 us -> 63 us
  other arithmetic: 23.4 us -> 2.81 us
  Pallas kernels: 41.6 us -> 26.1 us
  starting transfers between devices: 53.5 us -> 63.7 us
  local copies, waits for them, and re-layouts: 12.1 us -> 14.8 us
    ppermute x43 -> x44, waiting for transfers between devices: 41.9 us -> 63 us  [move(): return lax.ppermute(x, AXES, pairs)]
    dynamic_update_slice x20 -> x36, other arithmetic: 18.3 us -> 2.13 us  [put(): lax.dynamic_update_slice(total, value, (first, lon_from * span, lat_from...]
    pallas_call x1, Pallas kernels: 21.4 us -> 10.1 us  [blocked_body(): pl.pallas_call(field_kernel, out_shape=jax.ShapeDtypeStruct((levels, heig...]
    ppermute x43 -> x44, starting transfers between devices: 53.5 us -> 63.7 us  [move(): return lax.ppermute(x, AXES, pairs)]
    pallas_call x2 -> x4, Pallas kernels: 20.1 us -> 11.1 us  [call(): pl.pallas_call(kernel, out_shape=outs, in_specs=[pl.BlockSpec(memory_spac...]
    unnamed x27 -> x24, local copies, waits for them, and re-layouts: 3.04 us -> 11.4 us
    broadcast_in_dim x1 -> x4, local copies, waits for them, and re-layouts: 7.11 us -> 0.03 us  [column(): return jnp.broadcast_to(rim, (levels, height, 8, chans))]
    pallas_call x0 -> x1, Pallas kernels: none -> 4.87 us  [blocked_body(): pl.pallas_call(lines_kernel, out_shape=[jax.ShapeDtypeStruct((levels, row...]
  transfers between devices with their start and end apart: 43 -> 44, of which waited for: 11 -> 16; matrix products, arithmetic and copies ran while one was open for 17% -> 4% of each run, Pallas kernels for 23% -> 12%
where the time goes in v2:
time: 172 us
  starting transfers between devices  63.7 us (37%)
  waiting for transfers between devices  63 us (37%)
  Pallas kernels  26.1 us (15%)
  local copies, waits for them, and re-layouts  14.8 us (9%)
  other arithmetic  2.81 us (2%)
    ppermute x44, starting transfers between devices, move(): return lax.ppermute(x, AXES, pairs)  63.7 us
    ppermute x44, waiting for transfers between devices, move(): return lax.ppermute(x, AXES, pairs)  63 us
    unnamed x24, local copies, waits for them, and re-layouts  11.4 us
    pallas_call x4, Pallas kernels, call(): pl.pallas_call(kernel, out_shape=outs, in_specs=[pl.BlockSpec(memory_spac...  11.1 us
    pallas_call x1, Pallas kernels, blocked_body(): pl.pallas_call(field_kernel, out_shape=jax.ShapeDtypeStruct((levels, heig...  10.1 us
    pallas_call x1, Pallas kernels, blocked_body(): pl.pallas_call(lines_kernel, out_shape=[jax.ShapeDtypeStruct((levels, row...  4.87 us
  transfers between devices with their start and end apart: 44, of which 16 were waited for; matrix products, arithmetic and copies ran while one was open for 4% of the time, Pallas kernels for 12%

profile of v2, /device:TPU:0, one launch (start us, length us, event | category | flops | bytes accessed | tf_op | source)
XLA Modules:
  0.0 172.1 jit_solution(7420591440053918843)
XLA Ops:
  0.7 1.0 copy-done
  4.1 3.1 %collective-permute-start = (bf16[416,128]{1,0:T(8,128)(2,1)S(1)}, bf16[416,128]{1,0:T(8,128)(2,1)S(1)}, u32[]{:S(2)}, u32[]{:S(2)}) collective-permute-start(bf16[416,128]{1,0:T(8,128)(2,1)S(1)} %get-tuple-element.11), channel_id=1, source_target_pairs={{0,1},{1,2},{2,3},{3,0},{4,5},{5,6},{6,7},{7,4},{8,9},{9,10},{10,1... | collective-permute-start | bytes 319496 | tf_op jit(solution)/shard_map/ppermute | solution.py:98
  7.8 2.1 %collective-permute-start.1 = (bf16[416,128]{1,0:T(8,128)(2,1)S(1)}, bf16[416,128]{1,0:T(8,128)(2,1)S(1)}, u32[]{:S(2)}, u32[]{:S(2)}) collective-permute-start(bf16[416,128]{1,0:T(8,128)(2,1)S(1)} %get-tuple-element.12), channel_id=1, source_target_pairs={{0,3},{1,0},{2,1},{3,2},{4,7},{5,4},{6,5},{7,6},{8,11},{9,8},{10,9... | collective-permute-start | bytes 319496 | tf_op jit(solution)/shard_map/ppermute | solution.py:98
  10.9 1.5 collective-permute-start.10
  13.4 3.4 %collective-permute-start.2 = (bf16[4,64,256]{2,1,0:T(8,128)(2,1)S(1)}, bf16[4,64,256]{2,1,0:T(8,128)(2,1)S(1)}, u32[]{:S(2)}, u32[]{:S(2)}) collective-permute-start(bf16[4,64,256]{2,1,0:T(8,128)(2,1)S(1)} %get-tuple-element.18), channel_id=1, source_target_pairs={{0,4},{1,5},{2,6},{3,7},{4,8},{5,9},{6,10},{7,11},{8,12},{9,13},{1... | collective-permute-start | bytes 393224 | tf_op jit(solution)/shard_map/ppermute | solution.py:98
  16.9 1.3 collective-permute-start.3
  19.2 3.0 %collective-permute-start.12 = (bf16[2,768,128]{2,1,0:T(8,128)(2,1)S(1)}, bf16[2,768,128]{2,1,0:T(8,128)(2,1)S(1)}, u32[]{:S(2)}, u32[]{:S(2)}) collective-permute-start(bf16[2,768,128]{2,1,0:T(8,128)(2,1)S(1)} %pad_maximum_fusion.4.g0), channel_id=1, source_target_pairs={{0,3},{1,0},{2,1},{3,2},{4,7},{5,4},{6,5},{7,6},{8,11},{9,8},{10,9... | collective-permute-start | bytes 1179656 | tf_op jit(solution)/shard_map/ppermute | solution.py:98
  22.2 3.1 %collective-permute-done.3 = bf16[4,64,256]{2,1,0:T(8,128)(2,1)S(1)} collective-permute-done((bf16[4,64,256]{2,1,0:T(8,128)(2,1)S(1)}, bf16[4,64,256]{2,1,0:T(8,128)(2,1)S(1)}, u32[]{:S(2)}, u32[]{:S(2)}) %collective-permute-start.3) | collective-permute-done | bytes 131104 | tf_op jit(solution)/shard_map/ppermute | solution.py:98
  25.6 2.1 %collective-permute-start.6 = (bf16[4,384,128]{2,1,0:T(8,128)(2,1)S(1)}, bf16[4,384,128]{2,1,0:T(8,128)(2,1)S(1)}, u32[]{:S(2)}, u32[]{:S(2)}) collective-permute-start(bf16[4,384,128]{2,1,0:T(8,128)(2,1)S(1)} %pad_maximum_fusion.3.x_own), channel_id=1, source_target_pairs={{0,4},{1,5},{2,6},{3,7},{4,0},{5,1},{6,2},{7,3},{8,12},{9,13},{10,... | collective-permute-start | bytes 1179656 | tf_op jit(solution)/shard_map/ppermute | solution.py:98
  27.9 3.7 %collective-permute-done.11.g1 = bf16[2,768,128]{2,1,0:T(8,128)(2,1)S(1)} collective-permute-done((bf16[2,768,128]{2,1,0:T(8,128)(2,1)S(1)}, bf16[2,768,128]{2,1,0:T(8,128)(2,1)S(1)}, u32[]{:S(2)}, u32[]{:S(2)}) %collective-permute-start.11) | collective-permute-done | bytes 393248 | tf_op jit(solution)/shard_map/ppermute | solution.py:98
  31.6 5.4 %collective-permute-start.8 = (bf16[4,384,128]{2,1,0:T(8,128)(2,1)S(1)}, bf16[4,384,128]{2,1,0:T(8,128)(2,1)S(1)}, u32[]{:S(2)}, u32[]{:S(2)}) collective-permute-start(bf16[4,384,128]{2,1,0:T(8,128)(2,1)S(1)} %pad_maximum_fusion.3.x_own), channel_id=1, source_target_pairs={{0,12},{1,13},{2,14},{3,15},{4,8},{5,9},{6,10},{7,11},{8,4},{9,5},... | collective-permute-start | bytes 1179656 | tf_op jit(solution)/shard_map/ppermute | solution.py:98
  38.5 2.4 %collective-permute-start.16 = (bf16[768,128]{1,0:T(8,128)(2,1)}, bf16[768,128]{1,0:T(8,128)(2,1)S(1)}, u32[]{:S(2)}, u32[]{:S(2)}) collective-permute-start(bf16[768,128]{1,0:T(8,128)(2,1)} %slice_bitcast_fusion.1), channel_id=1, source_target_pairs={{0,1},{1,2},{2,3},{3,0},{4,5},{5,6},{6,7},{7,4},{8,9},{9,10},{10,1... | collective-permute-start | bytes 589832 | tf_op jit(solution)/shard_map/ppermute | solution.py:98
  41.7 1.4 collective-permute-start.17
  43.1 4.3 %collective-permute-done.7.x_y = bf16[4,384,128]{2,1,0:T(8,128)(2,1)S(1)} collective-permute-done((bf16[4,384,128]{2,1,0:T(8,128)(2,1)S(1)}, bf16[4,384,128]{2,1,0:T(8,128)(2,1)S(1)}, u32[]{:S(2)}, u32[]{:S(2)}) %collective-permute-start.7) | collective-permute-done | bytes 393248 | tf_op jit(solution)/shard_map/ppermute | solution.py:98
  47.3 4.9 %lines.1 = (bf16[4,18,192,256]{3,2,1,0:T(8,128)(2,1)S(1)}, f32[27,256,512]{2,1,0:T(8,128)}) custom-call(s32[3]{0:T(128)S(1)} %pad_add_fusion.pos.refs_0_, bf16[4,384,128]{2,1,0:T(8,128)(2,1)S(1)} %pad_maximum_fusion.3.x_own, bf16[4,384,128]{2,1,0:T(8,128)(2,1)S(1)} %collective-permute-done.6.x_x, bf16[4,384,128]{2,1,0:T(8,128)(2,1)S(1)} %collective-permute-done.7.x_y, ...), custom_call_target="tpu_custom_call" | custom-call | bytes 12582912 | tf_op jit(solution)/shard_map/lines/pallas_call | solution.py:373
  53.4 3.0 %copy-done.4 = bf16[256,27,512]{2,0,1:T(8,128)(2,1)S(1)} copy-done((bf16[256,27,512]{2,0,1:T(8,128)(2,1)S(1)}, bf16[256,27,512]{2,0,1:T(8,128)(2,1)}, u32[]{:S(2)}) %copy-start.4) | copy-done | bytes 7077912
  56.4 10.1 %field.1.after = bf16[4,4,48,256]{3,2,1,0:T(8,128)(2,1)} custom-call(s32[3]{0:T(128)S(1)} %pad_add_fusion.pos.refs_0_, bf16[4,6,64,256]{3,2,1,0:T(8,128)(2,1)S(1)} %pad_maximum_fusion.mine, bf16[4,6,64,256]{3,2,1,0:T(8,128)(2,1)} %collective-permute-done.4.theirs, bf16[27,256,512]{2,1,0:T(8,128)(2,1)S(1)} %bitcast.171), custom_call_target="tpu_custom_call" | custom-call | flops 10871635968 | bytes 7077888 | tf_op jit(solution)/shard_map/field/pallas_call | solution.py:387
  67.5 6.3 %near.1.refs_2_ = f32[3,384,256]{2,1,0:T(8,128)S(1)} custom-call(s32[3]{0:T(128)S(1)} %pad_add_fusion.pos.refs_0_, bf16[4,18,192,256]{3,2,1,0:T(8,128)(2,1)S(1)} %get-tuple-element.16.xs.refs_1_, bf16[2,768,128]{2,1,0:T(8,128)(2,1)S(1)} %pad_maximum_fusion.4.g0, bf16[2,768,128]{2,1,0:T(8,128)(2,1)S(1)} %collective-permute-done.11.g1, ...), custom_call_target="tpu_custom_call" | custom-call | flops 5435817984 | bytes 10616832 | tf_op jit(solution)/shard_map/near/pallas_call | solution.py:124
  73.9 3.4 %far.1 = f32[1744,128]{1,0:T(8,128)S(1)} custom-call(s32[3]{0:T(128)S(1)} %pad_add_fusion.pos.refs_0_, bf16[4,18,192,256]{3,2,1,0:T(8,128)(2,1)S(1)} %get-tuple-element.16.xs.refs_1_, f32[3,384,256]{2,1,0:T(8,128)S(1)} %near.1.refs_2_, bf16[768,128]{1,0:T(8,128)(2,1)S(1)} %collective-permute-done.16.refs_3_, ...), custom_call_target="tpu_custom_call" | custom-call | flops 1811939328 | bytes 9936896 | tf_op jit(solution)/shard_map/far/pallas_call | solution.py:124
  77.5 3.0 %collective-permute-start.20 = (f16[1744,128]{1,0:T(8,128)(2,1)S(1)}, f16[1744,128]{1,0:T(8,128)(2,1)S(1)}, u32[]{:S(2)}, u32[]{:S(2)}) collective-permute-start(f16[1744,128]{1,0:T(8,128)(2,1)S(1)} %convert_element_type.311), channel_id=1, source_target_pairs={{0,4},{1,5},{2,6},{3,7},{4,0},{5,1},{6,2},{7,3},{8,12},{9,13},{10,... | collective-permute-start | bytes 1339400 | tf_op jit(solution)/shard_map/ppermute | solution.py:98
  80.6 2.4 %collective-permute-start.24 = (f16[1360,128]{1,0:T(8,128)(2,1)S(1)}, f16[1360,128]{1,0:T(8,128)(2,1)S(1)}, u32[]{:S(2)}, u32[]{:S(2)}) collective-permute-start(f16[1360,128]{1,0:T(8,128)(2,1)S(1)} %slice.438), channel_id=1, source_target_pairs={{0,1},{1,2},{2,3},{3,0},{4,5},{5,6},{6,7},{7,4},{8,9},{9,10},{10,1... | collective-permute-start | bytes 1044488 | tf_op jit(solution)/shard_map/ppermute | solution.py:98
  83.0 1.5 collective-permute-start.29
  84.7 8.9 %collective-permute-done.24 = f16[1360,128]{1,0:T(8,128)(2,1)S(1)} collective-permute-done((f16[1360,128]{1,0:T(8,128)(2,1)S(1)}, f16[1360,128]{1,0:T(8,128)(2,1)S(1)}, u32[]{:S(2)}, u32[]{:S(2)}) %collective-permute-start.24) | collective-permute-done | bytes 348192 | tf_op jit(solution)/shard_map/ppermute | solution.py:98
  94.1 6.7 %collective-permute-done.29 = f16[1360,128]{1,0:T(8,128)(2,1)S(1)} collective-permute-done((f16[1360,128]{1,0:T(8,128)(2,1)S(1)}, f16[1360,128]{1,0:T(8,128)(2,1)S(1)}, u32[]{:S(2)}, u32[]{:S(2)}) %collective-permute-start.29) | collective-permute-done | bytes 348192 | tf_op jit(solution)/shard_map/ppermute | solution.py:98
  100.9 2.6 %collective-permute-start.37 = (f16[704,128]{1,0:T(8,128)(2,1)S(1)}, f16[704,128]{1,0:T(8,128)(2,1)S(1)}, u32[]{:S(2)}, u32[]{:S(2)}) collective-permute-start(f16[704,128]{1,0:T(8,128)(2,1)S(1)} %slice.480), channel_id=1, source_target_pairs={{0,3},{1,0},{2,1},{3,2},{4,7},{5,4},{6,5},{7,6},{8,11},{9,8},{10,9... | collective-permute-start | bytes 540680 | tf_op jit(solution)/shard_map/ppermute | solution.py:98
  104.2 1.9 %collective-permute-start.26 = (f16[1360,128]{1,0:T(8,128)(2,1)S(1)}, f16[1360,128]{1,0:T(8,128)(2,1)S(1)}, u32[]{:S(2)}, u32[]{:S(2)}) collective-permute-start(f16[1360,128]{1,0:T(8,128)(2,1)S(1)} %collective-permute-done.24), channel_id=1, source_target_pairs={{0,8},{1,9},{2,10},{3,11},{4,12},{5,13},{6,14},{7,15},{8,0},{9,1},... | collective-permute-start | bytes 1044488 | tf_op jit(solution)/shard_map/ppermute | solution.py:98
  107.6 1.1 collective-permute-start.31
  109.4 5.2 %collective-permute-done.25 = f16[1360,128]{1,0:T(8,128)(2,1)S(1)} collective-permute-done((f16[1360,128]{1,0:T(8,128)(2,1)S(1)}, f16[1360,128]{1,0:T(8,128)(2,1)S(1)}, u32[]{:S(2)}, u32[]{:S(2)}) %collective-permute-start.25) | collective-permute-done | bytes 348192 | tf_op jit(solution)/shard_map/ppermute | solution.py:98
  114.7 1.0 collective-permute-start.23
  115.7 1.4 collective-permute-start.38
  117.1 5.0 %collective-permute-done.30 = f16[1360,128]{1,0:T(8,128)(2,1)S(1)} collective-permute-done((f16[1360,128]{1,0:T(8,128)(2,1)S(1)}, f16[1360,128]{1,0:T(8,128)(2,1)S(1)}, u32[]{:S(2)}, u32[]{:S(2)}) %collective-permute-start.30) | collective-permute-done | bytes 348192 | tf_op jit(solution)/shard_map/ppermute | solution.py:98
  122.1 1.0 collective-permute-start.39
  123.5 1.4 collective-permute-start.27
  125.1 2.8 %collective-permute-done.22 = f16[1040,128]{1,0:T(8,128)(2,1)S(1)} collective-permute-done((f16[1040,128]{1,0:T(8,128)(2,1)S(1)}, f16[1040,128]{1,0:T(8,128)(2,1)S(1)}, u32[]{:S(2)}, u32[]{:S(2)}) %collective-permute-start.22) | collective-permute-done | bytes 266272 | tf_op jit(solution)/shard_map/ppermute | solution.py:98
  127.8 1.0 collective-permute-start.28
  129.1 1.4 collective-permute-start.32
  131.0 5.9 %collective-permute-done.27 = f16[656,128]{1,0:T(8,128)(2,1)S(1)} collective-permute-done((f16[656,128]{1,0:T(8,128)(2,1)S(1)}, f16[656,128]{1,0:T(8,128)(2,1)S(1)}, u32[]{:S(2)}, u32[]{:S(2)}) %collective-permute-start.27) | collective-permute-done | bytes 167968 | tf_op jit(solution)/shard_map/ppermute | solution.py:98
  136.9 1.0 collective-permute-start.33
  138.7 1.7 %collective-permute-start.34 = (f16[1600,128]{1,0:T(8,128)(2,1)S(1)}, f16[1600,128]{1,0:T(8,128)(2,1)S(1)}, u32[]{:S(2)}, u32[]{:S(2)}) collective-permute-start(f16[1600,128]{1,0:T(8,128)(2,1)S(1)} %pad_maximum_fusion.2), channel_id=1, source_target_pairs={{0,1},{1,2},{2,3},{3,0},{4,5},{5,6},{6,7},{7,4},{8,9},{9,10},{10,1... | collective-permute-start | bytes 1228808 | tf_op jit(solution)/shard_map/ppermute | solution.py:98
  140.6 2.1 %collective-permute-start.35 = (f16[1600,128]{1,0:T(8,128)(2,1)S(1)}, f16[1600,128]{1,0:T(8,128)(2,1)S(1)}, u32[]{:S(2)}, u32[]{:S(2)}) collective-permute-start(f16[1600,128]{1,0:T(8,128)(2,1)S(1)} %pad_maximum_fusion.2), channel_id=1, source_target_pairs={{0,3},{1,0},{2,1},{3,2},{4,7},{5,4},{6,5},{7,6},{8,11},{9,8},{10,9... | collective-permute-start | bytes 1228808 | tf_op jit(solution)/shard_map/ppermute | solution.py:98
  142.8 1.2 collective-permute-start.42
  144.2 1.7 collective-permute-start.43
  146.4 1.8 %collective-permute-done.42 = f16[656,128]{1,0:T(8,128)(2,1)S(1)} collective-permute-done((f16[656,128]{1,0:T(8,128)(2,1)S(1)}, f16[656,128]{1,0:T(8,128)(2,1)S(1)}, u32[]{:S(2)}, u32[]{:S(2)}) %collective-permute-start.42) | collective-permute-done | bytes 167968 | tf_op jit(solution)/shard_map/ppermute | solution.py:98
  148.3 4.7 %collective-permute-done.34 = f16[1600,128]{1,0:T(8,128)(2,1)S(1)} collective-permute-done((f16[1600,128]{1,0:T(8,128)(2,1)S(1)}, f16[1600,128]{1,0:T(8,128)(2,1)S(1)}, u32[]{:S(2)}, u32[]{:S(2)}) %collective-permute-start.34) | collective-permute-done | bytes 409632 | tf_op jit(solution)/shard_map/ppermute | solution.py:98
  153.1 6.1 %collective-permute-done.35 = f16[1600,128]{1,0:T(8,128)(2,1)S(1)} collective-permute-done((f16[1600,128]{1,0:T(8,128)(2,1)S(1)}, f16[1600,128]{1,0:T(8,128)(2,1)S(1)}, u32[]{:S(2)}, u32[]{:S(2)}) %collective-permute-start.35) | collective-permute-done | bytes 409632 | tf_op jit(solution)/shard_map/ppermute | solution.py:98
  159.2 4.0 %collective-permute-start.41 = (f16[800,128]{1,0:T(8,128)(2,1)S(1)}, f16[800,128]{1,0:T(8,128)(2,1)S(1)}, u32[]{:S(2)}, u32[]{:S(2)}) collective-permute-start(f16[800,128]{1,0:T(8,128)(2,1)S(1)} %slice.492), channel_id=1, source_target_pairs={{0,3},{1,0},{2,1},{3,2},{4,7},{5,4},{6,5},{7,6},{8,11},{9,8},{10,9... | collective-permute-start | bytes 614408 | tf_op jit(solution)/shard_map/ppermute | solution.py:98
  164.3 2.3 %collective-permute-done.41 = f16[800,128]{1,0:T(8,128)(2,1)S(1)} collective-permute-done((f16[800,128]{1,0:T(8,128)(2,1)S(1)}, f16[800,128]{1,0:T(8,128)(2,1)S(1)}, u32[]{:S(2)}, u32[]{:S(2)}) %collective-permute-start.41) | collective-permute-done | bytes 204832 | tf_op jit(solution)/shard_map/ppermute | solution.py:98
  166.8 5.3 %copy-done.6 = f32[27,256,512]{2,1,0:T(8,128)} copy-done((f32[27,256,512]{2,1,0:T(8,128)}, f32[27,256,512]{2,1,0:T(8,128)S(1)}, u32[]{:S(2)}) %copy-start.6) | copy-done | bytes 14155800
  (189 shorter events, 18.8 us)
Async XLA Ops:
  4.1 8.4 %collective-permute-start = (bf16[416,128]{1,0:T(8,128)(2,1)S(1)}, bf16[416,128]{1,0:T(8,128)(2,1)S(1)}, u32[]{:S(2)}, u32[]{:S(2)}) collective-permute-start(bf16[416,128]{1,0:T(8,128)(2,1)S(1)} %get-tuple-element.11), channel_id=1, source_target_pairs={{0,1},{1,2},{2,3},{3,0},{4,5},{5,6},{6,7},{7,4},{8,9},{9,10},{10,1... | collective-permute-start | bytes 319496 | tf_op jit(solution)/shard_map/ppermute | solution.py:98
  7.2 11.0 %collective-permute-start.9 = (bf16[768,128]{1,0:T(8,128)(2,1)S(1)}, bf16[768,128]{1,0:T(8,128)(2,1)S(1)}, u32[]{:S(2)}, u32[]{:S(2)}) collective-permute-start(bf16[768,128]{1,0:T(8,128)(2,1)S(1)} %get-tuple-element.10.after), channel_id=1, source_target_pairs={{0,0},{1,1},{2,2},{3,3},{4,4},{5,5},{6,6},{7,7},{8,16},{9,17},{10,... | collective-permute-start | bytes 589832 | tf_op jit(solution)/shard_map/ppermute | solution.py:98
  7.8 5.5 %collective-permute-start.1 = (bf16[416,128]{1,0:T(8,128)(2,1)S(1)}, bf16[416,128]{1,0:T(8,128)(2,1)S(1)}, u32[]{:S(2)}, u32[]{:S(2)}) collective-permute-start(bf16[416,128]{1,0:T(8,128)(2,1)S(1)} %get-tuple-element.12), channel_id=1, source_target_pairs={{0,3},{1,0},{2,1},{3,2},{4,7},{5,4},{6,5},{7,6},{8,11},{9,8},{10,9... | collective-permute-start | bytes 319496 | tf_op jit(solution)/shard_map/ppermute | solution.py:98
  9.9 15.6 %collective-permute-start.5 = (bf16[384,128]{1,0:T(8,128)(2,1)S(1)}, bf16[384,128]{1,0:T(8,128)(2,1)S(1)}, u32[]{:S(2)}, u32[]{:S(2)}) collective-permute-start(bf16[384,128]{1,0:T(8,128)(2,1)S(1)} %get-tuple-element.14), channel_id=1, source_target_pairs={{0,2},{1,3},{2,0},{3,1},{4,6},{5,7},{6,4},{7,5},{8,10},{9,11},{10,... | collective-permute-start | bytes 294920 | tf_op jit(solution)/shard_map/ppermute | solution.py:98
  10.9 7.3 %collective-permute-start.10 = (bf16[768,128]{1,0:T(8,128)(2,1)S(1)}, bf16[768,128]{1,0:T(8,128)(2,1)S(1)}, u32[]{:S(2)}, u32[]{:S(2)}) collective-permute-start(bf16[768,128]{1,0:T(8,128)(2,1)S(1)} %get-tuple-element.17), channel_id=1, source_target_pairs={{0,4},{1,5},{2,6},{3,7},{4,0},{5,1},{6,2},{7,3},{8,20},{9,21},{10,... | collective-permute-start | bytes 589832 | tf_op jit(solution)/shard_map/ppermute | solution.py:98
  13.4 8.7 %collective-permute-start.2 = (bf16[4,64,256]{2,1,0:T(8,128)(2,1)S(1)}, bf16[4,64,256]{2,1,0:T(8,128)(2,1)S(1)}, u32[]{:S(2)}, u32[]{:S(2)}) collective-permute-start(bf16[4,64,256]{2,1,0:T(8,128)(2,1)S(1)} %get-tuple-element.18), channel_id=1, source_target_pairs={{0,4},{1,5},{2,6},{3,7},{4,8},{5,9},{6,10},{7,11},{8,12},{9,13},{1... | collective-permute-start | bytes 393224 | tf_op jit(solution)/shard_map/ppermute | solution.py:98
  16.9 8.5 %collective-permute-start.3 = (bf16[4,64,256]{2,1,0:T(8,128)(2,1)S(1)}, bf16[4,64,256]{2,1,0:T(8,128)(2,1)S(1)}, u32[]{:S(2)}, u32[]{:S(2)}) collective-permute-start(bf16[4,64,256]{2,1,0:T(8,128)(2,1)S(1)} %get-tuple-element.19), channel_id=1, source_target_pairs={{4,0},{5,1},{6,2},{7,3},{8,4},{9,5},{10,6},{11,7},{12,8},{13,9},{1... | collective-permute-start | bytes 393224 | tf_op jit(solution)/shard_map/ppermute | solution.py:98
  18.2 13.4 %collective-permute-start.11 = (bf16[2,768,128]{2,1,0:T(8,128)(2,1)S(1)}, bf16[2,768,128]{2,1,0:T(8,128)(2,1)S(1)}, u32[]{:S(2)}, u32[]{:S(2)}) collective-permute-start(bf16[2,768,128]{2,1,0:T(8,128)(2,1)S(1)} %pad_maximum_fusion.4.g0), channel_id=1, source_target_pairs={{0,1},{1,2},{2,3},{3,0},{4,5},{5,6},{6,7},{7,4},{8,9},{9,10},{10,1... | collective-permute-start | bytes 1179656 | tf_op jit(solution)/shard_map/ppermute | solution.py:98
  19.2 19.4 %collective-permute-start.12 = (bf16[2,768,128]{2,1,0:T(8,128)(2,1)S(1)}, bf16[2,768,128]{2,1,0:T(8,128)(2,1)S(1)}, u32[]{:S(2)}, u32[]{:S(2)}) collective-permute-start(bf16[2,768,128]{2,1,0:T(8,128)(2,1)S(1)} %pad_maximum_fusion.4.g0), channel_id=1, source_target_pairs={{0,3},{1,0},{2,1},{3,2},{4,7},{5,4},{6,5},{7,6},{8,11},{9,8},{10,9... | collective-permute-start | bytes 1179656 | tf_op jit(solution)/shard_map/ppermute | solution.py:98
  25.4 27.9 %collective-permute-start.4 = (bf16[4,6,64,256]{3,2,1,0:T(8,128)(2,1)S(1)}, bf16[4,6,64,256]{3,2,1,0:T(8,128)(2,1)}, u32[]{:S(2)}, u32[]{:S(2)}) collective-permute-start(bf16[4,6,64,256]{3,2,1,0:T(8,128)(2,1)S(1)} %pad_maximum_fusion.mine), channel_id=1, source_target_pairs={{0,16},{1,17},{2,18},{3,19},{4,20},{5,21},{6,22},{7,23},{8,24},{9,... | collective-permute-start | bytes 2359304 | tf_op jit(solution)/shard_map/ppermute | solution.py:98
  25.6 16.1 %collective-permute-start.6 = (bf16[4,384,128]{2,1,0:T(8,128)(2,1)S(1)}, bf16[4,384,128]{2,1,0:T(8,128)(2,1)S(1)}, u32[]{:S(2)}, u32[]{:S(2)}) collective-permute-start(bf16[4,384,128]{2,1,0:T(8,128)(2,1)S(1)} %pad_maximum_fusion.3.x_own), channel_id=1, source_target_pairs={{0,4},{1,5},{2,6},{3,7},{4,0},{5,1},{6,2},{7,3},{8,12},{9,13},{10,... | collective-permute-start | bytes 1179656 | tf_op jit(solution)/shard_map/ppermute | solution.py:98
  27.7 19.6 %collective-permute-start.7 = (bf16[4,384,128]{2,1,0:T(8,128)(2,1)S(1)}, bf16[4,384,128]{2,1,0:T(8,128)(2,1)S(1)}, u32[]{:S(2)}, u32[]{:S(2)}) collective-permute-start(bf16[4,384,128]{2,1,0:T(8,128)(2,1)S(1)} %pad_maximum_fusion.3.x_own), channel_id=1, source_target_pairs={{0,8},{1,9},{2,10},{3,11},{4,12},{5,13},{6,14},{7,15},{8,0},{9,1},... | collective-permute-start | bytes 1179656 | tf_op jit(solution)/shard_map/ppermute | solution.py:98
  31.6 15.7 %collective-permute-start.8 = (bf16[4,384,128]{2,1,0:T(8,128)(2,1)S(1)}, bf16[4,384,128]{2,1,0:T(8,128)(2,1)S(1)}, u32[]{:S(2)}, u32[]{:S(2)}) collective-permute-start(bf16[4,384,128]{2,1,0:T(8,128)(2,1)S(1)} %pad_maximum_fusion.3.x_own), channel_id=1, source_target_pairs={{0,12},{1,13},{2,14},{3,15},{4,8},{5,9},{6,10},{7,11},{8,4},{9,5},... | collective-permute-start | bytes 1179656 | tf_op jit(solution)/shard_map/ppermute | solution.py:98
  38.5 14.2 %collective-permute-start.16 = (bf16[768,128]{1,0:T(8,128)(2,1)}, bf16[768,128]{1,0:T(8,128)(2,1)S(1)}, u32[]{:S(2)}, u32[]{:S(2)}) collective-permute-start(bf16[768,128]{1,0:T(8,128)(2,1)} %slice_bitcast_fusion.1), channel_id=1, source_target_pairs={{0,1},{1,2},{2,3},{3,0},{4,5},{5,6},{6,7},{7,4},{8,9},{9,10},{10,1... | collective-permute-start | bytes 589832 | tf_op jit(solution)/shard_map/ppermute | solution.py:98
  41.7 11.2 %collective-permute-start.17 = (bf16[768,128]{1,0:T(8,128)(2,1)}, bf16[768,128]{1,0:T(8,128)(2,1)S(1)}, u32[]{:S(2)}, u32[]{:S(2)}) collective-permute-start(bf16[768,128]{1,0:T(8,128)(2,1)} %slice_bitcast_fusion), channel_id=1, source_target_pairs={{0,3},{1,0},{2,1},{3,2},{4,7},{5,4},{6,5},{7,6},{8,11},{9,8},{10,9... | collective-permute-start | bytes 589832 | tf_op jit(solution)/shard_map/ppermute | solution.py:98
  47.3 19.2 %collective-permute-start.13 = (bf16[2,768,128]{2,1,0:T(8,128)(2,1)S(1)}, bf16[2,768,128]{2,1,0:T(8,128)(2,1)S(1)}, u32[]{:S(2)}, u32[]{:S(2)}) collective-permute-start(bf16[2,768,128]{2,1,0:T(8,128)(2,1)S(1)} %pad_maximum_fusion.4.g0), channel_id=1, source_target_pairs={{0,16},{1,17},{2,18},{3,19},{4,20},{5,21},{6,22},{7,23},{8,24},{9,... | collective-permute-start | bytes 1179656 | tf_op jit(solution)/shard_map/ppermute | solution.py:98
  52.2 14.3 %collective-permute-start.14 = (bf16[2,768,128]{2,1,0:T(8,128)(2,1)S(1)}, bf16[2,768,128]{2,1,0:T(8,128)(2,1)S(1)}, u32[]{:S(2)}, u32[]{:S(2)}) collective-permute-start(bf16[2,768,128]{2,1,0:T(8,128)(2,1)S(1)} %collective-permute-done.11.g1), channel_id=1, source_target_pairs={{0,16},{1,17},{2,18},{3,19},{4,20},{5,21},{6,22},{7,23},{8,24},{9,... | collective-permute-start | bytes 1179656 | tf_op jit(solution)/shard_map/ppermute | solution.py:98
  52.8 13.7 %collective-permute-start.15 = (bf16[2,768,128]{2,1,0:T(8,128)(2,1)}, bf16[2,768,128]{2,1,0:T(8,128)(2,1)S(1)}, u32[]{:S(2)}, u32[]{:S(2)}) collective-permute-start(bf16[2,768,128]{2,1,0:T(8,128)(2,1)} %copy-done.2), channel_id=1, source_target_pairs={{0,16},{1,17},{2,18},{3,19},{4,20},{5,21},{6,22},{7,23},{8,24},{9,... | collective-permute-start | bytes 1179656 | tf_op jit(solution)/shard_map/ppermute | solution.py:98
  52.9 21.0 %collective-permute-start.18 = (bf16[768,128]{1,0:T(8,128)(2,1)S(1)}, bf16[768,128]{1,0:T(8,128)(2,1)S(1)}, u32[]{:S(2)}, u32[]{:S(2)}) collective-permute-start(bf16[768,128]{1,0:T(8,128)(2,1)S(1)} %collective-permute-done.16.refs_3_), channel_id=1, source_target_pairs={{0,16},{1,17},{2,18},{3,19},{4,20},{5,21},{6,22},{7,23},{8,24},{9,... | collective-permute-start | bytes 589832 | tf_op jit(solution)/shard_map/ppermute | solution.py:98
  53.3 20.6 %collective-permute-start.19 = (bf16[768,128]{1,0:T(8,128)(2,1)S(1)}, bf16[768,128]{1,0:T(8,128)(2,1)S(1)}, u32[]{:S(2)}, u32[]{:S(2)}) collective-permute-start(bf16[768,128]{1,0:T(8,128)(2,1)S(1)} %collective-permute-done.17.refs_4_), channel_id=1, source_target_pairs={{0,16},{1,17},{2,18},{3,19},{4,20},{5,21},{6,22},{7,23},{8,24},{9,... | collective-permute-start | bytes 589832 | tf_op jit(solution)/shard_map/ppermute | solution.py:98
  67.5 17.0 %slice-start = ((s8[14155776]{0:T(1024)(128)(4,1)}), s8[1572864]{0:T(1024)(128)(4,1)S(1)}, s32[]{:S(2)}) async-start(s8[14155776]{0:T(1024)(128)(4,1)} %bitcast.220), calls=%async_computation | async-start | bytes 3145728
  67.5 17.0 %slice-start.1 = ((s8[14155776]{0:T(1024)(128)(4,1)}), s8[4194304]{0:T(1024)(128)(4,1)S(1)}, s32[]{:S(2)}) async-start(s8[14155776]{0:T(1024)(128)(4,1)} %bitcast.220), calls=%async_computation.1 | async-start | bytes 8388608
  67.5 17.0 %slice-start.2 = ((s8[14155776]{0:T(1024)(128)(4,1)}), s8[4194304]{0:T(1024)(128)(4,1)S(1)}, s32[]{:S(2)}) async-start(s8[14155776]{0:T(1024)(128)(4,1)} %bitcast.220), calls=%async_computation.2 | async-start | bytes 8388608
  73.8 10.7 %slice-start.3 = ((s8[14155776]{0:T(1024)(128)(4,1)}), s8[4194304]{0:T(1024)(128)(4,1)S(1)}, s32[]{:S(2)}) async-start(s8[14155776]{0:T(1024)(128)(4,1)} %bitcast.220), calls=%async_computation.3 | async-start | bytes 8388608
  77.5 26.7 %collective-permute-start.20 = (f16[1744,128]{1,0:T(8,128)(2,1)S(1)}, f16[1744,128]{1,0:T(8,128)(2,1)S(1)}, u32[]{:S(2)}, u32[]{:S(2)}) collective-permute-start(f16[1744,128]{1,0:T(8,128)(2,1)S(1)} %convert_element_type.311), channel_id=1, source_target_pairs={{0,4},{1,5},{2,6},{3,7},{4,0},{5,1},{6,2},{7,3},{8,12},{9,13},{10,... | collective-permute-start | bytes 1339400 | tf_op jit(solution)/shard_map/ppermute | solution.py:98
  80.5 25.9 %collective-permute-start.21 = (f16[1744,128]{1,0:T(8,128)(2,1)S(1)}, f16[1744,128]{1,0:T(8,128)(2,1)S(1)}, u32[]{:S(2)}, u32[]{:S(2)}) collective-permute-start(f16[1744,128]{1,0:T(8,128)(2,1)S(1)} %convert_element_type.311), channel_id=1, source_target_pairs={{0,8},{1,9},{2,10},{3,11},{4,12},{5,13},{6,14},{7,15},{8,0},{9,1},... | collective-permute-start | bytes 1339400 | tf_op jit(solution)/shard_map/ppermute | solution.py:98
  80.6 13.0 %collective-permute-start.24 = (f16[1360,128]{1,0:T(8,128)(2,1)S(1)}, f16[1360,128]{1,0:T(8,128)(2,1)S(1)}, u32[]{:S(2)}, u32[]{:S(2)}) collective-permute-start(f16[1360,128]{1,0:T(8,128)(2,1)S(1)} %slice.438), channel_id=1, source_target_pairs={{0,1},{1,2},{2,3},{3,0},{4,5},{5,6},{6,7},{7,4},{8,9},{9,10},{10,1... | collective-permute-start | bytes 1044488 | tf_op jit(solution)/shard_map/ppermute | solution.py:98
  83.0 17.9 %collective-permute-start.29 = (f16[1360,128]{1,0:T(8,128)(2,1)S(1)}, f16[1360,128]{1,0:T(8,128)(2,1)S(1)}, u32[]{:S(2)}, u32[]{:S(2)}) collective-permute-start(f16[1360,128]{1,0:T(8,128)(2,1)S(1)} %slice.438), channel_id=1, source_target_pairs={{0,3},{1,0},{2,1},{3,2},{4,7},{5,4},{6,5},{7,6},{8,11},{9,8},{10,9... | collective-permute-start | bytes 1044488 | tf_op jit(solution)/shard_map/ppermute | solution.py:98
  93.6 14.0 %collective-permute-start.36 = (f16[656,128]{1,0:T(8,128)(2,1)S(1)}, f16[656,128]{1,0:T(8,128)(2,1)S(1)}, u32[]{:S(2)}, u32[]{:S(2)}) collective-permute-start(f16[656,128]{1,0:T(8,128)(2,1)S(1)} %slice.479), channel_id=1, source_target_pairs={{0,1},{1,2},{2,3},{3,0},{4,5},{5,6},{6,7},{7,4},{8,9},{9,10},{10,1... | collective-permute-start | bytes 503816 | tf_op jit(solution)/shard_map/ppermute | solution.py:98
  100.9 7.9 %collective-permute-start.37 = (f16[704,128]{1,0:T(8,128)(2,1)S(1)}, f16[704,128]{1,0:T(8,128)(2,1)S(1)}, u32[]{:S(2)}, u32[]{:S(2)}) collective-permute-start(f16[704,128]{1,0:T(8,128)(2,1)S(1)} %slice.480), channel_id=1, source_target_pairs={{0,3},{1,0},{2,1},{3,2},{4,7},{5,4},{6,5},{7,6},{8,11},{9,8},{10,9... | collective-permute-start | bytes 540680 | tf_op jit(solution)/shard_map/ppermute | solution.py:98
  103.5 11.2 %collective-permute-start.25 = (f16[1360,128]{1,0:T(8,128)(2,1)S(1)}, f16[1360,128]{1,0:T(8,128)(2,1)S(1)}, u32[]{:S(2)}, u32[]{:S(2)}) collective-permute-start(f16[1360,128]{1,0:T(8,128)(2,1)S(1)} %collective-permute-done.24), channel_id=1, source_target_pairs={{0,4},{1,5},{2,6},{3,7},{4,0},{5,1},{6,2},{7,3},{8,12},{9,13},{10,... | collective-permute-start | bytes 1044488 | tf_op jit(solution)/shard_map/ppermute | solution.py:98
  104.2 11.5 %collective-permute-start.26 = (f16[1360,128]{1,0:T(8,128)(2,1)S(1)}, f16[1360,128]{1,0:T(8,128)(2,1)S(1)}, u32[]{:S(2)}, u32[]{:S(2)}) collective-permute-start(f16[1360,128]{1,0:T(8,128)(2,1)S(1)} %collective-permute-done.24), channel_id=1, source_target_pairs={{0,8},{1,9},{2,10},{3,11},{4,12},{5,13},{6,14},{7,15},{8,0},{9,1},... | collective-permute-start | bytes 1044488 | tf_op jit(solution)/shard_map/ppermute | solution.py:98
  106.4 15.7 %collective-permute-start.30 = (f16[1360,128]{1,0:T(8,128)(2,1)S(1)}, f16[1360,128]{1,0:T(8,128)(2,1)S(1)}, u32[]{:S(2)}, u32[]{:S(2)}) collective-permute-start(f16[1360,128]{1,0:T(8,128)(2,1)S(1)} %collective-permute-done.29), channel_id=1, source_target_pairs={{0,4},{1,5},{2,6},{3,7},{4,0},{5,1},{6,2},{7,3},{8,12},{9,13},{10,... | collective-permute-start | bytes 1044488 | tf_op jit(solution)/shard_map/ppermute | solution.py:98
  107.6 15.9 %collective-permute-start.31 = (f16[1360,128]{1,0:T(8,128)(2,1)S(1)}, f16[1360,128]{1,0:T(8,128)(2,1)S(1)}, u32[]{:S(2)}, u32[]{:S(2)}) collective-permute-start(f16[1360,128]{1,0:T(8,128)(2,1)S(1)} %collective-permute-done.29), channel_id=1, source_target_pairs={{0,8},{1,9},{2,10},{3,11},{4,12},{5,13},{6,14},{7,15},{8,0},{9,1},... | collective-permute-start | bytes 1044488 | tf_op jit(solution)/shard_map/ppermute | solution.py:98
  108.8 19.1 %collective-permute-start.22 = (f16[1040,128]{1,0:T(8,128)(2,1)S(1)}, f16[1040,128]{1,0:T(8,128)(2,1)S(1)}, u32[]{:S(2)}, u32[]{:S(2)}) collective-permute-start(f16[1040,128]{1,0:T(8,128)(2,1)S(1)} %slice.433), channel_id=1, source_target_pairs={{0,4},{1,5},{2,6},{3,7},{4,0},{5,1},{6,2},{7,3},{8,12},{9,13},{10,... | collective-permute-start | bytes 798728 | tf_op jit(solution)/shard_map/ppermute | solution.py:98
  114.7 14.4 %collective-permute-start.23 = (f16[704,128]{1,0:T(8,128)(2,1)S(1)}, f16[704,128]{1,0:T(8,128)(2,1)S(1)}, u32[]{:S(2)}, u32[]{:S(2)}) collective-permute-start(f16[704,128]{1,0:T(8,128)(2,1)S(1)} %slice.437), channel_id=1, source_target_pairs={{0,8},{1,9},{2,10},{3,11},{4,12},{5,13},{6,14},{7,15},{8,0},{9,1},... | collective-permute-start | bytes 540680 | tf_op jit(solution)/shard_map/ppermute | solution.py:98
  115.7 27.0 %collective-permute-start.38 = (f16[1360,128]{1,0:T(8,128)(2,1)S(1)}, f16[1360,128]{1,0:T(8,128)(2,1)S(1)}, u32[]{:S(2)}, u32[]{:S(2)}) collective-permute-start(f16[1360,128]{1,0:T(8,128)(2,1)S(1)} %constant_dynamic-update-slice_fusion), channel_id=1, source_target_pairs={{0,4},{1,5},{2,6},{3,7},{4,0},{5,1},{6,2},{7,3},{8,12},{9,13},{10,... | collective-permute-start | bytes 1044488 | tf_op jit(solution)/shard_map/ppermute | solution.py:98
  122.1 18.4 %collective-permute-start.39 = (f16[1360,128]{1,0:T(8,128)(2,1)S(1)}, f16[1360,128]{1,0:T(8,128)(2,1)S(1)}, u32[]{:S(2)}, u32[]{:S(2)}) collective-permute-start(f16[1360,128]{1,0:T(8,128)(2,1)S(1)} %constant_dynamic-update-slice_fusion), channel_id=1, source_target_pairs={{0,8},{1,9},{2,10},{3,11},{4,12},{5,13},{6,14},{7,15},{8,0},{9,1},... | collective-permute-start | bytes 1044488 | tf_op jit(solution)/shard_map/ppermute | solution.py:98
  123.5 13.4 %collective-permute-start.27 = (f16[656,128]{1,0:T(8,128)(2,1)S(1)}, f16[656,128]{1,0:T(8,128)(2,1)S(1)}, u32[]{:S(2)}, u32[]{:S(2)}) collective-permute-start(f16[656,128]{1,0:T(8,128)(2,1)S(1)} %slice.445), channel_id=1, source_target_pairs={{0,4},{1,5},{2,6},{3,7},{4,0},{5,1},{6,2},{7,3},{8,12},{9,13},{10,... | collective-permute-start | bytes 503816 | tf_op jit(solution)/shard_map/ppermute | solution.py:98
  127.8 16.4 %collective-permute-start.28 = (f16[704,128]{1,0:T(8,128)(2,1)S(1)}, f16[704,128]{1,0:T(8,128)(2,1)S(1)}, u32[]{:S(2)}, u32[]{:S(2)}) collective-permute-start(f16[704,128]{1,0:T(8,128)(2,1)S(1)} %slice.448), channel_id=1, source_target_pairs={{0,8},{1,9},{2,10},{3,11},{4,12},{5,13},{6,14},{7,15},{8,0},{9,1},... | collective-permute-start | bytes 540680 | tf_op jit(solution)/shard_map/ppermute | solution.py:98
  129.1 9.6 %collective-permute-start.32 = (f16[656,128]{1,0:T(8,128)(2,1)S(1)}, f16[656,128]{1,0:T(8,128)(2,1)S(1)}, u32[]{:S(2)}, u32[]{:S(2)}) collective-permute-start(f16[656,128]{1,0:T(8,128)(2,1)S(1)} %slice.455), channel_id=1, source_target_pairs={{0,4},{1,5},{2,6},{3,7},{4,0},{5,1},{6,2},{7,3},{8,12},{9,13},{10,... | collective-permute-start | bytes 503816 | tf_op jit(solution)/shard_map/ppermute | solution.py:98
  136.9 9.5 %collective-permute-start.33 = (f16[704,128]{1,0:T(8,128)(2,1)S(1)}, f16[704,128]{1,0:T(8,128)(2,1)S(1)}, u32[]{:S(2)}, u32[]{:S(2)}) collective-permute-start(f16[704,128]{1,0:T(8,128)(2,1)S(1)} %slice.458), channel_id=1, source_target_pairs={{0,8},{1,9},{2,10},{3,11},{4,12},{5,13},{6,14},{7,15},{8,0},{9,1},... | collective-permute-start | bytes 540680 | tf_op jit(solution)/shard_map/ppermute | solution.py:98
  138.7 14.3 %collective-permute-start.34 = (f16[1600,128]{1,0:T(8,128)(2,1)S(1)}, f16[1600,128]{1,0:T(8,128)(2,1)S(1)}, u32[]{:S(2)}, u32[]{:S(2)}) collective-permute-start(f16[1600,128]{1,0:T(8,128)(2,1)S(1)} %pad_maximum_fusion.2), channel_id=1, source_target_pairs={{0,1},{1,2},{2,3},{3,0},{4,5},{5,6},{6,7},{7,4},{8,9},{9,10},{10,1... | collective-permute-start | bytes 1228808 | tf_op jit(solution)/shard_map/ppermute | solution.py:98
  140.6 18.6 %collective-permute-start.35 = (f16[1600,128]{1,0:T(8,128)(2,1)S(1)}, f16[1600,128]{1,0:T(8,128)(2,1)S(1)}, u32[]{:S(2)}, u32[]{:S(2)}) collective-permute-start(f16[1600,128]{1,0:T(8,128)(2,1)S(1)} %pad_maximum_fusion.2), channel_id=1, source_target_pairs={{0,3},{1,0},{2,1},{3,2},{4,7},{5,4},{6,5},{7,6},{8,11},{9,8},{10,9... | collective-permute-start | bytes 1228808 | tf_op jit(solution)/shard_map/ppermute | solution.py:98
  142.8 5.4 %collective-permute-start.42 = (f16[656,128]{1,0:T(8,128)(2,1)S(1)}, f16[656,128]{1,0:T(8,128)(2,1)S(1)}, u32[]{:S(2)}, u32[]{:S(2)}) collective-permute-start(f16[656,128]{1,0:T(8,128)(2,1)S(1)} %slice.497), channel_id=1, source_target_pairs={{0,4},{1,5},{2,6},{3,7},{4,0},{5,1},{6,2},{7,3},{8,12},{9,13},{10,... | collective-permute-start | bytes 503816 | tf_op jit(solution)/shard_map/ppermute | solution.py:98
  144.2 22.5 %collective-permute-start.43 = (f16[704,128]{1,0:T(8,128)(2,1)S(1)}, f16[704,128]{1,0:T(8,128)(2,1)S(1)}, u32[]{:S(2)}, u32[]{:S(2)}) collective-permute-start(f16[704,128]{1,0:T(8,128)(2,1)S(1)} %slice.500), channel_id=1, source_target_pairs={{0,8},{1,9},{2,10},{3,11},{4,12},{5,13},{6,14},{7,15},{8,0},{9,1},... | collective-permute-start | bytes 540680 | tf_op jit(solution)/shard_map/ppermute | solution.py:98
  153.0 11.1 %collective-permute-start.40 = (f16[800,128]{1,0:T(8,128)(2,1)S(1)}, f16[800,128]{1,0:T(8,128)(2,1)S(1)}, u32[]{:S(2)}, u32[]{:S(2)}) collective-permute-start(f16[800,128]{1,0:T(8,128)(2,1)S(1)} %slice.487), channel_id=1, source_target_pairs={{0,1},{1,2},{2,3},{3,0},{4,5},{5,6},{6,7},{7,4},{8,9},{9,10},{10,1... | collective-permute-start | bytes 614408 | tf_op jit(solution)/shard_map/ppermute | solution.py:98
  159.2 7.3 %collective-permute-start.41 = (f16[800,128]{1,0:T(8,128)(2,1)S(1)}, f16[800,128]{1,0:T(8,128)(2,1)S(1)}, u32[]{:S(2)}, u32[]{:S(2)}) collective-permute-start(f16[800,128]{1,0:T(8,128)(2,1)S(1)} %slice.492), channel_id=1, source_target_pairs={{0,3},{1,0},{2,1},{3,2},{4,7},{5,4},{6,5},{7,6},{8,11},{9,8},{10,9... | collective-permute-start | bytes 614408 | tf_op jit(solution)/shard_map/ppermute | solution.py:98
  (7 other events, 24.6 us)

commit v3 on v2

--- a/solution.py
+++ b/solution.py
@@ -162,6 +162,23 @@
         out[many + levels * height :, :] = rim[:, wide:]
 
 
+def rims_kernel(pos, g, from_west, from_east, after1, after2, broad, low, high):
+    del after1, after2
+    levels, height, width, chans = g.shape
+    many = from_west.shape[0] - 2 * levels * height
+    wide = chans // 2
+    broad[:, :, 0:width, :] = g[...]
+    for message, at in ((from_west, width), (from_east, width + 8)):
+        for half in range(2):
+            first = many + half * levels * height
+            rim = message[first : first + levels * height, :].reshape(levels, height, 1, wide)
+            broad[:, :, at : at + 8, half * wide : (half + 1) * wide] = jnp.broadcast_to(
+                rim, (levels, height, 8, wide)
+            )
+    low[...] = broad[:, 0]
+    high[...] = broad[:, height - 1]
+
+
 def lines_kernel(pos, x_own, x_x, x_y, x_d, xs, blank):
     del blank
     lat = pos[1]
@@ -222,8 +239,7 @@
             acc[lat_by, to : to + many, :] = total
 
 
-def near_kernel(pos, xs, g0, g1, g3, s0, s1, s3, after, acc, gt):
-    del after
+def near_kernel(pos, xs, g0, g1, g3, s0, s1, s3, acc, gt):
     levels = xs.shape[0]
     right = lax.rem(pos[1], 2)
     for core, parts in ((pos[0], (g0, g3, g1)), (1 - pos[0], (s0, s3, s1))):
@@ -233,7 +249,8 @@
     add_taps(acc, gt, xs, (0, 1, 3))
 
 
-def far_kernel(pos, xs, part, g2a, g2b, s2a, s2b, out, gt, acc, *, early):
+def far_kernel(pos, xs, part, g2a, g2b, s2a, s2b, after, out, gt, acc):
+    del after
     levels, rows, circle, lanes = xs.shape
     span = lanes // 4
     filters = out.shape[1]
@@ -245,27 +262,23 @@
     add_taps(acc, gt, xs, (2,))
     scale = 1.0 / math.sqrt(levels * (rows - 2) * circle)
 
-    def place(tap):
-        return tap * span + (16 if tap >= early else 0)
-
     most = jnp.zeros((span, filters), jnp.float32)
     for lat_by in range(3):
         for lev_at in range(3):
             block = acc[lat_by, lev_at * filters : (lev_at + 1) * filters, :].T * scale
             for lon_at in range(3):
-                at = place((2 - lev_at) * 9 + lat_by * 3 + lon_at)
+                at = ((2 - lev_at) * 9 + lat_by * 3 + lon_at) * span
                 value = block[lon_at * span : (lon_at + 1) * span]
                 out[at : at + span, :] = value
                 most = jnp.maximum(most, jnp.abs(value))
     top = jnp.maximum(jnp.max(most, axis=(0, 1), keepdims=True), 1e-30)
     power = jnp.broadcast_to(jnp.ceil(jnp.log(top) * (1.0 / math.log(2.0))), (16, filters))
-    factor = jnp.exp2(14.0 - power[0:1])
-    out[0 : early * span, :] = out[0 : early * span, :] * factor
-    out[early * span + 16 :, :] = out[early * span + 16 :, :] * factor
-    out[early * span : early * span + 16, :] = power
-
-
-def field_kernel(pos, mine, theirs, w, out, copies, acc):
+    out[27 * span :, :] = power
+    out[0 : 27 * span, :] = out[0 : 27 * span, :] * jnp.exp2(14.0 - power[0:1])
+
+
+def field_kernel(pos, after, mine, theirs, w, out, copies, acc):
+    del after
     step = pl.program_id(0)
     levels, height, width, chans = out.shape
     many = mine.shape[-1]
@@ -347,17 +360,6 @@
     g1 = move(g0, lon_by(1))
     g3 = move(g0, lon_by(-1))
 
-    def column(message):
-        rim = message[many:].reshape(2, edge, span * 2)
-        rim = jnp.concatenate([rim[0], rim[1]], axis=-1).reshape(levels, height, 1, chans)
-        return jnp.broadcast_to(rim, (levels, height, 8, chans))
-
-    broad = jnp.concatenate([g_cells, column(x_r1), column(x_r3)], axis=2)
-    from_lo = move(broad[:, height - 1], north)
-    from_hi = move(broad[:, 0], south)
-    mine = jnp.concatenate([from_lo[:, None], broad, from_hi[:, None]], axis=1)
-    theirs = move(mine, sibling)
-
     s0 = move(g0, sibling)
     x_own = jnp.stack([x0, x_r1[:many], x_r2, x_r3[:many]])
     x_x = move(x_own, lat_xor(1))
@@ -369,6 +371,22 @@
     s3 = move(g3, sibling)
     s2a = move(g2a, sibling)
     s2b = move(g2b, sibling)
+
+    strip = jax.ShapeDtypeStruct((levels, width + 16, chans), bf16)
+    broad, low, high = call(
+        rims_kernel,
+        [jax.ShapeDtypeStruct((levels, height, width + 16, chans), bf16), strip, strip],
+        (pos, g_cells, x_r1, x_r3, x_x, x_d),
+        [],
+        0,
+        "rims",
+        16,
+        held=2,
+    )
+    from_lo = move(high, north)
+    from_hi = move(low, south)
+    mine = jnp.concatenate([from_lo[:, None], broad, from_hi[:, None]], axis=1)
+    theirs = move(mine, sibling)
 
     xs, total = pl.pallas_call(
         lines_kernel,
@@ -383,6 +401,51 @@
         name="lines",
     )(pos, x_own, x_x, x_y, x_d)
 
+    work = 2 * 27 * span * wide * rows * circle * levels
+    (part,) = call(
+        near_kernel,
+        [jax.ShapeDtypeStruct((3, 3 * wide, 4 * span), f32)],
+        (pos, xs, g0, g1, g3, s0, s1, s3),
+        [VMEM((levels * wide, 3 * rows * width), bf16)],
+        work,
+        "near",
+        28,
+    )
+    (grads,) = call(
+        far_kernel,
+        [jax.ShapeDtypeStruct((27 * span + 16, wide), f32)],
+        (pos, xs, part, g2a, g2b, s2a, s2b, theirs),
+        [VMEM((levels * wide, rows * width), bf16), VMEM((3, 3 * wide, 4 * span), f32)],
+        work // 3,
+        "far",
+        28,
+        held=1,
+    )
+    own = grads.astype(jnp.float16)
+
+    early = 7
+    cut, end = early * span, 27 * span
+    size = own.shape[0] - cut
+    half = size // 32 * 16
+    step_rows = cut + 16
+
+    def to_plane(share):
+        return [move(share, lat_xor(tag)) for tag in (1, 2, 3)]
+
+    late = own[cut:]
+    from_3 = move(late, lon_by(1))
+    from_1 = move(late, lon_by(-1))
+    plane = [own] + to_plane(own)
+    block = [x for p in plane for x in (p[:cut], p[end:])]
+    both = to_plane(jnp.concatenate([from_3, from_1]))
+    by_3 = move(jnp.concatenate([from_3[:half]] + block), lon_by(1))
+    by_1 = move(jnp.concatenate([from_1[half:]] + block), lon_by(-1))
+    from_2 = jnp.concatenate([by_3[:half], by_1[: size - half]])
+    across = to_plane(from_2)
+    early_3, early_1 = by_3[half:], by_1[size - half :]
+    early_2a = move(early_3[: 2 * step_rows], lon_by(1))
+    early_2b = move(early_1[2 * step_rows :], lon_by(-1))
+
     whole = lambda t: (0, 0, 0, 0)
     field = pl.pallas_call(
         field_kernel,
@@ -390,6 +453,7 @@
         grid=(9,),
         in_specs=[
             pl.BlockSpec(memory_space=SMEM),
+            pl.BlockSpec(memory_space=pl.ANY),
             pl.BlockSpec(mine.shape, whole),
             pl.BlockSpec(mine.shape, whole),
             pl.BlockSpec((3, chans, filters), lambda t: (t, 0, 0)),
@@ -402,105 +466,39 @@
         cost_estimate=pl.CostEstimate(
             flops=4 * 27 * chans * filters * cells, bytes_accessed=27 * chans * filters * 2, transcendentals=0
         ),
-        compiler_params=pltpu.CompilerParams(vmem_limit_bytes=32 * 1024 * 1024),
+        compiler_params=pltpu.CompilerParams(vmem_limit_bytes=56 * 1024 * 1024),
         name="field",
-    )(pos, mine, theirs, taps)
-
-    work = 2 * 27 * span * wide * rows * circle * levels
-    (part,) = call(
-        near_kernel,
-        [jax.ShapeDtypeStruct((3, 3 * wide, 4 * span), f32)],
-        (pos, xs, g0, g1, g3, s0, s1, s3, field),
-        [VMEM((levels * wide, 3 * rows * width), bf16)],
-        work,
-        "near",
-        28,
-        held=1,
-    )
-    early = 6
-    (grads,) = call(
-        lambda *refs: far_kernel(*refs, early=early),
-        [jax.ShapeDtypeStruct((27 * span + 16, wide), f32)],
-        (pos, xs, part, g2a, g2b, s2a, s2b),
-        [VMEM((levels * wide, rows * width), bf16), VMEM((3, 3 * wide, 4 * span), f32)],
-        work // 3,
-        "far",
-        28,
-    )
-    own = grads.astype(jnp.float16)
-
-    front, back = early * span + 16, early * span
-    middle = 16 + 10 * span
-
-    def put(total, piece, power, first, last, lat_from, lon_from):
-        factor = jnp.exp2(power.astype(f32) - 14.0)
+    )(pos, grads, mine, theirs, taps)
+
+    def put(total, piece, power, first, last, tag, step):
+        factor = jnp.exp2(power[0:1].astype(f32) - 14.0)
         value = piece.reshape(last - first, span, wide).astype(f32) * factor[None]
-        return lax.dynamic_update_slice(total, value, (first, lon_from * span, lat_from * wide))
-
-    def put_late(total, piece, lat_from, lon_from):
-        return put(total, piece[16:], piece[0:1], early, 27, lat_from, lon_from)
-
-    def put_split(total, top, bottom, lat_from, lon_from):
-        total = put(total, top[16:], top[0:1], early, early + 10, lat_from, lon_from)
-        return put(total, bottom, top[0:1], early + 10, 27, lat_from, lon_from)
-
-    def put_whole(total, piece, lat_from, lon_from):
-        total = put(total, piece[:back], piece[back : back + 1], 0, early, lat_from, lon_from)
-        return put_late(total, piece[back:], lat_from, lon_from)
-
-    late = own[back:]
-    from_1 = move(late, lon_by(1))
-    from_3 = move(late, lon_by(-1))
-    by_x = move(own, lat_xor(1))
-    by_y = move(own, lat_xor(2))
-    cut = back + middle
-    top = move(by_y[:cut], lat_xor(1))
-    bottom = move(by_x[cut:], lat_xor(2))
-    opp_top = move(from_1[:middle], lon_by(1))
-    opp_bottom = move(from_3[middle:], lon_by(-1))
-
-    def exchange(share):
-        to_x = move(share, lat_xor(1))
-        to_y = move(share, lat_xor(2))
-        return to_x, to_y, move(to_y[:middle], lat_xor(1)), move(to_x[middle:], lat_xor(2))
-
-    block = jnp.concatenate([own[:front], by_x[:front], by_y[:front], top[:front]])
-    near_1 = exchange(from_1)
-    near_3 = exchange(from_3)
-    early_1 = move(block, lon_by(1))
-    early_3 = move(block, lon_by(-1))
-    from_2 = jnp.concatenate([opp_top, opp_bottom])
-    across = exchange(from_2)
-    early_2a = move(early_1[: 2 * front], lon_by(1))
-    early_2b = move(early_3[2 * front :], lon_by(-1))
-
-    total = put_whole(total, own, lat, lon)
-    total = put_whole(total, by_x, lat ^ 1, lon)
-    total = put_whole(total, by_y, lat ^ 2, lon)
-    total = put(total, top[:back], top[back : back + 1], 0, early, lat ^ 3, lon)
-    total = put_split(total, top[back:], bottom, lat ^ 3, lon)
-
-    def put_early(total, pieces, tags, lon_from):
+        at = (first, lax.rem(lon + step, 4) * span, (lat ^ tag) * wide)
+        return lax.dynamic_update_slice(total, value, at)
+
+    def put_late(total, piece, tag, step):
+        return put(total, piece[: end - cut], piece[end - cut :], early, 27, tag, step)
+
+    def put_early(total, pieces, tags, step):
         for at, tag in enumerate(tags):
-            piece = pieces[at * front : (at + 1) * front]
-            total = put(total, piece[:back], piece[back : back + 1], 0, early, lat ^ tag, lon_from)
+            piece = pieces[at * step_rows : (at + 1) * step_rows]
+            total = put(total, piece[:cut], piece[cut:], 0, early, tag, step)
         return total
 
-    for share, (to_x, to_y, upper, lower), step in ((from_1, near_1, 3), (from_3, near_3, 1)):
-        there = lax.rem(lon + step, 4)
-        total = put_late(total, share, lat, there)
-        total = put_late(total, to_x, lat ^ 1, there)
-        total = put_late(total, to_y, lat ^ 2, there)
-        total = put_split(total, upper, lower, lat ^ 3, there)
-    there = lax.rem(lon + 2, 4)
-    total = put_early(total, early_1, (0, 1, 2, 3), lax.rem(lon + 3, 4))
-    total = put_early(total, early_3, (0, 1, 2, 3), lax.rem(lon + 1, 4))
-    total = put_late(total, from_2, lat, there)
-    total = put_late(total, across[0], lat ^ 1, there)
-    total = put_late(total, across[1], lat ^ 2, there)
-    total = put_early(total, early_2a, (0, 1), there)
-    total = put_early(total, early_2b, (2, 3), there)
-    total = put_split(total, across[2], across[3], lat ^ 3, there)
+    for tag, piece in enumerate(plane):
+        total = put(total, piece[:end], piece[end:], 0, 27, tag, 0)
+    total = put_late(total, from_3, 0, 3)
+    total = put_late(total, from_1, 0, 1)
+    for tag, piece in enumerate(both):
+        total = put_late(total, piece[:size], tag + 1, 3)
+        total = put_late(total, piece[size:], tag + 1, 1)
+    total = put_early(total, early_3, (0, 1, 2, 3), 3)
+    total = put_early(total, early_1, (0, 1, 2, 3), 1)
+    total = put_late(total, from_2, 0, 2)
+    total = put_early(total, early_2a, (0, 1), 2)
+    total = put_early(total, early_2b, (2, 3), 2)
+    for tag, piece in enumerate(across):
+        total = put_late(total, piece, tag + 1, 2)
     return (jnp.transpose(field, (3, 0, 1, 2)), jnp.transpose(total, (1, 0, 2)))
 
 

time: 172 us -> 154 us (0.90)
  waiting for transfers between devices: 63 us -> 39.4 us
  other arithmetic: 2.81 us -> 24.8 us
  starting transfers between devices: 63.7 us -> 51 us
  local copies, waits for them, and re-layouts: 14.8 us -> 8.23 us
  Pallas kernels: 26.1 us -> 29.2 us
    ppermute x44 -> x35, waiting for transfers between devices: 63 us -> 39.4 us  [move(): return lax.ppermute(x, AXES, pairs)]
    dynamic_update_slice x36 -> x28, other arithmetic: 2.13 us -> 23.3 us  [put(): return lax.dynamic_update_slice(total, value, at)]
    ppermute x44 -> x35, starting transfers between devices: 63.7 us -> 51 us  [move(): return lax.ppermute(x, AXES, pairs)]
    unnamed x24, local copies, waits for them, and re-layouts: 11.4 us -> 4.19 us
    pallas_call x1, Pallas kernels: 10.1 us -> 11.9 us  [blocked_body(): pl.pallas_call(field_kernel, out_shape=jax.ShapeDtypeStruct((levels, heig...]
    pallas_call x4 -> x5, Pallas kernels: 11.1 us -> 12.4 us  [call(): pl.pallas_call(kernel, out_shape=outs, in_specs=[pl.BlockSpec(memory_spac...]
  transfers between devices with their start and end apart: 44 -> 35, of which waited for: 16 -> 12; matrix products, arithmetic and copies ran while one was open for 4% -> 18% of each run, Pallas kernels for 12% -> 16%
where the time goes in v3:
time: 154 us
  starting transfers between devices  51 us (33%)
  waiting for transfers between devices  39.4 us (26%)
  Pallas kernels  29.2 us (19%)
  other arithmetic  24.8 us (16%)
  local copies, waits for them, and re-layouts  8.23 us (5%)
    ppermute x35, starting transfers between devices, move(): return lax.ppermute(x, AXES, pairs)  51 us
    ppermute x35, waiting for transfers between devices, move(): return lax.ppermute(x, AXES, pairs)  39.4 us
    dynamic_update_slice x28, other arithmetic, put(): return lax.dynamic_update_slice(total, value, at)  23.3 us
    pallas_call x5, Pallas kernels, call(): pl.pallas_call(kernel, out_shape=outs, in_specs=[pl.BlockSpec(memory_spac...  12.4 us
    pallas_call x1, Pallas kernels, blocked_body(): pl.pallas_call(field_kernel, out_shape=jax.ShapeDtypeStruct((levels, heig...  11.9 us
    pallas_call x1, Pallas kernels, blocked_body(): pl.pallas_call(lines_kernel, out_shape=[jax.ShapeDtypeStruct((levels, row...  4.86 us
    unnamed x24, local copies, waits for them, and re-layouts  4.19 us
  transfers between devices with their start and end apart: 35, of which 12 were waited for; matrix products, arithmetic and copies ran while one was open for 18% of the time, Pallas kernels for 16%

profile of v3, /device:TPU:0, one launch (start us, length us, event | category | flops | bytes accessed | tf_op | source)
XLA Modules:
  0.0 153.7 jit_solution(2845948923479550281)
XLA Ops:
  0.7 1.0 copy-done.1
  2.3 1.0 copy-done.3
  4.1 5.1 %collective-permute-start.2 = (bf16[416,128]{1,0:T(8,128)(2,1)S(1)}, bf16[416,128]{1,0:T(8,128)(2,1)S(1)}, u32[]{:S(2)}, u32[]{:S(2)}) collective-permute-start(bf16[416,128]{1,0:T(8,128)(2,1)S(1)} %get-tuple-element.17), channel_id=1, source_target_pairs={{0,3},{1,0},{2,1},{3,2},{4,7},{5,4},{6,5},{7,6},{8,11},{9,8},{10,9... | collective-permute-start | bytes 319496 | tf_op jit(solution)/shard_map/ppermute | solution.py:98
  9.9 1.0 collective-permute-start
  10.9 1.5 collective-permute-start.7
  12.5 4.1 %collective-permute-done.from_west = bf16[416,128]{1,0:T(8,128)(2,1)S(1)} collective-permute-done((bf16[416,128]{1,0:T(8,128)(2,1)S(1)}, bf16[416,128]{1,0:T(8,128)(2,1)S(1)}, u32[]{:S(2)}, u32[]{:S(2)}) %collective-permute-start) | collective-permute-done | bytes 106528 | tf_op jit(solution)/shard_map/ppermute | solution.py:98
  16.5 2.9 %collective-permute-done.1 = bf16[384,128]{1,0:T(8,128)(2,1)S(1)} collective-permute-done((bf16[384,128]{1,0:T(8,128)(2,1)S(1)}, bf16[384,128]{1,0:T(8,128)(2,1)S(1)}, u32[]{:S(2)}, u32[]{:S(2)}) %collective-permute-start.1) | collective-permute-done | bytes 98336 | tf_op jit(solution)/shard_map/ppermute | solution.py:98
  19.5 1.6 %collective-permute-start.3 = (bf16[4,384,128]{2,1,0:T(8,128)(2,1)S(1)}, bf16[4,384,128]{2,1,0:T(8,128)(2,1)S(1)}, u32[]{:S(2)}, u32[]{:S(2)}) collective-permute-start(bf16[4,384,128]{2,1,0:T(8,128)(2,1)S(1)} %pad_maximum_fusion.1.x_own), channel_id=1, source_target_pairs={{0,4},{1,5},{2,6},{3,7},{4,0},{5,1},{6,2},{7,3},{8,12},{9,13},{10,... | collective-permute-start | bytes 1179656 | tf_op jit(solution)/shard_map/ppermute | solution.py:98
  22.6 3.0 %collective-permute-start.9 = (bf16[2,768,128]{2,1,0:T(8,128)(2,1)S(1)}, bf16[2,768,128]{2,1,0:T(8,128)(2,1)}, u32[]{:S(2)}, u32[]{:S(2)}) collective-permute-start(bf16[2,768,128]{2,1,0:T(8,128)(2,1)S(1)} %pad_maximum_fusion.2.g0), channel_id=1, source_target_pairs={{0,3},{1,0},{2,1},{3,2},{4,7},{5,4},{6,5},{7,6},{8,11},{9,8},{10,9... | collective-permute-start | bytes 1179656 | tf_op jit(solution)/shard_map/ppermute | solution.py:98
  25.6 1.4 collective-permute-start.4
  27.0 4.5 %collective-permute-done.3.x_x.after1 = bf16[4,384,128]{2,1,0:T(8,128)(2,1)S(1)} collective-permute-done((bf16[4,384,128]{2,1,0:T(8,128)(2,1)S(1)}, bf16[4,384,128]{2,1,0:T(8,128)(2,1)S(1)}, u32[]{:S(2)}, u32[]{:S(2)}) %collective-permute-start.3) | collective-permute-done | bytes 393248 | tf_op jit(solution)/shard_map/ppermute | solution.py:98
  31.5 7.3 %collective-permute-done.5.x_d.after2 = bf16[4,384,128]{2,1,0:T(8,128)(2,1)S(1)} collective-permute-done((bf16[4,384,128]{2,1,0:T(8,128)(2,1)S(1)}, bf16[4,384,128]{2,1,0:T(8,128)(2,1)S(1)}, u32[]{:S(2)}, u32[]{:S(2)}) %collective-permute-start.5) | collective-permute-done | bytes 393248 | tf_op jit(solution)/shard_map/ppermute | solution.py:98
  39.5 1.3 collective-permute-start.18
  40.8 4.6 %collective-permute-start.17 = (bf16[4,64,256]{2,1,0:T(8,128)(2,1)S(1)}, bf16[4,64,256]{2,1,0:T(8,128)(2,1)S(1)}, u32[]{:S(2)}, u32[]{:S(2)}) collective-permute-start(bf16[4,64,256]{2,1,0:T(8,128)(2,1)S(1)} %get-tuple-element.20), channel_id=1, source_target_pairs={{0,4},{1,5},{2,6},{3,7},{4,8},{5,9},{6,10},{7,11},{8,12},{9,13},{1... | collective-permute-start | bytes 393224 | tf_op jit(solution)/shard_map/ppermute | solution.py:98
  46.6 1.3 collective-permute-done.17
  47.9 1.0 pad_maximum_fusion.mine
  48.9 1.6 %slice_bitcast_fusion = bf16[768,128]{1,0:T(8,128)(2,1)} fusion(bf16[2,768,128]{2,1,0:T(8,128)(2,1)} %collective-permute-done.9.g3), kind=kLoop, calls=%fused_computation.63 | loop fusion | bytes 393216 | tf_op jit(solution)/shard_map/squeeze | solution.py:369
  50.5 1.2 collective-permute-start.13
  52.4 2.7 %collective-permute-start.14 = (bf16[768,128]{1,0:T(8,128)(2,1)}, bf16[768,128]{1,0:T(8,128)(2,1)S(1)}, u32[]{:S(2)}, u32[]{:S(2)}) collective-permute-start(bf16[768,128]{1,0:T(8,128)(2,1)} %slice_bitcast_fusion), channel_id=1, source_target_pairs={{0,3},{1,0},{2,1},{3,2},{4,7},{5,4},{6,5},{7,6},{8,11},{9,8},{10,9... | collective-permute-start | bytes 589832 | tf_op jit(solution)/shard_map/ppermute | solution.py:98
  55.1 4.9 %lines.1 = (bf16[4,18,192,256]{3,2,1,0:T(8,128)(2,1)S(1)}, f32[27,256,512]{2,1,0:T(8,128)}) custom-call(s32[3]{0:T(128)S(1)} %pad_add_fusion.pos, bf16[4,384,128]{2,1,0:T(8,128)(2,1)S(1)} %pad_maximum_fusion.1.x_own, bf16[4,384,128]{2,1,0:T(8,128)(2,1)S(1)} %collective-permute-done.3.x_x.after1, bf16[4,384,128]{2,1,0:T(8,128)(2,1)S(1)} %collective-permute-done.4.x_y, ...), custom_call_target="tpu_custom_call" | custom-call | bytes 12582912 | tf_op jit(solution)/shard_map/lines/pallas_call | solution.py:391
  60.2 3.8 %collective-permute-done.14.g2b = bf16[768,128]{1,0:T(8,128)(2,1)S(1)} collective-permute-done((bf16[768,128]{1,0:T(8,128)(2,1)}, bf16[768,128]{1,0:T(8,128)(2,1)S(1)}, u32[]{:S(2)}, u32[]{:S(2)}) %collective-permute-start.14) | collective-permute-done | bytes 196640 | tf_op jit(solution)/shard_map/ppermute | solution.py:98
  64.1 1.0 copy-done.6
  65.1 7.0 %near.1.part = f32[3,384,256]{2,1,0:T(8,128)S(1)} custom-call(s32[3]{0:T(128)S(1)} %pad_add_fusion.pos, bf16[4,18,192,256]{3,2,1,0:T(8,128)(2,1)S(1)} %get-tuple-element.18.xs, bf16[2,768,128]{2,1,0:T(8,128)(2,1)S(1)} %pad_maximum_fusion.2.g0, bf16[2,768,128]{2,1,0:T(8,128)(2,1)S(1)} %collective-permute-done.8.g1, ...), custom_call_target="tpu_custom_call" | custom-call | flops 5435817984 | bytes 10616832 | tf_op jit(solution)/shard_map/near/pallas_call | solution.py:124
  72.2 3.4 %far.1.after = f32[1744,128]{1,0:T(8,128)S(1)} custom-call(s32[3]{0:T(128)S(1)} %pad_add_fusion.pos, bf16[4,18,192,256]{3,2,1,0:T(8,128)(2,1)S(1)} %get-tuple-element.18.xs, f32[3,384,256]{2,1,0:T(8,128)S(1)} %near.1.part, bf16[768,128]{1,0:T(8,128)(2,1)S(1)} %collective-permute-done.13.g2a, bf16[768,128]{1,0:T(8,128)(2,1)S(1)} %collective-permute-done.14.g2b, ...), custom_call_target="tpu_custom_call" | custom-call | flops 1811939328 | bytes 9936896 | tf_op jit(solution)/shard_map/far/pallas_call | solution.py:124
  75.7 2.5 %collective-permute-start.20 = (f16[1744,128]{1,0:T(8,128)(2,1)S(1)}, f16[1744,128]{1,0:T(8,128)(2,1)S(1)}, u32[]{:S(2)}, u32[]{:S(2)}) collective-permute-start(f16[1744,128]{1,0:T(8,128)(2,1)S(1)} %convert_element_type.255), channel_id=1, source_target_pairs={{0,4},{1,5},{2,6},{3,7},{4,0},{5,1},{6,2},{7,3},{8,12},{9,13},{10,... | collective-permute-start | bytes 1339400 | tf_op jit(solution)/shard_map/ppermute | solution.py:98
  78.2 1.9 %collective-permute-start.21 = (f16[1744,128]{1,0:T(8,128)(2,1)S(1)}, f16[1744,128]{1,0:T(8,128)(2,1)S(1)}, u32[]{:S(2)}, u32[]{:S(2)}) collective-permute-start(f16[1744,128]{1,0:T(8,128)(2,1)S(1)} %convert_element_type.255), channel_id=1, source_target_pairs={{0,8},{1,9},{2,10},{3,11},{4,12},{5,13},{6,14},{7,15},{8,0},{9,1},... | collective-permute-start | bytes 1339400 | tf_op jit(solution)/shard_map/ppermute | solution.py:98
  80.1 1.4 collective-permute-start.22
  82.2 3.3 %collective-permute-start.24 = (f16[1296,128]{1,0:T(8,128)(2,1)S(1)}, f16[1296,128]{1,0:T(8,128)(2,1)S(1)}, u32[]{:S(2)}, u32[]{:S(2)}) collective-permute-start(f16[1296,128]{1,0:T(8,128)(2,1)S(1)} %slice.435), channel_id=1, source_target_pairs={{0,3},{1,0},{2,1},{3,2},{4,7},{5,4},{6,5},{7,6},{8,11},{9,8},{10,9... | collective-permute-start | bytes 995336 | tf_op jit(solution)/shard_map/ppermute | solution.py:98
  85.5 11.9 %field.1 = bf16[4,4,48,256]{3,2,1,0:T(8,128)(2,1)} custom-call(s32[3]{0:T(128)} %copy-done.4, f32[1744,128]{1,0:T(8,128)} %copy-done, bf16[4,6,64,256]{3,2,1,0:T(8,128)(2,1)} %pad_maximum_fusion.mine, bf16[4,6,64,256]{3,2,1,0:T(8,128)(2,1)} %copy-done.2, bf16[27,256,512]{2,1,0:T(8,128)(2,1)} %bitcast.173), custom_call_target="tpu_custom_call" | custom-call | flops 10871635968 | bytes 7077888 | tf_op jit(solution)/shard_map/field/pallas_call | solution.py:450
  97.4 1.0 fusion.3
  99.3 1.5 %collective-permute-start.26 = (f16[2592,128]{1,0:T(8,128)(2,1)S(1)}, f16[2592,128]{1,0:T(8,128)(2,1)S(1)}, u32[]{:S(2)}, u32[]{:S(2)}) collective-permute-start(f16[2592,128]{1,0:T(8,128)(2,1)S(1)} %constant_dynamic-update-slice_fusion), channel_id=1, source_target_pairs={{0,8},{1,9},{2,10},{3,11},{4,12},{5,13},{6,14},{7,15},{8,0},{9,1},... | collective-permute-start | bytes 1990664 | tf_op jit(solution)/shard_map/ppermute | solution.py:98
  101.2 1.5 collective-permute-start.27
  102.9 1.4 collective-permute-start.28
  104.3 2.5 %collective-permute-start.29 = (f16[2512,128]{1,0:T(8,128)(2,1)S(1)}, f16[2512,128]{1,0:T(8,128)(2,1)S(1)}, u32[]{:S(2)}, u32[]{:S(2)}) collective-permute-start(f16[2512,128]{1,0:T(8,128)(2,1)S(1)} %get-tuple-element.53), channel_id=1, source_target_pairs={{0,3},{1,0},{2,1},{3,2},{4,7},{5,4},{6,5},{7,6},{8,11},{9,8},{10,9... | collective-permute-start | bytes 1929224 | tf_op jit(solution)/shard_map/ppermute | solution.py:98
  106.9 1.0 fusion.2
  108.0 1.0 fusion.1
  109.1 1.0 fusion
  111.9 4.7 %collective-permute-done.25 = f16[2592,128]{1,0:T(8,128)(2,1)S(1)} collective-permute-done((f16[2592,128]{1,0:T(8,128)(2,1)S(1)}, f16[2592,128]{1,0:T(8,128)(2,1)S(1)}, u32[]{:S(2)}, u32[]{:S(2)}) %collective-permute-start.25) | collective-permute-done | bytes 663584 | tf_op jit(solution)/shard_map/ppermute | solution.py:98
  116.8 0.9 fusion.13
  118.6 9.8 %collective-permute-done.26 = f16[2592,128]{1,0:T(8,128)(2,1)S(1)} collective-permute-done((f16[2592,128]{1,0:T(8,128)(2,1)S(1)}, f16[2592,128]{1,0:T(8,128)(2,1)S(1)}, u32[]{:S(2)}, u32[]{:S(2)}) %collective-permute-start.26) | collective-permute-done | bytes 663584 | tf_op jit(solution)/shard_map/ppermute | solution.py:98
  128.6 0.9 fusion.11
  132.4 1.3 collective-permute-start.30
  136.9 2.4 %collective-permute-start.32 = (f16[1296,128]{1,0:T(8,128)(2,1)S(1)}, f16[1296,128]{1,0:T(8,128)(2,1)S(1)}, u32[]{:S(2)}, u32[]{:S(2)}) collective-permute-start(f16[1296,128]{1,0:T(8,128)(2,1)S(1)} %pad_maximum_fusion.3), channel_id=1, source_target_pairs={{0,4},{1,5},{2,6},{3,7},{4,0},{5,1},{6,2},{7,3},{8,12},{9,13},{10,... | collective-permute-start | bytes 995336 | tf_op jit(solution)/shard_map/ppermute | solution.py:98
  139.4 1.7 %collective-permute-start.33 = (f16[1296,128]{1,0:T(8,128)(2,1)S(1)}, f16[1296,128]{1,0:T(8,128)(2,1)S(1)}, u32[]{:S(2)}, u32[]{:S(2)}) collective-permute-start(f16[1296,128]{1,0:T(8,128)(2,1)S(1)} %pad_maximum_fusion.3), channel_id=1, source_target_pairs={{0,8},{1,9},{2,10},{3,11},{4,12},{5,13},{6,14},{7,15},{8,0},{9,1},... | collective-permute-start | bytes 995336 | tf_op jit(solution)/shard_map/ppermute | solution.py:98
  141.2 2.6 %collective-permute-start.31 = (f16[928,128]{1,0:T(8,128)(2,1)S(1)}, f16[928,128]{1,0:T(8,128)(2,1)S(1)}, u32[]{:S(2)}, u32[]{:S(2)}) collective-permute-start(f16[928,128]{1,0:T(8,128)(2,1)S(1)} %slice.488), channel_id=1, source_target_pairs={{0,3},{1,0},{2,1},{3,2},{4,7},{5,4},{6,5},{7,6},{8,11},{9,8},{10,9... | collective-permute-start | bytes 712712 | tf_op jit(solution)/shard_map/ppermute | solution.py:98
  150.7 0.9 fusion.6
  151.8 0.9 fusion.5
  152.8 0.9 fusion.4
  (131 shorter events, 25.7 us)
Async XLA Ops:
  0.7 71.4 %copy-start.4 = (s32[3]{0:T(128)}, s32[3]{0:T(128)S(1)}, u32[]{:S(2)}) copy-start(s32[3]{0:T(128)S(1)} %pad_add_fusion.pos) | copy-start | bytes 40
  0.7 1.0 copy-start.1
  2.3 1.0 copy-start.3
  4.1 8.3 %collective-permute-start.2 = (bf16[416,128]{1,0:T(8,128)(2,1)S(1)}, bf16[416,128]{1,0:T(8,128)(2,1)S(1)}, u32[]{:S(2)}, u32[]{:S(2)}) collective-permute-start(bf16[416,128]{1,0:T(8,128)(2,1)S(1)} %get-tuple-element.17), channel_id=1, source_target_pairs={{0,3},{1,0},{2,1},{3,2},{4,7},{5,4},{6,5},{7,6},{8,11},{9,8},{10,9... | collective-permute-start | bytes 319496 | tf_op jit(solution)/shard_map/ppermute | solution.py:98
  9.2 12.5 %collective-permute-start.6 = (bf16[768,128]{1,0:T(8,128)(2,1)S(1)}, bf16[768,128]{1,0:T(8,128)(2,1)S(1)}, u32[]{:S(2)}, u32[]{:S(2)}) collective-permute-start(bf16[768,128]{1,0:T(8,128)(2,1)S(1)} %get-tuple-element.13.after), channel_id=1, source_target_pairs={{0,0},{1,1},{2,2},{3,3},{4,4},{5,5},{6,6},{7,7},{8,16},{9,17},{10,... | collective-permute-start | bytes 589832 | tf_op jit(solution)/shard_map/ppermute | solution.py:98
  9.9 9.6 %collective-permute-start.1 = (bf16[384,128]{1,0:T(8,128)(2,1)S(1)}, bf16[384,128]{1,0:T(8,128)(2,1)S(1)}, u32[]{:S(2)}, u32[]{:S(2)}) collective-permute-start(bf16[384,128]{1,0:T(8,128)(2,1)S(1)} %get-tuple-element.16), channel_id=1, source_target_pairs={{0,2},{1,3},{2,0},{3,1},{4,6},{5,7},{6,4},{7,5},{8,10},{9,11},{10,... | collective-permute-start | bytes 294920 | tf_op jit(solution)/shard_map/ppermute | solution.py:98
  9.9 6.6 %collective-permute-start = (bf16[416,128]{1,0:T(8,128)(2,1)S(1)}, bf16[416,128]{1,0:T(8,128)(2,1)S(1)}, u32[]{:S(2)}, u32[]{:S(2)}) collective-permute-start(bf16[416,128]{1,0:T(8,128)(2,1)S(1)} %get-tuple-element.15), channel_id=1, source_target_pairs={{0,1},{1,2},{2,3},{3,0},{4,5},{5,6},{6,7},{7,4},{8,9},{9,10},{10,1... | collective-permute-start | bytes 319496 | tf_op jit(solution)/shard_map/ppermute | solution.py:98
  10.9 10.7 %collective-permute-start.7 = (bf16[768,128]{1,0:T(8,128)(2,1)S(1)}, bf16[768,128]{1,0:T(8,128)(2,1)S(1)}, u32[]{:S(2)}, u32[]{:S(2)}) collective-permute-start(bf16[768,128]{1,0:T(8,128)(2,1)S(1)} %get-tuple-element.19), channel_id=1, source_target_pairs={{0,4},{1,5},{2,6},{3,7},{4,0},{5,1},{6,2},{7,3},{8,20},{9,21},{10,... | collective-permute-start | bytes 589832 | tf_op jit(solution)/shard_map/ppermute | solution.py:98
  19.5 12.0 %collective-permute-start.3 = (bf16[4,384,128]{2,1,0:T(8,128)(2,1)S(1)}, bf16[4,384,128]{2,1,0:T(8,128)(2,1)S(1)}, u32[]{:S(2)}, u32[]{:S(2)}) collective-permute-start(bf16[4,384,128]{2,1,0:T(8,128)(2,1)S(1)} %pad_maximum_fusion.1.x_own), channel_id=1, source_target_pairs={{0,4},{1,5},{2,6},{3,7},{4,0},{5,1},{6,2},{7,3},{8,12},{9,13},{10,... | collective-permute-start | bytes 1179656 | tf_op jit(solution)/shard_map/ppermute | solution.py:98
  21.1 17.8 %collective-permute-start.5 = (bf16[4,384,128]{2,1,0:T(8,128)(2,1)S(1)}, bf16[4,384,128]{2,1,0:T(8,128)(2,1)S(1)}, u32[]{:S(2)}, u32[]{:S(2)}) collective-permute-start(bf16[4,384,128]{2,1,0:T(8,128)(2,1)S(1)} %pad_maximum_fusion.1.x_own), channel_id=1, source_target_pairs={{0,12},{1,13},{2,14},{3,15},{4,8},{5,9},{6,10},{7,11},{8,4},{9,5},... | collective-permute-start | bytes 1179656 | tf_op jit(solution)/shard_map/ppermute | solution.py:98
  21.7 19.1 %collective-permute-start.8 = (bf16[2,768,128]{2,1,0:T(8,128)(2,1)S(1)}, bf16[2,768,128]{2,1,0:T(8,128)(2,1)S(1)}, u32[]{:S(2)}, u32[]{:S(2)}) collective-permute-start(bf16[2,768,128]{2,1,0:T(8,128)(2,1)S(1)} %pad_maximum_fusion.2.g0), channel_id=1, source_target_pairs={{0,1},{1,2},{2,3},{3,0},{4,5},{5,6},{6,7},{7,4},{8,9},{9,10},{10,1... | collective-permute-start | bytes 1179656 | tf_op jit(solution)/shard_map/ppermute | solution.py:98
  22.6 23.5 %collective-permute-start.9 = (bf16[2,768,128]{2,1,0:T(8,128)(2,1)S(1)}, bf16[2,768,128]{2,1,0:T(8,128)(2,1)}, u32[]{:S(2)}, u32[]{:S(2)}) collective-permute-start(bf16[2,768,128]{2,1,0:T(8,128)(2,1)S(1)} %pad_maximum_fusion.2.g0), channel_id=1, source_target_pairs={{0,3},{1,0},{2,1},{3,2},{4,7},{5,4},{6,5},{7,6},{8,11},{9,8},{10,9... | collective-permute-start | bytes 1179656 | tf_op jit(solution)/shard_map/ppermute | solution.py:98
  25.6 24.9 %collective-permute-start.4 = (bf16[4,384,128]{2,1,0:T(8,128)(2,1)S(1)}, bf16[4,384,128]{2,1,0:T(8,128)(2,1)S(1)}, u32[]{:S(2)}, u32[]{:S(2)}) collective-permute-start(bf16[4,384,128]{2,1,0:T(8,128)(2,1)S(1)} %pad_maximum_fusion.1.x_own), channel_id=1, source_target_pairs={{0,8},{1,9},{2,10},{3,11},{4,12},{5,13},{6,14},{7,15},{8,0},{9,1},... | collective-permute-start | bytes 1179656 | tf_op jit(solution)/shard_map/ppermute | solution.py:98
  31.5 20.1 %collective-permute-start.10 = (bf16[2,768,128]{2,1,0:T(8,128)(2,1)S(1)}, bf16[2,768,128]{2,1,0:T(8,128)(2,1)S(1)}, u32[]{:S(2)}, u32[]{:S(2)}) collective-permute-start(bf16[2,768,128]{2,1,0:T(8,128)(2,1)S(1)} %pad_maximum_fusion.2.g0), channel_id=1, source_target_pairs={{0,16},{1,17},{2,18},{3,19},{4,20},{5,21},{6,22},{7,23},{8,24},{9,... | collective-permute-start | bytes 1179656 | tf_op jit(solution)/shard_map/ppermute | solution.py:98
  39.5 6.9 %collective-permute-start.18 = (bf16[4,64,256]{2,1,0:T(8,128)(2,1)S(1)}, bf16[4,64,256]{2,1,0:T(8,128)(2,1)S(1)}, u32[]{:S(2)}, u32[]{:S(2)}) collective-permute-start(bf16[4,64,256]{2,1,0:T(8,128)(2,1)S(1)} %get-tuple-element.22), channel_id=1, source_target_pairs={{4,0},{5,1},{6,2},{7,3},{8,4},{9,5},{10,6},{11,7},{12,8},{13,9},{1... | collective-permute-start | bytes 393224 | tf_op jit(solution)/shard_map/ppermute | solution.py:98
  40.8 7.1 %collective-permute-start.17 = (bf16[4,64,256]{2,1,0:T(8,128)(2,1)S(1)}, bf16[4,64,256]{2,1,0:T(8,128)(2,1)S(1)}, u32[]{:S(2)}, u32[]{:S(2)}) collective-permute-start(bf16[4,64,256]{2,1,0:T(8,128)(2,1)S(1)} %get-tuple-element.20), channel_id=1, source_target_pairs={{0,4},{1,5},{2,6},{3,7},{4,8},{5,9},{6,10},{7,11},{8,12},{9,13},{1... | collective-permute-start | bytes 393224 | tf_op jit(solution)/shard_map/ppermute | solution.py:98
  46.1 18.0 %collective-permute-start.11 = (bf16[2,768,128]{2,1,0:T(8,128)(2,1)S(1)}, bf16[2,768,128]{2,1,0:T(8,128)(2,1)}, u32[]{:S(2)}, u32[]{:S(2)}) collective-permute-start(bf16[2,768,128]{2,1,0:T(8,128)(2,1)S(1)} %collective-permute-done.8.g1), channel_id=1, source_target_pairs={{0,16},{1,17},{2,18},{3,19},{4,20},{5,21},{6,22},{7,23},{8,24},{9,... | collective-permute-start | bytes 1179656 | tf_op jit(solution)/shard_map/ppermute | solution.py:98
  46.4 17.7 %collective-permute-start.12 = (bf16[2,768,128]{2,1,0:T(8,128)(2,1)}, bf16[2,768,128]{2,1,0:T(8,128)(2,1)}, u32[]{:S(2)}, u32[]{:S(2)}) collective-permute-start(bf16[2,768,128]{2,1,0:T(8,128)(2,1)} %collective-permute-done.9.g3), channel_id=1, source_target_pairs={{0,16},{1,17},{2,18},{3,19},{4,20},{5,21},{6,22},{7,23},{8,24},{9,... | collective-permute-start | bytes 1179656 | tf_op jit(solution)/shard_map/ppermute | solution.py:98
  48.9 23.3 %collective-permute-start.19 = (bf16[4,6,64,256]{3,2,1,0:T(8,128)(2,1)}, bf16[4,6,64,256]{3,2,1,0:T(8,128)(2,1)S(1)}, u32[]{:S(2)}, u32[]{:S(2)}) collective-permute-start(bf16[4,6,64,256]{3,2,1,0:T(8,128)(2,1)} %pad_maximum_fusion.mine), channel_id=1, source_target_pairs={{0,16},{1,17},{2,18},{3,19},{4,20},{5,21},{6,22},{7,23},{8,24},{9,... | collective-permute-start | bytes 2359304 | tf_op jit(solution)/shard_map/ppermute | solution.py:98
  50.5 9.8 %collective-permute-start.13 = (bf16[768,128]{1,0:T(8,128)(2,1)}, bf16[768,128]{1,0:T(8,128)(2,1)S(1)}, u32[]{:S(2)}, u32[]{:S(2)}) collective-permute-start(bf16[768,128]{1,0:T(8,128)(2,1)} %slice_bitcast_fusion.1), channel_id=1, source_target_pairs={{0,1},{1,2},{2,3},{3,0},{4,5},{5,6},{6,7},{7,4},{8,9},{9,10},{10,1... | collective-permute-start | bytes 589832 | tf_op jit(solution)/shard_map/ppermute | solution.py:98
  51.7 0.7 copy-start.5
  52.4 11.6 %collective-permute-start.14 = (bf16[768,128]{1,0:T(8,128)(2,1)}, bf16[768,128]{1,0:T(8,128)(2,1)S(1)}, u32[]{:S(2)}, u32[]{:S(2)}) collective-permute-start(bf16[768,128]{1,0:T(8,128)(2,1)} %slice_bitcast_fusion), channel_id=1, source_target_pairs={{0,3},{1,0},{2,1},{3,2},{4,7},{5,4},{6,5},{7,6},{8,11},{9,8},{10,9... | collective-permute-start | bytes 589832 | tf_op jit(solution)/shard_map/ppermute | solution.py:98
  60.2 11.9 %collective-permute-start.15 = (bf16[768,128]{1,0:T(8,128)(2,1)S(1)}, bf16[768,128]{1,0:T(8,128)(2,1)S(1)}, u32[]{:S(2)}, u32[]{:S(2)}) collective-permute-start(bf16[768,128]{1,0:T(8,128)(2,1)S(1)} %collective-permute-done.13.g2a), channel_id=1, source_target_pairs={{0,16},{1,17},{2,18},{3,19},{4,20},{5,21},{6,22},{7,23},{8,24},{9,... | collective-permute-start | bytes 589832 | tf_op jit(solution)/shard_map/ppermute | solution.py:98
  64.0 8.1 %collective-permute-start.16 = (bf16[768,128]{1,0:T(8,128)(2,1)S(1)}, bf16[768,128]{1,0:T(8,128)(2,1)S(1)}, u32[]{:S(2)}, u32[]{:S(2)}) collective-permute-start(bf16[768,128]{1,0:T(8,128)(2,1)S(1)} %collective-permute-done.14.g2b), channel_id=1, source_target_pairs={{0,16},{1,17},{2,18},{3,19},{4,20},{5,21},{6,22},{7,23},{8,24},{9,... | collective-permute-start | bytes 589832 | tf_op jit(solution)/shard_map/ppermute | solution.py:98
  64.1 1.0 copy-start.6
  72.2 13.3 %copy-start.2 = (bf16[4,6,64,256]{3,2,1,0:T(8,128)(2,1)}, bf16[4,6,64,256]{3,2,1,0:T(8,128)(2,1)S(1)}, u32[]{:S(2)}) copy-start(bf16[4,6,64,256]{3,2,1,0:T(8,128)(2,1)S(1)} %collective-permute-done.19.after.theirs) | copy-start | bytes 2359300
  75.6 9.8 %copy-start = (f32[1744,128]{1,0:T(8,128)}, f32[1744,128]{1,0:T(8,128)S(1)}, u32[]{:S(2)}) copy-start(f32[1744,128]{1,0:T(8,128)S(1)} %far.1.after) | copy-start | bytes 2678788
  75.7 25.5 %collective-permute-start.20 = (f16[1744,128]{1,0:T(8,128)(2,1)S(1)}, f16[1744,128]{1,0:T(8,128)(2,1)S(1)}, u32[]{:S(2)}, u32[]{:S(2)}) collective-permute-start(f16[1744,128]{1,0:T(8,128)(2,1)S(1)} %convert_element_type.255), channel_id=1, source_target_pairs={{0,4},{1,5},{2,6},{3,7},{4,0},{5,1},{6,2},{7,3},{8,12},{9,13},{10,... | collective-permute-start | bytes 1339400 | tf_op jit(solution)/shard_map/ppermute | solution.py:98
  78.2 24.6 %collective-permute-start.21 = (f16[1744,128]{1,0:T(8,128)(2,1)S(1)}, f16[1744,128]{1,0:T(8,128)(2,1)S(1)}, u32[]{:S(2)}, u32[]{:S(2)}) collective-permute-start(f16[1744,128]{1,0:T(8,128)(2,1)S(1)} %convert_element_type.255), channel_id=1, source_target_pairs={{0,8},{1,9},{2,10},{3,11},{4,12},{5,13},{6,14},{7,15},{8,0},{9,1},... | collective-permute-start | bytes 1339400 | tf_op jit(solution)/shard_map/ppermute | solution.py:98
  80.1 22.7 %collective-permute-start.22 = (f16[1744,128]{1,0:T(8,128)(2,1)S(1)}, f16[1744,128]{1,0:T(8,128)(2,1)S(1)}, u32[]{:S(2)}, u32[]{:S(2)}) collective-permute-start(f16[1744,128]{1,0:T(8,128)(2,1)S(1)} %convert_element_type.255), channel_id=1, source_target_pairs={{0,12},{1,13},{2,14},{3,15},{4,8},{5,9},{6,10},{7,11},{8,4},{9,5},... | collective-permute-start | bytes 1339400 | tf_op jit(solution)/shard_map/ppermute | solution.py:98
  81.6 16.8 %collective-permute-start.23 = (f16[1296,128]{1,0:T(8,128)(2,1)S(1)}, f16[1296,128]{1,0:T(8,128)(2,1)S(1)}, u32[]{:S(2)}, u32[]{:S(2)}) collective-permute-start(f16[1296,128]{1,0:T(8,128)(2,1)S(1)} %slice.435), channel_id=1, source_target_pairs={{0,1},{1,2},{2,3},{3,0},{4,5},{5,6},{6,7},{7,4},{8,9},{9,10},{10,1... | collective-permute-start | bytes 995336 | tf_op jit(solution)/shard_map/ppermute | solution.py:98
  82.2 16.4 %collective-permute-start.24 = (f16[1296,128]{1,0:T(8,128)(2,1)S(1)}, f16[1296,128]{1,0:T(8,128)(2,1)S(1)}, u32[]{:S(2)}, u32[]{:S(2)}) collective-permute-start(f16[1296,128]{1,0:T(8,128)(2,1)S(1)} %slice.435), channel_id=1, source_target_pairs={{0,3},{1,0},{2,1},{3,2},{4,7},{5,4},{6,5},{7,6},{8,11},{9,8},{10,9... | collective-permute-start | bytes 995336 | tf_op jit(solution)/shard_map/ppermute | solution.py:98
  98.7 17.9 %collective-permute-start.25 = (f16[2592,128]{1,0:T(8,128)(2,1)S(1)}, f16[2592,128]{1,0:T(8,128)(2,1)S(1)}, u32[]{:S(2)}, u32[]{:S(2)}) collective-permute-start(f16[2592,128]{1,0:T(8,128)(2,1)S(1)} %constant_dynamic-update-slice_fusion), channel_id=1, source_target_pairs={{0,4},{1,5},{2,6},{3,7},{4,0},{5,1},{6,2},{7,3},{8,12},{9,13},{10,... | collective-permute-start | bytes 1990664 | tf_op jit(solution)/shard_map/ppermute | solution.py:98
  99.3 29.1 %collective-permute-start.26 = (f16[2592,128]{1,0:T(8,128)(2,1)S(1)}, f16[2592,128]{1,0:T(8,128)(2,1)S(1)}, u32[]{:S(2)}, u32[]{:S(2)}) collective-permute-start(f16[2592,128]{1,0:T(8,128)(2,1)S(1)} %constant_dynamic-update-slice_fusion), channel_id=1, source_target_pairs={{0,8},{1,9},{2,10},{3,11},{4,12},{5,13},{6,14},{7,15},{8,0},{9,1},... | collective-permute-start | bytes 1990664 | tf_op jit(solution)/shard_map/ppermute | solution.py:98
  101.2 29.1 %collective-permute-start.27 = (f16[2592,128]{1,0:T(8,128)(2,1)S(1)}, f16[2592,128]{1,0:T(8,128)(2,1)S(1)}, u32[]{:S(2)}, u32[]{:S(2)}) collective-permute-start(f16[2592,128]{1,0:T(8,128)(2,1)S(1)} %constant_dynamic-update-slice_fusion), channel_id=1, source_target_pairs={{0,12},{1,13},{2,14},{3,15},{4,8},{5,9},{6,10},{7,11},{8,4},{9,5},... | collective-permute-start | bytes 1990664 | tf_op jit(solution)/shard_map/ppermute | solution.py:98
  102.9 29.4 %collective-permute-start.28 = (f16[2496,128]{1,0:T(8,128)(2,1)S(1)}, f16[2496,128]{1,0:T(8,128)(2,1)S(1)}, u32[]{:S(2)}, u32[]{:S(2)}) collective-permute-start(f16[2496,128]{1,0:T(8,128)(2,1)S(1)} %get-tuple-element.54), channel_id=1, source_target_pairs={{0,1},{1,2},{2,3},{3,0},{4,5},{5,6},{6,7},{7,4},{8,9},{9,10},{10,1... | collective-permute-start | bytes 1916936 | tf_op jit(solution)/shard_map/ppermute | solution.py:98
  104.3 32.4 %collective-permute-start.29 = (f16[2512,128]{1,0:T(8,128)(2,1)S(1)}, f16[2512,128]{1,0:T(8,128)(2,1)S(1)}, u32[]{:S(2)}, u32[]{:S(2)}) collective-permute-start(f16[2512,128]{1,0:T(8,128)(2,1)S(1)} %get-tuple-element.53), channel_id=1, source_target_pairs={{0,3},{1,0},{2,1},{3,2},{4,7},{5,4},{6,5},{7,6},{8,11},{9,8},{10,9... | collective-permute-start | bytes 1929224 | tf_op jit(solution)/shard_map/ppermute | solution.py:98
  132.4 15.2 %collective-permute-start.30 = (f16[928,128]{1,0:T(8,128)(2,1)S(1)}, f16[928,128]{1,0:T(8,128)(2,1)S(1)}, u32[]{:S(2)}, u32[]{:S(2)}) collective-permute-start(f16[928,128]{1,0:T(8,128)(2,1)S(1)} %slice.483), channel_id=1, source_target_pairs={{0,1},{1,2},{2,3},{3,0},{4,5},{5,6},{6,7},{7,4},{8,9},{9,10},{10,1... | collective-permute-start | bytes 712712 | tf_op jit(solution)/shard_map/ppermute | solution.py:98
  136.9 13.7 %collective-permute-start.32 = (f16[1296,128]{1,0:T(8,128)(2,1)S(1)}, f16[1296,128]{1,0:T(8,128)(2,1)S(1)}, u32[]{:S(2)}, u32[]{:S(2)}) collective-permute-start(f16[1296,128]{1,0:T(8,128)(2,1)S(1)} %pad_maximum_fusion.3), channel_id=1, source_target_pairs={{0,4},{1,5},{2,6},{3,7},{4,0},{5,1},{6,2},{7,3},{8,12},{9,13},{10,... | collective-permute-start | bytes 995336 | tf_op jit(solution)/shard_map/ppermute | solution.py:98
  139.4 12.4 %collective-permute-start.33 = (f16[1296,128]{1,0:T(8,128)(2,1)S(1)}, f16[1296,128]{1,0:T(8,128)(2,1)S(1)}, u32[]{:S(2)}, u32[]{:S(2)}) collective-permute-start(f16[1296,128]{1,0:T(8,128)(2,1)S(1)} %pad_maximum_fusion.3), channel_id=1, source_target_pairs={{0,8},{1,9},{2,10},{3,11},{4,12},{5,13},{6,14},{7,15},{8,0},{9,1},... | collective-permute-start | bytes 995336 | tf_op jit(solution)/shard_map/ppermute | solution.py:98
  141.1 11.6 %collective-permute-start.34 = (f16[1296,128]{1,0:T(8,128)(2,1)S(1)}, f16[1296,128]{1,0:T(8,128)(2,1)S(1)}, u32[]{:S(2)}, u32[]{:S(2)}) collective-permute-start(f16[1296,128]{1,0:T(8,128)(2,1)S(1)} %pad_maximum_fusion.3), channel_id=1, source_target_pairs={{0,12},{1,13},{2,14},{3,15},{4,8},{5,9},{6,10},{7,11},{8,4},{9,5},... | collective-permute-start | bytes 995336 | tf_op jit(solution)/shard_map/ppermute | solution.py:98
  141.2 8.0 %collective-permute-start.31 = (f16[928,128]{1,0:T(8,128)(2,1)S(1)}, f16[928,128]{1,0:T(8,128)(2,1)S(1)}, u32[]{:S(2)}, u32[]{:S(2)}) collective-permute-start(f16[928,128]{1,0:T(8,128)(2,1)S(1)} %slice.488), channel_id=1, source_target_pairs={{0,3},{1,0},{2,1},{3,2},{4,7},{5,4},{6,5},{7,6},{8,11},{9,8},{10,9... | collective-permute-start | bytes 712712 | tf_op jit(solution)/shard_map/ppermute | solution.py:98

commit v4 on v3

--- a/solution.py
+++ b/solution.py
@@ -110,14 +110,6 @@
     return (1 - c, a, o)
 
 
-def north(c, a, o):
-    return (c, a + 1, o) if a < 3 else None
-
-
-def south(c, a, o):
-    return (c, a - 1, o) if a > 0 else None
-
-
 def call(kernel, outs, ins, scratch, flops, name, limit, held=0):
     read = len(ins) - 1 - held
     moved = sum(math.prod(x.shape) * x.dtype.itemsize for x in list(ins[1 : 1 + read]) + list(outs))
@@ -162,21 +154,86 @@
         out[many + levels * height :, :] = rim[:, wide:]
 
 
-def rims_kernel(pos, g, from_west, from_east, after1, after2, broad, low, high):
-    del after1, after2
+def pair_kernel(pos, one, two, out):
+    del pos
+    out[0] = one[...]
+    out[1] = two[...]
+
+
+def split_kernel(pos, here, west, east, first, second, near):
+    del pos
+    first[...] = west[0]
+    second[...] = east[1]
+    for at, part in enumerate((here, west, east)):
+        near[2 * at : 2 * at + 2] = part[...]
+
+
+def spread_kernel(pos, x0, x1, x2, x3, g, by_x, by_y, by_d):
     levels, height, width, chans = g.shape
-    many = from_west.shape[0] - 2 * levels * height
-    wide = chans // 2
-    broad[:, :, 0:width, :] = g[...]
-    for message, at in ((from_west, width), (from_east, width + 8)):
+    many, wide = x0.shape[0], chans // 2
+    line, edge = levels * width, levels * height
+    for out in (by_x, by_y, by_d):
+        for at, piece in enumerate((x0, x1, x2, x3)):
+            out[at * many : (at + 1) * many, :] = piece[0:many, :]
+    even = lax.rem(pos[1], 2) == 0
+    low, high = g[:, 0], g[:, height - 1]
+    for out, upward in ((by_x, even), (by_d, jnp.logical_not(even))):
+        facing = jnp.where(upward, high, low).reshape(line, chans)
         for half in range(2):
-            first = many + half * levels * height
-            rim = message[first : first + levels * height, :].reshape(levels, height, 1, wide)
-            broad[:, :, at : at + 8, half * wide : (half + 1) * wide] = jnp.broadcast_to(
-                rim, (levels, height, 8, wide)
-            )
-    low[...] = broad[:, 0]
-    high[...] = broad[:, height - 1]
+            first = 4 * many + half * line
+            out[first : first + line, :] = facing[:, half * wide : (half + 1) * wide]
+        first = 4 * many + 2 * line
+        out[first : first + 2 * edge, :] = x1[many : many + 2 * edge, :]
+        out[first + 2 * edge : first + 4 * edge, :] = x3[many : many + 2 * edge, :]
+
+
+def rims_kernel(pos, g, from_west, from_east, by_x, by_d, after, mine):
+    del after
+    levels, height, width, chans = g.shape
+    edge, line, wide = levels * height, levels * width, chans // 2
+    many = from_west.shape[0] - 2 * edge
+    mine[:, 1 : height + 1, 0:width, :] = g[...]
+
+    def columns(message, first, at, rows):
+        for half in range(2):
+            rim = message[first + half * edge : first + (half + 1) * edge, :].reshape(levels, height, wide)
+            for row, to in rows:
+                mine[:, to, at : at + 8, half * wide : (half + 1) * wide] = jnp.broadcast_to(
+                    rim[:, row : row + 1], (levels, 8, wide)
+                )
+
+    inner = [(row, row + 1) for row in range(height)]
+    columns(from_west, many, width, inner)
+    columns(from_east, many, width + 8, inner)
+
+    def lines(message, row, to):
+        first = 4 * many
+        for half in range(2):
+            strip = message[first + half * line : first + (half + 1) * line, :]
+            mine[:, to, 0:width, half * wide : (half + 1) * wide] = strip.reshape(levels, width, wide)
+        columns(message, first + 2 * line, width, [(row, to)])
+        columns(message, first + 2 * line + 2 * edge, width + 8, [(row, to)])
+
+    lat = pos[1]
+    odd = lax.rem(lat, 2)
+
+    @pl.when(odd == 1)
+    def _():
+        lines(by_x, height - 1, 0)
+        lines(by_d, 0, height + 1)
+
+    @pl.when(odd == 0)
+    def _():
+        lines(by_d, height - 1, 0)
+        lines(by_x, 0, height + 1)
+
+    @pl.when(lat == 0)
+    def _():
+        mine[:, 0] = jnp.zeros_like(mine[:, 0])
+
+    @pl.when(lat == 3)
+    def _():
+        mine[:, height + 1] = jnp.zeros_like(mine[:, height + 1])
 
 
 def lines_kernel(pos, x_own, x_x, x_y, x_d, xs, blank):
@@ -185,12 +242,15 @@
     levels, rows, circle, lanes = xs.shape
     rows, width, span, half = rows - 2, circle // 4, lanes // 4, levels // 2
     height = rows // 4
+    many = half * height * width
     xs[:, 0] = jnp.zeros_like(xs[:, 0])
     xs[:, rows + 1] = jnp.zeros_like(xs[:, rows + 1])
     low = lax.broadcasted_iota(jnp.int32, (circle, 2 * span), 1) < span
     for tag, ref in enumerate((x_own, x_x, x_y, x_d)):
         start = (lat ^ tag) * height
-        strips = [ref.at[(4 - at) % 4].reshape(half, height, width, 2 * span) for at in range(4)]
+        strips = [
+            ref.at[pl.ds((4 - at) % 4 * many, many)].reshape(half, height, width, 2 * span) for at in range(4)
+        ]
 
         @pl.loop(0, half * height)
         def _(step, strips=strips, start=start):
@@ -239,12 +299,12 @@
             acc[lat_by, to : to + many, :] = total
 
 
-def near_kernel(pos, xs, g0, g1, g3, s0, s1, s3, acc, gt):
+def near_kernel(pos, xs, g, s, acc, gt):
     levels = xs.shape[0]
     right = lax.rem(pos[1], 2)
-    for core, parts in ((pos[0], (g0, g3, g1)), (1 - pos[0], (s0, s3, s1))):
-        for slot, part in enumerate(parts):
-            turn(gt, slot, core, part[right], part[1 - right], levels)
+    for core, parts in ((pos[0], g), (1 - pos[0], s)):
+        for slot, at in enumerate((0, 4, 2)):
+            turn(gt, slot, core, parts[at + right], parts[at + 1 - right], levels)
     acc[...] = jnp.zeros_like(acc)
     add_taps(acc, gt, xs, (0, 1, 3))
 
@@ -356,36 +416,51 @@
     x_r1 = move(x1, lon_by(1))
     x_r3 = move(x3, lon_by(-1))
     x_r2 = move(x2, lon_by(2))
-    g0 = jnp.stack([g_s, g_o])
+    pair = jax.ShapeDtypeStruct((2, cells, wide), bf16)
+    (g0,) = call(pair_kernel, [pair], (pos, g_s, g_o), [], 0, "pair", 16)
     g1 = move(g0, lon_by(1))
     g3 = move(g0, lon_by(-1))
 
-    s0 = move(g0, sibling)
-    x_own = jnp.stack([x0, x_r1[:many], x_r2, x_r3[:many]])
+    inner = 4 * many
+    outer = inner + 2 * levels * width + 4 * edge
+    x_own, x_own_y, x_own_d = call(
+        spread_kernel,
+        [jax.ShapeDtypeStruct((count, 2 * span), bf16) for count in (outer, inner, outer)],
+        (pos, x0, x_r1, x_r2, x_r3, g_cells),
+        [],
+        0,
+        "spread",
+        16,
+    )
     x_x = move(x_own, lat_xor(1))
-    x_y = move(x_own, lat_xor(2))
-    x_d = move(x_own, lat_xor(3))
-    g2a = move(g1[0], lon_by(1))
-    g2b = move(g3[1], lon_by(-1))
-    s1 = move(g1, sibling)
-    s3 = move(g3, sibling)
+    x_y = move(x_own_y, lat_xor(2))
+    x_d = move(x_own_d, lat_xor(3))
+    block = jax.ShapeDtypeStruct((cells, wide), bf16)
+    far_a, far_b, g_near = call(
+        split_kernel,
+        [block, block, jax.ShapeDtypeStruct((6, cells, wide), bf16)],
+        (pos, g0, g1, g3),
+        [],
+        0,
+        "split",
+        16,
+    )
+    g2a = move(far_a, lon_by(1))
+    g2b = move(far_b, lon_by(-1))
+    s_near = move(g_near, sibling)
     s2a = move(g2a, sibling)
     s2b = move(g2b, sibling)
 
-    strip = jax.ShapeDtypeStruct((levels, width + 16, chans), bf16)
-    broad, low, high = call(
+    (mine,) = call(
         rims_kernel,
-        [jax.ShapeDtypeStruct((levels, height, width + 16, chans), bf16), strip, strip],
-        (pos, g_cells, x_r1, x_r3, x_x, x_d),
+        [jax.ShapeDtypeStruct((levels, height + 2, width + 16, chans), bf16)],
+        (pos, g_cells, x_r1, x_r3, x_x, x_d, s_near),
         [],
         0,
         "rims",
         16,
-        held=2,
-    )
-    from_lo = move(high, north)
-    from_hi = move(low, south)
-    mine = jnp.concatenate([from_lo[:, None], broad, from_hi[:, None]], axis=1)
+        held=1,
+    )
     theirs = move(mine, sibling)
 
     xs, total = pl.pallas_call(
@@ -405,7 +480,7 @@
     (part,) = call(
         near_kernel,
         [jax.ShapeDtypeStruct((3, 3 * wide, 4 * span), f32)],
-        (pos, xs, g0, g1, g3, s0, s1, s3),
+        (pos, xs, g_near, s_near),
         [VMEM((levels * wide, 3 * rows * width), bf16)],
         work,
         "near",

time: 154 us -> 180 us (1.17)
  waiting for transfers between devices: 39.4 us -> 71.8 us
  starting transfers between devices: 51 us -> 42.5 us
  Pallas kernels: 29.2 us -> 34 us
    ppermute x35 -> x31, waiting for transfers between devices: 39.4 us -> 71.8 us  [move(): return lax.ppermute(x, AXES, pairs)]
    ppermute x35 -> x31, starting transfers between devices: 51 us -> 42.5 us  [move(): return lax.ppermute(x, AXES, pairs)]
    pallas_call x5 -> x8, Pallas kernels: 12.4 us -> 16.8 us  [call(): pl.pallas_call(kernel, out_shape=outs, in_specs=[pl.BlockSpec(memory_spac...]
    squeeze x2 -> x0, local copies, waits for them, and re-layouts: 2.31 us -> none  [the longest x1 1.62 us: blocked_body(): g2b = move(g3[1], lon_by(-1))]
    unnamed x24 -> x26, local copies, waits for them, and re-layouts: 4.19 us -> 5.02 us
  transfers between devices with their start and end apart: 35 -> 31, of which waited for: 12 -> 13; matrix products, arithmetic and copies ran while one was open for 18% -> 14% of each run, Pallas kernels for 16% -> 15%
where the time goes in v4:
time: 180 us
  waiting for transfers between devices  71.8 us (40%)
  starting transfers between devices  42.5 us (24%)
  Pallas kernels  34 us (19%)
  other arithmetic  23.8 us (13%)
  local copies, waits for them, and re-layouts  6.73 us (4%)
    ppermute x31, waiting for transfers between devices, move(): return lax.ppermute(x, AXES, pairs)  71.8 us
    ppermute x31, starting transfers between devices, move(): return lax.ppermute(x, AXES, pairs)  42.5 us
    dynamic_update_slice x28, other arithmetic, put(): return lax.dynamic_update_slice(total, value, at)  23.3 us
    pallas_call x8, Pallas kernels, call(): pl.pallas_call(kernel, out_shape=outs, in_specs=[pl.BlockSpec(memory_spac...  16.8 us
    pallas_call x1, Pallas kernels, blocked_body(): pl.pallas_call(field_kernel, out_shape=jax.ShapeDtypeStruct((levels, heig...  11.9 us
    pallas_call x1, Pallas kernels, blocked_body(): pl.pallas_call(lines_kernel, out_shape=[jax.ShapeDtypeStruct((levels, row...  5.33 us
    unnamed x26, local copies, waits for them, and re-layouts  5.02 us
  transfers between devices with their start and end apart: 31, of which 13 were waited for; matrix products, arithmetic and copies ran while one was open for 14% of the time, Pallas kernels for 15%

profile of v4, /device:TPU:0, one launch (start us, length us, event | category | flops | bytes accessed | tf_op | source)
XLA Modules:
  0.0 179.9 jit_solution(8476584298362962444)
XLA Ops:
  0.7 1.0 copy-done
  3.0 3.0 %collective-permute-start.7 = (bf16[768,128]{1,0:T(8,128)(2,1)S(1)}, bf16[768,128]{1,0:T(8,128)(2,1)S(1)}, u32[]{:S(2)}, u32[]{:S(2)}) collective-permute-start(bf16[768,128]{1,0:T(8,128)(2,1)S(1)} %get-tuple-element.25), channel_id=1, source_target_pairs={{0,4},{1,5},{2,6},{3,7},{4,0},{5,1},{6,2},{7,3},{8,20},{9,21},{10,... | collective-permute-start | bytes 589832 | tf_op jit(solution)/shard_map/ppermute | solution.py:98
  6.0 3.6 %collective-permute-done.7.two = bf16[768,128]{1,0:T(8,128)(2,1)S(1)} collective-permute-done((bf16[768,128]{1,0:T(8,128)(2,1)S(1)}, bf16[768,128]{1,0:T(8,128)(2,1)S(1)}, u32[]{:S(2)}, u32[]{:S(2)}) %collective-permute-start.7) | collective-permute-done | bytes 196640 | tf_op jit(solution)/shard_map/ppermute | solution.py:98
  10.2 2.5 %collective-permute-start.8 = (bf16[2,768,128]{2,1,0:T(8,128)(2,1)S(1)}, bf16[2,768,128]{2,1,0:T(8,128)(2,1)S(1)}, u32[]{:S(2)}, u32[]{:S(2)}) collective-permute-start(bf16[2,768,128]{2,1,0:T(8,128)(2,1)S(1)} %pair.1.here), channel_id=1, source_target_pairs={{0,1},{1,2},{2,3},{3,0},{4,5},{5,6},{6,7},{7,4},{8,9},{9,10},{10,1... | collective-permute-start | bytes 1179656 | tf_op jit(solution)/shard_map/ppermute | solution.py:98
  12.8 2.1 %collective-permute-start.9 = (bf16[2,768,128]{2,1,0:T(8,128)(2,1)S(1)}, bf16[2,768,128]{2,1,0:T(8,128)(2,1)S(1)}, u32[]{:S(2)}, u32[]{:S(2)}) collective-permute-start(bf16[2,768,128]{2,1,0:T(8,128)(2,1)S(1)} %pair.1.here), channel_id=1, source_target_pairs={{0,3},{1,0},{2,1},{3,2},{4,7},{5,4},{6,5},{7,6},{8,11},{9,8},{10,9... | collective-permute-start | bytes 1179656 | tf_op jit(solution)/shard_map/ppermute | solution.py:98
  14.9 8.0 %collective-permute-done.8.west = bf16[2,768,128]{2,1,0:T(8,128)(2,1)S(1)} collective-permute-done((bf16[2,768,128]{2,1,0:T(8,128)(2,1)S(1)}, bf16[2,768,128]{2,1,0:T(8,128)(2,1)S(1)}, u32[]{:S(2)}, u32[]{:S(2)}) %collective-permute-start.8) | collective-permute-done | bytes 393248 | tf_op jit(solution)/shard_map/ppermute | solution.py:98
  22.9 10.1 %collective-permute-done.9.east = bf16[2,768,128]{2,1,0:T(8,128)(2,1)S(1)} collective-permute-done((bf16[2,768,128]{2,1,0:T(8,128)(2,1)S(1)}, bf16[2,768,128]{2,1,0:T(8,128)(2,1)S(1)}, u32[]{:S(2)}, u32[]{:S(2)}) %collective-permute-start.9) | collective-permute-done | bytes 393248 | tf_op jit(solution)/shard_map/ppermute | solution.py:98
  33.0 1.4 split.1
  34.5 1.3 copy-done.1
  35.8 1.0 copy-done.4
  38.3 3.1 %collective-permute-start.2 = (bf16[416,128]{1,0:T(8,128)(2,1)S(1)}, bf16[416,128]{1,0:T(8,128)(2,1)S(1)}, u32[]{:S(2)}, u32[]{:S(2)}) collective-permute-start(bf16[416,128]{1,0:T(8,128)(2,1)S(1)} %get-tuple-element.20), channel_id=1, source_target_pairs={{0,3},{1,0},{2,1},{3,2},{4,7},{5,4},{6,5},{7,6},{8,11},{9,8},{10,9... | collective-permute-start | bytes 319496 | tf_op jit(solution)/shard_map/ppermute | solution.py:98
  41.5 8.1 %collective-permute-done.1.x2 = bf16[384,128]{1,0:T(8,128)(2,1)S(1)} collective-permute-done((bf16[384,128]{1,0:T(8,128)(2,1)S(1)}, bf16[384,128]{1,0:T(8,128)(2,1)S(1)}, u32[]{:S(2)}, u32[]{:S(2)}) %collective-permute-start.1) | collective-permute-done | bytes 98336 | tf_op jit(solution)/shard_map/ppermute | solution.py:98
  49.6 1.4 spread.1
  51.1 1.5 collective-permute-start.3
  52.6 2.0 %collective-permute-start.4 = (bf16[1536,128]{1,0:T(8,128)(2,1)}, bf16[1536,128]{1,0:T(8,128)(2,1)}, u32[]{:S(2)}, u32[]{:S(2)}) collective-permute-start(bf16[1536,128]{1,0:T(8,128)(2,1)} %get-tuple-element.22), channel_id=1, source_target_pairs={{0,8},{1,9},{2,10},{3,11},{4,12},{5,13},{6,14},{7,15},{8,0},{9,1},... | collective-permute-start | bytes 1179656 | tf_op jit(solution)/shard_map/ppermute | solution.py:98
  54.5 11.0 %collective-permute-done.3.x_x.by_x = bf16[1984,128]{1,0:T(8,128)(2,1)S(1)} collective-permute-done((bf16[1984,128]{1,0:T(8,128)(2,1)S(1)}, bf16[1984,128]{1,0:T(8,128)(2,1)S(1)}, u32[]{:S(2)}, u32[]{:S(2)}) %collective-permute-start.3) | collective-permute-done | bytes 507936 | tf_op jit(solution)/shard_map/ppermute | solution.py:98
  65.6 8.5 %collective-permute-done.5.x_d.by_d = bf16[1984,128]{1,0:T(8,128)(2,1)S(1)} collective-permute-done((bf16[1984,128]{1,0:T(8,128)(2,1)S(1)}, bf16[1984,128]{1,0:T(8,128)(2,1)S(1)}, u32[]{:S(2)}, u32[]{:S(2)}) %collective-permute-start.5) | collective-permute-done | bytes 507936 | tf_op jit(solution)/shard_map/ppermute | solution.py:98
  74.0 1.6 rims.1.mine
  75.6 3.8 %collective-permute-start.12 = (bf16[768,128]{1,0:T(8,128)(2,1)}, bf16[768,128]{1,0:T(8,128)(2,1)}, u32[]{:S(2)}, u32[]{:S(2)}) collective-permute-start(bf16[768,128]{1,0:T(8,128)(2,1)} %get-tuple-element.28), channel_id=1, source_target_pairs={{0,3},{1,0},{2,1},{3,2},{4,7},{5,4},{6,5},{7,6},{8,11},{9,8},{10,9... | collective-permute-start | bytes 589832 | tf_op jit(solution)/shard_map/ppermute | solution.py:98
  79.4 5.3 %lines.1 = (bf16[4,18,192,256]{3,2,1,0:T(8,128)(2,1)S(1)}, f32[27,256,512]{2,1,0:T(8,128)}) custom-call(s32[3]{0:T(128)S(1)} %pad_add_fusion.pos, bf16[1984,128]{1,0:T(8,128)(2,1)S(1)} %get-tuple-element.21.x_own, bf16[1984,128]{1,0:T(8,128)(2,1)S(1)} %collective-permute-done.3.x_x.by_x, bf16[1536,128]{1,0:T(8,128)(2,1)} %collective-permute-done.4.x_y, ...), custom_call_target="tpu_custom_call" | custom-call | bytes 12582912 | tf_op jit(solution)/shard_map/lines/pallas_call | solution.py:466
  85.4 2.0 %collective-permute-done.12.g2b = bf16[768,128]{1,0:T(8,128)(2,1)} collective-permute-done((bf16[768,128]{1,0:T(8,128)(2,1)}, bf16[768,128]{1,0:T(8,128)(2,1)}, u32[]{:S(2)}, u32[]{:S(2)}) %collective-permute-start.12) | collective-permute-done | bytes 196640 | tf_op jit(solution)/shard_map/ppermute | solution.py:98
  87.4 1.3 copy-done.7
  88.7 6.3 %near.1.part = f32[3,384,256]{2,1,0:T(8,128)S(1)} custom-call(s32[3]{0:T(128)S(1)} %pad_add_fusion.pos, bf16[4,18,192,256]{3,2,1,0:T(8,128)(2,1)S(1)} %get-tuple-element.24.xs, bf16[6,768,128]{2,1,0:T(8,128)(2,1)S(1)} %copy-done.7, bf16[6,768,128]{2,1,0:T(8,128)(2,1)S(1)} %collective-permute-done.10.s.after), custom_call_target="tpu_custom_call" | custom-call | flops 5435817984 | bytes 10616832 | tf_op jit(solution)/shard_map/near/pallas_call | solution.py:116
  95.1 4.2 %far.1.after = f32[1744,128]{1,0:T(8,128)S(1)} custom-call(s32[3]{0:T(128)S(1)} %pad_add_fusion.pos, bf16[4,18,192,256]{3,2,1,0:T(8,128)(2,1)S(1)} %get-tuple-element.24.xs, f32[3,384,256]{2,1,0:T(8,128)S(1)} %near.1.part, bf16[768,128]{1,0:T(8,128)(2,1)} %collective-permute-done.11.g2a, bf16[768,128]{1,0:T(8,128)(2,1)} %collective-permute-done.12.g2b, ...), custom_call_target="tpu_custom_call" | custom-call | flops 1811939328 | bytes 9936896 | tf_op jit(solution)/shard_map/far/pallas_call | solution.py:116
  99.4 1.3 collective-permute-start.16
  100.7 2.7 %collective-permute-start.17 = (f16[1744,128]{1,0:T(8,128)(2,1)S(1)}, f16[1744,128]{1,0:T(8,128)(2,1)S(1)}, u32[]{:S(2)}, u32[]{:S(2)}) collective-permute-start(f16[1744,128]{1,0:T(8,128)(2,1)S(1)} %convert_element_type.255), channel_id=1, source_target_pairs={{0,8},{1,9},{2,10},{3,11},{4,12},{5,13},{6,14},{7,15},{8,0},{9,1},... | collective-permute-start | bytes 1339400 | tf_op jit(solution)/shard_map/ppermute | solution.py:98
  103.8 3.6 %collective-permute-start.20 = (f16[1296,128]{1,0:T(8,128)(2,1)S(1)}, f16[1296,128]{1,0:T(8,128)(2,1)S(1)}, u32[]{:S(2)}, u32[]{:S(2)}) collective-permute-start(f16[1296,128]{1,0:T(8,128)(2,1)S(1)} %slice.415), channel_id=1, source_target_pairs={{0,3},{1,0},{2,1},{3,2},{4,7},{5,4},{6,5},{7,6},{8,11},{9,8},{10,9... | collective-permute-start | bytes 995336 | tf_op jit(solution)/shard_map/ppermute | solution.py:98
  107.3 11.9 %field.1 = bf16[4,4,48,256]{3,2,1,0:T(8,128)(2,1)} custom-call(s32[3]{0:T(128)} %copy-done.5, f32[1744,128]{1,0:T(8,128)} %copy-done.2, bf16[4,6,64,256]{3,2,1,0:T(8,128)(2,1)} %rims.1.mine, bf16[4,6,64,256]{3,2,1,0:T(8,128)(2,1)} %copy-done.3, bf16[27,256,512]{2,1,0:T(8,128)(2,1)} %bitcast.154), custom_call_target="tpu_custom_call" | custom-call | flops 10871635968 | bytes 7077888 | tf_op jit(solution)/shard_map/field/pallas_call | solution.py:525
  119.3 1.0 fusion.3
  121.3 1.5 collective-permute-start.21
  122.8 1.7 collective-permute-start.22
  125.6 1.5 collective-permute-start.24
  127.0 2.4 %collective-permute-start.25 = (f16[2512,128]{1,0:T(8,128)(2,1)S(1)}, f16[2512,128]{1,0:T(8,128)(2,1)S(1)}, u32[]{:S(2)}, u32[]{:S(2)}) collective-permute-start(f16[2512,128]{1,0:T(8,128)(2,1)S(1)} %get-tuple-element.59), channel_id=1, source_target_pairs={{0,3},{1,0},{2,1},{3,2},{4,7},{5,4},{6,5},{7,6},{8,11},{9,8},{10,9... | collective-permute-start | bytes 1929224 | tf_op jit(solution)/shard_map/ppermute | solution.py:98
  129.5 1.0 fusion.2
  130.6 1.0 fusion.1
  131.8 1.0 fusion
  134.5 4.7 %collective-permute-done.21 = f16[2592,128]{1,0:T(8,128)(2,1)S(1)} collective-permute-done((f16[2592,128]{1,0:T(8,128)(2,1)S(1)}, f16[2592,128]{1,0:T(8,128)(2,1)S(1)}, u32[]{:S(2)}, u32[]{:S(2)}) %collective-permute-start.21) | collective-permute-done | bytes 663584 | tf_op jit(solution)/shard_map/ppermute | solution.py:98
  139.4 0.9 fusion.13
  141.2 11.6 %collective-permute-done.22 = f16[2592,128]{1,0:T(8,128)(2,1)S(1)} collective-permute-done((f16[2592,128]{1,0:T(8,128)(2,1)S(1)}, f16[2592,128]{1,0:T(8,128)(2,1)S(1)}, u32[]{:S(2)}, u32[]{:S(2)}) %collective-permute-start.22) | collective-permute-done | bytes 663584 | tf_op jit(solution)/shard_map/ppermute | solution.py:98
  152.9 0.9 fusion.11
  156.7 1.6 collective-permute-start.26
  162.1 2.4 %collective-permute-start.29 = (f16[1296,128]{1,0:T(8,128)(2,1)S(1)}, f16[1296,128]{1,0:T(8,128)(2,1)S(1)}, u32[]{:S(2)}, u32[]{:S(2)}) collective-permute-start(f16[1296,128]{1,0:T(8,128)(2,1)S(1)} %pad_maximum_fusion), channel_id=1, source_target_pairs={{0,8},{1,9},{2,10},{3,11},{4,12},{5,13},{6,14},{7,15},{8,0},{9,1},... | collective-permute-start | bytes 995336 | tf_op jit(solution)/shard_map/ppermute | solution.py:98
  164.6 1.0 collective-permute-start.30
  165.6 1.9 %collective-permute-start.27 = (f16[928,128]{1,0:T(8,128)(2,1)S(1)}, f16[928,128]{1,0:T(8,128)(2,1)S(1)}, u32[]{:S(2)}, u32[]{:S(2)}) collective-permute-start(f16[928,128]{1,0:T(8,128)(2,1)S(1)} %slice.468), channel_id=1, source_target_pairs={{0,3},{1,0},{2,1},{3,2},{4,7},{5,4},{6,5},{7,6},{8,11},{9,8},{10,9... | collective-permute-start | bytes 712712 | tf_op jit(solution)/shard_map/ppermute | solution.py:98
  174.4 0.9 fusion.6
  175.3 1.8 collective-permute-done.29
  177.1 0.9 fusion.5
  179.0 0.9 fusion.4
  (121 shorter events, 24.5 us)
Async XLA Ops:
  0.7 94.3 %copy-start.5 = (s32[3]{0:T(128)}, s32[3]{0:T(128)S(1)}, u32[]{:S(2)}) copy-start(s32[3]{0:T(128)S(1)} %pad_add_fusion.pos) | copy-start | bytes 40
  0.7 1.0 copy-start
  2.3 3.7 %collective-permute-start.6 = (bf16[768,128]{1,0:T(8,128)(2,1)S(1)}, bf16[768,128]{1,0:T(8,128)(2,1)S(1)}, u32[]{:S(2)}, u32[]{:S(2)}) collective-permute-start(bf16[768,128]{1,0:T(8,128)(2,1)S(1)} %get-tuple-element.16.after), channel_id=1, source_target_pairs={{0,0},{1,1},{2,2},{3,3},{4,4},{5,5},{6,6},{7,7},{8,16},{9,17},{10,... | collective-permute-start | bytes 589832 | tf_op jit(solution)/shard_map/ppermute | solution.py:98
  3.0 6.7 %collective-permute-start.7 = (bf16[768,128]{1,0:T(8,128)(2,1)S(1)}, bf16[768,128]{1,0:T(8,128)(2,1)S(1)}, u32[]{:S(2)}, u32[]{:S(2)}) collective-permute-start(bf16[768,128]{1,0:T(8,128)(2,1)S(1)} %get-tuple-element.25), channel_id=1, source_target_pairs={{0,4},{1,5},{2,6},{3,7},{4,0},{5,1},{6,2},{7,3},{8,20},{9,21},{10,... | collective-permute-start | bytes 589832 | tf_op jit(solution)/shard_map/ppermute | solution.py:98
  10.2 12.7 %collective-permute-start.8 = (bf16[2,768,128]{2,1,0:T(8,128)(2,1)S(1)}, bf16[2,768,128]{2,1,0:T(8,128)(2,1)S(1)}, u32[]{:S(2)}, u32[]{:S(2)}) collective-permute-start(bf16[2,768,128]{2,1,0:T(8,128)(2,1)S(1)} %pair.1.here), channel_id=1, source_target_pairs={{0,1},{1,2},{2,3},{3,0},{4,5},{5,6},{6,7},{7,4},{8,9},{9,10},{10,1... | collective-permute-start | bytes 1179656 | tf_op jit(solution)/shard_map/ppermute | solution.py:98
  12.8 20.2 %collective-permute-start.9 = (bf16[2,768,128]{2,1,0:T(8,128)(2,1)S(1)}, bf16[2,768,128]{2,1,0:T(8,128)(2,1)S(1)}, u32[]{:S(2)}, u32[]{:S(2)}) collective-permute-start(bf16[2,768,128]{2,1,0:T(8,128)(2,1)S(1)} %pair.1.here), channel_id=1, source_target_pairs={{0,3},{1,0},{2,1},{3,2},{4,7},{5,4},{6,5},{7,6},{8,11},{9,8},{10,9... | collective-permute-start | bytes 1179656 | tf_op jit(solution)/shard_map/ppermute | solution.py:98
  34.4 39.6 %copy-start.6 = (bf16[6,768,128]{2,1,0:T(8,128)(2,1)}, bf16[6,768,128]{2,1,0:T(8,128)(2,1)S(1)}, u32[]{:S(2)}) copy-start(bf16[6,768,128]{2,1,0:T(8,128)(2,1)S(1)} %get-tuple-element.26.g) | copy-start | bytes 3538948
  34.4 39.6 %collective-permute-start.10 = (bf16[6,768,128]{2,1,0:T(8,128)(2,1)S(1)}, bf16[6,768,128]{2,1,0:T(8,128)(2,1)S(1)}, u32[]{:S(2)}, u32[]{:S(2)}) collective-permute-start(bf16[6,768,128]{2,1,0:T(8,128)(2,1)S(1)} %get-tuple-element.26.g), channel_id=1, source_target_pairs={{0,16},{1,17},{2,18},{3,19},{4,20},{5,21},{6,22},{7,23},{8,24},{9,... | collective-permute-start | bytes 3538952 | tf_op jit(solution)/shard_map/ppermute | solution.py:98
  34.5 1.3 copy-start.1
  35.8 1.0 copy-start.4
  37.6 12.0 %collective-permute-start = (bf16[416,128]{1,0:T(8,128)(2,1)S(1)}, bf16[416,128]{1,0:T(8,128)(2,1)S(1)}, u32[]{:S(2)}, u32[]{:S(2)}) collective-permute-start(bf16[416,128]{1,0:T(8,128)(2,1)S(1)} %get-tuple-element.18), channel_id=1, source_target_pairs={{0,1},{1,2},{2,3},{3,0},{4,5},{5,6},{6,7},{7,4},{8,9},{9,10},{10,1... | collective-permute-start | bytes 319496 | tf_op jit(solution)/shard_map/ppermute | solution.py:98
  38.3 11.3 %collective-permute-start.2 = (bf16[416,128]{1,0:T(8,128)(2,1)S(1)}, bf16[416,128]{1,0:T(8,128)(2,1)S(1)}, u32[]{:S(2)}, u32[]{:S(2)}) collective-permute-start(bf16[416,128]{1,0:T(8,128)(2,1)S(1)} %get-tuple-element.20), channel_id=1, source_target_pairs={{0,3},{1,0},{2,1},{3,2},{4,7},{5,4},{6,5},{7,6},{8,11},{9,8},{10,9... | collective-permute-start | bytes 319496 | tf_op jit(solution)/shard_map/ppermute | solution.py:98
  41.5 8.1 %collective-permute-start.1 = (bf16[384,128]{1,0:T(8,128)(2,1)S(1)}, bf16[384,128]{1,0:T(8,128)(2,1)S(1)}, u32[]{:S(2)}, u32[]{:S(2)}) collective-permute-start(bf16[384,128]{1,0:T(8,128)(2,1)S(1)} %get-tuple-element.19), channel_id=1, source_target_pairs={{0,2},{1,3},{2,0},{3,1},{4,6},{5,7},{6,4},{7,5},{8,10},{9,11},{10,... | collective-permute-start | bytes 294920 | tf_op jit(solution)/shard_map/ppermute | solution.py:98
  51.1 14.5 %collective-permute-start.3 = (bf16[1984,128]{1,0:T(8,128)(2,1)S(1)}, bf16[1984,128]{1,0:T(8,128)(2,1)S(1)}, u32[]{:S(2)}, u32[]{:S(2)}) collective-permute-start(bf16[1984,128]{1,0:T(8,128)(2,1)S(1)} %get-tuple-element.21.x_own), channel_id=1, source_target_pairs={{0,4},{1,5},{2,6},{3,7},{4,0},{5,1},{6,2},{7,3},{8,12},{9,13},{10,... | collective-permute-start | bytes 1523720 | tf_op jit(solution)/shard_map/ppermute | solution.py:98
  52.6 21.4 %collective-permute-start.5 = (bf16[1984,128]{1,0:T(8,128)(2,1)S(1)}, bf16[1984,128]{1,0:T(8,128)(2,1)S(1)}, u32[]{:S(2)}, u32[]{:S(2)}) collective-permute-start(bf16[1984,128]{1,0:T(8,128)(2,1)S(1)} %get-tuple-element.23), channel_id=1, source_target_pairs={{0,12},{1,13},{2,14},{3,15},{4,8},{5,9},{6,10},{7,11},{8,4},{9,5},... | collective-permute-start | bytes 1523720 | tf_op jit(solution)/shard_map/ppermute | solution.py:98
  52.6 26.8 %collective-permute-start.4 = (bf16[1536,128]{1,0:T(8,128)(2,1)}, bf16[1536,128]{1,0:T(8,128)(2,1)}, u32[]{:S(2)}, u32[]{:S(2)}) collective-permute-start(bf16[1536,128]{1,0:T(8,128)(2,1)} %get-tuple-element.22), channel_id=1, source_target_pairs={{0,8},{1,9},{2,10},{3,11},{4,12},{5,13},{6,14},{7,15},{8,0},{9,1},... | collective-permute-start | bytes 1179656 | tf_op jit(solution)/shard_map/ppermute | solution.py:98
  75.6 19.5 %collective-permute-start.15 = (bf16[4,6,64,256]{3,2,1,0:T(8,128)(2,1)}, bf16[4,6,64,256]{3,2,1,0:T(8,128)(2,1)S(1)}, u32[]{:S(2)}, u32[]{:S(2)}) collective-permute-start(bf16[4,6,64,256]{3,2,1,0:T(8,128)(2,1)} %rims.1.mine), channel_id=1, source_target_pairs={{0,16},{1,17},{2,18},{3,19},{4,20},{5,21},{6,22},{7,23},{8,24},{9,... | collective-permute-start | bytes 2359304 | tf_op jit(solution)/shard_map/ppermute | solution.py:98
  75.6 9.9 %collective-permute-start.11 = (bf16[768,128]{1,0:T(8,128)(2,1)}, bf16[768,128]{1,0:T(8,128)(2,1)}, u32[]{:S(2)}, u32[]{:S(2)}) collective-permute-start(bf16[768,128]{1,0:T(8,128)(2,1)} %get-tuple-element.27), channel_id=1, source_target_pairs={{0,1},{1,2},{2,3},{3,0},{4,5},{5,6},{6,7},{7,4},{8,9},{9,10},{10,1... | collective-permute-start | bytes 589832 | tf_op jit(solution)/shard_map/ppermute | solution.py:98
  75.6 11.8 %collective-permute-start.12 = (bf16[768,128]{1,0:T(8,128)(2,1)}, bf16[768,128]{1,0:T(8,128)(2,1)}, u32[]{:S(2)}, u32[]{:S(2)}) collective-permute-start(bf16[768,128]{1,0:T(8,128)(2,1)} %get-tuple-element.28), channel_id=1, source_target_pairs={{0,3},{1,0},{2,1},{3,2},{4,7},{5,4},{6,5},{7,6},{8,11},{9,8},{10,9... | collective-permute-start | bytes 589832 | tf_op jit(solution)/shard_map/ppermute | solution.py:98
  85.4 9.6 %collective-permute-start.13 = (bf16[768,128]{1,0:T(8,128)(2,1)}, bf16[768,128]{1,0:T(8,128)(2,1)S(1)}, u32[]{:S(2)}, u32[]{:S(2)}) collective-permute-start(bf16[768,128]{1,0:T(8,128)(2,1)} %collective-permute-done.11.g2a), channel_id=1, source_target_pairs={{0,16},{1,17},{2,18},{3,19},{4,20},{5,21},{6,22},{7,23},{8,24},{9,... | collective-permute-start | bytes 589832 | tf_op jit(solution)/shard_map/ppermute | solution.py:98
  87.4 7.6 %collective-permute-start.14 = (bf16[768,128]{1,0:T(8,128)(2,1)}, bf16[768,128]{1,0:T(8,128)(2,1)S(1)}, u32[]{:S(2)}, u32[]{:S(2)}) collective-permute-start(bf16[768,128]{1,0:T(8,128)(2,1)} %collective-permute-done.12.g2b), channel_id=1, source_target_pairs={{0,16},{1,17},{2,18},{3,19},{4,20},{5,21},{6,22},{7,23},{8,24},{9,... | collective-permute-start | bytes 589832 | tf_op jit(solution)/shard_map/ppermute | solution.py:98
  87.4 1.3 copy-start.7
  95.1 12.3 %copy-start.3 = (bf16[4,6,64,256]{3,2,1,0:T(8,128)(2,1)}, bf16[4,6,64,256]{3,2,1,0:T(8,128)(2,1)S(1)}, u32[]{:S(2)}) copy-start(bf16[4,6,64,256]{3,2,1,0:T(8,128)(2,1)S(1)} %collective-permute-done.15.after.theirs) | copy-start | bytes 2359300
  99.3 8.1 %copy-start.2 = (f32[1744,128]{1,0:T(8,128)}, f32[1744,128]{1,0:T(8,128)S(1)}, u32[]{:S(2)}) copy-start(f32[1744,128]{1,0:T(8,128)S(1)} %far.1.after) | copy-start | bytes 2678788
  99.4 25.6 %collective-permute-start.16 = (f16[1744,128]{1,0:T(8,128)(2,1)S(1)}, f16[1744,128]{1,0:T(8,128)(2,1)S(1)}, u32[]{:S(2)}, u32[]{:S(2)}) collective-permute-start(f16[1744,128]{1,0:T(8,128)(2,1)S(1)} %convert_element_type.255), channel_id=1, source_target_pairs={{0,4},{1,5},{2,6},{3,7},{4,0},{5,1},{6,2},{7,3},{8,12},{9,13},{10,... | collective-permute-start | bytes 1339400 | tf_op jit(solution)/shard_map/ppermute | solution.py:98
  100.7 24.7 %collective-permute-start.17 = (f16[1744,128]{1,0:T(8,128)(2,1)S(1)}, f16[1744,128]{1,0:T(8,128)(2,1)S(1)}, u32[]{:S(2)}, u32[]{:S(2)}) collective-permute-start(f16[1744,128]{1,0:T(8,128)(2,1)S(1)} %convert_element_type.255), channel_id=1, source_target_pairs={{0,8},{1,9},{2,10},{3,11},{4,12},{5,13},{6,14},{7,15},{8,0},{9,1},... | collective-permute-start | bytes 1339400 | tf_op jit(solution)/shard_map/ppermute | solution.py:98
  103.4 22.1 %collective-permute-start.18 = (f16[1744,128]{1,0:T(8,128)(2,1)S(1)}, f16[1744,128]{1,0:T(8,128)(2,1)S(1)}, u32[]{:S(2)}, u32[]{:S(2)}) collective-permute-start(f16[1744,128]{1,0:T(8,128)(2,1)S(1)} %convert_element_type.255), channel_id=1, source_target_pairs={{0,12},{1,13},{2,14},{3,15},{4,8},{5,9},{6,10},{7,11},{8,4},{9,5},... | collective-permute-start | bytes 1339400 | tf_op jit(solution)/shard_map/ppermute | solution.py:98
  103.5 16.9 %collective-permute-start.19 = (f16[1296,128]{1,0:T(8,128)(2,1)S(1)}, f16[1296,128]{1,0:T(8,128)(2,1)S(1)}, u32[]{:S(2)}, u32[]{:S(2)}) collective-permute-start(f16[1296,128]{1,0:T(8,128)(2,1)S(1)} %slice.415), channel_id=1, source_target_pairs={{0,1},{1,2},{2,3},{3,0},{4,5},{5,6},{6,7},{7,4},{8,9},{9,10},{10,1... | collective-permute-start | bytes 995336 | tf_op jit(solution)/shard_map/ppermute | solution.py:98
  103.8 17.5 %collective-permute-start.20 = (f16[1296,128]{1,0:T(8,128)(2,1)S(1)}, f16[1296,128]{1,0:T(8,128)(2,1)S(1)}, u32[]{:S(2)}, u32[]{:S(2)}) collective-permute-start(f16[1296,128]{1,0:T(8,128)(2,1)S(1)} %slice.415), channel_id=1, source_target_pairs={{0,3},{1,0},{2,1},{3,2},{4,7},{5,4},{6,5},{7,6},{8,11},{9,8},{10,9... | collective-permute-start | bytes 995336 | tf_op jit(solution)/shard_map/ppermute | solution.py:98
  121.3 17.9 %collective-permute-start.21 = (f16[2592,128]{1,0:T(8,128)(2,1)S(1)}, f16[2592,128]{1,0:T(8,128)(2,1)S(1)}, u32[]{:S(2)}, u32[]{:S(2)}) collective-permute-start(f16[2592,128]{1,0:T(8,128)(2,1)S(1)} %constant_dynamic-update-slice_fusion), channel_id=1, source_target_pairs={{0,4},{1,5},{2,6},{3,7},{4,0},{5,1},{6,2},{7,3},{8,12},{9,13},{10,... | collective-permute-start | bytes 1990664 | tf_op jit(solution)/shard_map/ppermute | solution.py:98
  122.8 29.9 %collective-permute-start.22 = (f16[2592,128]{1,0:T(8,128)(2,1)S(1)}, f16[2592,128]{1,0:T(8,128)(2,1)S(1)}, u32[]{:S(2)}, u32[]{:S(2)}) collective-permute-start(f16[2592,128]{1,0:T(8,128)(2,1)S(1)} %constant_dynamic-update-slice_fusion), channel_id=1, source_target_pairs={{0,8},{1,9},{2,10},{3,11},{4,12},{5,13},{6,14},{7,15},{8,0},{9,1},... | collective-permute-start | bytes 1990664 | tf_op jit(solution)/shard_map/ppermute | solution.py:98
  124.9 29.8 %collective-permute-start.23 = (f16[2592,128]{1,0:T(8,128)(2,1)S(1)}, f16[2592,128]{1,0:T(8,128)(2,1)S(1)}, u32[]{:S(2)}, u32[]{:S(2)}) collective-permute-start(f16[2592,128]{1,0:T(8,128)(2,1)S(1)} %constant_dynamic-update-slice_fusion), channel_id=1, source_target_pairs={{0,12},{1,13},{2,14},{3,15},{4,8},{5,9},{6,10},{7,11},{8,4},{9,5},... | collective-permute-start | bytes 1990664 | tf_op jit(solution)/shard_map/ppermute | solution.py:98
  125.6 31.1 %collective-permute-start.24 = (f16[2496,128]{1,0:T(8,128)(2,1)S(1)}, f16[2496,128]{1,0:T(8,128)(2,1)S(1)}, u32[]{:S(2)}, u32[]{:S(2)}) collective-permute-start(f16[2496,128]{1,0:T(8,128)(2,1)S(1)} %get-tuple-element.60), channel_id=1, source_target_pairs={{0,1},{1,2},{2,3},{3,0},{4,5},{5,6},{6,7},{7,4},{8,9},{9,10},{10,1... | collective-permute-start | bytes 1916936 | tf_op jit(solution)/shard_map/ppermute | solution.py:98
  127.0 34.3 %collective-permute-start.25 = (f16[2512,128]{1,0:T(8,128)(2,1)S(1)}, f16[2512,128]{1,0:T(8,128)(2,1)S(1)}, u32[]{:S(2)}, u32[]{:S(2)}) collective-permute-start(f16[2512,128]{1,0:T(8,128)(2,1)S(1)} %get-tuple-element.59), channel_id=1, source_target_pairs={{0,3},{1,0},{2,1},{3,2},{4,7},{5,4},{6,5},{7,6},{8,11},{9,8},{10,9... | collective-permute-start | bytes 1929224 | tf_op jit(solution)/shard_map/ppermute | solution.py:98
  156.7 14.6 %collective-permute-start.26 = (f16[928,128]{1,0:T(8,128)(2,1)S(1)}, f16[928,128]{1,0:T(8,128)(2,1)S(1)}, u32[]{:S(2)}, u32[]{:S(2)}) collective-permute-start(f16[928,128]{1,0:T(8,128)(2,1)S(1)} %slice.463), channel_id=1, source_target_pairs={{0,1},{1,2},{2,3},{3,0},{4,5},{5,6},{6,7},{7,4},{8,9},{9,10},{10,1... | collective-permute-start | bytes 712712 | tf_op jit(solution)/shard_map/ppermute | solution.py:98
  161.5 12.8 %collective-permute-start.28 = (f16[1296,128]{1,0:T(8,128)(2,1)S(1)}, f16[1296,128]{1,0:T(8,128)(2,1)S(1)}, u32[]{:S(2)}, u32[]{:S(2)}) collective-permute-start(f16[1296,128]{1,0:T(8,128)(2,1)S(1)} %pad_maximum_fusion), channel_id=1, source_target_pairs={{0,4},{1,5},{2,6},{3,7},{4,0},{5,1},{6,2},{7,3},{8,12},{9,13},{10,... | collective-permute-start | bytes 995336 | tf_op jit(solution)/shard_map/ppermute | solution.py:98
  162.1 15.0 %collective-permute-start.29 = (f16[1296,128]{1,0:T(8,128)(2,1)S(1)}, f16[1296,128]{1,0:T(8,128)(2,1)S(1)}, u32[]{:S(2)}, u32[]{:S(2)}) collective-permute-start(f16[1296,128]{1,0:T(8,128)(2,1)S(1)} %pad_maximum_fusion), channel_id=1, source_target_pairs={{0,8},{1,9},{2,10},{3,11},{4,12},{5,13},{6,14},{7,15},{8,0},{9,1},... | collective-permute-start | bytes 995336 | tf_op jit(solution)/shard_map/ppermute | solution.py:98
  164.6 14.3 %collective-permute-start.30 = (f16[1296,128]{1,0:T(8,128)(2,1)S(1)}, f16[1296,128]{1,0:T(8,128)(2,1)S(1)}, u32[]{:S(2)}, u32[]{:S(2)}) collective-permute-start(f16[1296,128]{1,0:T(8,128)(2,1)S(1)} %pad_maximum_fusion), channel_id=1, source_target_pairs={{0,12},{1,13},{2,14},{3,15},{4,8},{5,9},{6,10},{7,11},{8,4},{9,5},... | collective-permute-start | bytes 995336 | tf_op jit(solution)/shard_map/ppermute | solution.py:98
  165.6 7.2 %collective-permute-start.27 = (f16[928,128]{1,0:T(8,128)(2,1)S(1)}, f16[928,128]{1,0:T(8,128)(2,1)S(1)}, u32[]{:S(2)}, u32[]{:S(2)}) collective-permute-start(f16[928,128]{1,0:T(8,128)(2,1)S(1)} %slice.468), channel_id=1, source_target_pairs={{0,3},{1,0},{2,1},{3,2},{4,7},{5,4},{6,5},{7,6},{8,11},{9,8},{10,9... | collective-permute-start | bytes 712712 | tf_op jit(solution)/shard_map/ppermute | solution.py:98

commit v5 on v4

--- a/solution.py
+++ b/solution.py
@@ -127,17 +127,12 @@
     )(*ins)
 
 
-def pack_grad_kernel(pos, g, g_same, g_other):
+def pack_kernel(pos, x, g, g_same, g_other, x0, x1, x2, x3, held):
+    levels, height, width, chans = x.shape
+    half, wide = levels // 2, chans // 2
     right = lax.rem(pos[1], 2)
-    wide = g.shape[-1] // 2
-    for out, half in ((g_same, right), (g_other, 1 - right)):
-        out[...] = g[:, :, :, pl.ds(pl.multiple_of(half * wide, wide), wide)].reshape(out.shape)
-
-
-def pack_input_kernel(pos, x, g, after, x0, x1, x2, x3, held):
-    del after
-    levels, height, width, chans = x.shape
-    half = levels // 2
+    for out, at in ((g_same, right), (g_other, 1 - right)):
+        out[...] = g[:, :, :, pl.ds(pl.multiple_of(at * wide, wide), wide)].reshape(out.shape)
     many = x0.shape[0]
     for block in range(4):
         at = block * (chans // 4)
@@ -147,28 +142,23 @@
     lon = pos[2]
     for step, out in enumerate((x0, x1, x2, x3)):
         out[0:many, :] = held[lax.rem(lon + step, 4)]
-    wide = chans // 2
     for out, column in ((x1, width - 1), (x3, 0)):
         rim = g[:, :, column, :].reshape(levels * height, chans)
         out[many : many + levels * height, :] = rim[:, 0:wide]
         out[many + levels * height :, :] = rim[:, wide:]
 
 
-def pair_kernel(pos, one, two, out):
-    del pos
-    out[0] = one[...]
-    out[1] = two[...]
-
-
-def split_kernel(pos, here, west, east, first, second, near):
-    del pos
+def split_kernel(pos, here, west, east, after1, after2, after3, first, second, near):
+    del pos, after1, after2, after3
     first[...] = west[0]
     second[...] = east[1]
     for at, part in enumerate((here, west, east)):
         near[2 * at : 2 * at + 2] = part[...]
 
 
-def spread_kernel(pos, x0, x1, x2, x3, g, by_x, by_y, by_d):
+def spread_kernel(pos, x0, x1, x2, x3, g, one, two, both, by_x, by_y, by_d):
+    both[0] = one[...]
+    both[1] = two[...]
     levels, height, width, chans = g.shape
     many, wide = x0.shape[0], chans // 2
     line, edge = levels * width, levels * height
@@ -397,53 +387,50 @@
 
     to_same = lambda c, a, o: (a // 2, 2 * c + a % 2, o)
     to_other = lambda c, a, o: (a // 2, 2 * c + 1 - a % 2, o)
-    g_same, g_other = call(
-        pack_grad_kernel, [jax.ShapeDtypeStruct((cells, wide), bf16)] * 2, (pos, g_cells), [], 0, "pack_grad", 16
+    many = cells // 2
+    block = jax.ShapeDtypeStruct((cells, wide), bf16)
+    g_same, g_other, x0, x1, x2, x3 = call(
+        pack_kernel,
+        [block, block]
+        + [jax.ShapeDtypeStruct((many + extra, 2 * span), bf16) for extra in (0, 2 * edge, 0, 2 * edge)],
+        (pos, x_cells, g_cells),
+        [VMEM((4, many, 2 * span), bf16)],
+        0,
+        "pack",
+        16,
     )
     g_s = move(g_same, to_same)
     g_o = move(g_other, to_other)
-    many = cells // 2
-    x0, x1, x2, x3 = call(
-        pack_input_kernel,
-        [jax.ShapeDtypeStruct((many + extra, 2 * span), bf16) for extra in (0, 2 * edge, 0, 2 * edge)],
-        (pos, x_cells, g_cells, g_same),
-        [VMEM((4, many, 2 * span), bf16)],
-        0,
-        "pack_input",
-        16,
-        held=1,
-    )
     x_r1 = move(x1, lon_by(1))
     x_r3 = move(x3, lon_by(-1))
     x_r2 = move(x2, lon_by(2))
-    pair = jax.ShapeDtypeStruct((2, cells, wide), bf16)
-    (g0,) = call(pair_kernel, [pair], (pos, g_s, g_o), [], 0, "pair", 16)
-    g1 = move(g0, lon_by(1))
-    g3 = move(g0, lon_by(-1))
 
     inner = 4 * many
     outer = inner + 2 * levels * width + 4 * edge
-    x_own, x_own_y, x_own_d = call(
+    g0, x_own, x_own_y, x_own_d = call(
         spread_kernel,
-        [jax.ShapeDtypeStruct((count, 2 * span), bf16) for count in (outer, inner, outer)],
-        (pos, x0, x_r1, x_r2, x_r3, g_cells),
+        [jax.ShapeDtypeStruct((2, cells, wide), bf16)]
+        + [jax.ShapeDtypeStruct((count, 2 * span), bf16) for count in (outer, inner, outer)],
+        (pos, x0, x_r1, x_r2, x_r3, g_cells, g_s, g_o),
         [],
         0,
         "spread",
         16,
     )
+    g1 = move(g0, lon_by(1))
+    g3 = move(g0, lon_by(-1))
     x_x = move(x_own, lat_xor(1))
     x_y = move(x_own_y, lat_xor(2))
     x_d = move(x_own_d, lat_xor(3))
-    block = jax.ShapeDtypeStruct((cells, wide), bf16)
     far_a, far_b, g_near = call(
         split_kernel,
         [block, block, jax.ShapeDtypeStruct((6, cells, wide), bf16)],
-        (pos, g0, g1, g3),
+        (pos, g0, g1, g3, x_x, x_y, x_d),
         [],
         0,
         "split",
         16,
+        held=3,
     )
     g2a = move(far_a, lon_by(1))
     g2b = move(far_b, lon_by(-1))
@@ -454,7 +441,7 @@
     (mine,) = call(
         rims_kernel,
         [jax.ShapeDtypeStruct((levels, height + 2, width + 16, chans), bf16)],
-        (pos, g_cells, x_r1, x_r3, x_x, x_d, s_near),
+        (pos, g_cells, x_r1, x_r3, x_x, x_d, far_a),
         [],
         0,
         "rims",
@@ -471,7 +458,7 @@
         ],
         in_specs=[pl.BlockSpec(memory_space=SMEM)] + [pl.BlockSpec(memory_space=VMEM)] * 4,
         out_specs=[pl.BlockSpec(memory_space=VMEM), pl.BlockSpec(memory_space=pl.ANY)],
-        cost_estimate=pl.CostEstimate(flops=0, bytes_accessed=12 * 2**20, transcendentals=0),
+        cost_estimate=pl.CostEstimate(flops=0, bytes_accessed=2**20, transcendentals=0),
         compiler_params=pltpu.CompilerParams(vmem_limit_bytes=24 * 1024 * 1024),
         name="lines",
     )(pos, x_own, x_x, x_y, x_d)

time: 180 us -> 155 us (0.86)
  waiting for transfers between devices: 71.8 us -> 47.3 us
    ppermute x31, waiting for transfers between devices: 71.8 us -> 47.3 us  [move(): return lax.ppermute(x, AXES, pairs)]
    pallas_call x8 -> x6, Pallas kernels: 16.8 us -> 15.7 us  [call(): pl.pallas_call(kernel, out_shape=outs, in_specs=[pl.BlockSpec(memory_spac...]
  transfers between devices with their start and end apart: 31 -> 31, of which waited for: 13 -> 8; matrix products, arithmetic and copies ran while one was open for 14% -> 16% of each run, Pallas kernels for 15% -> 16%
where the time goes in v5:
time: 155 us; the launch traced here: 154 us
  waiting for transfers between devices  47.3 us (31%)
  starting transfers between devices  43.6 us (28%)
  Pallas kernels  32.4 us (21%)
  other arithmetic  23.8 us (15%)
  local copies, waits for them, and re-layouts  6.16 us (4%)
    ppermute x31, waiting for transfers between devices, move(): return lax.ppermute(x, AXES, pairs)  47.3 us
    ppermute x31, starting transfers between devices, move(): return lax.ppermute(x, AXES, pairs)  43.6 us
    dynamic_update_slice x28, other arithmetic, put(): return lax.dynamic_update_slice(total, value, at)  23.3 us
    pallas_call x6, Pallas kernels, call(): pl.pallas_call(kernel, out_shape=outs, in_specs=[pl.BlockSpec(memory_spac...  15.7 us
    pallas_call x1, Pallas kernels, blocked_body(): pl.pallas_call(field_kernel, out_shape=jax.ShapeDtypeStruct((levels, heig...  11.9 us
    pallas_call x1, Pallas kernels, blocked_body(): pl.pallas_call(lines_kernel, out_shape=[jax.ShapeDtypeStruct((levels, row...  4.86 us
    unnamed x26, local copies, waits for them, and re-layouts  4.44 us
  transfers between devices with their start and end apart: 31, of which 8 were waited for; matrix products, arithmetic and copies ran while one was open for 16% of the time, Pallas kernels for 16%

profile of v5, /device:TPU:0, one launch (start us, length us, event | category | flops | bytes accessed | tf_op | source)
XLA Modules:
  0.0 154.3 jit_solution(13701745371295462304)
XLA Ops:
  0.7 1.0 copy-done.1
  1.7 1.0 copy-done.6
  4.2 3.0 %collective-permute-start.4 = (bf16[768,128]{1,0:T(8,128)(2,1)S(1)}, bf16[768,128]{1,0:T(8,128)(2,1)S(1)}, u32[]{:S(2)}, u32[]{:S(2)}) collective-permute-start(bf16[768,128]{1,0:T(8,128)(2,1)S(1)} %get-tuple-element.22), channel_id=1, source_target_pairs={{0,4},{1,5},{2,6},{3,7},{4,0},{5,1},{6,2},{7,3},{8,20},{9,21},{10,... | collective-permute-start | bytes 589832 | tf_op jit(solution)/shard_map/ppermute | solution.py:98
  7.2 1.6 %collective-permute-start = (bf16[416,128]{1,0:T(8,128)(2,1)S(1)}, bf16[416,128]{1,0:T(8,128)(2,1)S(1)}, u32[]{:S(2)}, u32[]{:S(2)}) collective-permute-start(bf16[416,128]{1,0:T(8,128)(2,1)S(1)} %get-tuple-element.18), channel_id=1, source_target_pairs={{0,1},{1,2},{2,3},{3,0},{4,5},{5,6},{6,7},{7,4},{8,9},{9,10},{10,1... | collective-permute-start | bytes 319496 | tf_op jit(solution)/shard_map/ppermute | solution.py:98
  8.8 2.2 %collective-permute-start.2 = (bf16[416,128]{1,0:T(8,128)(2,1)S(1)}, bf16[416,128]{1,0:T(8,128)(2,1)S(1)}, u32[]{:S(2)}, u32[]{:S(2)}) collective-permute-start(bf16[416,128]{1,0:T(8,128)(2,1)S(1)} %get-tuple-element.20), channel_id=1, source_target_pairs={{0,3},{1,0},{2,1},{3,2},{4,7},{5,4},{6,5},{7,6},{8,11},{9,8},{10,9... | collective-permute-start | bytes 319496 | tf_op jit(solution)/shard_map/ppermute | solution.py:98
  11.8 9.2 %collective-permute-done.1.x2 = bf16[384,128]{1,0:T(8,128)(2,1)S(1)} collective-permute-done((bf16[384,128]{1,0:T(8,128)(2,1)S(1)}, bf16[384,128]{1,0:T(8,128)(2,1)S(1)}, u32[]{:S(2)}, u32[]{:S(2)}) %collective-permute-start.1) | collective-permute-done | bytes 98336 | tf_op jit(solution)/shard_map/ppermute | solution.py:98
  21.1 1.0 copy-done.2
  22.9 2.0 %collective-permute-start.7 = (bf16[1984,128]{1,0:T(8,128)(2,1)S(1)}, bf16[1984,128]{1,0:T(8,128)(2,1)S(1)}, u32[]{:S(2)}, u32[]{:S(2)}) collective-permute-start(bf16[1984,128]{1,0:T(8,128)(2,1)S(1)} %get-tuple-element.25), channel_id=1, source_target_pairs={{0,12},{1,13},{2,14},{3,15},{4,8},{5,9},{6,10},{7,11},{8,4},{9,5},... | collective-permute-start | bytes 1523720 | tf_op jit(solution)/shard_map/ppermute | solution.py:98
  24.9 1.4 collective-permute-start.6
  26.3 3.8 %collective-permute-start.9 = (bf16[2,768,128]{2,1,0:T(8,128)(2,1)S(1)}, bf16[2,768,128]{2,1,0:T(8,128)(2,1)S(1)}, u32[]{:S(2)}, u32[]{:S(2)}) collective-permute-start(bf16[2,768,128]{2,1,0:T(8,128)(2,1)S(1)} %get-tuple-element.27.here), channel_id=1, source_target_pairs={{0,3},{1,0},{2,1},{3,2},{4,7},{5,4},{6,5},{7,6},{8,11},{9,8},{10,9... | collective-permute-start | bytes 1179656 | tf_op jit(solution)/shard_map/ppermute | solution.py:98
  30.2 15.9 %collective-permute-done.6.x_y.after2 = bf16[1536,128]{1,0:T(8,128)(2,1)S(1)} collective-permute-done((bf16[1536,128]{1,0:T(8,128)(2,1)S(1)}, bf16[1536,128]{1,0:T(8,128)(2,1)S(1)}, u32[]{:S(2)}, u32[]{:S(2)}) %collective-permute-start.6) | collective-permute-done | bytes 393248 | tf_op jit(solution)/shard_map/ppermute | solution.py:98
  46.1 1.8 %split.1 = (bf16[768,128]{1,0:T(8,128)(2,1)}, bf16[768,128]{1,0:T(8,128)(2,1)}, bf16[6,768,128]{2,1,0:T(8,128)(2,1)}) custom-call(s32[3]{0:T(128)S(1)} %pad_add_fusion.pos, bf16[2,768,128]{2,1,0:T(8,128)(2,1)S(1)} %get-tuple-element.27.here, bf16[2,768,128]{2,1,0:T(8,128)(2,1)S(1)} %collective-permute-done.8.west, ...), custom_call_target="tpu_custom_call" | custom-call | bytes 2752512 | tf_op jit(solution)/shard_map/split/pallas_call | solution.py:116
  48.0 1.0 copy-done.3
  50.5 3.5 %collective-permute-start.12 = (bf16[768,128]{1,0:T(8,128)(2,1)}, bf16[768,128]{1,0:T(8,128)(2,1)}, u32[]{:S(2)}, u32[]{:S(2)}) collective-permute-start(bf16[768,128]{1,0:T(8,128)(2,1)} %get-tuple-element.30), channel_id=1, source_target_pairs={{0,3},{1,0},{2,1},{3,2},{4,7},{5,4},{6,5},{7,6},{8,11},{9,8},{10,9... | collective-permute-start | bytes 589832 | tf_op jit(solution)/shard_map/ppermute | solution.py:98
  54.0 4.9 %lines.1 = (bf16[4,18,192,256]{3,2,1,0:T(8,128)(2,1)S(1)}, f32[27,256,512]{2,1,0:T(8,128)}) custom-call(s32[3]{0:T(128)S(1)} %pad_add_fusion.pos, bf16[1984,128]{1,0:T(8,128)(2,1)S(1)} %get-tuple-element.23.x_own, bf16[1984,128]{1,0:T(8,128)(2,1)S(1)} %collective-permute-done.5.x_x.after1.by_x, bf16[1536,128]{1,0:T(8,128)(2,1)S(1)} %collective-permute-done.6.x_y.after2, ...), custom_call_target="tpu_custom_call" | custom-call | bytes 1048576 | tf_op jit(solution)/shard_map/lines/pallas_call | solution.py:453
  58.9 1.2 collective-permute-done.11.g2a
  60.1 1.5 %collective-permute-done.12.g2b = bf16[768,128]{1,0:T(8,128)(2,1)} collective-permute-done((bf16[768,128]{1,0:T(8,128)(2,1)}, bf16[768,128]{1,0:T(8,128)(2,1)}, u32[]{:S(2)}, u32[]{:S(2)}) %collective-permute-start.12) | collective-permute-done | bytes 196640 | tf_op jit(solution)/shard_map/ppermute | solution.py:98
  61.7 7.4 %near.1.part = f32[3,384,256]{2,1,0:T(8,128)S(1)} custom-call(s32[3]{0:T(128)S(1)} %pad_add_fusion.pos, bf16[4,18,192,256]{3,2,1,0:T(8,128)(2,1)S(1)} %get-tuple-element.26.xs, bf16[6,768,128]{2,1,0:T(8,128)(2,1)} %get-tuple-element.28.g, bf16[6,768,128]{2,1,0:T(8,128)(2,1)} %collective-permute-done.10.s), custom_call_target="tpu_custom_call" | custom-call | flops 5435817984 | bytes 10616832 | tf_op jit(solution)/shard_map/near/pallas_call | solution.py:116
  69.2 4.2 %far.1.after = f32[1744,128]{1,0:T(8,128)S(1)} custom-call(s32[3]{0:T(128)S(1)} %pad_add_fusion.pos, bf16[4,18,192,256]{3,2,1,0:T(8,128)(2,1)S(1)} %get-tuple-element.26.xs, f32[3,384,256]{2,1,0:T(8,128)S(1)} %near.1.part, bf16[768,128]{1,0:T(8,128)(2,1)} %collective-permute-done.11.g2a, bf16[768,128]{1,0:T(8,128)(2,1)} %collective-permute-done.12.g2b, ...), custom_call_target="tpu_custom_call" | custom-call | flops 1811939328 | bytes 9936896 | tf_op jit(solution)/shard_map/far/pallas_call | solution.py:116
  74.3 2.3 %collective-permute-start.17 = (f16[1744,128]{1,0:T(8,128)(2,1)S(1)}, f16[1744,128]{1,0:T(8,128)(2,1)S(1)}, u32[]{:S(2)}, u32[]{:S(2)}) collective-permute-start(f16[1744,128]{1,0:T(8,128)(2,1)S(1)} %convert_element_type.255), channel_id=1, source_target_pairs={{0,8},{1,9},{2,10},{3,11},{4,12},{5,13},{6,14},{7,15},{8,0},{9,1},... | collective-permute-start | bytes 1339400 | tf_op jit(solution)/shard_map/ppermute | solution.py:98
  76.6 1.1 collective-permute-start.18
  77.8 1.3 collective-permute-start.19
  79.0 2.6 %collective-permute-start.20 = (f16[1296,128]{1,0:T(8,128)(2,1)S(1)}, f16[1296,128]{1,0:T(8,128)(2,1)S(1)}, u32[]{:S(2)}, u32[]{:S(2)}) collective-permute-start(f16[1296,128]{1,0:T(8,128)(2,1)S(1)} %slice.415), channel_id=1, source_target_pairs={{0,3},{1,0},{2,1},{3,2},{4,7},{5,4},{6,5},{7,6},{8,11},{9,8},{10,9... | collective-permute-start | bytes 995336 | tf_op jit(solution)/shard_map/ppermute | solution.py:98
  81.7 11.9 %field.1 = bf16[4,4,48,256]{3,2,1,0:T(8,128)(2,1)} custom-call(s32[3]{0:T(128)} %copy-done.7, f32[1744,128]{1,0:T(8,128)} %copy-done, bf16[4,6,64,256]{3,2,1,0:T(8,128)(2,1)} %copy-done.5, bf16[4,6,64,256]{3,2,1,0:T(8,128)(2,1)} %copy-done.4, bf16[27,256,512]{2,1,0:T(8,128)(2,1)} %bitcast.153), custom_call_target="tpu_custom_call" | custom-call | flops 10871635968 | bytes 7077888 | tf_op jit(solution)/shard_map/field/pallas_call | solution.py:512
  93.6 1.0 fusion.3
  96.3 1.7 %collective-permute-start.22 = (f16[2592,128]{1,0:T(8,128)(2,1)S(1)}, f16[2592,128]{1,0:T(8,128)(2,1)S(1)}, u32[]{:S(2)}, u32[]{:S(2)}) collective-permute-start(f16[2592,128]{1,0:T(8,128)(2,1)S(1)} %constant_dynamic-update-slice_fusion), channel_id=1, source_target_pairs={{0,8},{1,9},{2,10},{3,11},{4,12},{5,13},{6,14},{7,15},{8,0},{9,1},... | collective-permute-start | bytes 1990664 | tf_op jit(solution)/shard_map/ppermute | solution.py:98
  98.4 1.2 collective-permute-start.23
  99.9 1.5 collective-permute-start.24
  101.3 2.4 %collective-permute-start.25 = (f16[2512,128]{1,0:T(8,128)(2,1)S(1)}, f16[2512,128]{1,0:T(8,128)(2,1)S(1)}, u32[]{:S(2)}, u32[]{:S(2)}) collective-permute-start(f16[2512,128]{1,0:T(8,128)(2,1)S(1)} %get-tuple-element.61), channel_id=1, source_target_pairs={{0,3},{1,0},{2,1},{3,2},{4,7},{5,4},{6,5},{7,6},{8,11},{9,8},{10,9... | collective-permute-start | bytes 1929224 | tf_op jit(solution)/shard_map/ppermute | solution.py:98
  103.8 1.0 fusion.2
  104.9 1.0 fusion.1
  106.1 1.0 fusion
  107.1 0.9 fusion.15
  108.8 4.7 %collective-permute-done.21 = f16[2592,128]{1,0:T(8,128)(2,1)S(1)} collective-permute-done((f16[2592,128]{1,0:T(8,128)(2,1)S(1)}, f16[2592,128]{1,0:T(8,128)(2,1)S(1)}, u32[]{:S(2)}, u32[]{:S(2)}) %collective-permute-start.21) | collective-permute-done | bytes 663584 | tf_op jit(solution)/shard_map/ppermute | solution.py:98
  113.7 0.9 fusion.13
  114.6 0.9 fusion.12
  115.5 10.1 %collective-permute-done.22 = f16[2592,128]{1,0:T(8,128)(2,1)S(1)} collective-permute-done((f16[2592,128]{1,0:T(8,128)(2,1)S(1)}, f16[2592,128]{1,0:T(8,128)(2,1)S(1)}, u32[]{:S(2)}, u32[]{:S(2)}) %collective-permute-start.22) | collective-permute-done | bytes 663584 | tf_op jit(solution)/shard_map/ppermute | solution.py:98
  125.7 0.9 fusion.11
  127.7 0.9 fusion.9
  128.6 0.9 fusion.8
  129.5 2.0 %collective-permute-start.26 = (f16[928,128]{1,0:T(8,128)(2,1)S(1)}, f16[928,128]{1,0:T(8,128)(2,1)S(1)}, u32[]{:S(2)}, u32[]{:S(2)}) collective-permute-start(f16[928,128]{1,0:T(8,128)(2,1)S(1)} %slice.463), channel_id=1, source_target_pairs={{0,1},{1,2},{2,3},{3,0},{4,5},{5,6},{6,7},{7,4},{8,9},{9,10},{10,1... | collective-permute-start | bytes 712712 | tf_op jit(solution)/shard_map/ppermute | solution.py:98
  134.8 2.4 %collective-permute-start.28 = (f16[1296,128]{1,0:T(8,128)(2,1)S(1)}, f16[1296,128]{1,0:T(8,128)(2,1)S(1)}, u32[]{:S(2)}, u32[]{:S(2)}) collective-permute-start(f16[1296,128]{1,0:T(8,128)(2,1)S(1)} %pad_maximum_fusion), channel_id=1, source_target_pairs={{0,4},{1,5},{2,6},{3,7},{4,0},{5,1},{6,2},{7,3},{8,12},{9,13},{10,... | collective-permute-start | bytes 995336 | tf_op jit(solution)/shard_map/ppermute | solution.py:98
  137.2 1.7 %collective-permute-start.29 = (f16[1296,128]{1,0:T(8,128)(2,1)S(1)}, f16[1296,128]{1,0:T(8,128)(2,1)S(1)}, u32[]{:S(2)}, u32[]{:S(2)}) collective-permute-start(f16[1296,128]{1,0:T(8,128)(2,1)S(1)} %pad_maximum_fusion), channel_id=1, source_target_pairs={{0,8},{1,9},{2,10},{3,11},{4,12},{5,13},{6,14},{7,15},{8,0},{9,1},... | collective-permute-start | bytes 995336 | tf_op jit(solution)/shard_map/ppermute | solution.py:98
  139.0 1.7 %collective-permute-start.27 = (f16[928,128]{1,0:T(8,128)(2,1)S(1)}, f16[928,128]{1,0:T(8,128)(2,1)S(1)}, u32[]{:S(2)}, u32[]{:S(2)}) collective-permute-start(f16[928,128]{1,0:T(8,128)(2,1)S(1)} %slice.468), channel_id=1, source_target_pairs={{0,3},{1,0},{2,1},{3,2},{4,7},{5,4},{6,5},{7,6},{8,11},{9,8},{10,9... | collective-permute-start | bytes 712712 | tf_op jit(solution)/shard_map/ppermute | solution.py:98
  147.7 0.9 fusion.6
  148.6 3.7 %collective-permute-done.29 = f16[1296,128]{1,0:T(8,128)(2,1)S(1)} collective-permute-done((f16[1296,128]{1,0:T(8,128)(2,1)S(1)}, f16[1296,128]{1,0:T(8,128)(2,1)S(1)}, u32[]{:S(2)}, u32[]{:S(2)}) %collective-permute-start.29) | collective-permute-done | bytes 331808 | tf_op jit(solution)/shard_map/ppermute | solution.py:98
  152.4 0.9 fusion.5
  153.4 0.9 fusion.4
  (119 shorter events, 20.9 us)
Async XLA Ops:
  0.7 68.4 %copy-start.7 = (s32[3]{0:T(128)}, s32[3]{0:T(128)S(1)}, u32[]{:S(2)}) copy-start(s32[3]{0:T(128)S(1)} %pad_add_fusion.pos) | copy-start | bytes 40
  0.7 1.0 copy-start.1
  1.7 1.0 copy-start.6
  3.5 17.5 %collective-permute-start.3 = (bf16[768,128]{1,0:T(8,128)(2,1)S(1)}, bf16[768,128]{1,0:T(8,128)(2,1)S(1)}, u32[]{:S(2)}, u32[]{:S(2)}) collective-permute-start(bf16[768,128]{1,0:T(8,128)(2,1)S(1)} %get-tuple-element.21), channel_id=1, source_target_pairs={{0,0},{1,1},{2,2},{3,3},{4,4},{5,5},{6,6},{7,7},{8,16},{9,17},{10,... | collective-permute-start | bytes 589832 | tf_op jit(solution)/shard_map/ppermute | solution.py:98
  4.2 16.8 %collective-permute-start.4 = (bf16[768,128]{1,0:T(8,128)(2,1)S(1)}, bf16[768,128]{1,0:T(8,128)(2,1)S(1)}, u32[]{:S(2)}, u32[]{:S(2)}) collective-permute-start(bf16[768,128]{1,0:T(8,128)(2,1)S(1)} %get-tuple-element.22), channel_id=1, source_target_pairs={{0,4},{1,5},{2,6},{3,7},{4,0},{5,1},{6,2},{7,3},{8,20},{9,21},{10,... | collective-permute-start | bytes 589832 | tf_op jit(solution)/shard_map/ppermute | solution.py:98
  7.2 13.8 %collective-permute-start = (bf16[416,128]{1,0:T(8,128)(2,1)S(1)}, bf16[416,128]{1,0:T(8,128)(2,1)S(1)}, u32[]{:S(2)}, u32[]{:S(2)}) collective-permute-start(bf16[416,128]{1,0:T(8,128)(2,1)S(1)} %get-tuple-element.18), channel_id=1, source_target_pairs={{0,1},{1,2},{2,3},{3,0},{4,5},{5,6},{6,7},{7,4},{8,9},{9,10},{10,1... | collective-permute-start | bytes 319496 | tf_op jit(solution)/shard_map/ppermute | solution.py:98
  8.8 12.2 %collective-permute-start.2 = (bf16[416,128]{1,0:T(8,128)(2,1)S(1)}, bf16[416,128]{1,0:T(8,128)(2,1)S(1)}, u32[]{:S(2)}, u32[]{:S(2)}) collective-permute-start(bf16[416,128]{1,0:T(8,128)(2,1)S(1)} %get-tuple-element.20), channel_id=1, source_target_pairs={{0,3},{1,0},{2,1},{3,2},{4,7},{5,4},{6,5},{7,6},{8,11},{9,8},{10,9... | collective-permute-start | bytes 319496 | tf_op jit(solution)/shard_map/ppermute | solution.py:98
  11.0 10.0 %collective-permute-start.1 = (bf16[384,128]{1,0:T(8,128)(2,1)S(1)}, bf16[384,128]{1,0:T(8,128)(2,1)S(1)}, u32[]{:S(2)}, u32[]{:S(2)}) collective-permute-start(bf16[384,128]{1,0:T(8,128)(2,1)S(1)} %get-tuple-element.19), channel_id=1, source_target_pairs={{0,2},{1,3},{2,0},{3,1},{4,6},{5,7},{6,4},{7,5},{8,10},{9,11},{10,... | collective-permute-start | bytes 294920 | tf_op jit(solution)/shard_map/ppermute | solution.py:98
  21.1 1.0 copy-start.2
  22.8 23.3 %collective-permute-start.5 = (bf16[1984,128]{1,0:T(8,128)(2,1)S(1)}, bf16[1984,128]{1,0:T(8,128)(2,1)S(1)}, u32[]{:S(2)}, u32[]{:S(2)}) collective-permute-start(bf16[1984,128]{1,0:T(8,128)(2,1)S(1)} %get-tuple-element.23.x_own), channel_id=1, source_target_pairs={{0,4},{1,5},{2,6},{3,7},{4,0},{5,1},{6,2},{7,3},{8,12},{9,13},{10,... | collective-permute-start | bytes 1523720 | tf_op jit(solution)/shard_map/ppermute | solution.py:98
  22.9 23.2 %collective-permute-start.7 = (bf16[1984,128]{1,0:T(8,128)(2,1)S(1)}, bf16[1984,128]{1,0:T(8,128)(2,1)S(1)}, u32[]{:S(2)}, u32[]{:S(2)}) collective-permute-start(bf16[1984,128]{1,0:T(8,128)(2,1)S(1)} %get-tuple-element.25), channel_id=1, source_target_pairs={{0,12},{1,13},{2,14},{3,15},{4,8},{5,9},{6,10},{7,11},{8,4},{9,5},... | collective-permute-start | bytes 1523720 | tf_op jit(solution)/shard_map/ppermute | solution.py:98
  24.9 21.1 %collective-permute-start.6 = (bf16[1536,128]{1,0:T(8,128)(2,1)S(1)}, bf16[1536,128]{1,0:T(8,128)(2,1)S(1)}, u32[]{:S(2)}, u32[]{:S(2)}) collective-permute-start(bf16[1536,128]{1,0:T(8,128)(2,1)S(1)} %get-tuple-element.24), channel_id=1, source_target_pairs={{0,8},{1,9},{2,10},{3,11},{4,12},{5,13},{6,14},{7,15},{8,0},{9,1},... | collective-permute-start | bytes 1179656 | tf_op jit(solution)/shard_map/ppermute | solution.py:98
  26.3 19.7 %collective-permute-start.8 = (bf16[2,768,128]{2,1,0:T(8,128)(2,1)S(1)}, bf16[2,768,128]{2,1,0:T(8,128)(2,1)S(1)}, u32[]{:S(2)}, u32[]{:S(2)}) collective-permute-start(bf16[2,768,128]{2,1,0:T(8,128)(2,1)S(1)} %get-tuple-element.27.here), channel_id=1, source_target_pairs={{0,1},{1,2},{2,3},{3,0},{4,5},{5,6},{6,7},{7,4},{8,9},{9,10},{10,1... | collective-permute-start | bytes 1179656 | tf_op jit(solution)/shard_map/ppermute | solution.py:98
  26.3 19.7 %collective-permute-start.9 = (bf16[2,768,128]{2,1,0:T(8,128)(2,1)S(1)}, bf16[2,768,128]{2,1,0:T(8,128)(2,1)S(1)}, u32[]{:S(2)}, u32[]{:S(2)}) collective-permute-start(bf16[2,768,128]{2,1,0:T(8,128)(2,1)S(1)} %get-tuple-element.27.here), channel_id=1, source_target_pairs={{0,3},{1,0},{2,1},{3,2},{4,7},{5,4},{6,5},{7,6},{8,11},{9,8},{10,9... | collective-permute-start | bytes 1179656 | tf_op jit(solution)/shard_map/ppermute | solution.py:98
  48.0 13.7 %collective-permute-start.10 = (bf16[6,768,128]{2,1,0:T(8,128)(2,1)}, bf16[6,768,128]{2,1,0:T(8,128)(2,1)}, u32[]{:S(2)}, u32[]{:S(2)}) collective-permute-start(bf16[6,768,128]{2,1,0:T(8,128)(2,1)} %get-tuple-element.28.g), channel_id=1, source_target_pairs={{0,16},{1,17},{2,18},{3,19},{4,20},{5,21},{6,22},{7,23},{8,24},{9,... | collective-permute-start | bytes 3538952 | tf_op jit(solution)/shard_map/ppermute | solution.py:98
  48.0 1.0 copy-start.3
  49.6 23.7 %copy-start.5 = (bf16[4,6,64,256]{3,2,1,0:T(8,128)(2,1)}, bf16[4,6,64,256]{3,2,1,0:T(8,128)(2,1)S(1)}, u32[]{:S(2)}) copy-start(bf16[4,6,64,256]{3,2,1,0:T(8,128)(2,1)S(1)} %rims.1.mine) | copy-start | bytes 2359300
  49.6 19.5 %collective-permute-start.15 = (bf16[4,6,64,256]{3,2,1,0:T(8,128)(2,1)S(1)}, bf16[4,6,64,256]{3,2,1,0:T(8,128)(2,1)S(1)}, u32[]{:S(2)}, u32[]{:S(2)}) collective-permute-start(bf16[4,6,64,256]{3,2,1,0:T(8,128)(2,1)S(1)} %rims.1.mine), channel_id=1, source_target_pairs={{0,16},{1,17},{2,18},{3,19},{4,20},{5,21},{6,22},{7,23},{8,24},{9,... | collective-permute-start | bytes 2359304 | tf_op jit(solution)/shard_map/ppermute | solution.py:98
  50.2 9.9 %collective-permute-start.11 = (bf16[768,128]{1,0:T(8,128)(2,1)}, bf16[768,128]{1,0:T(8,128)(2,1)}, u32[]{:S(2)}, u32[]{:S(2)}) collective-permute-start(bf16[768,128]{1,0:T(8,128)(2,1)} %get-tuple-element.29.after), channel_id=1, source_target_pairs={{0,1},{1,2},{2,3},{3,0},{4,5},{5,6},{6,7},{7,4},{8,9},{9,10},{10,1... | collective-permute-start | bytes 589832 | tf_op jit(solution)/shard_map/ppermute | solution.py:98
  50.5 11.2 %collective-permute-start.12 = (bf16[768,128]{1,0:T(8,128)(2,1)}, bf16[768,128]{1,0:T(8,128)(2,1)}, u32[]{:S(2)}, u32[]{:S(2)}) collective-permute-start(bf16[768,128]{1,0:T(8,128)(2,1)} %get-tuple-element.30), channel_id=1, source_target_pairs={{0,3},{1,0},{2,1},{3,2},{4,7},{5,4},{6,5},{7,6},{8,11},{9,8},{10,9... | collective-permute-start | bytes 589832 | tf_op jit(solution)/shard_map/ppermute | solution.py:98
  60.1 9.0 %collective-permute-start.13 = (bf16[768,128]{1,0:T(8,128)(2,1)}, bf16[768,128]{1,0:T(8,128)(2,1)S(1)}, u32[]{:S(2)}, u32[]{:S(2)}) collective-permute-start(bf16[768,128]{1,0:T(8,128)(2,1)} %collective-permute-done.11.g2a), channel_id=1, source_target_pairs={{0,16},{1,17},{2,18},{3,19},{4,20},{5,21},{6,22},{7,23},{8,24},{9,... | collective-permute-start | bytes 589832 | tf_op jit(solution)/shard_map/ppermute | solution.py:98
  61.7 7.4 %collective-permute-start.14 = (bf16[768,128]{1,0:T(8,128)(2,1)}, bf16[768,128]{1,0:T(8,128)(2,1)S(1)}, u32[]{:S(2)}, u32[]{:S(2)}) collective-permute-start(bf16[768,128]{1,0:T(8,128)(2,1)} %collective-permute-done.12.g2b), channel_id=1, source_target_pairs={{0,16},{1,17},{2,18},{3,19},{4,20},{5,21},{6,22},{7,23},{8,24},{9,... | collective-permute-start | bytes 589832 | tf_op jit(solution)/shard_map/ppermute | solution.py:98
  69.1 12.5 %copy-start.4 = (bf16[4,6,64,256]{3,2,1,0:T(8,128)(2,1)}, bf16[4,6,64,256]{3,2,1,0:T(8,128)(2,1)S(1)}, u32[]{:S(2)}) copy-start(bf16[4,6,64,256]{3,2,1,0:T(8,128)(2,1)S(1)} %collective-permute-done.15.after.theirs) | copy-start | bytes 2359300
  73.4 8.3 %copy-start = (f32[1744,128]{1,0:T(8,128)}, f32[1744,128]{1,0:T(8,128)S(1)}, u32[]{:S(2)}) copy-start(f32[1744,128]{1,0:T(8,128)S(1)} %far.1.after) | copy-start | bytes 2678788
  73.5 24.9 %collective-permute-start.16 = (f16[1744,128]{1,0:T(8,128)(2,1)S(1)}, f16[1744,128]{1,0:T(8,128)(2,1)S(1)}, u32[]{:S(2)}, u32[]{:S(2)}) collective-permute-start(f16[1744,128]{1,0:T(8,128)(2,1)S(1)} %convert_element_type.255), channel_id=1, source_target_pairs={{0,4},{1,5},{2,6},{3,7},{4,0},{5,1},{6,2},{7,3},{8,12},{9,13},{10,... | collective-permute-start | bytes 1339400 | tf_op jit(solution)/shard_map/ppermute | solution.py:98
  74.3 25.4 %collective-permute-start.17 = (f16[1744,128]{1,0:T(8,128)(2,1)S(1)}, f16[1744,128]{1,0:T(8,128)(2,1)S(1)}, u32[]{:S(2)}, u32[]{:S(2)}) collective-permute-start(f16[1744,128]{1,0:T(8,128)(2,1)S(1)} %convert_element_type.255), channel_id=1, source_target_pairs={{0,8},{1,9},{2,10},{3,11},{4,12},{5,13},{6,14},{7,15},{8,0},{9,1},... | collective-permute-start | bytes 1339400 | tf_op jit(solution)/shard_map/ppermute | solution.py:98
  76.6 23.2 %collective-permute-start.18 = (f16[1744,128]{1,0:T(8,128)(2,1)S(1)}, f16[1744,128]{1,0:T(8,128)(2,1)S(1)}, u32[]{:S(2)}, u32[]{:S(2)}) collective-permute-start(f16[1744,128]{1,0:T(8,128)(2,1)S(1)} %convert_element_type.255), channel_id=1, source_target_pairs={{0,12},{1,13},{2,14},{3,15},{4,8},{5,9},{6,10},{7,11},{8,4},{9,5},... | collective-permute-start | bytes 1339400 | tf_op jit(solution)/shard_map/ppermute | solution.py:98
  77.8 16.9 %collective-permute-start.19 = (f16[1296,128]{1,0:T(8,128)(2,1)S(1)}, f16[1296,128]{1,0:T(8,128)(2,1)S(1)}, u32[]{:S(2)}, u32[]{:S(2)}) collective-permute-start(f16[1296,128]{1,0:T(8,128)(2,1)S(1)} %slice.415), channel_id=1, source_target_pairs={{0,1},{1,2},{2,3},{3,0},{4,5},{5,6},{6,7},{7,4},{8,9},{9,10},{10,1... | collective-permute-start | bytes 995336 | tf_op jit(solution)/shard_map/ppermute | solution.py:98
  79.0 16.5 %collective-permute-start.20 = (f16[1296,128]{1,0:T(8,128)(2,1)S(1)}, f16[1296,128]{1,0:T(8,128)(2,1)S(1)}, u32[]{:S(2)}, u32[]{:S(2)}) collective-permute-start(f16[1296,128]{1,0:T(8,128)(2,1)S(1)} %slice.415), channel_id=1, source_target_pairs={{0,3},{1,0},{2,1},{3,2},{4,7},{5,4},{6,5},{7,6},{8,11},{9,8},{10,9... | collective-permute-start | bytes 995336 | tf_op jit(solution)/shard_map/ppermute | solution.py:98
  95.6 17.9 %collective-permute-start.21 = (f16[2592,128]{1,0:T(8,128)(2,1)S(1)}, f16[2592,128]{1,0:T(8,128)(2,1)S(1)}, u32[]{:S(2)}, u32[]{:S(2)}) collective-permute-start(f16[2592,128]{1,0:T(8,128)(2,1)S(1)} %constant_dynamic-update-slice_fusion), channel_id=1, source_target_pairs={{0,4},{1,5},{2,6},{3,7},{4,0},{5,1},{6,2},{7,3},{8,12},{9,13},{10,... | collective-permute-start | bytes 1990664 | tf_op jit(solution)/shard_map/ppermute | solution.py:98
  96.3 29.3 %collective-permute-start.22 = (f16[2592,128]{1,0:T(8,128)(2,1)S(1)}, f16[2592,128]{1,0:T(8,128)(2,1)S(1)}, u32[]{:S(2)}, u32[]{:S(2)}) collective-permute-start(f16[2592,128]{1,0:T(8,128)(2,1)S(1)} %constant_dynamic-update-slice_fusion), channel_id=1, source_target_pairs={{0,8},{1,9},{2,10},{3,11},{4,12},{5,13},{6,14},{7,15},{8,0},{9,1},... | collective-permute-start | bytes 1990664 | tf_op jit(solution)/shard_map/ppermute | solution.py:98
  98.4 29.2 %collective-permute-start.23 = (f16[2592,128]{1,0:T(8,128)(2,1)S(1)}, f16[2592,128]{1,0:T(8,128)(2,1)S(1)}, u32[]{:S(2)}, u32[]{:S(2)}) collective-permute-start(f16[2592,128]{1,0:T(8,128)(2,1)S(1)} %constant_dynamic-update-slice_fusion), channel_id=1, source_target_pairs={{0,12},{1,13},{2,14},{3,15},{4,8},{5,9},{6,10},{7,11},{8,4},{9,5},... | collective-permute-start | bytes 1990664 | tf_op jit(solution)/shard_map/ppermute | solution.py:98
  99.9 29.6 %collective-permute-start.24 = (f16[2496,128]{1,0:T(8,128)(2,1)S(1)}, f16[2496,128]{1,0:T(8,128)(2,1)S(1)}, u32[]{:S(2)}, u32[]{:S(2)}) collective-permute-start(f16[2496,128]{1,0:T(8,128)(2,1)S(1)} %get-tuple-element.62), channel_id=1, source_target_pairs={{0,1},{1,2},{2,3},{3,0},{4,5},{5,6},{6,7},{7,4},{8,9},{9,10},{10,1... | collective-permute-start | bytes 1916936 | tf_op jit(solution)/shard_map/ppermute | solution.py:98
  101.3 33.2 %collective-permute-start.25 = (f16[2512,128]{1,0:T(8,128)(2,1)S(1)}, f16[2512,128]{1,0:T(8,128)(2,1)S(1)}, u32[]{:S(2)}, u32[]{:S(2)}) collective-permute-start(f16[2512,128]{1,0:T(8,128)(2,1)S(1)} %get-tuple-element.61), channel_id=1, source_target_pairs={{0,3},{1,0},{2,1},{3,2},{4,7},{5,4},{6,5},{7,6},{8,11},{9,8},{10,9... | collective-permute-start | bytes 1929224 | tf_op jit(solution)/shard_map/ppermute | solution.py:98
  129.5 15.1 %collective-permute-start.26 = (f16[928,128]{1,0:T(8,128)(2,1)S(1)}, f16[928,128]{1,0:T(8,128)(2,1)S(1)}, u32[]{:S(2)}, u32[]{:S(2)}) collective-permute-start(f16[928,128]{1,0:T(8,128)(2,1)S(1)} %slice.463), channel_id=1, source_target_pairs={{0,1},{1,2},{2,3},{3,0},{4,5},{5,6},{6,7},{7,4},{8,9},{9,10},{10,1... | collective-permute-start | bytes 712712 | tf_op jit(solution)/shard_map/ppermute | solution.py:98
  134.8 12.8 %collective-permute-start.28 = (f16[1296,128]{1,0:T(8,128)(2,1)S(1)}, f16[1296,128]{1,0:T(8,128)(2,1)S(1)}, u32[]{:S(2)}, u32[]{:S(2)}) collective-permute-start(f16[1296,128]{1,0:T(8,128)(2,1)S(1)} %pad_maximum_fusion), channel_id=1, source_target_pairs={{0,4},{1,5},{2,6},{3,7},{4,0},{5,1},{6,2},{7,3},{8,12},{9,13},{10,... | collective-permute-start | bytes 995336 | tf_op jit(solution)/shard_map/ppermute | solution.py:98
  137.2 15.1 %collective-permute-start.29 = (f16[1296,128]{1,0:T(8,128)(2,1)S(1)}, f16[1296,128]{1,0:T(8,128)(2,1)S(1)}, u32[]{:S(2)}, u32[]{:S(2)}) collective-permute-start(f16[1296,128]{1,0:T(8,128)(2,1)S(1)} %pad_maximum_fusion), channel_id=1, source_target_pairs={{0,8},{1,9},{2,10},{3,11},{4,12},{5,13},{6,14},{7,15},{8,0},{9,1},... | collective-permute-start | bytes 995336 | tf_op jit(solution)/shard_map/ppermute | solution.py:98
  139.0 14.3 %collective-permute-start.30 = (f16[1296,128]{1,0:T(8,128)(2,1)S(1)}, f16[1296,128]{1,0:T(8,128)(2,1)S(1)}, u32[]{:S(2)}, u32[]{:S(2)}) collective-permute-start(f16[1296,128]{1,0:T(8,128)(2,1)S(1)} %pad_maximum_fusion), channel_id=1, source_target_pairs={{0,12},{1,13},{2,14},{3,15},{4,8},{5,9},{6,10},{7,11},{8,4},{9,5},... | collective-permute-start | bytes 995336 | tf_op jit(solution)/shard_map/ppermute | solution.py:98
  139.0 7.1 %collective-permute-start.27 = (f16[928,128]{1,0:T(8,128)(2,1)S(1)}, f16[928,128]{1,0:T(8,128)(2,1)S(1)}, u32[]{:S(2)}, u32[]{:S(2)}) collective-permute-start(f16[928,128]{1,0:T(8,128)(2,1)S(1)} %slice.468), channel_id=1, source_target_pairs={{0,3},{1,0},{2,1},{3,2},{4,7},{5,4},{6,5},{7,6},{8,11},{9,8},{10,9... | collective-permute-start | bytes 712712 | tf_op jit(solution)/shard_map/ppermute | solution.py:98

commit v6 on v5

--- a/solution.py
+++ b/solution.py
@@ -156,29 +156,34 @@
         near[2 * at : 2 * at + 2] = part[...]
 
 
-def spread_kernel(pos, x0, x1, x2, x3, g, one, two, both, by_x, by_y, by_d):
-    both[0] = one[...]
-    both[1] = two[...]
+def spread_kernel(pos, x0, x1, x2, x3, g, one, two, both, own, rim_x, rim_d):
     levels, height, width, chans = g.shape
     many, wide = x0.shape[0], chans // 2
     line, edge = levels * width, levels * height
-    for out in (by_x, by_y, by_d):
-        for at, piece in enumerate((x0, x1, x2, x3)):
-            out[at * many : (at + 1) * many, :] = piece[0:many, :]
+    both[0] = one[...]
+    both[1] = two[...]
+    for at, piece in enumerate((x0, x1, x2, x3)):
+        own[at] = piece[0:many, :]
     even = lax.rem(pos[1], 2) == 0
     low, high = g[:, 0], g[:, height - 1]
-    for out, upward in ((by_x, even), (by_d, jnp.logical_not(even))):
+    for out, upward in ((rim_x, even), (rim_d, jnp.logical_not(even))):
         facing = jnp.where(upward, high, low).reshape(line, chans)
         for half in range(2):
-            first = 4 * many + half * line
-            out[first : first + line, :] = facing[:, half * wide : (half + 1) * wide]
-        first = 4 * many + 2 * line
+            out[half * line : (half + 1) * line, :] = facing[:, half * wide : (half + 1) * wide]
+        first = 2 * line
         out[first : first + 2 * edge, :] = x1[many : many + 2 * edge, :]
         out[first + 2 * edge : first + 4 * edge, :] = x3[many : many + 2 * edge, :]
 
 
-def rims_kernel(pos, g, from_west, from_east, by_x, by_d, after, mine):
-    del after
+def hand_kernel(pos, rim_x, rim_d, one, two, after, to_x, to_d, both):
+    del pos, after
+    to_x[...] = rim_x[...]
+    to_d[...] = rim_d[...]
+    both[0] = one[...]
+    both[1] = two[...]
+
+
+def rims_kernel(pos, g, from_west, from_east, by_x, by_d, mine):
     levels, height, width, chans = g.shape
     edge, line, wide = levels * height, levels * width, chans // 2
     many = from_west.shape[0] - 2 * edge
@@ -197,12 +202,11 @@
     columns(from_east, many, width + 8, inner)
 
     def lines(message, row, to):
-        first = 4 * many
         for half in range(2):
-            strip = message[first + half * line : first + (half + 1) * line, :]
+            strip = message[half * line : (half + 1) * line, :]
             mine[:, to, 0:width, half * wide : (half + 1) * wide] = strip.reshape(levels, width, wide)
-        columns(message, first + 2 * line, width, [(row, to)])
-        columns(message, first + 2 * line + 2 * edge, width + 8, [(row, to)])
+        columns(message, 2 * line, width, [(row, to)])
+        columns(message, 2 * line + 2 * edge, width + 8, [(row, to)])
 
     lat = pos[1]
     odd = lax.rem(lat, 2)
@@ -226,21 +230,18 @@
         mine[:, height + 1] = jnp.zeros_like(mine[:, height + 1])
 
 
-def lines_kernel(pos, x_own, x_x, x_y, x_d, xs, blank):
-    del blank
+def lines_kernel(pos, x_own, x_x, x_y, x_d, after, xs, blank):
+    del after, blank
     lat = pos[1]
     levels, rows, circle, lanes = xs.shape
     rows, width, span, half = rows - 2, circle // 4, lanes // 4, levels // 2
     height = rows // 4
-    many = half * height * width
     xs[:, 0] = jnp.zeros_like(xs[:, 0])
     xs[:, rows + 1] = jnp.zeros_like(xs[:, rows + 1])
     low = lax.broadcasted_iota(jnp.int32, (circle, 2 * span), 1) < span
     for tag, ref in enumerate((x_own, x_x, x_y, x_d)):
         start = (lat ^ tag) * height
-        strips = [
-            ref.at[pl.ds((4 - at) % 4 * many, many)].reshape(half, height, width, 2 * span) for at in range(4)
-        ]
+        strips = [ref.at[(4 - at) % 4].reshape(half, height, width, 2 * span) for at in range(4)]
 
         @pl.loop(0, half * height)
         def _(step, strips=strips, start=start):
@@ -267,11 +268,16 @@
         ] = block.T
 
 
-def add_taps(acc, gt, xs, places):
+def taps_kernel(pos, xs, g, s, g2, s2, out, gt, acc):
     levels, rows, circle, lanes = xs.shape
-    rows, width = rows - 2, circle // 4
+    rows, width, span = rows - 2, circle // 4, lanes // 4
     filters = gt.shape[0] // levels
     deep = rows * width
+    right = lax.rem(pos[1], 2)
+    for core, parts, last in ((pos[0], g, g2), (1 - pos[0], s, s2)):
+        for slot, (ref, at) in enumerate(((parts, 0), (parts, 4), (last, 0), (parts, 2))):
+            turn(gt, slot, core, ref[at + right], ref[at + 1 - right], levels)
+    acc[...] = jnp.zeros_like(acc)
 
     @pl.loop(0, 3)
     def _(lat_by):
@@ -280,51 +286,125 @@
             to = (first - lev + 1) * filters
             many = (last - first + 1) * filters
             total = acc[lat_by, to : to + many, :]
-            for slot, place in enumerate(places):
+            for place in range(4):
                 total += jnp.dot(
-                    gt[first * filters : (last + 1) * filters, slot * deep : (slot + 1) * deep],
+                    gt[first * filters : (last + 1) * filters, place * deep : (place + 1) * deep],
                     xs[lev, pl.ds(lat_by, rows), place * width : (place + 1) * width].reshape(deep, lanes),
                     preferred_element_type=jnp.float32,
                 )
             acc[lat_by, to : to + many, :] = total
 
-
-def near_kernel(pos, xs, g, s, acc, gt):
-    levels = xs.shape[0]
-    right = lax.rem(pos[1], 2)
-    for core, parts in ((pos[0], g), (1 - pos[0], s)):
-        for slot, at in enumerate((0, 4, 2)):
-            turn(gt, slot, core, parts[at + right], parts[at + 1 - right], levels)
-    acc[...] = jnp.zeros_like(acc)
-    add_taps(acc, gt, xs, (0, 1, 3))
-
-
-def far_kernel(pos, xs, part, g2a, g2b, s2a, s2b, after, out, gt, acc):
-    del after
-    levels, rows, circle, lanes = xs.shape
-    span = lanes // 4
-    filters = out.shape[1]
-    right = lax.rem(pos[1], 2) == 0
-    for core, same, other in ((pos[0], g2a, g2b), (1 - pos[0], s2a, s2b)):
-        one, two = same[...], other[...]
-        turn(gt, 0, core, jnp.where(right, one, two), jnp.where(right, two, one), levels)
-    acc[...] = part[...]
-    add_taps(acc, gt, xs, (2,))
-    scale = 1.0 / math.sqrt(levels * (rows - 2) * circle)
-
-    most = jnp.zeros((span, filters), jnp.float32)
+    scale = 1.0 / math.sqrt(levels * rows * circle)
     for lat_by in range(3):
         for lev_at in range(3):
             block = acc[lat_by, lev_at * filters : (lev_at + 1) * filters, :].T * scale
             for lon_at in range(3):
-                at = ((2 - lev_at) * 9 + lat_by * 3 + lon_at) * span
-                value = block[lon_at * span : (lon_at + 1) * span]
-                out[at : at + span, :] = value
-                most = jnp.maximum(most, jnp.abs(value))
+                out[(2 - lev_at) * 9 + lat_by * 3 + lon_at] = block[lon_at * span : (lon_at + 1) * span]
+
+
+def code_kernel(pos, held, after, out, late):
+    del pos, after
+    taps, span, filters = held.shape
+    most = jnp.abs(held[0])
+    for tap in range(1, taps):
+        most = jnp.maximum(most, jnp.abs(held[tap]))
     top = jnp.maximum(jnp.max(most, axis=(0, 1), keepdims=True), 1e-30)
-    power = jnp.broadcast_to(jnp.ceil(jnp.log(top) * (1.0 / math.log(2.0))), (16, filters))
-    out[27 * span :, :] = power
-    out[0 : 27 * span, :] = out[0 : 27 * span, :] * jnp.exp2(14.0 - power[0:1])
+    power = jnp.ceil(jnp.log(top) * (1.0 / math.log(2.0))) - 15.0
+    unit = jnp.broadcast_to(jnp.exp2(power), (16, filters)).astype(out.dtype).astype(jnp.float32)
+    shrink = 1.0 / unit[0:1]
+    skip = out.shape[0] - late.shape[0]
+    for tap in range(27):
+        value = held[tap] * shrink
+        square = value * value
+        code = (square * square * square * value * jnp.abs(value)).astype(out.dtype)
+        out[tap * span : (tap + 1) * span, :] = code
+        if tap * span >= skip:
+            late[tap * span - skip : (tap + 1) * span - skip, :] = code
+    out[27 * span :, :] = unit.astype(out.dtype)
+    late[27 * span - skip :, :] = unit.astype(out.dtype)
+
+
+def join_kernel(pos, own, x, y, d, west, east, after, both, by_3, by_1):
+    del pos, after
+    size = west.shape[0]
+    cut = own.shape[0] - size
+    end = own.shape[0] - 16
+    half = by_3.shape[0] - 4 * (cut + 16)
+    both[0:size, :] = west[...]
+    both[size:, :] = east[...]
+    by_3[0:half, :] = west[0:half, :]
+    by_1[0 : size - half, :] = east[half:, :]
+    for out, at in ((by_3, half), (by_1, size - half)):
+        for piece in (own, x, y, d):
+            out[at : at + cut, :] = piece[0:cut, :]
+            out[at + cut : at + cut + 16, :] = piece[end:, :]
+            at += cut + 16
+
+
+def across_kernel(pos, by_3, by_1, after, late, early_3, early_1):
+    del pos, after
+    size, many = late.shape[0], early_3.shape[0]
+    half = by_3.shape[0] - 2 * many
+    late[0:half, :] = by_3[0:half, :]
+    late[half:, :] = by_1[0 : size - half, :]
+    early_3[...] = by_3[half : half + many, :]
+    early_1[...] = by_1[size - half + many :, :]
+
+
+def unpack_kernel(pos, *refs, pieces, span):
+    count = 1 + max(piece[0] for piece in pieces)
+    sources = refs[:count]
+    total, buffers, sems = refs[-3:]
+    wide = buffers.shape[-1]
+
+    def target(piece):
+        _, _, _, first, many, tag, step = piece
+        lon_at = lax.rem(pos[2] + step, 4) * span
+        lat_at = (pos[1] ^ tag) * wide
+        return total.at[
+            pl.ds(first, many),
+            pl.ds(pl.multiple_of(lon_at, span), span),
+            pl.ds(pl.multiple_of(lat_at, wide), wide),
+        ]
+
+    def copy(at):
+        piece = pieces[at]
+        return pltpu.make_async_copy(buffers.at[at % 2, pl.ds(0, piece[4])], target(piece), sems.at[at % 2])
+
+    for at, (which, row, power_row, _, many, _, _) in enumerate(pieces):
+        if at >= 2:
+            copy(at - 2).wait()
+        source = sources[which]
+        unit = source[power_row : power_row + 16, :].astype(jnp.float32)[0:1]
+
+        @pl.loop(0, many)
+        def _(tap, source=source, row=row, unit=unit, at=at):
+            code = source[pl.ds(pl.multiple_of(row + tap * span, 16), span), :].astype(jnp.float32)
+            root = jnp.sqrt(jnp.sqrt(jnp.sqrt(jnp.abs(code)))) * unit
+            buffers[at % 2, tap] = jnp.where(code < 0, -root, root)
+
+        copy(at).start()
+    for at in range(max(len(pieces) - 2, 0), len(pieces)):
+        copy(at).wait()
+
+
+def unpack(pos, total, sources, after, pieces, span, name):
+    most = max(piece[4] for piece in pieces)
+    wide = sources[0].shape[-1]
+    ins = (pos, *sources, *after, total)
+    return pl.pallas_call(
+        lambda *refs: unpack_kernel(*refs, pieces=pieces, span=span),
+        out_shape=jax.ShapeDtypeStruct(total.shape, total.dtype),
+        in_specs=[pl.BlockSpec(memory_space=SMEM)]
+        + [pl.BlockSpec(memory_space=VMEM)] * len(sources)
+        + [pl.BlockSpec(memory_space=pl.ANY)] * (len(after) + 1),
+        out_specs=pl.BlockSpec(memory_space=pl.ANY),
+        scratch_shapes=[VMEM((2, most, span, wide), jnp.float32), pltpu.SemaphoreType.DMA((2,))],
+        input_output_aliases={len(ins) - 1: 0},
+        cost_estimate=pl.CostEstimate(flops=0, bytes_accessed=4 * 2**20, transcendentals=0),
+        compiler_params=pltpu.CompilerParams(vmem_limit_bytes=24 * 1024 * 1024),
+        name=name,
+    )(*ins)
 
 
 def field_kernel(pos, after, mine, theirs, w, out, copies, acc):
@@ -405,12 +485,10 @@
     x_r3 = move(x3, lon_by(-1))
     x_r2 = move(x2, lon_by(2))
 
-    inner = 4 * many
-    outer = inner + 2 * levels * width + 4 * edge
-    g0, x_own, x_own_y, x_own_d = call(
+    rim = jax.ShapeDtypeStruct((2 * levels * width + 4 * edge, 2 * span), bf16)
+    g0, x_own, rim_x, rim_d = call(
         spread_kernel,
-        [jax.ShapeDtypeStruct((2, cells, wide), bf16)]
-        + [jax.ShapeDtypeStruct((count, 2 * span), bf16) for count in (outer, inner, outer)],
+        [jax.ShapeDtypeStruct((2, cells, wide), bf16), jax.ShapeDtypeStruct((4, many, 2 * span), bf16), rim, rim],
         (pos, x0, x_r1, x_r2, x_r3, g_cells, g_s, g_o),
         [],
         0,
@@ -420,8 +498,8 @@
     g1 = move(g0, lon_by(1))
     g3 = move(g0, lon_by(-1))
     x_x = move(x_own, lat_xor(1))
-    x_y = move(x_own_y, lat_xor(2))
-    x_d = move(x_own_d, lat_xor(3))
+    x_y = move(x_own, lat_xor(2))
+    x_d = move(x_own, lat_xor(3))
     far_a, far_b, g_near = call(
         split_kernel,
         [block, block, jax.ShapeDtypeStruct((6, cells, wide), bf16)],
@@ -435,20 +513,6 @@
     g2a = move(far_a, lon_by(1))
     g2b = move(far_b, lon_by(-1))
     s_near = move(g_near, sibling)
-    s2a = move(g2a, sibling)
-    s2b = move(g2b, sibling)
-
-    (mine,) = call(
-        rims_kernel,
-        [jax.ShapeDtypeStruct((levels, height + 2, width + 16, chans), bf16)],
-        (pos, g_cells, x_r1, x_r3, x_x, x_d, far_a),
-        [],
-        0,
-        "rims",
-        16,
-        held=1,
-    )
-    theirs = move(mine, sibling)
 
     xs, total = pl.pallas_call(
         lines_kernel,
@@ -456,57 +520,55 @@
             jax.ShapeDtypeStruct((levels, rows + 2, circle, 4 * span), bf16),
             jax.ShapeDtypeStruct((27, chans, filters), f32),
         ],
-        in_specs=[pl.BlockSpec(memory_space=SMEM)] + [pl.BlockSpec(memory_space=VMEM)] * 4,
-        out_specs=[pl.BlockSpec(memory_space=VMEM), pl.BlockSpec(memory_space=pl.ANY)],
+        in_specs=[pl.BlockSpec(memory_space=SMEM)]
+        + [pl.BlockSpec(memory_space=VMEM)] * 4
+        + [pl.BlockSpec(memory_space=pl.ANY)],
+        out_specs=[pl.BlockSpec(memory_space=VMEM)] + [pl.BlockSpec(memory_space=pl.ANY)],
         cost_estimate=pl.CostEstimate(flops=0, bytes_accessed=2**20, transcendentals=0),
         compiler_params=pltpu.CompilerParams(vmem_limit_bytes=24 * 1024 * 1024),
         name="lines",
-    )(pos, x_own, x_x, x_y, x_d)
-
-    work = 2 * 27 * span * wide * rows * circle * levels
-    (part,) = call(
-        near_kernel,
-        [jax.ShapeDtypeStruct((3, 3 * wide, 4 * span), f32)],
-        (pos, xs, g_near, s_near),
-        [VMEM((levels * wide, 3 * rows * width), bf16)],
-        work,
-        "near",
-        28,
-    )
-    (grads,) = call(
-        far_kernel,
-        [jax.ShapeDtypeStruct((27 * span + 16, wide), f32)],
-        (pos, xs, part, g2a, g2b, s2a, s2b, theirs),
-        [VMEM((levels * wide, rows * width), bf16), VMEM((3, 3 * wide, 4 * span), f32)],
-        work // 3,
-        "far",
-        28,
+    )(pos, x_own, x_x, x_y, x_d, far_a)
+    rim_x, rim_d, g2 = call(
+        hand_kernel,
+        [rim, rim, jax.ShapeDtypeStruct((2, cells, wide), bf16)],
+        (pos, rim_x, rim_d, g2a, g2b, xs),
+        [],
+        0,
+        "hand",
+        16,
         held=1,
     )
-    own = grads.astype(jnp.float16)
+    s2 = move(g2, sibling)
+    by_x = move(rim_x, lat_xor(1))
+    by_d = move(rim_d, lat_xor(3))
+
+    (mine,) = call(
+        rims_kernel,
+        [jax.ShapeDtypeStruct((levels, height + 2, width + 16, chans), bf16)],
+        (pos, g_cells, x_r1, x_r3, by_x, by_d),
+        [],
+        0,
+        "rims",
+        16,
+    )
+    theirs = move(mine, sibling)
 
     early = 7
     cut, end = early * span, 27 * span
-    size = own.shape[0] - cut
+    size = end + 16 - cut
     half = size // 32 * 16
-    step_rows = cut + 16
-
-    def to_plane(share):
-        return [move(share, lat_xor(tag)) for tag in (1, 2, 3)]
-
-    late = own[cut:]
-    from_3 = move(late, lon_by(1))
-    from_1 = move(late, lon_by(-1))
-    plane = [own] + to_plane(own)
-    block = [x for p in plane for x in (p[:cut], p[end:])]
-    both = to_plane(jnp.concatenate([from_3, from_1]))
-    by_3 = move(jnp.concatenate([from_3[:half]] + block), lon_by(1))
-    by_1 = move(jnp.concatenate([from_1[half:]] + block), lon_by(-1))
-    from_2 = jnp.concatenate([by_3[:half], by_1[: size - half]])
-    across = to_plane(from_2)
-    early_3, early_1 = by_3[half:], by_1[size - half :]
-    early_2a = move(early_3[: 2 * step_rows], lon_by(1))
-    early_2b = move(early_1[2 * step_rows :], lon_by(-1))
+    first_rows = cut + 16
+    slab = lambda count: jax.ShapeDtypeStruct((count, wide), bf16)
+    (grads,) = call(
+        taps_kernel,
+        [jax.ShapeDtypeStruct((27, span, wide), f32)],
+        (pos, xs, g_near, s_near, g2, s2),
+        [VMEM((levels * wide, rows * circle), bf16), VMEM((3, 3 * wide, 4 * span), f32)],
+        2 * 27 * span * wide * rows * circle * levels,
+        "taps",
+        28,
+    )
+    own, late = call(code_kernel, [slab(end + 16), slab(size)], (pos, grads, theirs), [], 0, "code", 16, held=1)
 
     whole = lambda t: (0, 0, 0, 0)
     field = pl.pallas_call(
@@ -530,37 +592,61 @@
         ),
         compiler_params=pltpu.CompilerParams(vmem_limit_bytes=56 * 1024 * 1024),
         name="field",
-    )(pos, grads, mine, theirs, taps)
-
-    def put(total, piece, power, first, last, tag, step):
-        factor = jnp.exp2(power[0:1].astype(f32) - 14.0)
-        value = piece.reshape(last - first, span, wide).astype(f32) * factor[None]
-        at = (first, lax.rem(lon + step, 4) * span, (lat ^ tag) * wide)
-        return lax.dynamic_update_slice(total, value, at)
-
-    def put_late(total, piece, tag, step):
-        return put(total, piece[: end - cut], piece[end - cut :], early, 27, tag, step)
-
-    def put_early(total, pieces, tags, step):
-        for at, tag in enumerate(tags):
-            piece = pieces[at * step_rows : (at + 1) * step_rows]
-            total = put(total, piece[:cut], piece[cut:], 0, early, tag, step)
-        return total
-
-    for tag, piece in enumerate(plane):
-        total = put(total, piece[:end], piece[end:], 0, 27, tag, 0)
-    total = put_late(total, from_3, 0, 3)
-    total = put_late(total, from_1, 0, 1)
-    for tag, piece in enumerate(both):
-        total = put_late(total, piece[:size], tag + 1, 3)
-        total = put_late(total, piece[size:], tag + 1, 1)
-    total = put_early(total, early_3, (0, 1, 2, 3), 3)
-    total = put_early(total, early_1, (0, 1, 2, 3), 1)
-    total = put_late(total, from_2, 0, 2)
-    total = put_early(total, early_2a, (0, 1), 2)
-    total = put_early(total, early_2b, (2, 3), 2)
-    for tag, piece in enumerate(across):
-        total = put_late(total, piece, tag + 1, 2)
+    )(pos, own, mine, theirs, taps)
+
+    def to_plane(share):
+        return [move(share, lat_xor(tag)) for tag in (1, 2, 3)]
+
+    from_3 = move(late, lon_by(1))
+    from_1 = move(late, lon_by(-1))
+    plane = [own] + to_plane(own)
+    pair, z_3, z_1 = call(
+        join_kernel,
+        [slab(2 * size), slab(half + 4 * first_rows), slab(size - half + 4 * first_rows)],
+        (pos, *plane, from_3, from_1, field),
+        [],
+        0,
+        "join",
+        16,
+        held=1,
+    )
+    both = to_plane(pair)
+    by_3 = move(z_3, lon_by(1))
+    by_1 = move(z_1, lon_by(-1))
+    def late_piece(which, tag, step, row=0):
+        return (which, row, row + size - 16, early, 27 - early, tag, step)
+
+    def early_pieces(which, row, tags, step):
+        return [
+            (which, row + at * first_rows, row + at * first_rows + cut, 0, early, tag, step)
+            for at, tag in enumerate(tags)
+        ]
+
+    pieces = [(tag, 0, end, 0, 27, tag, 0) for tag in range(4)]
+    pieces += [late_piece(4, 0, 3), late_piece(5, 0, 1)]
+    total = unpack(pos, total, plane + [from_3, from_1], [pair], pieces, span, "unpack_1")
+    from_2, early_3, early_1 = call(
+        across_kernel,
+        [slab(size), slab(2 * first_rows), slab(2 * first_rows)],
+        (pos, by_3, by_1, total),
+        [],
+        0,
+        "across",
+        16,
+        held=1,
+    )
+    across = to_plane(from_2)
+    early_2a = move(early_3, lon_by(1))
+    early_2b = move(early_1, lon_by(-1))
+
+    pieces = [late_piece(tag - 1, tag, 3) for tag in (1, 2, 3)]
+    pieces += [late_piece(tag - 1, tag, 1, size) for tag in (1, 2, 3)]
+    pieces += early_pieces(3, half, (0, 1, 2, 3), 3) + early_pieces(4, size - half, (0, 1, 2, 3), 1)
+    pieces += [late_piece(5, 0, 2)]
+    total = unpack(pos, total, both + [by_3, by_1, from_2], [], pieces, span, "unpack_2")
+    pieces = early_pieces(0, 0, (0, 1), 2) + early_pieces(1, 0, (2, 3), 2)
+    pieces += [late_piece(tag + 1, tag, 2) for tag in (1, 2, 3)]
+    total = unpack(pos, total, [early_2a, early_2b] + across, [], pieces, span, "unpack_3")
     return (jnp.transpose(field, (3, 0, 1, 2)), jnp.transpose(total, (1, 0, 2)))
 
 

time: 155 us -> 170 us (1.097)
  other arithmetic: 23.8 us -> 0.08 us
  Pallas kernels: 32.4 us -> 54.3 us
  waiting for transfers between devices: 47.3 us -> 61 us
  local copies, waits for them, and re-layouts: 6.16 us -> 12 us
  starting transfers between devices: 43.6 us -> 40.8 us
    pallas_call x0 -> x3, Pallas kernels: none -> 23.4 us  [unpack(): pl.pallas_call(lambda *refs: unpack_kernel(*refs, pieces=pieces, span=spa...]
    dynamic_update_slice x28 -> x0, other arithmetic: 23.3 us -> none  [put(): return lax.dynamic_update_slice(total, value, at)]
    ppermute x31 -> x32, waiting for transfers between devices: 47.3 us -> 61 us  [move(): return lax.ppermute(x, AXES, pairs)]
    unnamed x26, local copies, waits for them, and re-layouts: 4.44 us -> 12 us
    ppermute x31 -> x32, starting transfers between devices: 43.6 us -> 40.8 us  [move(): return lax.ppermute(x, AXES, pairs)]
    pallas_call x6 -> x9, Pallas kernels: 15.7 us -> 14.2 us  [call(): pl.pallas_call(kernel, out_shape=outs, in_specs=[pl.BlockSpec(memory_spac...]
  transfers between devices with their start and end apart: 31 -> 32, of which waited for: 8 -> 10; matrix products, arithmetic and copies ran while one was open for 16% -> 0% of each run, Pallas kernels for 16% -> 27%
where the time goes in v6:
time: 170 us; the launch traced here: 169 us
  waiting for transfers between devices  61 us (36%)
  Pallas kernels  54.3 us (32%)
  starting transfers between devices  40.8 us (24%)
  local copies, waits for them, and re-layouts  12 us (7%)
    ppermute x32, waiting for transfers between devices, move(): return lax.ppermute(x, AXES, pairs)  61 us
    ppermute x32, starting transfers between devices, move(): return lax.ppermute(x, AXES, pairs)  40.8 us
    pallas_call x3, Pallas kernels, unpack(): pl.pallas_call(lambda *refs: unpack_kernel(*refs, pieces=pieces, span=spa...  23.4 us
    pallas_call x9, Pallas kernels, call(): pl.pallas_call(kernel, out_shape=outs, in_specs=[pl.BlockSpec(memory_spac...  14.2 us
    unnamed x26, local copies, waits for them, and re-layouts  12 us
    pallas_call x1, Pallas kernels, blocked_body(): pl.pallas_call(field_kernel, out_shape=jax.ShapeDtypeStruct((levels, heig...  11.9 us
    pallas_call x1, Pallas kernels, blocked_body(): pl.pallas_call(lines_kernel, out_shape=[jax.ShapeDtypeStruct((levels, row...  4.86 us
  transfers between devices with their start and end apart: 32, of which 10 were waited for; matrix products, arithmetic and copies ran while one was open for 0% of the time, Pallas kernels for 27%

profile of v6, /device:TPU:0, one launch (start us, length us, event | category | flops | bytes accessed | tf_op | source)
XLA Modules:
  0.0 169.2 jit_solution(16107852964628299155)
XLA Ops:
  0.7 1.0 copy-done.1
  1.7 1.0 copy-done.10
  2.7 0.8 pack.1
  3.5 0.7 collective-permute-start.3
  4.2 3.0 %collective-permute-start.4 = (bf16[768,128]{1,0:T(8,128)(2,1)S(1)}, bf16[768,128]{1,0:T(8,128)(2,1)S(1)}, u32[]{:S(2)}, u32[]{:S(2)}) collective-permute-start(bf16[768,128]{1,0:T(8,128)(2,1)S(1)} %get-tuple-element.33), channel_id=1, source_target_pairs={{0,4},{1,5},{2,6},{3,7},{4,0},{5,1},{6,2},{7,3},{8,20},{9,21},{10,... | collective-permute-start | bytes 589832 | tf_op jit(solution)/shard_map/ppermute | solution.py:98
  7.2 1.6 collective-permute-start
  8.8 2.2 %collective-permute-start.2 = (bf16[416,128]{1,0:T(8,128)(2,1)S(1)}, bf16[416,128]{1,0:T(8,128)(2,1)S(1)}, u32[]{:S(2)}, u32[]{:S(2)}) collective-permute-start(bf16[416,128]{1,0:T(8,128)(2,1)S(1)} %get-tuple-element.31), channel_id=1, source_target_pairs={{0,3},{1,0},{2,1},{3,2},{4,7},{5,4},{6,5},{7,6},{8,11},{9,8},{10,9... | collective-permute-start | bytes 319496 | tf_op jit(solution)/shard_map/ppermute | solution.py:98
  11.0 0.8 collective-permute-start.1
  11.8 9.2 %collective-permute-done.1.x2 = bf16[384,128]{1,0:T(8,128)(2,1)S(1)} collective-permute-done((bf16[384,128]{1,0:T(8,128)(2,1)S(1)}, bf16[384,128]{1,0:T(8,128)(2,1)S(1)}, u32[]{:S(2)}, u32[]{:S(2)}) %collective-permute-start.1) | collective-permute-done | bytes 98336 | tf_op jit(solution)/shard_map/ppermute | solution.py:98
  21.1 1.0 copy-done.2
  22.7 2.3 %collective-permute-start.9 = (bf16[2,768,128]{2,1,0:T(8,128)(2,1)S(1)}, bf16[2,768,128]{2,1,0:T(8,128)(2,1)S(1)}, u32[]{:S(2)}, u32[]{:S(2)}) collective-permute-start(bf16[2,768,128]{2,1,0:T(8,128)(2,1)S(1)} %get-tuple-element.35.here), channel_id=1, source_target_pairs={{0,3},{1,0},{2,1},{3,2},{4,7},{5,4},{6,5},{7,6},{8,11},{9,8},{10,9... | collective-permute-start | bytes 1179656 | tf_op jit(solution)/shard_map/ppermute | solution.py:98
  25.6 1.4 collective-permute-start.6
  27.0 1.5 collective-permute-start.5
  28.4 6.0 %collective-permute-done.9.east = bf16[2,768,128]{2,1,0:T(8,128)(2,1)S(1)} collective-permute-done((bf16[2,768,128]{2,1,0:T(8,128)(2,1)S(1)}, bf16[2,768,128]{2,1,0:T(8,128)(2,1)S(1)}, u32[]{:S(2)}, u32[]{:S(2)}) %collective-permute-start.9) | collective-permute-done | bytes 393248 | tf_op jit(solution)/shard_map/ppermute | solution.py:98
  34.5 8.3 %collective-permute-done.8.west = bf16[2,768,128]{2,1,0:T(8,128)(2,1)S(1)} collective-permute-done((bf16[2,768,128]{2,1,0:T(8,128)(2,1)S(1)}, bf16[2,768,128]{2,1,0:T(8,128)(2,1)S(1)}, u32[]{:S(2)}, u32[]{:S(2)}) %collective-permute-start.8) | collective-permute-done | bytes 393248 | tf_op jit(solution)/shard_map/ppermute | solution.py:98
  42.8 1.5 collective-permute-done.6.after2.x_y
  45.0 3.6 %collective-permute-start.12 = (bf16[768,128]{1,0:T(8,128)(2,1)S(1)}, bf16[768,128]{1,0:T(8,128)(2,1)S(1)}, u32[]{:S(2)}, u32[]{:S(2)}) collective-permute-start(bf16[768,128]{1,0:T(8,128)(2,1)S(1)} %get-tuple-element.41), channel_id=1, source_target_pairs={{0,3},{1,0},{2,1},{3,2},{4,7},{5,4},{6,5},{7,6},{8,11},{9,8},{10,9... | collective-permute-start | bytes 589832 | tf_op jit(solution)/shard_map/ppermute | solution.py:98
  48.6 4.9 %lines.1 = (bf16[4,18,192,256]{3,2,1,0:T(8,128)(2,1)S(1)}, f32[27,256,512]{2,1,0:T(8,128)}) custom-call(s32[3]{0:T(128)S(1)} %pad_add_fusion.pos.refs_0_, bf16[4,384,128]{2,1,0:T(8,128)(2,1)S(1)} %get-tuple-element.34.x_own, bf16[4,384,128]{2,1,0:T(8,128)(2,1)S(1)} %collective-permute-done.5.after1.x_x, ...), custom_call_target="tpu_custom_call" | custom-call | bytes 1048576 | tf_op jit(solution)/shard_map/lines/pallas_call | solution.py:517
  53.8 4.5 %collective-permute-done.11.one = bf16[768,128]{1,0:T(8,128)(2,1)S(1)} collective-permute-done((bf16[768,128]{1,0:T(8,128)(2,1)S(1)}, bf16[768,128]{1,0:T(8,128)(2,1)S(1)}, u32[]{:S(2)}, u32[]{:S(2)}) %collective-permute-start.11) | collective-permute-done | bytes 196640 | tf_op jit(solution)/shard_map/ppermute | solution.py:98
  59.0 1.5 collective-permute-start.14
  60.5 1.5 collective-permute-start.15
  62.0 3.0 %collective-permute-done.14.by_x = bf16[448,128]{1,0:T(8,128)(2,1)S(1)} collective-permute-done((bf16[448,128]{1,0:T(8,128)(2,1)S(1)}, bf16[448,128]{1,0:T(8,128)(2,1)S(1)}, u32[]{:S(2)}, u32[]{:S(2)}) %collective-permute-start.14) | collective-permute-done | bytes 114720 | tf_op jit(solution)/shard_map/ppermute | solution.py:98
  65.0 2.9 %collective-permute-done.15.by_d = bf16[448,128]{1,0:T(8,128)(2,1)S(1)} collective-permute-done((bf16[448,128]{1,0:T(8,128)(2,1)S(1)}, bf16[448,128]{1,0:T(8,128)(2,1)S(1)}, u32[]{:S(2)}, u32[]{:S(2)}) %collective-permute-start.15) | collective-permute-done | bytes 114720 | tf_op jit(solution)/shard_map/ppermute | solution.py:98
  67.9 1.0 copy-done.3
  68.9 0.7 rims.1.mine
  69.7 8.6 %taps.1.held = f32[27,64,128]{2,1,0:T(8,128)S(1)} custom-call(s32[3]{0:T(128)S(1)} %pad_add_fusion.pos.refs_0_, bf16[4,18,192,256]{3,2,1,0:T(8,128)(2,1)S(1)} %get-tuple-element.37.after.xs, bf16[6,768,128]{2,1,0:T(8,128)(2,1)S(1)} %get-tuple-element.38.g, bf16[6,768,128]{2,1,0:T(8,128)(2,1)S(1)} %collective-permute-done.10.s, ...), custom_call_target="tpu_custom_call" | custom-call | flops 5435817984 | bytes 11108352 | tf_op jit(solution)/shard_map/taps/pallas_call | solution.py:116
  78.3 1.0 code.1
  79.3 1.8 %collective-permute-start.21 = (bf16[1296,128]{1,0:T(8,128)(2,1)S(1)}, bf16[1296,128]{1,0:T(8,128)(2,1)S(1)}, u32[]{:S(2)}, u32[]{:S(2)}) collective-permute-start(bf16[1296,128]{1,0:T(8,128)(2,1)S(1)} %get-tuple-element.46), channel_id=1, source_target_pairs={{0,3},{1,0},{2,1},{3,2},{4,7},{5,4},{6,5},{7,6},{8,11},{9,8},{10,9... | collective-permute-start | bytes 995336 | tf_op jit(solution)/shard_map/ppermute | solution.py:98
  81.3 1.4 collective-permute-start.19
  83.4 1.5 collective-permute-start.17
  84.8 11.9 %field.1.after = bf16[4,4,48,256]{3,2,1,0:T(8,128)(2,1)} custom-call(s32[3]{0:T(128)} %copy-done.11, bf16[1744,128]{1,0:T(8,128)(2,1)} %copy-done.4, bf16[4,6,64,256]{3,2,1,0:T(8,128)(2,1)} %copy-done.7, bf16[4,6,64,256]{3,2,1,0:T(8,128)(2,1)} %copy-done.8, bf16[27,256,512]{2,1,0:T(8,128)(2,1)} %bitcast.14), custom_call_target="tpu_custom_call" | custom-call | flops 10871635968 | bytes 7077888 | tf_op jit(solution)/shard_map/field/pallas_call | solution.py:574
  96.7 7.3 %collective-permute-done.18.y.refs_3_ = bf16[1744,128]{1,0:T(8,128)(2,1)S(1)} collective-permute-done((bf16[1744,128]{1,0:T(8,128)(2,1)S(1)}, bf16[1744,128]{1,0:T(8,128)(2,1)S(1)}, u32[]{:S(2)}, u32[]{:S(2)}) %collective-permute-start.18) | collective-permute-done | bytes 446496 | tf_op jit(solution)/shard_map/ppermute | solution.py:98
  104.0 1.0 copy-done.5
  105.0 1.0 copy-done.9
  106.0 0.7 join.1
  106.8 1.5 collective-permute-start.31
  108.3 3.4 %collective-permute-start.23 = (bf16[2512,128]{1,0:T(8,128)(2,1)S(1)}, bf16[2512,128]{1,0:T(8,128)(2,1)S(1)}, u32[]{:S(2)}, u32[]{:S(2)}) collective-permute-start(bf16[2512,128]{1,0:T(8,128)(2,1)S(1)} %get-tuple-element.48), channel_id=1, source_target_pairs={{0,3},{1,0},{2,1},{3,2},{4,7},{5,4},{6,5},{7,6},{8,11},{9,8},{10,9... | collective-permute-start | bytes 1929224 | tf_op jit(solution)/shard_map/ppermute | solution.py:98
  112.3 1.5 collective-permute-start.29
  113.8 1.0 copy-done.6
  114.8 7.1 %unpack_1.1.after.refs_7_ = f32[27,256,512]{2,1,0:T(8,128)} custom-call(s32[3]{0:T(128)S(1)} %copy-done.12, bf16[1744,128]{1,0:T(8,128)(2,1)S(1)} %copy-done.6, bf16[1744,128]{1,0:T(8,128)(2,1)S(1)} %collective-permute-done.17.x.refs_2_, bf16[1744,128]{1,0:T(8,128)(2,1)S(1)} %collective-permute-done.18.y.refs_3_, ...), custom_call_target="tpu_custom_call", output_to_operand_aliasing={{}: (8, {})} | custom-call | bytes 4194304 | tf_op jit(solution)/shard_map/unpack_1/pallas_call | solution.py:395
  121.8 17.9 %collective-permute-done.22.by_3.refs_4_ = bf16[2496,128]{1,0:T(8,128)(2,1)S(1)} collective-permute-done((bf16[2496,128]{1,0:T(8,128)(2,1)S(1)}, bf16[2496,128]{1,0:T(8,128)(2,1)S(1)}, u32[]{:S(2)}, u32[]{:S(2)}) %collective-permute-start.22) | collective-permute-done | bytes 639008 | tf_op jit(solution)/shard_map/ppermute | solution.py:98
  139.8 5.0 %copy-done = f32[27,256,512]{2,1,0:T(8,128)S(1)} copy-done((f32[27,256,512]{2,1,0:T(8,128)S(1)}, f32[27,256,512]{2,1,0:T(8,128)}, u32[]{:S(2)}) %copy-start) | copy-done | bytes 14155800
  145.4 1.6 collective-permute-start.28
  147.5 1.5 collective-permute-start.26
  148.9 1.8 %collective-permute-start.24 = (bf16[928,128]{1,0:T(8,128)(2,1)S(1)}, bf16[928,128]{1,0:T(8,128)(2,1)S(1)}, u32[]{:S(2)}, u32[]{:S(2)}) collective-permute-start(bf16[928,128]{1,0:T(8,128)(2,1)S(1)} %get-tuple-element.51), channel_id=1, source_target_pairs={{0,1},{1,2},{2,3},{3,0},{4,5},{5,6},{6,7},{7,4},{8,9},{9,10},{10,1... | collective-permute-start | bytes 712712 | tf_op jit(solution)/shard_map/ppermute | solution.py:98
  150.7 2.0 %collective-permute-start.25 = (bf16[928,128]{1,0:T(8,128)(2,1)S(1)}, bf16[928,128]{1,0:T(8,128)(2,1)S(1)}, u32[]{:S(2)}, u32[]{:S(2)}) collective-permute-start(bf16[928,128]{1,0:T(8,128)(2,1)S(1)} %get-tuple-element.52), channel_id=1, source_target_pairs={{0,3},{1,0},{2,1},{3,2},{4,7},{5,4},{6,5},{7,6},{8,11},{9,8},{10,9... | collective-permute-start | bytes 712712 | tf_op jit(solution)/shard_map/ppermute | solution.py:98
  152.8 10.7 %unpack_2.1.refs_6_ = f32[27,256,512]{2,1,0:T(8,128)} custom-call(s32[3]{0:T(128)S(1)} %copy-done.12, bf16[2592,128]{1,0:T(8,128)(2,1)S(1)} %collective-permute-done.29.refs_1_, bf16[2592,128]{1,0:T(8,128)(2,1)S(1)} %collective-permute-done.30.refs_2_, bf16[2592,128]{1,0:T(8,128)(2,1)S(1)} %collective-permute-done.31.refs_3_, ...), custom_call_target="tpu_custom_call", output_to_operand_aliasing={{}: (7, {})} | custom-call | bytes 4194304 | tf_op jit(solution)/shard_map/unpack_2/pallas_call | solution.py:395
  163.6 5.6 %unpack_3.1 = f32[27,256,512]{2,1,0:T(8,128)} custom-call(s32[3]{0:T(128)S(1)} %copy-done.12, bf16[928,128]{1,0:T(8,128)(2,1)S(1)} %collective-permute-done.24.refs_1_, bf16[928,128]{1,0:T(8,128)(2,1)S(1)} %collective-permute-done.25.refs_2_, bf16[1296,128]{1,0:T(8,128)(2,1)S(1)} %collective-permute-done.26.refs_3_, ...), custom_call_target="tpu_custom_call", output_to_operand_aliasing={{}: (6, {})} | custom-call | bytes 4194304 | tf_op jit(solution)/shard_map/unpack_3/pallas_call | solution.py:395
  (57 shorter events, 5.9 us)
Async XLA Ops:
  0.7 77.6 %copy-start.11 = (s32[3]{0:T(128)}, s32[3]{0:T(128)S(1)}, u32[]{:S(2)}) copy-start(s32[3]{0:T(128)S(1)} %pad_add_fusion.pos.refs_0_) | copy-start | bytes 40
  0.7 1.0 copy-start.1
  1.7 1.0 copy-start.10
  3.5 17.5 %collective-permute-start.3 = (bf16[768,128]{1,0:T(8,128)(2,1)S(1)}, bf16[768,128]{1,0:T(8,128)(2,1)S(1)}, u32[]{:S(2)}, u32[]{:S(2)}) collective-permute-start(bf16[768,128]{1,0:T(8,128)(2,1)S(1)} %get-tuple-element.32), channel_id=1, source_target_pairs={{0,0},{1,1},{2,2},{3,3},{4,4},{5,5},{6,6},{7,7},{8,16},{9,17},{10,... | collective-permute-start | bytes 589832 | tf_op jit(solution)/shard_map/ppermute | solution.py:98
  4.2 16.8 %collective-permute-start.4 = (bf16[768,128]{1,0:T(8,128)(2,1)S(1)}, bf16[768,128]{1,0:T(8,128)(2,1)S(1)}, u32[]{:S(2)}, u32[]{:S(2)}) collective-permute-start(bf16[768,128]{1,0:T(8,128)(2,1)S(1)} %get-tuple-element.33), channel_id=1, source_target_pairs={{0,4},{1,5},{2,6},{3,7},{4,0},{5,1},{6,2},{7,3},{8,20},{9,21},{10,... | collective-permute-start | bytes 589832 | tf_op jit(solution)/shard_map/ppermute | solution.py:98
  7.2 13.8 %collective-permute-start = (bf16[416,128]{1,0:T(8,128)(2,1)S(1)}, bf16[416,128]{1,0:T(8,128)(2,1)S(1)}, u32[]{:S(2)}, u32[]{:S(2)}) collective-permute-start(bf16[416,128]{1,0:T(8,128)(2,1)S(1)} %get-tuple-element.29), channel_id=1, source_target_pairs={{0,1},{1,2},{2,3},{3,0},{4,5},{5,6},{6,7},{7,4},{8,9},{9,10},{10,1... | collective-permute-start | bytes 319496 | tf_op jit(solution)/shard_map/ppermute | solution.py:98
  8.8 12.2 %collective-permute-start.2 = (bf16[416,128]{1,0:T(8,128)(2,1)S(1)}, bf16[416,128]{1,0:T(8,128)(2,1)S(1)}, u32[]{:S(2)}, u32[]{:S(2)}) collective-permute-start(bf16[416,128]{1,0:T(8,128)(2,1)S(1)} %get-tuple-element.31), channel_id=1, source_target_pairs={{0,3},{1,0},{2,1},{3,2},{4,7},{5,4},{6,5},{7,6},{8,11},{9,8},{10,9... | collective-permute-start | bytes 319496 | tf_op jit(solution)/shard_map/ppermute | solution.py:98
  11.0 10.0 %collective-permute-start.1 = (bf16[384,128]{1,0:T(8,128)(2,1)S(1)}, bf16[384,128]{1,0:T(8,128)(2,1)S(1)}, u32[]{:S(2)}, u32[]{:S(2)}) collective-permute-start(bf16[384,128]{1,0:T(8,128)(2,1)S(1)} %get-tuple-element.30), channel_id=1, source_target_pairs={{0,2},{1,3},{2,0},{3,1},{4,6},{5,7},{6,4},{7,5},{8,10},{9,11},{10,... | collective-permute-start | bytes 294920 | tf_op jit(solution)/shard_map/ppermute | solution.py:98
  21.1 1.0 copy-start.2
  22.7 11.8 %collective-permute-start.9 = (bf16[2,768,128]{2,1,0:T(8,128)(2,1)S(1)}, bf16[2,768,128]{2,1,0:T(8,128)(2,1)S(1)}, u32[]{:S(2)}, u32[]{:S(2)}) collective-permute-start(bf16[2,768,128]{2,1,0:T(8,128)(2,1)S(1)} %get-tuple-element.35.here), channel_id=1, source_target_pairs={{0,3},{1,0},{2,1},{3,2},{4,7},{5,4},{6,5},{7,6},{8,11},{9,8},{10,9... | collective-permute-start | bytes 1179656 | tf_op jit(solution)/shard_map/ppermute | solution.py:98
  24.9 17.8 %collective-permute-start.8 = (bf16[2,768,128]{2,1,0:T(8,128)(2,1)S(1)}, bf16[2,768,128]{2,1,0:T(8,128)(2,1)S(1)}, u32[]{:S(2)}, u32[]{:S(2)}) collective-permute-start(bf16[2,768,128]{2,1,0:T(8,128)(2,1)S(1)} %get-tuple-element.35.here), channel_id=1, source_target_pairs={{0,1},{1,2},{2,3},{3,0},{4,5},{5,6},{6,7},{7,4},{8,9},{9,10},{10,1... | collective-permute-start | bytes 1179656 | tf_op jit(solution)/shard_map/ppermute | solution.py:98
  25.0 17.8 %collective-permute-start.7 = (bf16[4,384,128]{2,1,0:T(8,128)(2,1)S(1)}, bf16[4,384,128]{2,1,0:T(8,128)(2,1)S(1)}, u32[]{:S(2)}, u32[]{:S(2)}) collective-permute-start(bf16[4,384,128]{2,1,0:T(8,128)(2,1)S(1)} %get-tuple-element.34.x_own), channel_id=1, source_target_pairs={{0,12},{1,13},{2,14},{3,15},{4,8},{5,9},{6,10},{7,11},{8,4},{9,5},... | collective-permute-start | bytes 1179656 | tf_op jit(solution)/shard_map/ppermute | solution.py:98
  25.6 18.6 %collective-permute-start.6 = (bf16[4,384,128]{2,1,0:T(8,128)(2,1)S(1)}, bf16[4,384,128]{2,1,0:T(8,128)(2,1)S(1)}, u32[]{:S(2)}, u32[]{:S(2)}) collective-permute-start(bf16[4,384,128]{2,1,0:T(8,128)(2,1)S(1)} %get-tuple-element.34.x_own), channel_id=1, source_target_pairs={{0,8},{1,9},{2,10},{3,11},{4,12},{5,13},{6,14},{7,15},{8,0},{9,1},... | collective-permute-start | bytes 1179656 | tf_op jit(solution)/shard_map/ppermute | solution.py:98
  27.0 17.3 %collective-permute-start.5 = (bf16[4,384,128]{2,1,0:T(8,128)(2,1)S(1)}, bf16[4,384,128]{2,1,0:T(8,128)(2,1)S(1)}, u32[]{:S(2)}, u32[]{:S(2)}) collective-permute-start(bf16[4,384,128]{2,1,0:T(8,128)(2,1)S(1)} %get-tuple-element.34.x_own), channel_id=1, source_target_pairs={{0,4},{1,5},{2,6},{3,7},{4,0},{5,1},{6,2},{7,3},{8,12},{9,13},{10,... | collective-permute-start | bytes 1179656 | tf_op jit(solution)/shard_map/ppermute | solution.py:98
  44.9 24.8 %collective-permute-start.10 = (bf16[6,768,128]{2,1,0:T(8,128)(2,1)S(1)}, bf16[6,768,128]{2,1,0:T(8,128)(2,1)S(1)}, u32[]{:S(2)}, u32[]{:S(2)}) collective-permute-start(bf16[6,768,128]{2,1,0:T(8,128)(2,1)S(1)} %get-tuple-element.38.g), channel_id=1, source_target_pairs={{0,16},{1,17},{2,18},{3,19},{4,20},{5,21},{6,22},{7,23},{8,24},{9,... | collective-permute-start | bytes 3538952 | tf_op jit(solution)/shard_map/ppermute | solution.py:98
  45.0 8.9 %collective-permute-start.12 = (bf16[768,128]{1,0:T(8,128)(2,1)S(1)}, bf16[768,128]{1,0:T(8,128)(2,1)S(1)}, u32[]{:S(2)}, u32[]{:S(2)}) collective-permute-start(bf16[768,128]{1,0:T(8,128)(2,1)S(1)} %get-tuple-element.41), channel_id=1, source_target_pairs={{0,3},{1,0},{2,1},{3,2},{4,7},{5,4},{6,5},{7,6},{8,11},{9,8},{10,9... | collective-permute-start | bytes 589832 | tf_op jit(solution)/shard_map/ppermute | solution.py:98
  48.6 9.7 %collective-permute-start.11 = (bf16[768,128]{1,0:T(8,128)(2,1)S(1)}, bf16[768,128]{1,0:T(8,128)(2,1)S(1)}, u32[]{:S(2)}, u32[]{:S(2)}) collective-permute-start(bf16[768,128]{1,0:T(8,128)(2,1)S(1)} %get-tuple-element.36.after), channel_id=1, source_target_pairs={{0,1},{1,2},{2,3},{3,0},{4,5},{5,6},{6,7},{7,4},{8,9},{9,10},{10,1... | collective-permute-start | bytes 589832 | tf_op jit(solution)/shard_map/ppermute | solution.py:98
  58.9 10.8 %collective-permute-start.13 = (bf16[2,768,128]{2,1,0:T(8,128)(2,1)S(1)}, bf16[2,768,128]{2,1,0:T(8,128)(2,1)S(1)}, u32[]{:S(2)}, u32[]{:S(2)}) collective-permute-start(bf16[2,768,128]{2,1,0:T(8,128)(2,1)S(1)} %get-tuple-element.42.g2), channel_id=1, source_target_pairs={{0,16},{1,17},{2,18},{3,19},{4,20},{5,21},{6,22},{7,23},{8,24},{9,... | collective-permute-start | bytes 1179656 | tf_op jit(solution)/shard_map/ppermute | solution.py:98
  59.0 6.0 %collective-permute-start.14 = (bf16[448,128]{1,0:T(8,128)(2,1)S(1)}, bf16[448,128]{1,0:T(8,128)(2,1)S(1)}, u32[]{:S(2)}, u32[]{:S(2)}) collective-permute-start(bf16[448,128]{1,0:T(8,128)(2,1)S(1)} %get-tuple-element.43), channel_id=1, source_target_pairs={{0,4},{1,5},{2,6},{3,7},{4,0},{5,1},{6,2},{7,3},{8,12},{9,13},{10,... | collective-permute-start | bytes 344072 | tf_op jit(solution)/shard_map/ppermute | solution.py:98
  60.5 7.4 %collective-permute-start.15 = (bf16[448,128]{1,0:T(8,128)(2,1)S(1)}, bf16[448,128]{1,0:T(8,128)(2,1)S(1)}, u32[]{:S(2)}, u32[]{:S(2)}) collective-permute-start(bf16[448,128]{1,0:T(8,128)(2,1)S(1)} %get-tuple-element.44), channel_id=1, source_target_pairs={{0,12},{1,13},{2,14},{3,15},{4,8},{5,9},{6,10},{7,11},{8,4},{9,5},... | collective-permute-start | bytes 344072 | tf_op jit(solution)/shard_map/ppermute | solution.py:98
  67.9 1.0 copy-start.3
  69.6 15.2 %copy-start.7 = (bf16[4,6,64,256]{3,2,1,0:T(8,128)(2,1)}, bf16[4,6,64,256]{3,2,1,0:T(8,128)(2,1)S(1)}, u32[]{:S(2)}) copy-start(bf16[4,6,64,256]{3,2,1,0:T(8,128)(2,1)S(1)} %rims.1.mine) | copy-start | bytes 2359300
  69.6 8.7 %collective-permute-start.16 = (bf16[4,6,64,256]{3,2,1,0:T(8,128)(2,1)S(1)}, bf16[4,6,64,256]{3,2,1,0:T(8,128)(2,1)S(1)}, u32[]{:S(2)}, u32[]{:S(2)}) collective-permute-start(bf16[4,6,64,256]{3,2,1,0:T(8,128)(2,1)S(1)} %rims.1.mine), channel_id=1, source_target_pairs={{0,16},{1,17},{2,18},{3,19},{4,20},{5,21},{6,22},{7,23},{8,24},{9,... | collective-permute-start | bytes 2359304 | tf_op jit(solution)/shard_map/ppermute | solution.py:98
  78.3 6.6 %copy-start.8 = (bf16[4,6,64,256]{3,2,1,0:T(8,128)(2,1)}, bf16[4,6,64,256]{3,2,1,0:T(8,128)(2,1)S(1)}, u32[]{:S(2)}) copy-start(bf16[4,6,64,256]{3,2,1,0:T(8,128)(2,1)S(1)} %collective-permute-done.16.after.theirs) | copy-start | bytes 2359300
  79.2 5.6 %copy-start.4 = (bf16[1744,128]{1,0:T(8,128)(2,1)}, bf16[1744,128]{1,0:T(8,128)(2,1)S(1)}, u32[]{:S(2)}) copy-start(bf16[1744,128]{1,0:T(8,128)(2,1)S(1)} %get-tuple-element.45.after.own.refs_1_) | copy-start | bytes 1339396
  79.3 17.5 %collective-permute-start.21 = (bf16[1296,128]{1,0:T(8,128)(2,1)S(1)}, bf16[1296,128]{1,0:T(8,128)(2,1)S(1)}, u32[]{:S(2)}, u32[]{:S(2)}) collective-permute-start(bf16[1296,128]{1,0:T(8,128)(2,1)S(1)} %get-tuple-element.46), channel_id=1, source_target_pairs={{0,3},{1,0},{2,1},{3,2},{4,7},{5,4},{6,5},{7,6},{8,11},{9,8},{10,9... | collective-permute-start | bytes 995336 | tf_op jit(solution)/shard_map/ppermute | solution.py:98
  81.0 15.7 %collective-permute-start.20 = (bf16[1296,128]{1,0:T(8,128)(2,1)S(1)}, bf16[1296,128]{1,0:T(8,128)(2,1)S(1)}, u32[]{:S(2)}, u32[]{:S(2)}) collective-permute-start(bf16[1296,128]{1,0:T(8,128)(2,1)S(1)} %get-tuple-element.46), channel_id=1, source_target_pairs={{0,1},{1,2},{2,3},{3,0},{4,5},{5,6},{6,7},{7,4},{8,9},{9,10},{10,1... | collective-permute-start | bytes 995336 | tf_op jit(solution)/shard_map/ppermute | solution.py:98
  81.3 15.4 %collective-permute-start.19 = (bf16[1744,128]{1,0:T(8,128)(2,1)S(1)}, bf16[1744,128]{1,0:T(8,128)(2,1)S(1)}, u32[]{:S(2)}, u32[]{:S(2)}) collective-permute-start(bf16[1744,128]{1,0:T(8,128)(2,1)S(1)} %get-tuple-element.45.after.own.refs_1_), channel_id=1, source_target_pairs={{0,12},{1,13},{2,14},{3,15},{4,8},{5,9},{6,10},{7,11},{8,4},{9,5},... | collective-permute-start | bytes 1339400 | tf_op jit(solution)/shard_map/ppermute | solution.py:98
  82.8 21.2 %collective-permute-start.18 = (bf16[1744,128]{1,0:T(8,128)(2,1)S(1)}, bf16[1744,128]{1,0:T(8,128)(2,1)S(1)}, u32[]{:S(2)}, u32[]{:S(2)}) collective-permute-start(bf16[1744,128]{1,0:T(8,128)(2,1)S(1)} %get-tuple-element.45.after.own.refs_1_), channel_id=1, source_target_pairs={{0,8},{1,9},{2,10},{3,11},{4,12},{5,13},{6,14},{7,15},{8,0},{9,1},... | collective-permute-start | bytes 1339400 | tf_op jit(solution)/shard_map/ppermute | solution.py:98
  83.4 20.6 %collective-permute-start.17 = (bf16[1744,128]{1,0:T(8,128)(2,1)S(1)}, bf16[1744,128]{1,0:T(8,128)(2,1)S(1)}, u32[]{:S(2)}, u32[]{:S(2)}) collective-permute-start(bf16[1744,128]{1,0:T(8,128)(2,1)S(1)} %get-tuple-element.45.after.own.refs_1_), channel_id=1, source_target_pairs={{0,4},{1,5},{2,6},{3,7},{4,0},{5,1},{6,2},{7,3},{8,12},{9,13},{10,... | collective-permute-start | bytes 1339400 | tf_op jit(solution)/shard_map/ppermute | solution.py:98
  84.8 19.2 %copy-start.12 = (s32[3]{0:T(128)S(1)}, s32[3]{0:T(128)}, u32[]{:S(2)}) copy-start(s32[3]{0:T(128)} %copy-done.11) | copy-start | bytes 40
  104.0 1.0 copy-start.5
  105.0 1.0 copy-start.9
  106.8 40.7 %collective-permute-start.31 = (bf16[2592,128]{1,0:T(8,128)(2,1)S(1)}, bf16[2592,128]{1,0:T(8,128)(2,1)S(1)}, u32[]{:S(2)}, u32[]{:S(2)}) collective-permute-start(bf16[2592,128]{1,0:T(8,128)(2,1)S(1)} %get-tuple-element.49.refs_7_), channel_id=1, source_target_pairs={{0,12},{1,13},{2,14},{3,15},{4,8},{5,9},{6,10},{7,11},{8,4},{9,5},... | collective-permute-start | bytes 1990664 | tf_op jit(solution)/shard_map/ppermute | solution.py:98
  108.3 31.5 %collective-permute-start.23 = (bf16[2512,128]{1,0:T(8,128)(2,1)S(1)}, bf16[2512,128]{1,0:T(8,128)(2,1)S(1)}, u32[]{:S(2)}, u32[]{:S(2)}) collective-permute-start(bf16[2512,128]{1,0:T(8,128)(2,1)S(1)} %get-tuple-element.48), channel_id=1, source_target_pairs={{0,3},{1,0},{2,1},{3,2},{4,7},{5,4},{6,5},{7,6},{8,11},{9,8},{10,9... | collective-permute-start | bytes 1929224 | tf_op jit(solution)/shard_map/ppermute | solution.py:98
  111.7 28.1 %collective-permute-start.22 = (bf16[2496,128]{1,0:T(8,128)(2,1)S(1)}, bf16[2496,128]{1,0:T(8,128)(2,1)S(1)}, u32[]{:S(2)}, u32[]{:S(2)}) collective-permute-start(bf16[2496,128]{1,0:T(8,128)(2,1)S(1)} %get-tuple-element.47), channel_id=1, source_target_pairs={{0,1},{1,2},{2,3},{3,0},{4,5},{5,6},{6,7},{7,4},{8,9},{9,10},{10,1... | collective-permute-start | bytes 1916936 | tf_op jit(solution)/shard_map/ppermute | solution.py:98
  111.7 37.2 %collective-permute-start.30 = (bf16[2592,128]{1,0:T(8,128)(2,1)S(1)}, bf16[2592,128]{1,0:T(8,128)(2,1)S(1)}, u32[]{:S(2)}, u32[]{:S(2)}) collective-permute-start(bf16[2592,128]{1,0:T(8,128)(2,1)S(1)} %get-tuple-element.49.refs_7_), channel_id=1, source_target_pairs={{0,8},{1,9},{2,10},{3,11},{4,12},{5,13},{6,14},{7,15},{8,0},{9,1},... | collective-permute-start | bytes 1990664 | tf_op jit(solution)/shard_map/ppermute | solution.py:98
  112.3 38.4 %collective-permute-start.29 = (bf16[2592,128]{1,0:T(8,128)(2,1)S(1)}, bf16[2592,128]{1,0:T(8,128)(2,1)S(1)}, u32[]{:S(2)}, u32[]{:S(2)}) collective-permute-start(bf16[2592,128]{1,0:T(8,128)(2,1)S(1)} %get-tuple-element.49.refs_7_), channel_id=1, source_target_pairs={{0,4},{1,5},{2,6},{3,7},{4,0},{5,1},{6,2},{7,3},{8,12},{9,13},{10,... | collective-permute-start | bytes 1990664 | tf_op jit(solution)/shard_map/ppermute | solution.py:98
  113.8 1.0 copy-start.6
  139.8 5.0 %copy-start = (f32[27,256,512]{2,1,0:T(8,128)S(1)}, f32[27,256,512]{2,1,0:T(8,128)}, u32[]{:S(2)}) copy-start(f32[27,256,512]{2,1,0:T(8,128)} %unpack_1.1.after.refs_7_) | copy-start | bytes 42467332
  145.4 18.1 %collective-permute-start.28 = (bf16[1296,128]{1,0:T(8,128)(2,1)S(1)}, bf16[1296,128]{1,0:T(8,128)(2,1)S(1)}, u32[]{:S(2)}, u32[]{:S(2)}) collective-permute-start(bf16[1296,128]{1,0:T(8,128)(2,1)S(1)} %get-tuple-element.53.refs_6_), channel_id=1, source_target_pairs={{0,12},{1,13},{2,14},{3,15},{4,8},{5,9},{6,10},{7,11},{8,4},{9,5},... | collective-permute-start | bytes 995336 | tf_op jit(solution)/shard_map/ppermute | solution.py:98
  146.9 16.6 %collective-permute-start.27 = (bf16[1296,128]{1,0:T(8,128)(2,1)S(1)}, bf16[1296,128]{1,0:T(8,128)(2,1)S(1)}, u32[]{:S(2)}, u32[]{:S(2)}) collective-permute-start(bf16[1296,128]{1,0:T(8,128)(2,1)S(1)} %get-tuple-element.53.refs_6_), channel_id=1, source_target_pairs={{0,8},{1,9},{2,10},{3,11},{4,12},{5,13},{6,14},{7,15},{8,0},{9,1},... | collective-permute-start | bytes 995336 | tf_op jit(solution)/shard_map/ppermute | solution.py:98
  147.5 16.1 %collective-permute-start.26 = (bf16[1296,128]{1,0:T(8,128)(2,1)S(1)}, bf16[1296,128]{1,0:T(8,128)(2,1)S(1)}, u32[]{:S(2)}, u32[]{:S(2)}) collective-permute-start(bf16[1296,128]{1,0:T(8,128)(2,1)S(1)} %get-tuple-element.53.refs_6_), channel_id=1, source_target_pairs={{0,4},{1,5},{2,6},{3,7},{4,0},{5,1},{6,2},{7,3},{8,12},{9,13},{10,... | collective-permute-start | bytes 995336 | tf_op jit(solution)/shard_map/ppermute | solution.py:98
  148.9 14.6 %collective-permute-start.24 = (bf16[928,128]{1,0:T(8,128)(2,1)S(1)}, bf16[928,128]{1,0:T(8,128)(2,1)S(1)}, u32[]{:S(2)}, u32[]{:S(2)}) collective-permute-start(bf16[928,128]{1,0:T(8,128)(2,1)S(1)} %get-tuple-element.51), channel_id=1, source_target_pairs={{0,1},{1,2},{2,3},{3,0},{4,5},{5,6},{6,7},{7,4},{8,9},{9,10},{10,1... | collective-permute-start | bytes 712712 | tf_op jit(solution)/shard_map/ppermute | solution.py:98
  150.7 12.8 %collective-permute-start.25 = (bf16[928,128]{1,0:T(8,128)(2,1)S(1)}, bf16[928,128]{1,0:T(8,128)(2,1)S(1)}, u32[]{:S(2)}, u32[]{:S(2)}) collective-permute-start(bf16[928,128]{1,0:T(8,128)(2,1)S(1)} %get-tuple-element.52), channel_id=1, source_target_pairs={{0,3},{1,0},{2,1},{3,2},{4,7},{5,4},{6,5},{7,6},{8,11},{9,8},{10,9... | collective-permute-start | bytes 712712 | tf_op jit(solution)/shard_map/ppermute | solution.py:98

commit v7 on v6

--- a/solution.py
+++ b/solution.py
@@ -127,7 +127,7 @@
     )(*ins)
 
 
-def pack_kernel(pos, x, g, g_same, g_other, x0, x1, x2, x3, held):
+def pack_kernel(pos, x, g, g_same, g_other, x0, x1, x2, x3, rim_x, rim_d, held):
     levels, height, width, chans = x.shape
     half, wide = levels // 2, chans // 2
     right = lax.rem(pos[1], 2)
@@ -146,80 +146,73 @@
         rim = g[:, :, column, :].reshape(levels * height, chans)
         out[many : many + levels * height, :] = rim[:, 0:wide]
         out[many + levels * height :, :] = rim[:, wide:]
-
-
-def split_kernel(pos, here, west, east, after1, after2, after3, first, second, near):
-    del pos, after1, after2, after3
+    even = right == 0
+    low, high = g[:, 0], g[:, height - 1]
+    line = levels * width
+    for out, upward in ((rim_x, even), (rim_d, jnp.logical_not(even))):
+        facing = jnp.where(upward, high, low).reshape(line, chans)
+        for at in range(2):
+            out[at * line : (at + 1) * line, :] = facing[:, at * wide : (at + 1) * wide]
+
+
+def spread_kernel(pos, x0, x1, x2, x3, one, two, both, own, own_y):
+    del pos
+    many = x0.shape[0]
+    both[0] = one[...]
+    both[1] = two[...]
+    for at, piece in enumerate((x0, x1, x2, x3)):
+        own[at * many : (at + 1) * many, :] = piece[0:many, :]
+        own_y[at * many : (at + 1) * many, :] = piece[0:many, :]
+    extra = x1.shape[0] - many
+    own[4 * many : 4 * many + extra, :] = x1[many:, :]
+    own[4 * many + extra :, :] = x3[many:, :]
+
+
+def split_kernel(
+    pos, here, west, east, g, own, x_x, x_d, by_x, by_d, after, first, second, near, mine
+):
+    del after
     first[...] = west[0]
     second[...] = east[1]
     for at, part in enumerate((here, west, east)):
         near[2 * at : 2 * at + 2] = part[...]
 
-
-def spread_kernel(pos, x0, x1, x2, x3, g, one, two, both, own, rim_x, rim_d):
-    levels, height, width, chans = g.shape
-    many, wide = x0.shape[0], chans // 2
-    line, edge = levels * width, levels * height
-    both[0] = one[...]
-    both[1] = two[...]
-    for at, piece in enumerate((x0, x1, x2, x3)):
-        own[at] = piece[0:many, :]
-    even = lax.rem(pos[1], 2) == 0
-    low, high = g[:, 0], g[:, height - 1]
-    for out, upward in ((rim_x, even), (rim_d, jnp.logical_not(even))):
-        facing = jnp.where(upward, high, low).reshape(line, chans)
-        for half in range(2):
-            out[half * line : (half + 1) * line, :] = facing[:, half * wide : (half + 1) * wide]
-        first = 2 * line
-        out[first : first + 2 * edge, :] = x1[many : many + 2 * edge, :]
-        out[first + 2 * edge : first + 4 * edge, :] = x3[many : many + 2 * edge, :]
-
-
-def hand_kernel(pos, rim_x, rim_d, one, two, after, to_x, to_d, both):
-    del pos, after
-    to_x[...] = rim_x[...]
-    to_d[...] = rim_d[...]
-    both[0] = one[...]
-    both[1] = two[...]
-
-
-def rims_kernel(pos, g, from_west, from_east, by_x, by_d, mine):
     levels, height, width, chans = g.shape
     edge, line, wide = levels * height, levels * width, chans // 2
-    many = from_west.shape[0] - 2 * edge
+    inner = own.shape[0] - 4 * edge
     mine[:, 1 : height + 1, 0:width, :] = g[...]
 
-    def columns(message, first, at, rows):
+    def columns(message, rows):
+        for side in range(2):
+            for half in range(2):
+                start = inner + (2 * side + half) * edge
+                rim = message[start : start + edge, :].reshape(levels, height, wide)
+                at = width + 8 * side
+                for row, to in rows:
+                    mine[:, to, at : at + 8, half * wide : (half + 1) * wide] = jnp.broadcast_to(
+                        rim[:, row : row + 1], (levels, 8, wide)
+                    )
+
+    columns(own, [(row, row + 1) for row in range(height)])
+
+    def lines(strip, message, row, to):
         for half in range(2):
-            rim = message[first + half * edge : first + (half + 1) * edge, :].reshape(levels, height, wide)
-            for row, to in rows:
-                mine[:, to, at : at + 8, half * wide : (half + 1) * wide] = jnp.broadcast_to(
-                    rim[:, row : row + 1], (levels, 8, wide)
-                )
-
-    inner = [(row, row + 1) for row in range(height)]
-    columns(from_west, many, width, inner)
-    columns(from_east, many, width + 8, inner)
-
-    def lines(message, row, to):
-        for half in range(2):
-            strip = message[half * line : (half + 1) * line, :]
-            mine[:, to, 0:width, half * wide : (half + 1) * wide] = strip.reshape(levels, width, wide)
-        columns(message, 2 * line, width, [(row, to)])
-        columns(message, 2 * line + 2 * edge, width + 8, [(row, to)])
+            part = strip[half * line : (half + 1) * line, :]
+            mine[:, to, 0:width, half * wide : (half + 1) * wide] = part.reshape(levels, width, wide)
+        columns(message, [(row, to)])
 
     lat = pos[1]
     odd = lax.rem(lat, 2)
 
     @pl.when(odd == 1)
     def _():
-        lines(by_x, height - 1, 0)
-        lines(by_d, 0, height + 1)
+        lines(by_x, x_x, height - 1, 0)
+        lines(by_d, x_d, 0, height + 1)
 
     @pl.when(odd == 0)
     def _():
-        lines(by_d, height - 1, 0)
-        lines(by_x, 0, height + 1)
+        lines(by_d, x_d, height - 1, 0)
+        lines(by_x, x_x, 0, height + 1)
 
     @pl.when(lat == 0)
     def _():
@@ -228,6 +221,12 @@
     @pl.when(lat == 3)
     def _():
         mine[:, height + 1] = jnp.zeros_like(mine[:, height + 1])
+
+
+def pair_kernel(pos, one, two, after, both):
+    del pos, after
+    both[0] = one[...]
+    both[1] = two[...]
 
 
 def lines_kernel(pos, x_own, x_x, x_y, x_d, after, xs, blank):
@@ -236,12 +235,15 @@
     levels, rows, circle, lanes = xs.shape
     rows, width, span, half = rows - 2, circle // 4, lanes // 4, levels // 2
     height = rows // 4
+    many = half * height * width
     xs[:, 0] = jnp.zeros_like(xs[:, 0])
     xs[:, rows + 1] = jnp.zeros_like(xs[:, rows + 1])
     low = lax.broadcasted_iota(jnp.int32, (circle, 2 * span), 1) < span
     for tag, ref in enumerate((x_own, x_x, x_y, x_d)):
         start = (lat ^ tag) * height
-        strips = [ref.at[(4 - at) % 4].reshape(half, height, width, 2 * span) for at in range(4)]
+        strips = [
+            ref.at[pl.ds((4 - at) % 4 * many, many)].reshape(half, height, width, 2 * span) for at in range(4)
+        ]
 
         @pl.loop(0, half * height)
         def _(step, strips=strips, start=start):
@@ -380,7 +382,8 @@
         @pl.loop(0, many)
         def _(tap, source=source, row=row, unit=unit, at=at):
             code = source[pl.ds(pl.multiple_of(row + tap * span, 16), span), :].astype(jnp.float32)
-            root = jnp.sqrt(jnp.sqrt(jnp.sqrt(jnp.abs(code)))) * unit
+            root = lax.rsqrt(lax.rsqrt(jnp.abs(code)))
+            root = root * lax.rsqrt(jnp.maximum(root, 1e-30)) * unit
             buffers[at % 2, tap] = jnp.where(code < 0, -root, root)
 
         copy(at).start()
@@ -402,7 +405,7 @@
         scratch_shapes=[VMEM((2, most, span, wide), jnp.float32), pltpu.SemaphoreType.DMA((2,))],
         input_output_aliases={len(ins) - 1: 0},
         cost_estimate=pl.CostEstimate(flops=0, bytes_accessed=4 * 2**20, transcendentals=0),
-        compiler_params=pltpu.CompilerParams(vmem_limit_bytes=24 * 1024 * 1024),
+        compiler_params=pltpu.CompilerParams(vmem_limit_bytes=54 * 1024 * 1024),
         name=name,
     )(*ins)
 
@@ -469,10 +472,12 @@
     to_other = lambda c, a, o: (a // 2, 2 * c + 1 - a % 2, o)
     many = cells // 2
     block = jax.ShapeDtypeStruct((cells, wide), bf16)
-    g_same, g_other, x0, x1, x2, x3 = call(
+    strip = jax.ShapeDtypeStruct((2 * levels * width, 2 * span), bf16)
+    g_same, g_other, x0, x1, x2, x3, rim_x, rim_d = call(
         pack_kernel,
         [block, block]
-        + [jax.ShapeDtypeStruct((many + extra, 2 * span), bf16) for extra in (0, 2 * edge, 0, 2 * edge)],
+        + [jax.ShapeDtypeStruct((many + extra, 2 * span), bf16) for extra in (0, 2 * edge, 0, 2 * edge)]
+        + [strip, strip],
         (pos, x_cells, g_cells),
         [VMEM((4, many, 2 * span), bf16)],
         0,
@@ -484,36 +489,44 @@
     x_r1 = move(x1, lon_by(1))
     x_r3 = move(x3, lon_by(-1))
     x_r2 = move(x2, lon_by(2))
-
-    rim = jax.ShapeDtypeStruct((2 * levels * width + 4 * edge, 2 * span), bf16)
-    g0, x_own, rim_x, rim_d = call(
+    by_x = move(rim_x, lat_xor(1))
+    by_d = move(rim_d, lat_xor(3))
+
+    inner = 4 * many
+    g0, x_own, x_own_y = call(
         spread_kernel,
-        [jax.ShapeDtypeStruct((2, cells, wide), bf16), jax.ShapeDtypeStruct((4, many, 2 * span), bf16), rim, rim],
-        (pos, x0, x_r1, x_r2, x_r3, g_cells, g_s, g_o),
+        [jax.ShapeDtypeStruct((2, cells, wide), bf16)]
+        + [jax.ShapeDtypeStruct((count, 2 * span), bf16) for count in (inner + 4 * edge, inner)],
+        (pos, x0, x_r1, x_r2, x_r3, g_s, g_o),
         [],
         0,
         "spread",
         16,
     )
+    x_x = move(x_own, lat_xor(1))
+    x_d = move(x_own, lat_xor(3))
+    x_y = move(x_own_y, lat_xor(2))
     g1 = move(g0, lon_by(1))
     g3 = move(g0, lon_by(-1))
-    x_x = move(x_own, lat_xor(1))
-    x_y = move(x_own, lat_xor(2))
-    x_d = move(x_own, lat_xor(3))
-    far_a, far_b, g_near = call(
+    far_a, far_b, g_near, mine = call(
         split_kernel,
-        [block, block, jax.ShapeDtypeStruct((6, cells, wide), bf16)],
-        (pos, g0, g1, g3, x_x, x_y, x_d),
+        [
+            block,
+            block,
+            jax.ShapeDtypeStruct((6, cells, wide), bf16),
+            jax.ShapeDtypeStruct((levels, height + 2, width + 16, chans), bf16),
+        ],
+        (pos, g0, g1, g3, g_cells, x_own, x_x, x_d, by_x, by_d, x_y),
         [],
         0,
         "split",
         16,
-        held=3,
+        held=1,
     )
     g2a = move(far_a, lon_by(1))
     g2b = move(far_b, lon_by(-1))
     s_near = move(g_near, sibling)
-
+    theirs = move(mine, sibling)
     xs, total = pl.pallas_call(
         lines_kernel,
         out_shape=[
@@ -528,31 +541,10 @@
         compiler_params=pltpu.CompilerParams(vmem_limit_bytes=24 * 1024 * 1024),
         name="lines",
     )(pos, x_own, x_x, x_y, x_d, far_a)
-    rim_x, rim_d, g2 = call(
-        hand_kernel,
-        [rim, rim, jax.ShapeDtypeStruct((2, cells, wide), bf16)],
-        (pos, rim_x, rim_d, g2a, g2b, xs),
-        [],
-        0,
-        "hand",
-        16,
-        held=1,
+    (g2,) = call(
+        pair_kernel, [jax.ShapeDtypeStruct((2, cells, wide), bf16)], (pos, g2a, g2b, xs), [], 0, "pair", 16, held=1
     )
     s2 = move(g2, sibling)
-    by_x = move(rim_x, lat_xor(1))
-    by_d = move(rim_d, lat_xor(3))
-
-    (mine,) = call(
-        rims_kernel,
-        [jax.ShapeDtypeStruct((levels, height + 2, width + 16, chans), bf16)],
-        (pos, g_cells, x_r1, x_r3, by_x, by_d),
-        [],
-        0,
-        "rims",
-        16,
-    )
-    theirs = move(mine, sibling)
-
     early = 7
     cut, end = early * span, 27 * span
     size = end + 16 - cut
@@ -590,7 +582,7 @@
         cost_estimate=pl.CostEstimate(
             flops=4 * 27 * chans * filters * cells, bytes_accessed=27 * chans * filters * 2, transcendentals=0
         ),
-        compiler_params=pltpu.CompilerParams(vmem_limit_bytes=56 * 1024 * 1024),
+        compiler_params=pltpu.CompilerParams(vmem_limit_bytes=52 * 1024 * 1024),
         name="field",
     )(pos, own, mine, theirs, taps)
 

time: 170 us -> 164 us (0.965)
  waiting for transfers between devices: 61 us -> 54.6 us
  starting transfers between devices: 40.8 us -> 42.5 us
    ppermute x32, waiting for transfers between devices: 61 us -> 54.6 us  [move(): return lax.ppermute(x, AXES, pairs)]
    unnamed x26 -> x50, local copies, waits for them, and re-layouts: 12 us -> 11 us
    pallas_call x9 -> x8, Pallas kernels: 14.2 us -> 13.7 us  [call(): pl.pallas_call(kernel, out_shape=outs, in_specs=[pl.BlockSpec(memory_spac...]
  transfers between devices with their start and end apart: 32 -> 32, of which waited for: 10 -> 10; matrix products, arithmetic and copies ran while one was open for 0% -> 0% of each run, Pallas kernels for 27% -> 28%
where the time goes in v7:
time: 164 us
  waiting for transfers between devices  54.6 us (33%)
  Pallas kernels  54.5 us (33%)
  starting transfers between devices  42.5 us (26%)
  local copies, waits for them, and re-layouts  11 us (7%)
    ppermute x32, waiting for transfers between devices, move(): return lax.ppermute(x, AXES, pairs)  54.6 us
    ppermute x32, starting transfers between devices, move(): return lax.ppermute(x, AXES, pairs)  42.5 us
    pallas_call x3, Pallas kernels, unpack(): pl.pallas_call(lambda *refs: unpack_kernel(*refs, pieces=pieces, span=spa...  24.6 us
    pallas_call x8, Pallas kernels, call(): pl.pallas_call(kernel, out_shape=outs, in_specs=[pl.BlockSpec(memory_spac...  13.7 us
    pallas_call x1, Pallas kernels, blocked_body(): pl.pallas_call(field_kernel, out_shape=jax.ShapeDtypeStruct((levels, heig...  11.4 us
    unnamed x50, local copies, waits for them, and re-layouts  11 us
    pallas_call x1, Pallas kernels, blocked_body(): pl.pallas_call(lines_kernel, out_shape=[jax.ShapeDtypeStruct((levels, row...  4.86 us
  transfers between devices with their start and end apart: 32, of which 10 were waited for; matrix products, arithmetic and copies ran while one was open for 0% of the time, Pallas kernels for 28%

profile of v7, /device:TPU:0, one launch (start us, length us, event | category | flops | bytes accessed | tf_op | source)
XLA Modules:
  0.0 163.6 jit_solution(5771833013295274473)
XLA Ops:
  0.7 1.0 copy-done.7
  1.7 1.0 copy-done.13
  2.7 0.8 pack.1
  3.6 0.7 collective-permute-start.3
  4.2 3.0 %collective-permute-start.4 = (bf16[768,128]{1,0:T(8,128)(2,1)S(1)}, bf16[768,128]{1,0:T(8,128)(2,1)S(1)}, u32[]{:S(2)}, u32[]{:S(2)}) collective-permute-start(bf16[768,128]{1,0:T(8,128)(2,1)S(1)} %get-tuple-element.32), channel_id=1, source_target_pairs={{0,4},{1,5},{2,6},{3,7},{4,0},{5,1},{6,2},{7,3},{8,20},{9,21},{10,... | collective-permute-start | bytes 589832 | tf_op jit(solution)/shard_map/ppermute | solution.py:98
  7.2 1.6 collective-permute-start
  8.8 2.6 %collective-permute-start.1 = (bf16[384,128]{1,0:T(8,128)(2,1)S(1)}, bf16[384,128]{1,0:T(8,128)(2,1)S(1)}, u32[]{:S(2)}, u32[]{:S(2)}) collective-permute-start(bf16[384,128]{1,0:T(8,128)(2,1)S(1)} %get-tuple-element.29), channel_id=1, source_target_pairs={{0,2},{1,3},{2,0},{3,1},{4,6},{5,7},{6,4},{7,5},{8,10},{9,11},{10,... | collective-permute-start | bytes 294920 | tf_op jit(solution)/shard_map/ppermute | solution.py:98
  11.4 1.3 collective-permute-start.2
  12.8 6.2 %collective-permute-done.1.x2 = bf16[384,128]{1,0:T(8,128)(2,1)S(1)} collective-permute-done((bf16[384,128]{1,0:T(8,128)(2,1)S(1)}, bf16[384,128]{1,0:T(8,128)(2,1)S(1)}, u32[]{:S(2)}, u32[]{:S(2)}) %collective-permute-start.1) | collective-permute-done | bytes 98336 | tf_op jit(solution)/shard_map/ppermute | solution.py:98
  18.9 3.0 %collective-permute-start.11 = (bf16[384,128]{1,0:T(8,128)(2,1)S(1)}, bf16[384,128]{1,0:T(8,128)(2,1)S(1)}, u32[]{:S(2)}, u32[]{:S(2)}) collective-permute-start(bf16[384,128]{1,0:T(8,128)(2,1)S(1)} %get-tuple-element.37), channel_id=1, source_target_pairs={{0,12},{1,13},{2,14},{3,15},{4,8},{5,9},{6,10},{7,11},{8,4},{9,5},... | collective-permute-start | bytes 294920 | tf_op jit(solution)/shard_map/ppermute | solution.py:98
  22.8 1.9 %collective-permute-start.5 = (bf16[1600,128]{1,0:T(8,128)(2,1)S(1)}, bf16[1600,128]{1,0:T(8,128)(2,1)S(1)}, u32[]{:S(2)}, u32[]{:S(2)}) collective-permute-start(bf16[1600,128]{1,0:T(8,128)(2,1)S(1)} %get-tuple-element.33.own.x_own), channel_id=1, source_target_pairs={{0,4},{1,5},{2,6},{3,7},{4,0},{5,1},{6,2},{7,3},{8,12},{9,13},{10,... | collective-permute-start | bytes 1228808 | tf_op jit(solution)/shard_map/ppermute | solution.py:98
  24.6 1.6 collective-permute-start.6
  26.2 2.8 %collective-permute-start.9 = (bf16[2,768,128]{2,1,0:T(8,128)(2,1)S(1)}, bf16[2,768,128]{2,1,0:T(8,128)(2,1)S(1)}, u32[]{:S(2)}, u32[]{:S(2)}) collective-permute-start(bf16[2,768,128]{2,1,0:T(8,128)(2,1)S(1)} %get-tuple-element.35.here), channel_id=1, source_target_pairs={{0,3},{1,0},{2,1},{3,2},{4,7},{5,4},{6,5},{7,6},{8,11},{9,8},{10,9... | collective-permute-start | bytes 1179656 | tf_op jit(solution)/shard_map/ppermute | solution.py:98
  29.0 14.5 %collective-permute-done.6.after.x_y = bf16[1536,128]{1,0:T(8,128)(2,1)S(1)} collective-permute-done((bf16[1536,128]{1,0:T(8,128)(2,1)S(1)}, bf16[1536,128]{1,0:T(8,128)(2,1)S(1)}, u32[]{:S(2)}, u32[]{:S(2)}) %collective-permute-start.6) | collective-permute-done | bytes 393248 | tf_op jit(solution)/shard_map/ppermute | solution.py:98
  43.5 1.8 %collective-permute-done.8.west = bf16[2,768,128]{2,1,0:T(8,128)(2,1)S(1)} collective-permute-done((bf16[2,768,128]{2,1,0:T(8,128)(2,1)S(1)}, bf16[2,768,128]{2,1,0:T(8,128)(2,1)S(1)}, u32[]{:S(2)}, u32[]{:S(2)}) %collective-permute-start.8) | collective-permute-done | bytes 393248 | tf_op jit(solution)/shard_map/ppermute | solution.py:98
  45.3 1.0 copy-done.8
  46.3 0.8 split.1
  47.2 3.0 %collective-permute-start.14 = (bf16[768,128]{1,0:T(8,128)(2,1)S(1)}, bf16[768,128]{1,0:T(8,128)(2,1)S(1)}, u32[]{:S(2)}, u32[]{:S(2)}) collective-permute-start(bf16[768,128]{1,0:T(8,128)(2,1)S(1)} %get-tuple-element.41), channel_id=1, source_target_pairs={{0,3},{1,0},{2,1},{3,2},{4,7},{5,4},{6,5},{7,6},{8,11},{9,8},{10,9... | collective-permute-start | bytes 589832 | tf_op jit(solution)/shard_map/ppermute | solution.py:98
  50.1 4.9 %lines.1 = (bf16[4,18,192,256]{3,2,1,0:T(8,128)(2,1)S(1)}, f32[27,256,512]{2,1,0:T(8,128)}) custom-call(s32[3]{0:T(128)S(1)} %pad_add_fusion.pos.refs_0_, bf16[1600,128]{1,0:T(8,128)(2,1)S(1)} %get-tuple-element.33.own.x_own, bf16[1600,128]{1,0:T(8,128)(2,1)S(1)} %collective-permute-done.5.x_x, bf16[1536,128]{1,0:T(8,128)(2,1)S(1)} %collective-permute-done.6.after.x_y, ...), custom_call_target="tpu_custom_call" | custom-call | bytes 1048576 | tf_op jit(solution)/shard_map/lines/pallas_call | solution.py:530
  55.4 4.5 %collective-permute-done.13.one = bf16[768,128]{1,0:T(8,128)(2,1)S(1)} collective-permute-done((bf16[768,128]{1,0:T(8,128)(2,1)S(1)}, bf16[768,128]{1,0:T(8,128)(2,1)S(1)}, u32[]{:S(2)}, u32[]{:S(2)}) %collective-permute-start.13) | collective-permute-done | bytes 196640 | tf_op jit(solution)/shard_map/ppermute | solution.py:98
  61.0 1.2 collective-permute-done.15.s2
  62.3 8.6 %taps.1.held = f32[27,64,128]{2,1,0:T(8,128)S(1)} custom-call(s32[3]{0:T(128)S(1)} %pad_add_fusion.pos.refs_0_, bf16[4,18,192,256]{3,2,1,0:T(8,128)(2,1)S(1)} %get-tuple-element.39.after.xs, bf16[6,768,128]{2,1,0:T(8,128)(2,1)S(1)} %get-tuple-element.40.g, bf16[6,768,128]{2,1,0:T(8,128)(2,1)S(1)} %collective-permute-done.12.s, ...), custom_call_target="tpu_custom_call" | custom-call | flops 5435817984 | bytes 11108352 | tf_op jit(solution)/shard_map/taps/pallas_call | solution.py:116
  70.8 1.0 code.1
  71.8 1.8 %collective-permute-start.21 = (bf16[1296,128]{1,0:T(8,128)(2,1)S(1)}, bf16[1296,128]{1,0:T(8,128)(2,1)S(1)}, u32[]{:S(2)}, u32[]{:S(2)}) collective-permute-start(bf16[1296,128]{1,0:T(8,128)(2,1)S(1)} %get-tuple-element.44), channel_id=1, source_target_pairs={{0,3},{1,0},{2,1},{3,2},{4,7},{5,4},{6,5},{7,6},{8,11},{9,8},{10,9... | collective-permute-start | bytes 995336 | tf_op jit(solution)/shard_map/ppermute | solution.py:98
  73.9 1.6 collective-permute-start.19
  75.5 1.2 collective-permute-start.18
  76.6 1.1 collective-permute-start.17
  77.7 11.4 %field.1.after = bf16[4,4,48,256]{3,2,1,0:T(8,128)(2,1)} custom-call(s32[3]{0:T(128)S(1)} %pad_add_fusion.pos.refs_0_, bf16[1744,128]{1,0:T(8,128)(2,1)S(1)} %get-tuple-element.43.after.own.refs_1_, bf16[4,6,64,256]{3,2,1,0:T(8,128)(2,1)S(1)} %get-tuple-element.42.mine, bf16[4,6,64,256]{3,2,1,0:T(8,128)(2,1)S(1)} %collective-permute-done.16.after.theirs, ...), custom_call_target="tpu_custom_call" | custom-call | flops 10871635968 | bytes 7077888 | tf_op jit(solution)/shard_map/field/pallas_call | solution.py:566
  89.1 0.9 collective-permute-done.20.west.refs_5_
  90.0 6.2 %collective-permute-done.18.y.refs_3_ = bf16[1744,128]{1,0:T(8,128)(2,1)S(1)} collective-permute-done((bf16[1744,128]{1,0:T(8,128)(2,1)S(1)}, bf16[1744,128]{1,0:T(8,128)(2,1)S(1)}, u32[]{:S(2)}, u32[]{:S(2)}) %collective-permute-start.18) | collective-permute-done | bytes 446496 | tf_op jit(solution)/shard_map/ppermute | solution.py:98
  96.2 1.0 collective-permute-done.17.x.refs_2_
  97.2 1.0 copy-done.12
  98.2 0.7 join.1
  99.0 0.7 collective-permute-start.31
  99.7 3.4 %collective-permute-start.23 = (bf16[2512,128]{1,0:T(8,128)(2,1)S(1)}, bf16[2512,128]{1,0:T(8,128)(2,1)S(1)}, u32[]{:S(2)}, u32[]{:S(2)}) collective-permute-start(bf16[2512,128]{1,0:T(8,128)(2,1)S(1)} %get-tuple-element.46), channel_id=1, source_target_pairs={{0,3},{1,0},{2,1},{3,2},{4,7},{5,4},{6,5},{7,6},{8,11},{9,8},{10,9... | collective-permute-start | bytes 1929224 | tf_op jit(solution)/shard_map/ppermute | solution.py:98
  103.1 1.3 collective-permute-start.30
  104.4 1.5 collective-permute-start.29
  106.0 7.3 %unpack_1.1.after.refs_7_ = f32[27,256,512]{2,1,0:T(8,128)} custom-call(s32[3]{0:T(128)} %copy-done.15, bf16[1744,128]{1,0:T(8,128)(2,1)} %copy-done.3, bf16[1744,128]{1,0:T(8,128)(2,1)} %copy-done.6, bf16[1744,128]{1,0:T(8,128)(2,1)} %copy-done.5, bf16[1744,128]{1,0:T(8,128)(2,1)} %copy-done.4, ...), custom_call_target="tpu_custom_call", output_to_operand_aliasing={{}: (8, {})} | custom-call | bytes 4194304 | tf_op jit(solution)/shard_map/unpack_1/pallas_call | solution.py:398
  113.3 17.9 %collective-permute-done.22.by_3.refs_4_ = bf16[2496,128]{1,0:T(8,128)(2,1)S(1)} collective-permute-done((bf16[2496,128]{1,0:T(8,128)(2,1)S(1)}, bf16[2496,128]{1,0:T(8,128)(2,1)S(1)}, u32[]{:S(2)}, u32[]{:S(2)}) %collective-permute-start.22) | collective-permute-done | bytes 639008 | tf_op jit(solution)/shard_map/ppermute | solution.py:98
  131.2 5.2 %copy-done = f32[27,256,512]{2,1,0:T(8,128)S(1)} copy-done((f32[27,256,512]{2,1,0:T(8,128)S(1)}, f32[27,256,512]{2,1,0:T(8,128)}, u32[]{:S(2)}) %copy-start) | copy-done | bytes 14155800
  137.1 1.5 collective-permute-start.28
  138.5 0.7 collective-permute-start.27
  139.3 1.3 collective-permute-start.26
  140.6 1.8 %collective-permute-start.24 = (bf16[928,128]{1,0:T(8,128)(2,1)S(1)}, bf16[928,128]{1,0:T(8,128)(2,1)S(1)}, u32[]{:S(2)}, u32[]{:S(2)}) collective-permute-start(bf16[928,128]{1,0:T(8,128)(2,1)S(1)} %get-tuple-element.49), channel_id=1, source_target_pairs={{0,1},{1,2},{2,3},{3,0},{4,5},{5,6},{6,7},{7,4},{8,9},{9,10},{10,1... | collective-permute-start | bytes 712712 | tf_op jit(solution)/shard_map/ppermute | solution.py:98
  142.4 2.0 %collective-permute-start.25 = (bf16[928,128]{1,0:T(8,128)(2,1)S(1)}, bf16[928,128]{1,0:T(8,128)(2,1)S(1)}, u32[]{:S(2)}, u32[]{:S(2)}) collective-permute-start(bf16[928,128]{1,0:T(8,128)(2,1)S(1)} %get-tuple-element.50), channel_id=1, source_target_pairs={{0,3},{1,0},{2,1},{3,2},{4,7},{5,4},{6,5},{7,6},{8,11},{9,8},{10,9... | collective-permute-start | bytes 712712 | tf_op jit(solution)/shard_map/ppermute | solution.py:98
  144.5 11.3 %unpack_2.1.refs_6_ = f32[27,256,512]{2,1,0:T(8,128)} custom-call(s32[3]{0:T(128)} %copy-done.15, bf16[2592,128]{1,0:T(8,128)(2,1)} %copy-done.19, bf16[2592,128]{1,0:T(8,128)(2,1)} %copy-done.18, bf16[2592,128]{1,0:T(8,128)(2,1)} %copy-done.17, bf16[2496,128]{1,0:T(8,128)(2,1)} %copy-done.2, ...), custom_call_target="tpu_custom_call", output_to_operand_aliasing={{}: (7, {})} | custom-call | bytes 4194304 | tf_op jit(solution)/shard_map/unpack_2/pallas_call | solution.py:398
  156.8 0.7 copy-done.22
  157.5 6.0 %unpack_3.1 = f32[27,256,512]{2,1,0:T(8,128)} custom-call(s32[3]{0:T(128)} %copy-done.15, bf16[928,128]{1,0:T(8,128)(2,1)} %copy-done.23, bf16[928,128]{1,0:T(8,128)(2,1)} %copy-done.24, bf16[1296,128]{1,0:T(8,128)(2,1)} %copy-done.22, bf16[1296,128]{1,0:T(8,128)(2,1)} %copy-done.21, bf16[1296,128]{1,0:T(8,128)(2,1)} %copy-done.20, ...), custom_call_target="tpu_custom_call", output_to_operand_aliasing={{}: (6, {})} | custom-call | bytes 4194304 | tf_op jit(solution)/shard_map/unpack_3/pallas_call | solution.py:398
  (80 shorter events, 4.4 us)
Async XLA Ops:
  0.7 96.5 %copy-start.15 = (s32[3]{0:T(128)}, s32[3]{0:T(128)S(1)}, u32[]{:S(2)}) copy-start(s32[3]{0:T(128)S(1)} %pad_add_fusion.pos.refs_0_) | copy-start | bytes 40
  3.6 18.4 %collective-permute-start.3 = (bf16[768,128]{1,0:T(8,128)(2,1)S(1)}, bf16[768,128]{1,0:T(8,128)(2,1)S(1)}, u32[]{:S(2)}, u32[]{:S(2)}) collective-permute-start(bf16[768,128]{1,0:T(8,128)(2,1)S(1)} %get-tuple-element.31), channel_id=1, source_target_pairs={{0,0},{1,1},{2,2},{3,3},{4,4},{5,5},{6,6},{7,7},{8,16},{9,17},{10,... | collective-permute-start | bytes 589832 | tf_op jit(solution)/shard_map/ppermute | solution.py:98
  4.2 17.7 %collective-permute-start.4 = (bf16[768,128]{1,0:T(8,128)(2,1)S(1)}, bf16[768,128]{1,0:T(8,128)(2,1)S(1)}, u32[]{:S(2)}, u32[]{:S(2)}) collective-permute-start(bf16[768,128]{1,0:T(8,128)(2,1)S(1)} %get-tuple-element.32), channel_id=1, source_target_pairs={{0,4},{1,5},{2,6},{3,7},{4,0},{5,1},{6,2},{7,3},{8,20},{9,21},{10,... | collective-permute-start | bytes 589832 | tf_op jit(solution)/shard_map/ppermute | solution.py:98
  7.2 11.7 %collective-permute-start = (bf16[416,128]{1,0:T(8,128)(2,1)S(1)}, bf16[416,128]{1,0:T(8,128)(2,1)S(1)}, u32[]{:S(2)}, u32[]{:S(2)}) collective-permute-start(bf16[416,128]{1,0:T(8,128)(2,1)S(1)} %get-tuple-element.28), channel_id=1, source_target_pairs={{0,1},{1,2},{2,3},{3,0},{4,5},{5,6},{6,7},{7,4},{8,9},{9,10},{10,1... | collective-permute-start | bytes 319496 | tf_op jit(solution)/shard_map/ppermute | solution.py:98
  8.8 10.1 %collective-permute-start.1 = (bf16[384,128]{1,0:T(8,128)(2,1)S(1)}, bf16[384,128]{1,0:T(8,128)(2,1)S(1)}, u32[]{:S(2)}, u32[]{:S(2)}) collective-permute-start(bf16[384,128]{1,0:T(8,128)(2,1)S(1)} %get-tuple-element.29), channel_id=1, source_target_pairs={{0,2},{1,3},{2,0},{3,1},{4,6},{5,7},{6,4},{7,5},{8,10},{9,11},{10,... | collective-permute-start | bytes 294920 | tf_op jit(solution)/shard_map/ppermute | solution.py:98
  11.4 10.6 %collective-permute-start.2 = (bf16[416,128]{1,0:T(8,128)(2,1)S(1)}, bf16[416,128]{1,0:T(8,128)(2,1)S(1)}, u32[]{:S(2)}, u32[]{:S(2)}) collective-permute-start(bf16[416,128]{1,0:T(8,128)(2,1)S(1)} %get-tuple-element.30), channel_id=1, source_target_pairs={{0,3},{1,0},{2,1},{3,2},{4,7},{5,4},{6,5},{7,6},{8,11},{9,8},{10,9... | collective-permute-start | bytes 319496 | tf_op jit(solution)/shard_map/ppermute | solution.py:98
  18.9 7.3 %collective-permute-start.10 = (bf16[384,128]{1,0:T(8,128)(2,1)S(1)}, bf16[384,128]{1,0:T(8,128)(2,1)S(1)}, u32[]{:S(2)}, u32[]{:S(2)}) collective-permute-start(bf16[384,128]{1,0:T(8,128)(2,1)S(1)} %get-tuple-element.36), channel_id=1, source_target_pairs={{0,4},{1,5},{2,6},{3,7},{4,0},{5,1},{6,2},{7,3},{8,12},{9,13},{10,... | collective-permute-start | bytes 294920 | tf_op jit(solution)/shard_map/ppermute | solution.py:98
  18.9 10.1 %collective-permute-start.11 = (bf16[384,128]{1,0:T(8,128)(2,1)S(1)}, bf16[384,128]{1,0:T(8,128)(2,1)S(1)}, u32[]{:S(2)}, u32[]{:S(2)}) collective-permute-start(bf16[384,128]{1,0:T(8,128)(2,1)S(1)} %get-tuple-element.37), channel_id=1, source_target_pairs={{0,12},{1,13},{2,14},{3,15},{4,8},{5,9},{6,10},{7,11},{8,4},{9,5},... | collective-permute-start | bytes 294920 | tf_op jit(solution)/shard_map/ppermute | solution.py:98
  22.7 22.6 %collective-permute-start.7 = (bf16[1600,128]{1,0:T(8,128)(2,1)S(1)}, bf16[1600,128]{1,0:T(8,128)(2,1)S(1)}, u32[]{:S(2)}, u32[]{:S(2)}) collective-permute-start(bf16[1600,128]{1,0:T(8,128)(2,1)S(1)} %get-tuple-element.33.own.x_own), channel_id=1, source_target_pairs={{0,12},{1,13},{2,14},{3,15},{4,8},{5,9},{6,10},{7,11},{8,4},{9,5},... | collective-permute-start | bytes 1228808 | tf_op jit(solution)/shard_map/ppermute | solution.py:98
  22.8 22.5 %collective-permute-start.5 = (bf16[1600,128]{1,0:T(8,128)(2,1)S(1)}, bf16[1600,128]{1,0:T(8,128)(2,1)S(1)}, u32[]{:S(2)}, u32[]{:S(2)}) collective-permute-start(bf16[1600,128]{1,0:T(8,128)(2,1)S(1)} %get-tuple-element.33.own.x_own), channel_id=1, source_target_pairs={{0,4},{1,5},{2,6},{3,7},{4,0},{5,1},{6,2},{7,3},{8,12},{9,13},{10,... | collective-permute-start | bytes 1228808 | tf_op jit(solution)/shard_map/ppermute | solution.py:98
  24.6 18.9 %collective-permute-start.6 = (bf16[1536,128]{1,0:T(8,128)(2,1)S(1)}, bf16[1536,128]{1,0:T(8,128)(2,1)S(1)}, u32[]{:S(2)}, u32[]{:S(2)}) collective-permute-start(bf16[1536,128]{1,0:T(8,128)(2,1)S(1)} %get-tuple-element.34), channel_id=1, source_target_pairs={{0,8},{1,9},{2,10},{3,11},{4,12},{5,13},{6,14},{7,15},{8,0},{9,1},... | collective-permute-start | bytes 1179656 | tf_op jit(solution)/shard_map/ppermute | solution.py:98
  26.2 17.3 %collective-permute-start.9 = (bf16[2,768,128]{2,1,0:T(8,128)(2,1)S(1)}, bf16[2,768,128]{2,1,0:T(8,128)(2,1)S(1)}, u32[]{:S(2)}, u32[]{:S(2)}) collective-permute-start(bf16[2,768,128]{2,1,0:T(8,128)(2,1)S(1)} %get-tuple-element.35.here), channel_id=1, source_target_pairs={{0,3},{1,0},{2,1},{3,2},{4,7},{5,4},{6,5},{7,6},{8,11},{9,8},{10,9... | collective-permute-start | bytes 1179656 | tf_op jit(solution)/shard_map/ppermute | solution.py:98
  29.0 16.3 %collective-permute-start.8 = (bf16[2,768,128]{2,1,0:T(8,128)(2,1)S(1)}, bf16[2,768,128]{2,1,0:T(8,128)(2,1)S(1)}, u32[]{:S(2)}, u32[]{:S(2)}) collective-permute-start(bf16[2,768,128]{2,1,0:T(8,128)(2,1)S(1)} %get-tuple-element.35.here), channel_id=1, source_target_pairs={{0,1},{1,2},{2,3},{3,0},{4,5},{5,6},{6,7},{7,4},{8,9},{9,10},{10,1... | collective-permute-start | bytes 1179656 | tf_op jit(solution)/shard_map/ppermute | solution.py:98
  47.1 15.2 %collective-permute-start.12 = (bf16[6,768,128]{2,1,0:T(8,128)(2,1)S(1)}, bf16[6,768,128]{2,1,0:T(8,128)(2,1)S(1)}, u32[]{:S(2)}, u32[]{:S(2)}) collective-permute-start(bf16[6,768,128]{2,1,0:T(8,128)(2,1)S(1)} %get-tuple-element.40.g), channel_id=1, source_target_pairs={{0,16},{1,17},{2,18},{3,19},{4,20},{5,21},{6,22},{7,23},{8,24},{9,... | collective-permute-start | bytes 3538952 | tf_op jit(solution)/shard_map/ppermute | solution.py:98
  47.2 8.2 %collective-permute-start.14 = (bf16[768,128]{1,0:T(8,128)(2,1)S(1)}, bf16[768,128]{1,0:T(8,128)(2,1)S(1)}, u32[]{:S(2)}, u32[]{:S(2)}) collective-permute-start(bf16[768,128]{1,0:T(8,128)(2,1)S(1)} %get-tuple-element.41), channel_id=1, source_target_pairs={{0,3},{1,0},{2,1},{3,2},{4,7},{5,4},{6,5},{7,6},{8,11},{9,8},{10,9... | collective-permute-start | bytes 589832 | tf_op jit(solution)/shard_map/ppermute | solution.py:98
  50.1 9.8 %collective-permute-start.13 = (bf16[768,128]{1,0:T(8,128)(2,1)S(1)}, bf16[768,128]{1,0:T(8,128)(2,1)S(1)}, u32[]{:S(2)}, u32[]{:S(2)}) collective-permute-start(bf16[768,128]{1,0:T(8,128)(2,1)S(1)} %get-tuple-element.38.after), channel_id=1, source_target_pairs={{0,1},{1,2},{2,3},{3,0},{4,5},{5,6},{6,7},{7,4},{8,9},{9,10},{10,1... | collective-permute-start | bytes 589832 | tf_op jit(solution)/shard_map/ppermute | solution.py:98
  60.5 1.8 %collective-permute-start.15 = (bf16[2,768,128]{2,1,0:T(8,128)(2,1)S(1)}, bf16[2,768,128]{2,1,0:T(8,128)(2,1)S(1)}, u32[]{:S(2)}, u32[]{:S(2)}) collective-permute-start(bf16[2,768,128]{2,1,0:T(8,128)(2,1)S(1)} %pair.1.g2), channel_id=1, source_target_pairs={{0,16},{1,17},{2,18},{3,19},{4,20},{5,21},{6,22},{7,23},{8,24},{9,... | collective-permute-start | bytes 1179656 | tf_op jit(solution)/shard_map/ppermute | solution.py:98
  60.6 10.3 %collective-permute-start.16 = (bf16[4,6,64,256]{3,2,1,0:T(8,128)(2,1)S(1)}, bf16[4,6,64,256]{3,2,1,0:T(8,128)(2,1)S(1)}, u32[]{:S(2)}, u32[]{:S(2)}) collective-permute-start(bf16[4,6,64,256]{3,2,1,0:T(8,128)(2,1)S(1)} %get-tuple-element.42.mine), channel_id=1, source_target_pairs={{0,16},{1,17},{2,18},{3,19},{4,20},{5,21},{6,22},{7,23},{8,24},{9,... | collective-permute-start | bytes 2359304 | tf_op jit(solution)/shard_map/ppermute | solution.py:98
  71.8 25.4 %copy-start.3 = (bf16[1744,128]{1,0:T(8,128)(2,1)}, bf16[1744,128]{1,0:T(8,128)(2,1)S(1)}, u32[]{:S(2)}) copy-start(bf16[1744,128]{1,0:T(8,128)(2,1)S(1)} %get-tuple-element.43.after.own.refs_1_) | copy-start | bytes 1339396
  71.8 17.3 %collective-permute-start.21 = (bf16[1296,128]{1,0:T(8,128)(2,1)S(1)}, bf16[1296,128]{1,0:T(8,128)(2,1)S(1)}, u32[]{:S(2)}, u32[]{:S(2)}) collective-permute-start(bf16[1296,128]{1,0:T(8,128)(2,1)S(1)} %get-tuple-element.44), channel_id=1, source_target_pairs={{0,3},{1,0},{2,1},{3,2},{4,7},{5,4},{6,5},{7,6},{8,11},{9,8},{10,9... | collective-permute-start | bytes 995336 | tf_op jit(solution)/shard_map/ppermute | solution.py:98
  73.6 16.4 %collective-permute-start.20 = (bf16[1296,128]{1,0:T(8,128)(2,1)S(1)}, bf16[1296,128]{1,0:T(8,128)(2,1)S(1)}, u32[]{:S(2)}, u32[]{:S(2)}) collective-permute-start(bf16[1296,128]{1,0:T(8,128)(2,1)S(1)} %get-tuple-element.44), channel_id=1, source_target_pairs={{0,1},{1,2},{2,3},{3,0},{4,5},{5,6},{6,7},{7,4},{8,9},{9,10},{10,1... | collective-permute-start | bytes 995336 | tf_op jit(solution)/shard_map/ppermute | solution.py:98
  73.9 16.1 %collective-permute-start.19 = (bf16[1744,128]{1,0:T(8,128)(2,1)S(1)}, bf16[1744,128]{1,0:T(8,128)(2,1)S(1)}, u32[]{:S(2)}, u32[]{:S(2)}) collective-permute-start(bf16[1744,128]{1,0:T(8,128)(2,1)S(1)} %get-tuple-element.43.after.own.refs_1_), channel_id=1, source_target_pairs={{0,12},{1,13},{2,14},{3,15},{4,8},{5,9},{6,10},{7,11},{8,4},{9,5},... | collective-permute-start | bytes 1339400 | tf_op jit(solution)/shard_map/ppermute | solution.py:98
  75.5 20.7 %collective-permute-start.18 = (bf16[1744,128]{1,0:T(8,128)(2,1)S(1)}, bf16[1744,128]{1,0:T(8,128)(2,1)S(1)}, u32[]{:S(2)}, u32[]{:S(2)}) collective-permute-start(bf16[1744,128]{1,0:T(8,128)(2,1)S(1)} %get-tuple-element.43.after.own.refs_1_), channel_id=1, source_target_pairs={{0,8},{1,9},{2,10},{3,11},{4,12},{5,13},{6,14},{7,15},{8,0},{9,1},... | collective-permute-start | bytes 1339400 | tf_op jit(solution)/shard_map/ppermute | solution.py:98
  76.6 20.5 %collective-permute-start.17 = (bf16[1744,128]{1,0:T(8,128)(2,1)S(1)}, bf16[1744,128]{1,0:T(8,128)(2,1)S(1)}, u32[]{:S(2)}, u32[]{:S(2)}) collective-permute-start(bf16[1744,128]{1,0:T(8,128)(2,1)S(1)} %get-tuple-element.43.after.own.refs_1_), channel_id=1, source_target_pairs={{0,4},{1,5},{2,6},{3,7},{4,0},{5,1},{6,2},{7,3},{8,12},{9,13},{10,... | collective-permute-start | bytes 1339400 | tf_op jit(solution)/shard_map/ppermute | solution.py:98
  89.1 16.8 %copy-start.9 = (bf16[1296,128]{1,0:T(8,128)(2,1)}, bf16[1296,128]{1,0:T(8,128)(2,1)S(1)}, u32[]{:S(2)}) copy-start(bf16[1296,128]{1,0:T(8,128)(2,1)S(1)} %collective-permute-done.21.east.refs_6_) | copy-start | bytes 995332
  90.0 16.0 %copy-start.10 = (bf16[1296,128]{1,0:T(8,128)(2,1)}, bf16[1296,128]{1,0:T(8,128)(2,1)S(1)}, u32[]{:S(2)}) copy-start(bf16[1296,128]{1,0:T(8,128)(2,1)S(1)} %collective-permute-done.20.west.refs_5_) | copy-start | bytes 995332
  90.0 16.0 %copy-start.4 = (bf16[1744,128]{1,0:T(8,128)(2,1)}, bf16[1744,128]{1,0:T(8,128)(2,1)S(1)}, u32[]{:S(2)}) copy-start(bf16[1744,128]{1,0:T(8,128)(2,1)S(1)} %collective-permute-done.19.d.refs_4_) | copy-start | bytes 1339396
  96.2 9.8 %copy-start.5 = (bf16[1744,128]{1,0:T(8,128)(2,1)}, bf16[1744,128]{1,0:T(8,128)(2,1)S(1)}, u32[]{:S(2)}) copy-start(bf16[1744,128]{1,0:T(8,128)(2,1)S(1)} %collective-permute-done.18.y.refs_3_) | copy-start | bytes 1339396
  98.2 7.8 %copy-start.6 = (bf16[1744,128]{1,0:T(8,128)(2,1)}, bf16[1744,128]{1,0:T(8,128)(2,1)S(1)}, u32[]{:S(2)}) copy-start(bf16[1744,128]{1,0:T(8,128)(2,1)S(1)} %collective-permute-done.17.x.refs_2_) | copy-start | bytes 1339396
  99.0 7.0 %copy-start.11 = (bf16[2592,128]{1,0:T(8,128)(2,1)}, bf16[2592,128]{1,0:T(8,128)(2,1)S(1)}, u32[]{:S(2)}) copy-start(bf16[2592,128]{1,0:T(8,128)(2,1)S(1)} %get-tuple-element.47.refs_7_) | copy-start | bytes 1990660
  99.0 40.3 %collective-permute-start.31 = (bf16[2592,128]{1,0:T(8,128)(2,1)S(1)}, bf16[2592,128]{1,0:T(8,128)(2,1)S(1)}, u32[]{:S(2)}, u32[]{:S(2)}) collective-permute-start(bf16[2592,128]{1,0:T(8,128)(2,1)S(1)} %get-tuple-element.47.refs_7_), channel_id=1, source_target_pairs={{0,12},{1,13},{2,14},{3,15},{4,8},{5,9},{6,10},{7,11},{8,4},{9,5},... | collective-permute-start | bytes 1990664 | tf_op jit(solution)/shard_map/ppermute | solution.py:98
  99.7 31.5 %collective-permute-start.23 = (bf16[2512,128]{1,0:T(8,128)(2,1)S(1)}, bf16[2512,128]{1,0:T(8,128)(2,1)S(1)}, u32[]{:S(2)}, u32[]{:S(2)}) collective-permute-start(bf16[2512,128]{1,0:T(8,128)(2,1)S(1)} %get-tuple-element.46), channel_id=1, source_target_pairs={{0,3},{1,0},{2,1},{3,2},{4,7},{5,4},{6,5},{7,6},{8,11},{9,8},{10,9... | collective-permute-start | bytes 1929224 | tf_op jit(solution)/shard_map/ppermute | solution.py:98
  103.1 28.1 %collective-permute-start.22 = (bf16[2496,128]{1,0:T(8,128)(2,1)S(1)}, bf16[2496,128]{1,0:T(8,128)(2,1)S(1)}, u32[]{:S(2)}, u32[]{:S(2)}) collective-permute-start(bf16[2496,128]{1,0:T(8,128)(2,1)S(1)} %get-tuple-element.45), channel_id=1, source_target_pairs={{0,1},{1,2},{2,3},{3,0},{4,5},{5,6},{6,7},{7,4},{8,9},{9,10},{10,1... | collective-permute-start | bytes 1916936 | tf_op jit(solution)/shard_map/ppermute | solution.py:98
  103.1 37.5 %collective-permute-start.30 = (bf16[2592,128]{1,0:T(8,128)(2,1)S(1)}, bf16[2592,128]{1,0:T(8,128)(2,1)S(1)}, u32[]{:S(2)}, u32[]{:S(2)}) collective-permute-start(bf16[2592,128]{1,0:T(8,128)(2,1)S(1)} %get-tuple-element.47.refs_7_), channel_id=1, source_target_pairs={{0,8},{1,9},{2,10},{3,11},{4,12},{5,13},{6,14},{7,15},{8,0},{9,1},... | collective-permute-start | bytes 1990664 | tf_op jit(solution)/shard_map/ppermute | solution.py:98
  104.4 38.0 %collective-permute-start.29 = (bf16[2592,128]{1,0:T(8,128)(2,1)S(1)}, bf16[2592,128]{1,0:T(8,128)(2,1)S(1)}, u32[]{:S(2)}, u32[]{:S(2)}) collective-permute-start(bf16[2592,128]{1,0:T(8,128)(2,1)S(1)} %get-tuple-element.47.refs_7_), channel_id=1, source_target_pairs={{0,4},{1,5},{2,6},{3,7},{4,0},{5,1},{6,2},{7,3},{8,12},{9,13},{10,... | collective-permute-start | bytes 1990664 | tf_op jit(solution)/shard_map/ppermute | solution.py:98
  106.0 25.2 %copy-start.16 = (s32[3]{0:T(128)S(1)}, s32[3]{0:T(128)}, u32[]{:S(2)}) copy-start(s32[3]{0:T(128)} %copy-done.15) | copy-start | bytes 40
  131.2 13.3 %copy-start.2 = (bf16[2496,128]{1,0:T(8,128)(2,1)}, bf16[2496,128]{1,0:T(8,128)(2,1)S(1)}, u32[]{:S(2)}) copy-start(bf16[2496,128]{1,0:T(8,128)(2,1)S(1)} %collective-permute-done.22.by_3.refs_4_) | copy-start | bytes 1916932
  131.2 5.3 %copy-start = (f32[27,256,512]{2,1,0:T(8,128)S(1)}, f32[27,256,512]{2,1,0:T(8,128)}, u32[]{:S(2)}) copy-start(f32[27,256,512]{2,1,0:T(8,128)} %unpack_1.1.after.refs_7_) | copy-start | bytes 42467332
  136.5 8.0 %copy-start.1 = (bf16[2512,128]{1,0:T(8,128)(2,1)}, bf16[2512,128]{1,0:T(8,128)(2,1)S(1)}, u32[]{:S(2)}) copy-start(bf16[2512,128]{1,0:T(8,128)(2,1)S(1)} %collective-permute-done.23.by_1.refs_5_) | copy-start | bytes 1929220
  137.1 7.4 %copy-start.14 = (bf16[1296,128]{1,0:T(8,128)(2,1)}, bf16[1296,128]{1,0:T(8,128)(2,1)S(1)}, u32[]{:S(2)}) copy-start(bf16[1296,128]{1,0:T(8,128)(2,1)S(1)} %get-tuple-element.51.refs_6_) | copy-start | bytes 995332
  137.1 18.8 %collective-permute-start.28 = (bf16[1296,128]{1,0:T(8,128)(2,1)S(1)}, bf16[1296,128]{1,0:T(8,128)(2,1)S(1)}, u32[]{:S(2)}, u32[]{:S(2)}) collective-permute-start(bf16[1296,128]{1,0:T(8,128)(2,1)S(1)} %get-tuple-element.51.refs_6_), channel_id=1, source_target_pairs={{0,12},{1,13},{2,14},{3,15},{4,8},{5,9},{6,10},{7,11},{8,4},{9,5},... | collective-permute-start | bytes 995336 | tf_op jit(solution)/shard_map/ppermute | solution.py:98
  138.5 17.3 %collective-permute-start.27 = (bf16[1296,128]{1,0:T(8,128)(2,1)S(1)}, bf16[1296,128]{1,0:T(8,128)(2,1)S(1)}, u32[]{:S(2)}, u32[]{:S(2)}) collective-permute-start(bf16[1296,128]{1,0:T(8,128)(2,1)S(1)} %get-tuple-element.51.refs_6_), channel_id=1, source_target_pairs={{0,8},{1,9},{2,10},{3,11},{4,12},{5,13},{6,14},{7,15},{8,0},{9,1},... | collective-permute-start | bytes 995336 | tf_op jit(solution)/shard_map/ppermute | solution.py:98
  139.3 5.2 %copy-start.17 = (bf16[2592,128]{1,0:T(8,128)(2,1)}, bf16[2592,128]{1,0:T(8,128)(2,1)S(1)}, u32[]{:S(2)}) copy-start(bf16[2592,128]{1,0:T(8,128)(2,1)S(1)} %collective-permute-done.31.refs_3_) | copy-start | bytes 1990660
  139.3 16.6 %collective-permute-start.26 = (bf16[1296,128]{1,0:T(8,128)(2,1)S(1)}, bf16[1296,128]{1,0:T(8,128)(2,1)S(1)}, u32[]{:S(2)}, u32[]{:S(2)}) collective-permute-start(bf16[1296,128]{1,0:T(8,128)(2,1)S(1)} %get-tuple-element.51.refs_6_), channel_id=1, source_target_pairs={{0,4},{1,5},{2,6},{3,7},{4,0},{5,1},{6,2},{7,3},{8,12},{9,13},{10,... | collective-permute-start | bytes 995336 | tf_op jit(solution)/shard_map/ppermute | solution.py:98
  140.6 3.8 %copy-start.18 = (bf16[2592,128]{1,0:T(8,128)(2,1)}, bf16[2592,128]{1,0:T(8,128)(2,1)S(1)}, u32[]{:S(2)}) copy-start(bf16[2592,128]{1,0:T(8,128)(2,1)S(1)} %collective-permute-done.30.refs_2_) | copy-start | bytes 1990660
  140.6 15.1 %collective-permute-start.24 = (bf16[928,128]{1,0:T(8,128)(2,1)S(1)}, bf16[928,128]{1,0:T(8,128)(2,1)S(1)}, u32[]{:S(2)}, u32[]{:S(2)}) collective-permute-start(bf16[928,128]{1,0:T(8,128)(2,1)S(1)} %get-tuple-element.49), channel_id=1, source_target_pairs={{0,1},{1,2},{2,3},{3,0},{4,5},{5,6},{6,7},{7,4},{8,9},{9,10},{10,1... | collective-permute-start | bytes 712712 | tf_op jit(solution)/shard_map/ppermute | solution.py:98
  142.4 2.1 %copy-start.19 = (bf16[2592,128]{1,0:T(8,128)(2,1)}, bf16[2592,128]{1,0:T(8,128)(2,1)S(1)}, u32[]{:S(2)}) copy-start(bf16[2592,128]{1,0:T(8,128)(2,1)S(1)} %collective-permute-done.29.refs_1_) | copy-start | bytes 1990660
  142.4 13.4 %collective-permute-start.25 = (bf16[928,128]{1,0:T(8,128)(2,1)S(1)}, bf16[928,128]{1,0:T(8,128)(2,1)S(1)}, u32[]{:S(2)}, u32[]{:S(2)}) collective-permute-start(bf16[928,128]{1,0:T(8,128)(2,1)S(1)} %get-tuple-element.50), channel_id=1, source_target_pairs={{0,3},{1,0},{2,1},{3,2},{4,7},{5,4},{6,5},{7,6},{8,11},{9,8},{10,9... | collective-permute-start | bytes 712712 | tf_op jit(solution)/shard_map/ppermute | solution.py:98
  (9 other events, 8.0 us)

commit v8 on v7

--- a/solution.py
+++ b/solution.py
@@ -326,7 +326,7 @@
     late[27 * span - skip :, :] = unit.astype(out.dtype)
 
 
-def join_kernel(pos, own, x, y, d, west, east, after, both, by_3, by_1):
+def join_kernel(pos, west, east, own, x, y, d, after, both, by_3, by_1):
     del pos, after
     size = west.shape[0]
     cut = own.shape[0] - size
@@ -353,56 +353,56 @@
     early_1[...] = by_1[size - half + many :, :]
 
 
-def unpack_kernel(pos, *refs, pieces, span):
-    count = 1 + max(piece[0] for piece in pieces)
+def unpack_kernel(pos, *refs, slabs, count, span, group):
     sources = refs[:count]
-    total, buffers, sems = refs[-3:]
-    wide = buffers.shape[-1]
-
-    def target(piece):
-        _, _, _, first, many, tag, step = piece
-        lon_at = lax.rem(pos[2] + step, 4) * span
-        lat_at = (pos[1] ^ tag) * wide
-        return total.at[
-            pl.ds(first, many),
-            pl.ds(pl.multiple_of(lon_at, span), span),
-            pl.ds(pl.multiple_of(lat_at, wide), wide),
-        ]
+    total, token, buffers, sems = refs[-4:]
+    wide = buffers.shape[-1] // 4
+    token[...] = jnp.zeros_like(token)
+    parts = []
+    for step, first, taps, pieces in slabs:
+        for at in range(0, taps, group):
+            parts.append((step, first + at, min(group, taps - at), at, pieces))
 
     def copy(at):
-        piece = pieces[at]
-        return pltpu.make_async_copy(buffers.at[at % 2, pl.ds(0, piece[4])], target(piece), sems.at[at % 2])
-
-    for at, (which, row, power_row, _, many, _, _) in enumerate(pieces):
+        step, first, many, _, _ = parts[at]
+        lon_at = pl.multiple_of(lax.rem(pos[2] + step, 4) * span, span)
+        return pltpu.make_async_copy(
+            buffers.at[at % 2, pl.ds(0, many)], total.at[pl.ds(first, many), pl.ds(lon_at, span)], sems.at[at % 2]
+        )
+
+    for at, (_, _, many, skip, pieces) in enumerate(parts):
         if at >= 2:
             copy(at - 2).wait()
-        source = sources[which]
-        unit = source[power_row : power_row + 16, :].astype(jnp.float32)[0:1]
-
-        @pl.loop(0, many)
-        def _(tap, source=source, row=row, unit=unit, at=at):
-            code = source[pl.ds(pl.multiple_of(row + tap * span, 16), span), :].astype(jnp.float32)
-            root = lax.rsqrt(lax.rsqrt(jnp.abs(code)))
-            root = root * lax.rsqrt(jnp.maximum(root, 1e-30)) * unit
-            buffers[at % 2, tap] = jnp.where(code < 0, -root, root)
+        for tag, (which, row, power_row) in enumerate(pieces):
+            source = sources[which]
+            unit = source[power_row : power_row + 16, :].astype(jnp.float32)[0:1]
+            lanes = pl.ds(pl.multiple_of((pos[1] ^ tag) * wide, wide), wide)
+
+            @pl.loop(0, many)
+            def _(tap, source=source, start=row + skip * span, unit=unit, lanes=lanes, at=at):
+                code = source[pl.ds(pl.multiple_of(start + tap * span, 16), span), :].astype(jnp.float32)
+                root = lax.rsqrt(lax.rsqrt(jnp.abs(code)))
+                root = root * lax.rsqrt(jnp.maximum(root, 1e-30)) * unit
+                buffers[at % 2, tap, :, lanes] = jnp.where(code < 0, -root, root)
 
         copy(at).start()
-    for at in range(max(len(pieces) - 2, 0), len(pieces)):
+    for at in range(max(len(parts) - 2, 0), len(parts)):
         copy(at).wait()
 
 
-def unpack(pos, total, sources, after, pieces, span, name):
-    most = max(piece[4] for piece in pieces)
-    wide = sources[0].shape[-1]
+def unpack(pos, total, sources, after, slabs, span, name):
+    group = 7
+    wide = total.shape[2]
     ins = (pos, *sources, *after, total)
+    token = jax.ShapeDtypeStruct((8, 128), jnp.float32)
     return pl.pallas_call(
-        lambda *refs: unpack_kernel(*refs, pieces=pieces, span=span),
-        out_shape=jax.ShapeDtypeStruct(total.shape, total.dtype),
+        lambda *refs: unpack_kernel(*refs, slabs=slabs, count=len(sources), span=span, group=group),
+        out_shape=[jax.ShapeDtypeStruct(total.shape, total.dtype), token],
         in_specs=[pl.BlockSpec(memory_space=SMEM)]
         + [pl.BlockSpec(memory_space=VMEM)] * len(sources)
         + [pl.BlockSpec(memory_space=pl.ANY)] * (len(after) + 1),
-        out_specs=pl.BlockSpec(memory_space=pl.ANY),
-        scratch_shapes=[VMEM((2, most, span, wide), jnp.float32), pltpu.SemaphoreType.DMA((2,))],
+        out_specs=[pl.BlockSpec(memory_space=pl.ANY), pl.BlockSpec(memory_space=VMEM)],
+        scratch_shapes=[VMEM((2, group, span, wide), jnp.float32), pltpu.SemaphoreType.DMA((2,))],
         input_output_aliases={len(ins) - 1: 0},
         cost_estimate=pl.CostEstimate(flops=0, bytes_accessed=4 * 2**20, transcendentals=0),
         compiler_params=pltpu.CompilerParams(vmem_limit_bytes=54 * 1024 * 1024),
@@ -595,7 +595,7 @@
     pair, z_3, z_1 = call(
         join_kernel,
         [slab(2 * size), slab(half + 4 * first_rows), slab(size - half + 4 * first_rows)],
-        (pos, *plane, from_3, from_1, field),
+        (pos, from_3, from_1, *plane, field),
         [],
         0,
         "join",
@@ -605,22 +605,18 @@
     both = to_plane(pair)
     by_3 = move(z_3, lon_by(1))
     by_1 = move(z_1, lon_by(-1))
-    def late_piece(which, tag, step, row=0):
-        return (which, row, row + size - 16, early, 27 - early, tag, step)
-
-    def early_pieces(which, row, tags, step):
-        return [
-            (which, row + at * first_rows, row + at * first_rows + cut, 0, early, tag, step)
-            for at, tag in enumerate(tags)
-        ]
-
-    pieces = [(tag, 0, end, 0, 27, tag, 0) for tag in range(4)]
-    pieces += [late_piece(4, 0, 3), late_piece(5, 0, 1)]
-    total = unpack(pos, total, plane + [from_3, from_1], [pair], pieces, span, "unpack_1")
+    def late_piece(which, row=0):
+        return (which, row, row + size - 16)
+
+    def early_piece(which, row):
+        return (which, row, row + cut)
+
+    slabs = [(0, 0, 27, [(tag, 0, end) for tag in range(4)])]
+    total, token = unpack(pos, total, plane, [pair], slabs, span, "unpack_1")
     from_2, early_3, early_1 = call(
         across_kernel,
         [slab(size), slab(2 * first_rows), slab(2 * first_rows)],
-        (pos, by_3, by_1, total),
+        (pos, by_3, by_1, token),
         [],
         0,
         "across",
@@ -631,14 +627,18 @@
     early_2a = move(early_3, lon_by(1))
     early_2b = move(early_1, lon_by(-1))
 
-    pieces = [late_piece(tag - 1, tag, 3) for tag in (1, 2, 3)]
-    pieces += [late_piece(tag - 1, tag, 1, size) for tag in (1, 2, 3)]
-    pieces += early_pieces(3, half, (0, 1, 2, 3), 3) + early_pieces(4, size - half, (0, 1, 2, 3), 1)
-    pieces += [late_piece(5, 0, 2)]
-    total = unpack(pos, total, both + [by_3, by_1, from_2], [], pieces, span, "unpack_2")
-    pieces = early_pieces(0, 0, (0, 1), 2) + early_pieces(1, 0, (2, 3), 2)
-    pieces += [late_piece(tag + 1, tag, 2) for tag in (1, 2, 3)]
-    total = unpack(pos, total, [early_2a, early_2b] + across, [], pieces, span, "unpack_3")
+    slabs = [
+        (3, early, 27 - early, [late_piece(5)] + [late_piece(at) for at in range(3)]),
+        (1, early, 27 - early, [late_piece(6)] + [late_piece(at, size) for at in range(3)]),
+        (3, 0, early, [early_piece(3, half + tag * first_rows) for tag in range(4)]),
+        (1, 0, early, [early_piece(4, size - half + tag * first_rows) for tag in range(4)]),
+    ]
+    total, _ = unpack(pos, total, both + [by_3, by_1, from_3, from_1], [from_2], slabs, span, "unpack_2")
+    slabs = [
+        (2, 0, early, [early_piece(tag // 2, tag % 2 * first_rows) for tag in range(4)]),
+        (2, early, 27 - early, [late_piece(2 + tag) for tag in range(4)]),
+    ]
+    total, _ = unpack(pos, total, [early_2a, early_2b, from_2] + across, [], slabs, span, "unpack_3")
     return (jnp.transpose(field, (3, 0, 1, 2)), jnp.transpose(total, (1, 0, 2)))
 
 

time: 164 us -> 158 us (0.963)
  local copies, waits for them, and re-layouts: 11 us -> 5.82 us
  Pallas kernels: 54.5 us -> 52.8 us
    unnamed x50, local copies, waits for them, and re-layouts: 11 us -> 5.82 us
    pallas_call x3, Pallas kernels: 24.6 us -> 22.9 us  [unpack(): pl.pallas_call(lambda *refs: unpack_kernel(*refs, slabs=slabs, count=len(...]
  transfers between devices with their start and end apart: 32 -> 32, of which waited for: 10 -> 10; matrix products, arithmetic and copies ran while one was open for 0% -> 0% of each run, Pallas kernels for 28% -> 27%
where the time goes in v8:
time: 158 us
  waiting for transfers between devices  55.7 us (35%)
  Pallas kernels  52.8 us (33%)
  starting transfers between devices  42.5 us (27%)
  local copies, waits for them, and re-layouts  5.82 us (4%)
    ppermute x32, waiting for transfers between devices, move(): return lax.ppermute(x, AXES, pairs)  55.7 us
    ppermute x32, starting transfers between devices, move(): return lax.ppermute(x, AXES, pairs)  42.5 us
    pallas_call x3, Pallas kernels, unpack(): pl.pallas_call(lambda *refs: unpack_kernel(*refs, slabs=slabs, count=len(...  22.9 us
    pallas_call x8, Pallas kernels, call(): pl.pallas_call(kernel, out_shape=outs, in_specs=[pl.BlockSpec(memory_spac...  13.7 us
    pallas_call x1, Pallas kernels, blocked_body(): pl.pallas_call(field_kernel, out_shape=jax.ShapeDtypeStruct((levels, heig...  11.4 us
    unnamed x50, local copies, waits for them, and re-layouts  5.82 us
    pallas_call x1, Pallas kernels, blocked_body(): pl.pallas_call(lines_kernel, out_shape=[jax.ShapeDtypeStruct((levels, row...  4.86 us
  transfers between devices with their start and end apart: 32, of which 10 were waited for; matrix products, arithmetic and copies ran while one was open for 0% of the time, Pallas kernels for 27%

profile of v8, /device:TPU:0, one launch (start us, length us, event | category | flops | bytes accessed | tf_op | source)
XLA Modules:
  0.0 157.8 jit_solution(16087177065511275465)
XLA Ops:
  0.7 1.0 copy-done.6
  1.7 1.0 copy-done.13
  2.7 0.8 pack.1
  3.6 0.7 collective-permute-start.3
  4.2 3.0 %collective-permute-start.4 = (bf16[768,128]{1,0:T(8,128)(2,1)S(1)}, bf16[768,128]{1,0:T(8,128)(2,1)S(1)}, u32[]{:S(2)}, u32[]{:S(2)}) collective-permute-start(bf16[768,128]{1,0:T(8,128)(2,1)S(1)} %get-tuple-element.36), channel_id=1, source_target_pairs={{0,4},{1,5},{2,6},{3,7},{4,0},{5,1},{6,2},{7,3},{8,20},{9,21},{10,... | collective-permute-start | bytes 589832 | tf_op jit(solution)/shard_map/ppermute | solution.py:98
  7.2 1.6 collective-permute-start
  8.8 2.6 %collective-permute-start.1 = (bf16[384,128]{1,0:T(8,128)(2,1)S(1)}, bf16[384,128]{1,0:T(8,128)(2,1)S(1)}, u32[]{:S(2)}, u32[]{:S(2)}) collective-permute-start(bf16[384,128]{1,0:T(8,128)(2,1)S(1)} %get-tuple-element.33), channel_id=1, source_target_pairs={{0,2},{1,3},{2,0},{3,1},{4,6},{5,7},{6,4},{7,5},{8,10},{9,11},{10,... | collective-permute-start | bytes 294920 | tf_op jit(solution)/shard_map/ppermute | solution.py:98
  11.4 1.3 collective-permute-start.2
  12.8 6.2 %collective-permute-done.1.x2 = bf16[384,128]{1,0:T(8,128)(2,1)S(1)} collective-permute-done((bf16[384,128]{1,0:T(8,128)(2,1)S(1)}, bf16[384,128]{1,0:T(8,128)(2,1)S(1)}, u32[]{:S(2)}, u32[]{:S(2)}) %collective-permute-start.1) | collective-permute-done | bytes 98336 | tf_op jit(solution)/shard_map/ppermute | solution.py:98
  18.9 3.0 %collective-permute-start.11 = (bf16[384,128]{1,0:T(8,128)(2,1)S(1)}, bf16[384,128]{1,0:T(8,128)(2,1)S(1)}, u32[]{:S(2)}, u32[]{:S(2)}) collective-permute-start(bf16[384,128]{1,0:T(8,128)(2,1)S(1)} %get-tuple-element.41), channel_id=1, source_target_pairs={{0,12},{1,13},{2,14},{3,15},{4,8},{5,9},{6,10},{7,11},{8,4},{9,5},... | collective-permute-start | bytes 294920 | tf_op jit(solution)/shard_map/ppermute | solution.py:98
  22.0 0.7 spread.1
  22.8 1.9 %collective-permute-start.5 = (bf16[1600,128]{1,0:T(8,128)(2,1)S(1)}, bf16[1600,128]{1,0:T(8,128)(2,1)S(1)}, u32[]{:S(2)}, u32[]{:S(2)}) collective-permute-start(bf16[1600,128]{1,0:T(8,128)(2,1)S(1)} %get-tuple-element.37.own.x_own), channel_id=1, source_target_pairs={{0,4},{1,5},{2,6},{3,7},{4,0},{5,1},{6,2},{7,3},{8,12},{9,13},{10,... | collective-permute-start | bytes 1228808 | tf_op jit(solution)/shard_map/ppermute | solution.py:98
  24.6 1.6 collective-permute-start.6
  26.2 2.8 %collective-permute-start.9 = (bf16[2,768,128]{2,1,0:T(8,128)(2,1)S(1)}, bf16[2,768,128]{2,1,0:T(8,128)(2,1)S(1)}, u32[]{:S(2)}, u32[]{:S(2)}) collective-permute-start(bf16[2,768,128]{2,1,0:T(8,128)(2,1)S(1)} %get-tuple-element.39.here), channel_id=1, source_target_pairs={{0,3},{1,0},{2,1},{3,2},{4,7},{5,4},{6,5},{7,6},{8,11},{9,8},{10,9... | collective-permute-start | bytes 1179656 | tf_op jit(solution)/shard_map/ppermute | solution.py:98
  29.0 14.5 %collective-permute-done.6.after.x_y = bf16[1536,128]{1,0:T(8,128)(2,1)S(1)} collective-permute-done((bf16[1536,128]{1,0:T(8,128)(2,1)S(1)}, bf16[1536,128]{1,0:T(8,128)(2,1)S(1)}, u32[]{:S(2)}, u32[]{:S(2)}) %collective-permute-start.6) | collective-permute-done | bytes 393248 | tf_op jit(solution)/shard_map/ppermute | solution.py:98
  43.5 1.8 %collective-permute-done.8.west = bf16[2,768,128]{2,1,0:T(8,128)(2,1)S(1)} collective-permute-done((bf16[2,768,128]{2,1,0:T(8,128)(2,1)S(1)}, bf16[2,768,128]{2,1,0:T(8,128)(2,1)S(1)}, u32[]{:S(2)}, u32[]{:S(2)}) %collective-permute-start.8) | collective-permute-done | bytes 393248 | tf_op jit(solution)/shard_map/ppermute | solution.py:98
  45.3 1.0 copy-done.7
  46.3 0.8 split.1
  47.2 3.0 %collective-permute-start.14 = (bf16[768,128]{1,0:T(8,128)(2,1)S(1)}, bf16[768,128]{1,0:T(8,128)(2,1)S(1)}, u32[]{:S(2)}, u32[]{:S(2)}) collective-permute-start(bf16[768,128]{1,0:T(8,128)(2,1)S(1)} %get-tuple-element.45), channel_id=1, source_target_pairs={{0,3},{1,0},{2,1},{3,2},{4,7},{5,4},{6,5},{7,6},{8,11},{9,8},{10,9... | collective-permute-start | bytes 589832 | tf_op jit(solution)/shard_map/ppermute | solution.py:98
  50.1 4.9 %lines.1 = (bf16[4,18,192,256]{3,2,1,0:T(8,128)(2,1)S(1)}, f32[27,256,512]{2,1,0:T(8,128)}) custom-call(s32[3]{0:T(128)S(1)} %pad_add_fusion.pos.refs_0_, bf16[1600,128]{1,0:T(8,128)(2,1)S(1)} %get-tuple-element.37.own.x_own, bf16[1600,128]{1,0:T(8,128)(2,1)S(1)} %collective-permute-done.5.x_x, bf16[1536,128]{1,0:T(8,128)(2,1)S(1)} %collective-permute-done.6.after.x_y, ...), custom_call_target="tpu_custom_call" | custom-call | bytes 1048576 | tf_op jit(solution)/shard_map/lines/pallas_call | solution.py:530
  55.4 4.5 %collective-permute-done.13.one = bf16[768,128]{1,0:T(8,128)(2,1)S(1)} collective-permute-done((bf16[768,128]{1,0:T(8,128)(2,1)S(1)}, bf16[768,128]{1,0:T(8,128)(2,1)S(1)}, u32[]{:S(2)}, u32[]{:S(2)}) %collective-permute-start.13) | collective-permute-done | bytes 196640 | tf_op jit(solution)/shard_map/ppermute | solution.py:98
  61.0 1.2 collective-permute-done.15.s2
  62.3 8.6 %taps.1.held = f32[27,64,128]{2,1,0:T(8,128)S(1)} custom-call(s32[3]{0:T(128)S(1)} %pad_add_fusion.pos.refs_0_, bf16[4,18,192,256]{3,2,1,0:T(8,128)(2,1)S(1)} %get-tuple-element.43.after.xs, bf16[6,768,128]{2,1,0:T(8,128)(2,1)S(1)} %get-tuple-element.44.g, bf16[6,768,128]{2,1,0:T(8,128)(2,1)S(1)} %collective-permute-done.12.s, ...), custom_call_target="tpu_custom_call" | custom-call | flops 5435817984 | bytes 11108352 | tf_op jit(solution)/shard_map/taps/pallas_call | solution.py:116
  70.8 1.0 code.1
  71.8 1.8 %collective-permute-start.18 = (bf16[1296,128]{1,0:T(8,128)(2,1)S(1)}, bf16[1296,128]{1,0:T(8,128)(2,1)S(1)}, u32[]{:S(2)}, u32[]{:S(2)}) collective-permute-start(bf16[1296,128]{1,0:T(8,128)(2,1)S(1)} %get-tuple-element.48), channel_id=1, source_target_pairs={{0,3},{1,0},{2,1},{3,2},{4,7},{5,4},{6,5},{7,6},{8,11},{9,8},{10,9... | collective-permute-start | bytes 995336 | tf_op jit(solution)/shard_map/ppermute | solution.py:98
  73.9 1.6 %collective-permute-start.21 = (bf16[1744,128]{1,0:T(8,128)(2,1)S(1)}, bf16[1744,128]{1,0:T(8,128)(2,1)S(1)}, u32[]{:S(2)}, u32[]{:S(2)}) collective-permute-start(bf16[1744,128]{1,0:T(8,128)(2,1)S(1)} %get-tuple-element.47.after.own.refs_1_), channel_id=1, source_target_pairs={{0,12},{1,13},{2,14},{3,15},{4,8},{5,9},{6,10},{7,11},{8,4},{9,5},... | collective-permute-start | bytes 1339400 | tf_op jit(solution)/shard_map/ppermute | solution.py:98
  75.5 1.2 collective-permute-start.20
  76.6 1.1 collective-permute-start.19
  77.7 11.4 %field.1.after = bf16[4,4,48,256]{3,2,1,0:T(8,128)(2,1)} custom-call(s32[3]{0:T(128)S(1)} %pad_add_fusion.pos.refs_0_, bf16[1744,128]{1,0:T(8,128)(2,1)S(1)} %get-tuple-element.47.after.own.refs_1_, bf16[4,6,64,256]{3,2,1,0:T(8,128)(2,1)S(1)} %get-tuple-element.46.mine, bf16[4,6,64,256]{3,2,1,0:T(8,128)(2,1)S(1)} %collective-permute-done.16.after.theirs, ...), custom_call_target="tpu_custom_call" | custom-call | flops 10871635968 | bytes 7077888 | tf_op jit(solution)/shard_map/field/pallas_call | solution.py:566
  89.1 0.9 collective-permute-done.17.west.refs_6_
  90.0 6.2 %collective-permute-done.20.y.refs_3_ = bf16[1744,128]{1,0:T(8,128)(2,1)S(1)} collective-permute-done((bf16[1744,128]{1,0:T(8,128)(2,1)S(1)}, bf16[1744,128]{1,0:T(8,128)(2,1)S(1)}, u32[]{:S(2)}, u32[]{:S(2)}) %collective-permute-start.20) | collective-permute-done | bytes 446496 | tf_op jit(solution)/shard_map/ppermute | solution.py:98
  96.2 1.0 collective-permute-done.19.x.refs_2_
  97.2 1.0 copy-done.12
  98.2 0.7 join.1
  99.0 0.7 collective-permute-start.31
  99.7 3.4 %collective-permute-start.23 = (bf16[2512,128]{1,0:T(8,128)(2,1)S(1)}, bf16[2512,128]{1,0:T(8,128)(2,1)S(1)}, u32[]{:S(2)}, u32[]{:S(2)}) collective-permute-start(bf16[2512,128]{1,0:T(8,128)(2,1)S(1)} %get-tuple-element.50), channel_id=1, source_target_pairs={{0,3},{1,0},{2,1},{3,2},{4,7},{5,4},{6,5},{7,6},{8,11},{9,8},{10,9... | collective-permute-start | bytes 1929224 | tf_op jit(solution)/shard_map/ppermute | solution.py:98
  103.1 1.3 collective-permute-start.30
  104.4 1.5 collective-permute-start.29
  106.0 6.2 %unpack_1.1 = (f32[27,256,512]{2,1,0:T(8,128)}, f32[8,128]{1,0:T(8,128)}) custom-call(s32[3]{0:T(128)} %copy-done.14, bf16[1744,128]{1,0:T(8,128)(2,1)} %copy-done.2, bf16[1744,128]{1,0:T(8,128)(2,1)} %copy-done.5, bf16[1744,128]{1,0:T(8,128)(2,1)} %copy-done.4, bf16[1744,128]{1,0:T(8,128)(2,1)} %copy-done.3, ...), custom_call_target="tpu_custom_call", output_to_operand_aliasing={{0}: (6, {})} | custom-call | bytes 4194304 | tf_op jit(solution)/shard_map/unpack_1/pallas_call | solution.py:398
  112.2 19.0 %collective-permute-done.22.by_3.refs_4_ = bf16[2496,128]{1,0:T(8,128)(2,1)S(1)} collective-permute-done((bf16[2496,128]{1,0:T(8,128)(2,1)S(1)}, bf16[2496,128]{1,0:T(8,128)(2,1)S(1)}, u32[]{:S(2)}, u32[]{:S(2)}) %collective-permute-start.22) | collective-permute-done | bytes 639008 | tf_op jit(solution)/shard_map/ppermute | solution.py:98
  131.2 0.7 copy-done.16
  132.5 1.5 collective-permute-start.28
  134.0 0.7 collective-permute-start.27
  134.7 1.3 collective-permute-start.26
  136.1 1.8 %collective-permute-start.24 = (bf16[928,128]{1,0:T(8,128)(2,1)S(1)}, bf16[928,128]{1,0:T(8,128)(2,1)S(1)}, u32[]{:S(2)}, u32[]{:S(2)}) collective-permute-start(bf16[928,128]{1,0:T(8,128)(2,1)S(1)} %get-tuple-element.54), channel_id=1, source_target_pairs={{0,1},{1,2},{2,3},{3,0},{4,5},{5,6},{6,7},{7,4},{8,9},{9,10},{10,1... | collective-permute-start | bytes 712712 | tf_op jit(solution)/shard_map/ppermute | solution.py:98
  137.9 2.0 %collective-permute-start.25 = (bf16[928,128]{1,0:T(8,128)(2,1)S(1)}, bf16[928,128]{1,0:T(8,128)(2,1)S(1)}, u32[]{:S(2)}, u32[]{:S(2)}) collective-permute-start(bf16[928,128]{1,0:T(8,128)(2,1)S(1)} %get-tuple-element.55), channel_id=1, source_target_pairs={{0,3},{1,0},{2,1},{3,2},{4,7},{5,4},{6,5},{7,6},{8,11},{9,8},{10,9... | collective-permute-start | bytes 712712 | tf_op jit(solution)/shard_map/ppermute | solution.py:98
  140.0 10.4 %unpack_2.1 = (f32[27,256,512]{2,1,0:T(8,128)}, f32[8,128]{1,0:T(8,128)}) custom-call(s32[3]{0:T(128)} %copy-done.14, bf16[2592,128]{1,0:T(8,128)(2,1)} %copy-done.19, bf16[2592,128]{1,0:T(8,128)(2,1)} %copy-done.18, bf16[2592,128]{1,0:T(8,128)(2,1)} %copy-done.17, bf16[2496,128]{1,0:T(8,128)(2,1)} %copy-done.1, ...), custom_call_target="tpu_custom_call", output_to_operand_aliasing={{0}: (9, {})} | custom-call | bytes 4194304 | tf_op jit(solution)/shard_map/unpack_2/pallas_call | solution.py:398
  151.6 6.2 %unpack_3.1 = (f32[27,256,512]{2,1,0:T(8,128)}, f32[8,128]{1,0:T(8,128)}) custom-call(s32[3]{0:T(128)} %copy-done.14, bf16[928,128]{1,0:T(8,128)(2,1)} %copy-done.23, bf16[928,128]{1,0:T(8,128)(2,1)} %copy-done.24, bf16[1296,128]{1,0:T(8,128)(2,1)} %copy-done.8, bf16[1296,128]{1,0:T(8,128)(2,1)} %copy-done.22, ...), custom_call_target="tpu_custom_call", output_to_operand_aliasing={{0}: (7, {})} | custom-call | bytes 4194304 | tf_op jit(solution)/shard_map/unpack_3/pallas_call | solution.py:398
  (80 shorter events, 3.9 us)
Async XLA Ops:
  0.7 96.5 %copy-start.14 = (s32[3]{0:T(128)}, s32[3]{0:T(128)S(1)}, u32[]{:S(2)}) copy-start(s32[3]{0:T(128)S(1)} %pad_add_fusion.pos.refs_0_) | copy-start | bytes 40
  3.6 18.4 %collective-permute-start.3 = (bf16[768,128]{1,0:T(8,128)(2,1)S(1)}, bf16[768,128]{1,0:T(8,128)(2,1)S(1)}, u32[]{:S(2)}, u32[]{:S(2)}) collective-permute-start(bf16[768,128]{1,0:T(8,128)(2,1)S(1)} %get-tuple-element.35), channel_id=1, source_target_pairs={{0,0},{1,1},{2,2},{3,3},{4,4},{5,5},{6,6},{7,7},{8,16},{9,17},{10,... | collective-permute-start | bytes 589832 | tf_op jit(solution)/shard_map/ppermute | solution.py:98
  4.2 17.7 %collective-permute-start.4 = (bf16[768,128]{1,0:T(8,128)(2,1)S(1)}, bf16[768,128]{1,0:T(8,128)(2,1)S(1)}, u32[]{:S(2)}, u32[]{:S(2)}) collective-permute-start(bf16[768,128]{1,0:T(8,128)(2,1)S(1)} %get-tuple-element.36), channel_id=1, source_target_pairs={{0,4},{1,5},{2,6},{3,7},{4,0},{5,1},{6,2},{7,3},{8,20},{9,21},{10,... | collective-permute-start | bytes 589832 | tf_op jit(solution)/shard_map/ppermute | solution.py:98
  7.2 11.7 %collective-permute-start = (bf16[416,128]{1,0:T(8,128)(2,1)S(1)}, bf16[416,128]{1,0:T(8,128)(2,1)S(1)}, u32[]{:S(2)}, u32[]{:S(2)}) collective-permute-start(bf16[416,128]{1,0:T(8,128)(2,1)S(1)} %get-tuple-element.32), channel_id=1, source_target_pairs={{0,1},{1,2},{2,3},{3,0},{4,5},{5,6},{6,7},{7,4},{8,9},{9,10},{10,1... | collective-permute-start | bytes 319496 | tf_op jit(solution)/shard_map/ppermute | solution.py:98
  8.8 10.1 %collective-permute-start.1 = (bf16[384,128]{1,0:T(8,128)(2,1)S(1)}, bf16[384,128]{1,0:T(8,128)(2,1)S(1)}, u32[]{:S(2)}, u32[]{:S(2)}) collective-permute-start(bf16[384,128]{1,0:T(8,128)(2,1)S(1)} %get-tuple-element.33), channel_id=1, source_target_pairs={{0,2},{1,3},{2,0},{3,1},{4,6},{5,7},{6,4},{7,5},{8,10},{9,11},{10,... | collective-permute-start | bytes 294920 | tf_op jit(solution)/shard_map/ppermute | solution.py:98
  11.4 10.6 %collective-permute-start.2 = (bf16[416,128]{1,0:T(8,128)(2,1)S(1)}, bf16[416,128]{1,0:T(8,128)(2,1)S(1)}, u32[]{:S(2)}, u32[]{:S(2)}) collective-permute-start(bf16[416,128]{1,0:T(8,128)(2,1)S(1)} %get-tuple-element.34), channel_id=1, source_target_pairs={{0,3},{1,0},{2,1},{3,2},{4,7},{5,4},{6,5},{7,6},{8,11},{9,8},{10,9... | collective-permute-start | bytes 319496 | tf_op jit(solution)/shard_map/ppermute | solution.py:98
  18.9 7.3 %collective-permute-start.10 = (bf16[384,128]{1,0:T(8,128)(2,1)S(1)}, bf16[384,128]{1,0:T(8,128)(2,1)S(1)}, u32[]{:S(2)}, u32[]{:S(2)}) collective-permute-start(bf16[384,128]{1,0:T(8,128)(2,1)S(1)} %get-tuple-element.40), channel_id=1, source_target_pairs={{0,4},{1,5},{2,6},{3,7},{4,0},{5,1},{6,2},{7,3},{8,12},{9,13},{10,... | collective-permute-start | bytes 294920 | tf_op jit(solution)/shard_map/ppermute | solution.py:98
  18.9 10.1 %collective-permute-start.11 = (bf16[384,128]{1,0:T(8,128)(2,1)S(1)}, bf16[384,128]{1,0:T(8,128)(2,1)S(1)}, u32[]{:S(2)}, u32[]{:S(2)}) collective-permute-start(bf16[384,128]{1,0:T(8,128)(2,1)S(1)} %get-tuple-element.41), channel_id=1, source_target_pairs={{0,12},{1,13},{2,14},{3,15},{4,8},{5,9},{6,10},{7,11},{8,4},{9,5},... | collective-permute-start | bytes 294920 | tf_op jit(solution)/shard_map/ppermute | solution.py:98
  22.7 22.6 %collective-permute-start.7 = (bf16[1600,128]{1,0:T(8,128)(2,1)S(1)}, bf16[1600,128]{1,0:T(8,128)(2,1)S(1)}, u32[]{:S(2)}, u32[]{:S(2)}) collective-permute-start(bf16[1600,128]{1,0:T(8,128)(2,1)S(1)} %get-tuple-element.37.own.x_own), channel_id=1, source_target_pairs={{0,12},{1,13},{2,14},{3,15},{4,8},{5,9},{6,10},{7,11},{8,4},{9,5},... | collective-permute-start | bytes 1228808 | tf_op jit(solution)/shard_map/ppermute | solution.py:98
  22.8 22.5 %collective-permute-start.5 = (bf16[1600,128]{1,0:T(8,128)(2,1)S(1)}, bf16[1600,128]{1,0:T(8,128)(2,1)S(1)}, u32[]{:S(2)}, u32[]{:S(2)}) collective-permute-start(bf16[1600,128]{1,0:T(8,128)(2,1)S(1)} %get-tuple-element.37.own.x_own), channel_id=1, source_target_pairs={{0,4},{1,5},{2,6},{3,7},{4,0},{5,1},{6,2},{7,3},{8,12},{9,13},{10,... | collective-permute-start | bytes 1228808 | tf_op jit(solution)/shard_map/ppermute | solution.py:98
  24.6 18.9 %collective-permute-start.6 = (bf16[1536,128]{1,0:T(8,128)(2,1)S(1)}, bf16[1536,128]{1,0:T(8,128)(2,1)S(1)}, u32[]{:S(2)}, u32[]{:S(2)}) collective-permute-start(bf16[1536,128]{1,0:T(8,128)(2,1)S(1)} %get-tuple-element.38), channel_id=1, source_target_pairs={{0,8},{1,9},{2,10},{3,11},{4,12},{5,13},{6,14},{7,15},{8,0},{9,1},... | collective-permute-start | bytes 1179656 | tf_op jit(solution)/shard_map/ppermute | solution.py:98
  26.2 17.3 %collective-permute-start.9 = (bf16[2,768,128]{2,1,0:T(8,128)(2,1)S(1)}, bf16[2,768,128]{2,1,0:T(8,128)(2,1)S(1)}, u32[]{:S(2)}, u32[]{:S(2)}) collective-permute-start(bf16[2,768,128]{2,1,0:T(8,128)(2,1)S(1)} %get-tuple-element.39.here), channel_id=1, source_target_pairs={{0,3},{1,0},{2,1},{3,2},{4,7},{5,4},{6,5},{7,6},{8,11},{9,8},{10,9... | collective-permute-start | bytes 1179656 | tf_op jit(solution)/shard_map/ppermute | solution.py:98
  29.0 16.3 %collective-permute-start.8 = (bf16[2,768,128]{2,1,0:T(8,128)(2,1)S(1)}, bf16[2,768,128]{2,1,0:T(8,128)(2,1)S(1)}, u32[]{:S(2)}, u32[]{:S(2)}) collective-permute-start(bf16[2,768,128]{2,1,0:T(8,128)(2,1)S(1)} %get-tuple-element.39.here), channel_id=1, source_target_pairs={{0,1},{1,2},{2,3},{3,0},{4,5},{5,6},{6,7},{7,4},{8,9},{9,10},{10,1... | collective-permute-start | bytes 1179656 | tf_op jit(solution)/shard_map/ppermute | solution.py:98
  47.1 15.2 %collective-permute-start.12 = (bf16[6,768,128]{2,1,0:T(8,128)(2,1)S(1)}, bf16[6,768,128]{2,1,0:T(8,128)(2,1)S(1)}, u32[]{:S(2)}, u32[]{:S(2)}) collective-permute-start(bf16[6,768,128]{2,1,0:T(8,128)(2,1)S(1)} %get-tuple-element.44.g), channel_id=1, source_target_pairs={{0,16},{1,17},{2,18},{3,19},{4,20},{5,21},{6,22},{7,23},{8,24},{9,... | collective-permute-start | bytes 3538952 | tf_op jit(solution)/shard_map/ppermute | solution.py:98
  47.2 8.2 %collective-permute-start.14 = (bf16[768,128]{1,0:T(8,128)(2,1)S(1)}, bf16[768,128]{1,0:T(8,128)(2,1)S(1)}, u32[]{:S(2)}, u32[]{:S(2)}) collective-permute-start(bf16[768,128]{1,0:T(8,128)(2,1)S(1)} %get-tuple-element.45), channel_id=1, source_target_pairs={{0,3},{1,0},{2,1},{3,2},{4,7},{5,4},{6,5},{7,6},{8,11},{9,8},{10,9... | collective-permute-start | bytes 589832 | tf_op jit(solution)/shard_map/ppermute | solution.py:98
  50.1 9.8 %collective-permute-start.13 = (bf16[768,128]{1,0:T(8,128)(2,1)S(1)}, bf16[768,128]{1,0:T(8,128)(2,1)S(1)}, u32[]{:S(2)}, u32[]{:S(2)}) collective-permute-start(bf16[768,128]{1,0:T(8,128)(2,1)S(1)} %get-tuple-element.42.after), channel_id=1, source_target_pairs={{0,1},{1,2},{2,3},{3,0},{4,5},{5,6},{6,7},{7,4},{8,9},{9,10},{10,1... | collective-permute-start | bytes 589832 | tf_op jit(solution)/shard_map/ppermute | solution.py:98
  60.5 1.8 %collective-permute-start.15 = (bf16[2,768,128]{2,1,0:T(8,128)(2,1)S(1)}, bf16[2,768,128]{2,1,0:T(8,128)(2,1)S(1)}, u32[]{:S(2)}, u32[]{:S(2)}) collective-permute-start(bf16[2,768,128]{2,1,0:T(8,128)(2,1)S(1)} %pair.1.g2), channel_id=1, source_target_pairs={{0,16},{1,17},{2,18},{3,19},{4,20},{5,21},{6,22},{7,23},{8,24},{9,... | collective-permute-start | bytes 1179656 | tf_op jit(solution)/shard_map/ppermute | solution.py:98
  60.6 10.3 %collective-permute-start.16 = (bf16[4,6,64,256]{3,2,1,0:T(8,128)(2,1)S(1)}, bf16[4,6,64,256]{3,2,1,0:T(8,128)(2,1)S(1)}, u32[]{:S(2)}, u32[]{:S(2)}) collective-permute-start(bf16[4,6,64,256]{3,2,1,0:T(8,128)(2,1)S(1)} %get-tuple-element.46.mine), channel_id=1, source_target_pairs={{0,16},{1,17},{2,18},{3,19},{4,20},{5,21},{6,22},{7,23},{8,24},{9,... | collective-permute-start | bytes 2359304 | tf_op jit(solution)/shard_map/ppermute | solution.py:98
  71.8 25.4 %copy-start.2 = (bf16[1744,128]{1,0:T(8,128)(2,1)}, bf16[1744,128]{1,0:T(8,128)(2,1)S(1)}, u32[]{:S(2)}) copy-start(bf16[1744,128]{1,0:T(8,128)(2,1)S(1)} %get-tuple-element.47.after.own.refs_1_) | copy-start | bytes 1339396
  71.8 17.3 %collective-permute-start.18 = (bf16[1296,128]{1,0:T(8,128)(2,1)S(1)}, bf16[1296,128]{1,0:T(8,128)(2,1)S(1)}, u32[]{:S(2)}, u32[]{:S(2)}) collective-permute-start(bf16[1296,128]{1,0:T(8,128)(2,1)S(1)} %get-tuple-element.48), channel_id=1, source_target_pairs={{0,3},{1,0},{2,1},{3,2},{4,7},{5,4},{6,5},{7,6},{8,11},{9,8},{10,9... | collective-permute-start | bytes 995336 | tf_op jit(solution)/shard_map/ppermute | solution.py:98
  73.6 16.4 %collective-permute-start.17 = (bf16[1296,128]{1,0:T(8,128)(2,1)S(1)}, bf16[1296,128]{1,0:T(8,128)(2,1)S(1)}, u32[]{:S(2)}, u32[]{:S(2)}) collective-permute-start(bf16[1296,128]{1,0:T(8,128)(2,1)S(1)} %get-tuple-element.48), channel_id=1, source_target_pairs={{0,1},{1,2},{2,3},{3,0},{4,5},{5,6},{6,7},{7,4},{8,9},{9,10},{10,1... | collective-permute-start | bytes 995336 | tf_op jit(solution)/shard_map/ppermute | solution.py:98
  73.9 16.1 %collective-permute-start.21 = (bf16[1744,128]{1,0:T(8,128)(2,1)S(1)}, bf16[1744,128]{1,0:T(8,128)(2,1)S(1)}, u32[]{:S(2)}, u32[]{:S(2)}) collective-permute-start(bf16[1744,128]{1,0:T(8,128)(2,1)S(1)} %get-tuple-element.47.after.own.refs_1_), channel_id=1, source_target_pairs={{0,12},{1,13},{2,14},{3,15},{4,8},{5,9},{6,10},{7,11},{8,4},{9,5},... | collective-permute-start | bytes 1339400 | tf_op jit(solution)/shard_map/ppermute | solution.py:98
  75.5 20.7 %collective-permute-start.20 = (bf16[1744,128]{1,0:T(8,128)(2,1)S(1)}, bf16[1744,128]{1,0:T(8,128)(2,1)S(1)}, u32[]{:S(2)}, u32[]{:S(2)}) collective-permute-start(bf16[1744,128]{1,0:T(8,128)(2,1)S(1)} %get-tuple-element.47.after.own.refs_1_), channel_id=1, source_target_pairs={{0,8},{1,9},{2,10},{3,11},{4,12},{5,13},{6,14},{7,15},{8,0},{9,1},... | collective-permute-start | bytes 1339400 | tf_op jit(solution)/shard_map/ppermute | solution.py:98
  76.6 20.5 %collective-permute-start.19 = (bf16[1744,128]{1,0:T(8,128)(2,1)S(1)}, bf16[1744,128]{1,0:T(8,128)(2,1)S(1)}, u32[]{:S(2)}, u32[]{:S(2)}) collective-permute-start(bf16[1744,128]{1,0:T(8,128)(2,1)S(1)} %get-tuple-element.47.after.own.refs_1_), channel_id=1, source_target_pairs={{0,4},{1,5},{2,6},{3,7},{4,0},{5,1},{6,2},{7,3},{8,12},{9,13},{10,... | collective-permute-start | bytes 1339400 | tf_op jit(solution)/shard_map/ppermute | solution.py:98
  89.1 50.8 %copy-start.9 = (bf16[1296,128]{1,0:T(8,128)(2,1)}, bf16[1296,128]{1,0:T(8,128)(2,1)S(1)}, u32[]{:S(2)}) copy-start(bf16[1296,128]{1,0:T(8,128)(2,1)S(1)} %collective-permute-done.18.east.refs_7_) | copy-start | bytes 995332
  90.0 49.9 %copy-start.10 = (bf16[1296,128]{1,0:T(8,128)(2,1)}, bf16[1296,128]{1,0:T(8,128)(2,1)S(1)}, u32[]{:S(2)}) copy-start(bf16[1296,128]{1,0:T(8,128)(2,1)S(1)} %collective-permute-done.17.west.refs_6_) | copy-start | bytes 995332
  90.0 16.0 %copy-start.3 = (bf16[1744,128]{1,0:T(8,128)(2,1)}, bf16[1744,128]{1,0:T(8,128)(2,1)S(1)}, u32[]{:S(2)}) copy-start(bf16[1744,128]{1,0:T(8,128)(2,1)S(1)} %collective-permute-done.21.d.refs_4_) | copy-start | bytes 1339396
  96.2 9.8 %copy-start.4 = (bf16[1744,128]{1,0:T(8,128)(2,1)}, bf16[1744,128]{1,0:T(8,128)(2,1)S(1)}, u32[]{:S(2)}) copy-start(bf16[1744,128]{1,0:T(8,128)(2,1)S(1)} %collective-permute-done.20.y.refs_3_) | copy-start | bytes 1339396
  98.2 7.8 %copy-start.5 = (bf16[1744,128]{1,0:T(8,128)(2,1)}, bf16[1744,128]{1,0:T(8,128)(2,1)S(1)}, u32[]{:S(2)}) copy-start(bf16[1744,128]{1,0:T(8,128)(2,1)S(1)} %collective-permute-done.19.x.refs_2_) | copy-start | bytes 1339396
  99.0 7.0 %copy-start.11 = (bf16[2592,128]{1,0:T(8,128)(2,1)}, bf16[2592,128]{1,0:T(8,128)(2,1)S(1)}, u32[]{:S(2)}) copy-start(bf16[2592,128]{1,0:T(8,128)(2,1)S(1)} %get-tuple-element.51.refs_5_) | copy-start | bytes 1990660
  99.0 32.2 %copy-start.15 = (s32[3]{0:T(128)S(1)}, s32[3]{0:T(128)}, u32[]{:S(2)}) copy-start(s32[3]{0:T(128)} %copy-done.14) | copy-start | bytes 40
  99.0 35.7 %collective-permute-start.31 = (bf16[2592,128]{1,0:T(8,128)(2,1)S(1)}, bf16[2592,128]{1,0:T(8,128)(2,1)S(1)}, u32[]{:S(2)}, u32[]{:S(2)}) collective-permute-start(bf16[2592,128]{1,0:T(8,128)(2,1)S(1)} %get-tuple-element.51.refs_5_), channel_id=1, source_target_pairs={{0,12},{1,13},{2,14},{3,15},{4,8},{5,9},{6,10},{7,11},{8,4},{9,5},... | collective-permute-start | bytes 1990664 | tf_op jit(solution)/shard_map/ppermute | solution.py:98
  99.7 31.5 %collective-permute-start.23 = (bf16[2512,128]{1,0:T(8,128)(2,1)S(1)}, bf16[2512,128]{1,0:T(8,128)(2,1)S(1)}, u32[]{:S(2)}, u32[]{:S(2)}) collective-permute-start(bf16[2512,128]{1,0:T(8,128)(2,1)S(1)} %get-tuple-element.50), channel_id=1, source_target_pairs={{0,3},{1,0},{2,1},{3,2},{4,7},{5,4},{6,5},{7,6},{8,11},{9,8},{10,9... | collective-permute-start | bytes 1929224 | tf_op jit(solution)/shard_map/ppermute | solution.py:98
  103.1 28.1 %collective-permute-start.22 = (bf16[2496,128]{1,0:T(8,128)(2,1)S(1)}, bf16[2496,128]{1,0:T(8,128)(2,1)S(1)}, u32[]{:S(2)}, u32[]{:S(2)}) collective-permute-start(bf16[2496,128]{1,0:T(8,128)(2,1)S(1)} %get-tuple-element.49), channel_id=1, source_target_pairs={{0,1},{1,2},{2,3},{3,0},{4,5},{5,6},{6,7},{7,4},{8,9},{9,10},{10,1... | collective-permute-start | bytes 1916936 | tf_op jit(solution)/shard_map/ppermute | solution.py:98
  103.1 32.9 %collective-permute-start.30 = (bf16[2592,128]{1,0:T(8,128)(2,1)S(1)}, bf16[2592,128]{1,0:T(8,128)(2,1)S(1)}, u32[]{:S(2)}, u32[]{:S(2)}) collective-permute-start(bf16[2592,128]{1,0:T(8,128)(2,1)S(1)} %get-tuple-element.51.refs_5_), channel_id=1, source_target_pairs={{0,8},{1,9},{2,10},{3,11},{4,12},{5,13},{6,14},{7,15},{8,0},{9,1},... | collective-permute-start | bytes 1990664 | tf_op jit(solution)/shard_map/ppermute | solution.py:98
  104.4 33.4 %collective-permute-start.29 = (bf16[2592,128]{1,0:T(8,128)(2,1)S(1)}, bf16[2592,128]{1,0:T(8,128)(2,1)S(1)}, u32[]{:S(2)}, u32[]{:S(2)}) collective-permute-start(bf16[2592,128]{1,0:T(8,128)(2,1)S(1)} %get-tuple-element.51.refs_5_), channel_id=1, source_target_pairs={{0,4},{1,5},{2,6},{3,7},{4,0},{5,1},{6,2},{7,3},{8,12},{9,13},{10,... | collective-permute-start | bytes 1990664 | tf_op jit(solution)/shard_map/ppermute | solution.py:98
  131.2 8.7 %copy-start.1 = (bf16[2496,128]{1,0:T(8,128)(2,1)}, bf16[2496,128]{1,0:T(8,128)(2,1)S(1)}, u32[]{:S(2)}) copy-start(bf16[2496,128]{1,0:T(8,128)(2,1)S(1)} %collective-permute-done.22.by_3.refs_4_) | copy-start | bytes 1916932
  131.2 8.7 %copy-start = (bf16[2512,128]{1,0:T(8,128)(2,1)}, bf16[2512,128]{1,0:T(8,128)(2,1)S(1)}, u32[]{:S(2)}) copy-start(bf16[2512,128]{1,0:T(8,128)(2,1)S(1)} %collective-permute-done.23.by_1.refs_5_) | copy-start | bytes 1929220
  132.5 7.4 %copy-start.8 = (bf16[1296,128]{1,0:T(8,128)(2,1)}, bf16[1296,128]{1,0:T(8,128)(2,1)S(1)}, u32[]{:S(2)}) copy-start(bf16[1296,128]{1,0:T(8,128)(2,1)S(1)} %get-tuple-element.56.refs_8_.refs_3_) | copy-start | bytes 995332
  132.5 17.9 %collective-permute-start.28 = (bf16[1296,128]{1,0:T(8,128)(2,1)S(1)}, bf16[1296,128]{1,0:T(8,128)(2,1)S(1)}, u32[]{:S(2)}, u32[]{:S(2)}) collective-permute-start(bf16[1296,128]{1,0:T(8,128)(2,1)S(1)} %get-tuple-element.56.refs_8_.refs_3_), channel_id=1, source_target_pairs={{0,12},{1,13},{2,14},{3,15},{4,8},{5,9},{6,10},{7,11},{8,4},{9,5},... | collective-permute-start | bytes 995336 | tf_op jit(solution)/shard_map/ppermute | solution.py:98
  134.0 16.5 %collective-permute-start.27 = (bf16[1296,128]{1,0:T(8,128)(2,1)S(1)}, bf16[1296,128]{1,0:T(8,128)(2,1)S(1)}, u32[]{:S(2)}, u32[]{:S(2)}) collective-permute-start(bf16[1296,128]{1,0:T(8,128)(2,1)S(1)} %get-tuple-element.56.refs_8_.refs_3_), channel_id=1, source_target_pairs={{0,8},{1,9},{2,10},{3,11},{4,12},{5,13},{6,14},{7,15},{8,0},{9,1},... | collective-permute-start | bytes 995336 | tf_op jit(solution)/shard_map/ppermute | solution.py:98
  134.7 5.2 %copy-start.17 = (bf16[2592,128]{1,0:T(8,128)(2,1)}, bf16[2592,128]{1,0:T(8,128)(2,1)S(1)}, u32[]{:S(2)}) copy-start(bf16[2592,128]{1,0:T(8,128)(2,1)S(1)} %collective-permute-done.31.refs_3_) | copy-start | bytes 1990660
  134.7 15.7 %collective-permute-start.26 = (bf16[1296,128]{1,0:T(8,128)(2,1)S(1)}, bf16[1296,128]{1,0:T(8,128)(2,1)S(1)}, u32[]{:S(2)}, u32[]{:S(2)}) collective-permute-start(bf16[1296,128]{1,0:T(8,128)(2,1)S(1)} %get-tuple-element.56.refs_8_.refs_3_), channel_id=1, source_target_pairs={{0,4},{1,5},{2,6},{3,7},{4,0},{5,1},{6,2},{7,3},{8,12},{9,13},{10,... | collective-permute-start | bytes 995336 | tf_op jit(solution)/shard_map/ppermute | solution.py:98
  136.1 3.9 %copy-start.18 = (bf16[2592,128]{1,0:T(8,128)(2,1)}, bf16[2592,128]{1,0:T(8,128)(2,1)S(1)}, u32[]{:S(2)}) copy-start(bf16[2592,128]{1,0:T(8,128)(2,1)S(1)} %collective-permute-done.30.refs_2_) | copy-start | bytes 1990660
  136.1 14.3 %collective-permute-start.24 = (bf16[928,128]{1,0:T(8,128)(2,1)S(1)}, bf16[928,128]{1,0:T(8,128)(2,1)S(1)}, u32[]{:S(2)}, u32[]{:S(2)}) collective-permute-start(bf16[928,128]{1,0:T(8,128)(2,1)S(1)} %get-tuple-element.54), channel_id=1, source_target_pairs={{0,1},{1,2},{2,3},{3,0},{4,5},{5,6},{6,7},{7,4},{8,9},{9,10},{10,1... | collective-permute-start | bytes 712712 | tf_op jit(solution)/shard_map/ppermute | solution.py:98
  137.9 2.1 %copy-start.19 = (bf16[2592,128]{1,0:T(8,128)(2,1)}, bf16[2592,128]{1,0:T(8,128)(2,1)S(1)}, u32[]{:S(2)}) copy-start(bf16[2592,128]{1,0:T(8,128)(2,1)S(1)} %collective-permute-done.29.refs_1_) | copy-start | bytes 1990660
  137.9 12.5 %collective-permute-start.25 = (bf16[928,128]{1,0:T(8,128)(2,1)S(1)}, bf16[928,128]{1,0:T(8,128)(2,1)S(1)}, u32[]{:S(2)}, u32[]{:S(2)}) collective-permute-start(bf16[928,128]{1,0:T(8,128)(2,1)S(1)} %get-tuple-element.55), channel_id=1, source_target_pairs={{0,3},{1,0},{2,1},{3,2},{4,7},{5,4},{6,5},{7,6},{8,11},{9,8},{10,9... | collective-permute-start | bytes 712712 | tf_op jit(solution)/shard_map/ppermute | solution.py:98
  150.5 1.1 copy-start.22
  (9 other events, 8.0 us)

commit v9 on v8

--- a/solution.py
+++ b/solution.py
@@ -326,20 +326,20 @@
     late[27 * span - skip :, :] = unit.astype(out.dtype)
 
 
-def join_kernel(pos, west, east, own, x, y, d, after, both, by_3, by_1):
+def join_kernel(pos, west, east, plane, after, both, by_3, by_1):
     del pos, after
     size = west.shape[0]
-    cut = own.shape[0] - size
-    end = own.shape[0] - 16
+    rows = plane.shape[0] // 4
+    cut, end = rows - size, rows - 16
     half = by_3.shape[0] - 4 * (cut + 16)
     both[0:size, :] = west[...]
     both[size:, :] = east[...]
     by_3[0:half, :] = west[0:half, :]
     by_1[0 : size - half, :] = east[half:, :]
     for out, at in ((by_3, half), (by_1, size - half)):
-        for piece in (own, x, y, d):
-            out[at : at + cut, :] = piece[0:cut, :]
-            out[at + cut : at + cut + 16, :] = piece[end:, :]
+        for lat in range(4):
+            out[at : at + cut, :] = plane[lat * rows : lat * rows + cut, :]
+            out[at + cut : at + cut + 16, :] = plane[lat * rows + end : (lat + 1) * rows, :]
             at += cut + 16
 
 
@@ -373,17 +373,16 @@
     for at, (_, _, many, skip, pieces) in enumerate(parts):
         if at >= 2:
             copy(at - 2).wait()
-        for tag, (which, row, power_row) in enumerate(pieces):
-            source = sources[which]
-            unit = source[power_row : power_row + 16, :].astype(jnp.float32)[0:1]
-            lanes = pl.ds(pl.multiple_of((pos[1] ^ tag) * wide, wide), wide)
-
-            @pl.loop(0, many)
-            def _(tap, source=source, start=row + skip * span, unit=unit, lanes=lanes, at=at):
-                code = source[pl.ds(pl.multiple_of(start + tap * span, 16), span), :].astype(jnp.float32)
+        units = [sources[i][j : j + 16, :].astype(jnp.float32)[0:1] for i, _, j in pieces]
+
+        @pl.loop(0, many)
+        def _(tap, pieces=pieces, skip=skip, units=units, at=at):
+            for lat, (which, row, _) in enumerate(pieces):
+                start = pl.multiple_of(row + (skip + tap) * span, 16)
+                code = sources[which][pl.ds(start, span), :].astype(jnp.float32)
                 root = lax.rsqrt(lax.rsqrt(jnp.abs(code)))
-                root = root * lax.rsqrt(jnp.maximum(root, 1e-30)) * unit
-                buffers[at % 2, tap, :, lanes] = jnp.where(code < 0, -root, root)
+                root = root * lax.rsqrt(jnp.maximum(root, 1e-30)) * units[lat]
+                buffers[at % 2, tap, :, lat * wide : (lat + 1) * wide] = jnp.where(code < 0, -root, root)
 
         copy(at).start()
     for at in range(max(len(parts) - 2, 0), len(parts)):
@@ -587,15 +586,15 @@
     )(pos, own, mine, theirs, taps)
 
     def to_plane(share):
-        return [move(share, lat_xor(tag)) for tag in (1, 2, 3)]
+        return lax.all_gather(share, "lat", axis=0, tiled=True)
 
     from_3 = move(late, lon_by(1))
     from_1 = move(late, lon_by(-1))
-    plane = [own] + to_plane(own)
+    plane = to_plane(own)
     pair, z_3, z_1 = call(
         join_kernel,
         [slab(2 * size), slab(half + 4 * first_rows), slab(size - half + 4 * first_rows)],
-        (pos, from_3, from_1, *plane, field),
+        (pos, from_3, from_1, plane, field),
         [],
         0,
         "join",
@@ -611,8 +610,8 @@
     def early_piece(which, row):
         return (which, row, row + cut)
 
-    slabs = [(0, 0, 27, [(tag, 0, end) for tag in range(4)])]
-    total, token = unpack(pos, total, plane, [pair], slabs, span, "unpack_1")
+    slabs = [(0, 0, 27, [(0, at * (end + 16), at * (end + 16) + end) for at in range(4)])]
+    total, token = unpack(pos, total, [plane], [pair], slabs, span, "unpack_1")
     from_2, early_3, early_1 = call(
         across_kernel,
         [slab(size), slab(2 * first_rows), slab(2 * first_rows)],
@@ -628,17 +627,17 @@
     early_2b = move(early_1, lon_by(-1))
 
     slabs = [
-        (3, early, 27 - early, [late_piece(5)] + [late_piece(at) for at in range(3)]),
-        (1, early, 27 - early, [late_piece(6)] + [late_piece(at, size) for at in range(3)]),
-        (3, 0, early, [early_piece(3, half + tag * first_rows) for tag in range(4)]),
-        (1, 0, early, [early_piece(4, size - half + tag * first_rows) for tag in range(4)]),
+        (3, early, 27 - early, [late_piece(0, 2 * size * at) for at in range(4)]),
+        (1, early, 27 - early, [late_piece(0, 2 * size * at + size) for at in range(4)]),
+        (3, 0, early, [early_piece(1, half + at * first_rows) for at in range(4)]),
+        (1, 0, early, [early_piece(2, size - half + at * first_rows) for at in range(4)]),
     ]
-    total, _ = unpack(pos, total, both + [by_3, by_1, from_3, from_1], [from_2], slabs, span, "unpack_2")
+    total, _ = unpack(pos, total, [both, by_3, by_1], [from_2], slabs, span, "unpack_2")
     slabs = [
-        (2, 0, early, [early_piece(tag // 2, tag % 2 * first_rows) for tag in range(4)]),
-        (2, early, 27 - early, [late_piece(2 + tag) for tag in range(4)]),
+        (2, 0, early, [early_piece(at // 2, at % 2 * first_rows) for at in range(4)]),
+        (2, early, 27 - early, [late_piece(2, size * at) for at in range(4)]),
     ]
-    total, _ = unpack(pos, total, [early_2a, early_2b, from_2] + across, [], slabs, span, "unpack_3")
+    total, _ = unpack(pos, total, [early_2a, early_2b, across], [], slabs, span, "unpack_3")
     return (jnp.transpose(field, (3, 0, 1, 2)), jnp.transpose(total, (1, 0, 2)))
 
 

time: 158 us -> 199 us (1.26)
  waiting for transfers between devices: 55.7 us -> 94.5 us
  between operations: 0.96 us -> 13.9 us
  starting transfers between devices: 42.5 us -> 31.6 us
    all_gather x0 -> x3, waiting for transfers between devices: none -> 38.2 us  [to_plane(): return lax.all_gather(share, 'lat', axis=0, tiled=True)]
    ppermute x32 -> x23, starting transfers between devices: 42.5 us -> 31.5 us  [move(): return lax.ppermute(x, AXES, pairs)]
    pallas_call x3, Pallas kernels: 22.9 us -> 19.8 us  [unpack(): pl.pallas_call(lambda *refs: unpack_kernel(*refs, slabs=slabs, count=len(...]
    pallas_call x8, Pallas kernels: 13.7 us -> 16.1 us  [call(): pl.pallas_call(kernel, out_shape=outs, in_specs=[pl.BlockSpec(memory_spac...]
    ppermute x32 -> x23, waiting for transfers between devices: 55.7 us -> 56.3 us  [move(): return lax.ppermute(x, AXES, pairs)]
    unnamed x50 -> x24, local copies, waits for them, and re-layouts: 5.82 us -> 6.16 us
  transfers between devices with their start and end apart: 32 -> 26, of which waited for: 10 -> 11; matrix products, arithmetic and copies ran while one was open for 0% -> 0% of each run, Pallas kernels for 27% -> 21%
where the time goes in v9:
time: 199 us
  waiting for transfers between devices  94.5 us (47%)
  Pallas kernels  52.2 us (26%)
  starting transfers between devices  31.6 us (16%)
  between operations  13.9 us (7%)
  local copies, waits for them, and re-layouts  6.16 us (3%)
    ppermute x23, waiting for transfers between devices, move(): return lax.ppermute(x, AXES, pairs)  56.3 us
    all_gather x3, waiting for transfers between devices, to_plane(): return lax.all_gather(share, 'lat', axis=0, tiled=True)  38.2 us
    ppermute x23, starting transfers between devices, move(): return lax.ppermute(x, AXES, pairs)  31.5 us
    pallas_call x3, Pallas kernels, unpack(): pl.pallas_call(lambda *refs: unpack_kernel(*refs, slabs=slabs, count=len(...  19.8 us
    pallas_call x8, Pallas kernels, call(): pl.pallas_call(kernel, out_shape=outs, in_specs=[pl.BlockSpec(memory_spac...  16.1 us
    pallas_call x1, Pallas kernels, blocked_body(): pl.pallas_call(field_kernel, out_shape=jax.ShapeDtypeStruct((levels, heig...  11.4 us
    unnamed x24, local copies, waits for them, and re-layouts  6.16 us
    pallas_call x1, Pallas kernels, blocked_body(): pl.pallas_call(lines_kernel, out_shape=[jax.ShapeDtypeStruct((levels, row...  4.86 us
  transfers between devices with their start and end apart: 26, of which 11 were waited for; matrix products, arithmetic and copies ran while one was open for 0% of the time, Pallas kernels for 21%

profile of v9, /device:TPU:0, one launch (start us, length us, event | category | flops | bytes accessed | tf_op | source)
XLA Modules:
  0.0 198.6 jit_solution(12977662671334176310)
XLA Ops:
  7.2 0.1 pad_add_fusion.pos.refs_0_
  7.3 1.0 copy-done.3
  8.3 1.0 copy-done.6
  9.3 0.8 pack.1
  10.1 0.7 collective-permute-start.3
  10.8 3.0 %collective-permute-start.4 = (bf16[768,128]{1,0:T(8,128)(2,1)S(1)}, bf16[768,128]{1,0:T(8,128)(2,1)S(1)}, u32[]{:S(2)}, u32[]{:S(2)}) collective-permute-start(bf16[768,128]{1,0:T(8,128)(2,1)S(1)} %get-tuple-element.36), channel_id=1, source_target_pairs={{0,4},{1,5},{2,6},{3,7},{4,0},{5,1},{6,2},{7,3},{8,20},{9,21},{10,... | collective-permute-start | bytes 589832 | tf_op jit(solution)/shard_map/ppermute | solution.py:98
  13.8 1.6 collective-permute-start
  15.4 2.6 %collective-permute-start.1 = (bf16[384,128]{1,0:T(8,128)(2,1)S(1)}, bf16[384,128]{1,0:T(8,128)(2,1)S(1)}, u32[]{:S(2)}, u32[]{:S(2)}) collective-permute-start(bf16[384,128]{1,0:T(8,128)(2,1)S(1)} %get-tuple-element.33), channel_id=1, source_target_pairs={{0,2},{1,3},{2,0},{3,1},{4,6},{5,7},{6,4},{7,5},{8,10},{9,11},{10,... | collective-permute-start | bytes 294920 | tf_op jit(solution)/shard_map/ppermute | solution.py:98
  18.0 1.3 collective-permute-start.2
  19.3 6.2 %collective-permute-done.1.x2 = bf16[384,128]{1,0:T(8,128)(2,1)S(1)} collective-permute-done((bf16[384,128]{1,0:T(8,128)(2,1)S(1)}, bf16[384,128]{1,0:T(8,128)(2,1)S(1)}, u32[]{:S(2)}, u32[]{:S(2)}) %collective-permute-start.1) | collective-permute-done | bytes 98336 | tf_op jit(solution)/shard_map/ppermute | solution.py:98
  25.5 3.0 %collective-permute-start.11 = (bf16[384,128]{1,0:T(8,128)(2,1)S(1)}, bf16[384,128]{1,0:T(8,128)(2,1)S(1)}, u32[]{:S(2)}, u32[]{:S(2)}) collective-permute-start(bf16[384,128]{1,0:T(8,128)(2,1)S(1)} %get-tuple-element.41), channel_id=1, source_target_pairs={{0,12},{1,13},{2,14},{3,15},{4,8},{5,9},{6,10},{7,11},{8,4},{9,5},... | collective-permute-start | bytes 294920 | tf_op jit(solution)/shard_map/ppermute | solution.py:98
  28.6 0.7 spread.1
  29.3 0.1 collective-permute-start.7
  29.3 1.9 collective-permute-start.5
  31.2 1.6 collective-permute-start.6
  32.8 2.8 %collective-permute-start.9 = (bf16[2,768,128]{2,1,0:T(8,128)(2,1)S(1)}, bf16[2,768,128]{2,1,0:T(8,128)(2,1)S(1)}, u32[]{:S(2)}, u32[]{:S(2)}) collective-permute-start(bf16[2,768,128]{2,1,0:T(8,128)(2,1)S(1)} %get-tuple-element.39.here), channel_id=1, source_target_pairs={{0,3},{1,0},{2,1},{3,2},{4,7},{5,4},{6,5},{7,6},{8,11},{9,8},{10,9... | collective-permute-start | bytes 1179656 | tf_op jit(solution)/shard_map/ppermute | solution.py:98
  35.6 14.5 %collective-permute-done.6.after.x_y = bf16[1536,128]{1,0:T(8,128)(2,1)S(1)} collective-permute-done((bf16[1536,128]{1,0:T(8,128)(2,1)S(1)}, bf16[1536,128]{1,0:T(8,128)(2,1)S(1)}, u32[]{:S(2)}, u32[]{:S(2)}) %collective-permute-start.6) | collective-permute-done | bytes 393248 | tf_op jit(solution)/shard_map/ppermute | solution.py:98
  50.1 1.8 collective-permute-done.8.west
  51.9 1.0 copy-done.4
  52.9 0.8 split.1
  53.7 3.0 %collective-permute-start.14 = (bf16[768,128]{1,0:T(8,128)(2,1)S(1)}, bf16[768,128]{1,0:T(8,128)(2,1)S(1)}, u32[]{:S(2)}, u32[]{:S(2)}) collective-permute-start(bf16[768,128]{1,0:T(8,128)(2,1)S(1)} %get-tuple-element.45), channel_id=1, source_target_pairs={{0,3},{1,0},{2,1},{3,2},{4,7},{5,4},{6,5},{7,6},{8,11},{9,8},{10,9... | collective-permute-start | bytes 589832 | tf_op jit(solution)/shard_map/ppermute | solution.py:98
  56.7 4.9 %lines.1 = (bf16[4,18,192,256]{3,2,1,0:T(8,128)(2,1)S(1)}, f32[27,256,512]{2,1,0:T(8,128)}) custom-call(s32[3]{0:T(128)S(1)} %pad_add_fusion.pos.refs_0_, bf16[1600,128]{1,0:T(8,128)(2,1)S(1)} %get-tuple-element.37.own.x_own, bf16[1600,128]{1,0:T(8,128)(2,1)S(1)} %collective-permute-done.5.x_x, bf16[1536,128]{1,0:T(8,128)(2,1)S(1)} %collective-permute-done.6.after.x_y, ...), custom_call_target="tpu_custom_call" | custom-call | bytes 1048576 | tf_op jit(solution)/shard_map/lines/pallas_call | solution.py:529
  61.6 0.4 collective-permute-done.14.two
  62.0 4.5 %collective-permute-done.13.one = bf16[768,128]{1,0:T(8,128)(2,1)S(1)} collective-permute-done((bf16[768,128]{1,0:T(8,128)(2,1)S(1)}, bf16[768,128]{1,0:T(8,128)(2,1)S(1)}, u32[]{:S(2)}, u32[]{:S(2)}) %collective-permute-start.13) | collective-permute-done | bytes 196640 | tf_op jit(solution)/shard_map/ppermute | solution.py:98
  66.5 0.6 pair.1.g2
  67.1 0.5 collective-permute-start.16
  67.6 1.2 collective-permute-done.15.s2
  68.8 8.5 %taps.1.held = f32[27,64,128]{2,1,0:T(8,128)S(1)} custom-call(s32[3]{0:T(128)S(1)} %pad_add_fusion.pos.refs_0_, bf16[4,18,192,256]{3,2,1,0:T(8,128)(2,1)S(1)} %get-tuple-element.43.after.xs, bf16[6,768,128]{2,1,0:T(8,128)(2,1)S(1)} %get-tuple-element.44.g, bf16[6,768,128]{2,1,0:T(8,128)(2,1)S(1)} %collective-permute-done.12.s, ...), custom_call_target="tpu_custom_call" | custom-call | flops 5435817984 | bytes 11108352 | tf_op jit(solution)/shard_map/taps/pallas_call | solution.py:116
  77.4 1.7 code.1
  79.2 1.8 collective-permute-start.18
  81.0 0.3 collective-permute-start.17
  81.3 11.4 %field.1.after = bf16[4,4,48,256]{3,2,1,0:T(8,128)(2,1)} custom-call(s32[3]{0:T(128)S(1)} %pad_add_fusion.pos.refs_0_, bf16[1744,128]{1,0:T(8,128)(2,1)} %get-tuple-element.47.after, bf16[4,6,64,256]{3,2,1,0:T(8,128)(2,1)S(1)} %get-tuple-element.46.mine, bf16[4,6,64,256]{3,2,1,0:T(8,128)(2,1)S(1)} %collective-permute-done.16.after.theirs, ...), custom_call_target="tpu_custom_call" | custom-call | flops 10871635968 | bytes 7077888 | tf_op jit(solution)/shard_map/field/pallas_call | solution.py:565
  92.7 4.7 %collective-permute-done.17.west = bf16[1296,128]{1,0:T(8,128)(2,1)S(1)} collective-permute-done((bf16[1296,128]{1,0:T(8,128)(2,1)S(1)}, bf16[1296,128]{1,0:T(8,128)(2,1)S(1)}, u32[]{:S(2)}, u32[]{:S(2)}) %collective-permute-start.17) | collective-permute-done | bytes 331808 | tf_op jit(solution)/shard_map/ppermute | solution.py:98
  97.4 14.1 %all-gather.4.cloned.1.call-done.plane.refs_1_ = bf16[6976,128]{1,0:T(8,128)(2,1)} async-done(((bf16[1744,128]{1,0:T(8,128)(2,1)}), bf16[6976,128]{1,0:T(8,128)(2,1)}) %all-gather.4.cloned.1.call-update) | async-done | bytes 1785872 | tf_op jit(solution)/shard_map/all_gather | solution.py:589
  111.5 1.5 copy-done
  113.0 1.0 copy-done.5
  113.9 1.6 join.1
  115.7 3.4 %collective-permute-start.20 = (bf16[2512,128]{1,0:T(8,128)(2,1)S(1)}, bf16[2512,128]{1,0:T(8,128)(2,1)S(1)}, u32[]{:S(2)}, u32[]{:S(2)}) collective-permute-start(bf16[2512,128]{1,0:T(8,128)(2,1)S(1)} %get-tuple-element.50), channel_id=1, source_target_pairs={{0,3},{1,0},{2,1},{3,2},{4,7},{5,4},{6,5},{7,6},{8,11},{9,8},{10,9... | collective-permute-start | bytes 1929224 | tf_op jit(solution)/shard_map/ppermute | solution.py:98
  119.0 5.4 %unpack_1.1 = (f32[27,256,512]{2,1,0:T(8,128)}, f32[8,128]{1,0:T(8,128)}) custom-call(s32[3]{0:T(128)} %copy-done.7, bf16[6976,128]{1,0:T(8,128)(2,1)} %all-gather.4.cloned.1.call-done.plane.refs_1_, bf16[2592,128]{1,0:T(8,128)(2,1)} %get-tuple-element.51.refs_2_, f32[27,256,512]{2,1,0:T(8,128)} %get-tuple-element.52.refs_3_), custom_call_target="tpu_custom_call", output_to_operand_aliasing={{0}: (3, {})} | custom-call | bytes 4194304 | tf_op jit(solution)/shard_map/unpack_1/pallas_call | solution.py:397
  124.5 23.0 %collective-permute-done.19.by_3.refs_2_ = bf16[2496,128]{1,0:T(8,128)(2,1)S(1)} collective-permute-done((bf16[2496,128]{1,0:T(8,128)(2,1)S(1)}, bf16[2496,128]{1,0:T(8,128)(2,1)S(1)}, u32[]{:S(2)}, u32[]{:S(2)}) %collective-permute-start.19) | collective-permute-done | bytes 639008 | tf_op jit(solution)/shard_map/ppermute | solution.py:98
  147.5 0.7 copy-done.9
  148.1 1.4 across.1
  149.5 1.6 collective-permute-start.21
  151.1 2.3 %collective-permute-start.22 = (bf16[928,128]{1,0:T(8,128)(2,1)S(1)}, bf16[928,128]{1,0:T(8,128)(2,1)S(1)}, u32[]{:S(2)}, u32[]{:S(2)}) collective-permute-start(bf16[928,128]{1,0:T(8,128)(2,1)S(1)} %get-tuple-element.55), channel_id=1, source_target_pairs={{0,3},{1,0},{2,1},{3,2},{4,7},{5,4},{6,5},{7,6},{8,11},{9,8},{10,9... | collective-permute-start | bytes 712712 | tf_op jit(solution)/shard_map/ppermute | solution.py:98
  153.4 2.3 %all-gather.8.cloned.1.call-done.refs_1_ = bf16[10368,128]{1,0:T(8,128)(2,1)} async-done(((bf16[2592,128]{1,0:T(8,128)(2,1)}), bf16[10368,128]{1,0:T(8,128)(2,1)}) %all-gather.8.cloned.1.call-update) | async-done | bytes 2654224 | tf_op jit(solution)/shard_map/all_gather | solution.py:589
  155.7 8.9 %unpack_2.1 = (f32[27,256,512]{2,1,0:T(8,128)}, f32[8,128]{1,0:T(8,128)}) custom-call(s32[3]{0:T(128)} %copy-done.7, bf16[10368,128]{1,0:T(8,128)(2,1)} %all-gather.8.cloned.1.call-done.refs_1_, bf16[2496,128]{1,0:T(8,128)(2,1)} %copy-done.2, bf16[2512,128]{1,0:T(8,128)(2,1)} %copy-done.1, ...), custom_call_target="tpu_custom_call", output_to_operand_aliasing={{0}: (5, {})} | custom-call | bytes 4194304 | tf_op jit(solution)/shard_map/unpack_2/pallas_call | solution.py:397
  164.7 21.9 %all-gather.6.cloned.1.call-done.refs_3_ = bf16[5184,128]{1,0:T(8,128)(2,1)} async-done(((bf16[1296,128]{1,0:T(8,128)(2,1)}), bf16[5184,128]{1,0:T(8,128)(2,1)}) %all-gather.6.cloned.1.call-update) | async-done | bytes 1327120 | tf_op jit(solution)/shard_map/all_gather | solution.py:589
  186.5 5.5 %unpack_3.1 = (f32[27,256,512]{2,1,0:T(8,128)}, f32[8,128]{1,0:T(8,128)}) custom-call(s32[3]{0:T(128)} %copy-done.7, bf16[928,128]{1,0:T(8,128)(2,1)} %copy-done.10, bf16[928,128]{1,0:T(8,128)(2,1)} %copy-done.11, bf16[5184,128]{1,0:T(8,128)(2,1)} %all-gather.6.cloned.1.call-done.refs_3_, ...), custom_call_target="tpu_custom_call", output_to_operand_aliasing={{0}: (4, {})} | custom-call | bytes 4194304 | tf_op jit(solution)/shard_map/unpack_3/pallas_call | solution.py:397
  (45 shorter events, 0.4 us)
Async XLA Ops:
  7.2 104.3 %all-gather.4.cloned.1.call-start = ((), (), s32[]{:S(2)}) async-start(), calls=%async_computation | async-start | bytes 2232320 | tf_op jit(solution)/shard_map/all_gather | solution.py:589
  7.3 104.2 %copy-start.7 = (s32[3]{0:T(128)}, s32[3]{0:T(128)S(1)}, u32[]{:S(2)}) copy-start(s32[3]{0:T(128)S(1)} %pad_add_fusion.pos.refs_0_) | copy-start | bytes 40
  7.3 1.0 copy-start.3
  8.3 1.0 copy-start.6
  10.1 18.4 %collective-permute-start.3 = (bf16[768,128]{1,0:T(8,128)(2,1)S(1)}, bf16[768,128]{1,0:T(8,128)(2,1)S(1)}, u32[]{:S(2)}, u32[]{:S(2)}) collective-permute-start(bf16[768,128]{1,0:T(8,128)(2,1)S(1)} %get-tuple-element.35), channel_id=1, source_target_pairs={{0,0},{1,1},{2,2},{3,3},{4,4},{5,5},{6,6},{7,7},{8,16},{9,17},{10,... | collective-permute-start | bytes 589832 | tf_op jit(solution)/shard_map/ppermute | solution.py:98
  10.8 17.7 %collective-permute-start.4 = (bf16[768,128]{1,0:T(8,128)(2,1)S(1)}, bf16[768,128]{1,0:T(8,128)(2,1)S(1)}, u32[]{:S(2)}, u32[]{:S(2)}) collective-permute-start(bf16[768,128]{1,0:T(8,128)(2,1)S(1)} %get-tuple-element.36), channel_id=1, source_target_pairs={{0,4},{1,5},{2,6},{3,7},{4,0},{5,1},{6,2},{7,3},{8,20},{9,21},{10,... | collective-permute-start | bytes 589832 | tf_op jit(solution)/shard_map/ppermute | solution.py:98
  13.8 11.7 %collective-permute-start = (bf16[416,128]{1,0:T(8,128)(2,1)S(1)}, bf16[416,128]{1,0:T(8,128)(2,1)S(1)}, u32[]{:S(2)}, u32[]{:S(2)}) collective-permute-start(bf16[416,128]{1,0:T(8,128)(2,1)S(1)} %get-tuple-element.32), channel_id=1, source_target_pairs={{0,1},{1,2},{2,3},{3,0},{4,5},{5,6},{6,7},{7,4},{8,9},{9,10},{10,1... | collective-permute-start | bytes 319496 | tf_op jit(solution)/shard_map/ppermute | solution.py:98
  15.4 10.1 %collective-permute-start.1 = (bf16[384,128]{1,0:T(8,128)(2,1)S(1)}, bf16[384,128]{1,0:T(8,128)(2,1)S(1)}, u32[]{:S(2)}, u32[]{:S(2)}) collective-permute-start(bf16[384,128]{1,0:T(8,128)(2,1)S(1)} %get-tuple-element.33), channel_id=1, source_target_pairs={{0,2},{1,3},{2,0},{3,1},{4,6},{5,7},{6,4},{7,5},{8,10},{9,11},{10,... | collective-permute-start | bytes 294920 | tf_op jit(solution)/shard_map/ppermute | solution.py:98
  18.0 10.6 %collective-permute-start.2 = (bf16[416,128]{1,0:T(8,128)(2,1)S(1)}, bf16[416,128]{1,0:T(8,128)(2,1)S(1)}, u32[]{:S(2)}, u32[]{:S(2)}) collective-permute-start(bf16[416,128]{1,0:T(8,128)(2,1)S(1)} %get-tuple-element.34), channel_id=1, source_target_pairs={{0,3},{1,0},{2,1},{3,2},{4,7},{5,4},{6,5},{7,6},{8,11},{9,8},{10,9... | collective-permute-start | bytes 319496 | tf_op jit(solution)/shard_map/ppermute | solution.py:98
  25.5 7.3 %collective-permute-start.10 = (bf16[384,128]{1,0:T(8,128)(2,1)S(1)}, bf16[384,128]{1,0:T(8,128)(2,1)S(1)}, u32[]{:S(2)}, u32[]{:S(2)}) collective-permute-start(bf16[384,128]{1,0:T(8,128)(2,1)S(1)} %get-tuple-element.40), channel_id=1, source_target_pairs={{0,4},{1,5},{2,6},{3,7},{4,0},{5,1},{6,2},{7,3},{8,12},{9,13},{10,... | collective-permute-start | bytes 294920 | tf_op jit(solution)/shard_map/ppermute | solution.py:98
  25.5 10.1 %collective-permute-start.11 = (bf16[384,128]{1,0:T(8,128)(2,1)S(1)}, bf16[384,128]{1,0:T(8,128)(2,1)S(1)}, u32[]{:S(2)}, u32[]{:S(2)}) collective-permute-start(bf16[384,128]{1,0:T(8,128)(2,1)S(1)} %get-tuple-element.41), channel_id=1, source_target_pairs={{0,12},{1,13},{2,14},{3,15},{4,8},{5,9},{6,10},{7,11},{8,4},{9,5},... | collective-permute-start | bytes 294920 | tf_op jit(solution)/shard_map/ppermute | solution.py:98
  29.3 22.6 %collective-permute-start.7 = (bf16[1600,128]{1,0:T(8,128)(2,1)S(1)}, bf16[1600,128]{1,0:T(8,128)(2,1)S(1)}, u32[]{:S(2)}, u32[]{:S(2)}) collective-permute-start(bf16[1600,128]{1,0:T(8,128)(2,1)S(1)} %get-tuple-element.37.own.x_own), channel_id=1, source_target_pairs={{0,12},{1,13},{2,14},{3,15},{4,8},{5,9},{6,10},{7,11},{8,4},{9,5},... | collective-permute-start | bytes 1228808 | tf_op jit(solution)/shard_map/ppermute | solution.py:98
  29.3 22.5 %collective-permute-start.5 = (bf16[1600,128]{1,0:T(8,128)(2,1)S(1)}, bf16[1600,128]{1,0:T(8,128)(2,1)S(1)}, u32[]{:S(2)}, u32[]{:S(2)}) collective-permute-start(bf16[1600,128]{1,0:T(8,128)(2,1)S(1)} %get-tuple-element.37.own.x_own), channel_id=1, source_target_pairs={{0,4},{1,5},{2,6},{3,7},{4,0},{5,1},{6,2},{7,3},{8,12},{9,13},{10,... | collective-permute-start | bytes 1228808 | tf_op jit(solution)/shard_map/ppermute | solution.py:98
  31.2 18.9 %collective-permute-start.6 = (bf16[1536,128]{1,0:T(8,128)(2,1)S(1)}, bf16[1536,128]{1,0:T(8,128)(2,1)S(1)}, u32[]{:S(2)}, u32[]{:S(2)}) collective-permute-start(bf16[1536,128]{1,0:T(8,128)(2,1)S(1)} %get-tuple-element.38), channel_id=1, source_target_pairs={{0,8},{1,9},{2,10},{3,11},{4,12},{5,13},{6,14},{7,15},{8,0},{9,1},... | collective-permute-start | bytes 1179656 | tf_op jit(solution)/shard_map/ppermute | solution.py:98
  32.8 17.3 %collective-permute-start.9 = (bf16[2,768,128]{2,1,0:T(8,128)(2,1)S(1)}, bf16[2,768,128]{2,1,0:T(8,128)(2,1)S(1)}, u32[]{:S(2)}, u32[]{:S(2)}) collective-permute-start(bf16[2,768,128]{2,1,0:T(8,128)(2,1)S(1)} %get-tuple-element.39.here), channel_id=1, source_target_pairs={{0,3},{1,0},{2,1},{3,2},{4,7},{5,4},{6,5},{7,6},{8,11},{9,8},{10,9... | collective-permute-start | bytes 1179656 | tf_op jit(solution)/shard_map/ppermute | solution.py:98
  35.6 16.3 %collective-permute-start.8 = (bf16[2,768,128]{2,1,0:T(8,128)(2,1)S(1)}, bf16[2,768,128]{2,1,0:T(8,128)(2,1)S(1)}, u32[]{:S(2)}, u32[]{:S(2)}) collective-permute-start(bf16[2,768,128]{2,1,0:T(8,128)(2,1)S(1)} %get-tuple-element.39.here), channel_id=1, source_target_pairs={{0,1},{1,2},{2,3},{3,0},{4,5},{5,6},{6,7},{7,4},{8,9},{9,10},{10,1... | collective-permute-start | bytes 1179656 | tf_op jit(solution)/shard_map/ppermute | solution.py:98
  51.9 1.0 copy-start.4
  53.7 15.2 %collective-permute-start.12 = (bf16[6,768,128]{2,1,0:T(8,128)(2,1)S(1)}, bf16[6,768,128]{2,1,0:T(8,128)(2,1)S(1)}, u32[]{:S(2)}, u32[]{:S(2)}) collective-permute-start(bf16[6,768,128]{2,1,0:T(8,128)(2,1)S(1)} %get-tuple-element.44.g), channel_id=1, source_target_pairs={{0,16},{1,17},{2,18},{3,19},{4,20},{5,21},{6,22},{7,23},{8,24},{9,... | collective-permute-start | bytes 3538952 | tf_op jit(solution)/shard_map/ppermute | solution.py:98
  53.7 8.2 %collective-permute-start.14 = (bf16[768,128]{1,0:T(8,128)(2,1)S(1)}, bf16[768,128]{1,0:T(8,128)(2,1)S(1)}, u32[]{:S(2)}, u32[]{:S(2)}) collective-permute-start(bf16[768,128]{1,0:T(8,128)(2,1)S(1)} %get-tuple-element.45), channel_id=1, source_target_pairs={{0,3},{1,0},{2,1},{3,2},{4,7},{5,4},{6,5},{7,6},{8,11},{9,8},{10,9... | collective-permute-start | bytes 589832 | tf_op jit(solution)/shard_map/ppermute | solution.py:98
  56.7 9.8 %collective-permute-start.13 = (bf16[768,128]{1,0:T(8,128)(2,1)S(1)}, bf16[768,128]{1,0:T(8,128)(2,1)S(1)}, u32[]{:S(2)}, u32[]{:S(2)}) collective-permute-start(bf16[768,128]{1,0:T(8,128)(2,1)S(1)} %get-tuple-element.42.after), channel_id=1, source_target_pairs={{0,1},{1,2},{2,3},{3,0},{4,5},{5,6},{6,7},{7,4},{8,9},{9,10},{10,1... | collective-permute-start | bytes 589832 | tf_op jit(solution)/shard_map/ppermute | solution.py:98
  67.1 1.8 collective-permute-start.15
  67.1 10.3 %collective-permute-start.16 = (bf16[4,6,64,256]{3,2,1,0:T(8,128)(2,1)S(1)}, bf16[4,6,64,256]{3,2,1,0:T(8,128)(2,1)S(1)}, u32[]{:S(2)}, u32[]{:S(2)}) collective-permute-start(bf16[4,6,64,256]{3,2,1,0:T(8,128)(2,1)S(1)} %get-tuple-element.46.mine), channel_id=1, source_target_pairs={{0,16},{1,17},{2,18},{3,19},{4,20},{5,21},{6,22},{7,23},{8,24},{9,... | collective-permute-start | bytes 2359304 | tf_op jit(solution)/shard_map/ppermute | solution.py:98
  79.2 76.5 %all-gather.8.cloned.1.call-start = ((), (), s32[]{:S(2)}) async-start(), calls=%async_computation.2 | async-start | bytes 3317760 | tf_op jit(solution)/shard_map/all_gather | solution.py:589
  79.2 13.5 %collective-permute-start.18 = (bf16[1296,128]{1,0:T(8,128)(2,1)S(1)}, bf16[1296,128]{1,0:T(8,128)(2,1)S(1)}, u32[]{:S(2)}, u32[]{:S(2)}) collective-permute-start(bf16[1296,128]{1,0:T(8,128)(2,1)S(1)} %get-tuple-element.48), channel_id=1, source_target_pairs={{0,3},{1,0},{2,1},{3,2},{4,7},{5,4},{6,5},{7,6},{8,11},{9,8},{10,9... | collective-permute-start | bytes 995336 | tf_op jit(solution)/shard_map/ppermute | solution.py:98
  81.0 16.4 %collective-permute-start.17 = (bf16[1296,128]{1,0:T(8,128)(2,1)S(1)}, bf16[1296,128]{1,0:T(8,128)(2,1)S(1)}, u32[]{:S(2)}, u32[]{:S(2)}) collective-permute-start(bf16[1296,128]{1,0:T(8,128)(2,1)S(1)} %get-tuple-element.48), channel_id=1, source_target_pairs={{0,1},{1,2},{2,3},{3,0},{4,5},{5,6},{6,7},{7,4},{8,9},{9,10},{10,1... | collective-permute-start | bytes 995336 | tf_op jit(solution)/shard_map/ppermute | solution.py:98
  111.5 1.5 copy-start
  113.0 1.0 copy-start.5
  115.6 70.9 %all-gather.6.cloned.1.call-start = ((), (), s32[]{:S(2)}) async-start(), calls=%async_computation.1 | async-start | bytes 1658880 | tf_op jit(solution)/shard_map/all_gather | solution.py:589
  115.7 31.8 %collective-permute-start.20 = (bf16[2512,128]{1,0:T(8,128)(2,1)S(1)}, bf16[2512,128]{1,0:T(8,128)(2,1)S(1)}, u32[]{:S(2)}, u32[]{:S(2)}) collective-permute-start(bf16[2512,128]{1,0:T(8,128)(2,1)S(1)} %get-tuple-element.50), channel_id=1, source_target_pairs={{0,3},{1,0},{2,1},{3,2},{4,7},{5,4},{6,5},{7,6},{8,11},{9,8},{10,9... | collective-permute-start | bytes 1929224 | tf_op jit(solution)/shard_map/ppermute | solution.py:98
  119.0 28.4 %collective-permute-start.19 = (bf16[2496,128]{1,0:T(8,128)(2,1)S(1)}, bf16[2496,128]{1,0:T(8,128)(2,1)S(1)}, u32[]{:S(2)}, u32[]{:S(2)}) collective-permute-start(bf16[2496,128]{1,0:T(8,128)(2,1)S(1)} %get-tuple-element.49), channel_id=1, source_target_pairs={{0,1},{1,2},{2,3},{3,0},{4,5},{5,6},{6,7},{7,4},{8,9},{9,10},{10,1... | collective-permute-start | bytes 1916936 | tf_op jit(solution)/shard_map/ppermute | solution.py:98
  119.0 28.4 %copy-start.8 = (s32[3]{0:T(128)S(1)}, s32[3]{0:T(128)}, u32[]{:S(2)}) copy-start(s32[3]{0:T(128)} %copy-done.7) | copy-start | bytes 40
  147.5 8.2 %copy-start.2 = (bf16[2496,128]{1,0:T(8,128)(2,1)}, bf16[2496,128]{1,0:T(8,128)(2,1)S(1)}, u32[]{:S(2)}) copy-start(bf16[2496,128]{1,0:T(8,128)(2,1)S(1)} %collective-permute-done.19.by_3.refs_2_) | copy-start | bytes 1916932
  147.5 8.2 %copy-start.1 = (bf16[2512,128]{1,0:T(8,128)(2,1)}, bf16[2512,128]{1,0:T(8,128)(2,1)S(1)}, u32[]{:S(2)}) copy-start(bf16[2512,128]{1,0:T(8,128)(2,1)S(1)} %collective-permute-done.20.by_1.refs_3_) | copy-start | bytes 1929220
  147.5 0.7 copy-start.9
  149.5 15.1 %collective-permute-start.21 = (bf16[928,128]{1,0:T(8,128)(2,1)S(1)}, bf16[928,128]{1,0:T(8,128)(2,1)S(1)}, u32[]{:S(2)}, u32[]{:S(2)}) collective-permute-start(bf16[928,128]{1,0:T(8,128)(2,1)S(1)} %get-tuple-element.54), channel_id=1, source_target_pairs={{0,1},{1,2},{2,3},{3,0},{4,5},{5,6},{6,7},{7,4},{8,9},{9,10},{10,1... | collective-permute-start | bytes 712712 | tf_op jit(solution)/shard_map/ppermute | solution.py:98
  151.1 13.5 %collective-permute-start.22 = (bf16[928,128]{1,0:T(8,128)(2,1)S(1)}, bf16[928,128]{1,0:T(8,128)(2,1)S(1)}, u32[]{:S(2)}, u32[]{:S(2)}) collective-permute-start(bf16[928,128]{1,0:T(8,128)(2,1)S(1)} %get-tuple-element.55), channel_id=1, source_target_pairs={{0,3},{1,0},{2,1},{3,2},{4,7},{5,4},{6,5},{7,6},{8,11},{9,8},{10,9... | collective-permute-start | bytes 712712 | tf_op jit(solution)/shard_map/ppermute | solution.py:98
  164.6 21.9 %copy-start.10 = (bf16[928,128]{1,0:T(8,128)(2,1)}, bf16[928,128]{1,0:T(8,128)(2,1)S(1)}, u32[]{:S(2)}) copy-start(bf16[928,128]{1,0:T(8,128)(2,1)S(1)} %collective-permute-done.21.refs_1_) | copy-start | bytes 712708
  164.6 21.9 %copy-start.11 = (bf16[928,128]{1,0:T(8,128)(2,1)}, bf16[928,128]{1,0:T(8,128)(2,1)S(1)}, u32[]{:S(2)}) copy-start(bf16[928,128]{1,0:T(8,128)(2,1)S(1)} %collective-permute-done.22.refs_2_) | copy-start | bytes 712708
Sparse Core Ops, SparseCore 0:
  79.3 32.1 all-gather.3
  115.7 39.8 all-gather.7
  157.5 28.9 all-gather.5

commit v10 on v8

--- a/solution.py
+++ b/solution.py
@@ -318,7 +318,7 @@
     for tap in range(27):
         value = held[tap] * shrink
         square = value * value
-        code = (square * square * square * value * jnp.abs(value)).astype(out.dtype)
+        code = (square * value * jnp.abs(value)).astype(out.dtype)
         out[tap * span : (tap + 1) * span, :] = code
         if tap * span >= skip:
             late[tap * span - skip : (tap + 1) * span - skip, :] = code
@@ -326,14 +326,19 @@
     late[27 * span - skip :, :] = unit.astype(out.dtype)
 
 
-def join_kernel(pos, west, east, own, x, y, d, after, both, by_3, by_1):
+def both_kernel(pos, west, east, after, both):
+    del pos, after
+    size = west.shape[0]
+    both[0:size, :] = west[...]
+    both[size:, :] = east[...]
+
+
+def join_kernel(pos, west, east, own, x, y, d, after, by_3, by_1):
     del pos, after
     size = west.shape[0]
     cut = own.shape[0] - size
     end = own.shape[0] - 16
     half = by_3.shape[0] - 4 * (cut + 16)
-    both[0:size, :] = west[...]
-    both[size:, :] = east[...]
     by_3[0:half, :] = west[0:half, :]
     by_1[0 : size - half, :] = east[half:, :]
     for out, at in ((by_3, half), (by_1, size - half)):
@@ -373,16 +378,15 @@
     for at, (_, _, many, skip, pieces) in enumerate(parts):
         if at >= 2:
             copy(at - 2).wait()
-        for tag, (which, row, power_row) in enumerate(pieces):
-            source = sources[which]
-            unit = source[power_row : power_row + 16, :].astype(jnp.float32)[0:1]
-            lanes = pl.ds(pl.multiple_of((pos[1] ^ tag) * wide, wide), wide)
-
-            @pl.loop(0, many)
-            def _(tap, source=source, start=row + skip * span, unit=unit, lanes=lanes, at=at):
-                code = source[pl.ds(pl.multiple_of(start + tap * span, 16), span), :].astype(jnp.float32)
-                root = lax.rsqrt(lax.rsqrt(jnp.abs(code)))
-                root = root * lax.rsqrt(jnp.maximum(root, 1e-30)) * unit
+        units = [sources[i][j : j + 16, :].astype(jnp.float32)[0:1] for i, _, j in pieces]
+
+        @pl.loop(0, many)
+        def _(tap, pieces=pieces, skip=skip, units=units, at=at):
+            for tag, (which, row, _) in enumerate(pieces):
+                start = pl.multiple_of(row + (skip + tap) * span, 16)
+                code = sources[which][pl.ds(start, span), :].astype(jnp.float32)
+                root = lax.rsqrt(lax.rsqrt(jnp.abs(code))) * units[tag]
+                lanes = pl.ds(pl.multiple_of((pos[1] ^ tag) * wide, wide), wide)
                 buffers[at % 2, tap, :, lanes] = jnp.where(code < 0, -root, root)
 
         copy(at).start()
@@ -545,7 +549,7 @@
         pair_kernel, [jax.ShapeDtypeStruct((2, cells, wide), bf16)], (pos, g2a, g2b, xs), [], 0, "pair", 16, held=1
     )
     s2 = move(g2, sibling)
-    early = 7
+    early = 6
     cut, end = early * span, 27 * span
     size = end + 16 - cut
     half = size // 32 * 16
@@ -592,10 +596,11 @@
     from_3 = move(late, lon_by(1))
     from_1 = move(late, lon_by(-1))
     plane = [own] + to_plane(own)
-    pair, z_3, z_1 = call(
+    (pair,) = call(both_kernel, [slab(2 * size)], (pos, from_3, from_1, field), [], 0, "both", 16, held=1)
+    z_3, z_1 = call(
         join_kernel,
-        [slab(2 * size), slab(half + 4 * first_rows), slab(size - half + 4 * first_rows)],
-        (pos, from_3, from_1, *plane, field),
+        [slab(half + 4 * first_rows), slab(size - half + 4 * first_rows)],
+        (pos, from_3, from_1, *plane, pair),
         [],
         0,
         "join",

time: 158 us -> 152 us (0.962)
  Pallas kernels: 52.8 us -> 49 us
  waiting for transfers between devices: 55.7 us -> 54.1 us
    pallas_call x3, Pallas kernels: 22.9 us -> 18.6 us  [unpack(): pl.pallas_call(lambda *refs: unpack_kernel(*refs, slabs=slabs, count=len(...]
    ppermute x32, waiting for transfers between devices: 55.7 us -> 54.1 us  [move(): return lax.ppermute(x, AXES, pairs)]
    pallas_call x8 -> x9, Pallas kernels: 13.7 us -> 14.1 us  [call(): pl.pallas_call(kernel, out_shape=outs, in_specs=[pl.BlockSpec(memory_spac...]
  transfers between devices with their start and end apart: 32 -> 32, of which waited for: 10 -> 11; matrix products, arithmetic and copies ran while one was open for 0% -> 0% of each run, Pallas kernels for 27% -> 27%
where the time goes in v10:
time: 152 us
  waiting for transfers between devices  54.1 us (36%)
  Pallas kernels  49 us (32%)
  starting transfers between devices  41.9 us (28%)
  local copies, waits for them, and re-layouts  5.57 us (4%)
    ppermute x32, waiting for transfers between devices, move(): return lax.ppermute(x, AXES, pairs)  54.1 us
    ppermute x32, starting transfers between devices, move(): return lax.ppermute(x, AXES, pairs)  41.9 us
    pallas_call x3, Pallas kernels, unpack(): pl.pallas_call(lambda *refs: unpack_kernel(*refs, slabs=slabs, count=len(...  18.6 us
    pallas_call x9, Pallas kernels, call(): pl.pallas_call(kernel, out_shape=outs, in_specs=[pl.BlockSpec(memory_spac...  14.1 us
    pallas_call x1, Pallas kernels, blocked_body(): pl.pallas_call(field_kernel, out_shape=jax.ShapeDtypeStruct((levels, heig...  11.4 us
    unnamed x50, local copies, waits for them, and re-layouts  5.57 us
    pallas_call x1, Pallas kernels, blocked_body(): pl.pallas_call(lines_kernel, out_shape=[jax.ShapeDtypeStruct((levels, row...  4.86 us
  transfers between devices with their start and end apart: 32, of which 11 were waited for; matrix products, arithmetic and copies ran while one was open for 0% of the time, Pallas kernels for 27%

profile of v10, /device:TPU:0, one launch (start us, length us, event | category | flops | bytes accessed | tf_op | source)
XLA Modules:
  0.0 151.6 jit_solution(1485032652186463267)
XLA Ops:
  0.7 1.0 copy-done.9
  1.7 1.0 copy-done.12
  2.7 0.8 pack.1
  3.6 0.7 collective-permute-start.3
  4.2 3.0 %collective-permute-start.4 = (bf16[768,128]{1,0:T(8,128)(2,1)S(1)}, bf16[768,128]{1,0:T(8,128)(2,1)S(1)}, u32[]{:S(2)}, u32[]{:S(2)}) collective-permute-start(bf16[768,128]{1,0:T(8,128)(2,1)S(1)} %get-tuple-element.35), channel_id=1, source_target_pairs={{0,4},{1,5},{2,6},{3,7},{4,0},{5,1},{6,2},{7,3},{8,20},{9,21},{10,... | collective-permute-start | bytes 589832 | tf_op jit(solution)/shard_map/ppermute | solution.py:98
  7.2 1.6 %collective-permute-start = (bf16[416,128]{1,0:T(8,128)(2,1)S(1)}, bf16[416,128]{1,0:T(8,128)(2,1)S(1)}, u32[]{:S(2)}, u32[]{:S(2)}) collective-permute-start(bf16[416,128]{1,0:T(8,128)(2,1)S(1)} %get-tuple-element.31), channel_id=1, source_target_pairs={{0,1},{1,2},{2,3},{3,0},{4,5},{5,6},{6,7},{7,4},{8,9},{9,10},{10,1... | collective-permute-start | bytes 319496 | tf_op jit(solution)/shard_map/ppermute | solution.py:98
  8.8 2.6 %collective-permute-start.1 = (bf16[384,128]{1,0:T(8,128)(2,1)S(1)}, bf16[384,128]{1,0:T(8,128)(2,1)S(1)}, u32[]{:S(2)}, u32[]{:S(2)}) collective-permute-start(bf16[384,128]{1,0:T(8,128)(2,1)S(1)} %get-tuple-element.32), channel_id=1, source_target_pairs={{0,2},{1,3},{2,0},{3,1},{4,6},{5,7},{6,4},{7,5},{8,10},{9,11},{10,... | collective-permute-start | bytes 294920 | tf_op jit(solution)/shard_map/ppermute | solution.py:98
  11.4 1.3 collective-permute-start.2
  12.8 6.2 %collective-permute-done.1.x2 = bf16[384,128]{1,0:T(8,128)(2,1)S(1)} collective-permute-done((bf16[384,128]{1,0:T(8,128)(2,1)S(1)}, bf16[384,128]{1,0:T(8,128)(2,1)S(1)}, u32[]{:S(2)}, u32[]{:S(2)}) %collective-permute-start.1) | collective-permute-done | bytes 98336 | tf_op jit(solution)/shard_map/ppermute | solution.py:98
  18.9 3.0 %collective-permute-start.11 = (bf16[384,128]{1,0:T(8,128)(2,1)S(1)}, bf16[384,128]{1,0:T(8,128)(2,1)S(1)}, u32[]{:S(2)}, u32[]{:S(2)}) collective-permute-start(bf16[384,128]{1,0:T(8,128)(2,1)S(1)} %get-tuple-element.40), channel_id=1, source_target_pairs={{0,12},{1,13},{2,14},{3,15},{4,8},{5,9},{6,10},{7,11},{8,4},{9,5},... | collective-permute-start | bytes 294920 | tf_op jit(solution)/shard_map/ppermute | solution.py:98
  22.0 0.7 spread.1
  22.8 1.9 %collective-permute-start.5 = (bf16[1600,128]{1,0:T(8,128)(2,1)S(1)}, bf16[1600,128]{1,0:T(8,128)(2,1)S(1)}, u32[]{:S(2)}, u32[]{:S(2)}) collective-permute-start(bf16[1600,128]{1,0:T(8,128)(2,1)S(1)} %get-tuple-element.36.own.x_own), channel_id=1, source_target_pairs={{0,4},{1,5},{2,6},{3,7},{4,0},{5,1},{6,2},{7,3},{8,12},{9,13},{10,... | collective-permute-start | bytes 1228808 | tf_op jit(solution)/shard_map/ppermute | solution.py:98
  24.6 1.6 %collective-permute-start.6 = (bf16[1536,128]{1,0:T(8,128)(2,1)S(1)}, bf16[1536,128]{1,0:T(8,128)(2,1)S(1)}, u32[]{:S(2)}, u32[]{:S(2)}) collective-permute-start(bf16[1536,128]{1,0:T(8,128)(2,1)S(1)} %get-tuple-element.37), channel_id=1, source_target_pairs={{0,8},{1,9},{2,10},{3,11},{4,12},{5,13},{6,14},{7,15},{8,0},{9,1},... | collective-permute-start | bytes 1179656 | tf_op jit(solution)/shard_map/ppermute | solution.py:98
  26.2 2.8 %collective-permute-start.9 = (bf16[2,768,128]{2,1,0:T(8,128)(2,1)S(1)}, bf16[2,768,128]{2,1,0:T(8,128)(2,1)S(1)}, u32[]{:S(2)}, u32[]{:S(2)}) collective-permute-start(bf16[2,768,128]{2,1,0:T(8,128)(2,1)S(1)} %get-tuple-element.38.here), channel_id=1, source_target_pairs={{0,3},{1,0},{2,1},{3,2},{4,7},{5,4},{6,5},{7,6},{8,11},{9,8},{10,9... | collective-permute-start | bytes 1179656 | tf_op jit(solution)/shard_map/ppermute | solution.py:98
  29.0 14.5 %collective-permute-done.6.after.x_y = bf16[1536,128]{1,0:T(8,128)(2,1)S(1)} collective-permute-done((bf16[1536,128]{1,0:T(8,128)(2,1)S(1)}, bf16[1536,128]{1,0:T(8,128)(2,1)S(1)}, u32[]{:S(2)}, u32[]{:S(2)}) %collective-permute-start.6) | collective-permute-done | bytes 393248 | tf_op jit(solution)/shard_map/ppermute | solution.py:98
  43.5 1.8 %collective-permute-done.8.west = bf16[2,768,128]{2,1,0:T(8,128)(2,1)S(1)} collective-permute-done((bf16[2,768,128]{2,1,0:T(8,128)(2,1)S(1)}, bf16[2,768,128]{2,1,0:T(8,128)(2,1)S(1)}, u32[]{:S(2)}, u32[]{:S(2)}) %collective-permute-start.8) | collective-permute-done | bytes 393248 | tf_op jit(solution)/shard_map/ppermute | solution.py:98
  45.3 1.0 copy-done.10
  46.3 0.8 split.1
  47.2 3.0 %collective-permute-start.14 = (bf16[768,128]{1,0:T(8,128)(2,1)S(1)}, bf16[768,128]{1,0:T(8,128)(2,1)S(1)}, u32[]{:S(2)}, u32[]{:S(2)}) collective-permute-start(bf16[768,128]{1,0:T(8,128)(2,1)S(1)} %get-tuple-element.44), channel_id=1, source_target_pairs={{0,3},{1,0},{2,1},{3,2},{4,7},{5,4},{6,5},{7,6},{8,11},{9,8},{10,9... | collective-permute-start | bytes 589832 | tf_op jit(solution)/shard_map/ppermute | solution.py:98
  50.1 4.9 %lines.1 = (bf16[4,18,192,256]{3,2,1,0:T(8,128)(2,1)S(1)}, f32[27,256,512]{2,1,0:T(8,128)}) custom-call(s32[3]{0:T(128)S(1)} %pad_add_fusion.pos.refs_0_, bf16[1600,128]{1,0:T(8,128)(2,1)S(1)} %get-tuple-element.36.own.x_own, bf16[1600,128]{1,0:T(8,128)(2,1)S(1)} %collective-permute-done.5.x_x, bf16[1536,128]{1,0:T(8,128)(2,1)S(1)} %collective-permute-done.6.after.x_y, ...), custom_call_target="tpu_custom_call" | custom-call | bytes 1048576 | tf_op jit(solution)/shard_map/lines/pallas_call | solution.py:534
  55.4 4.5 %collective-permute-done.13.one = bf16[768,128]{1,0:T(8,128)(2,1)S(1)} collective-permute-done((bf16[768,128]{1,0:T(8,128)(2,1)S(1)}, bf16[768,128]{1,0:T(8,128)(2,1)S(1)}, u32[]{:S(2)}, u32[]{:S(2)}) %collective-permute-start.13) | collective-permute-done | bytes 196640 | tf_op jit(solution)/shard_map/ppermute | solution.py:98
  61.0 1.2 collective-permute-done.15.s2
  62.3 8.6 %taps.1.held = f32[27,64,128]{2,1,0:T(8,128)S(1)} custom-call(s32[3]{0:T(128)S(1)} %pad_add_fusion.pos.refs_0_, bf16[4,18,192,256]{3,2,1,0:T(8,128)(2,1)S(1)} %get-tuple-element.42.after.xs, bf16[6,768,128]{2,1,0:T(8,128)(2,1)S(1)} %get-tuple-element.43.g, bf16[6,768,128]{2,1,0:T(8,128)(2,1)S(1)} %collective-permute-done.12.s, ...), custom_call_target="tpu_custom_call" | custom-call | flops 5435817984 | bytes 11108352 | tf_op jit(solution)/shard_map/taps/pallas_call | solution.py:116
  70.8 0.9 code.1
  71.8 1.8 %collective-permute-start.18 = (bf16[1360,128]{1,0:T(8,128)(2,1)S(1)}, bf16[1360,128]{1,0:T(8,128)(2,1)S(1)}, u32[]{:S(2)}, u32[]{:S(2)}) collective-permute-start(bf16[1360,128]{1,0:T(8,128)(2,1)S(1)} %get-tuple-element.47), channel_id=1, source_target_pairs={{0,3},{1,0},{2,1},{3,2},{4,7},{5,4},{6,5},{7,6},{8,11},{9,8},{10,9... | collective-permute-start | bytes 1044488 | tf_op jit(solution)/shard_map/ppermute | solution.py:98
  73.8 1.6 %collective-permute-start.21 = (bf16[1744,128]{1,0:T(8,128)(2,1)S(1)}, bf16[1744,128]{1,0:T(8,128)(2,1)S(1)}, u32[]{:S(2)}, u32[]{:S(2)}) collective-permute-start(bf16[1744,128]{1,0:T(8,128)(2,1)S(1)} %get-tuple-element.46.after.own.refs_1_), channel_id=1, source_target_pairs={{0,12},{1,13},{2,14},{3,15},{4,8},{5,9},{6,10},{7,11},{8,4},{9,5},... | collective-permute-start | bytes 1339400 | tf_op jit(solution)/shard_map/ppermute | solution.py:98
  75.4 1.2 collective-permute-start.20
  76.6 1.1 collective-permute-start.19
  77.7 11.4 %field.1.after = bf16[4,4,48,256]{3,2,1,0:T(8,128)(2,1)} custom-call(s32[3]{0:T(128)S(1)} %pad_add_fusion.pos.refs_0_, bf16[1744,128]{1,0:T(8,128)(2,1)S(1)} %get-tuple-element.46.after.own.refs_1_, bf16[4,6,64,256]{3,2,1,0:T(8,128)(2,1)S(1)} %get-tuple-element.45.mine, bf16[4,6,64,256]{3,2,1,0:T(8,128)(2,1)S(1)} %collective-permute-done.16.after.theirs, ...), custom_call_target="tpu_custom_call" | custom-call | flops 10871635968 | bytes 7077888 | tf_op jit(solution)/shard_map/field/pallas_call | solution.py:570
  89.1 1.6 %collective-permute-done.17.west.refs_6_ = bf16[1360,128]{1,0:T(8,128)(2,1)S(1)} collective-permute-done((bf16[1360,128]{1,0:T(8,128)(2,1)S(1)}, bf16[1360,128]{1,0:T(8,128)(2,1)S(1)}, u32[]{:S(2)}, u32[]{:S(2)}) %collective-permute-start.17) | collective-permute-done | bytes 348192 | tf_op jit(solution)/shard_map/ppermute | solution.py:98
  90.6 1.0 copy-done.13
  92.2 1.7 %collective-permute-start.31 = (bf16[2720,128]{1,0:T(8,128)(2,1)S(1)}, bf16[2720,128]{1,0:T(8,128)(2,1)S(1)}, u32[]{:S(2)}, u32[]{:S(2)}) collective-permute-start(bf16[2720,128]{1,0:T(8,128)(2,1)S(1)} %both.1.after.refs_5_), channel_id=1, source_target_pairs={{0,12},{1,13},{2,14},{3,15},{4,8},{5,9},{6,10},{7,11},{8,4},{9,5},... | collective-permute-start | bytes 2088968 | tf_op jit(solution)/shard_map/ppermute | solution.py:98
  93.9 3.1 %collective-permute-done.20.y.refs_3_ = bf16[1744,128]{1,0:T(8,128)(2,1)S(1)} collective-permute-done((bf16[1744,128]{1,0:T(8,128)(2,1)S(1)}, bf16[1744,128]{1,0:T(8,128)(2,1)S(1)}, u32[]{:S(2)}, u32[]{:S(2)}) %collective-permute-start.20) | collective-permute-done | bytes 446496 | tf_op jit(solution)/shard_map/ppermute | solution.py:98
  97.0 1.4 collective-permute-done.19.x.refs_2_
  98.4 0.7 join.1
  99.1 3.6 %collective-permute-start.23 = (bf16[2288,128]{1,0:T(8,128)(2,1)S(1)}, bf16[2288,128]{1,0:T(8,128)(2,1)S(1)}, u32[]{:S(2)}, u32[]{:S(2)}) collective-permute-start(bf16[2288,128]{1,0:T(8,128)(2,1)S(1)} %get-tuple-element.49), channel_id=1, source_target_pairs={{0,3},{1,0},{2,1},{3,2},{4,7},{5,4},{6,5},{7,6},{8,11},{9,8},{10,9... | collective-permute-start | bytes 1757192 | tf_op jit(solution)/shard_map/ppermute | solution.py:98
  102.7 1.1 collective-permute-start.29
  103.8 5.1 %unpack_1.1 = (f32[27,256,512]{2,1,0:T(8,128)}, f32[8,128]{1,0:T(8,128)}) custom-call(s32[3]{0:T(128)} %copy-done.14, bf16[1744,128]{1,0:T(8,128)(2,1)} %copy-done.5, bf16[1744,128]{1,0:T(8,128)(2,1)} %copy-done.8, bf16[1744,128]{1,0:T(8,128)(2,1)} %copy-done.7, bf16[1744,128]{1,0:T(8,128)(2,1)} %copy-done.6, ...), custom_call_target="tpu_custom_call", output_to_operand_aliasing={{0}: (6, {})} | custom-call | bytes 4194304 | tf_op jit(solution)/shard_map/unpack_1/pallas_call | solution.py:402
  108.9 18.6 %collective-permute-done.22.by_3.refs_4_ = bf16[2272,128]{1,0:T(8,128)(2,1)S(1)} collective-permute-done((bf16[2272,128]{1,0:T(8,128)(2,1)S(1)}, bf16[2272,128]{1,0:T(8,128)(2,1)S(1)}, u32[]{:S(2)}, u32[]{:S(2)}) %collective-permute-start.22) | collective-permute-done | bytes 581664 | tf_op jit(solution)/shard_map/ppermute | solution.py:98
  128.8 1.6 %collective-permute-start.28 = (bf16[1360,128]{1,0:T(8,128)(2,1)S(1)}, bf16[1360,128]{1,0:T(8,128)(2,1)S(1)}, u32[]{:S(2)}, u32[]{:S(2)}) collective-permute-start(bf16[1360,128]{1,0:T(8,128)(2,1)S(1)} %get-tuple-element.54.refs_8_.refs_3_), channel_id=1, source_target_pairs={{0,12},{1,13},{2,14},{3,15},{4,8},{5,9},{6,10},{7,11},{8,4},{9,5},... | collective-permute-start | bytes 1044488 | tf_op jit(solution)/shard_map/ppermute | solution.py:98
  130.4 1.3 collective-permute-start.27
  131.7 0.7 collective-permute-start.26
  132.4 1.8 %collective-permute-start.24 = (bf16[800,128]{1,0:T(8,128)(2,1)S(1)}, bf16[800,128]{1,0:T(8,128)(2,1)S(1)}, u32[]{:S(2)}, u32[]{:S(2)}) collective-permute-start(bf16[800,128]{1,0:T(8,128)(2,1)S(1)} %get-tuple-element.52), channel_id=1, source_target_pairs={{0,1},{1,2},{2,3},{3,0},{4,5},{5,6},{6,7},{7,4},{8,9},{9,10},{10,1... | collective-permute-start | bytes 614408 | tf_op jit(solution)/shard_map/ppermute | solution.py:98
  134.2 2.0 %collective-permute-start.25 = (bf16[800,128]{1,0:T(8,128)(2,1)S(1)}, bf16[800,128]{1,0:T(8,128)(2,1)S(1)}, u32[]{:S(2)}, u32[]{:S(2)}) collective-permute-start(bf16[800,128]{1,0:T(8,128)(2,1)S(1)} %get-tuple-element.53), channel_id=1, source_target_pairs={{0,3},{1,0},{2,1},{3,2},{4,7},{5,4},{6,5},{7,6},{8,11},{9,8},{10,9... | collective-permute-start | bytes 614408 | tf_op jit(solution)/shard_map/ppermute | solution.py:98
  136.2 8.4 %unpack_2.1 = (f32[27,256,512]{2,1,0:T(8,128)}, f32[8,128]{1,0:T(8,128)}) custom-call(s32[3]{0:T(128)} %copy-done.14, bf16[2720,128]{1,0:T(8,128)(2,1)} %copy-done.19, bf16[2720,128]{1,0:T(8,128)(2,1)} %copy-done.18, bf16[2720,128]{1,0:T(8,128)(2,1)} %copy-done.17, bf16[2272,128]{1,0:T(8,128)(2,1)} %copy-done.4, ...), custom_call_target="tpu_custom_call", output_to_operand_aliasing={{0}: (9, {})} | custom-call | bytes 4194304 | tf_op jit(solution)/shard_map/unpack_2/pallas_call | solution.py:402
  144.7 0.8 collective-permute-done.27.refs_5_
  145.6 0.7 copy-done.21
  146.4 5.1 %unpack_3.1 = (f32[27,256,512]{2,1,0:T(8,128)}, f32[8,128]{1,0:T(8,128)}) custom-call(s32[3]{0:T(128)} %copy-done.14, bf16[800,128]{1,0:T(8,128)(2,1)} %copy-done.23, bf16[800,128]{1,0:T(8,128)(2,1)} %copy-done.24, bf16[1360,128]{1,0:T(8,128)(2,1)} %copy-done.11, bf16[1360,128]{1,0:T(8,128)(2,1)} %copy-done.22, ...), custom_call_target="tpu_custom_call", output_to_operand_aliasing={{0}: (7, {})} | custom-call | bytes 4194304 | tf_op jit(solution)/shard_map/unpack_3/pallas_call | solution.py:402
  (81 shorter events, 4.2 us)
Async XLA Ops:
  0.7 97.7 %copy-start.14 = (s32[3]{0:T(128)}, s32[3]{0:T(128)S(1)}, u32[]{:S(2)}) copy-start(s32[3]{0:T(128)S(1)} %pad_add_fusion.pos.refs_0_) | copy-start | bytes 40
  0.7 1.0 copy-start.9
  3.6 18.4 %collective-permute-start.3 = (bf16[768,128]{1,0:T(8,128)(2,1)S(1)}, bf16[768,128]{1,0:T(8,128)(2,1)S(1)}, u32[]{:S(2)}, u32[]{:S(2)}) collective-permute-start(bf16[768,128]{1,0:T(8,128)(2,1)S(1)} %get-tuple-element.34), channel_id=1, source_target_pairs={{0,0},{1,1},{2,2},{3,3},{4,4},{5,5},{6,6},{7,7},{8,16},{9,17},{10,... | collective-permute-start | bytes 589832 | tf_op jit(solution)/shard_map/ppermute | solution.py:98
  4.2 17.7 %collective-permute-start.4 = (bf16[768,128]{1,0:T(8,128)(2,1)S(1)}, bf16[768,128]{1,0:T(8,128)(2,1)S(1)}, u32[]{:S(2)}, u32[]{:S(2)}) collective-permute-start(bf16[768,128]{1,0:T(8,128)(2,1)S(1)} %get-tuple-element.35), channel_id=1, source_target_pairs={{0,4},{1,5},{2,6},{3,7},{4,0},{5,1},{6,2},{7,3},{8,20},{9,21},{10,... | collective-permute-start | bytes 589832 | tf_op jit(solution)/shard_map/ppermute | solution.py:98
  7.2 11.7 %collective-permute-start = (bf16[416,128]{1,0:T(8,128)(2,1)S(1)}, bf16[416,128]{1,0:T(8,128)(2,1)S(1)}, u32[]{:S(2)}, u32[]{:S(2)}) collective-permute-start(bf16[416,128]{1,0:T(8,128)(2,1)S(1)} %get-tuple-element.31), channel_id=1, source_target_pairs={{0,1},{1,2},{2,3},{3,0},{4,5},{5,6},{6,7},{7,4},{8,9},{9,10},{10,1... | collective-permute-start | bytes 319496 | tf_op jit(solution)/shard_map/ppermute | solution.py:98
  8.8 10.1 %collective-permute-start.1 = (bf16[384,128]{1,0:T(8,128)(2,1)S(1)}, bf16[384,128]{1,0:T(8,128)(2,1)S(1)}, u32[]{:S(2)}, u32[]{:S(2)}) collective-permute-start(bf16[384,128]{1,0:T(8,128)(2,1)S(1)} %get-tuple-element.32), channel_id=1, source_target_pairs={{0,2},{1,3},{2,0},{3,1},{4,6},{5,7},{6,4},{7,5},{8,10},{9,11},{10,... | collective-permute-start | bytes 294920 | tf_op jit(solution)/shard_map/ppermute | solution.py:98
  11.4 10.6 %collective-permute-start.2 = (bf16[416,128]{1,0:T(8,128)(2,1)S(1)}, bf16[416,128]{1,0:T(8,128)(2,1)S(1)}, u32[]{:S(2)}, u32[]{:S(2)}) collective-permute-start(bf16[416,128]{1,0:T(8,128)(2,1)S(1)} %get-tuple-element.33), channel_id=1, source_target_pairs={{0,3},{1,0},{2,1},{3,2},{4,7},{5,4},{6,5},{7,6},{8,11},{9,8},{10,9... | collective-permute-start | bytes 319496 | tf_op jit(solution)/shard_map/ppermute | solution.py:98
  18.9 7.3 %collective-permute-start.10 = (bf16[384,128]{1,0:T(8,128)(2,1)S(1)}, bf16[384,128]{1,0:T(8,128)(2,1)S(1)}, u32[]{:S(2)}, u32[]{:S(2)}) collective-permute-start(bf16[384,128]{1,0:T(8,128)(2,1)S(1)} %get-tuple-element.39), channel_id=1, source_target_pairs={{0,4},{1,5},{2,6},{3,7},{4,0},{5,1},{6,2},{7,3},{8,12},{9,13},{10,... | collective-permute-start | bytes 294920 | tf_op jit(solution)/shard_map/ppermute | solution.py:98
  18.9 10.1 %collective-permute-start.11 = (bf16[384,128]{1,0:T(8,128)(2,1)S(1)}, bf16[384,128]{1,0:T(8,128)(2,1)S(1)}, u32[]{:S(2)}, u32[]{:S(2)}) collective-permute-start(bf16[384,128]{1,0:T(8,128)(2,1)S(1)} %get-tuple-element.40), channel_id=1, source_target_pairs={{0,12},{1,13},{2,14},{3,15},{4,8},{5,9},{6,10},{7,11},{8,4},{9,5},... | collective-permute-start | bytes 294920 | tf_op jit(solution)/shard_map/ppermute | solution.py:98
  22.7 22.6 %collective-permute-start.7 = (bf16[1600,128]{1,0:T(8,128)(2,1)S(1)}, bf16[1600,128]{1,0:T(8,128)(2,1)S(1)}, u32[]{:S(2)}, u32[]{:S(2)}) collective-permute-start(bf16[1600,128]{1,0:T(8,128)(2,1)S(1)} %get-tuple-element.36.own.x_own), channel_id=1, source_target_pairs={{0,12},{1,13},{2,14},{3,15},{4,8},{5,9},{6,10},{7,11},{8,4},{9,5},... | collective-permute-start | bytes 1228808 | tf_op jit(solution)/shard_map/ppermute | solution.py:98
  22.8 22.5 %collective-permute-start.5 = (bf16[1600,128]{1,0:T(8,128)(2,1)S(1)}, bf16[1600,128]{1,0:T(8,128)(2,1)S(1)}, u32[]{:S(2)}, u32[]{:S(2)}) collective-permute-start(bf16[1600,128]{1,0:T(8,128)(2,1)S(1)} %get-tuple-element.36.own.x_own), channel_id=1, source_target_pairs={{0,4},{1,5},{2,6},{3,7},{4,0},{5,1},{6,2},{7,3},{8,12},{9,13},{10,... | collective-permute-start | bytes 1228808 | tf_op jit(solution)/shard_map/ppermute | solution.py:98
  24.6 18.9 %collective-permute-start.6 = (bf16[1536,128]{1,0:T(8,128)(2,1)S(1)}, bf16[1536,128]{1,0:T(8,128)(2,1)S(1)}, u32[]{:S(2)}, u32[]{:S(2)}) collective-permute-start(bf16[1536,128]{1,0:T(8,128)(2,1)S(1)} %get-tuple-element.37), channel_id=1, source_target_pairs={{0,8},{1,9},{2,10},{3,11},{4,12},{5,13},{6,14},{7,15},{8,0},{9,1},... | collective-permute-start | bytes 1179656 | tf_op jit(solution)/shard_map/ppermute | solution.py:98
  26.2 17.3 %collective-permute-start.9 = (bf16[2,768,128]{2,1,0:T(8,128)(2,1)S(1)}, bf16[2,768,128]{2,1,0:T(8,128)(2,1)S(1)}, u32[]{:S(2)}, u32[]{:S(2)}) collective-permute-start(bf16[2,768,128]{2,1,0:T(8,128)(2,1)S(1)} %get-tuple-element.38.here), channel_id=1, source_target_pairs={{0,3},{1,0},{2,1},{3,2},{4,7},{5,4},{6,5},{7,6},{8,11},{9,8},{10,9... | collective-permute-start | bytes 1179656 | tf_op jit(solution)/shard_map/ppermute | solution.py:98
  29.0 16.3 %collective-permute-start.8 = (bf16[2,768,128]{2,1,0:T(8,128)(2,1)S(1)}, bf16[2,768,128]{2,1,0:T(8,128)(2,1)S(1)}, u32[]{:S(2)}, u32[]{:S(2)}) collective-permute-start(bf16[2,768,128]{2,1,0:T(8,128)(2,1)S(1)} %get-tuple-element.38.here), channel_id=1, source_target_pairs={{0,1},{1,2},{2,3},{3,0},{4,5},{5,6},{6,7},{7,4},{8,9},{9,10},{10,1... | collective-permute-start | bytes 1179656 | tf_op jit(solution)/shard_map/ppermute | solution.py:98
  47.1 15.2 %collective-permute-start.12 = (bf16[6,768,128]{2,1,0:T(8,128)(2,1)S(1)}, bf16[6,768,128]{2,1,0:T(8,128)(2,1)S(1)}, u32[]{:S(2)}, u32[]{:S(2)}) collective-permute-start(bf16[6,768,128]{2,1,0:T(8,128)(2,1)S(1)} %get-tuple-element.43.g), channel_id=1, source_target_pairs={{0,16},{1,17},{2,18},{3,19},{4,20},{5,21},{6,22},{7,23},{8,24},{9,... | collective-permute-start | bytes 3538952 | tf_op jit(solution)/shard_map/ppermute | solution.py:98
  47.2 8.2 %collective-permute-start.14 = (bf16[768,128]{1,0:T(8,128)(2,1)S(1)}, bf16[768,128]{1,0:T(8,128)(2,1)S(1)}, u32[]{:S(2)}, u32[]{:S(2)}) collective-permute-start(bf16[768,128]{1,0:T(8,128)(2,1)S(1)} %get-tuple-element.44), channel_id=1, source_target_pairs={{0,3},{1,0},{2,1},{3,2},{4,7},{5,4},{6,5},{7,6},{8,11},{9,8},{10,9... | collective-permute-start | bytes 589832 | tf_op jit(solution)/shard_map/ppermute | solution.py:98
  50.1 9.8 %collective-permute-start.13 = (bf16[768,128]{1,0:T(8,128)(2,1)S(1)}, bf16[768,128]{1,0:T(8,128)(2,1)S(1)}, u32[]{:S(2)}, u32[]{:S(2)}) collective-permute-start(bf16[768,128]{1,0:T(8,128)(2,1)S(1)} %get-tuple-element.41.after), channel_id=1, source_target_pairs={{0,1},{1,2},{2,3},{3,0},{4,5},{5,6},{6,7},{7,4},{8,9},{9,10},{10,1... | collective-permute-start | bytes 589832 | tf_op jit(solution)/shard_map/ppermute | solution.py:98
  60.5 1.8 %collective-permute-start.15 = (bf16[2,768,128]{2,1,0:T(8,128)(2,1)S(1)}, bf16[2,768,128]{2,1,0:T(8,128)(2,1)S(1)}, u32[]{:S(2)}, u32[]{:S(2)}) collective-permute-start(bf16[2,768,128]{2,1,0:T(8,128)(2,1)S(1)} %pair.1.g2), channel_id=1, source_target_pairs={{0,16},{1,17},{2,18},{3,19},{4,20},{5,21},{6,22},{7,23},{8,24},{9,... | collective-permute-start | bytes 1179656 | tf_op jit(solution)/shard_map/ppermute | solution.py:98
  60.6 10.3 %collective-permute-start.16 = (bf16[4,6,64,256]{3,2,1,0:T(8,128)(2,1)S(1)}, bf16[4,6,64,256]{3,2,1,0:T(8,128)(2,1)S(1)}, u32[]{:S(2)}, u32[]{:S(2)}) collective-permute-start(bf16[4,6,64,256]{3,2,1,0:T(8,128)(2,1)S(1)} %get-tuple-element.45.mine), channel_id=1, source_target_pairs={{0,16},{1,17},{2,18},{3,19},{4,20},{5,21},{6,22},{7,23},{8,24},{9,... | collective-permute-start | bytes 2359304 | tf_op jit(solution)/shard_map/ppermute | solution.py:98
  71.7 26.7 %copy-start.5 = (bf16[1744,128]{1,0:T(8,128)(2,1)}, bf16[1744,128]{1,0:T(8,128)(2,1)S(1)}, u32[]{:S(2)}) copy-start(bf16[1744,128]{1,0:T(8,128)(2,1)S(1)} %get-tuple-element.46.after.own.refs_1_) | copy-start | bytes 1339396
  71.8 17.3 %collective-permute-start.18 = (bf16[1360,128]{1,0:T(8,128)(2,1)S(1)}, bf16[1360,128]{1,0:T(8,128)(2,1)S(1)}, u32[]{:S(2)}, u32[]{:S(2)}) collective-permute-start(bf16[1360,128]{1,0:T(8,128)(2,1)S(1)} %get-tuple-element.47), channel_id=1, source_target_pairs={{0,3},{1,0},{2,1},{3,2},{4,7},{5,4},{6,5},{7,6},{8,11},{9,8},{10,9... | collective-permute-start | bytes 1044488 | tf_op jit(solution)/shard_map/ppermute | solution.py:98
  73.5 17.1 %collective-permute-start.17 = (bf16[1360,128]{1,0:T(8,128)(2,1)S(1)}, bf16[1360,128]{1,0:T(8,128)(2,1)S(1)}, u32[]{:S(2)}, u32[]{:S(2)}) collective-permute-start(bf16[1360,128]{1,0:T(8,128)(2,1)S(1)} %get-tuple-element.47), channel_id=1, source_target_pairs={{0,1},{1,2},{2,3},{3,0},{4,5},{5,6},{6,7},{7,4},{8,9},{9,10},{10,1... | collective-permute-start | bytes 1044488 | tf_op jit(solution)/shard_map/ppermute | solution.py:98
  73.8 20.1 %collective-permute-start.21 = (bf16[1744,128]{1,0:T(8,128)(2,1)S(1)}, bf16[1744,128]{1,0:T(8,128)(2,1)S(1)}, u32[]{:S(2)}, u32[]{:S(2)}) collective-permute-start(bf16[1744,128]{1,0:T(8,128)(2,1)S(1)} %get-tuple-element.46.after.own.refs_1_), channel_id=1, source_target_pairs={{0,12},{1,13},{2,14},{3,15},{4,8},{5,9},{6,10},{7,11},{8,4},{9,5},... | collective-permute-start | bytes 1339400 | tf_op jit(solution)/shard_map/ppermute | solution.py:98
  75.4 21.6 %collective-permute-start.20 = (bf16[1744,128]{1,0:T(8,128)(2,1)S(1)}, bf16[1744,128]{1,0:T(8,128)(2,1)S(1)}, u32[]{:S(2)}, u32[]{:S(2)}) collective-permute-start(bf16[1744,128]{1,0:T(8,128)(2,1)S(1)} %get-tuple-element.46.after.own.refs_1_), channel_id=1, source_target_pairs={{0,8},{1,9},{2,10},{3,11},{4,12},{5,13},{6,14},{7,15},{8,0},{9,1},... | collective-permute-start | bytes 1339400 | tf_op jit(solution)/shard_map/ppermute | solution.py:98
  76.6 21.8 %collective-permute-start.19 = (bf16[1744,128]{1,0:T(8,128)(2,1)S(1)}, bf16[1744,128]{1,0:T(8,128)(2,1)S(1)}, u32[]{:S(2)}, u32[]{:S(2)}) collective-permute-start(bf16[1744,128]{1,0:T(8,128)(2,1)S(1)} %get-tuple-element.46.after.own.refs_1_), channel_id=1, source_target_pairs={{0,4},{1,5},{2,6},{3,7},{4,0},{5,1},{6,2},{7,3},{8,12},{9,13},{10,... | collective-permute-start | bytes 1339400 | tf_op jit(solution)/shard_map/ppermute | solution.py:98
  89.1 47.1 %copy-start.1 = (bf16[1360,128]{1,0:T(8,128)(2,1)}, bf16[1360,128]{1,0:T(8,128)(2,1)S(1)}, u32[]{:S(2)}) copy-start(bf16[1360,128]{1,0:T(8,128)(2,1)S(1)} %collective-permute-done.18.east.refs_7_) | copy-start | bytes 1044484
  91.6 44.6 %copy-start.2 = (bf16[1360,128]{1,0:T(8,128)(2,1)}, bf16[1360,128]{1,0:T(8,128)(2,1)S(1)}, u32[]{:S(2)}) copy-start(bf16[1360,128]{1,0:T(8,128)(2,1)S(1)} %collective-permute-done.17.west.refs_6_) | copy-start | bytes 1044484
  92.2 11.6 %copy-start = (bf16[2720,128]{1,0:T(8,128)(2,1)}, bf16[2720,128]{1,0:T(8,128)(2,1)S(1)}, u32[]{:S(2)}) copy-start(bf16[2720,128]{1,0:T(8,128)(2,1)S(1)} %both.1.after.refs_5_) | copy-start | bytes 2088964
  92.2 39.4 %collective-permute-start.31 = (bf16[2720,128]{1,0:T(8,128)(2,1)S(1)}, bf16[2720,128]{1,0:T(8,128)(2,1)S(1)}, u32[]{:S(2)}, u32[]{:S(2)}) collective-permute-start(bf16[2720,128]{1,0:T(8,128)(2,1)S(1)} %both.1.after.refs_5_), channel_id=1, source_target_pairs={{0,12},{1,13},{2,14},{3,15},{4,8},{5,9},{6,10},{7,11},{8,4},{9,5},... | collective-permute-start | bytes 2088968 | tf_op jit(solution)/shard_map/ppermute | solution.py:98
  93.9 9.9 %copy-start.6 = (bf16[1744,128]{1,0:T(8,128)(2,1)}, bf16[1744,128]{1,0:T(8,128)(2,1)S(1)}, u32[]{:S(2)}) copy-start(bf16[1744,128]{1,0:T(8,128)(2,1)S(1)} %collective-permute-done.21.d.refs_4_) | copy-start | bytes 1339396
  97.0 6.8 %copy-start.7 = (bf16[1744,128]{1,0:T(8,128)(2,1)}, bf16[1744,128]{1,0:T(8,128)(2,1)S(1)}, u32[]{:S(2)}) copy-start(bf16[1744,128]{1,0:T(8,128)(2,1)S(1)} %collective-permute-done.20.y.refs_3_) | copy-start | bytes 1339396
  98.4 5.4 %copy-start.8 = (bf16[1744,128]{1,0:T(8,128)(2,1)}, bf16[1744,128]{1,0:T(8,128)(2,1)S(1)}, u32[]{:S(2)}) copy-start(bf16[1744,128]{1,0:T(8,128)(2,1)S(1)} %collective-permute-done.19.x.refs_2_) | copy-start | bytes 1339396
  99.1 28.4 %copy-start.15 = (s32[3]{0:T(128)S(1)}, s32[3]{0:T(128)}, u32[]{:S(2)}) copy-start(s32[3]{0:T(128)} %copy-done.14) | copy-start | bytes 40
  99.1 28.4 %collective-permute-start.23 = (bf16[2288,128]{1,0:T(8,128)(2,1)S(1)}, bf16[2288,128]{1,0:T(8,128)(2,1)S(1)}, u32[]{:S(2)}, u32[]{:S(2)}) collective-permute-start(bf16[2288,128]{1,0:T(8,128)(2,1)S(1)} %get-tuple-element.49), channel_id=1, source_target_pairs={{0,3},{1,0},{2,1},{3,2},{4,7},{5,4},{6,5},{7,6},{8,11},{9,8},{10,9... | collective-permute-start | bytes 1757192 | tf_op jit(solution)/shard_map/ppermute | solution.py:98
  102.7 24.8 %collective-permute-start.22 = (bf16[2272,128]{1,0:T(8,128)(2,1)S(1)}, bf16[2272,128]{1,0:T(8,128)(2,1)S(1)}, u32[]{:S(2)}, u32[]{:S(2)}) collective-permute-start(bf16[2272,128]{1,0:T(8,128)(2,1)S(1)} %get-tuple-element.48), channel_id=1, source_target_pairs={{0,1},{1,2},{2,3},{3,0},{4,5},{5,6},{6,7},{7,4},{8,9},{9,10},{10,1... | collective-permute-start | bytes 1744904 | tf_op jit(solution)/shard_map/ppermute | solution.py:98
  102.7 29.7 %collective-permute-start.30 = (bf16[2720,128]{1,0:T(8,128)(2,1)S(1)}, bf16[2720,128]{1,0:T(8,128)(2,1)S(1)}, u32[]{:S(2)}, u32[]{:S(2)}) collective-permute-start(bf16[2720,128]{1,0:T(8,128)(2,1)S(1)} %both.1.after.refs_5_), channel_id=1, source_target_pairs={{0,8},{1,9},{2,10},{3,11},{4,12},{5,13},{6,14},{7,15},{8,0},{9,1},... | collective-permute-start | bytes 2088968 | tf_op jit(solution)/shard_map/ppermute | solution.py:98
  102.7 31.4 %collective-permute-start.29 = (bf16[2720,128]{1,0:T(8,128)(2,1)S(1)}, bf16[2720,128]{1,0:T(8,128)(2,1)S(1)}, u32[]{:S(2)}, u32[]{:S(2)}) collective-permute-start(bf16[2720,128]{1,0:T(8,128)(2,1)S(1)} %both.1.after.refs_5_), channel_id=1, source_target_pairs={{0,4},{1,5},{2,6},{3,7},{4,0},{5,1},{6,2},{7,3},{8,12},{9,13},{10,... | collective-permute-start | bytes 2088968 | tf_op jit(solution)/shard_map/ppermute | solution.py:98
  127.5 8.7 %copy-start.4 = (bf16[2272,128]{1,0:T(8,128)(2,1)}, bf16[2272,128]{1,0:T(8,128)(2,1)S(1)}, u32[]{:S(2)}) copy-start(bf16[2272,128]{1,0:T(8,128)(2,1)S(1)} %collective-permute-done.22.by_3.refs_4_) | copy-start | bytes 1744900
  127.5 8.7 %copy-start.3 = (bf16[2288,128]{1,0:T(8,128)(2,1)}, bf16[2288,128]{1,0:T(8,128)(2,1)S(1)}, u32[]{:S(2)}) copy-start(bf16[2288,128]{1,0:T(8,128)(2,1)S(1)} %collective-permute-done.23.by_1.refs_5_) | copy-start | bytes 1757188
  128.8 7.4 %copy-start.11 = (bf16[1360,128]{1,0:T(8,128)(2,1)}, bf16[1360,128]{1,0:T(8,128)(2,1)S(1)}, u32[]{:S(2)}) copy-start(bf16[1360,128]{1,0:T(8,128)(2,1)S(1)} %get-tuple-element.54.refs_8_.refs_3_) | copy-start | bytes 1044484
  128.8 15.9 %collective-permute-start.28 = (bf16[1360,128]{1,0:T(8,128)(2,1)S(1)}, bf16[1360,128]{1,0:T(8,128)(2,1)S(1)}, u32[]{:S(2)}, u32[]{:S(2)}) collective-permute-start(bf16[1360,128]{1,0:T(8,128)(2,1)S(1)} %get-tuple-element.54.refs_8_.refs_3_), channel_id=1, source_target_pairs={{0,12},{1,13},{2,14},{3,15},{4,8},{5,9},{6,10},{7,11},{8,4},{9,5},... | collective-permute-start | bytes 1044488 | tf_op jit(solution)/shard_map/ppermute | solution.py:98
  130.4 15.2 %collective-permute-start.27 = (bf16[1360,128]{1,0:T(8,128)(2,1)S(1)}, bf16[1360,128]{1,0:T(8,128)(2,1)S(1)}, u32[]{:S(2)}, u32[]{:S(2)}) collective-permute-start(bf16[1360,128]{1,0:T(8,128)(2,1)S(1)} %get-tuple-element.54.refs_8_.refs_3_), channel_id=1, source_target_pairs={{0,8},{1,9},{2,10},{3,11},{4,12},{5,13},{6,14},{7,15},{8,0},{9,1},... | collective-permute-start | bytes 1044488 | tf_op jit(solution)/shard_map/ppermute | solution.py:98
  131.7 4.5 %copy-start.17 = (bf16[2720,128]{1,0:T(8,128)(2,1)}, bf16[2720,128]{1,0:T(8,128)(2,1)S(1)}, u32[]{:S(2)}) copy-start(bf16[2720,128]{1,0:T(8,128)(2,1)S(1)} %collective-permute-done.31.refs_3_) | copy-start | bytes 2088964
  131.7 13.9 %collective-permute-start.26 = (bf16[1360,128]{1,0:T(8,128)(2,1)S(1)}, bf16[1360,128]{1,0:T(8,128)(2,1)S(1)}, u32[]{:S(2)}, u32[]{:S(2)}) collective-permute-start(bf16[1360,128]{1,0:T(8,128)(2,1)S(1)} %get-tuple-element.54.refs_8_.refs_3_), channel_id=1, source_target_pairs={{0,4},{1,5},{2,6},{3,7},{4,0},{5,1},{6,2},{7,3},{8,12},{9,13},{10,... | collective-permute-start | bytes 1044488 | tf_op jit(solution)/shard_map/ppermute | solution.py:98
  132.4 3.9 %copy-start.18 = (bf16[2720,128]{1,0:T(8,128)(2,1)}, bf16[2720,128]{1,0:T(8,128)(2,1)S(1)}, u32[]{:S(2)}) copy-start(bf16[2720,128]{1,0:T(8,128)(2,1)S(1)} %collective-permute-done.30.refs_2_) | copy-start | bytes 2088964
  132.4 12.3 %collective-permute-start.24 = (bf16[800,128]{1,0:T(8,128)(2,1)S(1)}, bf16[800,128]{1,0:T(8,128)(2,1)S(1)}, u32[]{:S(2)}, u32[]{:S(2)}) collective-permute-start(bf16[800,128]{1,0:T(8,128)(2,1)S(1)} %get-tuple-element.52), channel_id=1, source_target_pairs={{0,1},{1,2},{2,3},{3,0},{4,5},{5,6},{6,7},{7,4},{8,9},{9,10},{10,1... | collective-permute-start | bytes 614408 | tf_op jit(solution)/shard_map/ppermute | solution.py:98
  134.2 2.1 %copy-start.19 = (bf16[2720,128]{1,0:T(8,128)(2,1)}, bf16[2720,128]{1,0:T(8,128)(2,1)S(1)}, u32[]{:S(2)}) copy-start(bf16[2720,128]{1,0:T(8,128)(2,1)S(1)} %collective-permute-done.29.refs_1_) | copy-start | bytes 2088964
  134.2 10.5 %collective-permute-start.25 = (bf16[800,128]{1,0:T(8,128)(2,1)S(1)}, bf16[800,128]{1,0:T(8,128)(2,1)S(1)}, u32[]{:S(2)}, u32[]{:S(2)}) collective-permute-start(bf16[800,128]{1,0:T(8,128)(2,1)S(1)} %get-tuple-element.53), channel_id=1, source_target_pairs={{0,3},{1,0},{2,1},{3,2},{4,7},{5,4},{6,5},{7,6},{8,11},{9,8},{10,9... | collective-permute-start | bytes 614408 | tf_op jit(solution)/shard_map/ppermute | solution.py:98
  (9 other events, 8.0 us)

commit v11 on v10

--- a/solution.py
+++ b/solution.py
@@ -155,11 +155,9 @@
             out[at * line : (at + 1) * line, :] = facing[:, at * wide : (at + 1) * wide]
 
 
-def spread_kernel(pos, x0, x1, x2, x3, one, two, both, own, own_y):
+def spread_kernel(pos, x0, x1, x2, x3, own, own_y):
     del pos
     many = x0.shape[0]
-    both[0] = one[...]
-    both[1] = two[...]
     for at, piece in enumerate((x0, x1, x2, x3)):
         own[at * many : (at + 1) * many, :] = piece[0:many, :]
         own_y[at * many : (at + 1) * many, :] = piece[0:many, :]
@@ -304,7 +302,7 @@
                 out[(2 - lev_at) * 9 + lat_by * 3 + lon_at] = block[lon_at * span : (lon_at + 1) * span]
 
 
-def code_kernel(pos, held, after, out, late):
+def code_kernel(pos, held, after, out, late, rest):
     del pos, after
     taps, span, filters = held.shape
     most = jnp.abs(held[0])
@@ -314,29 +312,30 @@
     power = jnp.ceil(jnp.log(top) * (1.0 / math.log(2.0))) - 15.0
     unit = jnp.broadcast_to(jnp.exp2(power), (16, filters)).astype(out.dtype).astype(jnp.float32)
     shrink = 1.0 / unit[0:1]
-    skip = out.shape[0] - late.shape[0]
-    for tap in range(27):
+    unit = unit.astype(out.dtype)
+    for tap in range(taps):
         value = held[tap] * shrink
         square = value * value
         code = (square * value * jnp.abs(value)).astype(out.dtype)
-        out[tap * span : (tap + 1) * span, :] = code
-        if tap * span >= skip:
-            late[tap * span - skip : (tap + 1) * span - skip, :] = code
-    out[27 * span :, :] = unit.astype(out.dtype)
-    late[27 * span - skip :, :] = unit.astype(out.dtype)
-
-
-def both_kernel(pos, west, east, after, both):
+        for ref, many in ((out, out.shape[0] - 16), (late, late.shape[0] - 16), (rest, rest.shape[0])):
+            at = tap * span if ref is out else tap * span - (taps * span - many)
+            if 0 <= at < many:
+                ref[at : at + span, :] = code
+    out[out.shape[0] - 16 :, :] = unit
+    late[late.shape[0] - 16 :, :] = unit
+
+
+def both_kernel(pos, west, east, rest, after, both):
     del pos, after
     size = west.shape[0]
     both[0:size, :] = west[...]
-    both[size:, :] = east[...]
-
-
-def join_kernel(pos, west, east, own, x, y, d, after, by_3, by_1):
+    both[size : 2 * size, :] = east[...]
+    both[2 * size :, :] = rest[...]
+
+
+def join_kernel(pos, west, east, own, x, y, d, after, by_3, by_1, *, cut):
     del pos, after
     size = west.shape[0]
-    cut = own.shape[0] - size
     end = own.shape[0] - 16
     half = by_3.shape[0] - 4 * (cut + 16)
     by_3[0:half, :] = west[0:half, :]
@@ -358,9 +357,10 @@
     early_1[...] = by_1[size - half + many :, :]
 
 
-def unpack_kernel(pos, *refs, slabs, count, span, group):
+def unpack_kernel(pos, *refs, slabs, count, span):
     sources = refs[:count]
     total, token, buffers, sems = refs[-4:]
+    slots, group = buffers.shape[:2]
     wide = buffers.shape[-1] // 4
     token[...] = jnp.zeros_like(token)
     parts = []
@@ -372,41 +372,40 @@
         step, first, many, _, _ = parts[at]
         lon_at = pl.multiple_of(lax.rem(pos[2] + step, 4) * span, span)
         return pltpu.make_async_copy(
-            buffers.at[at % 2, pl.ds(0, many)], total.at[pl.ds(first, many), pl.ds(lon_at, span)], sems.at[at % 2]
+            buffers.at[at % slots, pl.ds(0, many)],
+            total.at[pl.ds(first, many), pl.ds(lon_at, span)],
+            sems.at[at % slots],
         )
 
     for at, (_, _, many, skip, pieces) in enumerate(parts):
-        if at >= 2:
-            copy(at - 2).wait()
-        units = [sources[i][j : j + 16, :].astype(jnp.float32)[0:1] for i, _, j in pieces]
-
-        @pl.loop(0, many)
-        def _(tap, pieces=pieces, skip=skip, units=units, at=at):
-            for tag, (which, row, _) in enumerate(pieces):
-                start = pl.multiple_of(row + (skip + tap) * span, 16)
-                code = sources[which][pl.ds(start, span), :].astype(jnp.float32)
-                root = lax.rsqrt(lax.rsqrt(jnp.abs(code))) * units[tag]
-                lanes = pl.ds(pl.multiple_of((pos[1] ^ tag) * wide, wide), wide)
-                buffers[at % 2, tap, :, lanes] = jnp.where(code < 0, -root, root)
-
+        if at >= slots:
+            copy(at - slots).wait()
+        for tag, (which, row, (power_in, power_row)) in enumerate(pieces):
+            unit = sources[power_in][power_row : power_row + 16, :].astype(jnp.float32)[0:1]
+            lanes = pl.ds(pl.multiple_of((pos[1] ^ tag) * wide, wide), wide)
+            for tap in range(many):
+                start = row + (skip + tap) * span
+                code = sources[which][start : start + span, :].astype(jnp.float32)
+                root = lax.rsqrt(lax.rsqrt(jnp.abs(code))) * unit
+                buffers[at % slots, tap, :, lanes] = jnp.where(code < 0, -root, root)
         copy(at).start()
-    for at in range(max(len(parts) - 2, 0), len(parts)):
+    for at in range(max(len(parts) - slots, 0), len(parts)):
         copy(at).wait()
 
 
 def unpack(pos, total, sources, after, slabs, span, name):
-    group = 7
+    slots, group = 4, 3
     wide = total.shape[2]
     ins = (pos, *sources, *after, total)
     token = jax.ShapeDtypeStruct((8, 128), jnp.float32)
     return pl.pallas_call(
-        lambda *refs: unpack_kernel(*refs, slabs=slabs, count=len(sources), span=span, group=group),
+        lambda *refs: unpack_kernel(*refs, slabs=slabs, count=len(sources), span=span),
         out_shape=[jax.ShapeDtypeStruct(total.shape, total.dtype), token],
         in_specs=[pl.BlockSpec(memory_space=SMEM)]
         + [pl.BlockSpec(memory_space=VMEM)] * len(sources)
         + [pl.BlockSpec(memory_space=pl.ANY)] * (len(after) + 1),
         out_specs=[pl.BlockSpec(memory_space=pl.ANY), pl.BlockSpec(memory_space=VMEM)],
-        scratch_shapes=[VMEM((2, group, span, wide), jnp.float32), pltpu.SemaphoreType.DMA((2,))],
+        scratch_shapes=[VMEM((slots, group, span, wide), jnp.float32), pltpu.SemaphoreType.DMA((slots,))],
         input_output_aliases={len(ins) - 1: 0},
         cost_estimate=pl.CostEstimate(flops=0, bytes_accessed=4 * 2**20, transcendentals=0),
         compiler_params=pltpu.CompilerParams(vmem_limit_bytes=54 * 1024 * 1024),
@@ -497,11 +496,13 @@
     by_d = move(rim_d, lat_xor(3))
 
     inner = 4 * many
-    g0, x_own, x_own_y = call(
+    (g0,) = call(
+        pair_kernel, [jax.ShapeDtypeStruct((2, cells, wide), bf16)], (pos, g_s, g_o, x0), [], 0, "pair_0", 16, held=1
+    )
+    x_own, x_own_y = call(
         spread_kernel,
-        [jax.ShapeDtypeStruct((2, cells, wide), bf16)]
-        + [jax.ShapeDtypeStruct((count, 2 * span), bf16) for count in (inner + 4 * edge, inner)],
-        (pos, x0, x_r1, x_r2, x_r3, g_s, g_o),
+        [jax.ShapeDtypeStruct((count, 2 * span), bf16) for count in (inner + 4 * edge, inner)],
+        (pos, x0, x_r1, x_r2, x_r3),
         [],
         0,
         "spread",
@@ -549,11 +550,12 @@
         pair_kernel, [jax.ShapeDtypeStruct((2, cells, wide), bf16)], (pos, g2a, g2b, xs), [], 0, "pair", 16, held=1
     )
     s2 = move(g2, sibling)
-    early = 6
+    early, middle = 9, 17
     cut, end = early * span, 27 * span
     size = end + 16 - cut
     half = size // 32 * 16
     first_rows = cut + 16
+    own_rows = middle * span + 16
     slab = lambda count: jax.ShapeDtypeStruct((count, wide), bf16)
     (grads,) = call(
         taps_kernel,
@@ -564,7 +566,16 @@
         "taps",
         28,
     )
-    own, late = call(code_kernel, [slab(end + 16), slab(size)], (pos, grads, theirs), [], 0, "code", 16, held=1)
+    own, late, rest = call(
+        code_kernel,
+        [slab(own_rows), slab(size), slab(end - middle * span)],
+        (pos, grads, theirs),
+        [],
+        0,
+        "code",
+        16,
+        held=1,
+    )
 
     whole = lambda t: (0, 0, 0, 0)
     field = pl.pallas_call(
@@ -596,9 +607,18 @@
     from_3 = move(late, lon_by(1))
     from_1 = move(late, lon_by(-1))
     plane = [own] + to_plane(own)
-    (pair,) = call(both_kernel, [slab(2 * size)], (pos, from_3, from_1, field), [], 0, "both", 16, held=1)
+    (pair,) = call(
+        both_kernel,
+        [slab(2 * size + end - middle * span)],
+        (pos, from_3, from_1, rest, field),
+        [],
+        0,
+        "both",
+        16,
+        held=1,
+    )
     z_3, z_1 = call(
-        join_kernel,
+        lambda *refs: join_kernel(*refs, cut=cut),
         [slab(half + 4 * first_rows), slab(size - half + 4 * first_rows)],
         (pos, from_3, from_1, *plane, pair),
         [],
@@ -611,12 +631,12 @@
     by_3 = move(z_3, lon_by(1))
     by_1 = move(z_1, lon_by(-1))
     def late_piece(which, row=0):
-        return (which, row, row + size - 16)
+        return (which, row, (which, row + size - 16))
 
     def early_piece(which, row):
-        return (which, row, row + cut)
-
-    slabs = [(0, 0, 27, [(tag, 0, end) for tag in range(4)])]
+        return (which, row, (which, row + cut))
+
+    slabs = [(0, 0, middle, [(tag, 0, (tag, own_rows - 16)) for tag in range(4)])]
     total, token = unpack(pos, total, plane, [pair], slabs, span, "unpack_1")
     from_2, early_3, early_1 = call(
         across_kernel,
@@ -632,13 +652,17 @@
     early_2a = move(early_3, lon_by(1))
     early_2b = move(early_1, lon_by(-1))
 
+    unit = own_rows - 16
     slabs = [
         (3, early, 27 - early, [late_piece(5)] + [late_piece(at) for at in range(3)]),
         (1, early, 27 - early, [late_piece(6)] + [late_piece(at, size) for at in range(3)]),
+        (0, middle, 27 - middle, [(7, 0, (8, unit))] + [(at, 2 * size, (9 + at, unit)) for at in range(3)]),
         (3, 0, early, [early_piece(3, half + tag * first_rows) for tag in range(4)]),
         (1, 0, early, [early_piece(4, size - half + tag * first_rows) for tag in range(4)]),
     ]
-    total, _ = unpack(pos, total, both + [by_3, by_1, from_3, from_1], [from_2], slabs, span, "unpack_2")
+    total, _ = unpack(
+        pos, total, both + [by_3, by_1, from_3, from_1, rest] + plane, [from_2], slabs, span, "unpack_2"
+    )
     slabs = [
         (2, 0, early, [early_piece(tag // 2, tag % 2 * first_rows) for tag in range(4)]),
         (2, early, 27 - early, [late_piece(2 + tag) for tag in range(4)]),

time: 152 us -> 157 us (1.033)
  waiting for transfers between devices: 54.1 us -> 60.5 us
    ppermute x32, waiting for transfers between devices: 54.1 us -> 60.5 us  [move(): return lax.ppermute(x, AXES, pairs)]
    pallas_call x3, Pallas kernels: 18.6 us -> 16.8 us  [unpack(): pl.pallas_call(lambda *refs: unpack_kernel(*refs, slabs=slabs, count=len(...]
    pallas_call x9 -> x10, Pallas kernels: 14.1 us -> 14.7 us  [call(): pl.pallas_call(kernel, out_shape=outs, in_specs=[pl.BlockSpec(memory_spac...]
    unnamed x50 -> x52, local copies, waits for them, and re-layouts: 5.57 us -> 5.83 us
  transfers between devices with their start and end apart: 32 -> 32, of which waited for: 11 -> 9; matrix products, arithmetic and copies ran while one was open for 0% -> 0% of each run, Pallas kernels for 27% -> 26%
where the time goes in v11:
time: 157 us
  waiting for transfers between devices  60.5 us (39%)
  Pallas kernels  47.7 us (30%)
  starting transfers between devices  41.4 us (26%)
  local copies, waits for them, and re-layouts  5.83 us (4%)
    ppermute x32, waiting for transfers between devices, move(): return lax.ppermute(x, AXES, pairs)  60.5 us
    ppermute x32, starting transfers between devices, move(): return lax.ppermute(x, AXES, pairs)  41.4 us
    pallas_call x3, Pallas kernels, unpack(): pl.pallas_call(lambda *refs: unpack_kernel(*refs, slabs=slabs, count=len(...  16.8 us
    pallas_call x10, Pallas kernels, call(): pl.pallas_call(kernel, out_shape=outs, in_specs=[pl.BlockSpec(memory_spac...  14.7 us
    pallas_call x1, Pallas kernels, blocked_body(): pl.pallas_call(field_kernel, out_shape=jax.ShapeDtypeStruct((levels, heig...  11.4 us
    unnamed x52, local copies, waits for them, and re-layouts  5.83 us
    pallas_call x1, Pallas kernels, blocked_body(): pl.pallas_call(lines_kernel, out_shape=[jax.ShapeDtypeStruct((levels, row...  4.86 us
  transfers between devices with their start and end apart: 32, of which 9 were waited for; matrix products, arithmetic and copies ran while one was open for 0% of the time, Pallas kernels for 26%

profile of v11, /device:TPU:0, one launch (start us, length us, event | category | flops | bytes accessed | tf_op | source)
XLA Modules:
  0.0 156.6 jit_solution(15379589554168263046)
XLA Ops:
  0.7 1.0 copy-done.9
  1.7 1.0 copy-done.13
  2.7 0.8 pack.1
  3.6 0.7 collective-permute-start.6
  4.2 3.1 %collective-permute-start = (bf16[416,128]{1,0:T(8,128)(2,1)S(1)}, bf16[416,128]{1,0:T(8,128)(2,1)S(1)}, u32[]{:S(2)}, u32[]{:S(2)}) collective-permute-start(bf16[416,128]{1,0:T(8,128)(2,1)S(1)} %get-tuple-element.31), channel_id=1, source_target_pairs={{0,1},{1,2},{2,3},{3,0},{4,5},{5,6},{6,7},{7,4},{8,9},{9,10},{10,1... | collective-permute-start | bytes 319496 | tf_op jit(solution)/shard_map/ppermute | solution.py:98
  7.3 1.5 collective-permute-start.7
  8.8 2.6 %collective-permute-start.1 = (bf16[384,128]{1,0:T(8,128)(2,1)S(1)}, bf16[384,128]{1,0:T(8,128)(2,1)S(1)}, u32[]{:S(2)}, u32[]{:S(2)}) collective-permute-start(bf16[384,128]{1,0:T(8,128)(2,1)S(1)} %get-tuple-element.32), channel_id=1, source_target_pairs={{0,2},{1,3},{2,0},{3,1},{4,6},{5,7},{6,4},{7,5},{8,10},{9,11},{10,... | collective-permute-start | bytes 294920 | tf_op jit(solution)/shard_map/ppermute | solution.py:98
  11.4 1.3 collective-permute-start.2
  12.7 5.6 %collective-permute-done.1.x2 = bf16[384,128]{1,0:T(8,128)(2,1)S(1)} collective-permute-done((bf16[384,128]{1,0:T(8,128)(2,1)S(1)}, bf16[384,128]{1,0:T(8,128)(2,1)S(1)}, u32[]{:S(2)}, u32[]{:S(2)}) %collective-permute-start.1) | collective-permute-done | bytes 98336 | tf_op jit(solution)/shard_map/ppermute | solution.py:98
  18.4 2.8 %collective-permute-start.11 = (bf16[384,128]{1,0:T(8,128)(2,1)S(1)}, bf16[384,128]{1,0:T(8,128)(2,1)S(1)}, u32[]{:S(2)}, u32[]{:S(2)}) collective-permute-start(bf16[384,128]{1,0:T(8,128)(2,1)S(1)} %get-tuple-element.39), channel_id=1, source_target_pairs={{0,12},{1,13},{2,14},{3,15},{4,8},{5,9},{6,10},{7,11},{8,4},{9,5},... | collective-permute-start | bytes 294920 | tf_op jit(solution)/shard_map/ppermute | solution.py:98
  21.2 0.6 spread.1
  22.0 2.0 %collective-permute-start.3 = (bf16[1600,128]{1,0:T(8,128)(2,1)S(1)}, bf16[1600,128]{1,0:T(8,128)(2,1)S(1)}, u32[]{:S(2)}, u32[]{:S(2)}) collective-permute-start(bf16[1600,128]{1,0:T(8,128)(2,1)S(1)} %get-tuple-element.34.own.x_own), channel_id=1, source_target_pairs={{0,4},{1,5},{2,6},{3,7},{4,0},{5,1},{6,2},{7,3},{8,12},{9,13},{10,... | collective-permute-start | bytes 1228808 | tf_op jit(solution)/shard_map/ppermute | solution.py:98
  24.1 1.3 collective-permute-start.4
  26.0 3.5 %collective-permute-start.9 = (bf16[2,768,128]{2,1,0:T(8,128)(2,1)S(1)}, bf16[2,768,128]{2,1,0:T(8,128)(2,1)S(1)}, u32[]{:S(2)}, u32[]{:S(2)}) collective-permute-start(bf16[2,768,128]{2,1,0:T(8,128)(2,1)S(1)} %pair_0.1.here), channel_id=1, source_target_pairs={{0,3},{1,0},{2,1},{3,2},{4,7},{5,4},{6,5},{7,6},{8,11},{9,8},{10,9... | collective-permute-start | bytes 1179656 | tf_op jit(solution)/shard_map/ppermute | solution.py:98
  29.4 13.6 %collective-permute-done.4.after.x_y = bf16[1536,128]{1,0:T(8,128)(2,1)S(1)} collective-permute-done((bf16[1536,128]{1,0:T(8,128)(2,1)S(1)}, bf16[1536,128]{1,0:T(8,128)(2,1)S(1)}, u32[]{:S(2)}, u32[]{:S(2)}) %collective-permute-start.4) | collective-permute-done | bytes 393248 | tf_op jit(solution)/shard_map/ppermute | solution.py:98
  43.1 2.0 %collective-permute-done.8.west = bf16[2,768,128]{2,1,0:T(8,128)(2,1)S(1)} collective-permute-done((bf16[2,768,128]{2,1,0:T(8,128)(2,1)S(1)}, bf16[2,768,128]{2,1,0:T(8,128)(2,1)S(1)}, u32[]{:S(2)}, u32[]{:S(2)}) %collective-permute-start.8) | collective-permute-done | bytes 393248 | tf_op jit(solution)/shard_map/ppermute | solution.py:98
  45.1 1.0 copy-done.10
  46.1 0.8 split.1
  46.9 3.2 %collective-permute-start.14 = (bf16[768,128]{1,0:T(8,128)(2,1)S(1)}, bf16[768,128]{1,0:T(8,128)(2,1)S(1)}, u32[]{:S(2)}, u32[]{:S(2)}) collective-permute-start(bf16[768,128]{1,0:T(8,128)(2,1)S(1)} %get-tuple-element.43), channel_id=1, source_target_pairs={{0,3},{1,0},{2,1},{3,2},{4,7},{5,4},{6,5},{7,6},{8,11},{9,8},{10,9... | collective-permute-start | bytes 589832 | tf_op jit(solution)/shard_map/ppermute | solution.py:98
  50.1 4.9 %lines.1 = (bf16[4,18,192,256]{3,2,1,0:T(8,128)(2,1)S(1)}, f32[27,256,512]{2,1,0:T(8,128)}) custom-call(s32[3]{0:T(128)S(1)} %pad_add_fusion.pos.refs_0_, bf16[1600,128]{1,0:T(8,128)(2,1)S(1)} %get-tuple-element.34.own.x_own, bf16[1600,128]{1,0:T(8,128)(2,1)S(1)} %collective-permute-done.3.x_x, bf16[1536,128]{1,0:T(8,128)(2,1)S(1)} %collective-permute-done.4.after.x_y, ...), custom_call_target="tpu_custom_call" | custom-call | bytes 1048576 | tf_op jit(solution)/shard_map/lines/pallas_call | solution.py:535
  55.3 4.5 %collective-permute-done.13.one = bf16[768,128]{1,0:T(8,128)(2,1)S(1)} collective-permute-done((bf16[768,128]{1,0:T(8,128)(2,1)S(1)}, bf16[768,128]{1,0:T(8,128)(2,1)S(1)}, u32[]{:S(2)}, u32[]{:S(2)}) %collective-permute-start.13) | collective-permute-done | bytes 196640 | tf_op jit(solution)/shard_map/ppermute | solution.py:98
  59.8 0.6 pair.1.g2
  61.0 1.2 collective-permute-done.15.s2
  62.2 8.6 %taps.1.held = f32[27,64,128]{2,1,0:T(8,128)S(1)} custom-call(s32[3]{0:T(128)S(1)} %pad_add_fusion.pos.refs_0_, bf16[4,18,192,256]{3,2,1,0:T(8,128)(2,1)S(1)} %get-tuple-element.41.after.xs, bf16[6,768,128]{2,1,0:T(8,128)(2,1)S(1)} %get-tuple-element.42.g, bf16[6,768,128]{2,1,0:T(8,128)(2,1)S(1)} %collective-permute-done.12.s, ...), custom_call_target="tpu_custom_call" | custom-call | flops 5435817984 | bytes 11108352 | tf_op jit(solution)/shard_map/taps/pallas_call | solution.py:116
  70.7 0.9 code.1
  71.7 2.0 %collective-permute-start.21 = (bf16[1104,128]{1,0:T(8,128)(2,1)S(1)}, bf16[1104,128]{1,0:T(8,128)(2,1)S(1)}, u32[]{:S(2)}, u32[]{:S(2)}) collective-permute-start(bf16[1104,128]{1,0:T(8,128)(2,1)S(1)} %get-tuple-element.45.after.refs_3_.refs_1_.refs_9_), channel_id=1, source_target_pairs={{0,12},{1,13},{2,14},{3,15},{4,8},{5,9},{6,10},{7,11},{8,4},{9,5},... | collective-permute-start | bytes 847880 | tf_op jit(solution)/shard_map/ppermute | solution.py:98
  74.1 1.1 collective-permute-start.19
  75.2 1.7 %collective-permute-start.18 = (bf16[1168,128]{1,0:T(8,128)(2,1)S(1)}, bf16[1168,128]{1,0:T(8,128)(2,1)S(1)}, u32[]{:S(2)}, u32[]{:S(2)}) collective-permute-start(bf16[1168,128]{1,0:T(8,128)(2,1)S(1)} %get-tuple-element.46), channel_id=1, source_target_pairs={{0,3},{1,0},{2,1},{3,2},{4,7},{5,4},{6,5},{7,6},{8,11},{9,8},{10,9... | collective-permute-start | bytes 897032 | tf_op jit(solution)/shard_map/ppermute | solution.py:98
  77.2 11.4 %field.1.after = bf16[4,4,48,256]{3,2,1,0:T(8,128)(2,1)} custom-call(s32[3]{0:T(128)S(1)} %pad_add_fusion.pos.refs_0_, bf16[1104,128]{1,0:T(8,128)(2,1)S(1)} %get-tuple-element.45.after.refs_3_.refs_1_.refs_9_, bf16[4,6,64,256]{3,2,1,0:T(8,128)(2,1)S(1)} %get-tuple-element.44.mine, bf16[4,6,64,256]{3,2,1,0:T(8,128)(2,1)S(1)} %collective-permute-done.16.after.theirs, ...), custom_call_target="tpu_custom_call" | custom-call | flops 10871635968 | bytes 7077888 | tf_op jit(solution)/shard_map/field/pallas_call | solution.py:581
  88.6 2.4 %collective-permute-done.17.west.refs_1_.refs_6_ = bf16[1168,128]{1,0:T(8,128)(2,1)S(1)} collective-permute-done((bf16[1168,128]{1,0:T(8,128)(2,1)S(1)}, bf16[1168,128]{1,0:T(8,128)(2,1)S(1)}, u32[]{:S(2)}, u32[]{:S(2)}) %collective-permute-start.17) | collective-permute-done | bytes 299040 | tf_op jit(solution)/shard_map/ppermute | solution.py:98
  91.1 1.1 copy-done.14
  92.2 0.6 both.1.refs_7_.refs_5_
  92.8 2.4 %collective-permute-start.31 = (bf16[2976,128]{1,0:T(8,128)(2,1)S(1)}, bf16[2976,128]{1,0:T(8,128)(2,1)S(1)}, u32[]{:S(2)}, u32[]{:S(2)}) collective-permute-start(bf16[2976,128]{1,0:T(8,128)(2,1)S(1)} %both.1.refs_7_.refs_5_), channel_id=1, source_target_pairs={{0,12},{1,13},{2,14},{3,15},{4,8},{5,9},{6,10},{7,11},{8,4},{9,5},... | collective-permute-start | bytes 2285576 | tf_op jit(solution)/shard_map/ppermute | solution.py:98
  95.2 0.6 join.1
  95.9 1.8 %collective-permute-start.23 = (bf16[2960,128]{1,0:T(8,128)(2,1)S(1)}, bf16[2960,128]{1,0:T(8,128)(2,1)S(1)}, u32[]{:S(2)}, u32[]{:S(2)}) collective-permute-start(bf16[2960,128]{1,0:T(8,128)(2,1)S(1)} %get-tuple-element.49), channel_id=1, source_target_pairs={{0,3},{1,0},{2,1},{3,2},{4,7},{5,4},{6,5},{7,6},{8,11},{9,8},{10,9... | collective-permute-start | bytes 2273288 | tf_op jit(solution)/shard_map/ppermute | solution.py:98
  98.0 0.8 collective-permute-start.29
  99.2 3.6 %unpack_1.1 = (f32[27,256,512]{2,1,0:T(8,128)}, f32[8,128]{1,0:T(8,128)}) custom-call(s32[3]{0:T(128)} %copy-done.15, bf16[1104,128]{1,0:T(8,128)(2,1)} %copy-done.5, bf16[1104,128]{1,0:T(8,128)(2,1)} %copy-done.8, bf16[1104,128]{1,0:T(8,128)(2,1)} %copy-done.7, bf16[1104,128]{1,0:T(8,128)(2,1)} %copy-done.6, ...), custom_call_target="tpu_custom_call", output_to_operand_aliasing={{0}: (6, {})} | custom-call | bytes 4194304 | tf_op jit(solution)/shard_map/unpack_1/pallas_call | solution.py:401
  102.8 28.5 %collective-permute-done.22.by_3.refs_4_ = bf16[2944,128]{1,0:T(8,128)(2,1)S(1)} collective-permute-done((bf16[2944,128]{1,0:T(8,128)(2,1)S(1)}, bf16[2944,128]{1,0:T(8,128)(2,1)S(1)}, u32[]{:S(2)}, u32[]{:S(2)}) %collective-permute-start.22) | collective-permute-done | bytes 753696 | tf_op jit(solution)/shard_map/ppermute | solution.py:98
  131.3 0.7 copy-done.17
  132.0 0.6 across.1
  132.6 0.8 collective-permute-start.24
  133.4 3.1 %collective-permute-start.25 = (bf16[1184,128]{1,0:T(8,128)(2,1)S(1)}, bf16[1184,128]{1,0:T(8,128)(2,1)S(1)}, u32[]{:S(2)}, u32[]{:S(2)}) collective-permute-start(bf16[1184,128]{1,0:T(8,128)(2,1)S(1)} %get-tuple-element.53), channel_id=1, source_target_pairs={{0,3},{1,0},{2,1},{3,2},{4,7},{5,4},{6,5},{7,6},{8,11},{9,8},{10,9... | collective-permute-start | bytes 909320 | tf_op jit(solution)/shard_map/ppermute | solution.py:98
  136.5 0.9 collective-permute-start.28
  137.9 2.1 %collective-permute-start.26 = (bf16[1168,128]{1,0:T(8,128)(2,1)S(1)}, bf16[1168,128]{1,0:T(8,128)(2,1)S(1)}, u32[]{:S(2)}, u32[]{:S(2)}) collective-permute-start(bf16[1168,128]{1,0:T(8,128)(2,1)S(1)} %get-tuple-element.54.refs_13_.refs_3_), channel_id=1, source_target_pairs={{0,4},{1,5},{2,6},{3,7},{4,0},{5,1},{6,2},{7,3},{8,12},{9,13},{10,... | collective-permute-start | bytes 897032 | tf_op jit(solution)/shard_map/ppermute | solution.py:98
  140.0 8.5 %unpack_2.1 = (f32[27,256,512]{2,1,0:T(8,128)}, f32[8,128]{1,0:T(8,128)}) custom-call(s32[3]{0:T(128)} %copy-done.15, bf16[2976,128]{1,0:T(8,128)(2,1)} %copy-done.20, bf16[2976,128]{1,0:T(8,128)(2,1)} %copy-done.19, bf16[2976,128]{1,0:T(8,128)(2,1)} %copy-done.18, bf16[2944,128]{1,0:T(8,128)(2,1)} %copy-done.2, ...), custom_call_target="tpu_custom_call", output_to_operand_aliasing={{0}: (14, {})} | custom-call | bytes 4194304 | tf_op jit(solution)/shard_map/unpack_2/pallas_call | solution.py:401
  148.6 2.3 %collective-permute-done.27.refs_5_ = bf16[1168,128]{1,0:T(8,128)(2,1)S(1)} collective-permute-done((bf16[1168,128]{1,0:T(8,128)(2,1)S(1)}, bf16[1168,128]{1,0:T(8,128)(2,1)S(1)}, u32[]{:S(2)}, u32[]{:S(2)}) %collective-permute-start.27) | collective-permute-done | bytes 299040 | tf_op jit(solution)/shard_map/ppermute | solution.py:98
  150.9 0.7 copy-done.24
  151.9 4.6 %unpack_3.1 = (f32[27,256,512]{2,1,0:T(8,128)}, f32[8,128]{1,0:T(8,128)}) custom-call(s32[3]{0:T(128)} %copy-done.15, bf16[1184,128]{1,0:T(8,128)(2,1)} %copy-done.21, bf16[1184,128]{1,0:T(8,128)(2,1)} %copy-done.22, bf16[1168,128]{1,0:T(8,128)(2,1)} %copy-done.11, bf16[1168,128]{1,0:T(8,128)(2,1)} %copy-done.25, ...), custom_call_target="tpu_custom_call", output_to_operand_aliasing={{0}: (7, {})} | custom-call | bytes 4194304 | tf_op jit(solution)/shard_map/unpack_3/pallas_call | solution.py:401
  (84 shorter events, 4.3 us)
Async XLA Ops:
  0.7 94.5 %copy-start.15 = (s32[3]{0:T(128)}, s32[3]{0:T(128)S(1)}, u32[]{:S(2)}) copy-start(s32[3]{0:T(128)S(1)} %pad_add_fusion.pos.refs_0_) | copy-start | bytes 40
  3.6 18.5 %collective-permute-start.6 = (bf16[768,128]{1,0:T(8,128)(2,1)S(1)}, bf16[768,128]{1,0:T(8,128)(2,1)S(1)}, u32[]{:S(2)}, u32[]{:S(2)}) collective-permute-start(bf16[768,128]{1,0:T(8,128)(2,1)S(1)} %get-tuple-element.36), channel_id=1, source_target_pairs={{0,0},{1,1},{2,2},{3,3},{4,4},{5,5},{6,6},{7,7},{8,16},{9,17},{10,... | collective-permute-start | bytes 589832 | tf_op jit(solution)/shard_map/ppermute | solution.py:98
  4.2 14.1 %collective-permute-start = (bf16[416,128]{1,0:T(8,128)(2,1)S(1)}, bf16[416,128]{1,0:T(8,128)(2,1)S(1)}, u32[]{:S(2)}, u32[]{:S(2)}) collective-permute-start(bf16[416,128]{1,0:T(8,128)(2,1)S(1)} %get-tuple-element.31), channel_id=1, source_target_pairs={{0,1},{1,2},{2,3},{3,0},{4,5},{5,6},{6,7},{7,4},{8,9},{9,10},{10,1... | collective-permute-start | bytes 319496 | tf_op jit(solution)/shard_map/ppermute | solution.py:98
  7.3 16.7 %collective-permute-start.7 = (bf16[768,128]{1,0:T(8,128)(2,1)S(1)}, bf16[768,128]{1,0:T(8,128)(2,1)S(1)}, u32[]{:S(2)}, u32[]{:S(2)}) collective-permute-start(bf16[768,128]{1,0:T(8,128)(2,1)S(1)} %get-tuple-element.37), channel_id=1, source_target_pairs={{0,4},{1,5},{2,6},{3,7},{4,0},{5,1},{6,2},{7,3},{8,20},{9,21},{10,... | collective-permute-start | bytes 589832 | tf_op jit(solution)/shard_map/ppermute | solution.py:98
  8.8 9.6 %collective-permute-start.1 = (bf16[384,128]{1,0:T(8,128)(2,1)S(1)}, bf16[384,128]{1,0:T(8,128)(2,1)S(1)}, u32[]{:S(2)}, u32[]{:S(2)}) collective-permute-start(bf16[384,128]{1,0:T(8,128)(2,1)S(1)} %get-tuple-element.32), channel_id=1, source_target_pairs={{0,2},{1,3},{2,0},{3,1},{4,6},{5,7},{6,4},{7,5},{8,10},{9,11},{10,... | collective-permute-start | bytes 294920 | tf_op jit(solution)/shard_map/ppermute | solution.py:98
  11.4 9.8 %collective-permute-start.2 = (bf16[416,128]{1,0:T(8,128)(2,1)S(1)}, bf16[416,128]{1,0:T(8,128)(2,1)S(1)}, u32[]{:S(2)}, u32[]{:S(2)}) collective-permute-start(bf16[416,128]{1,0:T(8,128)(2,1)S(1)} %get-tuple-element.33), channel_id=1, source_target_pairs={{0,3},{1,0},{2,1},{3,2},{4,7},{5,4},{6,5},{7,6},{8,11},{9,8},{10,9... | collective-permute-start | bytes 319496 | tf_op jit(solution)/shard_map/ppermute | solution.py:98
  18.4 7.6 %collective-permute-start.10 = (bf16[384,128]{1,0:T(8,128)(2,1)S(1)}, bf16[384,128]{1,0:T(8,128)(2,1)S(1)}, u32[]{:S(2)}, u32[]{:S(2)}) collective-permute-start(bf16[384,128]{1,0:T(8,128)(2,1)S(1)} %get-tuple-element.38), channel_id=1, source_target_pairs={{0,4},{1,5},{2,6},{3,7},{4,0},{5,1},{6,2},{7,3},{8,12},{9,13},{10,... | collective-permute-start | bytes 294920 | tf_op jit(solution)/shard_map/ppermute | solution.py:98
  18.4 11.1 %collective-permute-start.11 = (bf16[384,128]{1,0:T(8,128)(2,1)S(1)}, bf16[384,128]{1,0:T(8,128)(2,1)S(1)}, u32[]{:S(2)}, u32[]{:S(2)}) collective-permute-start(bf16[384,128]{1,0:T(8,128)(2,1)S(1)} %get-tuple-element.39), channel_id=1, source_target_pairs={{0,12},{1,13},{2,14},{3,15},{4,8},{5,9},{6,10},{7,11},{8,4},{9,5},... | collective-permute-start | bytes 294920 | tf_op jit(solution)/shard_map/ppermute | solution.py:98
  21.8 21.2 %collective-permute-start.5 = (bf16[1600,128]{1,0:T(8,128)(2,1)S(1)}, bf16[1600,128]{1,0:T(8,128)(2,1)S(1)}, u32[]{:S(2)}, u32[]{:S(2)}) collective-permute-start(bf16[1600,128]{1,0:T(8,128)(2,1)S(1)} %get-tuple-element.34.own.x_own), channel_id=1, source_target_pairs={{0,12},{1,13},{2,14},{3,15},{4,8},{5,9},{6,10},{7,11},{8,4},{9,5},... | collective-permute-start | bytes 1228808 | tf_op jit(solution)/shard_map/ppermute | solution.py:98
  22.0 21.0 %collective-permute-start.3 = (bf16[1600,128]{1,0:T(8,128)(2,1)S(1)}, bf16[1600,128]{1,0:T(8,128)(2,1)S(1)}, u32[]{:S(2)}, u32[]{:S(2)}) collective-permute-start(bf16[1600,128]{1,0:T(8,128)(2,1)S(1)} %get-tuple-element.34.own.x_own), channel_id=1, source_target_pairs={{0,4},{1,5},{2,6},{3,7},{4,0},{5,1},{6,2},{7,3},{8,12},{9,13},{10,... | collective-permute-start | bytes 1228808 | tf_op jit(solution)/shard_map/ppermute | solution.py:98
  24.1 19.0 %collective-permute-start.4 = (bf16[1536,128]{1,0:T(8,128)(2,1)S(1)}, bf16[1536,128]{1,0:T(8,128)(2,1)S(1)}, u32[]{:S(2)}, u32[]{:S(2)}) collective-permute-start(bf16[1536,128]{1,0:T(8,128)(2,1)S(1)} %get-tuple-element.35), channel_id=1, source_target_pairs={{0,8},{1,9},{2,10},{3,11},{4,12},{5,13},{6,14},{7,15},{8,0},{9,1},... | collective-permute-start | bytes 1179656 | tf_op jit(solution)/shard_map/ppermute | solution.py:98
  26.0 17.1 %collective-permute-start.9 = (bf16[2,768,128]{2,1,0:T(8,128)(2,1)S(1)}, bf16[2,768,128]{2,1,0:T(8,128)(2,1)S(1)}, u32[]{:S(2)}, u32[]{:S(2)}) collective-permute-start(bf16[2,768,128]{2,1,0:T(8,128)(2,1)S(1)} %pair_0.1.here), channel_id=1, source_target_pairs={{0,3},{1,0},{2,1},{3,2},{4,7},{5,4},{6,5},{7,6},{8,11},{9,8},{10,9... | collective-permute-start | bytes 1179656 | tf_op jit(solution)/shard_map/ppermute | solution.py:98
  29.4 15.6 %collective-permute-start.8 = (bf16[2,768,128]{2,1,0:T(8,128)(2,1)S(1)}, bf16[2,768,128]{2,1,0:T(8,128)(2,1)S(1)}, u32[]{:S(2)}, u32[]{:S(2)}) collective-permute-start(bf16[2,768,128]{2,1,0:T(8,128)(2,1)S(1)} %pair_0.1.here), channel_id=1, source_target_pairs={{0,1},{1,2},{2,3},{3,0},{4,5},{5,6},{6,7},{7,4},{8,9},{9,10},{10,1... | collective-permute-start | bytes 1179656 | tf_op jit(solution)/shard_map/ppermute | solution.py:98
  46.8 15.3 %collective-permute-start.12 = (bf16[6,768,128]{2,1,0:T(8,128)(2,1)S(1)}, bf16[6,768,128]{2,1,0:T(8,128)(2,1)S(1)}, u32[]{:S(2)}, u32[]{:S(2)}) collective-permute-start(bf16[6,768,128]{2,1,0:T(8,128)(2,1)S(1)} %get-tuple-element.42.g), channel_id=1, source_target_pairs={{0,16},{1,17},{2,18},{3,19},{4,20},{5,21},{6,22},{7,23},{8,24},{9,... | collective-permute-start | bytes 3538952 | tf_op jit(solution)/shard_map/ppermute | solution.py:98
  46.9 8.4 %collective-permute-start.14 = (bf16[768,128]{1,0:T(8,128)(2,1)S(1)}, bf16[768,128]{1,0:T(8,128)(2,1)S(1)}, u32[]{:S(2)}, u32[]{:S(2)}) collective-permute-start(bf16[768,128]{1,0:T(8,128)(2,1)S(1)} %get-tuple-element.43), channel_id=1, source_target_pairs={{0,3},{1,0},{2,1},{3,2},{4,7},{5,4},{6,5},{7,6},{8,11},{9,8},{10,9... | collective-permute-start | bytes 589832 | tf_op jit(solution)/shard_map/ppermute | solution.py:98
  50.1 9.7 %collective-permute-start.13 = (bf16[768,128]{1,0:T(8,128)(2,1)S(1)}, bf16[768,128]{1,0:T(8,128)(2,1)S(1)}, u32[]{:S(2)}, u32[]{:S(2)}) collective-permute-start(bf16[768,128]{1,0:T(8,128)(2,1)S(1)} %get-tuple-element.40.after), channel_id=1, source_target_pairs={{0,1},{1,2},{2,3},{3,0},{4,5},{5,6},{6,7},{7,4},{8,9},{9,10},{10,1... | collective-permute-start | bytes 589832 | tf_op jit(solution)/shard_map/ppermute | solution.py:98
  60.4 1.8 %collective-permute-start.15 = (bf16[2,768,128]{2,1,0:T(8,128)(2,1)S(1)}, bf16[2,768,128]{2,1,0:T(8,128)(2,1)S(1)}, u32[]{:S(2)}, u32[]{:S(2)}) collective-permute-start(bf16[2,768,128]{2,1,0:T(8,128)(2,1)S(1)} %pair.1.g2), channel_id=1, source_target_pairs={{0,16},{1,17},{2,18},{3,19},{4,20},{5,21},{6,22},{7,23},{8,24},{9,... | collective-permute-start | bytes 1179656 | tf_op jit(solution)/shard_map/ppermute | solution.py:98
  60.5 10.3 %collective-permute-start.16 = (bf16[4,6,64,256]{3,2,1,0:T(8,128)(2,1)S(1)}, bf16[4,6,64,256]{3,2,1,0:T(8,128)(2,1)S(1)}, u32[]{:S(2)}, u32[]{:S(2)}) collective-permute-start(bf16[4,6,64,256]{3,2,1,0:T(8,128)(2,1)S(1)} %get-tuple-element.44.mine), channel_id=1, source_target_pairs={{0,16},{1,17},{2,18},{3,19},{4,20},{5,21},{6,22},{7,23},{8,24},{9,... | collective-permute-start | bytes 2359304 | tf_op jit(solution)/shard_map/ppermute | solution.py:98
  71.6 19.4 %copy-start.12 = (bf16[640,128]{1,0:T(8,128)(2,1)}, bf16[640,128]{1,0:T(8,128)(2,1)S(1)}, u32[]{:S(2)}) copy-start(bf16[640,128]{1,0:T(8,128)(2,1)S(1)} %get-tuple-element.47.rest.refs_8_) | copy-start | bytes 491524
  71.7 23.6 %copy-start.5 = (bf16[1104,128]{1,0:T(8,128)(2,1)}, bf16[1104,128]{1,0:T(8,128)(2,1)S(1)}, u32[]{:S(2)}) copy-start(bf16[1104,128]{1,0:T(8,128)(2,1)S(1)} %get-tuple-element.45.after.refs_3_.refs_1_.refs_9_) | copy-start | bytes 847876
  71.7 23.5 %collective-permute-start.21 = (bf16[1104,128]{1,0:T(8,128)(2,1)S(1)}, bf16[1104,128]{1,0:T(8,128)(2,1)S(1)}, u32[]{:S(2)}, u32[]{:S(2)}) collective-permute-start(bf16[1104,128]{1,0:T(8,128)(2,1)S(1)} %get-tuple-element.45.after.refs_3_.refs_1_.refs_9_), channel_id=1, source_target_pairs={{0,12},{1,13},{2,14},{3,15},{4,8},{5,9},{6,10},{7,11},{8,4},{9,5},... | collective-permute-start | bytes 847880 | tf_op jit(solution)/shard_map/ppermute | solution.py:98
  73.6 21.6 %collective-permute-start.20 = (bf16[1104,128]{1,0:T(8,128)(2,1)S(1)}, bf16[1104,128]{1,0:T(8,128)(2,1)S(1)}, u32[]{:S(2)}, u32[]{:S(2)}) collective-permute-start(bf16[1104,128]{1,0:T(8,128)(2,1)S(1)} %get-tuple-element.45.after.refs_3_.refs_1_.refs_9_), channel_id=1, source_target_pairs={{0,8},{1,9},{2,10},{3,11},{4,12},{5,13},{6,14},{7,15},{8,0},{9,1},... | collective-permute-start | bytes 847880 | tf_op jit(solution)/shard_map/ppermute | solution.py:98
  74.1 21.1 %collective-permute-start.19 = (bf16[1104,128]{1,0:T(8,128)(2,1)S(1)}, bf16[1104,128]{1,0:T(8,128)(2,1)S(1)}, u32[]{:S(2)}, u32[]{:S(2)}) collective-permute-start(bf16[1104,128]{1,0:T(8,128)(2,1)S(1)} %get-tuple-element.45.after.refs_3_.refs_1_.refs_9_), channel_id=1, source_target_pairs={{0,4},{1,5},{2,6},{3,7},{4,0},{5,1},{6,2},{7,3},{8,12},{9,13},{10,... | collective-permute-start | bytes 847880 | tf_op jit(solution)/shard_map/ppermute | solution.py:98
  75.2 13.4 %collective-permute-start.18 = (bf16[1168,128]{1,0:T(8,128)(2,1)S(1)}, bf16[1168,128]{1,0:T(8,128)(2,1)S(1)}, u32[]{:S(2)}, u32[]{:S(2)}) collective-permute-start(bf16[1168,128]{1,0:T(8,128)(2,1)S(1)} %get-tuple-element.46), channel_id=1, source_target_pairs={{0,3},{1,0},{2,1},{3,2},{4,7},{5,4},{6,5},{7,6},{8,11},{9,8},{10,9... | collective-permute-start | bytes 897032 | tf_op jit(solution)/shard_map/ppermute | solution.py:98
  76.9 14.1 %collective-permute-start.17 = (bf16[1168,128]{1,0:T(8,128)(2,1)S(1)}, bf16[1168,128]{1,0:T(8,128)(2,1)S(1)}, u32[]{:S(2)}, u32[]{:S(2)}) collective-permute-start(bf16[1168,128]{1,0:T(8,128)(2,1)S(1)} %get-tuple-element.46), channel_id=1, source_target_pairs={{0,1},{1,2},{2,3},{3,0},{4,5},{5,6},{6,7},{7,4},{8,9},{9,10},{10,1... | collective-permute-start | bytes 897032 | tf_op jit(solution)/shard_map/ppermute | solution.py:98
  88.6 51.4 %copy-start.3 = (bf16[1168,128]{1,0:T(8,128)(2,1)}, bf16[1168,128]{1,0:T(8,128)(2,1)S(1)}, u32[]{:S(2)}) copy-start(bf16[1168,128]{1,0:T(8,128)(2,1)S(1)} %collective-permute-done.18.east.refs_2_.refs_7_) | copy-start | bytes 897028
  91.1 48.9 %copy-start.4 = (bf16[1168,128]{1,0:T(8,128)(2,1)}, bf16[1168,128]{1,0:T(8,128)(2,1)S(1)}, u32[]{:S(2)}) copy-start(bf16[1168,128]{1,0:T(8,128)(2,1)S(1)} %collective-permute-done.17.west.refs_1_.refs_6_) | copy-start | bytes 897028
  92.8 6.4 %copy-start = (bf16[2976,128]{1,0:T(8,128)(2,1)}, bf16[2976,128]{1,0:T(8,128)(2,1)S(1)}, u32[]{:S(2)}) copy-start(bf16[2976,128]{1,0:T(8,128)(2,1)S(1)} %both.1.refs_7_.refs_5_) | copy-start | bytes 2285572
  92.8 43.7 %collective-permute-start.31 = (bf16[2976,128]{1,0:T(8,128)(2,1)S(1)}, bf16[2976,128]{1,0:T(8,128)(2,1)S(1)}, u32[]{:S(2)}, u32[]{:S(2)}) collective-permute-start(bf16[2976,128]{1,0:T(8,128)(2,1)S(1)} %both.1.refs_7_.refs_5_), channel_id=1, source_target_pairs={{0,12},{1,13},{2,14},{3,15},{4,8},{5,9},{6,10},{7,11},{8,4},{9,5},... | collective-permute-start | bytes 2285576 | tf_op jit(solution)/shard_map/ppermute | solution.py:98
  95.2 4.0 %copy-start.6 = (bf16[1104,128]{1,0:T(8,128)(2,1)}, bf16[1104,128]{1,0:T(8,128)(2,1)S(1)}, u32[]{:S(2)}) copy-start(bf16[1104,128]{1,0:T(8,128)(2,1)S(1)} %collective-permute-done.21.refs_6_.refs_4_.refs_12_) | copy-start | bytes 847876
  95.2 4.0 %copy-start.7 = (bf16[1104,128]{1,0:T(8,128)(2,1)}, bf16[1104,128]{1,0:T(8,128)(2,1)S(1)}, u32[]{:S(2)}) copy-start(bf16[1104,128]{1,0:T(8,128)(2,1)S(1)} %collective-permute-done.20.refs_5_.refs_3_.refs_11_) | copy-start | bytes 847876
  95.2 3.9 %copy-start.8 = (bf16[1104,128]{1,0:T(8,128)(2,1)}, bf16[1104,128]{1,0:T(8,128)(2,1)S(1)}, u32[]{:S(2)}) copy-start(bf16[1104,128]{1,0:T(8,128)(2,1)S(1)} %collective-permute-done.19.refs_4_.refs_2_.refs_10_) | copy-start | bytes 847876
  95.9 35.4 %copy-start.16 = (s32[3]{0:T(128)S(1)}, s32[3]{0:T(128)}, u32[]{:S(2)}) copy-start(s32[3]{0:T(128)} %copy-done.15) | copy-start | bytes 40
  95.9 35.4 %collective-permute-start.23 = (bf16[2960,128]{1,0:T(8,128)(2,1)S(1)}, bf16[2960,128]{1,0:T(8,128)(2,1)S(1)}, u32[]{:S(2)}, u32[]{:S(2)}) collective-permute-start(bf16[2960,128]{1,0:T(8,128)(2,1)S(1)} %get-tuple-element.49), channel_id=1, source_target_pairs={{0,3},{1,0},{2,1},{3,2},{4,7},{5,4},{6,5},{7,6},{8,11},{9,8},{10,9... | collective-permute-start | bytes 2273288 | tf_op jit(solution)/shard_map/ppermute | solution.py:98
  97.7 39.7 %collective-permute-start.30 = (bf16[2976,128]{1,0:T(8,128)(2,1)S(1)}, bf16[2976,128]{1,0:T(8,128)(2,1)S(1)}, u32[]{:S(2)}, u32[]{:S(2)}) collective-permute-start(bf16[2976,128]{1,0:T(8,128)(2,1)S(1)} %both.1.refs_7_.refs_5_), channel_id=1, source_target_pairs={{0,8},{1,9},{2,10},{3,11},{4,12},{5,13},{6,14},{7,15},{8,0},{9,1},... | collective-permute-start | bytes 2285576 | tf_op jit(solution)/shard_map/ppermute | solution.py:98
  98.0 39.9 %collective-permute-start.29 = (bf16[2976,128]{1,0:T(8,128)(2,1)S(1)}, bf16[2976,128]{1,0:T(8,128)(2,1)S(1)}, u32[]{:S(2)}, u32[]{:S(2)}) collective-permute-start(bf16[2976,128]{1,0:T(8,128)(2,1)S(1)} %both.1.refs_7_.refs_5_), channel_id=1, source_target_pairs={{0,4},{1,5},{2,6},{3,7},{4,0},{5,1},{6,2},{7,3},{8,12},{9,13},{10,... | collective-permute-start | bytes 2285576 | tf_op jit(solution)/shard_map/ppermute | solution.py:98
  98.8 32.5 %collective-permute-start.22 = (bf16[2944,128]{1,0:T(8,128)(2,1)S(1)}, bf16[2944,128]{1,0:T(8,128)(2,1)S(1)}, u32[]{:S(2)}, u32[]{:S(2)}) collective-permute-start(bf16[2944,128]{1,0:T(8,128)(2,1)S(1)} %get-tuple-element.48), channel_id=1, source_target_pairs={{0,1},{1,2},{2,3},{3,0},{4,5},{5,6},{6,7},{7,4},{8,9},{9,10},{10,1... | collective-permute-start | bytes 2261000 | tf_op jit(solution)/shard_map/ppermute | solution.py:98
  131.3 8.7 %copy-start.2 = (bf16[2944,128]{1,0:T(8,128)(2,1)}, bf16[2944,128]{1,0:T(8,128)(2,1)S(1)}, u32[]{:S(2)}) copy-start(bf16[2944,128]{1,0:T(8,128)(2,1)S(1)} %collective-permute-done.22.by_3.refs_4_) | copy-start | bytes 2260996
  131.3 8.7 %copy-start.1 = (bf16[2960,128]{1,0:T(8,128)(2,1)}, bf16[2960,128]{1,0:T(8,128)(2,1)S(1)}, u32[]{:S(2)}) copy-start(bf16[2960,128]{1,0:T(8,128)(2,1)S(1)} %collective-permute-done.23.by_1.refs_5_) | copy-start | bytes 2273284
  132.6 7.4 %copy-start.11 = (bf16[1168,128]{1,0:T(8,128)(2,1)}, bf16[1168,128]{1,0:T(8,128)(2,1)S(1)}, u32[]{:S(2)}) copy-start(bf16[1168,128]{1,0:T(8,128)(2,1)S(1)} %get-tuple-element.54.refs_13_.refs_3_) | copy-start | bytes 897028
  132.6 18.2 %collective-permute-start.24 = (bf16[1184,128]{1,0:T(8,128)(2,1)S(1)}, bf16[1184,128]{1,0:T(8,128)(2,1)S(1)}, u32[]{:S(2)}, u32[]{:S(2)}) collective-permute-start(bf16[1184,128]{1,0:T(8,128)(2,1)S(1)} %get-tuple-element.52), channel_id=1, source_target_pairs={{0,1},{1,2},{2,3},{3,0},{4,5},{5,6},{6,7},{7,4},{8,9},{9,10},{10,1... | collective-permute-start | bytes 909320 | tf_op jit(solution)/shard_map/ppermute | solution.py:98
  133.4 17.4 %collective-permute-start.25 = (bf16[1184,128]{1,0:T(8,128)(2,1)S(1)}, bf16[1184,128]{1,0:T(8,128)(2,1)S(1)}, u32[]{:S(2)}, u32[]{:S(2)}) collective-permute-start(bf16[1184,128]{1,0:T(8,128)(2,1)S(1)} %get-tuple-element.53), channel_id=1, source_target_pairs={{0,3},{1,0},{2,1},{3,2},{4,7},{5,4},{6,5},{7,6},{8,11},{9,8},{10,9... | collective-permute-start | bytes 909320 | tf_op jit(solution)/shard_map/ppermute | solution.py:98
  136.5 3.5 %copy-start.18 = (bf16[2976,128]{1,0:T(8,128)(2,1)}, bf16[2976,128]{1,0:T(8,128)(2,1)S(1)}, u32[]{:S(2)}) copy-start(bf16[2976,128]{1,0:T(8,128)(2,1)S(1)} %collective-permute-done.31.refs_3_) | copy-start | bytes 2285572
  136.5 12.1 %collective-permute-start.28 = (bf16[1168,128]{1,0:T(8,128)(2,1)S(1)}, bf16[1168,128]{1,0:T(8,128)(2,1)S(1)}, u32[]{:S(2)}, u32[]{:S(2)}) collective-permute-start(bf16[1168,128]{1,0:T(8,128)(2,1)S(1)} %get-tuple-element.54.refs_13_.refs_3_), channel_id=1, source_target_pairs={{0,12},{1,13},{2,14},{3,15},{4,8},{5,9},{6,10},{7,11},{8,4},{9,5},... | collective-permute-start | bytes 897032 | tf_op jit(solution)/shard_map/ppermute | solution.py:98
  137.4 2.6 %copy-start.19 = (bf16[2976,128]{1,0:T(8,128)(2,1)}, bf16[2976,128]{1,0:T(8,128)(2,1)S(1)}, u32[]{:S(2)}) copy-start(bf16[2976,128]{1,0:T(8,128)(2,1)S(1)} %collective-permute-done.30.refs_2_) | copy-start | bytes 2285572
  137.4 13.4 %collective-permute-start.27 = (bf16[1168,128]{1,0:T(8,128)(2,1)S(1)}, bf16[1168,128]{1,0:T(8,128)(2,1)S(1)}, u32[]{:S(2)}, u32[]{:S(2)}) collective-permute-start(bf16[1168,128]{1,0:T(8,128)(2,1)S(1)} %get-tuple-element.54.refs_13_.refs_3_), channel_id=1, source_target_pairs={{0,8},{1,9},{2,10},{3,11},{4,12},{5,13},{6,14},{7,15},{8,0},{9,1},... | collective-permute-start | bytes 897032 | tf_op jit(solution)/shard_map/ppermute | solution.py:98
  137.9 12.9 %collective-permute-start.26 = (bf16[1168,128]{1,0:T(8,128)(2,1)S(1)}, bf16[1168,128]{1,0:T(8,128)(2,1)S(1)}, u32[]{:S(2)}, u32[]{:S(2)}) collective-permute-start(bf16[1168,128]{1,0:T(8,128)(2,1)S(1)} %get-tuple-element.54.refs_13_.refs_3_), channel_id=1, source_target_pairs={{0,4},{1,5},{2,6},{3,7},{4,0},{5,1},{6,2},{7,3},{8,12},{9,13},{10,... | collective-permute-start | bytes 897032 | tf_op jit(solution)/shard_map/ppermute | solution.py:98
  148.5 2.3 %copy-start.23 = (bf16[1168,128]{1,0:T(8,128)(2,1)}, bf16[1168,128]{1,0:T(8,128)(2,1)S(1)}, u32[]{:S(2)}) copy-start(bf16[1168,128]{1,0:T(8,128)(2,1)S(1)} %collective-permute-done.28.refs_6_) | copy-start | bytes 897028
  (10 other events, 10.4 us)

commit v12 on v11

--- a/solution.py
+++ b/solution.py
@@ -325,36 +325,33 @@
     late[late.shape[0] - 16 :, :] = unit
 
 
-def both_kernel(pos, west, east, rest, after, both):
+def both_kernel(pos, west, east, rest, after, both, half_3, half_1):
     del pos, after
-    size = west.shape[0]
+    size, half = west.shape[0], half_3.shape[0]
     both[0:size, :] = west[...]
     both[size : 2 * size, :] = east[...]
     both[2 * size :, :] = rest[...]
-
-
-def join_kernel(pos, west, east, own, x, y, d, after, by_3, by_1, *, cut):
+    half_3[...] = west[0:half, :]
+    half_1[...] = east[half:, :]
+
+
+def across_kernel(pos, half_3, half_1, own, x, y, d, late, block):
+    del pos
+    half = half_3.shape[0]
+    late[0:half, :] = half_3[...]
+    late[half:, :] = half_1[...]
+    end = own.shape[0] - 16
+    rows = block.shape[0] // 4
+    for at, piece in enumerate((own, x, y, d)):
+        block[at * rows : (at + 1) * rows - 16, :] = piece[0 : rows - 16, :]
+        block[(at + 1) * rows - 16 : (at + 1) * rows, :] = piece[end:, :]
+
+
+def hand_kernel(pos, block_3, block_1, after, first, second):
     del pos, after
-    size = west.shape[0]
-    end = own.shape[0] - 16
-    half = by_3.shape[0] - 4 * (cut + 16)
-    by_3[0:half, :] = west[0:half, :]
-    by_1[0 : size - half, :] = east[half:, :]
-    for out, at in ((by_3, half), (by_1, size - half)):
-        for piece in (own, x, y, d):
-            out[at : at + cut, :] = piece[0:cut, :]
-            out[at + cut : at + cut + 16, :] = piece[end:, :]
-            at += cut + 16
-
-
-def across_kernel(pos, by_3, by_1, after, late, early_3, early_1):
-    del pos, after
-    size, many = late.shape[0], early_3.shape[0]
-    half = by_3.shape[0] - 2 * many
-    late[0:half, :] = by_3[0:half, :]
-    late[half:, :] = by_1[0 : size - half, :]
-    early_3[...] = by_3[half : half + many, :]
-    early_1[...] = by_1[size - half + many :, :]
+    many = first.shape[0]
+    first[...] = block_3[0:many, :]
+    second[...] = block_1[many:, :]
 
 
 def unpack_kernel(pos, *refs, slabs, count, span):
@@ -408,7 +405,7 @@
         scratch_shapes=[VMEM((slots, group, span, wide), jnp.float32), pltpu.SemaphoreType.DMA((slots,))],
         input_output_aliases={len(ins) - 1: 0},
         cost_estimate=pl.CostEstimate(flops=0, bytes_accessed=4 * 2**20, transcendentals=0),
-        compiler_params=pltpu.CompilerParams(vmem_limit_bytes=54 * 1024 * 1024),
+        compiler_params=pltpu.CompilerParams(vmem_limit_bytes=51 * 1024 * 1024),
         name=name,
     )(*ins)
 
@@ -550,7 +547,7 @@
         pair_kernel, [jax.ShapeDtypeStruct((2, cells, wide), bf16)], (pos, g2a, g2b, xs), [], 0, "pair", 16, held=1
     )
     s2 = move(g2, sibling)
-    early, middle = 9, 17
+    early, middle = 7, 19
     cut, end = early * span, 27 * span
     size = end + 16 - cut
     half = size // 32 * 16
@@ -597,7 +594,7 @@
         cost_estimate=pl.CostEstimate(
             flops=4 * 27 * chans * filters * cells, bytes_accessed=27 * chans * filters * 2, transcendentals=0
         ),
-        compiler_params=pltpu.CompilerParams(vmem_limit_bytes=52 * 1024 * 1024),
+        compiler_params=pltpu.CompilerParams(vmem_limit_bytes=20 * 1024 * 1024),
         name="field",
     )(pos, own, mine, theirs, taps)
 
@@ -607,9 +604,9 @@
     from_3 = move(late, lon_by(1))
     from_1 = move(late, lon_by(-1))
     plane = [own] + to_plane(own)
-    (pair,) = call(
+    pair, half_3, half_1 = call(
         both_kernel,
-        [slab(2 * size + end - middle * span)],
+        [slab(2 * size + end - middle * span), slab(half), slab(size - half)],
         (pos, from_3, from_1, rest, field),
         [],
         0,
@@ -617,19 +614,16 @@
         16,
         held=1,
     )
-    z_3, z_1 = call(
-        lambda *refs: join_kernel(*refs, cut=cut),
-        [slab(half + 4 * first_rows), slab(size - half + 4 * first_rows)],
-        (pos, from_3, from_1, *plane, pair),
-        [],
-        0,
-        "join",
-        16,
-        held=1,
-    )
+    half_3 = move(half_3, lon_by(1))
+    half_1 = move(half_1, lon_by(-1))
     both = to_plane(pair)
-    by_3 = move(z_3, lon_by(1))
-    by_1 = move(z_1, lon_by(-1))
+    from_2, block = call(
+        across_kernel, [slab(size), slab(4 * first_rows)], (pos, half_3, half_1, *plane), [], 0, "across", 16
+    )
+    early_3 = move(block, lon_by(1))
+    early_1 = move(block, lon_by(-1))
+    across = to_plane(from_2)
+
     def late_piece(which, row=0):
         return (which, row, (which, row + size - 16))
 
@@ -637,31 +631,22 @@
         return (which, row, (which, row + cut))
 
     slabs = [(0, 0, middle, [(tag, 0, (tag, own_rows - 16)) for tag in range(4)])]
-    total, token = unpack(pos, total, plane, [pair], slabs, span, "unpack_1")
-    from_2, early_3, early_1 = call(
-        across_kernel,
-        [slab(size), slab(2 * first_rows), slab(2 * first_rows)],
-        (pos, by_3, by_1, token),
-        [],
-        0,
-        "across",
-        16,
-        held=1,
-    )
-    across = to_plane(from_2)
-    early_2a = move(early_3, lon_by(1))
-    early_2b = move(early_1, lon_by(-1))
-
+    total, token = unpack(pos, total, plane, [block], slabs, span, "unpack_1")
+    hand_3, hand_1 = call(
+        hand_kernel, [slab(2 * first_rows)] * 2, (pos, early_3, early_1, token), [], 0, "hand", 16, held=1
+    )
+    early_2a = move(hand_3, lon_by(1))
+    early_2b = move(hand_1, lon_by(-1))
     unit = own_rows - 16
     slabs = [
         (3, early, 27 - early, [late_piece(5)] + [late_piece(at) for at in range(3)]),
         (1, early, 27 - early, [late_piece(6)] + [late_piece(at, size) for at in range(3)]),
         (0, middle, 27 - middle, [(7, 0, (8, unit))] + [(at, 2 * size, (9 + at, unit)) for at in range(3)]),
-        (3, 0, early, [early_piece(3, half + tag * first_rows) for tag in range(4)]),
-        (1, 0, early, [early_piece(4, size - half + tag * first_rows) for tag in range(4)]),
+        (3, 0, early, [early_piece(3, tag * first_rows) for tag in range(4)]),
+        (1, 0, early, [early_piece(4, tag * first_rows) for tag in range(4)]),
     ]
     total, _ = unpack(
-        pos, total, both + [by_3, by_1, from_3, from_1, rest] + plane, [from_2], slabs, span, "unpack_2"
+        pos, total, both + [early_3, early_1, from_3, from_1, rest] + plane, [hand_3], slabs, span, "unpack_2"
     )
     slabs = [
         (2, 0, early, [early_piece(tag // 2, tag % 2 * first_rows) for tag in range(4)]),

time: 157 us -> 147 us (0.936)
  waiting for transfers between devices: 60.5 us -> 51 us
  starting transfers between devices: 41.4 us -> 47.7 us
  Pallas kernels: 47.7 us -> 42.9 us
  local copies, waits for them, and re-layouts: 5.83 us -> 4.01 us
    ppermute x32 -> x34, waiting for transfers between devices: 60.5 us -> 51 us  [move(): return lax.ppermute(x, AXES, pairs)]
    ppermute x32 -> x34, starting transfers between devices: 41.4 us -> 47.7 us  [move(): return lax.ppermute(x, AXES, pairs)]
    pallas_call x3, Pallas kernels: 16.8 us -> 13.9 us  [unpack(): pl.pallas_call(lambda *refs: unpack_kernel(*refs, slabs=slabs, count=len(...]
    pallas_call x1, Pallas kernels: 11.4 us -> 9.52 us  [blocked_body(): pl.pallas_call(field_kernel, out_shape=jax.ShapeDtypeStruct((levels, heig...]
    unnamed x52 -> x20, local copies, waits for them, and re-layouts: 5.83 us -> 4.01 us
  transfers between devices with their start and end apart: 32 -> 34, of which waited for: 9 -> 13; matrix products, arithmetic and copies ran while one was open for 0% -> 0% of each run, Pallas kernels for 26% -> 25%
where the time goes in v12:
time: 147 us
  waiting for transfers between devices  51 us (35%)
  starting transfers between devices  47.7 us (32%)
  Pallas kernels  42.9 us (29%)
  local copies, waits for them, and re-layouts  4.01 us (3%)
    ppermute x34, waiting for transfers between devices, move(): return lax.ppermute(x, AXES, pairs)  51 us
    ppermute x34, starting transfers between devices, move(): return lax.ppermute(x, AXES, pairs)  47.7 us
    pallas_call x10, Pallas kernels, call(): pl.pallas_call(kernel, out_shape=outs, in_specs=[pl.BlockSpec(memory_spac...  14.6 us
    pallas_call x3, Pallas kernels, unpack(): pl.pallas_call(lambda *refs: unpack_kernel(*refs, slabs=slabs, count=len(...  13.9 us
    pallas_call x1, Pallas kernels, blocked_body(): pl.pallas_call(field_kernel, out_shape=jax.ShapeDtypeStruct((levels, heig...  9.52 us
    pallas_call x1, Pallas kernels, blocked_body(): pl.pallas_call(lines_kernel, out_shape=[jax.ShapeDtypeStruct((levels, row...  4.86 us
    unnamed x20, local copies, waits for them, and re-layouts  4.01 us
  transfers between devices with their start and end apart: 34, of which 13 were waited for; matrix products, arithmetic and copies ran while one was open for 0% of the time, Pallas kernels for 25%

profile of v12, /device:TPU:0, one launch (start us, length us, event | category | flops | bytes accessed | tf_op | source)
XLA Modules:
  0.0 146.7 jit_solution(8619475777658844635)
XLA Ops:
  0.7 1.0 copy-done.1
  1.7 1.0 copy-done.3
  2.7 0.8 pack.1
  3.6 0.7 collective-permute-start.6
  4.2 3.1 %collective-permute-start = (bf16[416,128]{1,0:T(8,128)(2,1)S(1)}, bf16[416,128]{1,0:T(8,128)(2,1)S(1)}, u32[]{:S(2)}, u32[]{:S(2)}) collective-permute-start(bf16[416,128]{1,0:T(8,128)(2,1)S(1)} %get-tuple-element.33), channel_id=1, source_target_pairs={{0,1},{1,2},{2,3},{3,0},{4,5},{5,6},{6,7},{7,4},{8,9},{9,10},{10,1... | collective-permute-start | bytes 319496 | tf_op jit(solution)/shard_map/ppermute | solution.py:98
  7.3 1.5 %collective-permute-start.7 = (bf16[768,128]{1,0:T(8,128)(2,1)S(1)}, bf16[768,128]{1,0:T(8,128)(2,1)S(1)}, u32[]{:S(2)}, u32[]{:S(2)}) collective-permute-start(bf16[768,128]{1,0:T(8,128)(2,1)S(1)} %get-tuple-element.39), channel_id=1, source_target_pairs={{0,4},{1,5},{2,6},{3,7},{4,0},{5,1},{6,2},{7,3},{8,20},{9,21},{10,... | collective-permute-start | bytes 589832 | tf_op jit(solution)/shard_map/ppermute | solution.py:98
  8.8 2.6 %collective-permute-start.1 = (bf16[384,128]{1,0:T(8,128)(2,1)S(1)}, bf16[384,128]{1,0:T(8,128)(2,1)S(1)}, u32[]{:S(2)}, u32[]{:S(2)}) collective-permute-start(bf16[384,128]{1,0:T(8,128)(2,1)S(1)} %get-tuple-element.34), channel_id=1, source_target_pairs={{0,2},{1,3},{2,0},{3,1},{4,6},{5,7},{6,4},{7,5},{8,10},{9,11},{10,... | collective-permute-start | bytes 294920 | tf_op jit(solution)/shard_map/ppermute | solution.py:98
  11.4 1.3 collective-permute-start.2
  12.7 5.6 %collective-permute-done.1.x2 = bf16[384,128]{1,0:T(8,128)(2,1)S(1)} collective-permute-done((bf16[384,128]{1,0:T(8,128)(2,1)S(1)}, bf16[384,128]{1,0:T(8,128)(2,1)S(1)}, u32[]{:S(2)}, u32[]{:S(2)}) %collective-permute-start.1) | collective-permute-done | bytes 98336 | tf_op jit(solution)/shard_map/ppermute | solution.py:98
  18.4 2.8 %collective-permute-start.11 = (bf16[384,128]{1,0:T(8,128)(2,1)S(1)}, bf16[384,128]{1,0:T(8,128)(2,1)S(1)}, u32[]{:S(2)}, u32[]{:S(2)}) collective-permute-start(bf16[384,128]{1,0:T(8,128)(2,1)S(1)} %get-tuple-element.41), channel_id=1, source_target_pairs={{0,12},{1,13},{2,14},{3,15},{4,8},{5,9},{6,10},{7,11},{8,4},{9,5},... | collective-permute-start | bytes 294920 | tf_op jit(solution)/shard_map/ppermute | solution.py:98
  21.8 1.2 collective-permute-start.3
  23.0 1.1 collective-permute-start.5
  24.1 1.3 collective-permute-start.4
  26.0 0.7 collective-permute-start.8
  26.7 3.3 %collective-permute-start.9 = (bf16[2,768,128]{2,1,0:T(8,128)(2,1)S(1)}, bf16[2,768,128]{2,1,0:T(8,128)(2,1)S(1)}, u32[]{:S(2)}, u32[]{:S(2)}) collective-permute-start(bf16[2,768,128]{2,1,0:T(8,128)(2,1)S(1)} %pair_0.1.here), channel_id=1, source_target_pairs={{0,3},{1,0},{2,1},{3,2},{4,7},{5,4},{6,5},{7,6},{8,11},{9,8},{10,9... | collective-permute-start | bytes 1179656 | tf_op jit(solution)/shard_map/ppermute | solution.py:98
  29.9 5.2 %collective-permute-done.4.after.x_y = bf16[1536,128]{1,0:T(8,128)(2,1)S(1)} collective-permute-done((bf16[1536,128]{1,0:T(8,128)(2,1)S(1)}, bf16[1536,128]{1,0:T(8,128)(2,1)S(1)}, u32[]{:S(2)}, u32[]{:S(2)}) %collective-permute-start.4) | collective-permute-done | bytes 393248 | tf_op jit(solution)/shard_map/ppermute | solution.py:98
  35.2 8.2 %collective-permute-done.5.x_d = bf16[1600,128]{1,0:T(8,128)(2,1)S(1)} collective-permute-done((bf16[1600,128]{1,0:T(8,128)(2,1)S(1)}, bf16[1600,128]{1,0:T(8,128)(2,1)S(1)}, u32[]{:S(2)}, u32[]{:S(2)}) %collective-permute-start.5) | collective-permute-done | bytes 409632 | tf_op jit(solution)/shard_map/ppermute | solution.py:98
  43.4 1.2 collective-permute-done.9.east
  44.7 1.0 copy-done.2
  45.7 0.8 split.1
  46.5 1.0 collective-permute-start.13
  47.5 2.9 %collective-permute-start.14 = (bf16[768,128]{1,0:T(8,128)(2,1)S(1)}, bf16[768,128]{1,0:T(8,128)(2,1)S(1)}, u32[]{:S(2)}, u32[]{:S(2)}) collective-permute-start(bf16[768,128]{1,0:T(8,128)(2,1)S(1)} %get-tuple-element.45), channel_id=1, source_target_pairs={{0,3},{1,0},{2,1},{3,2},{4,7},{5,4},{6,5},{7,6},{8,11},{9,8},{10,9... | collective-permute-start | bytes 589832 | tf_op jit(solution)/shard_map/ppermute | solution.py:98
  50.4 4.9 %lines.1 = (bf16[4,18,192,256]{3,2,1,0:T(8,128)(2,1)S(1)}, f32[27,256,512]{2,1,0:T(8,128)}) custom-call(s32[3]{0:T(128)S(1)} %pad_add_fusion.pos.refs_0_, bf16[1600,128]{1,0:T(8,128)(2,1)S(1)} %get-tuple-element.36.own.x_own, bf16[1600,128]{1,0:T(8,128)(2,1)S(1)} %collective-permute-done.3.x_x, bf16[1536,128]{1,0:T(8,128)(2,1)S(1)} %collective-permute-done.4.after.x_y, ...), custom_call_target="tpu_custom_call" | custom-call | bytes 1048576 | tf_op jit(solution)/shard_map/lines/pallas_call | solution.py:532
  55.3 0.8 collective-permute-done.13.one
  56.1 2.6 %collective-permute-done.14.two = bf16[768,128]{1,0:T(8,128)(2,1)S(1)} collective-permute-done((bf16[768,128]{1,0:T(8,128)(2,1)S(1)}, bf16[768,128]{1,0:T(8,128)(2,1)S(1)}, u32[]{:S(2)}, u32[]{:S(2)}) %collective-permute-start.14) | collective-permute-done | bytes 196640 | tf_op jit(solution)/shard_map/ppermute | solution.py:98
  59.9 1.2 collective-permute-done.15.s2
  61.1 8.5 %taps.1.held = f32[27,64,128]{2,1,0:T(8,128)S(1)} custom-call(s32[3]{0:T(128)S(1)} %pad_add_fusion.pos.refs_0_, bf16[4,18,192,256]{3,2,1,0:T(8,128)(2,1)S(1)} %get-tuple-element.43.after.xs, bf16[6,768,128]{2,1,0:T(8,128)(2,1)S(1)} %get-tuple-element.44.g, bf16[6,768,128]{2,1,0:T(8,128)(2,1)S(1)} %collective-permute-done.12.s, ...), custom_call_target="tpu_custom_call" | custom-call | flops 5435817984 | bytes 11108352 | tf_op jit(solution)/shard_map/taps/pallas_call | solution.py:116
  69.6 0.9 code.1
  70.5 0.7 collective-permute-start.17
  71.2 3.2 %collective-permute-start.18 = (bf16[1296,128]{1,0:T(8,128)(2,1)S(1)}, bf16[1296,128]{1,0:T(8,128)(2,1)S(1)}, u32[]{:S(2)}, u32[]{:S(2)}) collective-permute-start(bf16[1296,128]{1,0:T(8,128)(2,1)S(1)} %get-tuple-element.48), channel_id=1, source_target_pairs={{0,3},{1,0},{2,1},{3,2},{4,7},{5,4},{6,5},{7,6},{8,11},{9,8},{10,9... | collective-permute-start | bytes 995336 | tf_op jit(solution)/shard_map/ppermute | solution.py:98
  74.4 1.3 collective-permute-start.21
  75.7 1.7 %collective-permute-start.22 = (bf16[1232,128]{1,0:T(8,128)(2,1)S(1)}, bf16[1232,128]{1,0:T(8,128)(2,1)S(1)}, u32[]{:S(2)}, u32[]{:S(2)}) collective-permute-start(bf16[1232,128]{1,0:T(8,128)(2,1)S(1)} %get-tuple-element.47.after.own.refs_1_.refs_9_), channel_id=1, source_target_pairs={{0,8},{1,9},{2,10},{3,11},{4,12},{5,13},{6,14},{7,15},{8,0},{9,1},... | collective-permute-start | bytes 946184 | tf_op jit(solution)/shard_map/ppermute | solution.py:98
  77.9 9.5 %field.1.after = bf16[4,4,48,256]{3,2,1,0:T(8,128)(2,1)} custom-call(s32[3]{0:T(128)S(1)} %pad_add_fusion.pos.refs_0_, bf16[1232,128]{1,0:T(8,128)(2,1)S(1)} %get-tuple-element.47.after.own.refs_1_.refs_9_, bf16[4,6,64,256]{3,2,1,0:T(8,128)(2,1)S(1)} %get-tuple-element.46.mine, bf16[4,6,64,256]{3,2,1,0:T(8,128)(2,1)S(1)} %collective-permute-done.16.after.theirs, ...), custom_call_target="tpu_custom_call" | custom-call | flops 10871635968 | bytes 7077888 | tf_op jit(solution)/shard_map/field/pallas_call | solution.py:578
  87.9 1.0 copy-done.4
  89.5 1.3 collective-permute-start.31
  90.8 1.7 %collective-permute-start.32 = (bf16[3104,128]{1,0:T(8,128)(2,1)S(1)}, bf16[3104,128]{1,0:T(8,128)(2,1)S(1)}, u32[]{:S(2)}, u32[]{:S(2)}) collective-permute-start(bf16[3104,128]{1,0:T(8,128)(2,1)S(1)} %get-tuple-element.58), channel_id=1, source_target_pairs={{0,8},{1,9},{2,10},{3,11},{4,12},{5,13},{6,14},{7,15},{8,0},{9,1},... | collective-permute-start | bytes 2383880 | tf_op jit(solution)/shard_map/ppermute | solution.py:98
  93.1 2.2 %collective-permute-start.20 = (bf16[656,128]{1,0:T(8,128)(2,1)S(1)}, bf16[656,128]{1,0:T(8,128)(2,1)S(1)}, u32[]{:S(2)}, u32[]{:S(2)}) collective-permute-start(bf16[656,128]{1,0:T(8,128)(2,1)S(1)} %get-tuple-element.51), channel_id=1, source_target_pairs={{0,3},{1,0},{2,1},{3,2},{4,7},{5,4},{6,5},{7,6},{8,11},{9,8},{10,9... | collective-permute-start | bytes 503816 | tf_op jit(solution)/shard_map/ppermute | solution.py:98
  95.3 7.8 %collective-permute-done.19.half_3 = bf16[640,128]{1,0:T(8,128)(2,1)S(1)} collective-permute-done((bf16[640,128]{1,0:T(8,128)(2,1)S(1)}, bf16[640,128]{1,0:T(8,128)(2,1)S(1)}, u32[]{:S(2)}, u32[]{:S(2)}) %collective-permute-start.19) | collective-permute-done | bytes 163872 | tf_op jit(solution)/shard_map/ppermute | solution.py:98
  104.0 3.5 %collective-permute-start.25 = (bf16[1856,128]{1,0:T(8,128)(2,1)S(1)}, bf16[1856,128]{1,0:T(8,128)(2,1)S(1)}, u32[]{:S(2)}, u32[]{:S(2)}) collective-permute-start(bf16[1856,128]{1,0:T(8,128)(2,1)S(1)} %get-tuple-element.52.refs_5_), channel_id=1, source_target_pairs={{0,3},{1,0},{2,1},{3,2},{4,7},{5,4},{6,5},{7,6},{8,11},{9,8},{10,9... | collective-permute-start | bytes 1425416 | tf_op jit(solution)/shard_map/ppermute | solution.py:98
  107.6 11.8 %collective-permute-done.24.block_3.refs_4_ = bf16[1856,128]{1,0:T(8,128)(2,1)S(1)} collective-permute-done((bf16[1856,128]{1,0:T(8,128)(2,1)S(1)}, bf16[1856,128]{1,0:T(8,128)(2,1)S(1)}, u32[]{:S(2)}, u32[]{:S(2)}) %collective-permute-start.24) | collective-permute-done | bytes 475168 | tf_op jit(solution)/shard_map/ppermute | solution.py:98
  119.3 1.3 collective-permute-start.28
  120.6 5.0 %collective-permute-done.25.block_1.refs_5_ = bf16[1856,128]{1,0:T(8,128)(2,1)S(1)} collective-permute-done((bf16[1856,128]{1,0:T(8,128)(2,1)S(1)}, bf16[1856,128]{1,0:T(8,128)(2,1)S(1)}, u32[]{:S(2)}, u32[]{:S(2)}) %collective-permute-start.25) | collective-permute-done | bytes 475168 | tf_op jit(solution)/shard_map/ppermute | solution.py:98
  126.1 1.1 collective-permute-start.30
  127.2 2.5 %unpack_1.1 = (f32[27,256,512]{2,1,0:T(8,128)}, f32[8,128]{1,0:T(8,128)S(1)}) custom-call(s32[3]{0:T(128)S(1)} %pad_add_fusion.pos.refs_0_, bf16[1232,128]{1,0:T(8,128)(2,1)S(1)} %get-tuple-element.47.after.own.refs_1_.refs_9_, bf16[1232,128]{1,0:T(8,128)(2,1)S(1)} %collective-permute-done.21.x.refs_2_.refs_10_, ...), custom_call_target="tpu_custom_call", output_to_operand_aliasing={{0}: (6, {})} | custom-call | bytes 4194304 | tf_op jit(solution)/shard_map/unpack_1/pallas_call | solution.py:398
  130.2 1.5 %collective-permute-start.26 = (bf16[928,128]{1,0:T(8,128)(2,1)S(1)}, bf16[928,128]{1,0:T(8,128)(2,1)S(1)}, u32[]{:S(2)}, u32[]{:S(2)}) collective-permute-start(bf16[928,128]{1,0:T(8,128)(2,1)S(1)} %get-tuple-element.55.refs_13_), channel_id=1, source_target_pairs={{0,1},{1,2},{2,3},{3,0},{4,5},{5,6},{6,7},{7,4},{8,9},{9,10},{10,1... | collective-permute-start | bytes 712712 | tf_op jit(solution)/shard_map/ppermute | solution.py:98
  131.8 2.4 %collective-permute-start.27 = (bf16[928,128]{1,0:T(8,128)(2,1)S(1)}, bf16[928,128]{1,0:T(8,128)(2,1)S(1)}, u32[]{:S(2)}, u32[]{:S(2)}) collective-permute-start(bf16[928,128]{1,0:T(8,128)(2,1)S(1)} %get-tuple-element.56), channel_id=1, source_target_pairs={{0,3},{1,0},{2,1},{3,2},{4,7},{5,4},{6,5},{7,6},{8,11},{9,8},{10,9... | collective-permute-start | bytes 712712 | tf_op jit(solution)/shard_map/ppermute | solution.py:98
  134.1 7.6 %unpack_2.1 = (f32[27,256,512]{2,1,0:T(8,128)}, f32[8,128]{1,0:T(8,128)}) custom-call(s32[3]{0:T(128)S(1)} %pad_add_fusion.pos.refs_0_, bf16[3104,128]{1,0:T(8,128)(2,1)} %copy-done.5, bf16[3104,128]{1,0:T(8,128)(2,1)} %copy-done.6, bf16[3104,128]{1,0:T(8,128)(2,1)} %copy-done.7, ...), custom_call_target="tpu_custom_call", output_to_operand_aliasing={{0}: (14, {})} | custom-call | bytes 4194304 | tf_op jit(solution)/shard_map/unpack_2/pallas_call | solution.py:398
  142.7 3.8 %unpack_3.1 = (f32[27,256,512]{2,1,0:T(8,128)}, f32[8,128]{1,0:T(8,128)}) custom-call(s32[3]{0:T(128)S(1)} %pad_add_fusion.pos.refs_0_, bf16[928,128]{1,0:T(8,128)(2,1)S(1)} %collective-permute-done.26.refs_1_, bf16[928,128]{1,0:T(8,128)(2,1)S(1)} %collective-permute-done.27.refs_2_, ...), custom_call_target="tpu_custom_call", output_to_operand_aliasing={{0}: (7, {})} | custom-call | bytes 4194304 | tf_op jit(solution)/shard_map/unpack_3/pallas_call | solution.py:398
  (57 shorter events, 7.5 us)
Async XLA Ops:
  0.7 1.0 copy-start.1
  1.7 1.0 copy-start.3
  3.6 19.4 %collective-permute-start.6 = (bf16[768,128]{1,0:T(8,128)(2,1)S(1)}, bf16[768,128]{1,0:T(8,128)(2,1)S(1)}, u32[]{:S(2)}, u32[]{:S(2)}) collective-permute-start(bf16[768,128]{1,0:T(8,128)(2,1)S(1)} %get-tuple-element.38), channel_id=1, source_target_pairs={{0,0},{1,1},{2,2},{3,3},{4,4},{5,5},{6,6},{7,7},{8,16},{9,17},{10,... | collective-permute-start | bytes 589832 | tf_op jit(solution)/shard_map/ppermute | solution.py:98
  4.2 14.1 %collective-permute-start = (bf16[416,128]{1,0:T(8,128)(2,1)S(1)}, bf16[416,128]{1,0:T(8,128)(2,1)S(1)}, u32[]{:S(2)}, u32[]{:S(2)}) collective-permute-start(bf16[416,128]{1,0:T(8,128)(2,1)S(1)} %get-tuple-element.33), channel_id=1, source_target_pairs={{0,1},{1,2},{2,3},{3,0},{4,5},{5,6},{6,7},{7,4},{8,9},{9,10},{10,1... | collective-permute-start | bytes 319496 | tf_op jit(solution)/shard_map/ppermute | solution.py:98
  7.3 16.7 %collective-permute-start.7 = (bf16[768,128]{1,0:T(8,128)(2,1)S(1)}, bf16[768,128]{1,0:T(8,128)(2,1)S(1)}, u32[]{:S(2)}, u32[]{:S(2)}) collective-permute-start(bf16[768,128]{1,0:T(8,128)(2,1)S(1)} %get-tuple-element.39), channel_id=1, source_target_pairs={{0,4},{1,5},{2,6},{3,7},{4,0},{5,1},{6,2},{7,3},{8,20},{9,21},{10,... | collective-permute-start | bytes 589832 | tf_op jit(solution)/shard_map/ppermute | solution.py:98
  8.8 9.6 %collective-permute-start.1 = (bf16[384,128]{1,0:T(8,128)(2,1)S(1)}, bf16[384,128]{1,0:T(8,128)(2,1)S(1)}, u32[]{:S(2)}, u32[]{:S(2)}) collective-permute-start(bf16[384,128]{1,0:T(8,128)(2,1)S(1)} %get-tuple-element.34), channel_id=1, source_target_pairs={{0,2},{1,3},{2,0},{3,1},{4,6},{5,7},{6,4},{7,5},{8,10},{9,11},{10,... | collective-permute-start | bytes 294920 | tf_op jit(solution)/shard_map/ppermute | solution.py:98
  11.4 9.8 %collective-permute-start.2 = (bf16[416,128]{1,0:T(8,128)(2,1)S(1)}, bf16[416,128]{1,0:T(8,128)(2,1)S(1)}, u32[]{:S(2)}, u32[]{:S(2)}) collective-permute-start(bf16[416,128]{1,0:T(8,128)(2,1)S(1)} %get-tuple-element.35), channel_id=1, source_target_pairs={{0,3},{1,0},{2,1},{3,2},{4,7},{5,4},{6,5},{7,6},{8,11},{9,8},{10,9... | collective-permute-start | bytes 319496 | tf_op jit(solution)/shard_map/ppermute | solution.py:98
  18.4 7.6 %collective-permute-start.10 = (bf16[384,128]{1,0:T(8,128)(2,1)S(1)}, bf16[384,128]{1,0:T(8,128)(2,1)S(1)}, u32[]{:S(2)}, u32[]{:S(2)}) collective-permute-start(bf16[384,128]{1,0:T(8,128)(2,1)S(1)} %get-tuple-element.40), channel_id=1, source_target_pairs={{0,4},{1,5},{2,6},{3,7},{4,0},{5,1},{6,2},{7,3},{8,12},{9,13},{10,... | collective-permute-start | bytes 294920 | tf_op jit(solution)/shard_map/ppermute | solution.py:98
  18.4 8.3 %collective-permute-start.11 = (bf16[384,128]{1,0:T(8,128)(2,1)S(1)}, bf16[384,128]{1,0:T(8,128)(2,1)S(1)}, u32[]{:S(2)}, u32[]{:S(2)}) collective-permute-start(bf16[384,128]{1,0:T(8,128)(2,1)S(1)} %get-tuple-element.41), channel_id=1, source_target_pairs={{0,12},{1,13},{2,14},{3,15},{4,8},{5,9},{6,10},{7,11},{8,4},{9,5},... | collective-permute-start | bytes 294920 | tf_op jit(solution)/shard_map/ppermute | solution.py:98
  21.8 13.4 %collective-permute-start.3 = (bf16[1600,128]{1,0:T(8,128)(2,1)S(1)}, bf16[1600,128]{1,0:T(8,128)(2,1)S(1)}, u32[]{:S(2)}, u32[]{:S(2)}) collective-permute-start(bf16[1600,128]{1,0:T(8,128)(2,1)S(1)} %get-tuple-element.36.own.x_own), channel_id=1, source_target_pairs={{0,4},{1,5},{2,6},{3,7},{4,0},{5,1},{6,2},{7,3},{8,12},{9,13},{10,... | collective-permute-start | bytes 1228808 | tf_op jit(solution)/shard_map/ppermute | solution.py:98
  23.0 20.4 %collective-permute-start.5 = (bf16[1600,128]{1,0:T(8,128)(2,1)S(1)}, bf16[1600,128]{1,0:T(8,128)(2,1)S(1)}, u32[]{:S(2)}, u32[]{:S(2)}) collective-permute-start(bf16[1600,128]{1,0:T(8,128)(2,1)S(1)} %get-tuple-element.36.own.x_own), channel_id=1, source_target_pairs={{0,12},{1,13},{2,14},{3,15},{4,8},{5,9},{6,10},{7,11},{8,4},{9,5},... | collective-permute-start | bytes 1228808 | tf_op jit(solution)/shard_map/ppermute | solution.py:98
  24.1 11.1 %collective-permute-start.4 = (bf16[1536,128]{1,0:T(8,128)(2,1)S(1)}, bf16[1536,128]{1,0:T(8,128)(2,1)S(1)}, u32[]{:S(2)}, u32[]{:S(2)}) collective-permute-start(bf16[1536,128]{1,0:T(8,128)(2,1)S(1)} %get-tuple-element.37), channel_id=1, source_target_pairs={{0,8},{1,9},{2,10},{3,11},{4,12},{5,13},{6,14},{7,15},{8,0},{9,1},... | collective-permute-start | bytes 1179656 | tf_op jit(solution)/shard_map/ppermute | solution.py:98
  26.0 17.5 %collective-permute-start.8 = (bf16[2,768,128]{2,1,0:T(8,128)(2,1)S(1)}, bf16[2,768,128]{2,1,0:T(8,128)(2,1)S(1)}, u32[]{:S(2)}, u32[]{:S(2)}) collective-permute-start(bf16[2,768,128]{2,1,0:T(8,128)(2,1)S(1)} %pair_0.1.here), channel_id=1, source_target_pairs={{0,1},{1,2},{2,3},{3,0},{4,5},{5,6},{6,7},{7,4},{8,9},{9,10},{10,1... | collective-permute-start | bytes 1179656 | tf_op jit(solution)/shard_map/ppermute | solution.py:98
  26.7 18.0 %collective-permute-start.9 = (bf16[2,768,128]{2,1,0:T(8,128)(2,1)S(1)}, bf16[2,768,128]{2,1,0:T(8,128)(2,1)S(1)}, u32[]{:S(2)}, u32[]{:S(2)}) collective-permute-start(bf16[2,768,128]{2,1,0:T(8,128)(2,1)S(1)} %pair_0.1.here), channel_id=1, source_target_pairs={{0,3},{1,0},{2,1},{3,2},{4,7},{5,4},{6,5},{7,6},{8,11},{9,8},{10,9... | collective-permute-start | bytes 1179656 | tf_op jit(solution)/shard_map/ppermute | solution.py:98
  44.7 1.0 copy-start.2
  46.4 14.6 %collective-permute-start.12 = (bf16[6,768,128]{2,1,0:T(8,128)(2,1)S(1)}, bf16[6,768,128]{2,1,0:T(8,128)(2,1)S(1)}, u32[]{:S(2)}, u32[]{:S(2)}) collective-permute-start(bf16[6,768,128]{2,1,0:T(8,128)(2,1)S(1)} %get-tuple-element.44.g), channel_id=1, source_target_pairs={{0,16},{1,17},{2,18},{3,19},{4,20},{5,21},{6,22},{7,23},{8,24},{9,... | collective-permute-start | bytes 3538952 | tf_op jit(solution)/shard_map/ppermute | solution.py:98
  46.5 9.6 %collective-permute-start.13 = (bf16[768,128]{1,0:T(8,128)(2,1)S(1)}, bf16[768,128]{1,0:T(8,128)(2,1)S(1)}, u32[]{:S(2)}, u32[]{:S(2)}) collective-permute-start(bf16[768,128]{1,0:T(8,128)(2,1)S(1)} %get-tuple-element.42.after), channel_id=1, source_target_pairs={{0,1},{1,2},{2,3},{3,0},{4,5},{5,6},{6,7},{7,4},{8,9},{9,10},{10,1... | collective-permute-start | bytes 589832 | tf_op jit(solution)/shard_map/ppermute | solution.py:98
  47.5 11.2 %collective-permute-start.14 = (bf16[768,128]{1,0:T(8,128)(2,1)S(1)}, bf16[768,128]{1,0:T(8,128)(2,1)S(1)}, u32[]{:S(2)}, u32[]{:S(2)}) collective-permute-start(bf16[768,128]{1,0:T(8,128)(2,1)S(1)} %get-tuple-element.45), channel_id=1, source_target_pairs={{0,3},{1,0},{2,1},{3,2},{4,7},{5,4},{6,5},{7,6},{8,11},{9,8},{10,9... | collective-permute-start | bytes 589832 | tf_op jit(solution)/shard_map/ppermute | solution.py:98
  58.7 19.2 %slice-start = ((s8[7077888]{0:T(1024)(128)(4,1)}), s8[4194304]{0:T(1024)(128)(4,1)S(1)}, s32[]{:S(2)}) async-start(s8[7077888]{0:T(1024)(128)(4,1)} %bitcast.12), calls=%async_computation | async-start | bytes 8388608
  59.3 1.8 %collective-permute-start.15 = (bf16[2,768,128]{2,1,0:T(8,128)(2,1)S(1)}, bf16[2,768,128]{2,1,0:T(8,128)(2,1)S(1)}, u32[]{:S(2)}, u32[]{:S(2)}) collective-permute-start(bf16[2,768,128]{2,1,0:T(8,128)(2,1)S(1)} %pair.1.g2), channel_id=1, source_target_pairs={{0,16},{1,17},{2,18},{3,19},{4,20},{5,21},{6,22},{7,23},{8,24},{9,... | collective-permute-start | bytes 1179656 | tf_op jit(solution)/shard_map/ppermute | solution.py:98
  59.4 18.5 %slice-start.1 = ((s8[7077888]{0:T(1024)(128)(4,1)}), s8[2883584]{0:T(1024)(128)(4,1)S(1)}, s32[]{:S(2)}) async-start(s8[7077888]{0:T(1024)(128)(4,1)} %bitcast.12), calls=%async_computation.1 | async-start | bytes 5767168
  59.4 10.2 %collective-permute-start.16 = (bf16[4,6,64,256]{3,2,1,0:T(8,128)(2,1)S(1)}, bf16[4,6,64,256]{3,2,1,0:T(8,128)(2,1)S(1)}, u32[]{:S(2)}, u32[]{:S(2)}) collective-permute-start(bf16[4,6,64,256]{3,2,1,0:T(8,128)(2,1)S(1)} %get-tuple-element.46.mine), channel_id=1, source_target_pairs={{0,16},{1,17},{2,18},{3,19},{4,20},{5,21},{6,22},{7,23},{8,24},{9,... | collective-permute-start | bytes 2359304 | tf_op jit(solution)/shard_map/ppermute | solution.py:98
  70.5 16.9 %collective-permute-start.17 = (bf16[1296,128]{1,0:T(8,128)(2,1)S(1)}, bf16[1296,128]{1,0:T(8,128)(2,1)S(1)}, u32[]{:S(2)}, u32[]{:S(2)}) collective-permute-start(bf16[1296,128]{1,0:T(8,128)(2,1)S(1)} %get-tuple-element.48), channel_id=1, source_target_pairs={{0,1},{1,2},{2,3},{3,0},{4,5},{5,6},{6,7},{7,4},{8,9},{9,10},{10,1... | collective-permute-start | bytes 995336 | tf_op jit(solution)/shard_map/ppermute | solution.py:98
  71.2 16.7 %collective-permute-start.18 = (bf16[1296,128]{1,0:T(8,128)(2,1)S(1)}, bf16[1296,128]{1,0:T(8,128)(2,1)S(1)}, u32[]{:S(2)}, u32[]{:S(2)}) collective-permute-start(bf16[1296,128]{1,0:T(8,128)(2,1)S(1)} %get-tuple-element.48), channel_id=1, source_target_pairs={{0,3},{1,0},{2,1},{3,2},{4,7},{5,4},{6,5},{7,6},{8,11},{9,8},{10,9... | collective-permute-start | bytes 995336 | tf_op jit(solution)/shard_map/ppermute | solution.py:98
  74.4 18.2 %collective-permute-start.21 = (bf16[1232,128]{1,0:T(8,128)(2,1)S(1)}, bf16[1232,128]{1,0:T(8,128)(2,1)S(1)}, u32[]{:S(2)}, u32[]{:S(2)}) collective-permute-start(bf16[1232,128]{1,0:T(8,128)(2,1)S(1)} %get-tuple-element.47.after.own.refs_1_.refs_9_), channel_id=1, source_target_pairs={{0,4},{1,5},{2,6},{3,7},{4,0},{5,1},{6,2},{7,3},{8,12},{9,13},{10,... | collective-permute-start | bytes 946184 | tf_op jit(solution)/shard_map/ppermute | solution.py:98
  75.7 17.4 %collective-permute-start.22 = (bf16[1232,128]{1,0:T(8,128)(2,1)S(1)}, bf16[1232,128]{1,0:T(8,128)(2,1)S(1)}, u32[]{:S(2)}, u32[]{:S(2)}) collective-permute-start(bf16[1232,128]{1,0:T(8,128)(2,1)S(1)} %get-tuple-element.47.after.own.refs_1_.refs_9_), channel_id=1, source_target_pairs={{0,8},{1,9},{2,10},{3,11},{4,12},{5,13},{6,14},{7,15},{8,0},{9,1},... | collective-permute-start | bytes 946184 | tf_op jit(solution)/shard_map/ppermute | solution.py:98
  77.4 17.8 %collective-permute-start.23 = (bf16[1232,128]{1,0:T(8,128)(2,1)S(1)}, bf16[1232,128]{1,0:T(8,128)(2,1)S(1)}, u32[]{:S(2)}, u32[]{:S(2)}) collective-permute-start(bf16[1232,128]{1,0:T(8,128)(2,1)S(1)} %get-tuple-element.47.after.own.refs_1_.refs_9_), channel_id=1, source_target_pairs={{0,12},{1,13},{2,14},{3,15},{4,8},{5,9},{6,10},{7,11},{8,4},{9,5},... | collective-permute-start | bytes 946184 | tf_op jit(solution)/shard_map/ppermute | solution.py:98
  87.9 1.0 copy-start.4
  89.5 36.6 %collective-permute-start.31 = (bf16[3104,128]{1,0:T(8,128)(2,1)S(1)}, bf16[3104,128]{1,0:T(8,128)(2,1)S(1)}, u32[]{:S(2)}, u32[]{:S(2)}) collective-permute-start(bf16[3104,128]{1,0:T(8,128)(2,1)S(1)} %get-tuple-element.58), channel_id=1, source_target_pairs={{0,4},{1,5},{2,6},{3,7},{4,0},{5,1},{6,2},{7,3},{8,12},{9,13},{10,... | collective-permute-start | bytes 2383880 | tf_op jit(solution)/shard_map/ppermute | solution.py:98
  90.8 39.4 %collective-permute-start.32 = (bf16[3104,128]{1,0:T(8,128)(2,1)S(1)}, bf16[3104,128]{1,0:T(8,128)(2,1)S(1)}, u32[]{:S(2)}, u32[]{:S(2)}) collective-permute-start(bf16[3104,128]{1,0:T(8,128)(2,1)S(1)} %get-tuple-element.58), channel_id=1, source_target_pairs={{0,8},{1,9},{2,10},{3,11},{4,12},{5,13},{6,14},{7,15},{8,0},{9,1},... | collective-permute-start | bytes 2383880 | tf_op jit(solution)/shard_map/ppermute | solution.py:98
  92.6 39.2 %collective-permute-start.33 = (bf16[3104,128]{1,0:T(8,128)(2,1)S(1)}, bf16[3104,128]{1,0:T(8,128)(2,1)S(1)}, u32[]{:S(2)}, u32[]{:S(2)}) collective-permute-start(bf16[3104,128]{1,0:T(8,128)(2,1)S(1)} %get-tuple-element.58), channel_id=1, source_target_pairs={{0,12},{1,13},{2,14},{3,15},{4,8},{5,9},{6,10},{7,11},{8,4},{9,5},... | collective-permute-start | bytes 2383880 | tf_op jit(solution)/shard_map/ppermute | solution.py:98
  93.1 10.0 %collective-permute-start.20 = (bf16[656,128]{1,0:T(8,128)(2,1)S(1)}, bf16[656,128]{1,0:T(8,128)(2,1)S(1)}, u32[]{:S(2)}, u32[]{:S(2)}) collective-permute-start(bf16[656,128]{1,0:T(8,128)(2,1)S(1)} %get-tuple-element.51), channel_id=1, source_target_pairs={{0,3},{1,0},{2,1},{3,2},{4,7},{5,4},{6,5},{7,6},{8,11},{9,8},{10,9... | collective-permute-start | bytes 503816 | tf_op jit(solution)/shard_map/ppermute | solution.py:98
  95.3 7.8 %collective-permute-start.19 = (bf16[640,128]{1,0:T(8,128)(2,1)S(1)}, bf16[640,128]{1,0:T(8,128)(2,1)S(1)}, u32[]{:S(2)}, u32[]{:S(2)}) collective-permute-start(bf16[640,128]{1,0:T(8,128)(2,1)S(1)} %get-tuple-element.50), channel_id=1, source_target_pairs={{0,1},{1,2},{2,3},{3,0},{4,5},{5,6},{6,7},{7,4},{8,9},{9,10},{10,1... | collective-permute-start | bytes 491528 | tf_op jit(solution)/shard_map/ppermute | solution.py:98
  103.7 15.7 %collective-permute-start.24 = (bf16[1856,128]{1,0:T(8,128)(2,1)S(1)}, bf16[1856,128]{1,0:T(8,128)(2,1)S(1)}, u32[]{:S(2)}, u32[]{:S(2)}) collective-permute-start(bf16[1856,128]{1,0:T(8,128)(2,1)S(1)} %get-tuple-element.52.refs_5_), channel_id=1, source_target_pairs={{0,1},{1,2},{2,3},{3,0},{4,5},{5,6},{6,7},{7,4},{8,9},{9,10},{10,1... | collective-permute-start | bytes 1425416 | tf_op jit(solution)/shard_map/ppermute | solution.py:98
  104.0 21.6 %collective-permute-start.25 = (bf16[1856,128]{1,0:T(8,128)(2,1)S(1)}, bf16[1856,128]{1,0:T(8,128)(2,1)S(1)}, u32[]{:S(2)}, u32[]{:S(2)}) collective-permute-start(bf16[1856,128]{1,0:T(8,128)(2,1)S(1)} %get-tuple-element.52.refs_5_), channel_id=1, source_target_pairs={{0,3},{1,0},{2,1},{3,2},{4,7},{5,4},{6,5},{7,6},{8,11},{9,8},{10,9... | collective-permute-start | bytes 1425416 | tf_op jit(solution)/shard_map/ppermute | solution.py:98
  119.3 22.4 %collective-permute-start.28 = (bf16[1296,128]{1,0:T(8,128)(2,1)S(1)}, bf16[1296,128]{1,0:T(8,128)(2,1)S(1)}, u32[]{:S(2)}, u32[]{:S(2)}) collective-permute-start(bf16[1296,128]{1,0:T(8,128)(2,1)S(1)} %get-tuple-element.57.refs_3_), channel_id=1, source_target_pairs={{0,4},{1,5},{2,6},{3,7},{4,0},{5,1},{6,2},{7,3},{8,12},{9,13},{10,... | collective-permute-start | bytes 995336 | tf_op jit(solution)/shard_map/ppermute | solution.py:98
  125.6 8.5 %copy-start = (bf16[1856,128]{1,0:T(8,128)(2,1)}, bf16[1856,128]{1,0:T(8,128)(2,1)S(1)}, u32[]{:S(2)}) copy-start(bf16[1856,128]{1,0:T(8,128)(2,1)S(1)} %collective-permute-done.25.block_1.refs_5_) | copy-start | bytes 1425412
  125.6 16.6 %collective-permute-start.29 = (bf16[1296,128]{1,0:T(8,128)(2,1)S(1)}, bf16[1296,128]{1,0:T(8,128)(2,1)S(1)}, u32[]{:S(2)}, u32[]{:S(2)}) collective-permute-start(bf16[1296,128]{1,0:T(8,128)(2,1)S(1)} %get-tuple-element.57.refs_3_), channel_id=1, source_target_pairs={{0,8},{1,9},{2,10},{3,11},{4,12},{5,13},{6,14},{7,15},{8,0},{9,1},... | collective-permute-start | bytes 995336 | tf_op jit(solution)/shard_map/ppermute | solution.py:98
  126.1 8.0 %copy-start.5 = (bf16[3104,128]{1,0:T(8,128)(2,1)}, bf16[3104,128]{1,0:T(8,128)(2,1)S(1)}, u32[]{:S(2)}) copy-start(bf16[3104,128]{1,0:T(8,128)(2,1)S(1)} %collective-permute-done.31.refs_1_) | copy-start | bytes 2383876
  126.1 16.1 %collective-permute-start.30 = (bf16[1296,128]{1,0:T(8,128)(2,1)S(1)}, bf16[1296,128]{1,0:T(8,128)(2,1)S(1)}, u32[]{:S(2)}, u32[]{:S(2)}) collective-permute-start(bf16[1296,128]{1,0:T(8,128)(2,1)S(1)} %get-tuple-element.57.refs_3_), channel_id=1, source_target_pairs={{0,12},{1,13},{2,14},{3,15},{4,8},{5,9},{6,10},{7,11},{8,4},{9,5},... | collective-permute-start | bytes 995336 | tf_op jit(solution)/shard_map/ppermute | solution.py:98
  130.2 3.9 %copy-start.6 = (bf16[3104,128]{1,0:T(8,128)(2,1)}, bf16[3104,128]{1,0:T(8,128)(2,1)S(1)}, u32[]{:S(2)}) copy-start(bf16[3104,128]{1,0:T(8,128)(2,1)S(1)} %collective-permute-done.32.refs_2_) | copy-start | bytes 2383876
  130.2 12.0 %collective-permute-start.26 = (bf16[928,128]{1,0:T(8,128)(2,1)S(1)}, bf16[928,128]{1,0:T(8,128)(2,1)S(1)}, u32[]{:S(2)}, u32[]{:S(2)}) collective-permute-start(bf16[928,128]{1,0:T(8,128)(2,1)S(1)} %get-tuple-element.55.refs_13_), channel_id=1, source_target_pairs={{0,1},{1,2},{2,3},{3,0},{4,5},{5,6},{6,7},{7,4},{8,9},{9,10},{10,1... | collective-permute-start | bytes 712712 | tf_op jit(solution)/shard_map/ppermute | solution.py:98
  131.8 2.4 %copy-start.7 = (bf16[3104,128]{1,0:T(8,128)(2,1)}, bf16[3104,128]{1,0:T(8,128)(2,1)S(1)}, u32[]{:S(2)}) copy-start(bf16[3104,128]{1,0:T(8,128)(2,1)S(1)} %collective-permute-done.33.refs_3_) | copy-start | bytes 2383876
  131.8 10.9 %collective-permute-start.27 = (bf16[928,128]{1,0:T(8,128)(2,1)S(1)}, bf16[928,128]{1,0:T(8,128)(2,1)S(1)}, u32[]{:S(2)}, u32[]{:S(2)}) collective-permute-start(bf16[928,128]{1,0:T(8,128)(2,1)S(1)} %get-tuple-element.56), channel_id=1, source_target_pairs={{0,3},{1,0},{2,1},{3,2},{4,7},{5,4},{6,5},{7,6},{8,11},{9,8},{10,9... | collective-permute-start | bytes 712712 | tf_op jit(solution)/shard_map/ppermute | solution.py:98

commit v13 on v12

--- a/solution.py
+++ b/solution.py
@@ -110,15 +110,16 @@
     return (1 - c, a, o)
 
 
-def call(kernel, outs, ins, scratch, flops, name, limit, held=0):
+def call(kernel, outs, ins, scratch, flops, name, limit, held=0, far=()):
     read = len(ins) - 1 - held
+    spaces = [VMEM] * read + [pl.ANY] * held
+    for at in far:
+        spaces[at - 1] = pl.ANY
     moved = sum(math.prod(x.shape) * x.dtype.itemsize for x in list(ins[1 : 1 + read]) + list(outs))
     return pl.pallas_call(
         kernel,
         out_shape=outs,
-        in_specs=[pl.BlockSpec(memory_space=SMEM)]
-        + [pl.BlockSpec(memory_space=VMEM)] * read
-        + [pl.BlockSpec(memory_space=pl.ANY)] * held,
+        in_specs=[pl.BlockSpec(memory_space=space) for space in [SMEM] + spaces],
         out_specs=[pl.BlockSpec(memory_space=VMEM)] * len(outs),
         scratch_shapes=scratch,
         cost_estimate=pl.CostEstimate(flops=flops, bytes_accessed=moved, transcendentals=0),
@@ -127,13 +128,29 @@
     )(*ins)
 
 
-def pack_kernel(pos, x, g, g_same, g_other, x0, x1, x2, x3, rim_x, rim_d, held):
+def pack_kernel(pos, x_far, g_far, g_same, g_other, x0, x1, x2, x3, rim_x, rim_d, x, g, held, sems):
+    fetch_g = pltpu.make_async_copy(g_far, g, sems.at[0])
+    fetch_x = pltpu.make_async_copy(x_far, x, sems.at[1])
+    fetch_g.start()
+    fetch_x.start()
     levels, height, width, chans = x.shape
     half, wide = levels // 2, chans // 2
     right = lax.rem(pos[1], 2)
+    fetch_g.wait()
     for out, at in ((g_same, right), (g_other, 1 - right)):
         out[...] = g[:, :, :, pl.ds(pl.multiple_of(at * wide, wide), wide)].reshape(out.shape)
     many = x0.shape[0]
+    for out, column in ((x1, width - 1), (x3, 0)):
+        rim = g[:, :, column, :].reshape(levels * height, chans)
+        out[many : many + levels * height, :] = rim[:, 0:wide]
+        out[many + levels * height :, :] = rim[:, wide:]
+    low, high = g[:, 0], g[:, height - 1]
+    line = levels * width
+    for out, upward in ((rim_x, right == 0), (rim_d, right == 1)):
+        facing = jnp.where(upward, high, low).reshape(line, chans)
+        for at in range(2):
+            out[at * line : (at + 1) * line, :] = facing[:, at * wide : (at + 1) * wide]
+    fetch_x.wait()
     for block in range(4):
         at = block * (chans // 4)
         lo = x[0:half, :, :, at : at + chans // 4]
@@ -142,20 +159,9 @@
     lon = pos[2]
     for step, out in enumerate((x0, x1, x2, x3)):
         out[0:many, :] = held[lax.rem(lon + step, 4)]
-    for out, column in ((x1, width - 1), (x3, 0)):
-        rim = g[:, :, column, :].reshape(levels * height, chans)
-        out[many : many + levels * height, :] = rim[:, 0:wide]
-        out[many + levels * height :, :] = rim[:, wide:]
-    even = right == 0
-    low, high = g[:, 0], g[:, height - 1]
-    line = levels * width
-    for out, upward in ((rim_x, even), (rim_d, jnp.logical_not(even))):
-        facing = jnp.where(upward, high, low).reshape(line, chans)
-        for at in range(2):
-            out[at * line : (at + 1) * line, :] = facing[:, at * wide : (at + 1) * wide]
-
-
-def spread_kernel(pos, x0, x1, x2, x3, own, own_y):
+
+
+def spread_kernel(pos, x0, x1, x2, x3, rim_x, rim_d, own, own_y, to_x, to_d):
     del pos
     many = x0.shape[0]
     for at, piece in enumerate((x0, x1, x2, x3)):
@@ -164,21 +170,23 @@
     extra = x1.shape[0] - many
     own[4 * many : 4 * many + extra, :] = x1[many:, :]
     own[4 * many + extra :, :] = x3[many:, :]
+    to_x[...] = rim_x[...]
+    to_d[...] = rim_d[...]
 
 
 def split_kernel(
-    pos, here, west, east, g, own, x_x, x_d, by_x, by_d, after, first, second, near, mine
+    pos, here, west, east, g_far, own, x_x, x_d, by_x, by_d, after, first, second, near, mine, sems
 ):
     del after
+    levels, height, width, chans = g_far.shape
+    fetch = pltpu.make_async_copy(g_far, mine.at[:, pl.ds(1, height), pl.ds(0, width)], sems.at[0])
+    fetch.start()
     first[...] = west[0]
     second[...] = east[1]
     for at, part in enumerate((here, west, east)):
         near[2 * at : 2 * at + 2] = part[...]
-
-    levels, height, width, chans = g.shape
     edge, line, wide = levels * height, levels * width, chans // 2
     inner = own.shape[0] - 4 * edge
-    mine[:, 1 : height + 1, 0:width, :] = g[...]
 
     def columns(message, rows):
         for side in range(2):
@@ -219,6 +227,8 @@
     @pl.when(lat == 3)
     def _():
         mine[:, height + 1] = jnp.zeros_like(mine[:, height + 1])
+
+    fetch.wait()
 
 
 def pair_kernel(pos, one, two, after, both):
@@ -335,11 +345,15 @@
     half_1[...] = east[half:, :]
 
 
-def across_kernel(pos, half_3, half_1, own, x, y, d, late, block):
+def across_kernel(pos, half_3, half_1, late):
     del pos
     half = half_3.shape[0]
     late[0:half, :] = half_3[...]
     late[half:, :] = half_1[...]
+
+
+def block_kernel(pos, own, x, y, d, after, block):
+    del pos, after
     end = own.shape[0] - 16
     rows = block.shape[0] // 4
     for at, piece in enumerate((own, x, y, d)):
@@ -473,33 +487,38 @@
     many = cells // 2
     block = jax.ShapeDtypeStruct((cells, wide), bf16)
     strip = jax.ShapeDtypeStruct((2 * levels * width, 2 * span), bf16)
+    field_shape = (levels, height, width, chans)
     g_same, g_other, x0, x1, x2, x3, rim_x, rim_d = call(
         pack_kernel,
         [block, block]
         + [jax.ShapeDtypeStruct((many + extra, 2 * span), bf16) for extra in (0, 2 * edge, 0, 2 * edge)]
         + [strip, strip],
         (pos, x_cells, g_cells),
-        [VMEM((4, many, 2 * span), bf16)],
+        [
+            VMEM(field_shape, bf16),
+            VMEM(field_shape, bf16),
+            VMEM((4, many, 2 * span), bf16),
+            pltpu.SemaphoreType.DMA((2,)),
+        ],
         0,
         "pack",
         16,
+        far=(1, 2),
     )
     g_s = move(g_same, to_same)
     g_o = move(g_other, to_other)
     x_r1 = move(x1, lon_by(1))
     x_r3 = move(x3, lon_by(-1))
     x_r2 = move(x2, lon_by(2))
-    by_x = move(rim_x, lat_xor(1))
-    by_d = move(rim_d, lat_xor(3))
 
     inner = 4 * many
     (g0,) = call(
         pair_kernel, [jax.ShapeDtypeStruct((2, cells, wide), bf16)], (pos, g_s, g_o, x0), [], 0, "pair_0", 16, held=1
     )
-    x_own, x_own_y = call(
+    x_own, x_own_y, rim_x, rim_d = call(
         spread_kernel,
-        [jax.ShapeDtypeStruct((count, 2 * span), bf16) for count in (inner + 4 * edge, inner)],
-        (pos, x0, x_r1, x_r2, x_r3),
+        [jax.ShapeDtypeStruct((count, 2 * span), bf16) for count in (inner + 4 * edge, inner)] + [strip, strip],
+        (pos, x0, x_r1, x_r2, x_r3, rim_x, rim_d),
         [],
         0,
         "spread",
@@ -510,6 +529,8 @@
     x_y = move(x_own_y, lat_xor(2))
     g1 = move(g0, lon_by(1))
     g3 = move(g0, lon_by(-1))
+    by_x = move(rim_x, lat_xor(1))
+    by_d = move(rim_d, lat_xor(3))
     far_a, far_b, g_near, mine = call(
         split_kernel,
         [
@@ -519,16 +540,18 @@
             jax.ShapeDtypeStruct((levels, height + 2, width + 16, chans), bf16),
         ],
         (pos, g0, g1, g3, g_cells, x_own, x_x, x_d, by_x, by_d, x_y),
-        [],
+        [pltpu.SemaphoreType.DMA((1,))],
         0,
         "split",
         16,
         held=1,
+        far=(4,),
     )
     g2a = move(far_a, lon_by(1))
     g2b = move(far_b, lon_by(-1))
     s_near = move(g_near, sibling)
     theirs = move(mine, sibling)
+
     xs, total = pl.pallas_call(
         lines_kernel,
         out_shape=[
@@ -547,7 +570,7 @@
         pair_kernel, [jax.ShapeDtypeStruct((2, cells, wide), bf16)], (pos, g2a, g2b, xs), [], 0, "pair", 16, held=1
     )
     s2 = move(g2, sibling)
-    early, middle = 7, 19
+    early, middle = 6, 20
     cut, end = early * span, 27 * span
     size = end + 16 - cut
     half = size // 32 * 16
@@ -617,9 +640,8 @@
     half_3 = move(half_3, lon_by(1))
     half_1 = move(half_1, lon_by(-1))
     both = to_plane(pair)
-    from_2, block = call(
-        across_kernel, [slab(size), slab(4 * first_rows)], (pos, half_3, half_1, *plane), [], 0, "across", 16
-    )
+    (block,) = call(block_kernel, [slab(4 * first_rows)], (pos, *plane, pair), [], 0, "block", 16, held=1)
+    (from_2,) = call(across_kernel, [slab(size)], (pos, half_3, half_1), [], 0, "across", 16)
     early_3 = move(block, lon_by(1))
     early_1 = move(block, lon_by(-1))
     across = to_plane(from_2)

time: 147 us -> 149 us (1.014)
  waiting for transfers between devices: 51 us -> 52.6 us
    ppermute x34, waiting for transfers between devices: 51 us -> 52.6 us  [move(): return lax.ppermute(x, AXES, pairs)]
    pallas_call x10 -> x11, Pallas kernels: 14.6 us -> 15.6 us  [call(): pl.pallas_call(kernel, out_shape=outs, in_specs=[pl.BlockSpec(memory_spac...]
  transfers between devices with their start and end apart: 34 -> 34, of which waited for: 13 -> 14; matrix products, arithmetic and copies ran while one was open for 0% -> 0% of each run, Pallas kernels for 25% -> 25%
where the time goes in v13:
time: 149 us
  waiting for transfers between devices  52.6 us (35%)
  starting transfers between devices  47.6 us (32%)
  Pallas kernels  43.6 us (29%)
  local copies, waits for them, and re-layouts  4.01 us (3%)
    ppermute x34, waiting for transfers between devices, move(): return lax.ppermute(x, AXES, pairs)  52.6 us
    ppermute x34, starting transfers between devices, move(): return lax.ppermute(x, AXES, pairs)  47.6 us
    pallas_call x11, Pallas kernels, call(): pl.pallas_call(kernel, out_shape=outs, in_specs=[pl.BlockSpec(memory_spac...  15.6 us
    pallas_call x3, Pallas kernels, unpack(): pl.pallas_call(lambda *refs: unpack_kernel(*refs, slabs=slabs, count=len(...  13.6 us
    pallas_call x1, Pallas kernels, blocked_body(): pl.pallas_call(field_kernel, out_shape=jax.ShapeDtypeStruct((levels, heig...  9.52 us
    pallas_call x1, Pallas kernels, blocked_body(): pl.pallas_call(lines_kernel, out_shape=[jax.ShapeDtypeStruct((levels, row...  4.86 us
    unnamed x20, local copies, waits for them, and re-layouts  4.01 us
  transfers between devices with their start and end apart: 34, of which 14 were waited for; matrix products, arithmetic and copies ran while one was open for 0% of the time, Pallas kernels for 25%

profile of v13, /device:TPU:0, one launch (start us, length us, event | category | flops | bytes accessed | tf_op | source)
XLA Modules:
  0.0 149.0 jit_solution(7403733982990112186)
XLA Ops:
  0.7 1.0 copy-done.1
  1.7 1.0 copy-done.3
  2.7 1.3 pack.1
  4.7 3.1 %collective-permute-start = (bf16[416,128]{1,0:T(8,128)(2,1)S(1)}, bf16[416,128]{1,0:T(8,128)(2,1)S(1)}, u32[]{:S(2)}, u32[]{:S(2)}) collective-permute-start(bf16[416,128]{1,0:T(8,128)(2,1)S(1)} %get-tuple-element.33), channel_id=1, source_target_pairs={{0,1},{1,2},{2,3},{3,0},{4,5},{5,6},{6,7},{7,4},{8,9},{9,10},{10,1... | collective-permute-start | bytes 319496 | tf_op jit(solution)/shard_map/ppermute | solution.py:98
  7.8 2.1 %collective-permute-start.2 = (bf16[416,128]{1,0:T(8,128)(2,1)S(1)}, bf16[416,128]{1,0:T(8,128)(2,1)S(1)}, u32[]{:S(2)}, u32[]{:S(2)}) collective-permute-start(bf16[416,128]{1,0:T(8,128)(2,1)S(1)} %get-tuple-element.35), channel_id=1, source_target_pairs={{0,3},{1,0},{2,1},{3,2},{4,7},{5,4},{6,5},{7,6},{8,11},{9,8},{10,9... | collective-permute-start | bytes 319496 | tf_op jit(solution)/shard_map/ppermute | solution.py:98
  9.8 0.9 collective-permute-start.1
  10.8 1.5 %collective-permute-start.7 = (bf16[768,128]{1,0:T(8,128)(2,1)S(1)}, bf16[768,128]{1,0:T(8,128)(2,1)S(1)}, u32[]{:S(2)}, u32[]{:S(2)}) collective-permute-start(bf16[768,128]{1,0:T(8,128)(2,1)S(1)} %get-tuple-element.41), channel_id=1, source_target_pairs={{0,4},{1,5},{2,6},{3,7},{4,0},{5,1},{6,2},{7,3},{8,20},{9,21},{10,... | collective-permute-start | bytes 589832 | tf_op jit(solution)/shard_map/ppermute | solution.py:98
  12.3 7.0 %collective-permute-done.1.x2 = bf16[384,128]{1,0:T(8,128)(2,1)S(1)} collective-permute-done((bf16[384,128]{1,0:T(8,128)(2,1)S(1)}, bf16[384,128]{1,0:T(8,128)(2,1)S(1)}, u32[]{:S(2)}, u32[]{:S(2)}) %collective-permute-start.1) | collective-permute-done | bytes 98336 | tf_op jit(solution)/shard_map/ppermute | solution.py:98
  19.9 1.6 %collective-permute-start.10 = (bf16[384,128]{1,0:T(8,128)(2,1)S(1)}, bf16[384,128]{1,0:T(8,128)(2,1)S(1)}, u32[]{:S(2)}, u32[]{:S(2)}) collective-permute-start(bf16[384,128]{1,0:T(8,128)(2,1)S(1)} %get-tuple-element.42), channel_id=1, source_target_pairs={{0,4},{1,5},{2,6},{3,7},{4,0},{5,1},{6,2},{7,3},{8,12},{9,13},{10,... | collective-permute-start | bytes 294920 | tf_op jit(solution)/shard_map/ppermute | solution.py:98
  21.6 1.5 collective-permute-start.11
  23.0 1.5 %collective-permute-start.3 = (bf16[1600,128]{1,0:T(8,128)(2,1)S(1)}, bf16[1600,128]{1,0:T(8,128)(2,1)S(1)}, u32[]{:S(2)}, u32[]{:S(2)}) collective-permute-start(bf16[1600,128]{1,0:T(8,128)(2,1)S(1)} %get-tuple-element.38.own.x_own), channel_id=1, source_target_pairs={{0,4},{1,5},{2,6},{3,7},{4,0},{5,1},{6,2},{7,3},{8,12},{9,13},{10,... | collective-permute-start | bytes 1228808 | tf_op jit(solution)/shard_map/ppermute | solution.py:98
  25.0 1.6 %collective-permute-start.4 = (bf16[1536,128]{1,0:T(8,128)(2,1)S(1)}, bf16[1536,128]{1,0:T(8,128)(2,1)S(1)}, u32[]{:S(2)}, u32[]{:S(2)}) collective-permute-start(bf16[1536,128]{1,0:T(8,128)(2,1)S(1)} %get-tuple-element.39), channel_id=1, source_target_pairs={{0,8},{1,9},{2,10},{3,11},{4,12},{5,13},{6,14},{7,15},{8,0},{9,1},... | collective-permute-start | bytes 1179656 | tf_op jit(solution)/shard_map/ppermute | solution.py:98
  27.2 0.9 collective-permute-done.11.by_d
  28.0 3.0 %collective-permute-start.9 = (bf16[2,768,128]{2,1,0:T(8,128)(2,1)S(1)}, bf16[2,768,128]{2,1,0:T(8,128)(2,1)S(1)}, u32[]{:S(2)}, u32[]{:S(2)}) collective-permute-start(bf16[2,768,128]{2,1,0:T(8,128)(2,1)S(1)} %pair_0.1.here), channel_id=1, source_target_pairs={{0,3},{1,0},{2,1},{3,2},{4,7},{5,4},{6,5},{7,6},{8,11},{9,8},{10,9... | collective-permute-start | bytes 1179656 | tf_op jit(solution)/shard_map/ppermute | solution.py:98
  31.1 5.1 %collective-permute-done.4.after.x_y = bf16[1536,128]{1,0:T(8,128)(2,1)S(1)} collective-permute-done((bf16[1536,128]{1,0:T(8,128)(2,1)S(1)}, bf16[1536,128]{1,0:T(8,128)(2,1)S(1)}, u32[]{:S(2)}, u32[]{:S(2)}) %collective-permute-start.4) | collective-permute-done | bytes 393248 | tf_op jit(solution)/shard_map/ppermute | solution.py:98
  36.2 0.9 collective-permute-done.3.x_x
  37.0 8.3 %collective-permute-done.5.x_d = bf16[1600,128]{1,0:T(8,128)(2,1)S(1)} collective-permute-done((bf16[1600,128]{1,0:T(8,128)(2,1)S(1)}, bf16[1600,128]{1,0:T(8,128)(2,1)S(1)}, u32[]{:S(2)}, u32[]{:S(2)}) %collective-permute-start.5) | collective-permute-done | bytes 409632 | tf_op jit(solution)/shard_map/ppermute | solution.py:98
  45.3 1.5 %collective-permute-done.9.east = bf16[2,768,128]{2,1,0:T(8,128)(2,1)S(1)} collective-permute-done((bf16[2,768,128]{2,1,0:T(8,128)(2,1)S(1)}, bf16[2,768,128]{2,1,0:T(8,128)(2,1)S(1)}, u32[]{:S(2)}, u32[]{:S(2)}) %collective-permute-start.9) | collective-permute-done | bytes 393248 | tf_op jit(solution)/shard_map/ppermute | solution.py:98
  46.8 1.0 copy-done.2
  48.7 3.8 %collective-permute-start.14 = (bf16[768,128]{1,0:T(8,128)(2,1)S(1)}, bf16[768,128]{1,0:T(8,128)(2,1)S(1)}, u32[]{:S(2)}, u32[]{:S(2)}) collective-permute-start(bf16[768,128]{1,0:T(8,128)(2,1)S(1)} %get-tuple-element.47), channel_id=1, source_target_pairs={{0,3},{1,0},{2,1},{3,2},{4,7},{5,4},{6,5},{7,6},{8,11},{9,8},{10,9... | collective-permute-start | bytes 589832 | tf_op jit(solution)/shard_map/ppermute | solution.py:98
  52.5 4.9 %lines.1 = (bf16[4,18,192,256]{3,2,1,0:T(8,128)(2,1)S(1)}, f32[27,256,512]{2,1,0:T(8,128)}) custom-call(s32[3]{0:T(128)S(1)} %pad_add_fusion.pos.refs_0_, bf16[1600,128]{1,0:T(8,128)(2,1)S(1)} %get-tuple-element.38.own.x_own, bf16[1600,128]{1,0:T(8,128)(2,1)S(1)} %collective-permute-done.3.x_x, bf16[1536,128]{1,0:T(8,128)(2,1)S(1)} %collective-permute-done.4.after.x_y, ...), custom_call_target="tpu_custom_call" | custom-call | bytes 1048576 | tf_op jit(solution)/shard_map/lines/pallas_call | solution.py:555
  57.4 0.9 collective-permute-done.13.one
  58.3 1.9 %collective-permute-done.14.two = bf16[768,128]{1,0:T(8,128)(2,1)S(1)} collective-permute-done((bf16[768,128]{1,0:T(8,128)(2,1)S(1)}, bf16[768,128]{1,0:T(8,128)(2,1)S(1)}, u32[]{:S(2)}, u32[]{:S(2)}) %collective-permute-start.14) | collective-permute-done | bytes 196640 | tf_op jit(solution)/shard_map/ppermute | solution.py:98
  61.3 1.2 collective-permute-done.15.s2
  62.6 8.6 %taps.1.held = f32[27,64,128]{2,1,0:T(8,128)S(1)} custom-call(s32[3]{0:T(128)S(1)} %pad_add_fusion.pos.refs_0_, bf16[4,18,192,256]{3,2,1,0:T(8,128)(2,1)S(1)} %get-tuple-element.45.after.xs, bf16[6,768,128]{2,1,0:T(8,128)(2,1)S(1)} %get-tuple-element.46.g, bf16[6,768,128]{2,1,0:T(8,128)(2,1)S(1)} %collective-permute-done.12.s, ...), custom_call_target="tpu_custom_call" | custom-call | flops 5435817984 | bytes 11108352 | tf_op jit(solution)/shard_map/taps/pallas_call | solution.py:119
  71.1 0.9 code.1
  72.0 0.9 collective-permute-start.20
  72.9 3.0 %collective-permute-start.21 = (bf16[1360,128]{1,0:T(8,128)(2,1)S(1)}, bf16[1360,128]{1,0:T(8,128)(2,1)S(1)}, u32[]{:S(2)}, u32[]{:S(2)}) collective-permute-start(bf16[1360,128]{1,0:T(8,128)(2,1)S(1)} %get-tuple-element.50), channel_id=1, source_target_pairs={{0,3},{1,0},{2,1},{3,2},{4,7},{5,4},{6,5},{7,6},{8,11},{9,8},{10,9... | collective-permute-start | bytes 1044488 | tf_op jit(solution)/shard_map/ppermute | solution.py:98
  76.7 2.4 %collective-permute-start.18 = (bf16[1296,128]{1,0:T(8,128)(2,1)S(1)}, bf16[1296,128]{1,0:T(8,128)(2,1)S(1)}, u32[]{:S(2)}, u32[]{:S(2)}) collective-permute-start(bf16[1296,128]{1,0:T(8,128)(2,1)S(1)} %get-tuple-element.49.after.own.refs_1_.refs_9_), channel_id=1, source_target_pairs={{0,8},{1,9},{2,10},{3,11},{4,12},{5,13},{6,14},{7,15},{8,0},{9,1},... | collective-permute-start | bytes 995336 | tf_op jit(solution)/shard_map/ppermute | solution.py:98
  79.4 9.5 %field.1.after = bf16[4,4,48,256]{3,2,1,0:T(8,128)(2,1)} custom-call(s32[3]{0:T(128)S(1)} %pad_add_fusion.pos.refs_0_, bf16[1296,128]{1,0:T(8,128)(2,1)S(1)} %get-tuple-element.49.after.own.refs_1_.refs_9_, bf16[4,6,64,256]{3,2,1,0:T(8,128)(2,1)S(1)} %get-tuple-element.48.mine, bf16[4,6,64,256]{3,2,1,0:T(8,128)(2,1)S(1)} %collective-permute-done.16.after.theirs, ...), custom_call_target="tpu_custom_call" | custom-call | flops 10871635968 | bytes 7077888 | tf_op jit(solution)/shard_map/field/pallas_call | solution.py:601
  88.9 1.7 %collective-permute-done.21.east.refs_7_ = bf16[1360,128]{1,0:T(8,128)(2,1)S(1)} collective-permute-done((bf16[1360,128]{1,0:T(8,128)(2,1)S(1)}, bf16[1360,128]{1,0:T(8,128)(2,1)S(1)}, u32[]{:S(2)}, u32[]{:S(2)}) %collective-permute-start.21) | collective-permute-done | bytes 348192 | tf_op jit(solution)/shard_map/ppermute | solution.py:98
  90.7 1.0 copy-done.4
  92.3 1.2 collective-permute-start.31
  93.5 2.0 %collective-permute-start.32 = (bf16[3168,128]{1,0:T(8,128)(2,1)S(1)}, bf16[3168,128]{1,0:T(8,128)(2,1)S(1)}, u32[]{:S(2)}, u32[]{:S(2)}) collective-permute-start(bf16[3168,128]{1,0:T(8,128)(2,1)S(1)} %get-tuple-element.52.after), channel_id=1, source_target_pairs={{0,8},{1,9},{2,10},{3,11},{4,12},{5,13},{6,14},{7,15},{8,0},{9,1},... | collective-permute-start | bytes 2433032 | tf_op jit(solution)/shard_map/ppermute | solution.py:98
  95.9 1.8 %collective-permute-start.27 = (bf16[688,128]{1,0:T(8,128)(2,1)S(1)}, bf16[688,128]{1,0:T(8,128)(2,1)S(1)}, u32[]{:S(2)}, u32[]{:S(2)}) collective-permute-start(bf16[688,128]{1,0:T(8,128)(2,1)S(1)} %get-tuple-element.58), channel_id=1, source_target_pairs={{0,3},{1,0},{2,1},{3,2},{4,7},{5,4},{6,5},{7,6},{8,11},{9,8},{10,9... | collective-permute-start | bytes 528392 | tf_op jit(solution)/shard_map/ppermute | solution.py:98
  98.5 7.4 %collective-permute-done.26.half_3 = bf16[672,128]{1,0:T(8,128)(2,1)S(1)} collective-permute-done((bf16[672,128]{1,0:T(8,128)(2,1)S(1)}, bf16[672,128]{1,0:T(8,128)(2,1)S(1)}, u32[]{:S(2)}, u32[]{:S(2)}) %collective-permute-start.26) | collective-permute-done | bytes 172064 | tf_op jit(solution)/shard_map/ppermute | solution.py:98
  106.1 3.5 %collective-permute-start.23 = (bf16[1600,128]{1,0:T(8,128)(2,1)S(1)}, bf16[1600,128]{1,0:T(8,128)(2,1)S(1)}, u32[]{:S(2)}, u32[]{:S(2)}) collective-permute-start(bf16[1600,128]{1,0:T(8,128)(2,1)S(1)} %block.1.refs_5_), channel_id=1, source_target_pairs={{0,3},{1,0},{2,1},{3,2},{4,7},{5,4},{6,5},{7,6},{8,11},{9,8},{10,9... | collective-permute-start | bytes 1228808 | tf_op jit(solution)/shard_map/ppermute | solution.py:98
  110.2 9.8 %collective-permute-done.22.block_3.refs_4_ = bf16[1600,128]{1,0:T(8,128)(2,1)S(1)} collective-permute-done((bf16[1600,128]{1,0:T(8,128)(2,1)S(1)}, bf16[1600,128]{1,0:T(8,128)(2,1)S(1)}, u32[]{:S(2)}, u32[]{:S(2)}) %collective-permute-start.22) | collective-permute-done | bytes 409632 | tf_op jit(solution)/shard_map/ppermute | solution.py:98
  120.0 1.3 collective-permute-start.28
  121.3 3.6 %collective-permute-done.23.block_1.refs_5_ = bf16[1600,128]{1,0:T(8,128)(2,1)S(1)} collective-permute-done((bf16[1600,128]{1,0:T(8,128)(2,1)S(1)}, bf16[1600,128]{1,0:T(8,128)(2,1)S(1)}, u32[]{:S(2)}, u32[]{:S(2)}) %collective-permute-start.23) | collective-permute-done | bytes 409632 | tf_op jit(solution)/shard_map/ppermute | solution.py:98
  125.0 1.7 %collective-permute-start.29 = (bf16[1360,128]{1,0:T(8,128)(2,1)S(1)}, bf16[1360,128]{1,0:T(8,128)(2,1)S(1)}, u32[]{:S(2)}, u32[]{:S(2)}) collective-permute-start(bf16[1360,128]{1,0:T(8,128)(2,1)S(1)} %across.1.refs_3_), channel_id=1, source_target_pairs={{0,8},{1,9},{2,10},{3,11},{4,12},{5,13},{6,14},{7,15},{8,0},{9,1},... | collective-permute-start | bytes 1044488 | tf_op jit(solution)/shard_map/ppermute | solution.py:98
  126.7 1.5 %collective-permute-start.30 = (bf16[1360,128]{1,0:T(8,128)(2,1)S(1)}, bf16[1360,128]{1,0:T(8,128)(2,1)S(1)}, u32[]{:S(2)}, u32[]{:S(2)}) collective-permute-start(bf16[1360,128]{1,0:T(8,128)(2,1)S(1)} %across.1.refs_3_), channel_id=1, source_target_pairs={{0,12},{1,13},{2,14},{3,15},{4,8},{5,9},{6,10},{7,11},{8,4},{9,5},... | collective-permute-start | bytes 1044488 | tf_op jit(solution)/shard_map/ppermute | solution.py:98
  128.2 2.5 %unpack_1.1 = (f32[27,256,512]{2,1,0:T(8,128)}, f32[8,128]{1,0:T(8,128)S(1)}) custom-call(s32[3]{0:T(128)S(1)} %pad_add_fusion.pos.refs_0_, bf16[1296,128]{1,0:T(8,128)(2,1)S(1)} %get-tuple-element.49.after.own.refs_1_.refs_9_, bf16[1296,128]{1,0:T(8,128)(2,1)S(1)} %collective-permute-done.17.x.refs_2_.refs_10_, ...), custom_call_target="tpu_custom_call", output_to_operand_aliasing={{0}: (6, {})} | custom-call | bytes 4194304 | tf_op jit(solution)/shard_map/unpack_1/pallas_call | solution.py:412
  131.3 1.5 %collective-permute-start.24 = (bf16[800,128]{1,0:T(8,128)(2,1)S(1)}, bf16[800,128]{1,0:T(8,128)(2,1)S(1)}, u32[]{:S(2)}, u32[]{:S(2)}) collective-permute-start(bf16[800,128]{1,0:T(8,128)(2,1)S(1)} %get-tuple-element.55.refs_13_), channel_id=1, source_target_pairs={{0,1},{1,2},{2,3},{3,0},{4,5},{5,6},{6,7},{7,4},{8,9},{9,10},{10,1... | collective-permute-start | bytes 614408 | tf_op jit(solution)/shard_map/ppermute | solution.py:98
  132.8 2.4 %collective-permute-start.25 = (bf16[800,128]{1,0:T(8,128)(2,1)S(1)}, bf16[800,128]{1,0:T(8,128)(2,1)S(1)}, u32[]{:S(2)}, u32[]{:S(2)}) collective-permute-start(bf16[800,128]{1,0:T(8,128)(2,1)S(1)} %get-tuple-element.56), channel_id=1, source_target_pairs={{0,3},{1,0},{2,1},{3,2},{4,7},{5,4},{6,5},{7,6},{8,11},{9,8},{10,9... | collective-permute-start | bytes 614408 | tf_op jit(solution)/shard_map/ppermute | solution.py:98
  135.2 7.4 %unpack_2.1 = (f32[27,256,512]{2,1,0:T(8,128)}, f32[8,128]{1,0:T(8,128)}) custom-call(s32[3]{0:T(128)S(1)} %pad_add_fusion.pos.refs_0_, bf16[3168,128]{1,0:T(8,128)(2,1)} %copy-done.5, bf16[3168,128]{1,0:T(8,128)(2,1)} %copy-done.6, bf16[3168,128]{1,0:T(8,128)(2,1)} %copy-done.7, ...), custom_call_target="tpu_custom_call", output_to_operand_aliasing={{0}: (14, {})} | custom-call | bytes 4194304 | tf_op jit(solution)/shard_map/unpack_2/pallas_call | solution.py:412
  142.6 2.5 %collective-permute-done.29.refs_5_ = bf16[1360,128]{1,0:T(8,128)(2,1)S(1)} collective-permute-done((bf16[1360,128]{1,0:T(8,128)(2,1)S(1)}, bf16[1360,128]{1,0:T(8,128)(2,1)S(1)}, u32[]{:S(2)}, u32[]{:S(2)}) %collective-permute-start.29) | collective-permute-done | bytes 348192 | tf_op jit(solution)/shard_map/ppermute | solution.py:98
  145.1 3.7 %unpack_3.1 = (f32[27,256,512]{2,1,0:T(8,128)}, f32[8,128]{1,0:T(8,128)}) custom-call(s32[3]{0:T(128)S(1)} %pad_add_fusion.pos.refs_0_, bf16[800,128]{1,0:T(8,128)(2,1)S(1)} %collective-permute-done.24.refs_1_, bf16[800,128]{1,0:T(8,128)(2,1)S(1)} %collective-permute-done.25.refs_2_, ...), custom_call_target="tpu_custom_call", output_to_operand_aliasing={{0}: (7, {})} | custom-call | bytes 4194304 | tf_op jit(solution)/shard_map/unpack_3/pallas_call | solution.py:412
  (58 shorter events, 8.9 us)
Async XLA Ops:
  0.7 1.0 copy-start.1
  1.7 1.0 copy-start.3
  4.0 20.5 %collective-permute-start.6 = (bf16[768,128]{1,0:T(8,128)(2,1)S(1)}, bf16[768,128]{1,0:T(8,128)(2,1)S(1)}, u32[]{:S(2)}, u32[]{:S(2)}) collective-permute-start(bf16[768,128]{1,0:T(8,128)(2,1)S(1)} %get-tuple-element.40), channel_id=1, source_target_pairs={{0,0},{1,1},{2,2},{3,3},{4,4},{5,5},{6,6},{7,7},{8,16},{9,17},{10,... | collective-permute-start | bytes 589832 | tf_op jit(solution)/shard_map/ppermute | solution.py:98
  4.7 14.6 %collective-permute-start = (bf16[416,128]{1,0:T(8,128)(2,1)S(1)}, bf16[416,128]{1,0:T(8,128)(2,1)S(1)}, u32[]{:S(2)}, u32[]{:S(2)}) collective-permute-start(bf16[416,128]{1,0:T(8,128)(2,1)S(1)} %get-tuple-element.33), channel_id=1, source_target_pairs={{0,1},{1,2},{2,3},{3,0},{4,5},{5,6},{6,7},{7,4},{8,9},{9,10},{10,1... | collective-permute-start | bytes 319496 | tf_op jit(solution)/shard_map/ppermute | solution.py:98
  7.8 11.5 %collective-permute-start.2 = (bf16[416,128]{1,0:T(8,128)(2,1)S(1)}, bf16[416,128]{1,0:T(8,128)(2,1)S(1)}, u32[]{:S(2)}, u32[]{:S(2)}) collective-permute-start(bf16[416,128]{1,0:T(8,128)(2,1)S(1)} %get-tuple-element.35), channel_id=1, source_target_pairs={{0,3},{1,0},{2,1},{3,2},{4,7},{5,4},{6,5},{7,6},{8,11},{9,8},{10,9... | collective-permute-start | bytes 319496 | tf_op jit(solution)/shard_map/ppermute | solution.py:98
  9.8 9.4 %collective-permute-start.1 = (bf16[384,128]{1,0:T(8,128)(2,1)S(1)}, bf16[384,128]{1,0:T(8,128)(2,1)S(1)}, u32[]{:S(2)}, u32[]{:S(2)}) collective-permute-start(bf16[384,128]{1,0:T(8,128)(2,1)S(1)} %get-tuple-element.34), channel_id=1, source_target_pairs={{0,2},{1,3},{2,0},{3,1},{4,6},{5,7},{6,4},{7,5},{8,10},{9,11},{10,... | collective-permute-start | bytes 294920 | tf_op jit(solution)/shard_map/ppermute | solution.py:98
  10.8 14.2 %collective-permute-start.7 = (bf16[768,128]{1,0:T(8,128)(2,1)S(1)}, bf16[768,128]{1,0:T(8,128)(2,1)S(1)}, u32[]{:S(2)}, u32[]{:S(2)}) collective-permute-start(bf16[768,128]{1,0:T(8,128)(2,1)S(1)} %get-tuple-element.41), channel_id=1, source_target_pairs={{0,4},{1,5},{2,6},{3,7},{4,0},{5,1},{6,2},{7,3},{8,20},{9,21},{10,... | collective-permute-start | bytes 589832 | tf_op jit(solution)/shard_map/ppermute | solution.py:98
  19.9 7.2 %collective-permute-start.10 = (bf16[384,128]{1,0:T(8,128)(2,1)S(1)}, bf16[384,128]{1,0:T(8,128)(2,1)S(1)}, u32[]{:S(2)}, u32[]{:S(2)}) collective-permute-start(bf16[384,128]{1,0:T(8,128)(2,1)S(1)} %get-tuple-element.42), channel_id=1, source_target_pairs={{0,4},{1,5},{2,6},{3,7},{4,0},{5,1},{6,2},{7,3},{8,12},{9,13},{10,... | collective-permute-start | bytes 294920 | tf_op jit(solution)/shard_map/ppermute | solution.py:98
  21.6 6.5 %collective-permute-start.11 = (bf16[384,128]{1,0:T(8,128)(2,1)S(1)}, bf16[384,128]{1,0:T(8,128)(2,1)S(1)}, u32[]{:S(2)}, u32[]{:S(2)}) collective-permute-start(bf16[384,128]{1,0:T(8,128)(2,1)S(1)} %get-tuple-element.43), channel_id=1, source_target_pairs={{0,12},{1,13},{2,14},{3,15},{4,8},{5,9},{6,10},{7,11},{8,4},{9,5},... | collective-permute-start | bytes 294920 | tf_op jit(solution)/shard_map/ppermute | solution.py:98
  23.0 14.0 %collective-permute-start.3 = (bf16[1600,128]{1,0:T(8,128)(2,1)S(1)}, bf16[1600,128]{1,0:T(8,128)(2,1)S(1)}, u32[]{:S(2)}, u32[]{:S(2)}) collective-permute-start(bf16[1600,128]{1,0:T(8,128)(2,1)S(1)} %get-tuple-element.38.own.x_own), channel_id=1, source_target_pairs={{0,4},{1,5},{2,6},{3,7},{4,0},{5,1},{6,2},{7,3},{8,12},{9,13},{10,... | collective-permute-start | bytes 1228808 | tf_op jit(solution)/shard_map/ppermute | solution.py:98
  24.5 20.8 %collective-permute-start.5 = (bf16[1600,128]{1,0:T(8,128)(2,1)S(1)}, bf16[1600,128]{1,0:T(8,128)(2,1)S(1)}, u32[]{:S(2)}, u32[]{:S(2)}) collective-permute-start(bf16[1600,128]{1,0:T(8,128)(2,1)S(1)} %get-tuple-element.38.own.x_own), channel_id=1, source_target_pairs={{0,12},{1,13},{2,14},{3,15},{4,8},{5,9},{6,10},{7,11},{8,4},{9,5},... | collective-permute-start | bytes 1228808 | tf_op jit(solution)/shard_map/ppermute | solution.py:98
  25.0 11.2 %collective-permute-start.4 = (bf16[1536,128]{1,0:T(8,128)(2,1)S(1)}, bf16[1536,128]{1,0:T(8,128)(2,1)S(1)}, u32[]{:S(2)}, u32[]{:S(2)}) collective-permute-start(bf16[1536,128]{1,0:T(8,128)(2,1)S(1)} %get-tuple-element.39), channel_id=1, source_target_pairs={{0,8},{1,9},{2,10},{3,11},{4,12},{5,13},{6,14},{7,15},{8,0},{9,1},... | collective-permute-start | bytes 1179656 | tf_op jit(solution)/shard_map/ppermute | solution.py:98
  27.1 18.2 %collective-permute-start.8 = (bf16[2,768,128]{2,1,0:T(8,128)(2,1)S(1)}, bf16[2,768,128]{2,1,0:T(8,128)(2,1)S(1)}, u32[]{:S(2)}, u32[]{:S(2)}) collective-permute-start(bf16[2,768,128]{2,1,0:T(8,128)(2,1)S(1)} %pair_0.1.here), channel_id=1, source_target_pairs={{0,1},{1,2},{2,3},{3,0},{4,5},{5,6},{6,7},{7,4},{8,9},{9,10},{10,1... | collective-permute-start | bytes 1179656 | tf_op jit(solution)/shard_map/ppermute | solution.py:98
  28.0 18.8 %collective-permute-start.9 = (bf16[2,768,128]{2,1,0:T(8,128)(2,1)S(1)}, bf16[2,768,128]{2,1,0:T(8,128)(2,1)S(1)}, u32[]{:S(2)}, u32[]{:S(2)}) collective-permute-start(bf16[2,768,128]{2,1,0:T(8,128)(2,1)S(1)} %pair_0.1.here), channel_id=1, source_target_pairs={{0,3},{1,0},{2,1},{3,2},{4,7},{5,4},{6,5},{7,6},{8,11},{9,8},{10,9... | collective-permute-start | bytes 1179656 | tf_op jit(solution)/shard_map/ppermute | solution.py:98
  46.8 1.0 copy-start.2
  48.6 14.0 %collective-permute-start.12 = (bf16[6,768,128]{2,1,0:T(8,128)(2,1)S(1)}, bf16[6,768,128]{2,1,0:T(8,128)(2,1)S(1)}, u32[]{:S(2)}, u32[]{:S(2)}) collective-permute-start(bf16[6,768,128]{2,1,0:T(8,128)(2,1)S(1)} %get-tuple-element.46.g), channel_id=1, source_target_pairs={{0,16},{1,17},{2,18},{3,19},{4,20},{5,21},{6,22},{7,23},{8,24},{9,... | collective-permute-start | bytes 3538952 | tf_op jit(solution)/shard_map/ppermute | solution.py:98
  48.7 9.6 %collective-permute-start.13 = (bf16[768,128]{1,0:T(8,128)(2,1)S(1)}, bf16[768,128]{1,0:T(8,128)(2,1)S(1)}, u32[]{:S(2)}, u32[]{:S(2)}) collective-permute-start(bf16[768,128]{1,0:T(8,128)(2,1)S(1)} %get-tuple-element.44.after), channel_id=1, source_target_pairs={{0,1},{1,2},{2,3},{3,0},{4,5},{5,6},{6,7},{7,4},{8,9},{9,10},{10,1... | collective-permute-start | bytes 589832 | tf_op jit(solution)/shard_map/ppermute | solution.py:98
  48.7 11.5 %collective-permute-start.14 = (bf16[768,128]{1,0:T(8,128)(2,1)S(1)}, bf16[768,128]{1,0:T(8,128)(2,1)S(1)}, u32[]{:S(2)}, u32[]{:S(2)}) collective-permute-start(bf16[768,128]{1,0:T(8,128)(2,1)S(1)} %get-tuple-element.47), channel_id=1, source_target_pairs={{0,3},{1,0},{2,1},{3,2},{4,7},{5,4},{6,5},{7,6},{8,11},{9,8},{10,9... | collective-permute-start | bytes 589832 | tf_op jit(solution)/shard_map/ppermute | solution.py:98
  60.2 19.2 %slice-start = ((s8[7077888]{0:T(1024)(128)(4,1)}), s8[4194304]{0:T(1024)(128)(4,1)S(1)}, s32[]{:S(2)}) async-start(s8[7077888]{0:T(1024)(128)(4,1)} %bitcast.12), calls=%async_computation | async-start | bytes 8388608
  60.8 1.8 %collective-permute-start.15 = (bf16[2,768,128]{2,1,0:T(8,128)(2,1)S(1)}, bf16[2,768,128]{2,1,0:T(8,128)(2,1)S(1)}, u32[]{:S(2)}, u32[]{:S(2)}) collective-permute-start(bf16[2,768,128]{2,1,0:T(8,128)(2,1)S(1)} %pair.1.g2), channel_id=1, source_target_pairs={{0,16},{1,17},{2,18},{3,19},{4,20},{5,21},{6,22},{7,23},{8,24},{9,... | collective-permute-start | bytes 1179656 | tf_op jit(solution)/shard_map/ppermute | solution.py:98
  60.8 18.6 %slice-start.1 = ((s8[7077888]{0:T(1024)(128)(4,1)}), s8[2883584]{0:T(1024)(128)(4,1)S(1)}, s32[]{:S(2)}) async-start(s8[7077888]{0:T(1024)(128)(4,1)} %bitcast.12), calls=%async_computation.1 | async-start | bytes 5767168
  60.9 10.3 %collective-permute-start.16 = (bf16[4,6,64,256]{3,2,1,0:T(8,128)(2,1)S(1)}, bf16[4,6,64,256]{3,2,1,0:T(8,128)(2,1)S(1)}, u32[]{:S(2)}, u32[]{:S(2)}) collective-permute-start(bf16[4,6,64,256]{3,2,1,0:T(8,128)(2,1)S(1)} %get-tuple-element.48.mine), channel_id=1, source_target_pairs={{0,16},{1,17},{2,18},{3,19},{4,20},{5,21},{6,22},{7,23},{8,24},{9,... | collective-permute-start | bytes 2359304 | tf_op jit(solution)/shard_map/ppermute | solution.py:98
  72.0 16.9 %collective-permute-start.20 = (bf16[1360,128]{1,0:T(8,128)(2,1)S(1)}, bf16[1360,128]{1,0:T(8,128)(2,1)S(1)}, u32[]{:S(2)}, u32[]{:S(2)}) collective-permute-start(bf16[1360,128]{1,0:T(8,128)(2,1)S(1)} %get-tuple-element.50), channel_id=1, source_target_pairs={{0,1},{1,2},{2,3},{3,0},{4,5},{5,6},{6,7},{7,4},{8,9},{9,10},{10,1... | collective-permute-start | bytes 1044488 | tf_op jit(solution)/shard_map/ppermute | solution.py:98
  72.9 17.8 %collective-permute-start.21 = (bf16[1360,128]{1,0:T(8,128)(2,1)S(1)}, bf16[1360,128]{1,0:T(8,128)(2,1)S(1)}, u32[]{:S(2)}, u32[]{:S(2)}) collective-permute-start(bf16[1360,128]{1,0:T(8,128)(2,1)S(1)} %get-tuple-element.50), channel_id=1, source_target_pairs={{0,3},{1,0},{2,1},{3,2},{4,7},{5,4},{6,5},{7,6},{8,11},{9,8},{10,9... | collective-permute-start | bytes 1044488 | tf_op jit(solution)/shard_map/ppermute | solution.py:98
  75.9 19.6 %collective-permute-start.17 = (bf16[1296,128]{1,0:T(8,128)(2,1)S(1)}, bf16[1296,128]{1,0:T(8,128)(2,1)S(1)}, u32[]{:S(2)}, u32[]{:S(2)}) collective-permute-start(bf16[1296,128]{1,0:T(8,128)(2,1)S(1)} %get-tuple-element.49.after.own.refs_1_.refs_9_), channel_id=1, source_target_pairs={{0,4},{1,5},{2,6},{3,7},{4,0},{5,1},{6,2},{7,3},{8,12},{9,13},{10,... | collective-permute-start | bytes 995336 | tf_op jit(solution)/shard_map/ppermute | solution.py:98
  76.7 19.2 %collective-permute-start.18 = (bf16[1296,128]{1,0:T(8,128)(2,1)S(1)}, bf16[1296,128]{1,0:T(8,128)(2,1)S(1)}, u32[]{:S(2)}, u32[]{:S(2)}) collective-permute-start(bf16[1296,128]{1,0:T(8,128)(2,1)S(1)} %get-tuple-element.49.after.own.refs_1_.refs_9_), channel_id=1, source_target_pairs={{0,8},{1,9},{2,10},{3,11},{4,12},{5,13},{6,14},{7,15},{8,0},{9,1},... | collective-permute-start | bytes 995336 | tf_op jit(solution)/shard_map/ppermute | solution.py:98
  79.0 18.6 %collective-permute-start.19 = (bf16[1296,128]{1,0:T(8,128)(2,1)S(1)}, bf16[1296,128]{1,0:T(8,128)(2,1)S(1)}, u32[]{:S(2)}, u32[]{:S(2)}) collective-permute-start(bf16[1296,128]{1,0:T(8,128)(2,1)S(1)} %get-tuple-element.49.after.own.refs_1_.refs_9_), channel_id=1, source_target_pairs={{0,12},{1,13},{2,14},{3,15},{4,8},{5,9},{6,10},{7,11},{8,4},{9,5},... | collective-permute-start | bytes 995336 | tf_op jit(solution)/shard_map/ppermute | solution.py:98
  90.7 1.0 copy-start.4
  92.3 34.4 %collective-permute-start.31 = (bf16[3168,128]{1,0:T(8,128)(2,1)S(1)}, bf16[3168,128]{1,0:T(8,128)(2,1)S(1)}, u32[]{:S(2)}, u32[]{:S(2)}) collective-permute-start(bf16[3168,128]{1,0:T(8,128)(2,1)S(1)} %get-tuple-element.52.after), channel_id=1, source_target_pairs={{0,4},{1,5},{2,6},{3,7},{4,0},{5,1},{6,2},{7,3},{8,12},{9,13},{10,... | collective-permute-start | bytes 2433032 | tf_op jit(solution)/shard_map/ppermute | solution.py:98
  93.5 37.8 %collective-permute-start.32 = (bf16[3168,128]{1,0:T(8,128)(2,1)S(1)}, bf16[3168,128]{1,0:T(8,128)(2,1)S(1)}, u32[]{:S(2)}, u32[]{:S(2)}) collective-permute-start(bf16[3168,128]{1,0:T(8,128)(2,1)S(1)} %get-tuple-element.52.after), channel_id=1, source_target_pairs={{0,8},{1,9},{2,10},{3,11},{4,12},{5,13},{6,14},{7,15},{8,0},{9,1},... | collective-permute-start | bytes 2433032 | tf_op jit(solution)/shard_map/ppermute | solution.py:98
  95.5 37.3 %collective-permute-start.33 = (bf16[3168,128]{1,0:T(8,128)(2,1)S(1)}, bf16[3168,128]{1,0:T(8,128)(2,1)S(1)}, u32[]{:S(2)}, u32[]{:S(2)}) collective-permute-start(bf16[3168,128]{1,0:T(8,128)(2,1)S(1)} %get-tuple-element.52.after), channel_id=1, source_target_pairs={{0,12},{1,13},{2,14},{3,15},{4,8},{5,9},{6,10},{7,11},{8,4},{9,5},... | collective-permute-start | bytes 2433032 | tf_op jit(solution)/shard_map/ppermute | solution.py:98
  95.9 10.3 %collective-permute-start.27 = (bf16[688,128]{1,0:T(8,128)(2,1)S(1)}, bf16[688,128]{1,0:T(8,128)(2,1)S(1)}, u32[]{:S(2)}, u32[]{:S(2)}) collective-permute-start(bf16[688,128]{1,0:T(8,128)(2,1)S(1)} %get-tuple-element.58), channel_id=1, source_target_pairs={{0,3},{1,0},{2,1},{3,2},{4,7},{5,4},{6,5},{7,6},{8,11},{9,8},{10,9... | collective-permute-start | bytes 528392 | tf_op jit(solution)/shard_map/ppermute | solution.py:98
  97.7 8.2 %collective-permute-start.26 = (bf16[672,128]{1,0:T(8,128)(2,1)S(1)}, bf16[672,128]{1,0:T(8,128)(2,1)S(1)}, u32[]{:S(2)}, u32[]{:S(2)}) collective-permute-start(bf16[672,128]{1,0:T(8,128)(2,1)S(1)} %get-tuple-element.57), channel_id=1, source_target_pairs={{0,1},{1,2},{2,3},{3,0},{4,5},{5,6},{6,7},{7,4},{8,9},{9,10},{10,1... | collective-permute-start | bytes 516104 | tf_op jit(solution)/shard_map/ppermute | solution.py:98
  105.8 14.2 %collective-permute-start.22 = (bf16[1600,128]{1,0:T(8,128)(2,1)S(1)}, bf16[1600,128]{1,0:T(8,128)(2,1)S(1)}, u32[]{:S(2)}, u32[]{:S(2)}) collective-permute-start(bf16[1600,128]{1,0:T(8,128)(2,1)S(1)} %block.1.refs_5_), channel_id=1, source_target_pairs={{0,1},{1,2},{2,3},{3,0},{4,5},{5,6},{6,7},{7,4},{8,9},{9,10},{10,1... | collective-permute-start | bytes 1228808 | tf_op jit(solution)/shard_map/ppermute | solution.py:98
  106.1 18.8 %collective-permute-start.23 = (bf16[1600,128]{1,0:T(8,128)(2,1)S(1)}, bf16[1600,128]{1,0:T(8,128)(2,1)S(1)}, u32[]{:S(2)}, u32[]{:S(2)}) collective-permute-start(bf16[1600,128]{1,0:T(8,128)(2,1)S(1)} %block.1.refs_5_), channel_id=1, source_target_pairs={{0,3},{1,0},{2,1},{3,2},{4,7},{5,4},{6,5},{7,6},{8,11},{9,8},{10,9... | collective-permute-start | bytes 1228808 | tf_op jit(solution)/shard_map/ppermute | solution.py:98
  120.0 22.5 %collective-permute-start.28 = (bf16[1360,128]{1,0:T(8,128)(2,1)S(1)}, bf16[1360,128]{1,0:T(8,128)(2,1)S(1)}, u32[]{:S(2)}, u32[]{:S(2)}) collective-permute-start(bf16[1360,128]{1,0:T(8,128)(2,1)S(1)} %across.1.refs_3_), channel_id=1, source_target_pairs={{0,4},{1,5},{2,6},{3,7},{4,0},{5,1},{6,2},{7,3},{8,12},{9,13},{10,... | collective-permute-start | bytes 1044488 | tf_op jit(solution)/shard_map/ppermute | solution.py:98
  125.0 10.2 %copy-start = (bf16[1600,128]{1,0:T(8,128)(2,1)}, bf16[1600,128]{1,0:T(8,128)(2,1)S(1)}, u32[]{:S(2)}) copy-start(bf16[1600,128]{1,0:T(8,128)(2,1)S(1)} %collective-permute-done.23.block_1.refs_5_) | copy-start | bytes 1228804
  125.0 20.1 %collective-permute-start.29 = (bf16[1360,128]{1,0:T(8,128)(2,1)S(1)}, bf16[1360,128]{1,0:T(8,128)(2,1)S(1)}, u32[]{:S(2)}, u32[]{:S(2)}) collective-permute-start(bf16[1360,128]{1,0:T(8,128)(2,1)S(1)} %across.1.refs_3_), channel_id=1, source_target_pairs={{0,8},{1,9},{2,10},{3,11},{4,12},{5,13},{6,14},{7,15},{8,0},{9,1},... | collective-permute-start | bytes 1044488 | tf_op jit(solution)/shard_map/ppermute | solution.py:98
  126.7 8.5 %copy-start.5 = (bf16[3168,128]{1,0:T(8,128)(2,1)}, bf16[3168,128]{1,0:T(8,128)(2,1)S(1)}, u32[]{:S(2)}) copy-start(bf16[3168,128]{1,0:T(8,128)(2,1)S(1)} %collective-permute-done.31.refs_1_) | copy-start | bytes 2433028
  126.7 18.4 %collective-permute-start.30 = (bf16[1360,128]{1,0:T(8,128)(2,1)S(1)}, bf16[1360,128]{1,0:T(8,128)(2,1)S(1)}, u32[]{:S(2)}, u32[]{:S(2)}) collective-permute-start(bf16[1360,128]{1,0:T(8,128)(2,1)S(1)} %across.1.refs_3_), channel_id=1, source_target_pairs={{0,12},{1,13},{2,14},{3,15},{4,8},{5,9},{6,10},{7,11},{8,4},{9,5},... | collective-permute-start | bytes 1044488 | tf_op jit(solution)/shard_map/ppermute | solution.py:98
  131.3 3.9 %copy-start.6 = (bf16[3168,128]{1,0:T(8,128)(2,1)}, bf16[3168,128]{1,0:T(8,128)(2,1)S(1)}, u32[]{:S(2)}) copy-start(bf16[3168,128]{1,0:T(8,128)(2,1)S(1)} %collective-permute-done.32.refs_2_) | copy-start | bytes 2433028
  131.3 13.7 %collective-permute-start.24 = (bf16[800,128]{1,0:T(8,128)(2,1)S(1)}, bf16[800,128]{1,0:T(8,128)(2,1)S(1)}, u32[]{:S(2)}, u32[]{:S(2)}) collective-permute-start(bf16[800,128]{1,0:T(8,128)(2,1)S(1)} %get-tuple-element.55.refs_13_), channel_id=1, source_target_pairs={{0,1},{1,2},{2,3},{3,0},{4,5},{5,6},{6,7},{7,4},{8,9},{9,10},{10,1... | collective-permute-start | bytes 614408 | tf_op jit(solution)/shard_map/ppermute | solution.py:98
  132.8 2.4 %copy-start.7 = (bf16[3168,128]{1,0:T(8,128)(2,1)}, bf16[3168,128]{1,0:T(8,128)(2,1)S(1)}, u32[]{:S(2)}) copy-start(bf16[3168,128]{1,0:T(8,128)(2,1)S(1)} %collective-permute-done.33.refs_3_) | copy-start | bytes 2433028
  132.8 12.2 %collective-permute-start.25 = (bf16[800,128]{1,0:T(8,128)(2,1)S(1)}, bf16[800,128]{1,0:T(8,128)(2,1)S(1)}, u32[]{:S(2)}, u32[]{:S(2)}) collective-permute-start(bf16[800,128]{1,0:T(8,128)(2,1)S(1)} %get-tuple-element.56), channel_id=1, source_target_pairs={{0,3},{1,0},{2,1},{3,2},{4,7},{5,4},{6,5},{7,6},{8,11},{9,8},{10,9... | collective-permute-start | bytes 614408 | tf_op jit(solution)/shard_map/ppermute | solution.py:98

commit v14 on v12

--- a/solution.py
+++ b/solution.py
@@ -302,7 +302,7 @@
                 out[(2 - lev_at) * 9 + lat_by * 3 + lon_at] = block[lon_at * span : (lon_at + 1) * span]
 
 
-def code_kernel(pos, held, after, out, late, rest):
+def code_kernel(pos, held, after, out, late):
     del pos, after
     taps, span, filters = held.shape
     most = jnp.abs(held[0])
@@ -313,42 +313,51 @@
     unit = jnp.broadcast_to(jnp.exp2(power), (16, filters)).astype(out.dtype).astype(jnp.float32)
     shrink = 1.0 / unit[0:1]
     unit = unit.astype(out.dtype)
+    skip = out.shape[0] - late.shape[0]
     for tap in range(taps):
         value = held[tap] * shrink
         square = value * value
         code = (square * value * jnp.abs(value)).astype(out.dtype)
-        for ref, many in ((out, out.shape[0] - 16), (late, late.shape[0] - 16), (rest, rest.shape[0])):
-            at = tap * span if ref is out else tap * span - (taps * span - many)
-            if 0 <= at < many:
-                ref[at : at + span, :] = code
-    out[out.shape[0] - 16 :, :] = unit
-    late[late.shape[0] - 16 :, :] = unit
-
-
-def both_kernel(pos, west, east, rest, after, both, half_3, half_1):
+        out[tap * span : (tap + 1) * span, :] = code
+        if tap * span >= skip:
+            late[tap * span - skip : (tap + 1) * span - skip, :] = code
+    out[taps * span :, :] = unit
+    late[taps * span - skip :, :] = unit
+
+
+def both_kernel(pos, west, east, after, both, half_3, half_1):
     del pos, after
     size, half = west.shape[0], half_3.shape[0]
     both[0:size, :] = west[...]
-    both[size : 2 * size, :] = east[...]
-    both[2 * size :, :] = rest[...]
+    both[size:, :] = east[...]
     half_3[...] = west[0:half, :]
     half_1[...] = east[half:, :]
 
 
-def across_kernel(pos, half_3, half_1, own, x, y, d, late, block):
+def cross_kernel(pos, by_x, by_y, after, top, bottom):
+    del pos, after
+    cut = top.shape[0]
+    top[...] = by_y[0:cut, :]
+    bottom[...] = by_x[cut:, :]
+
+
+def across_kernel(pos, half_3, half_1, late):
     del pos
     half = half_3.shape[0]
     late[0:half, :] = half_3[...]
     late[half:, :] = half_1[...]
-    end = own.shape[0] - 16
+
+
+def block_kernel(pos, own, x, y, top, bottom, block):
+    del pos
     rows = block.shape[0] // 4
-    for at, piece in enumerate((own, x, y, d)):
+    for at, (piece, end) in enumerate(((own, own), (x, x), (y, y), (top, bottom))):
         block[at * rows : (at + 1) * rows - 16, :] = piece[0 : rows - 16, :]
-        block[(at + 1) * rows - 16 : (at + 1) * rows, :] = piece[end:, :]
-
-
-def hand_kernel(pos, block_3, block_1, after, first, second):
-    del pos, after
+        block[(at + 1) * rows - 16 : (at + 1) * rows, :] = end[end.shape[0] - 16 :, :]
+
+
+def hand_kernel(pos, block_3, block_1, first, second):
+    del pos
     many = first.shape[0]
     first[...] = block_3[0:many, :]
     second[...] = block_1[many:, :]
@@ -377,11 +386,12 @@
     for at, (_, _, many, skip, pieces) in enumerate(parts):
         if at >= slots:
             copy(at - slots).wait()
-        for tag, (which, row, (power_in, power_row)) in enumerate(pieces):
+        for tag, ((power_in, power_row), *segments) in enumerate(pieces):
             unit = sources[power_in][power_row : power_row + 16, :].astype(jnp.float32)[0:1]
             lanes = pl.ds(pl.multiple_of((pos[1] ^ tag) * wide, wide), wide)
             for tap in range(many):
-                start = row + (skip + tap) * span
+                begin, which, row = [segment for segment in segments if segment[0] <= skip + tap][-1]
+                start = row + (skip + tap - begin) * span
                 code = sources[which][start : start + span, :].astype(jnp.float32)
                 root = lax.rsqrt(lax.rsqrt(jnp.abs(code))) * unit
                 buffers[at % slots, tap, :, lanes] = jnp.where(code < 0, -root, root)
@@ -547,12 +557,12 @@
         pair_kernel, [jax.ShapeDtypeStruct((2, cells, wide), bf16)], (pos, g2a, g2b, xs), [], 0, "pair", 16, held=1
     )
     s2 = move(g2, sibling)
-    early, middle = 7, 19
+    early = 6
     cut, end = early * span, 27 * span
     size = end + 16 - cut
     half = size // 32 * 16
     first_rows = cut + 16
-    own_rows = middle * span + 16
+    own_cut, late_cut = 14 * span, (27 - early) // 2 * span
     slab = lambda count: jax.ShapeDtypeStruct((count, wide), bf16)
     (grads,) = call(
         taps_kernel,
@@ -563,17 +573,24 @@
         "taps",
         28,
     )
-    own, late, rest = call(
-        code_kernel,
-        [slab(own_rows), slab(size), slab(end - middle * span)],
-        (pos, grads, theirs),
-        [],
-        0,
-        "code",
-        16,
-        held=1,
-    )
-
+    own, late = call(code_kernel, [slab(end + 16), slab(size)], (pos, grads, theirs), [], 0, "code", 16, held=1)
+
+    def to_plane(share):
+        return move(share, lat_xor(1)), move(share, lat_xor(2))
+
+    def to_diagonal(by_x, by_y, cut, after, name):
+        top, bottom = call(
+            cross_kernel, [slab(cut), slab(by_x.shape[0] - cut)], (pos, by_x, by_y, after), [], 0, name, 16, held=1
+        )
+        return move(top, lat_xor(1)), move(bottom, lat_xor(2)), top
+
+    from_3 = move(late, lon_by(1))
+    from_1 = move(late, lon_by(-1))
+    own_x, own_y = to_plane(own)
+    own_top, own_bottom, crossed = to_diagonal(own_x, own_y, own_cut, own, "cross_1")
+    pair, half_3, half_1 = call(
+        both_kernel, [slab(2 * size), slab(half), slab(size - half)], (pos, from_3, from_1, crossed), [], 0, "both", 16, held=1
+    )
     whole = lambda t: (0, 0, 0, 0)
     field = pl.pallas_call(
         field_kernel,
@@ -596,63 +613,65 @@
         ),
         compiler_params=pltpu.CompilerParams(vmem_limit_bytes=20 * 1024 * 1024),
         name="field",
-    )(pos, own, mine, theirs, taps)
-
-    def to_plane(share):
-        return [move(share, lat_xor(tag)) for tag in (1, 2, 3)]
-
-    from_3 = move(late, lon_by(1))
-    from_1 = move(late, lon_by(-1))
-    plane = [own] + to_plane(own)
-    pair, half_3, half_1 = call(
-        both_kernel,
-        [slab(2 * size + end - middle * span), slab(half), slab(size - half)],
-        (pos, from_3, from_1, rest, field),
-        [],
-        0,
-        "both",
-        16,
-        held=1,
-    )
+    )(pos, pair, mine, theirs, taps)
+
     half_3 = move(half_3, lon_by(1))
     half_1 = move(half_1, lon_by(-1))
-    both = to_plane(pair)
-    from_2, block = call(
-        across_kernel, [slab(size), slab(4 * first_rows)], (pos, half_3, half_1, *plane), [], 0, "across", 16
+    pair_x, pair_y = to_plane(pair)
+    (block,) = call(
+        block_kernel, [slab(4 * first_rows)], (pos, own, own_x, own_y, own_top, own_bottom), [], 0, "block", 16
     )
     early_3 = move(block, lon_by(1))
     early_1 = move(block, lon_by(-1))
-    across = to_plane(from_2)
-
-    def late_piece(which, row=0):
-        return (which, row, (which, row + size - 16))
-
-    def early_piece(which, row):
-        return (which, row, (which, row + cut))
-
-    slabs = [(0, 0, middle, [(tag, 0, (tag, own_rows - 16)) for tag in range(4)])]
-    total, token = unpack(pos, total, plane, [block], slabs, span, "unpack_1")
-    hand_3, hand_1 = call(
-        hand_kernel, [slab(2 * first_rows)] * 2, (pos, early_3, early_1, token), [], 0, "hand", 16, held=1
-    )
+    (from_2,) = call(across_kernel, [slab(size)], (pos, half_3, half_1), [], 0, "across", 16)
+    pair_top, pair_bottom, _ = to_diagonal(pair_x, pair_y, size, field, "cross_2")
+    from_2x, from_2y = to_plane(from_2)
+    hand_3, hand_1 = call(hand_kernel, [slab(2 * first_rows)] * 2, (pos, early_3, early_1), [], 0, "hand", 16)
     early_2a = move(hand_3, lon_by(1))
     early_2b = move(hand_1, lon_by(-1))
-    unit = own_rows - 16
+
+    def late_piece(which, row=0):
+        return ((which, row + size - 16), (0, which, row))
+
+    def early_piece(which, row):
+        return ((which, row + cut), (0, which, row))
+
+    pieces = [((which, end), (0, which, 0)) for which in range(3)]
+    pieces.append(((4, end - own_cut), (0, 3, 0), (own_cut // span, 4, 0)))
+    total, token = unpack(
+        pos, total, [own, own_x, own_y, own_top, own_bottom], [block], [(0, 0, 27, pieces)], span, "unpack_1"
+    )
+    from_2top, from_2bottom, _ = to_diagonal(from_2x, from_2y, late_cut, token, "cross_3")
     slabs = [
-        (3, early, 27 - early, [late_piece(5)] + [late_piece(at) for at in range(3)]),
-        (1, early, 27 - early, [late_piece(6)] + [late_piece(at, size) for at in range(3)]),
-        (0, middle, 27 - middle, [(7, 0, (8, unit))] + [(at, 2 * size, (9 + at, unit)) for at in range(3)]),
-        (3, 0, early, [early_piece(3, tag * first_rows) for tag in range(4)]),
-        (1, 0, early, [early_piece(4, tag * first_rows) for tag in range(4)]),
+        (3, early, 27 - early, [late_piece(0), late_piece(2), late_piece(3), late_piece(4)]),
+        (1, early, 27 - early, [late_piece(1), late_piece(2, size), late_piece(3, size), late_piece(5)]),
+        (3, 0, early, [early_piece(6, tag * first_rows) for tag in range(4)]),
+        (1, 0, early, [early_piece(7, tag * first_rows) for tag in range(4)]),
     ]
     total, _ = unpack(
-        pos, total, both + [early_3, early_1, from_3, from_1, rest] + plane, [hand_3], slabs, span, "unpack_2"
-    )
+        pos,
+        total,
+        [from_3, from_1, pair_x, pair_y, pair_top, pair_bottom, early_3, early_1],
+        [hand_3],
+        slabs,
+        span,
+        "unpack_2",
+    )
+    pieces = [late_piece(2), late_piece(3), late_piece(4)]
+    pieces.append(((6, size - 16 - late_cut), (0, 5, 0), (late_cut // span, 6, 0)))
     slabs = [
         (2, 0, early, [early_piece(tag // 2, tag % 2 * first_rows) for tag in range(4)]),
-        (2, early, 27 - early, [late_piece(2 + tag) for tag in range(4)]),
+        (2, early, 27 - early, pieces),
     ]
-    total, _ = unpack(pos, total, [early_2a, early_2b, from_2] + across, [], slabs, span, "unpack_3")
+    total, _ = unpack(
+        pos,
+        total,
+        [early_2a, early_2b, from_2, from_2x, from_2y, from_2top, from_2bottom],
+        [],
+        slabs,
+        span,
+        "unpack_3",
+    )
     return (jnp.transpose(field, (3, 0, 1, 2)), jnp.transpose(total, (1, 0, 2)))
 
 

time: 147 us -> 154 us (1.048)
  waiting for transfers between devices: 51 us -> 54.2 us
  starting transfers between devices: 47.7 us -> 49.6 us
  Pallas kernels: 42.9 us -> 44.5 us
    ppermute x34 -> x37, waiting for transfers between devices: 51 us -> 54.2 us  [move(): return lax.ppermute(x, AXES, pairs)]
    pallas_call x10 -> x14, Pallas kernels: 14.6 us -> 16.9 us  [call(): pl.pallas_call(kernel, out_shape=outs, in_specs=[pl.BlockSpec(memory_spac...]
    ppermute x34 -> x37, starting transfers between devices: 47.7 us -> 49.6 us  [move(): return lax.ppermute(x, AXES, pairs)]
    unnamed x20 -> x16, local copies, waits for them, and re-layouts: 4.01 us -> 4 us
  transfers between devices with their start and end apart: 34 -> 37, of which waited for: 13 -> 14; matrix products, arithmetic and copies ran while one was open for 0% -> 0% of each run, Pallas kernels for 25% -> 25%
where the time goes in v14:
time: 154 us; the launch traced here: 153 us
  waiting for transfers between devices  54.2 us (35%)
  starting transfers between devices  49.6 us (32%)
  Pallas kernels  44.5 us (29%)
  local copies, waits for them, and re-layouts  4 us (3%)
    ppermute x37, waiting for transfers between devices, move(): return lax.ppermute(x, AXES, pairs)  54.2 us
    ppermute x37, starting transfers between devices, move(): return lax.ppermute(x, AXES, pairs)  49.6 us
    pallas_call x14, Pallas kernels, call(): pl.pallas_call(kernel, out_shape=outs, in_specs=[pl.BlockSpec(memory_spac...  16.9 us
    pallas_call x3, Pallas kernels, unpack(): pl.pallas_call(lambda *refs: unpack_kernel(*refs, slabs=slabs, count=len(...  13.2 us
    pallas_call x1, Pallas kernels, blocked_body(): pl.pallas_call(field_kernel, out_shape=jax.ShapeDtypeStruct((levels, heig...  9.51 us
    pallas_call x1, Pallas kernels, blocked_body(): pl.pallas_call(lines_kernel, out_shape=[jax.ShapeDtypeStruct((levels, row...  4.86 us
    unnamed x16, local copies, waits for them, and re-layouts  4 us
  transfers between devices with their start and end apart: 37, of which 14 were waited for; matrix products, arithmetic and copies ran while one was open for 0% of the time, Pallas kernels for 25%

profile of v14, /device:TPU:0, one launch (start us, length us, event | category | flops | bytes accessed | tf_op | source)
XLA Modules:
  0.0 153.5 jit_solution(10898296137210139898)
XLA Ops:
  0.7 1.0 copy-done.2
  1.7 1.0 copy-done.4
  2.7 0.8 pack.1
  4.2 3.1 %collective-permute-start = (bf16[416,128]{1,0:T(8,128)(2,1)S(1)}, bf16[416,128]{1,0:T(8,128)(2,1)S(1)}, u32[]{:S(2)}, u32[]{:S(2)}) collective-permute-start(bf16[416,128]{1,0:T(8,128)(2,1)S(1)} %get-tuple-element.36), channel_id=1, source_target_pairs={{0,1},{1,2},{2,3},{3,0},{4,5},{5,6},{6,7},{7,4},{8,9},{9,10},{10,1... | collective-permute-start | bytes 319496 | tf_op jit(solution)/shard_map/ppermute | solution.py:98
  7.3 1.5 collective-permute-start.7
  8.8 2.6 %collective-permute-start.1 = (bf16[384,128]{1,0:T(8,128)(2,1)S(1)}, bf16[384,128]{1,0:T(8,128)(2,1)S(1)}, u32[]{:S(2)}, u32[]{:S(2)}) collective-permute-start(bf16[384,128]{1,0:T(8,128)(2,1)S(1)} %get-tuple-element.37), channel_id=1, source_target_pairs={{0,2},{1,3},{2,0},{3,1},{4,6},{5,7},{6,4},{7,5},{8,10},{9,11},{10,... | collective-permute-start | bytes 294920 | tf_op jit(solution)/shard_map/ppermute | solution.py:98
  11.4 1.3 collective-permute-start.2
  12.7 5.6 %collective-permute-done.1.x2 = bf16[384,128]{1,0:T(8,128)(2,1)S(1)} collective-permute-done((bf16[384,128]{1,0:T(8,128)(2,1)S(1)}, bf16[384,128]{1,0:T(8,128)(2,1)S(1)}, u32[]{:S(2)}, u32[]{:S(2)}) %collective-permute-start.1) | collective-permute-done | bytes 98336 | tf_op jit(solution)/shard_map/ppermute | solution.py:98
  18.4 2.8 %collective-permute-start.11 = (bf16[384,128]{1,0:T(8,128)(2,1)S(1)}, bf16[384,128]{1,0:T(8,128)(2,1)S(1)}, u32[]{:S(2)}, u32[]{:S(2)}) collective-permute-start(bf16[384,128]{1,0:T(8,128)(2,1)S(1)} %get-tuple-element.44), channel_id=1, source_target_pairs={{0,12},{1,13},{2,14},{3,15},{4,8},{5,9},{6,10},{7,11},{8,4},{9,5},... | collective-permute-start | bytes 294920 | tf_op jit(solution)/shard_map/ppermute | solution.py:98
  21.8 1.2 collective-permute-start.3
  23.0 1.1 collective-permute-start.5
  24.1 1.3 collective-permute-start.4
  26.7 3.3 %collective-permute-start.9 = (bf16[2,768,128]{2,1,0:T(8,128)(2,1)S(1)}, bf16[2,768,128]{2,1,0:T(8,128)(2,1)S(1)}, u32[]{:S(2)}, u32[]{:S(2)}) collective-permute-start(bf16[2,768,128]{2,1,0:T(8,128)(2,1)S(1)} %pair_0.1.here), channel_id=1, source_target_pairs={{0,3},{1,0},{2,1},{3,2},{4,7},{5,4},{6,5},{7,6},{8,11},{9,8},{10,9... | collective-permute-start | bytes 1179656 | tf_op jit(solution)/shard_map/ppermute | solution.py:98
  29.9 5.2 %collective-permute-done.4.after.x_y = bf16[1536,128]{1,0:T(8,128)(2,1)S(1)} collective-permute-done((bf16[1536,128]{1,0:T(8,128)(2,1)S(1)}, bf16[1536,128]{1,0:T(8,128)(2,1)S(1)}, u32[]{:S(2)}, u32[]{:S(2)}) %collective-permute-start.4) | collective-permute-done | bytes 393248 | tf_op jit(solution)/shard_map/ppermute | solution.py:98
  35.2 8.2 %collective-permute-done.5.x_d = bf16[1600,128]{1,0:T(8,128)(2,1)S(1)} collective-permute-done((bf16[1600,128]{1,0:T(8,128)(2,1)S(1)}, bf16[1600,128]{1,0:T(8,128)(2,1)S(1)}, u32[]{:S(2)}, u32[]{:S(2)}) %collective-permute-start.5) | collective-permute-done | bytes 409632 | tf_op jit(solution)/shard_map/ppermute | solution.py:98
  43.4 1.2 collective-permute-done.9.east
  44.7 1.0 copy-done.3
  46.5 1.0 collective-permute-start.13
  47.5 2.9 %collective-permute-start.14 = (bf16[768,128]{1,0:T(8,128)(2,1)S(1)}, bf16[768,128]{1,0:T(8,128)(2,1)S(1)}, u32[]{:S(2)}, u32[]{:S(2)}) collective-permute-start(bf16[768,128]{1,0:T(8,128)(2,1)S(1)} %get-tuple-element.48), channel_id=1, source_target_pairs={{0,3},{1,0},{2,1},{3,2},{4,7},{5,4},{6,5},{7,6},{8,11},{9,8},{10,9... | collective-permute-start | bytes 589832 | tf_op jit(solution)/shard_map/ppermute | solution.py:98
  50.4 4.9 %lines.1 = (bf16[4,18,192,256]{3,2,1,0:T(8,128)(2,1)S(1)}, f32[27,256,512]{2,1,0:T(8,128)}) custom-call(s32[3]{0:T(128)S(1)} %pad_add_fusion.pos.refs_0_, bf16[1600,128]{1,0:T(8,128)(2,1)S(1)} %get-tuple-element.39.own.x_own, bf16[1600,128]{1,0:T(8,128)(2,1)S(1)} %collective-permute-done.3.x_x, bf16[1536,128]{1,0:T(8,128)(2,1)S(1)} %collective-permute-done.4.after.x_y, ...), custom_call_target="tpu_custom_call" | custom-call | bytes 1048576 | tf_op jit(solution)/shard_map/lines/pallas_call | solution.py:542
  55.3 0.8 collective-permute-done.13.one
  56.1 2.6 %collective-permute-done.14.two = bf16[768,128]{1,0:T(8,128)(2,1)S(1)} collective-permute-done((bf16[768,128]{1,0:T(8,128)(2,1)S(1)}, bf16[768,128]{1,0:T(8,128)(2,1)S(1)}, u32[]{:S(2)}, u32[]{:S(2)}) %collective-permute-start.14) | collective-permute-done | bytes 196640 | tf_op jit(solution)/shard_map/ppermute | solution.py:98
  59.9 1.2 collective-permute-done.15.s2
  61.1 8.6 %taps.1.held = f32[27,64,128]{2,1,0:T(8,128)S(1)} custom-call(s32[3]{0:T(128)S(1)} %pad_add_fusion.pos.refs_0_, bf16[4,18,192,256]{3,2,1,0:T(8,128)(2,1)S(1)} %get-tuple-element.46.after.xs, bf16[6,768,128]{2,1,0:T(8,128)(2,1)S(1)} %get-tuple-element.47.g, bf16[6,768,128]{2,1,0:T(8,128)(2,1)S(1)} %collective-permute-done.12.s, ...), custom_call_target="tpu_custom_call" | custom-call | flops 5435817984 | bytes 11108352 | tf_op jit(solution)/shard_map/taps/pallas_call | solution.py:116
  69.7 0.9 code.1
  70.6 1.3 collective-permute-start.19
  71.9 1.8 %collective-permute-start.20 = (bf16[1744,128]{1,0:T(8,128)(2,1)S(1)}, bf16[1744,128]{1,0:T(8,128)(2,1)S(1)}, u32[]{:S(2)}, u32[]{:S(2)}) collective-permute-start(bf16[1744,128]{1,0:T(8,128)(2,1)S(1)} %get-tuple-element.51.after.own.refs_1_), channel_id=1, source_target_pairs={{0,8},{1,9},{2,10},{3,11},{4,12},{5,13},{6,14},{7,15},{8,0},{9,1},... | collective-permute-start | bytes 1339400 | tf_op jit(solution)/shard_map/ppermute | solution.py:98
  74.2 3.2 %collective-permute-start.18 = (bf16[1360,128]{1,0:T(8,128)(2,1)S(1)}, bf16[1360,128]{1,0:T(8,128)(2,1)S(1)}, u32[]{:S(2)}, u32[]{:S(2)}) collective-permute-start(bf16[1360,128]{1,0:T(8,128)(2,1)S(1)} %get-tuple-element.50), channel_id=1, source_target_pairs={{0,3},{1,0},{2,1},{3,2},{4,7},{5,4},{6,5},{7,6},{8,11},{9,8},{10,9... | collective-permute-start | bytes 1044488 | tf_op jit(solution)/shard_map/ppermute | solution.py:98
  77.5 5.5 %collective-permute-done.19.by_x.x.refs_2_ = bf16[1744,128]{1,0:T(8,128)(2,1)S(1)} collective-permute-done((bf16[1744,128]{1,0:T(8,128)(2,1)S(1)}, bf16[1744,128]{1,0:T(8,128)(2,1)S(1)}, u32[]{:S(2)}, u32[]{:S(2)}) %collective-permute-start.19) | collective-permute-done | bytes 446496 | tf_op jit(solution)/shard_map/ppermute | solution.py:98
  82.9 1.0 collective-permute-done.20.by_y.y.refs_3_
  84.5 2.0 %collective-permute-done.17.west.refs_1_ = bf16[1360,128]{1,0:T(8,128)(2,1)S(1)} collective-permute-done((bf16[1360,128]{1,0:T(8,128)(2,1)S(1)}, bf16[1360,128]{1,0:T(8,128)(2,1)S(1)}, u32[]{:S(2)}, u32[]{:S(2)}) %collective-permute-start.17) | collective-permute-done | bytes 348192 | tf_op jit(solution)/shard_map/ppermute | solution.py:98
  86.5 4.5 %collective-permute-done.18.east.refs_2_ = bf16[1360,128]{1,0:T(8,128)(2,1)S(1)} collective-permute-done((bf16[1360,128]{1,0:T(8,128)(2,1)S(1)}, bf16[1360,128]{1,0:T(8,128)(2,1)S(1)}, u32[]{:S(2)}, u32[]{:S(2)}) %collective-permute-start.18) | collective-permute-done | bytes 348192 | tf_op jit(solution)/shard_map/ppermute | solution.py:98
  91.7 0.8 collective-permute-start.33
  92.5 1.3 collective-permute-start.21
  94.1 2.1 %collective-permute-start.28 = (bf16[688,128]{1,0:T(8,128)(2,1)S(1)}, bf16[688,128]{1,0:T(8,128)(2,1)S(1)}, u32[]{:S(2)}, u32[]{:S(2)}) collective-permute-start(bf16[688,128]{1,0:T(8,128)(2,1)S(1)} %get-tuple-element.58), channel_id=1, source_target_pairs={{0,3},{1,0},{2,1},{3,2},{4,7},{5,4},{6,5},{7,6},{8,11},{9,8},{10,9... | collective-permute-start | bytes 528392 | tf_op jit(solution)/shard_map/ppermute | solution.py:98
  96.1 7.5 %collective-permute-done.27.half_3 = bf16[672,128]{1,0:T(8,128)(2,1)S(1)} collective-permute-done((bf16[672,128]{1,0:T(8,128)(2,1)S(1)}, bf16[672,128]{1,0:T(8,128)(2,1)S(1)}, u32[]{:S(2)}, u32[]{:S(2)}) %collective-permute-start.27) | collective-permute-done | bytes 172064 | tf_op jit(solution)/shard_map/ppermute | solution.py:98
  103.6 1.8 %collective-permute-start.34 = (bf16[2720,128]{1,0:T(8,128)(2,1)S(1)}, bf16[2720,128]{1,0:T(8,128)(2,1)S(1)}, u32[]{:S(2)}, u32[]{:S(2)}) collective-permute-start(bf16[2720,128]{1,0:T(8,128)(2,1)S(1)} %get-tuple-element.53.after), channel_id=1, source_target_pairs={{0,8},{1,9},{2,10},{3,11},{4,12},{5,13},{6,14},{7,15},{8,0},{9,1},... | collective-permute-start | bytes 2088968 | tf_op jit(solution)/shard_map/ppermute | solution.py:98
  107.3 7.9 %collective-permute-done.21.top.refs_4_ = bf16[896,128]{1,0:T(8,128)(2,1)S(1)} collective-permute-done((bf16[896,128]{1,0:T(8,128)(2,1)S(1)}, bf16[896,128]{1,0:T(8,128)(2,1)S(1)}, u32[]{:S(2)}, u32[]{:S(2)}) %collective-permute-start.21) | collective-permute-done | bytes 229408 | tf_op jit(solution)/shard_map/ppermute | solution.py:98
  115.8 1.1 collective-permute-start.23
  116.8 2.8 %collective-permute-start.24 = (bf16[1600,128]{1,0:T(8,128)(2,1)S(1)}, bf16[1600,128]{1,0:T(8,128)(2,1)S(1)}, u32[]{:S(2)}, u32[]{:S(2)}) collective-permute-start(bf16[1600,128]{1,0:T(8,128)(2,1)S(1)} %block.1.refs_6_), channel_id=1, source_target_pairs={{0,3},{1,0},{2,1},{3,2},{4,7},{5,4},{6,5},{7,6},{8,11},{9,8},{10,9... | collective-permute-start | bytes 1228808 | tf_op jit(solution)/shard_map/ppermute | solution.py:98
  119.7 9.5 %field.1.after = bf16[4,4,48,256]{3,2,1,0:T(8,128)(2,1)} custom-call(s32[3]{0:T(128)S(1)} %pad_add_fusion.pos.refs_0_, bf16[2720,128]{1,0:T(8,128)(2,1)S(1)} %get-tuple-element.53.after, bf16[4,6,64,256]{3,2,1,0:T(8,128)(2,1)S(1)} %get-tuple-element.49.mine, bf16[4,6,64,256]{3,2,1,0:T(8,128)(2,1)S(1)} %collective-permute-done.16.after.theirs, ...), custom_call_target="tpu_custom_call" | custom-call | flops 10871635968 | bytes 7077888 | tf_op jit(solution)/shard_map/field/pallas_call | solution.py:595
  129.2 1.0 copy-done.5
  133.9 3.1 %collective-permute-start.26 = (bf16[800,128]{1,0:T(8,128)(2,1)S(1)}, bf16[800,128]{1,0:T(8,128)(2,1)S(1)}, u32[]{:S(2)}, u32[]{:S(2)}) collective-permute-start(bf16[800,128]{1,0:T(8,128)(2,1)S(1)} %get-tuple-element.56), channel_id=1, source_target_pairs={{0,3},{1,0},{2,1},{3,2},{4,7},{5,4},{6,5},{7,6},{8,11},{9,8},{10,9... | collective-permute-start | bytes 614408 | tf_op jit(solution)/shard_map/ppermute | solution.py:98
  137.0 3.1 %unpack_1.1 = (f32[27,256,512]{2,1,0:T(8,128)}, f32[8,128]{1,0:T(8,128)S(1)}) custom-call(s32[3]{0:T(128)S(1)} %pad_add_fusion.pos.refs_0_, bf16[1744,128]{1,0:T(8,128)(2,1)S(1)} %get-tuple-element.51.after.own.refs_1_, bf16[1744,128]{1,0:T(8,128)(2,1)S(1)} %collective-permute-done.19.by_x.x.refs_2_, ...), custom_call_target="tpu_custom_call", output_to_operand_aliasing={{0}: (7, {})} | custom-call | bytes 4194304 | tf_op jit(solution)/shard_map/unpack_1/pallas_call | solution.py:408
  140.8 1.1 collective-permute-start.32
  141.9 1.3 collective-permute-start.31
  143.2 6.4 %unpack_2.1 = (f32[27,256,512]{2,1,0:T(8,128)}, f32[8,128]{1,0:T(8,128)}) custom-call(s32[3]{0:T(128)S(1)} %pad_add_fusion.pos.refs_0_, bf16[1360,128]{1,0:T(8,128)(2,1)S(1)} %collective-permute-done.17.west.refs_1_, bf16[1360,128]{1,0:T(8,128)(2,1)S(1)} %collective-permute-done.18.east.refs_2_, ...), custom_call_target="tpu_custom_call", output_to_operand_aliasing={{0}: (10, {})} | custom-call | bytes 4194304 | tf_op jit(solution)/shard_map/unpack_2/pallas_call | solution.py:408
  149.6 3.7 %unpack_3.1 = (f32[27,256,512]{2,1,0:T(8,128)}, f32[8,128]{1,0:T(8,128)}) custom-call(s32[3]{0:T(128)S(1)} %pad_add_fusion.pos.refs_0_, bf16[800,128]{1,0:T(8,128)(2,1)S(1)} %collective-permute-done.25.refs_1_, bf16[800,128]{1,0:T(8,128)(2,1)S(1)} %collective-permute-done.26.refs_2_, ...), custom_call_target="tpu_custom_call", output_to_operand_aliasing={{0}: (8, {})} | custom-call | bytes 4194304 | tf_op jit(solution)/shard_map/unpack_3/pallas_call | solution.py:408
  (63 shorter events, 13.5 us)
Async XLA Ops:
  0.7 1.0 copy-start.2
  1.7 1.0 copy-start.4
  3.6 19.4 %collective-permute-start.6 = (bf16[768,128]{1,0:T(8,128)(2,1)S(1)}, bf16[768,128]{1,0:T(8,128)(2,1)S(1)}, u32[]{:S(2)}, u32[]{:S(2)}) collective-permute-start(bf16[768,128]{1,0:T(8,128)(2,1)S(1)} %get-tuple-element.41), channel_id=1, source_target_pairs={{0,0},{1,1},{2,2},{3,3},{4,4},{5,5},{6,6},{7,7},{8,16},{9,17},{10,... | collective-permute-start | bytes 589832 | tf_op jit(solution)/shard_map/ppermute | solution.py:98
  4.2 14.1 %collective-permute-start = (bf16[416,128]{1,0:T(8,128)(2,1)S(1)}, bf16[416,128]{1,0:T(8,128)(2,1)S(1)}, u32[]{:S(2)}, u32[]{:S(2)}) collective-permute-start(bf16[416,128]{1,0:T(8,128)(2,1)S(1)} %get-tuple-element.36), channel_id=1, source_target_pairs={{0,1},{1,2},{2,3},{3,0},{4,5},{5,6},{6,7},{7,4},{8,9},{9,10},{10,1... | collective-permute-start | bytes 319496 | tf_op jit(solution)/shard_map/ppermute | solution.py:98
  7.3 16.7 %collective-permute-start.7 = (bf16[768,128]{1,0:T(8,128)(2,1)S(1)}, bf16[768,128]{1,0:T(8,128)(2,1)S(1)}, u32[]{:S(2)}, u32[]{:S(2)}) collective-permute-start(bf16[768,128]{1,0:T(8,128)(2,1)S(1)} %get-tuple-element.42), channel_id=1, source_target_pairs={{0,4},{1,5},{2,6},{3,7},{4,0},{5,1},{6,2},{7,3},{8,20},{9,21},{10,... | collective-permute-start | bytes 589832 | tf_op jit(solution)/shard_map/ppermute | solution.py:98
  8.8 9.6 %collective-permute-start.1 = (bf16[384,128]{1,0:T(8,128)(2,1)S(1)}, bf16[384,128]{1,0:T(8,128)(2,1)S(1)}, u32[]{:S(2)}, u32[]{:S(2)}) collective-permute-start(bf16[384,128]{1,0:T(8,128)(2,1)S(1)} %get-tuple-element.37), channel_id=1, source_target_pairs={{0,2},{1,3},{2,0},{3,1},{4,6},{5,7},{6,4},{7,5},{8,10},{9,11},{10,... | collective-permute-start | bytes 294920 | tf_op jit(solution)/shard_map/ppermute | solution.py:98
  11.4 9.8 %collective-permute-start.2 = (bf16[416,128]{1,0:T(8,128)(2,1)S(1)}, bf16[416,128]{1,0:T(8,128)(2,1)S(1)}, u32[]{:S(2)}, u32[]{:S(2)}) collective-permute-start(bf16[416,128]{1,0:T(8,128)(2,1)S(1)} %get-tuple-element.38), channel_id=1, source_target_pairs={{0,3},{1,0},{2,1},{3,2},{4,7},{5,4},{6,5},{7,6},{8,11},{9,8},{10,9... | collective-permute-start | bytes 319496 | tf_op jit(solution)/shard_map/ppermute | solution.py:98
  18.4 7.6 %collective-permute-start.10 = (bf16[384,128]{1,0:T(8,128)(2,1)S(1)}, bf16[384,128]{1,0:T(8,128)(2,1)S(1)}, u32[]{:S(2)}, u32[]{:S(2)}) collective-permute-start(bf16[384,128]{1,0:T(8,128)(2,1)S(1)} %get-tuple-element.43), channel_id=1, source_target_pairs={{0,4},{1,5},{2,6},{3,7},{4,0},{5,1},{6,2},{7,3},{8,12},{9,13},{10,... | collective-permute-start | bytes 294920 | tf_op jit(solution)/shard_map/ppermute | solution.py:98
  18.4 8.3 %collective-permute-start.11 = (bf16[384,128]{1,0:T(8,128)(2,1)S(1)}, bf16[384,128]{1,0:T(8,128)(2,1)S(1)}, u32[]{:S(2)}, u32[]{:S(2)}) collective-permute-start(bf16[384,128]{1,0:T(8,128)(2,1)S(1)} %get-tuple-element.44), channel_id=1, source_target_pairs={{0,12},{1,13},{2,14},{3,15},{4,8},{5,9},{6,10},{7,11},{8,4},{9,5},... | collective-permute-start | bytes 294920 | tf_op jit(solution)/shard_map/ppermute | solution.py:98
  21.8 13.4 %collective-permute-start.3 = (bf16[1600,128]{1,0:T(8,128)(2,1)S(1)}, bf16[1600,128]{1,0:T(8,128)(2,1)S(1)}, u32[]{:S(2)}, u32[]{:S(2)}) collective-permute-start(bf16[1600,128]{1,0:T(8,128)(2,1)S(1)} %get-tuple-element.39.own.x_own), channel_id=1, source_target_pairs={{0,4},{1,5},{2,6},{3,7},{4,0},{5,1},{6,2},{7,3},{8,12},{9,13},{10,... | collective-permute-start | bytes 1228808 | tf_op jit(solution)/shard_map/ppermute | solution.py:98
  23.0 20.4 %collective-permute-start.5 = (bf16[1600,128]{1,0:T(8,128)(2,1)S(1)}, bf16[1600,128]{1,0:T(8,128)(2,1)S(1)}, u32[]{:S(2)}, u32[]{:S(2)}) collective-permute-start(bf16[1600,128]{1,0:T(8,128)(2,1)S(1)} %get-tuple-element.39.own.x_own), channel_id=1, source_target_pairs={{0,12},{1,13},{2,14},{3,15},{4,8},{5,9},{6,10},{7,11},{8,4},{9,5},... | collective-permute-start | bytes 1228808 | tf_op jit(solution)/shard_map/ppermute | solution.py:98
  24.1 11.1 %collective-permute-start.4 = (bf16[1536,128]{1,0:T(8,128)(2,1)S(1)}, bf16[1536,128]{1,0:T(8,128)(2,1)S(1)}, u32[]{:S(2)}, u32[]{:S(2)}) collective-permute-start(bf16[1536,128]{1,0:T(8,128)(2,1)S(1)} %get-tuple-element.40), channel_id=1, source_target_pairs={{0,8},{1,9},{2,10},{3,11},{4,12},{5,13},{6,14},{7,15},{8,0},{9,1},... | collective-permute-start | bytes 1179656 | tf_op jit(solution)/shard_map/ppermute | solution.py:98
  26.0 17.5 %collective-permute-start.8 = (bf16[2,768,128]{2,1,0:T(8,128)(2,1)S(1)}, bf16[2,768,128]{2,1,0:T(8,128)(2,1)S(1)}, u32[]{:S(2)}, u32[]{:S(2)}) collective-permute-start(bf16[2,768,128]{2,1,0:T(8,128)(2,1)S(1)} %pair_0.1.here), channel_id=1, source_target_pairs={{0,1},{1,2},{2,3},{3,0},{4,5},{5,6},{6,7},{7,4},{8,9},{9,10},{10,1... | collective-permute-start | bytes 1179656 | tf_op jit(solution)/shard_map/ppermute | solution.py:98
  26.7 18.0 %collective-permute-start.9 = (bf16[2,768,128]{2,1,0:T(8,128)(2,1)S(1)}, bf16[2,768,128]{2,1,0:T(8,128)(2,1)S(1)}, u32[]{:S(2)}, u32[]{:S(2)}) collective-permute-start(bf16[2,768,128]{2,1,0:T(8,128)(2,1)S(1)} %pair_0.1.here), channel_id=1, source_target_pairs={{0,3},{1,0},{2,1},{3,2},{4,7},{5,4},{6,5},{7,6},{8,11},{9,8},{10,9... | collective-permute-start | bytes 1179656 | tf_op jit(solution)/shard_map/ppermute | solution.py:98
  44.7 1.0 copy-start.3
  46.4 14.7 %collective-permute-start.12 = (bf16[6,768,128]{2,1,0:T(8,128)(2,1)S(1)}, bf16[6,768,128]{2,1,0:T(8,128)(2,1)S(1)}, u32[]{:S(2)}, u32[]{:S(2)}) collective-permute-start(bf16[6,768,128]{2,1,0:T(8,128)(2,1)S(1)} %get-tuple-element.47.g), channel_id=1, source_target_pairs={{0,16},{1,17},{2,18},{3,19},{4,20},{5,21},{6,22},{7,23},{8,24},{9,... | collective-permute-start | bytes 3538952 | tf_op jit(solution)/shard_map/ppermute | solution.py:98
  46.5 9.6 %collective-permute-start.13 = (bf16[768,128]{1,0:T(8,128)(2,1)S(1)}, bf16[768,128]{1,0:T(8,128)(2,1)S(1)}, u32[]{:S(2)}, u32[]{:S(2)}) collective-permute-start(bf16[768,128]{1,0:T(8,128)(2,1)S(1)} %get-tuple-element.45.after), channel_id=1, source_target_pairs={{0,1},{1,2},{2,3},{3,0},{4,5},{5,6},{6,7},{7,4},{8,9},{9,10},{10,1... | collective-permute-start | bytes 589832 | tf_op jit(solution)/shard_map/ppermute | solution.py:98
  47.5 11.2 %collective-permute-start.14 = (bf16[768,128]{1,0:T(8,128)(2,1)S(1)}, bf16[768,128]{1,0:T(8,128)(2,1)S(1)}, u32[]{:S(2)}, u32[]{:S(2)}) collective-permute-start(bf16[768,128]{1,0:T(8,128)(2,1)S(1)} %get-tuple-element.48), channel_id=1, source_target_pairs={{0,3},{1,0},{2,1},{3,2},{4,7},{5,4},{6,5},{7,6},{8,11},{9,8},{10,9... | collective-permute-start | bytes 589832 | tf_op jit(solution)/shard_map/ppermute | solution.py:98
  59.3 60.4 %slice-start = ((s8[7077888]{0:T(1024)(128)(4,1)}), s8[4194304]{0:T(1024)(128)(4,1)S(1)}, s32[]{:S(2)}) async-start(s8[7077888]{0:T(1024)(128)(4,1)} %bitcast.12), calls=%async_computation | async-start | bytes 8388608
  59.3 1.8 %collective-permute-start.15 = (bf16[2,768,128]{2,1,0:T(8,128)(2,1)S(1)}, bf16[2,768,128]{2,1,0:T(8,128)(2,1)S(1)}, u32[]{:S(2)}, u32[]{:S(2)}) collective-permute-start(bf16[2,768,128]{2,1,0:T(8,128)(2,1)S(1)} %pair.1.g2), channel_id=1, source_target_pairs={{0,16},{1,17},{2,18},{3,19},{4,20},{5,21},{6,22},{7,23},{8,24},{9,... | collective-permute-start | bytes 1179656 | tf_op jit(solution)/shard_map/ppermute | solution.py:98
  59.4 60.3 %slice-start.1 = ((s8[7077888]{0:T(1024)(128)(4,1)}), s8[2883584]{0:T(1024)(128)(4,1)S(1)}, s32[]{:S(2)}) async-start(s8[7077888]{0:T(1024)(128)(4,1)} %bitcast.12), calls=%async_computation.1 | async-start | bytes 5767168
  59.4 10.3 %collective-permute-start.16 = (bf16[4,6,64,256]{3,2,1,0:T(8,128)(2,1)S(1)}, bf16[4,6,64,256]{3,2,1,0:T(8,128)(2,1)S(1)}, u32[]{:S(2)}, u32[]{:S(2)}) collective-permute-start(bf16[4,6,64,256]{3,2,1,0:T(8,128)(2,1)S(1)} %get-tuple-element.49.mine), channel_id=1, source_target_pairs={{0,16},{1,17},{2,18},{3,19},{4,20},{5,21},{6,22},{7,23},{8,24},{9,... | collective-permute-start | bytes 2359304 | tf_op jit(solution)/shard_map/ppermute | solution.py:98
  70.6 12.3 %collective-permute-start.19 = (bf16[1744,128]{1,0:T(8,128)(2,1)S(1)}, bf16[1744,128]{1,0:T(8,128)(2,1)S(1)}, u32[]{:S(2)}, u32[]{:S(2)}) collective-permute-start(bf16[1744,128]{1,0:T(8,128)(2,1)S(1)} %get-tuple-element.51.after.own.refs_1_), channel_id=1, source_target_pairs={{0,4},{1,5},{2,6},{3,7},{4,0},{5,1},{6,2},{7,3},{8,12},{9,13},{10,... | collective-permute-start | bytes 1339400 | tf_op jit(solution)/shard_map/ppermute | solution.py:98
  71.9 12.0 %collective-permute-start.20 = (bf16[1744,128]{1,0:T(8,128)(2,1)S(1)}, bf16[1744,128]{1,0:T(8,128)(2,1)S(1)}, u32[]{:S(2)}, u32[]{:S(2)}) collective-permute-start(bf16[1744,128]{1,0:T(8,128)(2,1)S(1)} %get-tuple-element.51.after.own.refs_1_), channel_id=1, source_target_pairs={{0,8},{1,9},{2,10},{3,11},{4,12},{5,13},{6,14},{7,15},{8,0},{9,1},... | collective-permute-start | bytes 1339400 | tf_op jit(solution)/shard_map/ppermute | solution.py:98
  73.6 12.9 %collective-permute-start.17 = (bf16[1360,128]{1,0:T(8,128)(2,1)S(1)}, bf16[1360,128]{1,0:T(8,128)(2,1)S(1)}, u32[]{:S(2)}, u32[]{:S(2)}) collective-permute-start(bf16[1360,128]{1,0:T(8,128)(2,1)S(1)} %get-tuple-element.50), channel_id=1, source_target_pairs={{0,1},{1,2},{2,3},{3,0},{4,5},{5,6},{6,7},{7,4},{8,9},{9,10},{10,1... | collective-permute-start | bytes 1044488 | tf_op jit(solution)/shard_map/ppermute | solution.py:98
  74.2 16.8 %collective-permute-start.18 = (bf16[1360,128]{1,0:T(8,128)(2,1)S(1)}, bf16[1360,128]{1,0:T(8,128)(2,1)S(1)}, u32[]{:S(2)}, u32[]{:S(2)}) collective-permute-start(bf16[1360,128]{1,0:T(8,128)(2,1)S(1)} %get-tuple-element.50), channel_id=1, source_target_pairs={{0,3},{1,0},{2,1},{3,2},{4,7},{5,4},{6,5},{7,6},{8,11},{9,8},{10,9... | collective-permute-start | bytes 1044488 | tf_op jit(solution)/shard_map/ppermute | solution.py:98
  91.7 25.2 %collective-permute-start.33 = (bf16[2720,128]{1,0:T(8,128)(2,1)S(1)}, bf16[2720,128]{1,0:T(8,128)(2,1)S(1)}, u32[]{:S(2)}, u32[]{:S(2)}) collective-permute-start(bf16[2720,128]{1,0:T(8,128)(2,1)S(1)} %get-tuple-element.53.after), channel_id=1, source_target_pairs={{0,4},{1,5},{2,6},{3,7},{4,0},{5,1},{6,2},{7,3},{8,12},{9,13},{10,... | collective-permute-start | bytes 2088968 | tf_op jit(solution)/shard_map/ppermute | solution.py:98
  92.5 22.7 %collective-permute-start.21 = (bf16[896,128]{1,0:T(8,128)(2,1)S(1)}, bf16[896,128]{1,0:T(8,128)(2,1)S(1)}, u32[]{:S(2)}, u32[]{:S(2)}) collective-permute-start(bf16[896,128]{1,0:T(8,128)(2,1)S(1)} %get-tuple-element.52.after), channel_id=1, source_target_pairs={{0,4},{1,5},{2,6},{3,7},{4,0},{5,1},{6,2},{7,3},{8,12},{9,13},{10,... | collective-permute-start | bytes 688136 | tf_op jit(solution)/shard_map/ppermute | solution.py:98
  93.8 13.0 %collective-permute-start.22 = (bf16[848,128]{1,0:T(8,128)(2,1)S(1)}, bf16[848,128]{1,0:T(8,128)(2,1)S(1)}, u32[]{:S(2)}, u32[]{:S(2)}) collective-permute-start(bf16[848,128]{1,0:T(8,128)(2,1)S(1)} %get-tuple-element.54), channel_id=1, source_target_pairs={{0,8},{1,9},{2,10},{3,11},{4,12},{5,13},{6,14},{7,15},{8,0},{9,1},... | collective-permute-start | bytes 651272 | tf_op jit(solution)/shard_map/ppermute | solution.py:98
  94.1 11.4 %collective-permute-start.28 = (bf16[688,128]{1,0:T(8,128)(2,1)S(1)}, bf16[688,128]{1,0:T(8,128)(2,1)S(1)}, u32[]{:S(2)}, u32[]{:S(2)}) collective-permute-start(bf16[688,128]{1,0:T(8,128)(2,1)S(1)} %get-tuple-element.58), channel_id=1, source_target_pairs={{0,3},{1,0},{2,1},{3,2},{4,7},{5,4},{6,5},{7,6},{8,11},{9,8},{10,9... | collective-permute-start | bytes 528392 | tf_op jit(solution)/shard_map/ppermute | solution.py:98
  96.1 7.5 %collective-permute-start.27 = (bf16[672,128]{1,0:T(8,128)(2,1)S(1)}, bf16[672,128]{1,0:T(8,128)(2,1)S(1)}, u32[]{:S(2)}, u32[]{:S(2)}) collective-permute-start(bf16[672,128]{1,0:T(8,128)(2,1)S(1)} %get-tuple-element.57), channel_id=1, source_target_pairs={{0,1},{1,2},{2,3},{3,0},{4,5},{5,6},{6,7},{7,4},{8,9},{9,10},{10,1... | collective-permute-start | bytes 516104 | tf_op jit(solution)/shard_map/ppermute | solution.py:98
  103.6 25.5 %collective-permute-start.34 = (bf16[2720,128]{1,0:T(8,128)(2,1)S(1)}, bf16[2720,128]{1,0:T(8,128)(2,1)S(1)}, u32[]{:S(2)}, u32[]{:S(2)}) collective-permute-start(bf16[2720,128]{1,0:T(8,128)(2,1)S(1)} %get-tuple-element.53.after), channel_id=1, source_target_pairs={{0,8},{1,9},{2,10},{3,11},{4,12},{5,13},{6,14},{7,15},{8,0},{9,1},... | collective-permute-start | bytes 2088968 | tf_op jit(solution)/shard_map/ppermute | solution.py:98
  106.0 27.9 %collective-permute-start.29 = (bf16[1360,128]{1,0:T(8,128)(2,1)S(1)}, bf16[1360,128]{1,0:T(8,128)(2,1)S(1)}, u32[]{:S(2)}, u32[]{:S(2)}) collective-permute-start(bf16[1360,128]{1,0:T(8,128)(2,1)S(1)} %across.1.refs_3_), channel_id=1, source_target_pairs={{0,4},{1,5},{2,6},{3,7},{4,0},{5,1},{6,2},{7,3},{8,12},{9,13},{10,... | collective-permute-start | bytes 1044488 | tf_op jit(solution)/shard_map/ppermute | solution.py:98
  106.8 33.4 %collective-permute-start.30 = (bf16[1360,128]{1,0:T(8,128)(2,1)S(1)}, bf16[1360,128]{1,0:T(8,128)(2,1)S(1)}, u32[]{:S(2)}, u32[]{:S(2)}) collective-permute-start(bf16[1360,128]{1,0:T(8,128)(2,1)S(1)} %across.1.refs_3_), channel_id=1, source_target_pairs={{0,8},{1,9},{2,10},{3,11},{4,12},{5,13},{6,14},{7,15},{8,0},{9,1},... | collective-permute-start | bytes 1044488 | tf_op jit(solution)/shard_map/ppermute | solution.py:98
  115.8 15.8 %collective-permute-start.23 = (bf16[1600,128]{1,0:T(8,128)(2,1)S(1)}, bf16[1600,128]{1,0:T(8,128)(2,1)S(1)}, u32[]{:S(2)}, u32[]{:S(2)}) collective-permute-start(bf16[1600,128]{1,0:T(8,128)(2,1)S(1)} %block.1.refs_6_), channel_id=1, source_target_pairs={{0,1},{1,2},{2,3},{3,0},{4,5},{5,6},{6,7},{7,4},{8,9},{9,10},{10,1... | collective-permute-start | bytes 1228808 | tf_op jit(solution)/shard_map/ppermute | solution.py:98
  116.8 12.3 %copy-start = (bf16[2720,128]{1,0:T(8,128)(2,1)}, bf16[2720,128]{1,0:T(8,128)(2,1)S(1)}, u32[]{:S(2)}) copy-start(bf16[2720,128]{1,0:T(8,128)(2,1)S(1)} %collective-permute-done.33.by_x.refs_3_) | copy-start | bytes 2088964
  116.8 15.7 %collective-permute-start.24 = (bf16[1600,128]{1,0:T(8,128)(2,1)S(1)}, bf16[1600,128]{1,0:T(8,128)(2,1)S(1)}, u32[]{:S(2)}, u32[]{:S(2)}) collective-permute-start(bf16[1600,128]{1,0:T(8,128)(2,1)S(1)} %block.1.refs_6_), channel_id=1, source_target_pairs={{0,3},{1,0},{2,1},{3,2},{4,7},{5,4},{6,5},{7,6},{8,11},{9,8},{10,9... | collective-permute-start | bytes 1228808 | tf_op jit(solution)/shard_map/ppermute | solution.py:98
  129.2 1.0 copy-start.5
  130.2 13.0 %copy-start.1 = (bf16[2720,128]{1,0:T(8,128)(2,1)}, bf16[2720,128]{1,0:T(8,128)(2,1)S(1)}, u32[]{:S(2)}) copy-start(bf16[2720,128]{1,0:T(8,128)(2,1)S(1)} %collective-permute-done.34.by_y.refs_4_) | copy-start | bytes 2088964
  130.8 11.1 %collective-permute-start.35 = (bf16[1360,128]{1,0:T(8,128)(2,1)S(1)}, bf16[1360,128]{1,0:T(8,128)(2,1)S(1)}, u32[]{:S(2)}, u32[]{:S(2)}) collective-permute-start(bf16[1360,128]{1,0:T(8,128)(2,1)S(1)} %get-tuple-element.63), channel_id=1, source_target_pairs={{0,4},{1,5},{2,6},{3,7},{4,0},{5,1},{6,2},{7,3},{8,12},{9,13},{10,... | collective-permute-start | bytes 1044488 | tf_op jit(solution)/shard_map/ppermute | solution.py:98
  131.6 11.6 %collective-permute-start.36 = (bf16[1360,128]{1,0:T(8,128)(2,1)S(1)}, bf16[1360,128]{1,0:T(8,128)(2,1)S(1)}, u32[]{:S(2)}, u32[]{:S(2)}) collective-permute-start(bf16[1360,128]{1,0:T(8,128)(2,1)S(1)} %get-tuple-element.64), channel_id=1, source_target_pairs={{0,8},{1,9},{2,10},{3,11},{4,12},{5,13},{6,14},{7,15},{8,0},{9,1},... | collective-permute-start | bytes 1044488 | tf_op jit(solution)/shard_map/ppermute | solution.py:98
  133.1 16.4 %collective-permute-start.25 = (bf16[800,128]{1,0:T(8,128)(2,1)S(1)}, bf16[800,128]{1,0:T(8,128)(2,1)S(1)}, u32[]{:S(2)}, u32[]{:S(2)}) collective-permute-start(bf16[800,128]{1,0:T(8,128)(2,1)S(1)} %get-tuple-element.55.refs_9_), channel_id=1, source_target_pairs={{0,1},{1,2},{2,3},{3,0},{4,5},{5,6},{6,7},{7,4},{8,9},{9,10},{10,1... | collective-permute-start | bytes 614408 | tf_op jit(solution)/shard_map/ppermute | solution.py:98
  133.9 15.6 %collective-permute-start.26 = (bf16[800,128]{1,0:T(8,128)(2,1)S(1)}, bf16[800,128]{1,0:T(8,128)(2,1)S(1)}, u32[]{:S(2)}, u32[]{:S(2)}) collective-permute-start(bf16[800,128]{1,0:T(8,128)(2,1)S(1)} %get-tuple-element.56), channel_id=1, source_target_pairs={{0,3},{1,0},{2,1},{3,2},{4,7},{5,4},{6,5},{7,6},{8,11},{9,8},{10,9... | collective-permute-start | bytes 614408 | tf_op jit(solution)/shard_map/ppermute | solution.py:98
  140.8 8.8 %collective-permute-start.32 = (bf16[720,128]{1,0:T(8,128)(2,1)S(1)}, bf16[720,128]{1,0:T(8,128)(2,1)S(1)}, u32[]{:S(2)}, u32[]{:S(2)}) collective-permute-start(bf16[720,128]{1,0:T(8,128)(2,1)S(1)} %get-tuple-element.62), channel_id=1, source_target_pairs={{0,8},{1,9},{2,10},{3,11},{4,12},{5,13},{6,14},{7,15},{8,0},{9,1},... | collective-permute-start | bytes 552968 | tf_op jit(solution)/shard_map/ppermute | solution.py:98
  141.9 7.6 %collective-permute-start.31 = (bf16[640,128]{1,0:T(8,128)(2,1)S(1)}, bf16[640,128]{1,0:T(8,128)(2,1)S(1)}, u32[]{:S(2)}, u32[]{:S(2)}) collective-permute-start(bf16[640,128]{1,0:T(8,128)(2,1)S(1)} %get-tuple-element.61), channel_id=1, source_target_pairs={{0,4},{1,5},{2,6},{3,7},{4,0},{5,1},{6,2},{7,3},{8,12},{9,13},{10,... | collective-permute-start | bytes 491528 | tf_op jit(solution)/shard_map/ppermute | solution.py:98

commit v15 on v14

--- a/solution.py
+++ b/solution.py
@@ -325,8 +325,8 @@
     late[taps * span - skip :, :] = unit
 
 
-def both_kernel(pos, west, east, after, both, half_3, half_1):
-    del pos, after
+def both_kernel(pos, west, east, after1, after2, both, half_3, half_1):
+    del pos, after1, after2
     size, half = west.shape[0], half_3.shape[0]
     both[0:size, :] = west[...]
     both[size:, :] = east[...]
@@ -341,8 +341,8 @@
     bottom[...] = by_x[cut:, :]
 
 
-def across_kernel(pos, half_3, half_1, late):
-    del pos
+def across_kernel(pos, half_3, half_1, after, late):
+    del pos, after
     half = half_3.shape[0]
     late[0:half, :] = half_3[...]
     late[half:, :] = half_1[...]
@@ -582,15 +582,30 @@
         top, bottom = call(
             cross_kernel, [slab(cut), slab(by_x.shape[0] - cut)], (pos, by_x, by_y, after), [], 0, name, 16, held=1
         )
-        return move(top, lat_xor(1)), move(bottom, lat_xor(2)), top
+        return move(top, lat_xor(1)), move(bottom, lat_xor(2))
 
     from_3 = move(late, lon_by(1))
     from_1 = move(late, lon_by(-1))
     own_x, own_y = to_plane(own)
-    own_top, own_bottom, crossed = to_diagonal(own_x, own_y, own_cut, own, "cross_1")
+    own_top, own_bottom = to_diagonal(own_x, own_y, own_cut, own, "cross_1")
     pair, half_3, half_1 = call(
-        both_kernel, [slab(2 * size), slab(half), slab(size - half)], (pos, from_3, from_1, crossed), [], 0, "both", 16, held=1
-    )
+        both_kernel,
+        [slab(2 * size), slab(half), slab(size - half)],
+        (pos, from_3, from_1, own_top, own_bottom),
+        [],
+        0,
+        "both",
+        16,
+        held=2,
+    )
+    half_3 = move(half_3, lon_by(1))
+    half_1 = move(half_1, lon_by(-1))
+    pair_x, pair_y = to_plane(pair)
+    (block,) = call(
+        block_kernel, [slab(4 * first_rows)], (pos, own, own_x, own_y, own_top, own_bottom), [], 0, "block", 16
+    )
+    early_3 = move(block, lon_by(1))
+    early_1 = move(block, lon_by(-1))
     whole = lambda t: (0, 0, 0, 0)
     field = pl.pallas_call(
         field_kernel,
@@ -615,16 +630,8 @@
         name="field",
     )(pos, pair, mine, theirs, taps)
 
-    half_3 = move(half_3, lon_by(1))
-    half_1 = move(half_1, lon_by(-1))
-    pair_x, pair_y = to_plane(pair)
-    (block,) = call(
-        block_kernel, [slab(4 * first_rows)], (pos, own, own_x, own_y, own_top, own_bottom), [], 0, "block", 16
-    )
-    early_3 = move(block, lon_by(1))
-    early_1 = move(block, lon_by(-1))
-    (from_2,) = call(across_kernel, [slab(size)], (pos, half_3, half_1), [], 0, "across", 16)
-    pair_top, pair_bottom, _ = to_diagonal(pair_x, pair_y, size, field, "cross_2")
+    (from_2,) = call(across_kernel, [slab(size)], (pos, half_3, half_1, field), [], 0, "across", 16, held=1)
+    pair_top, pair_bottom = to_diagonal(pair_x, pair_y, size, block, "cross_2")
     from_2x, from_2y = to_plane(from_2)
     hand_3, hand_1 = call(hand_kernel, [slab(2 * first_rows)] * 2, (pos, early_3, early_1), [], 0, "hand", 16)
     early_2a = move(hand_3, lon_by(1))
@@ -641,7 +648,7 @@
     total, token = unpack(
         pos, total, [own, own_x, own_y, own_top, own_bottom], [block], [(0, 0, 27, pieces)], span, "unpack_1"
     )
-    from_2top, from_2bottom, _ = to_diagonal(from_2x, from_2y, late_cut, token, "cross_3")
+    from_2top, from_2bottom = to_diagonal(from_2x, from_2y, late_cut, token, "cross_3")
     slabs = [
         (3, early, 27 - early, [late_piece(0), late_piece(2), late_piece(3), late_piece(4)]),
         (1, early, 27 - early, [late_piece(1), late_piece(2, size), late_piece(3, size), late_piece(5)]),

time: 154 us -> 152 us (0.987)
  waiting for transfers between devices: 54.2 us -> 51.7 us
    ppermute x37, waiting for transfers between devices: 54.2 us -> 51.7 us  [move(): return lax.ppermute(x, AXES, pairs)]
where the time goes in v15:
time: 152 us
  waiting for transfers between devices  51.7 us (34%)
  starting transfers between devices  50.7 us (33%)
  Pallas kernels  44.5 us (29%)
  local copies, waits for them, and re-layouts  4 us (3%)
    ppermute x37, waiting for transfers between devices, move(): return lax.ppermute(x, AXES, pairs)  51.7 us
    ppermute x37, starting transfers between devices, move(): return lax.ppermute(x, AXES, pairs)  50.7 us
    pallas_call x14, Pallas kernels, call(): pl.pallas_call(kernel, out_shape=outs, in_specs=[pl.BlockSpec(memory_spac...  16.9 us
    pallas_call x3, Pallas kernels, unpack(): pl.pallas_call(lambda *refs: unpack_kernel(*refs, slabs=slabs, count=len(...  13.2 us
    pallas_call x1, Pallas kernels, blocked_body(): pl.pallas_call(field_kernel, out_shape=jax.ShapeDtypeStruct((levels, heig...  9.51 us
    pallas_call x1, Pallas kernels, blocked_body(): pl.pallas_call(lines_kernel, out_shape=[jax.ShapeDtypeStruct((levels, row...  4.86 us
    unnamed x16, local copies, waits for them, and re-layouts  4 us
  transfers between devices with their start and end apart: 37, of which 14 were waited for; matrix products, arithmetic and copies ran while one was open for 0% of the time, Pallas kernels for 25%

profile of v15, /device:TPU:0, one launch (start us, length us, event | category | flops | bytes accessed | tf_op | source)
XLA Modules:
  0.0 152.0 jit_solution(3306005090988930478)
XLA Ops:
  0.7 1.0 copy-done.2
  1.7 1.0 copy-done.4
  2.7 0.8 pack.1
  3.6 0.7 collective-permute-start.6
  4.2 3.1 %collective-permute-start = (bf16[416,128]{1,0:T(8,128)(2,1)S(1)}, bf16[416,128]{1,0:T(8,128)(2,1)S(1)}, u32[]{:S(2)}, u32[]{:S(2)}) collective-permute-start(bf16[416,128]{1,0:T(8,128)(2,1)S(1)} %get-tuple-element.36), channel_id=1, source_target_pairs={{0,1},{1,2},{2,3},{3,0},{4,5},{5,6},{6,7},{7,4},{8,9},{9,10},{10,1... | collective-permute-start | bytes 319496 | tf_op jit(solution)/shard_map/ppermute | solution.py:98
  7.3 1.5 collective-permute-start.7
  8.8 2.6 %collective-permute-start.1 = (bf16[384,128]{1,0:T(8,128)(2,1)S(1)}, bf16[384,128]{1,0:T(8,128)(2,1)S(1)}, u32[]{:S(2)}, u32[]{:S(2)}) collective-permute-start(bf16[384,128]{1,0:T(8,128)(2,1)S(1)} %get-tuple-element.37), channel_id=1, source_target_pairs={{0,2},{1,3},{2,0},{3,1},{4,6},{5,7},{6,4},{7,5},{8,10},{9,11},{10,... | collective-permute-start | bytes 294920 | tf_op jit(solution)/shard_map/ppermute | solution.py:98
  11.4 1.3 collective-permute-start.2
  12.7 5.6 %collective-permute-done.1.x2 = bf16[384,128]{1,0:T(8,128)(2,1)S(1)} collective-permute-done((bf16[384,128]{1,0:T(8,128)(2,1)S(1)}, bf16[384,128]{1,0:T(8,128)(2,1)S(1)}, u32[]{:S(2)}, u32[]{:S(2)}) %collective-permute-start.1) | collective-permute-done | bytes 98336 | tf_op jit(solution)/shard_map/ppermute | solution.py:98
  18.4 2.8 %collective-permute-start.11 = (bf16[384,128]{1,0:T(8,128)(2,1)S(1)}, bf16[384,128]{1,0:T(8,128)(2,1)S(1)}, u32[]{:S(2)}, u32[]{:S(2)}) collective-permute-start(bf16[384,128]{1,0:T(8,128)(2,1)S(1)} %get-tuple-element.44), channel_id=1, source_target_pairs={{0,12},{1,13},{2,14},{3,15},{4,8},{5,9},{6,10},{7,11},{8,4},{9,5},... | collective-permute-start | bytes 294920 | tf_op jit(solution)/shard_map/ppermute | solution.py:98
  21.2 0.6 spread.1
  22.0 2.0 %collective-permute-start.3 = (bf16[1600,128]{1,0:T(8,128)(2,1)S(1)}, bf16[1600,128]{1,0:T(8,128)(2,1)S(1)}, u32[]{:S(2)}, u32[]{:S(2)}) collective-permute-start(bf16[1600,128]{1,0:T(8,128)(2,1)S(1)} %get-tuple-element.39.own.x_own), channel_id=1, source_target_pairs={{0,4},{1,5},{2,6},{3,7},{4,0},{5,1},{6,2},{7,3},{8,12},{9,13},{10,... | collective-permute-start | bytes 1228808 | tf_op jit(solution)/shard_map/ppermute | solution.py:98
  24.1 1.3 collective-permute-start.4
  26.0 3.5 %collective-permute-start.9 = (bf16[2,768,128]{2,1,0:T(8,128)(2,1)S(1)}, bf16[2,768,128]{2,1,0:T(8,128)(2,1)S(1)}, u32[]{:S(2)}, u32[]{:S(2)}) collective-permute-start(bf16[2,768,128]{2,1,0:T(8,128)(2,1)S(1)} %pair_0.1.here), channel_id=1, source_target_pairs={{0,3},{1,0},{2,1},{3,2},{4,7},{5,4},{6,5},{7,6},{8,11},{9,8},{10,9... | collective-permute-start | bytes 1179656 | tf_op jit(solution)/shard_map/ppermute | solution.py:98
  29.4 13.6 %collective-permute-done.4.after.x_y = bf16[1536,128]{1,0:T(8,128)(2,1)S(1)} collective-permute-done((bf16[1536,128]{1,0:T(8,128)(2,1)S(1)}, bf16[1536,128]{1,0:T(8,128)(2,1)S(1)}, u32[]{:S(2)}, u32[]{:S(2)}) %collective-permute-start.4) | collective-permute-done | bytes 393248 | tf_op jit(solution)/shard_map/ppermute | solution.py:98
  43.1 2.0 %collective-permute-done.8.west = bf16[2,768,128]{2,1,0:T(8,128)(2,1)S(1)} collective-permute-done((bf16[2,768,128]{2,1,0:T(8,128)(2,1)S(1)}, bf16[2,768,128]{2,1,0:T(8,128)(2,1)S(1)}, u32[]{:S(2)}, u32[]{:S(2)}) %collective-permute-start.8) | collective-permute-done | bytes 393248 | tf_op jit(solution)/shard_map/ppermute | solution.py:98
  45.1 1.0 copy-done.3
  46.1 0.8 split.1
  46.9 3.2 %collective-permute-start.14 = (bf16[768,128]{1,0:T(8,128)(2,1)S(1)}, bf16[768,128]{1,0:T(8,128)(2,1)S(1)}, u32[]{:S(2)}, u32[]{:S(2)}) collective-permute-start(bf16[768,128]{1,0:T(8,128)(2,1)S(1)} %get-tuple-element.48), channel_id=1, source_target_pairs={{0,3},{1,0},{2,1},{3,2},{4,7},{5,4},{6,5},{7,6},{8,11},{9,8},{10,9... | collective-permute-start | bytes 589832 | tf_op jit(solution)/shard_map/ppermute | solution.py:98
  50.1 4.9 %lines.1 = (bf16[4,18,192,256]{3,2,1,0:T(8,128)(2,1)S(1)}, f32[27,256,512]{2,1,0:T(8,128)}) custom-call(s32[3]{0:T(128)S(1)} %pad_add_fusion.pos.refs_0_, bf16[1600,128]{1,0:T(8,128)(2,1)S(1)} %get-tuple-element.39.own.x_own, bf16[1600,128]{1,0:T(8,128)(2,1)S(1)} %collective-permute-done.3.x_x, bf16[1536,128]{1,0:T(8,128)(2,1)S(1)} %collective-permute-done.4.after.x_y, ...), custom_call_target="tpu_custom_call" | custom-call | bytes 1048576 | tf_op jit(solution)/shard_map/lines/pallas_call | solution.py:542
  55.3 4.5 %collective-permute-done.13.one = bf16[768,128]{1,0:T(8,128)(2,1)S(1)} collective-permute-done((bf16[768,128]{1,0:T(8,128)(2,1)S(1)}, bf16[768,128]{1,0:T(8,128)(2,1)S(1)}, u32[]{:S(2)}, u32[]{:S(2)}) %collective-permute-start.13) | collective-permute-done | bytes 196640 | tf_op jit(solution)/shard_map/ppermute | solution.py:98
  61.0 1.2 collective-permute-done.15.s2
  62.2 8.6 %taps.1.held = f32[27,64,128]{2,1,0:T(8,128)S(1)} custom-call(s32[3]{0:T(128)S(1)} %pad_add_fusion.pos.refs_0_, bf16[4,18,192,256]{3,2,1,0:T(8,128)(2,1)S(1)} %get-tuple-element.46.after.xs, bf16[6,768,128]{2,1,0:T(8,128)(2,1)S(1)} %get-tuple-element.47.g, bf16[6,768,128]{2,1,0:T(8,128)(2,1)S(1)} %collective-permute-done.12.s, ...), custom_call_target="tpu_custom_call" | custom-call | flops 5435817984 | bytes 11108352 | tf_op jit(solution)/shard_map/taps/pallas_call | solution.py:116
  70.7 0.9 code.1
  72.3 1.9 %collective-permute-start.19 = (bf16[1744,128]{1,0:T(8,128)(2,1)S(1)}, bf16[1744,128]{1,0:T(8,128)(2,1)S(1)}, u32[]{:S(2)}, u32[]{:S(2)}) collective-permute-start(bf16[1744,128]{1,0:T(8,128)(2,1)S(1)} %get-tuple-element.51.after.own.refs_1_), channel_id=1, source_target_pairs={{0,4},{1,5},{2,6},{3,7},{4,0},{5,1},{6,2},{7,3},{8,12},{9,13},{10,... | collective-permute-start | bytes 1339400 | tf_op jit(solution)/shard_map/ppermute | solution.py:98
  74.2 1.9 %collective-permute-start.18 = (bf16[1360,128]{1,0:T(8,128)(2,1)S(1)}, bf16[1360,128]{1,0:T(8,128)(2,1)S(1)}, u32[]{:S(2)}, u32[]{:S(2)}) collective-permute-start(bf16[1360,128]{1,0:T(8,128)(2,1)S(1)} %get-tuple-element.50), channel_id=1, source_target_pairs={{0,3},{1,0},{2,1},{3,2},{4,7},{5,4},{6,5},{7,6},{8,11},{9,8},{10,9... | collective-permute-start | bytes 1044488 | tf_op jit(solution)/shard_map/ppermute | solution.py:98
  76.2 7.8 %collective-permute-done.20.by_y.y.refs_3_ = bf16[1744,128]{1,0:T(8,128)(2,1)S(1)} collective-permute-done((bf16[1744,128]{1,0:T(8,128)(2,1)S(1)}, bf16[1744,128]{1,0:T(8,128)(2,1)S(1)}, u32[]{:S(2)}, u32[]{:S(2)}) %collective-permute-start.20) | collective-permute-done | bytes 446496 | tf_op jit(solution)/shard_map/ppermute | solution.py:98
  85.0 1.8 %collective-permute-start.21 = (bf16[896,128]{1,0:T(8,128)(2,1)S(1)}, bf16[896,128]{1,0:T(8,128)(2,1)S(1)}, u32[]{:S(2)}, u32[]{:S(2)}) collective-permute-start(bf16[896,128]{1,0:T(8,128)(2,1)S(1)} %get-tuple-element.52), channel_id=1, source_target_pairs={{0,4},{1,5},{2,6},{3,7},{4,0},{5,1},{6,2},{7,3},{8,12},{9,13},{10,... | collective-permute-start | bytes 688136 | tf_op jit(solution)/shard_map/ppermute | solution.py:98
  87.4 5.5 %collective-permute-done.17.west.refs_1_ = bf16[1360,128]{1,0:T(8,128)(2,1)S(1)} collective-permute-done((bf16[1360,128]{1,0:T(8,128)(2,1)S(1)}, bf16[1360,128]{1,0:T(8,128)(2,1)S(1)}, u32[]{:S(2)}, u32[]{:S(2)}) %collective-permute-start.17) | collective-permute-done | bytes 348192 | tf_op jit(solution)/shard_map/ppermute | solution.py:98
  93.5 1.7 %collective-permute-start.27 = (bf16[672,128]{1,0:T(8,128)(2,1)S(1)}, bf16[672,128]{1,0:T(8,128)(2,1)S(1)}, u32[]{:S(2)}, u32[]{:S(2)}) collective-permute-start(bf16[672,128]{1,0:T(8,128)(2,1)S(1)} %get-tuple-element.57), channel_id=1, source_target_pairs={{0,1},{1,2},{2,3},{3,0},{4,5},{5,6},{6,7},{7,4},{8,9},{9,10},{10,1... | collective-permute-start | bytes 516104 | tf_op jit(solution)/shard_map/ppermute | solution.py:98
  95.7 2.3 %collective-permute-start.24 = (bf16[1600,128]{1,0:T(8,128)(2,1)S(1)}, bf16[1600,128]{1,0:T(8,128)(2,1)S(1)}, u32[]{:S(2)}, u32[]{:S(2)}) collective-permute-start(bf16[1600,128]{1,0:T(8,128)(2,1)S(1)} %block.1.refs_6_.after), channel_id=1, source_target_pairs={{0,3},{1,0},{2,1},{3,2},{4,7},{5,4},{6,5},{7,6},{8,11},{9,8},{10,9... | collective-permute-start | bytes 1228808 | tf_op jit(solution)/shard_map/ppermute | solution.py:98
  98.5 1.0 collective-permute-start.33
  99.5 3.1 %collective-permute-done.27.half_3 = bf16[672,128]{1,0:T(8,128)(2,1)S(1)} collective-permute-done((bf16[672,128]{1,0:T(8,128)(2,1)S(1)}, bf16[672,128]{1,0:T(8,128)(2,1)S(1)}, u32[]{:S(2)}, u32[]{:S(2)}) %collective-permute-start.27) | collective-permute-done | bytes 172064 | tf_op jit(solution)/shard_map/ppermute | solution.py:98
  102.6 7.4 %collective-permute-start.28 = (bf16[688,128]{1,0:T(8,128)(2,1)S(1)}, bf16[688,128]{1,0:T(8,128)(2,1)S(1)}, u32[]{:S(2)}, u32[]{:S(2)}) collective-permute-start(bf16[688,128]{1,0:T(8,128)(2,1)S(1)} %get-tuple-element.58), channel_id=1, source_target_pairs={{0,3},{1,0},{2,1},{3,2},{4,7},{5,4},{6,5},{7,6},{8,11},{9,8},{10,9... | collective-permute-start | bytes 528392 | tf_op jit(solution)/shard_map/ppermute | solution.py:98
  110.1 9.5 %field.1.after = bf16[4,4,48,256]{3,2,1,0:T(8,128)(2,1)} custom-call(s32[3]{0:T(128)S(1)} %pad_add_fusion.pos.refs_0_, bf16[2720,128]{1,0:T(8,128)(2,1)S(1)} %get-tuple-element.54.after, bf16[4,6,64,256]{3,2,1,0:T(8,128)(2,1)S(1)} %get-tuple-element.49.mine, bf16[4,6,64,256]{3,2,1,0:T(8,128)(2,1)S(1)} %collective-permute-done.16.after.theirs, ...), custom_call_target="tpu_custom_call" | custom-call | flops 10871635968 | bytes 7077888 | tf_op jit(solution)/shard_map/field/pallas_call | solution.py:610
  119.6 1.9 %collective-permute-done.28.half_1 = bf16[688,128]{1,0:T(8,128)(2,1)S(1)} collective-permute-done((bf16[688,128]{1,0:T(8,128)(2,1)S(1)}, bf16[688,128]{1,0:T(8,128)(2,1)S(1)}, u32[]{:S(2)}, u32[]{:S(2)}) %collective-permute-start.28) | collective-permute-done | bytes 176160 | tf_op jit(solution)/shard_map/ppermute | solution.py:98
  121.5 1.0 copy-done.5
  123.5 0.9 collective-permute-start.29
  125.0 1.2 collective-permute-start.35
  126.2 1.7 %collective-permute-start.36 = (bf16[1360,128]{1,0:T(8,128)(2,1)S(1)}, bf16[1360,128]{1,0:T(8,128)(2,1)S(1)}, u32[]{:S(2)}, u32[]{:S(2)}) collective-permute-start(bf16[1360,128]{1,0:T(8,128)(2,1)S(1)} %get-tuple-element.64), channel_id=1, source_target_pairs={{0,8},{1,9},{2,10},{3,11},{4,12},{5,13},{6,14},{7,15},{8,0},{9,1},... | collective-permute-start | bytes 1044488 | tf_op jit(solution)/shard_map/ppermute | solution.py:98
  128.4 2.3 %collective-permute-start.26 = (bf16[800,128]{1,0:T(8,128)(2,1)S(1)}, bf16[800,128]{1,0:T(8,128)(2,1)S(1)}, u32[]{:S(2)}, u32[]{:S(2)}) collective-permute-start(bf16[800,128]{1,0:T(8,128)(2,1)S(1)} %get-tuple-element.56), channel_id=1, source_target_pairs={{0,3},{1,0},{2,1},{3,2},{4,7},{5,4},{6,5},{7,6},{8,11},{9,8},{10,9... | collective-permute-start | bytes 614408 | tf_op jit(solution)/shard_map/ppermute | solution.py:98
  130.7 3.5 %collective-permute-done.30.by_y.refs_5_ = bf16[1360,128]{1,0:T(8,128)(2,1)S(1)} collective-permute-done((bf16[1360,128]{1,0:T(8,128)(2,1)S(1)}, bf16[1360,128]{1,0:T(8,128)(2,1)S(1)}, u32[]{:S(2)}, u32[]{:S(2)}) %collective-permute-start.30) | collective-permute-done | bytes 348192 | tf_op jit(solution)/shard_map/ppermute | solution.py:98
  134.2 0.7 collective-permute-start.25
  134.9 3.1 %unpack_1.1 = (f32[27,256,512]{2,1,0:T(8,128)}, f32[8,128]{1,0:T(8,128)S(1)}) custom-call(s32[3]{0:T(128)S(1)} %pad_add_fusion.pos.refs_0_, bf16[1744,128]{1,0:T(8,128)(2,1)S(1)} %get-tuple-element.51.after.own.refs_1_, bf16[1744,128]{1,0:T(8,128)(2,1)S(1)} %collective-permute-done.19.by_x.x.refs_2_, ...), custom_call_target="tpu_custom_call", output_to_operand_aliasing={{0}: (7, {})} | custom-call | bytes 4194304 | tf_op jit(solution)/shard_map/unpack_1/pallas_call | solution.py:408
  139.2 0.8 collective-permute-done.35.refs_5_
  140.4 1.3 collective-permute-done.36.refs_6_
  141.7 6.4 %unpack_2.1 = (f32[27,256,512]{2,1,0:T(8,128)}, f32[8,128]{1,0:T(8,128)}) custom-call(s32[3]{0:T(128)S(1)} %pad_add_fusion.pos.refs_0_, bf16[1360,128]{1,0:T(8,128)(2,1)S(1)} %collective-permute-done.17.west.refs_1_, bf16[1360,128]{1,0:T(8,128)(2,1)S(1)} %collective-permute-done.18.east.refs_2_, ...), custom_call_target="tpu_custom_call", output_to_operand_aliasing={{0}: (10, {})} | custom-call | bytes 4194304 | tf_op jit(solution)/shard_map/unpack_2/pallas_call | solution.py:408
  148.1 3.7 %unpack_3.1 = (f32[27,256,512]{2,1,0:T(8,128)}, f32[8,128]{1,0:T(8,128)}) custom-call(s32[3]{0:T(128)S(1)} %pad_add_fusion.pos.refs_0_, bf16[800,128]{1,0:T(8,128)(2,1)S(1)} %collective-permute-done.25.refs_1_, bf16[800,128]{1,0:T(8,128)(2,1)S(1)} %collective-permute-done.26.refs_2_, ...), custom_call_target="tpu_custom_call", output_to_operand_aliasing={{0}: (8, {})} | custom-call | bytes 4194304 | tf_op jit(solution)/shard_map/unpack_3/pallas_call | solution.py:408
  (63 shorter events, 10.2 us)
Async XLA Ops:
  0.7 1.0 copy-start.2
  1.7 1.0 copy-start.4
  3.6 18.5 %collective-permute-start.6 = (bf16[768,128]{1,0:T(8,128)(2,1)S(1)}, bf16[768,128]{1,0:T(8,128)(2,1)S(1)}, u32[]{:S(2)}, u32[]{:S(2)}) collective-permute-start(bf16[768,128]{1,0:T(8,128)(2,1)S(1)} %get-tuple-element.41), channel_id=1, source_target_pairs={{0,0},{1,1},{2,2},{3,3},{4,4},{5,5},{6,6},{7,7},{8,16},{9,17},{10,... | collective-permute-start | bytes 589832 | tf_op jit(solution)/shard_map/ppermute | solution.py:98
  4.2 14.1 %collective-permute-start = (bf16[416,128]{1,0:T(8,128)(2,1)S(1)}, bf16[416,128]{1,0:T(8,128)(2,1)S(1)}, u32[]{:S(2)}, u32[]{:S(2)}) collective-permute-start(bf16[416,128]{1,0:T(8,128)(2,1)S(1)} %get-tuple-element.36), channel_id=1, source_target_pairs={{0,1},{1,2},{2,3},{3,0},{4,5},{5,6},{6,7},{7,4},{8,9},{9,10},{10,1... | collective-permute-start | bytes 319496 | tf_op jit(solution)/shard_map/ppermute | solution.py:98
  7.3 16.7 %collective-permute-start.7 = (bf16[768,128]{1,0:T(8,128)(2,1)S(1)}, bf16[768,128]{1,0:T(8,128)(2,1)S(1)}, u32[]{:S(2)}, u32[]{:S(2)}) collective-permute-start(bf16[768,128]{1,0:T(8,128)(2,1)S(1)} %get-tuple-element.42), channel_id=1, source_target_pairs={{0,4},{1,5},{2,6},{3,7},{4,0},{5,1},{6,2},{7,3},{8,20},{9,21},{10,... | collective-permute-start | bytes 589832 | tf_op jit(solution)/shard_map/ppermute | solution.py:98
  8.8 9.6 %collective-permute-start.1 = (bf16[384,128]{1,0:T(8,128)(2,1)S(1)}, bf16[384,128]{1,0:T(8,128)(2,1)S(1)}, u32[]{:S(2)}, u32[]{:S(2)}) collective-permute-start(bf16[384,128]{1,0:T(8,128)(2,1)S(1)} %get-tuple-element.37), channel_id=1, source_target_pairs={{0,2},{1,3},{2,0},{3,1},{4,6},{5,7},{6,4},{7,5},{8,10},{9,11},{10,... | collective-permute-start | bytes 294920 | tf_op jit(solution)/shard_map/ppermute | solution.py:98
  11.4 9.8 %collective-permute-start.2 = (bf16[416,128]{1,0:T(8,128)(2,1)S(1)}, bf16[416,128]{1,0:T(8,128)(2,1)S(1)}, u32[]{:S(2)}, u32[]{:S(2)}) collective-permute-start(bf16[416,128]{1,0:T(8,128)(2,1)S(1)} %get-tuple-element.38), channel_id=1, source_target_pairs={{0,3},{1,0},{2,1},{3,2},{4,7},{5,4},{6,5},{7,6},{8,11},{9,8},{10,9... | collective-permute-start | bytes 319496 | tf_op jit(solution)/shard_map/ppermute | solution.py:98
  18.4 7.6 %collective-permute-start.10 = (bf16[384,128]{1,0:T(8,128)(2,1)S(1)}, bf16[384,128]{1,0:T(8,128)(2,1)S(1)}, u32[]{:S(2)}, u32[]{:S(2)}) collective-permute-start(bf16[384,128]{1,0:T(8,128)(2,1)S(1)} %get-tuple-element.43), channel_id=1, source_target_pairs={{0,4},{1,5},{2,6},{3,7},{4,0},{5,1},{6,2},{7,3},{8,12},{9,13},{10,... | collective-permute-start | bytes 294920 | tf_op jit(solution)/shard_map/ppermute | solution.py:98
  18.4 11.1 %collective-permute-start.11 = (bf16[384,128]{1,0:T(8,128)(2,1)S(1)}, bf16[384,128]{1,0:T(8,128)(2,1)S(1)}, u32[]{:S(2)}, u32[]{:S(2)}) collective-permute-start(bf16[384,128]{1,0:T(8,128)(2,1)S(1)} %get-tuple-element.44), channel_id=1, source_target_pairs={{0,12},{1,13},{2,14},{3,15},{4,8},{5,9},{6,10},{7,11},{8,4},{9,5},... | collective-permute-start | bytes 294920 | tf_op jit(solution)/shard_map/ppermute | solution.py:98
  21.8 21.2 %collective-permute-start.5 = (bf16[1600,128]{1,0:T(8,128)(2,1)S(1)}, bf16[1600,128]{1,0:T(8,128)(2,1)S(1)}, u32[]{:S(2)}, u32[]{:S(2)}) collective-permute-start(bf16[1600,128]{1,0:T(8,128)(2,1)S(1)} %get-tuple-element.39.own.x_own), channel_id=1, source_target_pairs={{0,12},{1,13},{2,14},{3,15},{4,8},{5,9},{6,10},{7,11},{8,4},{9,5},... | collective-permute-start | bytes 1228808 | tf_op jit(solution)/shard_map/ppermute | solution.py:98
  22.0 21.0 %collective-permute-start.3 = (bf16[1600,128]{1,0:T(8,128)(2,1)S(1)}, bf16[1600,128]{1,0:T(8,128)(2,1)S(1)}, u32[]{:S(2)}, u32[]{:S(2)}) collective-permute-start(bf16[1600,128]{1,0:T(8,128)(2,1)S(1)} %get-tuple-element.39.own.x_own), channel_id=1, source_target_pairs={{0,4},{1,5},{2,6},{3,7},{4,0},{5,1},{6,2},{7,3},{8,12},{9,13},{10,... | collective-permute-start | bytes 1228808 | tf_op jit(solution)/shard_map/ppermute | solution.py:98
  24.1 19.0 %collective-permute-start.4 = (bf16[1536,128]{1,0:T(8,128)(2,1)S(1)}, bf16[1536,128]{1,0:T(8,128)(2,1)S(1)}, u32[]{:S(2)}, u32[]{:S(2)}) collective-permute-start(bf16[1536,128]{1,0:T(8,128)(2,1)S(1)} %get-tuple-element.40), channel_id=1, source_target_pairs={{0,8},{1,9},{2,10},{3,11},{4,12},{5,13},{6,14},{7,15},{8,0},{9,1},... | collective-permute-start | bytes 1179656 | tf_op jit(solution)/shard_map/ppermute | solution.py:98
  26.0 17.1 %collective-permute-start.9 = (bf16[2,768,128]{2,1,0:T(8,128)(2,1)S(1)}, bf16[2,768,128]{2,1,0:T(8,128)(2,1)S(1)}, u32[]{:S(2)}, u32[]{:S(2)}) collective-permute-start(bf16[2,768,128]{2,1,0:T(8,128)(2,1)S(1)} %pair_0.1.here), channel_id=1, source_target_pairs={{0,3},{1,0},{2,1},{3,2},{4,7},{5,4},{6,5},{7,6},{8,11},{9,8},{10,9... | collective-permute-start | bytes 1179656 | tf_op jit(solution)/shard_map/ppermute | solution.py:98
  29.4 15.6 %collective-permute-start.8 = (bf16[2,768,128]{2,1,0:T(8,128)(2,1)S(1)}, bf16[2,768,128]{2,1,0:T(8,128)(2,1)S(1)}, u32[]{:S(2)}, u32[]{:S(2)}) collective-permute-start(bf16[2,768,128]{2,1,0:T(8,128)(2,1)S(1)} %pair_0.1.here), channel_id=1, source_target_pairs={{0,1},{1,2},{2,3},{3,0},{4,5},{5,6},{6,7},{7,4},{8,9},{9,10},{10,1... | collective-permute-start | bytes 1179656 | tf_op jit(solution)/shard_map/ppermute | solution.py:98
  45.1 1.0 copy-start.3
  46.8 15.3 %collective-permute-start.12 = (bf16[6,768,128]{2,1,0:T(8,128)(2,1)S(1)}, bf16[6,768,128]{2,1,0:T(8,128)(2,1)S(1)}, u32[]{:S(2)}, u32[]{:S(2)}) collective-permute-start(bf16[6,768,128]{2,1,0:T(8,128)(2,1)S(1)} %get-tuple-element.47.g), channel_id=1, source_target_pairs={{0,16},{1,17},{2,18},{3,19},{4,20},{5,21},{6,22},{7,23},{8,24},{9,... | collective-permute-start | bytes 3538952 | tf_op jit(solution)/shard_map/ppermute | solution.py:98
  46.9 8.4 %collective-permute-start.14 = (bf16[768,128]{1,0:T(8,128)(2,1)S(1)}, bf16[768,128]{1,0:T(8,128)(2,1)S(1)}, u32[]{:S(2)}, u32[]{:S(2)}) collective-permute-start(bf16[768,128]{1,0:T(8,128)(2,1)S(1)} %get-tuple-element.48), channel_id=1, source_target_pairs={{0,3},{1,0},{2,1},{3,2},{4,7},{5,4},{6,5},{7,6},{8,11},{9,8},{10,9... | collective-permute-start | bytes 589832 | tf_op jit(solution)/shard_map/ppermute | solution.py:98
  50.1 9.7 %collective-permute-start.13 = (bf16[768,128]{1,0:T(8,128)(2,1)S(1)}, bf16[768,128]{1,0:T(8,128)(2,1)S(1)}, u32[]{:S(2)}, u32[]{:S(2)}) collective-permute-start(bf16[768,128]{1,0:T(8,128)(2,1)S(1)} %get-tuple-element.45.after), channel_id=1, source_target_pairs={{0,1},{1,2},{2,3},{3,0},{4,5},{5,6},{6,7},{7,4},{8,9},{9,10},{10,1... | collective-permute-start | bytes 589832 | tf_op jit(solution)/shard_map/ppermute | solution.py:98
  60.4 49.7 %slice-start = ((s8[7077888]{0:T(1024)(128)(4,1)}), s8[4194304]{0:T(1024)(128)(4,1)S(1)}, s32[]{:S(2)}) async-start(s8[7077888]{0:T(1024)(128)(4,1)} %bitcast.12), calls=%async_computation | async-start | bytes 8388608
  60.4 1.8 %collective-permute-start.15 = (bf16[2,768,128]{2,1,0:T(8,128)(2,1)S(1)}, bf16[2,768,128]{2,1,0:T(8,128)(2,1)S(1)}, u32[]{:S(2)}, u32[]{:S(2)}) collective-permute-start(bf16[2,768,128]{2,1,0:T(8,128)(2,1)S(1)} %pair.1.g2), channel_id=1, source_target_pairs={{0,16},{1,17},{2,18},{3,19},{4,20},{5,21},{6,22},{7,23},{8,24},{9,... | collective-permute-start | bytes 1179656 | tf_op jit(solution)/shard_map/ppermute | solution.py:98
  60.5 49.6 %slice-start.1 = ((s8[7077888]{0:T(1024)(128)(4,1)}), s8[2883584]{0:T(1024)(128)(4,1)S(1)}, s32[]{:S(2)}) async-start(s8[7077888]{0:T(1024)(128)(4,1)} %bitcast.12), calls=%async_computation.1 | async-start | bytes 5767168
  60.5 10.3 %collective-permute-start.16 = (bf16[4,6,64,256]{3,2,1,0:T(8,128)(2,1)S(1)}, bf16[4,6,64,256]{3,2,1,0:T(8,128)(2,1)S(1)}, u32[]{:S(2)}, u32[]{:S(2)}) collective-permute-start(bf16[4,6,64,256]{3,2,1,0:T(8,128)(2,1)S(1)} %get-tuple-element.49.mine), channel_id=1, source_target_pairs={{0,16},{1,17},{2,18},{3,19},{4,20},{5,21},{6,22},{7,23},{8,24},{9,... | collective-permute-start | bytes 2359304 | tf_op jit(solution)/shard_map/ppermute | solution.py:98
  71.6 12.4 %collective-permute-start.20 = (bf16[1744,128]{1,0:T(8,128)(2,1)S(1)}, bf16[1744,128]{1,0:T(8,128)(2,1)S(1)}, u32[]{:S(2)}, u32[]{:S(2)}) collective-permute-start(bf16[1744,128]{1,0:T(8,128)(2,1)S(1)} %get-tuple-element.51.after.own.refs_1_), channel_id=1, source_target_pairs={{0,8},{1,9},{2,10},{3,11},{4,12},{5,13},{6,14},{7,15},{8,0},{9,1},... | collective-permute-start | bytes 1339400 | tf_op jit(solution)/shard_map/ppermute | solution.py:98
  72.3 12.2 %collective-permute-start.19 = (bf16[1744,128]{1,0:T(8,128)(2,1)S(1)}, bf16[1744,128]{1,0:T(8,128)(2,1)S(1)}, u32[]{:S(2)}, u32[]{:S(2)}) collective-permute-start(bf16[1744,128]{1,0:T(8,128)(2,1)S(1)} %get-tuple-element.51.after.own.refs_1_), channel_id=1, source_target_pairs={{0,4},{1,5},{2,6},{3,7},{4,0},{5,1},{6,2},{7,3},{8,12},{9,13},{10,... | collective-permute-start | bytes 1339400 | tf_op jit(solution)/shard_map/ppermute | solution.py:98
  74.2 13.2 %collective-permute-start.18 = (bf16[1360,128]{1,0:T(8,128)(2,1)S(1)}, bf16[1360,128]{1,0:T(8,128)(2,1)S(1)}, u32[]{:S(2)}, u32[]{:S(2)}) collective-permute-start(bf16[1360,128]{1,0:T(8,128)(2,1)S(1)} %get-tuple-element.50), channel_id=1, source_target_pairs={{0,3},{1,0},{2,1},{3,2},{4,7},{5,4},{6,5},{7,6},{8,11},{9,8},{10,9... | collective-permute-start | bytes 1044488 | tf_op jit(solution)/shard_map/ppermute | solution.py:98
  76.0 16.8 %collective-permute-start.17 = (bf16[1360,128]{1,0:T(8,128)(2,1)S(1)}, bf16[1360,128]{1,0:T(8,128)(2,1)S(1)}, u32[]{:S(2)}, u32[]{:S(2)}) collective-permute-start(bf16[1360,128]{1,0:T(8,128)(2,1)S(1)} %get-tuple-element.50), channel_id=1, source_target_pairs={{0,1},{1,2},{2,3},{3,0},{4,5},{5,6},{6,7},{7,4},{8,9},{9,10},{10,1... | collective-permute-start | bytes 1044488 | tf_op jit(solution)/shard_map/ppermute | solution.py:98
  85.0 7.8 %collective-permute-start.21 = (bf16[896,128]{1,0:T(8,128)(2,1)S(1)}, bf16[896,128]{1,0:T(8,128)(2,1)S(1)}, u32[]{:S(2)}, u32[]{:S(2)}) collective-permute-start(bf16[896,128]{1,0:T(8,128)(2,1)S(1)} %get-tuple-element.52), channel_id=1, source_target_pairs={{0,4},{1,5},{2,6},{3,7},{4,0},{5,1},{6,2},{7,3},{8,12},{9,13},{10,... | collective-permute-start | bytes 688136 | tf_op jit(solution)/shard_map/ppermute | solution.py:98
  86.8 6.0 %collective-permute-start.22 = (bf16[848,128]{1,0:T(8,128)(2,1)S(1)}, bf16[848,128]{1,0:T(8,128)(2,1)S(1)}, u32[]{:S(2)}, u32[]{:S(2)}) collective-permute-start(bf16[848,128]{1,0:T(8,128)(2,1)S(1)} %get-tuple-element.53), channel_id=1, source_target_pairs={{0,8},{1,9},{2,10},{3,11},{4,12},{5,13},{6,14},{7,15},{8,0},{9,1},... | collective-permute-start | bytes 651272 | tf_op jit(solution)/shard_map/ppermute | solution.py:98
  93.5 9.2 %collective-permute-start.27 = (bf16[672,128]{1,0:T(8,128)(2,1)S(1)}, bf16[672,128]{1,0:T(8,128)(2,1)S(1)}, u32[]{:S(2)}, u32[]{:S(2)}) collective-permute-start(bf16[672,128]{1,0:T(8,128)(2,1)S(1)} %get-tuple-element.57), channel_id=1, source_target_pairs={{0,1},{1,2},{2,3},{3,0},{4,5},{5,6},{6,7},{7,4},{8,9},{9,10},{10,1... | collective-permute-start | bytes 516104 | tf_op jit(solution)/shard_map/ppermute | solution.py:98
  95.7 30.5 %collective-permute-start.24 = (bf16[1600,128]{1,0:T(8,128)(2,1)S(1)}, bf16[1600,128]{1,0:T(8,128)(2,1)S(1)}, u32[]{:S(2)}, u32[]{:S(2)}) collective-permute-start(bf16[1600,128]{1,0:T(8,128)(2,1)S(1)} %block.1.refs_6_.after), channel_id=1, source_target_pairs={{0,3},{1,0},{2,1},{3,2},{4,7},{5,4},{6,5},{7,6},{8,11},{9,8},{10,9... | collective-permute-start | bytes 1228808 | tf_op jit(solution)/shard_map/ppermute | solution.py:98
  98.0 29.9 %collective-permute-start.23 = (bf16[1600,128]{1,0:T(8,128)(2,1)S(1)}, bf16[1600,128]{1,0:T(8,128)(2,1)S(1)}, u32[]{:S(2)}, u32[]{:S(2)}) collective-permute-start(bf16[1600,128]{1,0:T(8,128)(2,1)S(1)} %block.1.refs_6_.after), channel_id=1, source_target_pairs={{0,1},{1,2},{2,3},{3,0},{4,5},{5,6},{6,7},{7,4},{8,9},{9,10},{10,1... | collective-permute-start | bytes 1228808 | tf_op jit(solution)/shard_map/ppermute | solution.py:98
  98.0 25.5 %collective-permute-start.34 = (bf16[2720,128]{1,0:T(8,128)(2,1)S(1)}, bf16[2720,128]{1,0:T(8,128)(2,1)S(1)}, u32[]{:S(2)}, u32[]{:S(2)}) collective-permute-start(bf16[2720,128]{1,0:T(8,128)(2,1)S(1)} %get-tuple-element.54.after), channel_id=1, source_target_pairs={{0,8},{1,9},{2,10},{3,11},{4,12},{5,13},{6,14},{7,15},{8,0},{9,1},... | collective-permute-start | bytes 2088968 | tf_op jit(solution)/shard_map/ppermute | solution.py:98
  98.5 25.9 %collective-permute-start.33 = (bf16[2720,128]{1,0:T(8,128)(2,1)S(1)}, bf16[2720,128]{1,0:T(8,128)(2,1)S(1)}, u32[]{:S(2)}, u32[]{:S(2)}) collective-permute-start(bf16[2720,128]{1,0:T(8,128)(2,1)S(1)} %get-tuple-element.54.after), channel_id=1, source_target_pairs={{0,4},{1,5},{2,6},{3,7},{4,0},{5,1},{6,2},{7,3},{8,12},{9,13},{10,... | collective-permute-start | bytes 2088968 | tf_op jit(solution)/shard_map/ppermute | solution.py:98
  102.6 18.9 %collective-permute-start.28 = (bf16[688,128]{1,0:T(8,128)(2,1)S(1)}, bf16[688,128]{1,0:T(8,128)(2,1)S(1)}, u32[]{:S(2)}, u32[]{:S(2)}) collective-permute-start(bf16[688,128]{1,0:T(8,128)(2,1)S(1)} %get-tuple-element.58), channel_id=1, source_target_pairs={{0,3},{1,0},{2,1},{3,2},{4,7},{5,4},{6,5},{7,6},{8,11},{9,8},{10,9... | collective-permute-start | bytes 528392 | tf_op jit(solution)/shard_map/ppermute | solution.py:98
  121.5 1.0 copy-start.5
  123.1 11.2 %collective-permute-start.30 = (bf16[1360,128]{1,0:T(8,128)(2,1)S(1)}, bf16[1360,128]{1,0:T(8,128)(2,1)S(1)}, u32[]{:S(2)}, u32[]{:S(2)}) collective-permute-start(bf16[1360,128]{1,0:T(8,128)(2,1)S(1)} %across.1.refs_3_), channel_id=1, source_target_pairs={{0,8},{1,9},{2,10},{3,11},{4,12},{5,13},{6,14},{7,15},{8,0},{9,1},... | collective-permute-start | bytes 1044488 | tf_op jit(solution)/shard_map/ppermute | solution.py:98
  123.5 18.2 %copy-start = (bf16[2720,128]{1,0:T(8,128)(2,1)}, bf16[2720,128]{1,0:T(8,128)(2,1)S(1)}, u32[]{:S(2)}) copy-start(bf16[2720,128]{1,0:T(8,128)(2,1)S(1)} %collective-permute-done.34.by_y.refs_4_) | copy-start | bytes 2088964
  123.5 14.6 %collective-permute-start.29 = (bf16[1360,128]{1,0:T(8,128)(2,1)S(1)}, bf16[1360,128]{1,0:T(8,128)(2,1)S(1)}, u32[]{:S(2)}, u32[]{:S(2)}) collective-permute-start(bf16[1360,128]{1,0:T(8,128)(2,1)S(1)} %across.1.refs_3_), channel_id=1, source_target_pairs={{0,4},{1,5},{2,6},{3,7},{4,0},{5,1},{6,2},{7,3},{8,12},{9,13},{10,... | collective-permute-start | bytes 1044488 | tf_op jit(solution)/shard_map/ppermute | solution.py:98
  124.4 17.3 %copy-start.1 = (bf16[2720,128]{1,0:T(8,128)(2,1)}, bf16[2720,128]{1,0:T(8,128)(2,1)S(1)}, u32[]{:S(2)}) copy-start(bf16[2720,128]{1,0:T(8,128)(2,1)S(1)} %collective-permute-done.33.by_x.refs_3_) | copy-start | bytes 2088964
  125.0 15.0 %collective-permute-start.35 = (bf16[1360,128]{1,0:T(8,128)(2,1)S(1)}, bf16[1360,128]{1,0:T(8,128)(2,1)S(1)}, u32[]{:S(2)}, u32[]{:S(2)}) collective-permute-start(bf16[1360,128]{1,0:T(8,128)(2,1)S(1)} %get-tuple-element.63), channel_id=1, source_target_pairs={{0,4},{1,5},{2,6},{3,7},{4,0},{5,1},{6,2},{7,3},{8,12},{9,13},{10,... | collective-permute-start | bytes 1044488 | tf_op jit(solution)/shard_map/ppermute | solution.py:98
  126.2 15.5 %collective-permute-start.36 = (bf16[1360,128]{1,0:T(8,128)(2,1)S(1)}, bf16[1360,128]{1,0:T(8,128)(2,1)S(1)}, u32[]{:S(2)}, u32[]{:S(2)}) collective-permute-start(bf16[1360,128]{1,0:T(8,128)(2,1)S(1)} %get-tuple-element.64), channel_id=1, source_target_pairs={{0,8},{1,9},{2,10},{3,11},{4,12},{5,13},{6,14},{7,15},{8,0},{9,1},... | collective-permute-start | bytes 1044488 | tf_op jit(solution)/shard_map/ppermute | solution.py:98
  128.4 19.6 %collective-permute-start.26 = (bf16[800,128]{1,0:T(8,128)(2,1)S(1)}, bf16[800,128]{1,0:T(8,128)(2,1)S(1)}, u32[]{:S(2)}, u32[]{:S(2)}) collective-permute-start(bf16[800,128]{1,0:T(8,128)(2,1)S(1)} %get-tuple-element.56), channel_id=1, source_target_pairs={{0,3},{1,0},{2,1},{3,2},{4,7},{5,4},{6,5},{7,6},{8,11},{9,8},{10,9... | collective-permute-start | bytes 614408 | tf_op jit(solution)/shard_map/ppermute | solution.py:98
  134.2 13.8 %collective-permute-start.25 = (bf16[800,128]{1,0:T(8,128)(2,1)S(1)}, bf16[800,128]{1,0:T(8,128)(2,1)S(1)}, u32[]{:S(2)}, u32[]{:S(2)}) collective-permute-start(bf16[800,128]{1,0:T(8,128)(2,1)S(1)} %get-tuple-element.55.refs_9_), channel_id=1, source_target_pairs={{0,1},{1,2},{2,3},{3,0},{4,5},{5,6},{6,7},{7,4},{8,9},{9,10},{10,1... | collective-permute-start | bytes 614408 | tf_op jit(solution)/shard_map/ppermute | solution.py:98
  138.7 9.4 %collective-permute-start.32 = (bf16[720,128]{1,0:T(8,128)(2,1)S(1)}, bf16[720,128]{1,0:T(8,128)(2,1)S(1)}, u32[]{:S(2)}, u32[]{:S(2)}) collective-permute-start(bf16[720,128]{1,0:T(8,128)(2,1)S(1)} %get-tuple-element.62), channel_id=1, source_target_pairs={{0,8},{1,9},{2,10},{3,11},{4,12},{5,13},{6,14},{7,15},{8,0},{9,1},... | collective-permute-start | bytes 552968 | tf_op jit(solution)/shard_map/ppermute | solution.py:98
  140.0 8.1 %collective-permute-start.31 = (bf16[640,128]{1,0:T(8,128)(2,1)S(1)}, bf16[640,128]{1,0:T(8,128)(2,1)S(1)}, u32[]{:S(2)}, u32[]{:S(2)}) collective-permute-start(bf16[640,128]{1,0:T(8,128)(2,1)S(1)} %get-tuple-element.61), channel_id=1, source_target_pairs={{0,4},{1,5},{2,6},{3,7},{4,0},{5,1},{6,2},{7,3},{8,12},{9,13},{10,... | collective-permute-start | bytes 491528 | tf_op jit(solution)/shard_map/ppermute | solution.py:98

commit v16 on v14

--- a/solution.py
+++ b/solution.py
@@ -325,8 +325,8 @@
     late[taps * span - skip :, :] = unit
 
 
-def both_kernel(pos, west, east, after, both, half_3, half_1):
-    del pos, after
+def both_kernel(pos, west, east, after1, after2, both, half_3, half_1):
+    del pos, after1, after2
     size, half = west.shape[0], half_3.shape[0]
     both[0:size, :] = west[...]
     both[size:, :] = east[...]
@@ -341,15 +341,15 @@
     bottom[...] = by_x[cut:, :]
 
 
-def across_kernel(pos, half_3, half_1, late):
-    del pos
+def across_kernel(pos, half_3, half_1, after, late):
+    del pos, after
     half = half_3.shape[0]
     late[0:half, :] = half_3[...]
     late[half:, :] = half_1[...]
 
 
-def block_kernel(pos, own, x, y, top, bottom, block):
-    del pos
+def block_kernel(pos, own, x, y, top, bottom, after, block):
+    del pos, after
     rows = block.shape[0] // 4
     for at, (piece, end) in enumerate(((own, own), (x, x), (y, y), (top, bottom))):
         block[at * rows : (at + 1) * rows - 16, :] = piece[0 : rows - 16, :]
@@ -575,22 +575,6 @@
     )
     own, late = call(code_kernel, [slab(end + 16), slab(size)], (pos, grads, theirs), [], 0, "code", 16, held=1)
 
-    def to_plane(share):
-        return move(share, lat_xor(1)), move(share, lat_xor(2))
-
-    def to_diagonal(by_x, by_y, cut, after, name):
-        top, bottom = call(
-            cross_kernel, [slab(cut), slab(by_x.shape[0] - cut)], (pos, by_x, by_y, after), [], 0, name, 16, held=1
-        )
-        return move(top, lat_xor(1)), move(bottom, lat_xor(2)), top
-
-    from_3 = move(late, lon_by(1))
-    from_1 = move(late, lon_by(-1))
-    own_x, own_y = to_plane(own)
-    own_top, own_bottom, crossed = to_diagonal(own_x, own_y, own_cut, own, "cross_1")
-    pair, half_3, half_1 = call(
-        both_kernel, [slab(2 * size), slab(half), slab(size - half)], (pos, from_3, from_1, crossed), [], 0, "both", 16, held=1
-    )
     whole = lambda t: (0, 0, 0, 0)
     field = pl.pallas_call(
         field_kernel,
@@ -613,18 +597,41 @@
         ),
         compiler_params=pltpu.CompilerParams(vmem_limit_bytes=20 * 1024 * 1024),
         name="field",
-    )(pos, pair, mine, theirs, taps)
-
+    )(pos, own, mine, theirs, taps)
+
+    def to_plane(share):
+        return move(share, lat_xor(1)), move(share, lat_xor(2))
+
+    def to_diagonal(by_x, by_y, cut, after, name):
+        top, bottom = call(
+            cross_kernel, [slab(cut), slab(by_x.shape[0] - cut)], (pos, by_x, by_y, after), [], 0, name, 16, held=1
+        )
+        return move(top, lat_xor(1)), move(bottom, lat_xor(2))
+
+    from_3 = move(late, lon_by(1))
+    from_1 = move(late, lon_by(-1))
+    own_x, own_y = to_plane(own)
+    own_top, own_bottom = to_diagonal(own_x, own_y, own_cut, field, "cross_1")
+    pair, half_3, half_1 = call(
+        both_kernel,
+        [slab(2 * size), slab(half), slab(size - half)],
+        (pos, from_3, from_1, own_top, own_bottom),
+        [],
+        0,
+        "both",
+        16,
+        held=2,
+    )
     half_3 = move(half_3, lon_by(1))
     half_1 = move(half_1, lon_by(-1))
     pair_x, pair_y = to_plane(pair)
     (block,) = call(
-        block_kernel, [slab(4 * first_rows)], (pos, own, own_x, own_y, own_top, own_bottom), [], 0, "block", 16
+        block_kernel, [slab(4 * first_rows)], (pos, own, own_x, own_y, own_top, own_bottom, half_3), [], 0, "block", 16, held=1
     )
     early_3 = move(block, lon_by(1))
     early_1 = move(block, lon_by(-1))
-    (from_2,) = call(across_kernel, [slab(size)], (pos, half_3, half_1), [], 0, "across", 16)
-    pair_top, pair_bottom, _ = to_diagonal(pair_x, pair_y, size, field, "cross_2")
+    (from_2,) = call(across_kernel, [slab(size)], (pos, half_3, half_1, block), [], 0, "across", 16, held=1)
+    pair_top, pair_bottom = to_diagonal(pair_x, pair_y, size, block, "cross_2")
     from_2x, from_2y = to_plane(from_2)
     hand_3, hand_1 = call(hand_kernel, [slab(2 * first_rows)] * 2, (pos, early_3, early_1), [], 0, "hand", 16)
     early_2a = move(hand_3, lon_by(1))
@@ -641,7 +648,7 @@
     total, token = unpack(
         pos, total, [own, own_x, own_y, own_top, own_bottom], [block], [(0, 0, 27, pieces)], span, "unpack_1"
     )
-    from_2top, from_2bottom, _ = to_diagonal(from_2x, from_2y, late_cut, token, "cross_3")
+    from_2top, from_2bottom = to_diagonal(from_2x, from_2y, late_cut, token, "cross_3")
     slabs = [
         (3, early, 27 - early, [late_piece(0), late_piece(2), late_piece(3), late_piece(4)]),
         (1, early, 27 - early, [late_piece(1), late_piece(2, size), late_piece(3, size), late_piece(5)]),

time: 154 us -> 148 us (0.961)
  waiting for transfers between devices: 54.2 us -> 49.8 us
    ppermute x37, waiting for transfers between devices: 54.2 us -> 49.8 us  [move(): return lax.ppermute(x, AXES, pairs)]
  transfers between devices with their start and end apart: 37 -> 37, of which waited for: 14 -> 13; matrix products, arithmetic and copies ran while one was open for 0% -> 0% of each run, Pallas kernels for 25% -> 25%
where the time goes in v16:
time: 148 us
  waiting for transfers between devices  49.8 us (34%)
  starting transfers between devices  48.3 us (33%)
  Pallas kernels  44.5 us (30%)
  local copies, waits for them, and re-layouts  4 us (3%)
    ppermute x37, waiting for transfers between devices, move(): return lax.ppermute(x, AXES, pairs)  49.8 us
    ppermute x37, starting transfers between devices, move(): return lax.ppermute(x, AXES, pairs)  48.3 us
    pallas_call x14, Pallas kernels, call(): pl.pallas_call(kernel, out_shape=outs, in_specs=[pl.BlockSpec(memory_spac...  16.9 us
    pallas_call x3, Pallas kernels, unpack(): pl.pallas_call(lambda *refs: unpack_kernel(*refs, slabs=slabs, count=len(...  13.3 us
    pallas_call x1, Pallas kernels, blocked_body(): pl.pallas_call(field_kernel, out_shape=jax.ShapeDtypeStruct((levels, heig...  9.51 us
    pallas_call x1, Pallas kernels, blocked_body(): pl.pallas_call(lines_kernel, out_shape=[jax.ShapeDtypeStruct((levels, row...  4.86 us
    unnamed x16, local copies, waits for them, and re-layouts  4 us
  transfers between devices with their start and end apart: 37, of which 13 were waited for; matrix products, arithmetic and copies ran while one was open for 0% of the time, Pallas kernels for 25%

profile of v16, /device:TPU:0, one launch (start us, length us, event | category | flops | bytes accessed | tf_op | source)
XLA Modules:
  0.0 147.8 jit_solution(16020907068970598250)
XLA Ops:
  0.7 1.0 copy-done.2
  1.7 1.0 copy-done.4
  2.7 0.8 pack.1
  4.2 3.1 %collective-permute-start = (bf16[416,128]{1,0:T(8,128)(2,1)S(1)}, bf16[416,128]{1,0:T(8,128)(2,1)S(1)}, u32[]{:S(2)}, u32[]{:S(2)}) collective-permute-start(bf16[416,128]{1,0:T(8,128)(2,1)S(1)} %get-tuple-element.36), channel_id=1, source_target_pairs={{0,1},{1,2},{2,3},{3,0},{4,5},{5,6},{6,7},{7,4},{8,9},{9,10},{10,1... | collective-permute-start | bytes 319496 | tf_op jit(solution)/shard_map/ppermute | solution.py:98
  7.3 1.5 %collective-permute-start.7 = (bf16[768,128]{1,0:T(8,128)(2,1)S(1)}, bf16[768,128]{1,0:T(8,128)(2,1)S(1)}, u32[]{:S(2)}, u32[]{:S(2)}) collective-permute-start(bf16[768,128]{1,0:T(8,128)(2,1)S(1)} %get-tuple-element.42), channel_id=1, source_target_pairs={{0,4},{1,5},{2,6},{3,7},{4,0},{5,1},{6,2},{7,3},{8,20},{9,21},{10,... | collective-permute-start | bytes 589832 | tf_op jit(solution)/shard_map/ppermute | solution.py:98
  8.8 2.6 %collective-permute-start.1 = (bf16[384,128]{1,0:T(8,128)(2,1)S(1)}, bf16[384,128]{1,0:T(8,128)(2,1)S(1)}, u32[]{:S(2)}, u32[]{:S(2)}) collective-permute-start(bf16[384,128]{1,0:T(8,128)(2,1)S(1)} %get-tuple-element.37), channel_id=1, source_target_pairs={{0,2},{1,3},{2,0},{3,1},{4,6},{5,7},{6,4},{7,5},{8,10},{9,11},{10,... | collective-permute-start | bytes 294920 | tf_op jit(solution)/shard_map/ppermute | solution.py:98
  11.4 1.3 collective-permute-start.2
  12.7 5.6 %collective-permute-done.1.x2 = bf16[384,128]{1,0:T(8,128)(2,1)S(1)} collective-permute-done((bf16[384,128]{1,0:T(8,128)(2,1)S(1)}, bf16[384,128]{1,0:T(8,128)(2,1)S(1)}, u32[]{:S(2)}, u32[]{:S(2)}) %collective-permute-start.1) | collective-permute-done | bytes 98336 | tf_op jit(solution)/shard_map/ppermute | solution.py:98
  18.4 2.8 %collective-permute-start.11 = (bf16[384,128]{1,0:T(8,128)(2,1)S(1)}, bf16[384,128]{1,0:T(8,128)(2,1)S(1)}, u32[]{:S(2)}, u32[]{:S(2)}) collective-permute-start(bf16[384,128]{1,0:T(8,128)(2,1)S(1)} %get-tuple-element.44), channel_id=1, source_target_pairs={{0,12},{1,13},{2,14},{3,15},{4,8},{5,9},{6,10},{7,11},{8,4},{9,5},... | collective-permute-start | bytes 294920 | tf_op jit(solution)/shard_map/ppermute | solution.py:98
  21.8 1.2 collective-permute-start.3
  23.0 1.1 collective-permute-start.5
  24.1 1.3 collective-permute-start.4
  26.7 3.3 %collective-permute-start.9 = (bf16[2,768,128]{2,1,0:T(8,128)(2,1)S(1)}, bf16[2,768,128]{2,1,0:T(8,128)(2,1)S(1)}, u32[]{:S(2)}, u32[]{:S(2)}) collective-permute-start(bf16[2,768,128]{2,1,0:T(8,128)(2,1)S(1)} %pair_0.1.here), channel_id=1, source_target_pairs={{0,3},{1,0},{2,1},{3,2},{4,7},{5,4},{6,5},{7,6},{8,11},{9,8},{10,9... | collective-permute-start | bytes 1179656 | tf_op jit(solution)/shard_map/ppermute | solution.py:98
  29.9 5.2 %collective-permute-done.4.after.x_y = bf16[1536,128]{1,0:T(8,128)(2,1)S(1)} collective-permute-done((bf16[1536,128]{1,0:T(8,128)(2,1)S(1)}, bf16[1536,128]{1,0:T(8,128)(2,1)S(1)}, u32[]{:S(2)}, u32[]{:S(2)}) %collective-permute-start.4) | collective-permute-done | bytes 393248 | tf_op jit(solution)/shard_map/ppermute | solution.py:98
  35.2 8.2 %collective-permute-done.5.x_d = bf16[1600,128]{1,0:T(8,128)(2,1)S(1)} collective-permute-done((bf16[1600,128]{1,0:T(8,128)(2,1)S(1)}, bf16[1600,128]{1,0:T(8,128)(2,1)S(1)}, u32[]{:S(2)}, u32[]{:S(2)}) %collective-permute-start.5) | collective-permute-done | bytes 409632 | tf_op jit(solution)/shard_map/ppermute | solution.py:98
  43.4 1.2 collective-permute-done.9.east
  44.7 1.0 copy-done.3
  45.7 0.8 split.1
  46.5 1.0 collective-permute-start.13
  47.5 2.9 %collective-permute-start.14 = (bf16[768,128]{1,0:T(8,128)(2,1)S(1)}, bf16[768,128]{1,0:T(8,128)(2,1)S(1)}, u32[]{:S(2)}, u32[]{:S(2)}) collective-permute-start(bf16[768,128]{1,0:T(8,128)(2,1)S(1)} %get-tuple-element.48), channel_id=1, source_target_pairs={{0,3},{1,0},{2,1},{3,2},{4,7},{5,4},{6,5},{7,6},{8,11},{9,8},{10,9... | collective-permute-start | bytes 589832 | tf_op jit(solution)/shard_map/ppermute | solution.py:98
  50.4 4.9 %lines.1 = (bf16[4,18,192,256]{3,2,1,0:T(8,128)(2,1)S(1)}, f32[27,256,512]{2,1,0:T(8,128)}) custom-call(s32[3]{0:T(128)S(1)} %pad_add_fusion.pos.refs_0_, bf16[1600,128]{1,0:T(8,128)(2,1)S(1)} %get-tuple-element.39.own.x_own, bf16[1600,128]{1,0:T(8,128)(2,1)S(1)} %collective-permute-done.3.x_x, bf16[1536,128]{1,0:T(8,128)(2,1)S(1)} %collective-permute-done.4.after.x_y, ...), custom_call_target="tpu_custom_call" | custom-call | bytes 1048576 | tf_op jit(solution)/shard_map/lines/pallas_call | solution.py:542
  55.3 0.8 collective-permute-done.13.one
  56.1 2.6 %collective-permute-done.14.two = bf16[768,128]{1,0:T(8,128)(2,1)S(1)} collective-permute-done((bf16[768,128]{1,0:T(8,128)(2,1)S(1)}, bf16[768,128]{1,0:T(8,128)(2,1)S(1)}, u32[]{:S(2)}, u32[]{:S(2)}) %collective-permute-start.14) | collective-permute-done | bytes 196640 | tf_op jit(solution)/shard_map/ppermute | solution.py:98
  59.9 1.2 collective-permute-done.15.s2
  61.1 8.5 %taps.1.held = f32[27,64,128]{2,1,0:T(8,128)S(1)} custom-call(s32[3]{0:T(128)S(1)} %pad_add_fusion.pos.refs_0_, bf16[4,18,192,256]{3,2,1,0:T(8,128)(2,1)S(1)} %get-tuple-element.46.after.xs, bf16[6,768,128]{2,1,0:T(8,128)(2,1)S(1)} %get-tuple-element.47.g, bf16[6,768,128]{2,1,0:T(8,128)(2,1)S(1)} %collective-permute-done.12.s, ...), custom_call_target="tpu_custom_call" | custom-call | flops 5435817984 | bytes 11108352 | tf_op jit(solution)/shard_map/taps/pallas_call | solution.py:116
  69.6 0.9 code.1
  70.5 1.3 collective-permute-start.17
  71.9 1.7 %collective-permute-start.18 = (bf16[1744,128]{1,0:T(8,128)(2,1)S(1)}, bf16[1744,128]{1,0:T(8,128)(2,1)S(1)}, u32[]{:S(2)}, u32[]{:S(2)}) collective-permute-start(bf16[1744,128]{1,0:T(8,128)(2,1)S(1)} %get-tuple-element.50.after.own.refs_1_), channel_id=1, source_target_pairs={{0,8},{1,9},{2,10},{3,11},{4,12},{5,13},{6,14},{7,15},{8,0},{9,1},... | collective-permute-start | bytes 1339400 | tf_op jit(solution)/shard_map/ppermute | solution.py:98
  74.2 3.2 %collective-permute-start.22 = (bf16[1360,128]{1,0:T(8,128)(2,1)S(1)}, bf16[1360,128]{1,0:T(8,128)(2,1)S(1)}, u32[]{:S(2)}, u32[]{:S(2)}) collective-permute-start(bf16[1360,128]{1,0:T(8,128)(2,1)S(1)} %get-tuple-element.53), channel_id=1, source_target_pairs={{0,3},{1,0},{2,1},{3,2},{4,7},{5,4},{6,5},{7,6},{8,11},{9,8},{10,9... | collective-permute-start | bytes 1044488 | tf_op jit(solution)/shard_map/ppermute | solution.py:98
  77.4 9.5 %field.1.after = bf16[4,4,48,256]{3,2,1,0:T(8,128)(2,1)} custom-call(s32[3]{0:T(128)S(1)} %pad_add_fusion.pos.refs_0_, bf16[1744,128]{1,0:T(8,128)(2,1)S(1)} %get-tuple-element.50.after.own.refs_1_, bf16[4,6,64,256]{3,2,1,0:T(8,128)(2,1)S(1)} %get-tuple-element.49.mine, bf16[4,6,64,256]{3,2,1,0:T(8,128)(2,1)S(1)} %collective-permute-done.16.after.theirs, ...), custom_call_target="tpu_custom_call" | custom-call | flops 10871635968 | bytes 7077888 | tf_op jit(solution)/shard_map/field/pallas_call | solution.py:579
  87.0 1.0 copy-done.5
  88.5 0.8 collective-permute-start.19
  89.7 1.4 collective-permute-done.22.east.refs_2_
  91.0 4.3 %collective-permute-done.20.after2.bottom.refs_5_ = bf16[848,128]{1,0:T(8,128)(2,1)S(1)} collective-permute-done((bf16[848,128]{1,0:T(8,128)(2,1)S(1)}, bf16[848,128]{1,0:T(8,128)(2,1)S(1)}, u32[]{:S(2)}, u32[]{:S(2)}) %collective-permute-start.20) | collective-permute-done | bytes 217120 | tf_op jit(solution)/shard_map/ppermute | solution.py:98
  96.0 1.3 collective-permute-start.33
  97.6 7.4 %collective-permute-done.23.after.half_3 = bf16[672,128]{1,0:T(8,128)(2,1)S(1)} collective-permute-done((bf16[672,128]{1,0:T(8,128)(2,1)S(1)}, bf16[672,128]{1,0:T(8,128)(2,1)S(1)}, u32[]{:S(2)}, u32[]{:S(2)}) %collective-permute-start.23) | collective-permute-done | bytes 172064 | tf_op jit(solution)/shard_map/ppermute | solution.py:98
  105.6 3.8 %collective-permute-start.28 = (bf16[688,128]{1,0:T(8,128)(2,1)S(1)}, bf16[688,128]{1,0:T(8,128)(2,1)S(1)}, u32[]{:S(2)}, u32[]{:S(2)}) collective-permute-start(bf16[688,128]{1,0:T(8,128)(2,1)S(1)} %get-tuple-element.57), channel_id=1, source_target_pairs={{0,3},{1,0},{2,1},{3,2},{4,7},{5,4},{6,5},{7,6},{8,11},{9,8},{10,9... | collective-permute-start | bytes 528392 | tf_op jit(solution)/shard_map/ppermute | solution.py:98
  109.5 9.4 %collective-permute-done.28.half_1 = bf16[688,128]{1,0:T(8,128)(2,1)S(1)} collective-permute-done((bf16[688,128]{1,0:T(8,128)(2,1)S(1)}, bf16[688,128]{1,0:T(8,128)(2,1)S(1)}, u32[]{:S(2)}, u32[]{:S(2)}) %collective-permute-start.28) | collective-permute-done | bytes 176160 | tf_op jit(solution)/shard_map/ppermute | solution.py:98
  119.5 0.9 collective-permute-start.29
  120.3 1.7 %collective-permute-start.30 = (bf16[1360,128]{1,0:T(8,128)(2,1)S(1)}, bf16[1360,128]{1,0:T(8,128)(2,1)S(1)}, u32[]{:S(2)}, u32[]{:S(2)}) collective-permute-start(bf16[1360,128]{1,0:T(8,128)(2,1)S(1)} %across.1.refs_3_), channel_id=1, source_target_pairs={{0,8},{1,9},{2,10},{3,11},{4,12},{5,13},{6,14},{7,15},{8,0},{9,1},... | collective-permute-start | bytes 1044488 | tf_op jit(solution)/shard_map/ppermute | solution.py:98
  122.7 1.3 collective-permute-start.35
  124.3 2.0 %collective-permute-done.25.block_1.refs_8_ = bf16[1600,128]{1,0:T(8,128)(2,1)S(1)} collective-permute-done((bf16[1600,128]{1,0:T(8,128)(2,1)S(1)}, bf16[1600,128]{1,0:T(8,128)(2,1)S(1)}, u32[]{:S(2)}, u32[]{:S(2)}) %collective-permute-start.25) | collective-permute-done | bytes 409632 | tf_op jit(solution)/shard_map/ppermute | solution.py:98
  127.2 3.9 %collective-permute-start.27 = (bf16[800,128]{1,0:T(8,128)(2,1)S(1)}, bf16[800,128]{1,0:T(8,128)(2,1)S(1)}, u32[]{:S(2)}, u32[]{:S(2)}) collective-permute-start(bf16[800,128]{1,0:T(8,128)(2,1)S(1)} %get-tuple-element.56), channel_id=1, source_target_pairs={{0,3},{1,0},{2,1},{3,2},{4,7},{5,4},{6,5},{7,6},{8,11},{9,8},{10,9... | collective-permute-start | bytes 614408 | tf_op jit(solution)/shard_map/ppermute | solution.py:98
  131.1 3.1 %unpack_1.1 = (f32[27,256,512]{2,1,0:T(8,128)}, f32[8,128]{1,0:T(8,128)S(1)}) custom-call(s32[3]{0:T(128)S(1)} %pad_add_fusion.pos.refs_0_, bf16[1744,128]{1,0:T(8,128)(2,1)S(1)} %get-tuple-element.50.after.own.refs_1_, bf16[1744,128]{1,0:T(8,128)(2,1)S(1)} %collective-permute-done.17.by_x.x.refs_2_, ...), custom_call_target="tpu_custom_call", output_to_operand_aliasing={{0}: (7, {})} | custom-call | bytes 4194304 | tf_op jit(solution)/shard_map/unpack_1/pallas_call | solution.py:408
  134.8 1.8 %collective-permute-start.32 = (bf16[720,128]{1,0:T(8,128)(2,1)S(1)}, bf16[720,128]{1,0:T(8,128)(2,1)S(1)}, u32[]{:S(2)}, u32[]{:S(2)}) collective-permute-start(bf16[720,128]{1,0:T(8,128)(2,1)S(1)} %get-tuple-element.61), channel_id=1, source_target_pairs={{0,8},{1,9},{2,10},{3,11},{4,12},{5,13},{6,14},{7,15},{8,0},{9,1},... | collective-permute-start | bytes 552968 | tf_op jit(solution)/shard_map/ppermute | solution.py:98
  136.6 0.8 collective-permute-start.31
  137.5 6.4 %unpack_2.1 = (f32[27,256,512]{2,1,0:T(8,128)}, f32[8,128]{1,0:T(8,128)}) custom-call(s32[3]{0:T(128)S(1)} %pad_add_fusion.pos.refs_0_, bf16[1360,128]{1,0:T(8,128)(2,1)S(1)} %collective-permute-done.21.west.refs_1_, bf16[1360,128]{1,0:T(8,128)(2,1)S(1)} %collective-permute-done.22.east.refs_2_, ...), custom_call_target="tpu_custom_call", output_to_operand_aliasing={{0}: (10, {})} | custom-call | bytes 4194304 | tf_op jit(solution)/shard_map/unpack_2/pallas_call | solution.py:408
  143.9 3.7 %unpack_3.1 = (f32[27,256,512]{2,1,0:T(8,128)}, f32[8,128]{1,0:T(8,128)}) custom-call(s32[3]{0:T(128)S(1)} %pad_add_fusion.pos.refs_0_, bf16[800,128]{1,0:T(8,128)(2,1)S(1)} %collective-permute-done.26.refs_1_, bf16[800,128]{1,0:T(8,128)(2,1)S(1)} %collective-permute-done.27.refs_2_, ...), custom_call_target="tpu_custom_call", output_to_operand_aliasing={{0}: (8, {})} | custom-call | bytes 4194304 | tf_op jit(solution)/shard_map/unpack_3/pallas_call | solution.py:408
  (63 shorter events, 9.9 us)
Async XLA Ops:
  0.7 1.0 copy-start.2
  1.7 1.0 copy-start.4
  3.6 19.4 %collective-permute-start.6 = (bf16[768,128]{1,0:T(8,128)(2,1)S(1)}, bf16[768,128]{1,0:T(8,128)(2,1)S(1)}, u32[]{:S(2)}, u32[]{:S(2)}) collective-permute-start(bf16[768,128]{1,0:T(8,128)(2,1)S(1)} %get-tuple-element.41), channel_id=1, source_target_pairs={{0,0},{1,1},{2,2},{3,3},{4,4},{5,5},{6,6},{7,7},{8,16},{9,17},{10,... | collective-permute-start | bytes 589832 | tf_op jit(solution)/shard_map/ppermute | solution.py:98
  4.2 14.1 %collective-permute-start = (bf16[416,128]{1,0:T(8,128)(2,1)S(1)}, bf16[416,128]{1,0:T(8,128)(2,1)S(1)}, u32[]{:S(2)}, u32[]{:S(2)}) collective-permute-start(bf16[416,128]{1,0:T(8,128)(2,1)S(1)} %get-tuple-element.36), channel_id=1, source_target_pairs={{0,1},{1,2},{2,3},{3,0},{4,5},{5,6},{6,7},{7,4},{8,9},{9,10},{10,1... | collective-permute-start | bytes 319496 | tf_op jit(solution)/shard_map/ppermute | solution.py:98
  7.3 16.7 %collective-permute-start.7 = (bf16[768,128]{1,0:T(8,128)(2,1)S(1)}, bf16[768,128]{1,0:T(8,128)(2,1)S(1)}, u32[]{:S(2)}, u32[]{:S(2)}) collective-permute-start(bf16[768,128]{1,0:T(8,128)(2,1)S(1)} %get-tuple-element.42), channel_id=1, source_target_pairs={{0,4},{1,5},{2,6},{3,7},{4,0},{5,1},{6,2},{7,3},{8,20},{9,21},{10,... | collective-permute-start | bytes 589832 | tf_op jit(solution)/shard_map/ppermute | solution.py:98
  8.8 9.6 %collective-permute-start.1 = (bf16[384,128]{1,0:T(8,128)(2,1)S(1)}, bf16[384,128]{1,0:T(8,128)(2,1)S(1)}, u32[]{:S(2)}, u32[]{:S(2)}) collective-permute-start(bf16[384,128]{1,0:T(8,128)(2,1)S(1)} %get-tuple-element.37), channel_id=1, source_target_pairs={{0,2},{1,3},{2,0},{3,1},{4,6},{5,7},{6,4},{7,5},{8,10},{9,11},{10,... | collective-permute-start | bytes 294920 | tf_op jit(solution)/shard_map/ppermute | solution.py:98
  11.4 9.8 %collective-permute-start.2 = (bf16[416,128]{1,0:T(8,128)(2,1)S(1)}, bf16[416,128]{1,0:T(8,128)(2,1)S(1)}, u32[]{:S(2)}, u32[]{:S(2)}) collective-permute-start(bf16[416,128]{1,0:T(8,128)(2,1)S(1)} %get-tuple-element.38), channel_id=1, source_target_pairs={{0,3},{1,0},{2,1},{3,2},{4,7},{5,4},{6,5},{7,6},{8,11},{9,8},{10,9... | collective-permute-start | bytes 319496 | tf_op jit(solution)/shard_map/ppermute | solution.py:98
  18.4 7.6 %collective-permute-start.10 = (bf16[384,128]{1,0:T(8,128)(2,1)S(1)}, bf16[384,128]{1,0:T(8,128)(2,1)S(1)}, u32[]{:S(2)}, u32[]{:S(2)}) collective-permute-start(bf16[384,128]{1,0:T(8,128)(2,1)S(1)} %get-tuple-element.43), channel_id=1, source_target_pairs={{0,4},{1,5},{2,6},{3,7},{4,0},{5,1},{6,2},{7,3},{8,12},{9,13},{10,... | collective-permute-start | bytes 294920 | tf_op jit(solution)/shard_map/ppermute | solution.py:98
  18.4 8.3 %collective-permute-start.11 = (bf16[384,128]{1,0:T(8,128)(2,1)S(1)}, bf16[384,128]{1,0:T(8,128)(2,1)S(1)}, u32[]{:S(2)}, u32[]{:S(2)}) collective-permute-start(bf16[384,128]{1,0:T(8,128)(2,1)S(1)} %get-tuple-element.44), channel_id=1, source_target_pairs={{0,12},{1,13},{2,14},{3,15},{4,8},{5,9},{6,10},{7,11},{8,4},{9,5},... | collective-permute-start | bytes 294920 | tf_op jit(solution)/shard_map/ppermute | solution.py:98
  21.8 13.4 %collective-permute-start.3 = (bf16[1600,128]{1,0:T(8,128)(2,1)S(1)}, bf16[1600,128]{1,0:T(8,128)(2,1)S(1)}, u32[]{:S(2)}, u32[]{:S(2)}) collective-permute-start(bf16[1600,128]{1,0:T(8,128)(2,1)S(1)} %get-tuple-element.39.own.x_own), channel_id=1, source_target_pairs={{0,4},{1,5},{2,6},{3,7},{4,0},{5,1},{6,2},{7,3},{8,12},{9,13},{10,... | collective-permute-start | bytes 1228808 | tf_op jit(solution)/shard_map/ppermute | solution.py:98
  23.0 20.4 %collective-permute-start.5 = (bf16[1600,128]{1,0:T(8,128)(2,1)S(1)}, bf16[1600,128]{1,0:T(8,128)(2,1)S(1)}, u32[]{:S(2)}, u32[]{:S(2)}) collective-permute-start(bf16[1600,128]{1,0:T(8,128)(2,1)S(1)} %get-tuple-element.39.own.x_own), channel_id=1, source_target_pairs={{0,12},{1,13},{2,14},{3,15},{4,8},{5,9},{6,10},{7,11},{8,4},{9,5},... | collective-permute-start | bytes 1228808 | tf_op jit(solution)/shard_map/ppermute | solution.py:98
  24.1 11.1 %collective-permute-start.4 = (bf16[1536,128]{1,0:T(8,128)(2,1)S(1)}, bf16[1536,128]{1,0:T(8,128)(2,1)S(1)}, u32[]{:S(2)}, u32[]{:S(2)}) collective-permute-start(bf16[1536,128]{1,0:T(8,128)(2,1)S(1)} %get-tuple-element.40), channel_id=1, source_target_pairs={{0,8},{1,9},{2,10},{3,11},{4,12},{5,13},{6,14},{7,15},{8,0},{9,1},... | collective-permute-start | bytes 1179656 | tf_op jit(solution)/shard_map/ppermute | solution.py:98
  26.0 17.5 %collective-permute-start.8 = (bf16[2,768,128]{2,1,0:T(8,128)(2,1)S(1)}, bf16[2,768,128]{2,1,0:T(8,128)(2,1)S(1)}, u32[]{:S(2)}, u32[]{:S(2)}) collective-permute-start(bf16[2,768,128]{2,1,0:T(8,128)(2,1)S(1)} %pair_0.1.here), channel_id=1, source_target_pairs={{0,1},{1,2},{2,3},{3,0},{4,5},{5,6},{6,7},{7,4},{8,9},{9,10},{10,1... | collective-permute-start | bytes 1179656 | tf_op jit(solution)/shard_map/ppermute | solution.py:98
  26.7 18.0 %collective-permute-start.9 = (bf16[2,768,128]{2,1,0:T(8,128)(2,1)S(1)}, bf16[2,768,128]{2,1,0:T(8,128)(2,1)S(1)}, u32[]{:S(2)}, u32[]{:S(2)}) collective-permute-start(bf16[2,768,128]{2,1,0:T(8,128)(2,1)S(1)} %pair_0.1.here), channel_id=1, source_target_pairs={{0,3},{1,0},{2,1},{3,2},{4,7},{5,4},{6,5},{7,6},{8,11},{9,8},{10,9... | collective-permute-start | bytes 1179656 | tf_op jit(solution)/shard_map/ppermute | solution.py:98
  44.7 1.0 copy-start.3
  46.4 14.6 %collective-permute-start.12 = (bf16[6,768,128]{2,1,0:T(8,128)(2,1)S(1)}, bf16[6,768,128]{2,1,0:T(8,128)(2,1)S(1)}, u32[]{:S(2)}, u32[]{:S(2)}) collective-permute-start(bf16[6,768,128]{2,1,0:T(8,128)(2,1)S(1)} %get-tuple-element.47.g), channel_id=1, source_target_pairs={{0,16},{1,17},{2,18},{3,19},{4,20},{5,21},{6,22},{7,23},{8,24},{9,... | collective-permute-start | bytes 3538952 | tf_op jit(solution)/shard_map/ppermute | solution.py:98
  46.5 9.6 %collective-permute-start.13 = (bf16[768,128]{1,0:T(8,128)(2,1)S(1)}, bf16[768,128]{1,0:T(8,128)(2,1)S(1)}, u32[]{:S(2)}, u32[]{:S(2)}) collective-permute-start(bf16[768,128]{1,0:T(8,128)(2,1)S(1)} %get-tuple-element.45.after), channel_id=1, source_target_pairs={{0,1},{1,2},{2,3},{3,0},{4,5},{5,6},{6,7},{7,4},{8,9},{9,10},{10,1... | collective-permute-start | bytes 589832 | tf_op jit(solution)/shard_map/ppermute | solution.py:98
  47.5 11.2 %collective-permute-start.14 = (bf16[768,128]{1,0:T(8,128)(2,1)S(1)}, bf16[768,128]{1,0:T(8,128)(2,1)S(1)}, u32[]{:S(2)}, u32[]{:S(2)}) collective-permute-start(bf16[768,128]{1,0:T(8,128)(2,1)S(1)} %get-tuple-element.48), channel_id=1, source_target_pairs={{0,3},{1,0},{2,1},{3,2},{4,7},{5,4},{6,5},{7,6},{8,11},{9,8},{10,9... | collective-permute-start | bytes 589832 | tf_op jit(solution)/shard_map/ppermute | solution.py:98
  58.7 18.7 %slice-start = ((s8[7077888]{0:T(1024)(128)(4,1)}), s8[4194304]{0:T(1024)(128)(4,1)S(1)}, s32[]{:S(2)}) async-start(s8[7077888]{0:T(1024)(128)(4,1)} %bitcast.12), calls=%async_computation | async-start | bytes 8388608
  59.3 1.8 %collective-permute-start.15 = (bf16[2,768,128]{2,1,0:T(8,128)(2,1)S(1)}, bf16[2,768,128]{2,1,0:T(8,128)(2,1)S(1)}, u32[]{:S(2)}, u32[]{:S(2)}) collective-permute-start(bf16[2,768,128]{2,1,0:T(8,128)(2,1)S(1)} %pair.1.g2), channel_id=1, source_target_pairs={{0,16},{1,17},{2,18},{3,19},{4,20},{5,21},{6,22},{7,23},{8,24},{9,... | collective-permute-start | bytes 1179656 | tf_op jit(solution)/shard_map/ppermute | solution.py:98
  59.4 18.1 %slice-start.1 = ((s8[7077888]{0:T(1024)(128)(4,1)}), s8[2883584]{0:T(1024)(128)(4,1)S(1)}, s32[]{:S(2)}) async-start(s8[7077888]{0:T(1024)(128)(4,1)} %bitcast.12), calls=%async_computation.1 | async-start | bytes 5767168
  59.4 10.2 %collective-permute-start.16 = (bf16[4,6,64,256]{3,2,1,0:T(8,128)(2,1)S(1)}, bf16[4,6,64,256]{3,2,1,0:T(8,128)(2,1)S(1)}, u32[]{:S(2)}, u32[]{:S(2)}) collective-permute-start(bf16[4,6,64,256]{3,2,1,0:T(8,128)(2,1)S(1)} %get-tuple-element.49.mine), channel_id=1, source_target_pairs={{0,16},{1,17},{2,18},{3,19},{4,20},{5,21},{6,22},{7,23},{8,24},{9,... | collective-permute-start | bytes 2359304 | tf_op jit(solution)/shard_map/ppermute | solution.py:98
  70.5 16.4 %collective-permute-start.17 = (bf16[1744,128]{1,0:T(8,128)(2,1)S(1)}, bf16[1744,128]{1,0:T(8,128)(2,1)S(1)}, u32[]{:S(2)}, u32[]{:S(2)}) collective-permute-start(bf16[1744,128]{1,0:T(8,128)(2,1)S(1)} %get-tuple-element.50.after.own.refs_1_), channel_id=1, source_target_pairs={{0,4},{1,5},{2,6},{3,7},{4,0},{5,1},{6,2},{7,3},{8,12},{9,13},{10,... | collective-permute-start | bytes 1339400 | tf_op jit(solution)/shard_map/ppermute | solution.py:98
  71.9 15.1 %collective-permute-start.18 = (bf16[1744,128]{1,0:T(8,128)(2,1)S(1)}, bf16[1744,128]{1,0:T(8,128)(2,1)S(1)}, u32[]{:S(2)}, u32[]{:S(2)}) collective-permute-start(bf16[1744,128]{1,0:T(8,128)(2,1)S(1)} %get-tuple-element.50.after.own.refs_1_), channel_id=1, source_target_pairs={{0,8},{1,9},{2,10},{3,11},{4,12},{5,13},{6,14},{7,15},{8,0},{9,1},... | collective-permute-start | bytes 1339400 | tf_op jit(solution)/shard_map/ppermute | solution.py:98
  73.6 16.0 %collective-permute-start.21 = (bf16[1360,128]{1,0:T(8,128)(2,1)S(1)}, bf16[1360,128]{1,0:T(8,128)(2,1)S(1)}, u32[]{:S(2)}, u32[]{:S(2)}) collective-permute-start(bf16[1360,128]{1,0:T(8,128)(2,1)S(1)} %get-tuple-element.53), channel_id=1, source_target_pairs={{0,1},{1,2},{2,3},{3,0},{4,5},{5,6},{6,7},{7,4},{8,9},{9,10},{10,1... | collective-permute-start | bytes 1044488 | tf_op jit(solution)/shard_map/ppermute | solution.py:98
  74.2 16.8 %collective-permute-start.22 = (bf16[1360,128]{1,0:T(8,128)(2,1)S(1)}, bf16[1360,128]{1,0:T(8,128)(2,1)S(1)}, u32[]{:S(2)}, u32[]{:S(2)}) collective-permute-start(bf16[1360,128]{1,0:T(8,128)(2,1)S(1)} %get-tuple-element.53), channel_id=1, source_target_pairs={{0,3},{1,0},{2,1},{3,2},{4,7},{5,4},{6,5},{7,6},{8,11},{9,8},{10,9... | collective-permute-start | bytes 1044488 | tf_op jit(solution)/shard_map/ppermute | solution.py:98
  87.0 1.0 copy-start.5
  88.5 6.8 %collective-permute-start.19 = (bf16[896,128]{1,0:T(8,128)(2,1)S(1)}, bf16[896,128]{1,0:T(8,128)(2,1)S(1)}, u32[]{:S(2)}, u32[]{:S(2)}) collective-permute-start(bf16[896,128]{1,0:T(8,128)(2,1)S(1)} %get-tuple-element.51), channel_id=1, source_target_pairs={{0,4},{1,5},{2,6},{3,7},{4,0},{5,1},{6,2},{7,3},{8,12},{9,13},{10,... | collective-permute-start | bytes 688136 | tf_op jit(solution)/shard_map/ppermute | solution.py:98
  89.4 6.0 %collective-permute-start.20 = (bf16[848,128]{1,0:T(8,128)(2,1)S(1)}, bf16[848,128]{1,0:T(8,128)(2,1)S(1)}, u32[]{:S(2)}, u32[]{:S(2)}) collective-permute-start(bf16[848,128]{1,0:T(8,128)(2,1)S(1)} %get-tuple-element.52), channel_id=1, source_target_pairs={{0,8},{1,9},{2,10},{3,11},{4,12},{5,13},{6,14},{7,15},{8,0},{9,1},... | collective-permute-start | bytes 651272 | tf_op jit(solution)/shard_map/ppermute | solution.py:98
  96.0 24.3 %collective-permute-start.33 = (bf16[2720,128]{1,0:T(8,128)(2,1)S(1)}, bf16[2720,128]{1,0:T(8,128)(2,1)S(1)}, u32[]{:S(2)}, u32[]{:S(2)}) collective-permute-start(bf16[2720,128]{1,0:T(8,128)(2,1)S(1)} %get-tuple-element.62), channel_id=1, source_target_pairs={{0,4},{1,5},{2,6},{3,7},{4,0},{5,1},{6,2},{7,3},{8,12},{9,13},{10,... | collective-permute-start | bytes 2088968 | tf_op jit(solution)/shard_map/ppermute | solution.py:98
  97.3 24.8 %collective-permute-start.34 = (bf16[2720,128]{1,0:T(8,128)(2,1)S(1)}, bf16[2720,128]{1,0:T(8,128)(2,1)S(1)}, u32[]{:S(2)}, u32[]{:S(2)}) collective-permute-start(bf16[2720,128]{1,0:T(8,128)(2,1)S(1)} %get-tuple-element.62), channel_id=1, source_target_pairs={{0,8},{1,9},{2,10},{3,11},{4,12},{5,13},{6,14},{7,15},{8,0},{9,1},... | collective-permute-start | bytes 2088968 | tf_op jit(solution)/shard_map/ppermute | solution.py:98
  97.6 7.4 %collective-permute-start.23 = (bf16[672,128]{1,0:T(8,128)(2,1)S(1)}, bf16[672,128]{1,0:T(8,128)(2,1)S(1)}, u32[]{:S(2)}, u32[]{:S(2)}) collective-permute-start(bf16[672,128]{1,0:T(8,128)(2,1)S(1)} %get-tuple-element.54), channel_id=1, source_target_pairs={{0,1},{1,2},{2,3},{3,0},{4,5},{5,6},{6,7},{7,4},{8,9},{9,10},{10,1... | collective-permute-start | bytes 516104 | tf_op jit(solution)/shard_map/ppermute | solution.py:98
  105.6 18.4 %collective-permute-start.24 = (bf16[1600,128]{1,0:T(8,128)(2,1)S(1)}, bf16[1600,128]{1,0:T(8,128)(2,1)S(1)}, u32[]{:S(2)}, u32[]{:S(2)}) collective-permute-start(bf16[1600,128]{1,0:T(8,128)(2,1)S(1)} %block.1.after.refs_6_), channel_id=1, source_target_pairs={{0,1},{1,2},{2,3},{3,0},{4,5},{5,6},{6,7},{7,4},{8,9},{9,10},{10,1... | collective-permute-start | bytes 1228808 | tf_op jit(solution)/shard_map/ppermute | solution.py:98
  105.6 13.3 %collective-permute-start.28 = (bf16[688,128]{1,0:T(8,128)(2,1)S(1)}, bf16[688,128]{1,0:T(8,128)(2,1)S(1)}, u32[]{:S(2)}, u32[]{:S(2)}) collective-permute-start(bf16[688,128]{1,0:T(8,128)(2,1)S(1)} %get-tuple-element.57), channel_id=1, source_target_pairs={{0,3},{1,0},{2,1},{3,2},{4,7},{5,4},{6,5},{7,6},{8,11},{9,8},{10,9... | collective-permute-start | bytes 528392 | tf_op jit(solution)/shard_map/ppermute | solution.py:98
  109.4 16.8 %collective-permute-start.25 = (bf16[1600,128]{1,0:T(8,128)(2,1)S(1)}, bf16[1600,128]{1,0:T(8,128)(2,1)S(1)}, u32[]{:S(2)}, u32[]{:S(2)}) collective-permute-start(bf16[1600,128]{1,0:T(8,128)(2,1)S(1)} %block.1.after.refs_6_), channel_id=1, source_target_pairs={{0,3},{1,0},{2,1},{3,2},{4,7},{5,4},{6,5},{7,6},{8,11},{9,8},{10,9... | collective-permute-start | bytes 1228808 | tf_op jit(solution)/shard_map/ppermute | solution.py:98
  119.5 7.7 %collective-permute-start.29 = (bf16[1360,128]{1,0:T(8,128)(2,1)S(1)}, bf16[1360,128]{1,0:T(8,128)(2,1)S(1)}, u32[]{:S(2)}, u32[]{:S(2)}) collective-permute-start(bf16[1360,128]{1,0:T(8,128)(2,1)S(1)} %across.1.refs_3_), channel_id=1, source_target_pairs={{0,4},{1,5},{2,6},{3,7},{4,0},{5,1},{6,2},{7,3},{8,12},{9,13},{10,... | collective-permute-start | bytes 1044488 | tf_op jit(solution)/shard_map/ppermute | solution.py:98
  120.3 17.1 %copy-start = (bf16[2720,128]{1,0:T(8,128)(2,1)}, bf16[2720,128]{1,0:T(8,128)(2,1)S(1)}, u32[]{:S(2)}) copy-start(bf16[2720,128]{1,0:T(8,128)(2,1)S(1)} %collective-permute-done.33.by_x.refs_3_) | copy-start | bytes 2088964
  120.3 13.9 %collective-permute-start.30 = (bf16[1360,128]{1,0:T(8,128)(2,1)S(1)}, bf16[1360,128]{1,0:T(8,128)(2,1)S(1)}, u32[]{:S(2)}, u32[]{:S(2)}) collective-permute-start(bf16[1360,128]{1,0:T(8,128)(2,1)S(1)} %across.1.refs_3_), channel_id=1, source_target_pairs={{0,8},{1,9},{2,10},{3,11},{4,12},{5,13},{6,14},{7,15},{8,0},{9,1},... | collective-permute-start | bytes 1044488 | tf_op jit(solution)/shard_map/ppermute | solution.py:98
  122.1 15.4 %copy-start.1 = (bf16[2720,128]{1,0:T(8,128)(2,1)}, bf16[2720,128]{1,0:T(8,128)(2,1)S(1)}, u32[]{:S(2)}) copy-start(bf16[2720,128]{1,0:T(8,128)(2,1)S(1)} %collective-permute-done.34.by_y.refs_4_) | copy-start | bytes 2088964
  122.7 14.0 %collective-permute-start.35 = (bf16[1360,128]{1,0:T(8,128)(2,1)S(1)}, bf16[1360,128]{1,0:T(8,128)(2,1)S(1)}, u32[]{:S(2)}, u32[]{:S(2)}) collective-permute-start(bf16[1360,128]{1,0:T(8,128)(2,1)S(1)} %get-tuple-element.63), channel_id=1, source_target_pairs={{0,4},{1,5},{2,6},{3,7},{4,0},{5,1},{6,2},{7,3},{8,12},{9,13},{10,... | collective-permute-start | bytes 1044488 | tf_op jit(solution)/shard_map/ppermute | solution.py:98
  124.0 13.5 %collective-permute-start.36 = (bf16[1360,128]{1,0:T(8,128)(2,1)S(1)}, bf16[1360,128]{1,0:T(8,128)(2,1)S(1)}, u32[]{:S(2)}, u32[]{:S(2)}) collective-permute-start(bf16[1360,128]{1,0:T(8,128)(2,1)S(1)} %get-tuple-element.64), channel_id=1, source_target_pairs={{0,8},{1,9},{2,10},{3,11},{4,12},{5,13},{6,14},{7,15},{8,0},{9,1},... | collective-permute-start | bytes 1044488 | tf_op jit(solution)/shard_map/ppermute | solution.py:98
  126.8 17.1 %collective-permute-start.26 = (bf16[800,128]{1,0:T(8,128)(2,1)S(1)}, bf16[800,128]{1,0:T(8,128)(2,1)S(1)}, u32[]{:S(2)}, u32[]{:S(2)}) collective-permute-start(bf16[800,128]{1,0:T(8,128)(2,1)S(1)} %get-tuple-element.55.refs_9_), channel_id=1, source_target_pairs={{0,1},{1,2},{2,3},{3,0},{4,5},{5,6},{6,7},{7,4},{8,9},{9,10},{10,1... | collective-permute-start | bytes 614408 | tf_op jit(solution)/shard_map/ppermute | solution.py:98
  127.2 16.7 %collective-permute-start.27 = (bf16[800,128]{1,0:T(8,128)(2,1)S(1)}, bf16[800,128]{1,0:T(8,128)(2,1)S(1)}, u32[]{:S(2)}, u32[]{:S(2)}) collective-permute-start(bf16[800,128]{1,0:T(8,128)(2,1)S(1)} %get-tuple-element.56), channel_id=1, source_target_pairs={{0,3},{1,0},{2,1},{3,2},{4,7},{5,4},{6,5},{7,6},{8,11},{9,8},{10,9... | collective-permute-start | bytes 614408 | tf_op jit(solution)/shard_map/ppermute | solution.py:98
  134.8 9.0 %collective-permute-start.32 = (bf16[720,128]{1,0:T(8,128)(2,1)S(1)}, bf16[720,128]{1,0:T(8,128)(2,1)S(1)}, u32[]{:S(2)}, u32[]{:S(2)}) collective-permute-start(bf16[720,128]{1,0:T(8,128)(2,1)S(1)} %get-tuple-element.61), channel_id=1, source_target_pairs={{0,8},{1,9},{2,10},{3,11},{4,12},{5,13},{6,14},{7,15},{8,0},{9,1},... | collective-permute-start | bytes 552968 | tf_op jit(solution)/shard_map/ppermute | solution.py:98
  136.6 7.2 %collective-permute-start.31 = (bf16[640,128]{1,0:T(8,128)(2,1)S(1)}, bf16[640,128]{1,0:T(8,128)(2,1)S(1)}, u32[]{:S(2)}, u32[]{:S(2)}) collective-permute-start(bf16[640,128]{1,0:T(8,128)(2,1)S(1)} %get-tuple-element.60), channel_id=1, source_target_pairs={{0,4},{1,5},{2,6},{3,7},{4,0},{5,1},{6,2},{7,3},{8,12},{9,13},{10,... | collective-permute-start | bytes 491528 | tf_op jit(solution)/shard_map/ppermute | solution.py:98

commit v17 on v16

--- a/solution.py
+++ b/solution.py
@@ -334,8 +334,8 @@
     half_1[...] = east[half:, :]
 
 
-def cross_kernel(pos, by_x, by_y, after, top, bottom):
-    del pos, after
+def cross_kernel(pos, by_x, by_y, after1, after2, top, bottom):
+    del pos, after1, after2
     cut = top.shape[0]
     top[...] = by_y[0:cut, :]
     bottom[...] = by_x[cut:, :]
@@ -348,8 +348,8 @@
     late[half:, :] = half_1[...]
 
 
-def block_kernel(pos, own, x, y, top, bottom, after, block):
-    del pos, after
+def block_kernel(pos, own, x, y, top, bottom, block):
+    del pos
     rows = block.shape[0] // 4
     for at, (piece, end) in enumerate(((own, own), (x, x), (y, y), (top, bottom))):
         block[at * rows : (at + 1) * rows - 16, :] = piece[0 : rows - 16, :]
@@ -557,7 +557,7 @@
         pair_kernel, [jax.ShapeDtypeStruct((2, cells, wide), bf16)], (pos, g2a, g2b, xs), [], 0, "pair", 16, held=1
     )
     s2 = move(g2, sibling)
-    early = 6
+    early = 3
     cut, end = early * span, 27 * span
     size = end + 16 - cut
     half = size // 32 * 16
@@ -602,16 +602,16 @@
     def to_plane(share):
         return move(share, lat_xor(1)), move(share, lat_xor(2))
 
-    def to_diagonal(by_x, by_y, cut, after, name):
+    def to_diagonal(by_x, by_y, cut, after1, after2, name):
         top, bottom = call(
-            cross_kernel, [slab(cut), slab(by_x.shape[0] - cut)], (pos, by_x, by_y, after), [], 0, name, 16, held=1
+            cross_kernel, [slab(cut), slab(by_x.shape[0] - cut)], (pos, by_x, by_y, after1, after2), [], 0, name, 16, held=2
         )
         return move(top, lat_xor(1)), move(bottom, lat_xor(2))
 
     from_3 = move(late, lon_by(1))
     from_1 = move(late, lon_by(-1))
     own_x, own_y = to_plane(own)
-    own_top, own_bottom = to_diagonal(own_x, own_y, own_cut, field, "cross_1")
+    own_top, own_bottom = to_diagonal(own_x, own_y, own_cut, field, own, "cross_1")
     pair, half_3, half_1 = call(
         both_kernel,
         [slab(2 * size), slab(half), slab(size - half)],
@@ -626,12 +626,12 @@
     half_1 = move(half_1, lon_by(-1))
     pair_x, pair_y = to_plane(pair)
     (block,) = call(
-        block_kernel, [slab(4 * first_rows)], (pos, own, own_x, own_y, own_top, own_bottom, half_3), [], 0, "block", 16, held=1
+        block_kernel, [slab(4 * first_rows)], (pos, own, own_x, own_y, own_top, own_bottom), [], 0, "block", 16
     )
     early_3 = move(block, lon_by(1))
     early_1 = move(block, lon_by(-1))
-    (from_2,) = call(across_kernel, [slab(size)], (pos, half_3, half_1, block), [], 0, "across", 16, held=1)
-    pair_top, pair_bottom = to_diagonal(pair_x, pair_y, size, block, "cross_2")
+    (from_2,) = call(across_kernel, [slab(size)], (pos, half_3, half_1, pair), [], 0, "across", 16, held=1)
+    pair_top, pair_bottom = to_diagonal(pair_x, pair_y, size, early_1, early_3, "cross_2")
     from_2x, from_2y = to_plane(from_2)
     hand_3, hand_1 = call(hand_kernel, [slab(2 * first_rows)] * 2, (pos, early_3, early_1), [], 0, "hand", 16)
     early_2a = move(hand_3, lon_by(1))
@@ -648,7 +648,7 @@
     total, token = unpack(
         pos, total, [own, own_x, own_y, own_top, own_bottom], [block], [(0, 0, 27, pieces)], span, "unpack_1"
     )
-    from_2top, from_2bottom = to_diagonal(from_2x, from_2y, late_cut, token, "cross_3")
+    from_2top, from_2bottom = to_diagonal(from_2x, from_2y, late_cut, token, pair, "cross_3")
     slabs = [
         (3, early, 27 - early, [late_piece(0), late_piece(2), late_piece(3), late_piece(4)]),
         (1, early, 27 - early, [late_piece(1), late_piece(2, size), late_piece(3, size), late_piece(5)]),

time: 148 us -> 146 us (0.986)
  waiting for transfers between devices: 49.8 us -> 46.8 us
    ppermute x37, waiting for transfers between devices: 49.8 us -> 46.8 us  [move(): return lax.ppermute(x, AXES, pairs)]
    unnamed x16 -> x14, local copies, waits for them, and re-layouts: 4 us -> 4 us
  transfers between devices with their start and end apart: 37 -> 37, of which waited for: 13 -> 15; matrix products, arithmetic and copies ran while one was open for 0% -> 0% of each run, Pallas kernels for 25% -> 26%
where the time goes in v17:
time: 146 us; the launch traced here: 145 us
  starting transfers between devices  49.1 us (34%)
  waiting for transfers between devices  46.8 us (32%)
  Pallas kernels  44.3 us (30%)
  local copies, waits for them, and re-layouts  4 us (3%)
    ppermute x37, starting transfers between devices, move(): return lax.ppermute(x, AXES, pairs)  49.1 us
    ppermute x37, waiting for transfers between devices, move(): return lax.ppermute(x, AXES, pairs)  46.8 us
    pallas_call x14, Pallas kernels, call(): pl.pallas_call(kernel, out_shape=outs, in_specs=[pl.BlockSpec(memory_spac...  16.9 us
    pallas_call x3, Pallas kernels, unpack(): pl.pallas_call(lambda *refs: unpack_kernel(*refs, slabs=slabs, count=len(...  13.1 us
    pallas_call x1, Pallas kernels, blocked_body(): pl.pallas_call(field_kernel, out_shape=jax.ShapeDtypeStruct((levels, heig...  9.44 us
    pallas_call x1, Pallas kernels, blocked_body(): pl.pallas_call(lines_kernel, out_shape=[jax.ShapeDtypeStruct((levels, row...  4.86 us
    unnamed x14, local copies, waits for them, and re-layouts  4 us
  transfers between devices with their start and end apart: 37, of which 15 were waited for; matrix products, arithmetic and copies ran while one was open for 0% of the time, Pallas kernels for 26%

profile of v17, /device:TPU:0, one launch (start us, length us, event | category | flops | bytes accessed | tf_op | source)
XLA Modules:
  0.0 145.4 jit_solution(11120033960231886813)
XLA Ops:
  0.7 1.0 copy-done.1
  1.7 1.0 copy-done.3
  4.2 3.1 %collective-permute-start = (bf16[416,128]{1,0:T(8,128)(2,1)S(1)}, bf16[416,128]{1,0:T(8,128)(2,1)S(1)}, u32[]{:S(2)}, u32[]{:S(2)}) collective-permute-start(bf16[416,128]{1,0:T(8,128)(2,1)S(1)} %get-tuple-element.36), channel_id=1, source_target_pairs={{0,1},{1,2},{2,3},{3,0},{4,5},{5,6},{6,7},{7,4},{8,9},{9,10},{10,1... | collective-permute-start | bytes 319496 | tf_op jit(solution)/shard_map/ppermute | solution.py:98
  7.3 1.5 %collective-permute-start.7 = (bf16[768,128]{1,0:T(8,128)(2,1)S(1)}, bf16[768,128]{1,0:T(8,128)(2,1)S(1)}, u32[]{:S(2)}, u32[]{:S(2)}) collective-permute-start(bf16[768,128]{1,0:T(8,128)(2,1)S(1)} %get-tuple-element.42), channel_id=1, source_target_pairs={{0,4},{1,5},{2,6},{3,7},{4,0},{5,1},{6,2},{7,3},{8,20},{9,21},{10,... | collective-permute-start | bytes 589832 | tf_op jit(solution)/shard_map/ppermute | solution.py:98
  8.8 2.6 %collective-permute-start.1 = (bf16[384,128]{1,0:T(8,128)(2,1)S(1)}, bf16[384,128]{1,0:T(8,128)(2,1)S(1)}, u32[]{:S(2)}, u32[]{:S(2)}) collective-permute-start(bf16[384,128]{1,0:T(8,128)(2,1)S(1)} %get-tuple-element.37), channel_id=1, source_target_pairs={{0,2},{1,3},{2,0},{3,1},{4,6},{5,7},{6,4},{7,5},{8,10},{9,11},{10,... | collective-permute-start | bytes 294920 | tf_op jit(solution)/shard_map/ppermute | solution.py:98
  11.4 1.3 collective-permute-start.2
  12.7 5.6 %collective-permute-done.1.x2 = bf16[384,128]{1,0:T(8,128)(2,1)S(1)} collective-permute-done((bf16[384,128]{1,0:T(8,128)(2,1)S(1)}, bf16[384,128]{1,0:T(8,128)(2,1)S(1)}, u32[]{:S(2)}, u32[]{:S(2)}) %collective-permute-start.1) | collective-permute-done | bytes 98336 | tf_op jit(solution)/shard_map/ppermute | solution.py:98
  18.4 2.8 %collective-permute-start.11 = (bf16[384,128]{1,0:T(8,128)(2,1)S(1)}, bf16[384,128]{1,0:T(8,128)(2,1)S(1)}, u32[]{:S(2)}, u32[]{:S(2)}) collective-permute-start(bf16[384,128]{1,0:T(8,128)(2,1)S(1)} %get-tuple-element.44), channel_id=1, source_target_pairs={{0,12},{1,13},{2,14},{3,15},{4,8},{5,9},{6,10},{7,11},{8,4},{9,5},... | collective-permute-start | bytes 294920 | tf_op jit(solution)/shard_map/ppermute | solution.py:98
  22.0 2.0 %collective-permute-start.3 = (bf16[1600,128]{1,0:T(8,128)(2,1)S(1)}, bf16[1600,128]{1,0:T(8,128)(2,1)S(1)}, u32[]{:S(2)}, u32[]{:S(2)}) collective-permute-start(bf16[1600,128]{1,0:T(8,128)(2,1)S(1)} %get-tuple-element.39.own.x_own), channel_id=1, source_target_pairs={{0,4},{1,5},{2,6},{3,7},{4,0},{5,1},{6,2},{7,3},{8,12},{9,13},{10,... | collective-permute-start | bytes 1228808 | tf_op jit(solution)/shard_map/ppermute | solution.py:98
  24.1 1.3 collective-permute-start.4
  26.0 3.5 %collective-permute-start.9 = (bf16[2,768,128]{2,1,0:T(8,128)(2,1)S(1)}, bf16[2,768,128]{2,1,0:T(8,128)(2,1)S(1)}, u32[]{:S(2)}, u32[]{:S(2)}) collective-permute-start(bf16[2,768,128]{2,1,0:T(8,128)(2,1)S(1)} %pair_0.1.here), channel_id=1, source_target_pairs={{0,3},{1,0},{2,1},{3,2},{4,7},{5,4},{6,5},{7,6},{8,11},{9,8},{10,9... | collective-permute-start | bytes 1179656 | tf_op jit(solution)/shard_map/ppermute | solution.py:98
  29.4 13.6 %collective-permute-done.4.after.x_y = bf16[1536,128]{1,0:T(8,128)(2,1)S(1)} collective-permute-done((bf16[1536,128]{1,0:T(8,128)(2,1)S(1)}, bf16[1536,128]{1,0:T(8,128)(2,1)S(1)}, u32[]{:S(2)}, u32[]{:S(2)}) %collective-permute-start.4) | collective-permute-done | bytes 393248 | tf_op jit(solution)/shard_map/ppermute | solution.py:98
  43.1 2.0 %collective-permute-done.8.west = bf16[2,768,128]{2,1,0:T(8,128)(2,1)S(1)} collective-permute-done((bf16[2,768,128]{2,1,0:T(8,128)(2,1)S(1)}, bf16[2,768,128]{2,1,0:T(8,128)(2,1)S(1)}, u32[]{:S(2)}, u32[]{:S(2)}) %collective-permute-start.8) | collective-permute-done | bytes 393248 | tf_op jit(solution)/shard_map/ppermute | solution.py:98
  45.1 1.0 copy-done.2
  46.9 3.2 %collective-permute-start.14 = (bf16[768,128]{1,0:T(8,128)(2,1)S(1)}, bf16[768,128]{1,0:T(8,128)(2,1)S(1)}, u32[]{:S(2)}, u32[]{:S(2)}) collective-permute-start(bf16[768,128]{1,0:T(8,128)(2,1)S(1)} %get-tuple-element.48), channel_id=1, source_target_pairs={{0,3},{1,0},{2,1},{3,2},{4,7},{5,4},{6,5},{7,6},{8,11},{9,8},{10,9... | collective-permute-start | bytes 589832 | tf_op jit(solution)/shard_map/ppermute | solution.py:98
  50.1 4.9 %lines.1 = (bf16[4,18,192,256]{3,2,1,0:T(8,128)(2,1)S(1)}, f32[27,256,512]{2,1,0:T(8,128)}) custom-call(s32[3]{0:T(128)S(1)} %pad_add_fusion.pos.refs_0_, bf16[1600,128]{1,0:T(8,128)(2,1)S(1)} %get-tuple-element.39.own.x_own, bf16[1600,128]{1,0:T(8,128)(2,1)S(1)} %collective-permute-done.3.x_x, bf16[1536,128]{1,0:T(8,128)(2,1)S(1)} %collective-permute-done.4.after.x_y, ...), custom_call_target="tpu_custom_call" | custom-call | bytes 1048576 | tf_op jit(solution)/shard_map/lines/pallas_call | solution.py:542
  55.3 4.5 %collective-permute-done.13.one = bf16[768,128]{1,0:T(8,128)(2,1)S(1)} collective-permute-done((bf16[768,128]{1,0:T(8,128)(2,1)S(1)}, bf16[768,128]{1,0:T(8,128)(2,1)S(1)}, u32[]{:S(2)}, u32[]{:S(2)}) %collective-permute-start.13) | collective-permute-done | bytes 196640 | tf_op jit(solution)/shard_map/ppermute | solution.py:98
  61.0 1.2 collective-permute-done.15.s2
  62.2 8.6 %taps.1.held = f32[27,64,128]{2,1,0:T(8,128)S(1)} custom-call(s32[3]{0:T(128)S(1)} %pad_add_fusion.pos.refs_0_, bf16[4,18,192,256]{3,2,1,0:T(8,128)(2,1)S(1)} %get-tuple-element.46.after.xs, bf16[6,768,128]{2,1,0:T(8,128)(2,1)S(1)} %get-tuple-element.47.g, bf16[6,768,128]{2,1,0:T(8,128)(2,1)S(1)} %collective-permute-done.12.s, ...), custom_call_target="tpu_custom_call" | custom-call | flops 5435817984 | bytes 11108352 | tf_op jit(solution)/shard_map/taps/pallas_call | solution.py:116
  70.7 0.9 code.1
  71.6 1.8 %collective-permute-start.26 = (bf16[1552,128]{1,0:T(8,128)(2,1)S(1)}, bf16[1552,128]{1,0:T(8,128)(2,1)S(1)}, u32[]{:S(2)}, u32[]{:S(2)}) collective-permute-start(bf16[1552,128]{1,0:T(8,128)(2,1)S(1)} %get-tuple-element.55), channel_id=1, source_target_pairs={{0,3},{1,0},{2,1},{3,2},{4,7},{5,4},{6,5},{7,6},{8,11},{9,8},{10,9... | collective-permute-start | bytes 1191944 | tf_op jit(solution)/shard_map/ppermute | solution.py:98
  73.7 1.0 collective-permute-start.18
  74.7 1.4 collective-permute-start.17
  76.2 9.4 %field.1.after1 = bf16[4,4,48,256]{3,2,1,0:T(8,128)(2,1)} custom-call(s32[3]{0:T(128)S(1)} %pad_add_fusion.pos.refs_0_, bf16[1744,128]{1,0:T(8,128)(2,1)S(1)} %get-tuple-element.50.after.after2.own.refs_1_, bf16[4,6,64,256]{3,2,1,0:T(8,128)(2,1)S(1)} %get-tuple-element.49.mine, bf16[4,6,64,256]{3,2,1,0:T(8,128)(2,1)S(1)} %collective-permute-done.16.after.theirs, ...), custom_call_target="tpu_custom_call" | custom-call | flops 10871635968 | bytes 7077888 | tf_op jit(solution)/shard_map/field/pallas_call | solution.py:579
  86.5 1.0 copy-done.4
  88.1 1.3 collective-permute-start.19
  89.8 2.8 %collective-permute-done.25.west.refs_1_ = bf16[1552,128]{1,0:T(8,128)(2,1)S(1)} collective-permute-done((bf16[1552,128]{1,0:T(8,128)(2,1)S(1)}, bf16[1552,128]{1,0:T(8,128)(2,1)S(1)}, u32[]{:S(2)}, u32[]{:S(2)}) %collective-permute-start.25) | collective-permute-done | bytes 397344 | tf_op jit(solution)/shard_map/ppermute | solution.py:98
  92.6 2.7 %collective-permute-done.20.bottom.after2.refs_5_ = bf16[848,128]{1,0:T(8,128)(2,1)S(1)} collective-permute-done((bf16[848,128]{1,0:T(8,128)(2,1)S(1)}, bf16[848,128]{1,0:T(8,128)(2,1)S(1)}, u32[]{:S(2)}, u32[]{:S(2)}) %collective-permute-start.20) | collective-permute-done | bytes 217120 | tf_op jit(solution)/shard_map/ppermute | solution.py:98
  96.4 1.2 collective-permute-start.33
  97.6 1.7 %collective-permute-start.27 = (bf16[768,128]{1,0:T(8,128)(2,1)S(1)}, bf16[768,128]{1,0:T(8,128)(2,1)S(1)}, u32[]{:S(2)}, u32[]{:S(2)}) collective-permute-start(bf16[768,128]{1,0:T(8,128)(2,1)S(1)} %get-tuple-element.56), channel_id=1, source_target_pairs={{0,1},{1,2},{2,3},{3,0},{4,5},{5,6},{6,7},{7,4},{8,9},{9,10},{10,1... | collective-permute-start | bytes 589832 | tf_op jit(solution)/shard_map/ppermute | solution.py:98
  99.8 2.2 %collective-permute-start.22 = (bf16[832,128]{1,0:T(8,128)(2,1)S(1)}, bf16[832,128]{1,0:T(8,128)(2,1)S(1)}, u32[]{:S(2)}, u32[]{:S(2)}) collective-permute-start(bf16[832,128]{1,0:T(8,128)(2,1)S(1)} %block.1.refs_6_), channel_id=1, source_target_pairs={{0,3},{1,0},{2,1},{3,2},{4,7},{5,4},{6,5},{7,6},{8,11},{9,8},{10,9... | collective-permute-start | bytes 638984 | tf_op jit(solution)/shard_map/ppermute | solution.py:98
  102.0 1.7 %collective-permute-start.28 = (bf16[784,128]{1,0:T(8,128)(2,1)S(1)}, bf16[784,128]{1,0:T(8,128)(2,1)S(1)}, u32[]{:S(2)}, u32[]{:S(2)}) collective-permute-start(bf16[784,128]{1,0:T(8,128)(2,1)S(1)} %get-tuple-element.57), channel_id=1, source_target_pairs={{0,3},{1,0},{2,1},{3,2},{4,7},{5,4},{6,5},{7,6},{8,11},{9,8},{10,9... | collective-permute-start | bytes 602120 | tf_op jit(solution)/shard_map/ppermute | solution.py:98
  103.7 3.5 %collective-permute-done.27.half_3 = bf16[768,128]{1,0:T(8,128)(2,1)S(1)} collective-permute-done((bf16[768,128]{1,0:T(8,128)(2,1)S(1)}, bf16[768,128]{1,0:T(8,128)(2,1)S(1)}, u32[]{:S(2)}, u32[]{:S(2)}) %collective-permute-start.27) | collective-permute-done | bytes 196640 | tf_op jit(solution)/shard_map/ppermute | solution.py:98
  107.2 4.7 %collective-permute-start.21 = (bf16[832,128]{1,0:T(8,128)(2,1)S(1)}, bf16[832,128]{1,0:T(8,128)(2,1)S(1)}, u32[]{:S(2)}, u32[]{:S(2)}) collective-permute-start(bf16[832,128]{1,0:T(8,128)(2,1)S(1)} %block.1.refs_6_), channel_id=1, source_target_pairs={{0,1},{1,2},{2,3},{3,0},{4,5},{5,6},{6,7},{7,4},{8,9},{9,10},{10,1... | collective-permute-start | bytes 638984 | tf_op jit(solution)/shard_map/ppermute | solution.py:98
  111.9 2.3 %collective-permute-done.28.half_1 = bf16[784,128]{1,0:T(8,128)(2,1)S(1)} collective-permute-done((bf16[784,128]{1,0:T(8,128)(2,1)S(1)}, bf16[784,128]{1,0:T(8,128)(2,1)S(1)}, u32[]{:S(2)}, u32[]{:S(2)}) %collective-permute-start.28) | collective-permute-done | bytes 200736 | tf_op jit(solution)/shard_map/ppermute | solution.py:98
  114.8 1.1 collective-permute-start.30
  115.9 1.3 collective-permute-start.29
  117.2 2.2 %collective-permute-done.21.block_3.after2.refs_7_ = bf16[832,128]{1,0:T(8,128)(2,1)S(1)} collective-permute-done((bf16[832,128]{1,0:T(8,128)(2,1)S(1)}, bf16[832,128]{1,0:T(8,128)(2,1)S(1)}, u32[]{:S(2)}, u32[]{:S(2)}) %collective-permute-start.21) | collective-permute-done | bytes 213024 | tf_op jit(solution)/shard_map/ppermute | solution.py:98
  120.2 1.1 collective-permute-start.36
  121.3 3.1 %unpack_1.1 = (f32[27,256,512]{2,1,0:T(8,128)}, f32[8,128]{1,0:T(8,128)S(1)}) custom-call(s32[3]{0:T(128)S(1)} %pad_add_fusion.pos.refs_0_, bf16[1744,128]{1,0:T(8,128)(2,1)S(1)} %get-tuple-element.50.after.after2.own.refs_1_, bf16[1744,128]{1,0:T(8,128)(2,1)S(1)} %collective-permute-done.17.by_x.x.refs_2_, ...), custom_call_target="tpu_custom_call", output_to_operand_aliasing={{0}: (7, {})} | custom-call | bytes 4194304 | tf_op jit(solution)/shard_map/unpack_1/pallas_call | solution.py:408
  124.4 2.6 %collective-permute-done.30.by_y.refs_5_ = bf16[1552,128]{1,0:T(8,128)(2,1)S(1)} collective-permute-done((bf16[1552,128]{1,0:T(8,128)(2,1)S(1)}, bf16[1552,128]{1,0:T(8,128)(2,1)S(1)}, u32[]{:S(2)}, u32[]{:S(2)}) %collective-permute-start.30) | collective-permute-done | bytes 397344 | tf_op jit(solution)/shard_map/ppermute | solution.py:98
  127.0 1.0 collective-permute-done.29.by_x.refs_4_
  128.6 1.1 collective-permute-start.32
  129.7 0.9 collective-permute-start.31
  131.1 2.2 %collective-permute-start.24 = (bf16[416,128]{1,0:T(8,128)(2,1)S(1)}, bf16[416,128]{1,0:T(8,128)(2,1)S(1)}, u32[]{:S(2)}, u32[]{:S(2)}) collective-permute-start(bf16[416,128]{1,0:T(8,128)(2,1)S(1)} %get-tuple-element.54), channel_id=1, source_target_pairs={{0,3},{1,0},{2,1},{3,2},{4,7},{5,4},{6,5},{7,6},{8,11},{9,8},{10,9... | collective-permute-start | bytes 319496 | tf_op jit(solution)/shard_map/ppermute | solution.py:98
  133.4 1.4 collective-permute-done.35.refs_5_
  135.2 6.2 %unpack_2.1 = (f32[27,256,512]{2,1,0:T(8,128)}, f32[8,128]{1,0:T(8,128)}) custom-call(s32[3]{0:T(128)S(1)} %pad_add_fusion.pos.refs_0_, bf16[1552,128]{1,0:T(8,128)(2,1)S(1)} %collective-permute-done.25.west.refs_1_, bf16[1552,128]{1,0:T(8,128)(2,1)S(1)} %collective-permute-done.26.east.refs_2_, ...), custom_call_target="tpu_custom_call", output_to_operand_aliasing={{0}: (10, {})} | custom-call | bytes 4194304 | tf_op jit(solution)/shard_map/unpack_2/pallas_call | solution.py:408
  141.5 3.7 %unpack_3.1 = (f32[27,256,512]{2,1,0:T(8,128)}, f32[8,128]{1,0:T(8,128)}) custom-call(s32[3]{0:T(128)S(1)} %pad_add_fusion.pos.refs_0_, bf16[416,128]{1,0:T(8,128)(2,1)S(1)} %collective-permute-done.23.refs_1_, bf16[416,128]{1,0:T(8,128)(2,1)S(1)} %collective-permute-done.24.refs_2_, ...), custom_call_target="tpu_custom_call", output_to_operand_aliasing={{0}: (8, {})} | custom-call | bytes 4194304 | tf_op jit(solution)/shard_map/unpack_3/pallas_call | solution.py:408
  (61 shorter events, 12.0 us)
Async XLA Ops:
  0.7 1.0 copy-start.1
  1.7 1.0 copy-start.3
  3.6 18.5 %collective-permute-start.6 = (bf16[768,128]{1,0:T(8,128)(2,1)S(1)}, bf16[768,128]{1,0:T(8,128)(2,1)S(1)}, u32[]{:S(2)}, u32[]{:S(2)}) collective-permute-start(bf16[768,128]{1,0:T(8,128)(2,1)S(1)} %get-tuple-element.41), channel_id=1, source_target_pairs={{0,0},{1,1},{2,2},{3,3},{4,4},{5,5},{6,6},{7,7},{8,16},{9,17},{10,... | collective-permute-start | bytes 589832 | tf_op jit(solution)/shard_map/ppermute | solution.py:98
  4.2 14.1 %collective-permute-start = (bf16[416,128]{1,0:T(8,128)(2,1)S(1)}, bf16[416,128]{1,0:T(8,128)(2,1)S(1)}, u32[]{:S(2)}, u32[]{:S(2)}) collective-permute-start(bf16[416,128]{1,0:T(8,128)(2,1)S(1)} %get-tuple-element.36), channel_id=1, source_target_pairs={{0,1},{1,2},{2,3},{3,0},{4,5},{5,6},{6,7},{7,4},{8,9},{9,10},{10,1... | collective-permute-start | bytes 319496 | tf_op jit(solution)/shard_map/ppermute | solution.py:98
  7.3 16.7 %collective-permute-start.7 = (bf16[768,128]{1,0:T(8,128)(2,1)S(1)}, bf16[768,128]{1,0:T(8,128)(2,1)S(1)}, u32[]{:S(2)}, u32[]{:S(2)}) collective-permute-start(bf16[768,128]{1,0:T(8,128)(2,1)S(1)} %get-tuple-element.42), channel_id=1, source_target_pairs={{0,4},{1,5},{2,6},{3,7},{4,0},{5,1},{6,2},{7,3},{8,20},{9,21},{10,... | collective-permute-start | bytes 589832 | tf_op jit(solution)/shard_map/ppermute | solution.py:98
  8.8 9.6 %collective-permute-start.1 = (bf16[384,128]{1,0:T(8,128)(2,1)S(1)}, bf16[384,128]{1,0:T(8,128)(2,1)S(1)}, u32[]{:S(2)}, u32[]{:S(2)}) collective-permute-start(bf16[384,128]{1,0:T(8,128)(2,1)S(1)} %get-tuple-element.37), channel_id=1, source_target_pairs={{0,2},{1,3},{2,0},{3,1},{4,6},{5,7},{6,4},{7,5},{8,10},{9,11},{10,... | collective-permute-start | bytes 294920 | tf_op jit(solution)/shard_map/ppermute | solution.py:98
  11.4 9.8 %collective-permute-start.2 = (bf16[416,128]{1,0:T(8,128)(2,1)S(1)}, bf16[416,128]{1,0:T(8,128)(2,1)S(1)}, u32[]{:S(2)}, u32[]{:S(2)}) collective-permute-start(bf16[416,128]{1,0:T(8,128)(2,1)S(1)} %get-tuple-element.38), channel_id=1, source_target_pairs={{0,3},{1,0},{2,1},{3,2},{4,7},{5,4},{6,5},{7,6},{8,11},{9,8},{10,9... | collective-permute-start | bytes 319496 | tf_op jit(solution)/shard_map/ppermute | solution.py:98
  18.4 7.6 %collective-permute-start.10 = (bf16[384,128]{1,0:T(8,128)(2,1)S(1)}, bf16[384,128]{1,0:T(8,128)(2,1)S(1)}, u32[]{:S(2)}, u32[]{:S(2)}) collective-permute-start(bf16[384,128]{1,0:T(8,128)(2,1)S(1)} %get-tuple-element.43), channel_id=1, source_target_pairs={{0,4},{1,5},{2,6},{3,7},{4,0},{5,1},{6,2},{7,3},{8,12},{9,13},{10,... | collective-permute-start | bytes 294920 | tf_op jit(solution)/shard_map/ppermute | solution.py:98
  18.4 11.1 %collective-permute-start.11 = (bf16[384,128]{1,0:T(8,128)(2,1)S(1)}, bf16[384,128]{1,0:T(8,128)(2,1)S(1)}, u32[]{:S(2)}, u32[]{:S(2)}) collective-permute-start(bf16[384,128]{1,0:T(8,128)(2,1)S(1)} %get-tuple-element.44), channel_id=1, source_target_pairs={{0,12},{1,13},{2,14},{3,15},{4,8},{5,9},{6,10},{7,11},{8,4},{9,5},... | collective-permute-start | bytes 294920 | tf_op jit(solution)/shard_map/ppermute | solution.py:98
  21.8 21.2 %collective-permute-start.5 = (bf16[1600,128]{1,0:T(8,128)(2,1)S(1)}, bf16[1600,128]{1,0:T(8,128)(2,1)S(1)}, u32[]{:S(2)}, u32[]{:S(2)}) collective-permute-start(bf16[1600,128]{1,0:T(8,128)(2,1)S(1)} %get-tuple-element.39.own.x_own), channel_id=1, source_target_pairs={{0,12},{1,13},{2,14},{3,15},{4,8},{5,9},{6,10},{7,11},{8,4},{9,5},... | collective-permute-start | bytes 1228808 | tf_op jit(solution)/shard_map/ppermute | solution.py:98
  22.0 21.0 %collective-permute-start.3 = (bf16[1600,128]{1,0:T(8,128)(2,1)S(1)}, bf16[1600,128]{1,0:T(8,128)(2,1)S(1)}, u32[]{:S(2)}, u32[]{:S(2)}) collective-permute-start(bf16[1600,128]{1,0:T(8,128)(2,1)S(1)} %get-tuple-element.39.own.x_own), channel_id=1, source_target_pairs={{0,4},{1,5},{2,6},{3,7},{4,0},{5,1},{6,2},{7,3},{8,12},{9,13},{10,... | collective-permute-start | bytes 1228808 | tf_op jit(solution)/shard_map/ppermute | solution.py:98
  24.1 19.0 %collective-permute-start.4 = (bf16[1536,128]{1,0:T(8,128)(2,1)S(1)}, bf16[1536,128]{1,0:T(8,128)(2,1)S(1)}, u32[]{:S(2)}, u32[]{:S(2)}) collective-permute-start(bf16[1536,128]{1,0:T(8,128)(2,1)S(1)} %get-tuple-element.40), channel_id=1, source_target_pairs={{0,8},{1,9},{2,10},{3,11},{4,12},{5,13},{6,14},{7,15},{8,0},{9,1},... | collective-permute-start | bytes 1179656 | tf_op jit(solution)/shard_map/ppermute | solution.py:98
  26.0 17.1 %collective-permute-start.9 = (bf16[2,768,128]{2,1,0:T(8,128)(2,1)S(1)}, bf16[2,768,128]{2,1,0:T(8,128)(2,1)S(1)}, u32[]{:S(2)}, u32[]{:S(2)}) collective-permute-start(bf16[2,768,128]{2,1,0:T(8,128)(2,1)S(1)} %pair_0.1.here), channel_id=1, source_target_pairs={{0,3},{1,0},{2,1},{3,2},{4,7},{5,4},{6,5},{7,6},{8,11},{9,8},{10,9... | collective-permute-start | bytes 1179656 | tf_op jit(solution)/shard_map/ppermute | solution.py:98
  29.4 15.6 %collective-permute-start.8 = (bf16[2,768,128]{2,1,0:T(8,128)(2,1)S(1)}, bf16[2,768,128]{2,1,0:T(8,128)(2,1)S(1)}, u32[]{:S(2)}, u32[]{:S(2)}) collective-permute-start(bf16[2,768,128]{2,1,0:T(8,128)(2,1)S(1)} %pair_0.1.here), channel_id=1, source_target_pairs={{0,1},{1,2},{2,3},{3,0},{4,5},{5,6},{6,7},{7,4},{8,9},{9,10},{10,1... | collective-permute-start | bytes 1179656 | tf_op jit(solution)/shard_map/ppermute | solution.py:98
  45.1 1.0 copy-start.2
  46.8 15.3 %collective-permute-start.12 = (bf16[6,768,128]{2,1,0:T(8,128)(2,1)S(1)}, bf16[6,768,128]{2,1,0:T(8,128)(2,1)S(1)}, u32[]{:S(2)}, u32[]{:S(2)}) collective-permute-start(bf16[6,768,128]{2,1,0:T(8,128)(2,1)S(1)} %get-tuple-element.47.g), channel_id=1, source_target_pairs={{0,16},{1,17},{2,18},{3,19},{4,20},{5,21},{6,22},{7,23},{8,24},{9,... | collective-permute-start | bytes 3538952 | tf_op jit(solution)/shard_map/ppermute | solution.py:98
  46.9 8.4 %collective-permute-start.14 = (bf16[768,128]{1,0:T(8,128)(2,1)S(1)}, bf16[768,128]{1,0:T(8,128)(2,1)S(1)}, u32[]{:S(2)}, u32[]{:S(2)}) collective-permute-start(bf16[768,128]{1,0:T(8,128)(2,1)S(1)} %get-tuple-element.48), channel_id=1, source_target_pairs={{0,3},{1,0},{2,1},{3,2},{4,7},{5,4},{6,5},{7,6},{8,11},{9,8},{10,9... | collective-permute-start | bytes 589832 | tf_op jit(solution)/shard_map/ppermute | solution.py:98
  50.1 9.7 %collective-permute-start.13 = (bf16[768,128]{1,0:T(8,128)(2,1)S(1)}, bf16[768,128]{1,0:T(8,128)(2,1)S(1)}, u32[]{:S(2)}, u32[]{:S(2)}) collective-permute-start(bf16[768,128]{1,0:T(8,128)(2,1)S(1)} %get-tuple-element.45.after), channel_id=1, source_target_pairs={{0,1},{1,2},{2,3},{3,0},{4,5},{5,6},{6,7},{7,4},{8,9},{9,10},{10,1... | collective-permute-start | bytes 589832 | tf_op jit(solution)/shard_map/ppermute | solution.py:98
  59.8 16.4 %slice-start = ((s8[7077888]{0:T(1024)(128)(4,1)}), s8[4194304]{0:T(1024)(128)(4,1)S(1)}, s32[]{:S(2)}) async-start(s8[7077888]{0:T(1024)(128)(4,1)} %bitcast.12), calls=%async_computation | async-start | bytes 8388608
  60.4 1.8 %collective-permute-start.15 = (bf16[2,768,128]{2,1,0:T(8,128)(2,1)S(1)}, bf16[2,768,128]{2,1,0:T(8,128)(2,1)S(1)}, u32[]{:S(2)}, u32[]{:S(2)}) collective-permute-start(bf16[2,768,128]{2,1,0:T(8,128)(2,1)S(1)} %pair.1.g2), channel_id=1, source_target_pairs={{0,16},{1,17},{2,18},{3,19},{4,20},{5,21},{6,22},{7,23},{8,24},{9,... | collective-permute-start | bytes 1179656 | tf_op jit(solution)/shard_map/ppermute | solution.py:98
  60.5 15.7 %slice-start.1 = ((s8[7077888]{0:T(1024)(128)(4,1)}), s8[2883584]{0:T(1024)(128)(4,1)S(1)}, s32[]{:S(2)}) async-start(s8[7077888]{0:T(1024)(128)(4,1)} %bitcast.12), calls=%async_computation.1 | async-start | bytes 5767168
  60.5 10.3 %collective-permute-start.16 = (bf16[4,6,64,256]{3,2,1,0:T(8,128)(2,1)S(1)}, bf16[4,6,64,256]{3,2,1,0:T(8,128)(2,1)S(1)}, u32[]{:S(2)}, u32[]{:S(2)}) collective-permute-start(bf16[4,6,64,256]{3,2,1,0:T(8,128)(2,1)S(1)} %get-tuple-element.49.mine), channel_id=1, source_target_pairs={{0,16},{1,17},{2,18},{3,19},{4,20},{5,21},{6,22},{7,23},{8,24},{9,... | collective-permute-start | bytes 2359304 | tf_op jit(solution)/shard_map/ppermute | solution.py:98
  71.6 18.2 %collective-permute-start.26 = (bf16[1552,128]{1,0:T(8,128)(2,1)S(1)}, bf16[1552,128]{1,0:T(8,128)(2,1)S(1)}, u32[]{:S(2)}, u32[]{:S(2)}) collective-permute-start(bf16[1552,128]{1,0:T(8,128)(2,1)S(1)} %get-tuple-element.55), channel_id=1, source_target_pairs={{0,3},{1,0},{2,1},{3,2},{4,7},{5,4},{6,5},{7,6},{8,11},{9,8},{10,9... | collective-permute-start | bytes 1191944 | tf_op jit(solution)/shard_map/ppermute | solution.py:98
  73.4 19.2 %collective-permute-start.25 = (bf16[1552,128]{1,0:T(8,128)(2,1)S(1)}, bf16[1552,128]{1,0:T(8,128)(2,1)S(1)}, u32[]{:S(2)}, u32[]{:S(2)}) collective-permute-start(bf16[1552,128]{1,0:T(8,128)(2,1)S(1)} %get-tuple-element.55), channel_id=1, source_target_pairs={{0,1},{1,2},{2,3},{3,0},{4,5},{5,6},{6,7},{7,4},{8,9},{9,10},{10,1... | collective-permute-start | bytes 1191944 | tf_op jit(solution)/shard_map/ppermute | solution.py:98
  73.7 11.9 %collective-permute-start.18 = (bf16[1744,128]{1,0:T(8,128)(2,1)S(1)}, bf16[1744,128]{1,0:T(8,128)(2,1)S(1)}, u32[]{:S(2)}, u32[]{:S(2)}) collective-permute-start(bf16[1744,128]{1,0:T(8,128)(2,1)S(1)} %get-tuple-element.50.after.after2.own.refs_1_), channel_id=1, source_target_pairs={{0,8},{1,9},{2,10},{3,11},{4,12},{5,13},{6,14},{7,15},{8,0},{9,1},... | collective-permute-start | bytes 1339400 | tf_op jit(solution)/shard_map/ppermute | solution.py:98
  74.7 11.7 %collective-permute-start.17 = (bf16[1744,128]{1,0:T(8,128)(2,1)S(1)}, bf16[1744,128]{1,0:T(8,128)(2,1)S(1)}, u32[]{:S(2)}, u32[]{:S(2)}) collective-permute-start(bf16[1744,128]{1,0:T(8,128)(2,1)S(1)} %get-tuple-element.50.after.after2.own.refs_1_), channel_id=1, source_target_pairs={{0,4},{1,5},{2,6},{3,7},{4,0},{5,1},{6,2},{7,3},{8,12},{9,13},{10,... | collective-permute-start | bytes 1339400 | tf_op jit(solution)/shard_map/ppermute | solution.py:98
  86.5 1.0 copy-start.4
  88.1 7.2 %collective-permute-start.19 = (bf16[896,128]{1,0:T(8,128)(2,1)S(1)}, bf16[896,128]{1,0:T(8,128)(2,1)S(1)}, u32[]{:S(2)}, u32[]{:S(2)}) collective-permute-start(bf16[896,128]{1,0:T(8,128)(2,1)S(1)} %get-tuple-element.51), channel_id=1, source_target_pairs={{0,4},{1,5},{2,6},{3,7},{4,0},{5,1},{6,2},{7,3},{8,12},{9,13},{10,... | collective-permute-start | bytes 688136 | tf_op jit(solution)/shard_map/ppermute | solution.py:98
  89.4 5.9 %collective-permute-start.20 = (bf16[848,128]{1,0:T(8,128)(2,1)S(1)}, bf16[848,128]{1,0:T(8,128)(2,1)S(1)}, u32[]{:S(2)}, u32[]{:S(2)}) collective-permute-start(bf16[848,128]{1,0:T(8,128)(2,1)S(1)} %get-tuple-element.52), channel_id=1, source_target_pairs={{0,8},{1,9},{2,10},{3,11},{4,12},{5,13},{6,14},{7,15},{8,0},{9,1},... | collective-permute-start | bytes 651272 | tf_op jit(solution)/shard_map/ppermute | solution.py:98
  95.9 23.5 %collective-permute-start.34 = (bf16[3104,128]{1,0:T(8,128)(2,1)S(1)}, bf16[3104,128]{1,0:T(8,128)(2,1)S(1)}, u32[]{:S(2)}, u32[]{:S(2)}) collective-permute-start(bf16[3104,128]{1,0:T(8,128)(2,1)S(1)} %get-tuple-element.58.after.after2), channel_id=1, source_target_pairs={{0,8},{1,9},{2,10},{3,11},{4,12},{5,13},{6,14},{7,15},{8,0},{9,1},... | collective-permute-start | bytes 2383880 | tf_op jit(solution)/shard_map/ppermute | solution.py:98
  96.4 23.1 %collective-permute-start.33 = (bf16[3104,128]{1,0:T(8,128)(2,1)S(1)}, bf16[3104,128]{1,0:T(8,128)(2,1)S(1)}, u32[]{:S(2)}, u32[]{:S(2)}) collective-permute-start(bf16[3104,128]{1,0:T(8,128)(2,1)S(1)} %get-tuple-element.58.after.after2), channel_id=1, source_target_pairs={{0,4},{1,5},{2,6},{3,7},{4,0},{5,1},{6,2},{7,3},{8,12},{9,13},{10,... | collective-permute-start | bytes 2383880 | tf_op jit(solution)/shard_map/ppermute | solution.py:98
  97.6 9.6 %collective-permute-start.27 = (bf16[768,128]{1,0:T(8,128)(2,1)S(1)}, bf16[768,128]{1,0:T(8,128)(2,1)S(1)}, u32[]{:S(2)}, u32[]{:S(2)}) collective-permute-start(bf16[768,128]{1,0:T(8,128)(2,1)S(1)} %get-tuple-element.56), channel_id=1, source_target_pairs={{0,1},{1,2},{2,3},{3,0},{4,5},{5,6},{6,7},{7,4},{8,9},{9,10},{10,1... | collective-permute-start | bytes 589832 | tf_op jit(solution)/shard_map/ppermute | solution.py:98
  99.8 16.1 %collective-permute-start.22 = (bf16[832,128]{1,0:T(8,128)(2,1)S(1)}, bf16[832,128]{1,0:T(8,128)(2,1)S(1)}, u32[]{:S(2)}, u32[]{:S(2)}) collective-permute-start(bf16[832,128]{1,0:T(8,128)(2,1)S(1)} %block.1.refs_6_), channel_id=1, source_target_pairs={{0,3},{1,0},{2,1},{3,2},{4,7},{5,4},{6,5},{7,6},{8,11},{9,8},{10,9... | collective-permute-start | bytes 638984 | tf_op jit(solution)/shard_map/ppermute | solution.py:98
  102.0 12.2 %collective-permute-start.28 = (bf16[784,128]{1,0:T(8,128)(2,1)S(1)}, bf16[784,128]{1,0:T(8,128)(2,1)S(1)}, u32[]{:S(2)}, u32[]{:S(2)}) collective-permute-start(bf16[784,128]{1,0:T(8,128)(2,1)S(1)} %get-tuple-element.57), channel_id=1, source_target_pairs={{0,3},{1,0},{2,1},{3,2},{4,7},{5,4},{6,5},{7,6},{8,11},{9,8},{10,9... | collective-permute-start | bytes 602120 | tf_op jit(solution)/shard_map/ppermute | solution.py:98
  107.2 12.3 %collective-permute-start.21 = (bf16[832,128]{1,0:T(8,128)(2,1)S(1)}, bf16[832,128]{1,0:T(8,128)(2,1)S(1)}, u32[]{:S(2)}, u32[]{:S(2)}) collective-permute-start(bf16[832,128]{1,0:T(8,128)(2,1)S(1)} %block.1.refs_6_), channel_id=1, source_target_pairs={{0,1},{1,2},{2,3},{3,0},{4,5},{5,6},{6,7},{7,4},{8,9},{9,10},{10,1... | collective-permute-start | bytes 638984 | tf_op jit(solution)/shard_map/ppermute | solution.py:98
  114.8 12.2 %collective-permute-start.30 = (bf16[1552,128]{1,0:T(8,128)(2,1)S(1)}, bf16[1552,128]{1,0:T(8,128)(2,1)S(1)}, u32[]{:S(2)}, u32[]{:S(2)}) collective-permute-start(bf16[1552,128]{1,0:T(8,128)(2,1)S(1)} %across.1.refs_3_), channel_id=1, source_target_pairs={{0,8},{1,9},{2,10},{3,11},{4,12},{5,13},{6,14},{7,15},{8,0},{9,1},... | collective-permute-start | bytes 1191944 | tf_op jit(solution)/shard_map/ppermute | solution.py:98
  115.9 12.1 %collective-permute-start.29 = (bf16[1552,128]{1,0:T(8,128)(2,1)S(1)}, bf16[1552,128]{1,0:T(8,128)(2,1)S(1)}, u32[]{:S(2)}, u32[]{:S(2)}) collective-permute-start(bf16[1552,128]{1,0:T(8,128)(2,1)S(1)} %across.1.refs_3_), channel_id=1, source_target_pairs={{0,4},{1,5},{2,6},{3,7},{4,0},{5,1},{6,2},{7,3},{8,12},{9,13},{10,... | collective-permute-start | bytes 1191944 | tf_op jit(solution)/shard_map/ppermute | solution.py:98
  119.5 15.8 %copy-start = (bf16[3104,128]{1,0:T(8,128)(2,1)}, bf16[3104,128]{1,0:T(8,128)(2,1)S(1)}, u32[]{:S(2)}) copy-start(bf16[3104,128]{1,0:T(8,128)(2,1)S(1)} %collective-permute-done.34.by_y.refs_4_) | copy-start | bytes 2383876
  120.1 14.7 %collective-permute-start.35 = (bf16[1552,128]{1,0:T(8,128)(2,1)S(1)}, bf16[1552,128]{1,0:T(8,128)(2,1)S(1)}, u32[]{:S(2)}, u32[]{:S(2)}) collective-permute-start(bf16[1552,128]{1,0:T(8,128)(2,1)S(1)} %get-tuple-element.63), channel_id=1, source_target_pairs={{0,4},{1,5},{2,6},{3,7},{4,0},{5,1},{6,2},{7,3},{8,12},{9,13},{10,... | collective-permute-start | bytes 1191944 | tf_op jit(solution)/shard_map/ppermute | solution.py:98
  120.2 15.1 %collective-permute-start.36 = (bf16[1552,128]{1,0:T(8,128)(2,1)S(1)}, bf16[1552,128]{1,0:T(8,128)(2,1)S(1)}, u32[]{:S(2)}, u32[]{:S(2)}) collective-permute-start(bf16[1552,128]{1,0:T(8,128)(2,1)S(1)} %get-tuple-element.64), channel_id=1, source_target_pairs={{0,8},{1,9},{2,10},{3,11},{4,12},{5,13},{6,14},{7,15},{8,0},{9,1},... | collective-permute-start | bytes 1191944 | tf_op jit(solution)/shard_map/ppermute | solution.py:98
  128.6 12.8 %collective-permute-start.32 = (bf16[784,128]{1,0:T(8,128)(2,1)S(1)}, bf16[784,128]{1,0:T(8,128)(2,1)S(1)}, u32[]{:S(2)}, u32[]{:S(2)}) collective-permute-start(bf16[784,128]{1,0:T(8,128)(2,1)S(1)} %get-tuple-element.62), channel_id=1, source_target_pairs={{0,8},{1,9},{2,10},{3,11},{4,12},{5,13},{6,14},{7,15},{8,0},{9,1},... | collective-permute-start | bytes 602120 | tf_op jit(solution)/shard_map/ppermute | solution.py:98
  129.7 11.8 %collective-permute-start.31 = (bf16[768,128]{1,0:T(8,128)(2,1)S(1)}, bf16[768,128]{1,0:T(8,128)(2,1)S(1)}, u32[]{:S(2)}, u32[]{:S(2)}) collective-permute-start(bf16[768,128]{1,0:T(8,128)(2,1)S(1)} %get-tuple-element.61), channel_id=1, source_target_pairs={{0,4},{1,5},{2,6},{3,7},{4,0},{5,1},{6,2},{7,3},{8,12},{9,13},{10,... | collective-permute-start | bytes 589832 | tf_op jit(solution)/shard_map/ppermute | solution.py:98
  131.1 10.3 %collective-permute-start.24 = (bf16[416,128]{1,0:T(8,128)(2,1)S(1)}, bf16[416,128]{1,0:T(8,128)(2,1)S(1)}, u32[]{:S(2)}, u32[]{:S(2)}) collective-permute-start(bf16[416,128]{1,0:T(8,128)(2,1)S(1)} %get-tuple-element.54), channel_id=1, source_target_pairs={{0,3},{1,0},{2,1},{3,2},{4,7},{5,4},{6,5},{7,6},{8,11},{9,8},{10,9... | collective-permute-start | bytes 319496 | tf_op jit(solution)/shard_map/ppermute | solution.py:98
  134.8 6.6 %collective-permute-start.23 = (bf16[416,128]{1,0:T(8,128)(2,1)S(1)}, bf16[416,128]{1,0:T(8,128)(2,1)S(1)}, u32[]{:S(2)}, u32[]{:S(2)}) collective-permute-start(bf16[416,128]{1,0:T(8,128)(2,1)S(1)} %get-tuple-element.53.refs_9_), channel_id=1, source_target_pairs={{0,1},{1,2},{2,3},{3,0},{4,5},{5,6},{6,7},{7,4},{8,9},{9,10},{10,1... | collective-permute-start | bytes 319496 | tf_op jit(solution)/shard_map/ppermute | solution.py:98

commit v18 on v17

--- a/solution.py
+++ b/solution.py
@@ -155,8 +155,8 @@
             out[at * line : (at + 1) * line, :] = facing[:, at * wide : (at + 1) * wide]
 
 
-def spread_kernel(pos, x0, x1, x2, x3, own, own_y):
-    del pos
+def spread_kernel(pos, x0, x1, x2, x3, after1, after2, own, own_y):
+    del pos, after1, after2
     many = x0.shape[0]
     for at, piece in enumerate((x0, x1, x2, x3)):
         own[at * many : (at + 1) * many, :] = piece[0:many, :]
@@ -166,15 +166,15 @@
     own[4 * many + extra :, :] = x3[many:, :]
 
 
-def split_kernel(
-    pos, here, west, east, g, own, x_x, x_d, by_x, by_d, after, first, second, near, mine
-):
+def split_kernel(pos, west, east, first, second):
+    del pos
+    many = first.shape[0]
+    first[...] = west[0:many, :]
+    second[...] = east[many : 2 * many, :]
+
+
+def mine_kernel(pos, g, own, x_x, x_d, by_x, by_d, after, mine):
     del after
-    first[...] = west[0]
-    second[...] = east[1]
-    for at, part in enumerate((here, west, east)):
-        near[2 * at : 2 * at + 2] = part[...]
-
     levels, height, width, chans = g.shape
     edge, line, wide = levels * height, levels * width, chans // 2
     inner = own.shape[0] - 4 * edge
@@ -225,6 +225,14 @@
     del pos, after
     both[0] = one[...]
     both[1] = two[...]
+
+
+def first_pair_kernel(pos, one, two, after1, after2, after3, both):
+    del pos, after1, after2, after3
+    many = one.shape[0]
+    both[0:many, :] = one[...]
+    both[many : 2 * many, :] = two[...]
+    both[2 * many :, :] = jnp.zeros((both.shape[0] - 2 * many, both.shape[1]), both.dtype)
 
 
 def lines_kernel(pos, x_own, x_x, x_y, x_d, after, xs, blank):
@@ -268,15 +276,19 @@
         ] = block.T
 
 
-def taps_kernel(pos, xs, g, s, g2, s2, out, gt, acc):
+def taps_kernel(pos, xs, g0, g1, g3, s0, s1, s3, g2, s2, out, gt, acc):
     levels, rows, circle, lanes = xs.shape
     rows, width, span = rows - 2, circle // 4, lanes // 4
     filters = gt.shape[0] // levels
     deep = rows * width
     right = lax.rem(pos[1], 2)
-    for core, parts, last in ((pos[0], g, g2), (1 - pos[0], s, s2)):
-        for slot, (ref, at) in enumerate(((parts, 0), (parts, 4), (last, 0), (parts, 2))):
-            turn(gt, slot, core, ref[at + right], ref[at + 1 - right], levels)
+    many = g2.shape[1]
+    for core, parts, last in ((pos[0], (g0, g3, g1), g2), (1 - pos[0], (s0, s3, s1), s2)):
+        for slot, part in zip((0, 1, 3), parts):
+            first = part[pl.ds(pl.multiple_of(right * many, many), many), :]
+            second = part[pl.ds(pl.multiple_of((1 - right) * many, many), many), :]
+            turn(gt, slot, core, first, second, levels)
+        turn(gt, 2, core, last[right], last[1 - right], levels)
     acc[...] = jnp.zeros_like(acc)
 
     @pl.loop(0, 3)
@@ -504,41 +516,34 @@
 
     inner = 4 * many
     (g0,) = call(
-        pair_kernel, [jax.ShapeDtypeStruct((2, cells, wide), bf16)], (pos, g_s, g_o, x0), [], 0, "pair_0", 16, held=1
+        first_pair_kernel,
+        [jax.ShapeDtypeStruct((2 * cells + 80, wide), bf16)],
+        (pos, g_s, g_o, x_r1, x_r2, x_r3),
+        [],
+        0,
+        "pair_0",
+        16,
+        held=3,
     )
     x_own, x_own_y = call(
         spread_kernel,
         [jax.ShapeDtypeStruct((count, 2 * span), bf16) for count in (inner + 4 * edge, inner)],
-        (pos, x0, x_r1, x_r2, x_r3),
+        (pos, x0, x_r1, x_r2, x_r3, by_x, by_d),
         [],
         0,
         "spread",
         16,
+        held=2,
     )
     x_x = move(x_own, lat_xor(1))
     x_d = move(x_own, lat_xor(3))
     x_y = move(x_own_y, lat_xor(2))
     g1 = move(g0, lon_by(1))
     g3 = move(g0, lon_by(-1))
-    far_a, far_b, g_near, mine = call(
-        split_kernel,
-        [
-            block,
-            block,
-            jax.ShapeDtypeStruct((6, cells, wide), bf16),
-            jax.ShapeDtypeStruct((levels, height + 2, width + 16, chans), bf16),
-        ],
-        (pos, g0, g1, g3, g_cells, x_own, x_x, x_d, by_x, by_d, x_y),
-        [],
-        0,
-        "split",
-        16,
-        held=1,
-    )
+    far_a, far_b = call(split_kernel, [block, block], (pos, g1, g3), [], 0, "split", 16)
     g2a = move(far_a, lon_by(1))
     g2b = move(far_b, lon_by(-1))
-    s_near = move(g_near, sibling)
-    theirs = move(mine, sibling)
+    s0, s1, s3 = move(g0, sibling), move(g1, sibling), move(g3, sibling)
     xs, total = pl.pallas_call(
         lines_kernel,
         out_shape=[
@@ -553,6 +558,17 @@
         compiler_params=pltpu.CompilerParams(vmem_limit_bytes=24 * 1024 * 1024),
         name="lines",
     )(pos, x_own, x_x, x_y, x_d, far_a)
+    (mine,) = call(
+        mine_kernel,
+        [jax.ShapeDtypeStruct((levels, height + 2, width + 16, chans), bf16)],
+        (pos, g_cells, x_own, x_x, x_d, by_x, by_d, xs),
+        [],
+        0,
+        "mine",
+        16,
+        held=1,
+    )
+    theirs = move(mine, sibling)
     (g2,) = call(
         pair_kernel, [jax.ShapeDtypeStruct((2, cells, wide), bf16)], (pos, g2a, g2b, xs), [], 0, "pair", 16, held=1
     )
@@ -567,7 +583,7 @@
     (grads,) = call(
         taps_kernel,
         [jax.ShapeDtypeStruct((27, span, wide), f32)],
-        (pos, xs, g_near, s_near, g2, s2),
+        (pos, xs, g0, g1, g3, s0, s1, s3, g2, s2),
         [VMEM((levels * wide, rows * circle), bf16), VMEM((3, 3 * wide, 4 * span), f32)],
         2 * 27 * span * wide * rows * circle * levels,
         "taps",

time: 146 us -> 146 us (level)
    ppermute x37 -> x39, waiting for transfers between devices: 46.8 us -> 45.7 us  [move(): return lax.ppermute(x, AXES, pairs)]
    pallas_call x14 -> x15, Pallas kernels: 16.9 us -> 17.4 us  [call(): pl.pallas_call(kernel, out_shape=outs, in_specs=[pl.BlockSpec(memory_spac...]
    ppermute x37 -> x39, starting transfers between devices: 49.1 us -> 49.5 us  [move(): return lax.ppermute(x, AXES, pairs)]
  transfers between devices with their start and end apart: 37 -> 39, of which waited for: 15 -> 14; matrix products, arithmetic and copies ran while one was open for 0% -> 0% of each run, Pallas kernels for 26% -> 26%
where the time goes in v18:
time: 146 us; the launch traced here: 145 us
  starting transfers between devices  49.5 us (34%)
  waiting for transfers between devices  45.7 us (31%)
  Pallas kernels  44.8 us (31%)
  local copies, waits for them, and re-layouts  4 us (3%)
    ppermute x39, starting transfers between devices, move(): return lax.ppermute(x, AXES, pairs)  49.5 us
    ppermute x39, waiting for transfers between devices, move(): return lax.ppermute(x, AXES, pairs)  45.7 us
    pallas_call x15, Pallas kernels, call(): pl.pallas_call(kernel, out_shape=outs, in_specs=[pl.BlockSpec(memory_spac...  17.4 us
    pallas_call x3, Pallas kernels, unpack(): pl.pallas_call(lambda *refs: unpack_kernel(*refs, slabs=slabs, count=len(...  13.1 us
    pallas_call x1, Pallas kernels, blocked_body(): pl.pallas_call(field_kernel, out_shape=jax.ShapeDtypeStruct((levels, heig...  9.5 us
    pallas_call x1, Pallas kernels, blocked_body(): pl.pallas_call(lines_kernel, out_shape=[jax.ShapeDtypeStruct((levels, row...  4.87 us
    unnamed x14, local copies, waits for them, and re-layouts  4 us
  transfers between devices with their start and end apart: 39, of which 14 were waited for; matrix products, arithmetic and copies ran while one was open for 0% of the time, Pallas kernels for 26%

profile of v18, /device:TPU:0, one launch (start us, length us, event | category | flops | bytes accessed | tf_op | source)
XLA Modules:
  0.0 145.2 jit_solution(12698803449170328321)
XLA Ops:
  0.7 1.0 copy-done.1
  1.7 1.0 copy-done.3
  2.7 0.8 pack.1
  4.2 3.0 %collective-permute-start.9 = (bf16[768,128]{1,0:T(8,128)(2,1)S(1)}, bf16[768,128]{1,0:T(8,128)(2,1)S(1)}, u32[]{:S(2)}, u32[]{:S(2)}) collective-permute-start(bf16[768,128]{1,0:T(8,128)(2,1)S(1)} %get-tuple-element.42), channel_id=1, source_target_pairs={{0,4},{1,5},{2,6},{3,7},{4,0},{5,1},{6,2},{7,3},{8,20},{9,21},{10,... | collective-permute-start | bytes 589832 | tf_op jit(solution)/shard_map/ppermute | solution.py:98
  7.2 1.6 %collective-permute-start = (bf16[416,128]{1,0:T(8,128)(2,1)S(1)}, bf16[416,128]{1,0:T(8,128)(2,1)S(1)}, u32[]{:S(2)}, u32[]{:S(2)}) collective-permute-start(bf16[416,128]{1,0:T(8,128)(2,1)S(1)} %get-tuple-element.34), channel_id=1, source_target_pairs={{0,1},{1,2},{2,3},{3,0},{4,5},{5,6},{6,7},{7,4},{8,9},{9,10},{10,1... | collective-permute-start | bytes 319496 | tf_op jit(solution)/shard_map/ppermute | solution.py:98
  8.8 2.2 %collective-permute-start.2 = (bf16[416,128]{1,0:T(8,128)(2,1)S(1)}, bf16[416,128]{1,0:T(8,128)(2,1)S(1)}, u32[]{:S(2)}, u32[]{:S(2)}) collective-permute-start(bf16[416,128]{1,0:T(8,128)(2,1)S(1)} %get-tuple-element.36), channel_id=1, source_target_pairs={{0,3},{1,0},{2,1},{3,2},{4,7},{5,4},{6,5},{7,6},{8,11},{9,8},{10,9... | collective-permute-start | bytes 319496 | tf_op jit(solution)/shard_map/ppermute | solution.py:98
  11.9 9.2 %collective-permute-done.1.x2.after2 = bf16[384,128]{1,0:T(8,128)(2,1)S(1)} collective-permute-done((bf16[384,128]{1,0:T(8,128)(2,1)S(1)}, bf16[384,128]{1,0:T(8,128)(2,1)S(1)}, u32[]{:S(2)}, u32[]{:S(2)}) %collective-permute-start.1) | collective-permute-done | bytes 98336 | tf_op jit(solution)/shard_map/ppermute | solution.py:98
  21.7 2.3 %collective-permute-start.11 = (bf16[1616,128]{1,0:T(8,128)(2,1)S(1)}, bf16[1616,128]{1,0:T(8,128)(2,1)S(1)}, u32[]{:S(2)}, u32[]{:S(2)}) collective-permute-start(bf16[1616,128]{1,0:T(8,128)(2,1)S(1)} %pair_0.1.g0), channel_id=1, source_target_pairs={{0,3},{1,0},{2,1},{3,2},{4,7},{5,4},{6,5},{7,6},{8,11},{9,8},{10,9... | collective-permute-start | bytes 1241096 | tf_op jit(solution)/shard_map/ppermute | solution.py:98
  24.5 2.3 %collective-permute-start.4 = (bf16[384,128]{1,0:T(8,128)(2,1)S(1)}, bf16[384,128]{1,0:T(8,128)(2,1)S(1)}, u32[]{:S(2)}, u32[]{:S(2)}) collective-permute-start(bf16[384,128]{1,0:T(8,128)(2,1)S(1)} %get-tuple-element.38), channel_id=1, source_target_pairs={{0,12},{1,13},{2,14},{3,15},{4,8},{5,9},{6,10},{7,11},{8,4},{9,5},... | collective-permute-start | bytes 294920 | tf_op jit(solution)/shard_map/ppermute | solution.py:98
  26.8 2.7 %collective-permute-done.3.after1.by_x = bf16[384,128]{1,0:T(8,128)(2,1)S(1)} collective-permute-done((bf16[384,128]{1,0:T(8,128)(2,1)S(1)}, bf16[384,128]{1,0:T(8,128)(2,1)S(1)}, u32[]{:S(2)}, u32[]{:S(2)}) %collective-permute-start.3) | collective-permute-done | bytes 98336 | tf_op jit(solution)/shard_map/ppermute | solution.py:98
  29.5 1.2 collective-permute-done.4.after2.by_d
  31.4 1.7 %collective-permute-start.7 = (bf16[1600,128]{1,0:T(8,128)(2,1)S(1)}, bf16[1600,128]{1,0:T(8,128)(2,1)S(1)}, u32[]{:S(2)}, u32[]{:S(2)}) collective-permute-start(bf16[1600,128]{1,0:T(8,128)(2,1)S(1)} %get-tuple-element.39.x_own.own), channel_id=1, source_target_pairs={{0,12},{1,13},{2,14},{3,15},{4,8},{5,9},{6,10},{7,11},{8,4},{9,5},... | collective-permute-start | bytes 1228808 | tf_op jit(solution)/shard_map/ppermute | solution.py:98
  33.0 1.2 collective-permute-start.5
  34.9 7.7 %collective-permute-done.10.west.g1 = bf16[1616,128]{1,0:T(8,128)(2,1)S(1)} collective-permute-done((bf16[1616,128]{1,0:T(8,128)(2,1)S(1)}, bf16[1616,128]{1,0:T(8,128)(2,1)S(1)}, u32[]{:S(2)}, u32[]{:S(2)}) %collective-permute-start.10) | collective-permute-done | bytes 413728 | tf_op jit(solution)/shard_map/ppermute | solution.py:98
  43.2 1.9 %collective-permute-start.16 = (bf16[768,128]{1,0:T(8,128)(2,1)S(1)}, bf16[768,128]{1,0:T(8,128)(2,1)S(1)}, u32[]{:S(2)}, u32[]{:S(2)}) collective-permute-start(bf16[768,128]{1,0:T(8,128)(2,1)S(1)} %get-tuple-element.45), channel_id=1, source_target_pairs={{0,3},{1,0},{2,1},{3,2},{4,7},{5,4},{6,5},{7,6},{8,11},{9,8},{10,9... | collective-permute-start | bytes 589832 | tf_op jit(solution)/shard_map/ppermute | solution.py:98
  45.3 4.9 %collective-permute-done.6.x_y = bf16[1536,128]{1,0:T(8,128)(2,1)S(1)} collective-permute-done((bf16[1536,128]{1,0:T(8,128)(2,1)S(1)}, bf16[1536,128]{1,0:T(8,128)(2,1)S(1)}, u32[]{:S(2)}, u32[]{:S(2)}) %collective-permute-start.6) | collective-permute-done | bytes 393248 | tf_op jit(solution)/shard_map/ppermute | solution.py:98
  51.0 4.9 %lines.1 = (bf16[4,18,192,256]{3,2,1,0:T(8,128)(2,1)S(1)}, f32[27,256,512]{2,1,0:T(8,128)}) custom-call(s32[3]{0:T(128)S(1)} %pad_add_fusion.pos.refs_0_, bf16[1600,128]{1,0:T(8,128)(2,1)S(1)} %get-tuple-element.39.x_own.own, bf16[1600,128]{1,0:T(8,128)(2,1)S(1)} %collective-permute-done.5.x_x, bf16[1536,128]{1,0:T(8,128)(2,1)S(1)} %collective-permute-done.6.x_y, ...), custom_call_target="tpu_custom_call" | custom-call | bytes 1048576 | tf_op jit(solution)/shard_map/lines/pallas_call | solution.py:547
  57.1 1.0 copy-done.2
  58.9 8.6 %taps.1.held = f32[27,64,128]{2,1,0:T(8,128)S(1)} custom-call(s32[3]{0:T(128)S(1)} %pad_add_fusion.pos.refs_0_, bf16[4,18,192,256]{3,2,1,0:T(8,128)(2,1)S(1)} %get-tuple-element.44.after.xs, bf16[1616,128]{1,0:T(8,128)(2,1)S(1)} %pair_0.1.g0, bf16[1616,128]{1,0:T(8,128)(2,1)S(1)} %collective-permute-done.10.west.g1, ...), custom_call_target="tpu_custom_call" | custom-call | flops 5435817984 | bytes 11231232 | tf_op jit(solution)/shard_map/taps/pallas_call | solution.py:116
  67.5 0.9 code.1
  68.4 3.9 %collective-permute-start.28 = (bf16[1552,128]{1,0:T(8,128)(2,1)S(1)}, bf16[1552,128]{1,0:T(8,128)(2,1)S(1)}, u32[]{:S(2)}, u32[]{:S(2)}) collective-permute-start(bf16[1552,128]{1,0:T(8,128)(2,1)S(1)} %get-tuple-element.51), channel_id=1, source_target_pairs={{0,3},{1,0},{2,1},{3,2},{4,7},{5,4},{6,5},{7,6},{8,11},{9,8},{10,9... | collective-permute-start | bytes 1191944 | tf_op jit(solution)/shard_map/ppermute | solution.py:98
  72.3 1.3 collective-permute-start.20
  74.2 9.5 %field.1.after1 = bf16[4,4,48,256]{3,2,1,0:T(8,128)(2,1)} custom-call(s32[3]{0:T(128)S(1)} %pad_add_fusion.pos.refs_0_, bf16[1744,128]{1,0:T(8,128)(2,1)S(1)} %get-tuple-element.46.after.after2.own.refs_1_, bf16[4,6,64,256]{3,2,1,0:T(8,128)(2,1)S(1)} %mine.1, bf16[4,6,64,256]{3,2,1,0:T(8,128)(2,1)S(1)} %collective-permute-done.18.after.theirs, ...), custom_call_target="tpu_custom_call" | custom-call | flops 10871635968 | bytes 7077888 | tf_op jit(solution)/shard_map/field/pallas_call | solution.py:595
  83.7 1.0 collective-permute-done.20.by_y.y.refs_3_
  84.7 1.0 collective-permute-done.19.by_x.x.refs_2_
  85.6 1.0 copy-done.4
  87.8 1.4 collective-permute-start.22
  89.3 1.4 collective-permute-done.27.west.refs_1_
  90.7 3.2 %collective-permute-done.22.bottom.after2.refs_5_ = bf16[848,128]{1,0:T(8,128)(2,1)S(1)} collective-permute-done((bf16[848,128]{1,0:T(8,128)(2,1)S(1)}, bf16[848,128]{1,0:T(8,128)(2,1)S(1)}, u32[]{:S(2)}, u32[]{:S(2)}) %collective-permute-start.22) | collective-permute-done | bytes 217120 | tf_op jit(solution)/shard_map/ppermute | solution.py:98
  94.5 1.5 %collective-permute-start.36 = (bf16[3104,128]{1,0:T(8,128)(2,1)S(1)}, bf16[3104,128]{1,0:T(8,128)(2,1)S(1)}, u32[]{:S(2)}, u32[]{:S(2)}) collective-permute-start(bf16[3104,128]{1,0:T(8,128)(2,1)S(1)} %get-tuple-element.54.after.after2), channel_id=1, source_target_pairs={{0,8},{1,9},{2,10},{3,11},{4,12},{5,13},{6,14},{7,15},{8,0},{9,1},... | collective-permute-start | bytes 2383880 | tf_op jit(solution)/shard_map/ppermute | solution.py:98
  96.0 0.8 collective-permute-start.35
  97.3 3.9 %collective-permute-start.24 = (bf16[832,128]{1,0:T(8,128)(2,1)S(1)}, bf16[832,128]{1,0:T(8,128)(2,1)S(1)}, u32[]{:S(2)}, u32[]{:S(2)}) collective-permute-start(bf16[832,128]{1,0:T(8,128)(2,1)S(1)} %block.1.refs_6_), channel_id=1, source_target_pairs={{0,3},{1,0},{2,1},{3,2},{4,7},{5,4},{6,5},{7,6},{8,11},{9,8},{10,9... | collective-permute-start | bytes 638984 | tf_op jit(solution)/shard_map/ppermute | solution.py:98
  101.2 1.6 %collective-permute-start.30 = (bf16[784,128]{1,0:T(8,128)(2,1)S(1)}, bf16[784,128]{1,0:T(8,128)(2,1)S(1)}, u32[]{:S(2)}, u32[]{:S(2)}) collective-permute-start(bf16[784,128]{1,0:T(8,128)(2,1)S(1)} %get-tuple-element.53), channel_id=1, source_target_pairs={{0,3},{1,0},{2,1},{3,2},{4,7},{5,4},{6,5},{7,6},{8,11},{9,8},{10,9... | collective-permute-start | bytes 602120 | tf_op jit(solution)/shard_map/ppermute | solution.py:98
  102.9 3.6 %collective-permute-done.29.half_3 = bf16[768,128]{1,0:T(8,128)(2,1)S(1)} collective-permute-done((bf16[768,128]{1,0:T(8,128)(2,1)S(1)}, bf16[768,128]{1,0:T(8,128)(2,1)S(1)}, u32[]{:S(2)}, u32[]{:S(2)}) %collective-permute-start.29) | collective-permute-done | bytes 196640 | tf_op jit(solution)/shard_map/ppermute | solution.py:98
  106.4 2.1 %collective-permute-start.23 = (bf16[832,128]{1,0:T(8,128)(2,1)S(1)}, bf16[832,128]{1,0:T(8,128)(2,1)S(1)}, u32[]{:S(2)}, u32[]{:S(2)}) collective-permute-start(bf16[832,128]{1,0:T(8,128)(2,1)S(1)} %block.1.refs_6_), channel_id=1, source_target_pairs={{0,1},{1,2},{2,3},{3,0},{4,5},{5,6},{6,7},{7,4},{8,9},{9,10},{10,1... | collective-permute-start | bytes 638984 | tf_op jit(solution)/shard_map/ppermute | solution.py:98
  108.5 4.1 %collective-permute-done.30.half_1 = bf16[784,128]{1,0:T(8,128)(2,1)S(1)} collective-permute-done((bf16[784,128]{1,0:T(8,128)(2,1)S(1)}, bf16[784,128]{1,0:T(8,128)(2,1)S(1)}, u32[]{:S(2)}, u32[]{:S(2)}) %collective-permute-start.30) | collective-permute-done | bytes 200736 | tf_op jit(solution)/shard_map/ppermute | solution.py:98
  113.2 1.3 collective-permute-start.32
  115.3 4.3 %collective-permute-done.23.block_3.after2.refs_7_ = bf16[832,128]{1,0:T(8,128)(2,1)S(1)} collective-permute-done((bf16[832,128]{1,0:T(8,128)(2,1)S(1)}, bf16[832,128]{1,0:T(8,128)(2,1)S(1)}, u32[]{:S(2)}, u32[]{:S(2)}) %collective-permute-start.23) | collective-permute-done | bytes 213024 | tf_op jit(solution)/shard_map/ppermute | solution.py:98
  120.3 1.3 collective-permute-start.37
  121.5 0.9 collective-permute-start.38
  122.4 3.1 %unpack_1.1 = (f32[27,256,512]{2,1,0:T(8,128)}, f32[8,128]{1,0:T(8,128)S(1)}) custom-call(s32[3]{0:T(128)S(1)} %pad_add_fusion.pos.refs_0_, bf16[1744,128]{1,0:T(8,128)(2,1)S(1)} %get-tuple-element.46.after.after2.own.refs_1_, bf16[1744,128]{1,0:T(8,128)(2,1)S(1)} %collective-permute-done.19.by_x.x.refs_2_, ...), custom_call_target="tpu_custom_call", output_to_operand_aliasing={{0}: (7, {})} | custom-call | bytes 4194304 | tf_op jit(solution)/shard_map/unpack_1/pallas_call | solution.py:420
  125.6 1.1 collective-permute-done.31.by_x.refs_4_
  127.2 0.8 collective-permute-start.34
  128.1 1.2 collective-permute-start.33
  129.9 3.3 %collective-permute-start.26 = (bf16[416,128]{1,0:T(8,128)(2,1)S(1)}, bf16[416,128]{1,0:T(8,128)(2,1)S(1)}, u32[]{:S(2)}, u32[]{:S(2)}) collective-permute-start(bf16[416,128]{1,0:T(8,128)(2,1)S(1)} %get-tuple-element.50), channel_id=1, source_target_pairs={{0,3},{1,0},{2,1},{3,2},{4,7},{5,4},{6,5},{7,6},{8,11},{9,8},{10,9... | collective-permute-start | bytes 319496 | tf_op jit(solution)/shard_map/ppermute | solution.py:98
  133.1 2.0 %collective-permute-start.25 = (bf16[416,128]{1,0:T(8,128)(2,1)S(1)}, bf16[416,128]{1,0:T(8,128)(2,1)S(1)}, u32[]{:S(2)}, u32[]{:S(2)}) collective-permute-start(bf16[416,128]{1,0:T(8,128)(2,1)S(1)} %get-tuple-element.49.refs_9_), channel_id=1, source_target_pairs={{0,1},{1,2},{2,3},{3,0},{4,5},{5,6},{6,7},{7,4},{8,9},{9,10},{10,1... | collective-permute-start | bytes 319496 | tf_op jit(solution)/shard_map/ppermute | solution.py:98
  135.1 6.2 %unpack_2.1 = (f32[27,256,512]{2,1,0:T(8,128)}, f32[8,128]{1,0:T(8,128)}) custom-call(s32[3]{0:T(128)S(1)} %pad_add_fusion.pos.refs_0_, bf16[1552,128]{1,0:T(8,128)(2,1)S(1)} %collective-permute-done.27.west.refs_1_, bf16[1552,128]{1,0:T(8,128)(2,1)S(1)} %collective-permute-done.28.east.refs_2_, ...), custom_call_target="tpu_custom_call", output_to_operand_aliasing={{0}: (10, {})} | custom-call | bytes 4194304 | tf_op jit(solution)/shard_map/unpack_2/pallas_call | solution.py:420
  141.3 3.7 %unpack_3.1 = (f32[27,256,512]{2,1,0:T(8,128)}, f32[8,128]{1,0:T(8,128)}) custom-call(s32[3]{0:T(128)S(1)} %pad_add_fusion.pos.refs_0_, bf16[416,128]{1,0:T(8,128)(2,1)S(1)} %collective-permute-done.25.refs_1_, bf16[416,128]{1,0:T(8,128)(2,1)S(1)} %collective-permute-done.26.refs_2_, ...), custom_call_target="tpu_custom_call", output_to_operand_aliasing={{0}: (8, {})} | custom-call | bytes 4194304 | tf_op jit(solution)/shard_map/unpack_3/pallas_call | solution.py:420
  (66 shorter events, 13.8 us)
Async XLA Ops:
  0.7 1.0 copy-start.1
  1.7 1.0 copy-start.3
  3.6 17.5 %collective-permute-start.8 = (bf16[768,128]{1,0:T(8,128)(2,1)S(1)}, bf16[768,128]{1,0:T(8,128)(2,1)S(1)}, u32[]{:S(2)}, u32[]{:S(2)}) collective-permute-start(bf16[768,128]{1,0:T(8,128)(2,1)S(1)} %get-tuple-element.41), channel_id=1, source_target_pairs={{0,0},{1,1},{2,2},{3,3},{4,4},{5,5},{6,6},{7,7},{8,16},{9,17},{10,... | collective-permute-start | bytes 589832 | tf_op jit(solution)/shard_map/ppermute | solution.py:98
  4.2 16.8 %collective-permute-start.9 = (bf16[768,128]{1,0:T(8,128)(2,1)S(1)}, bf16[768,128]{1,0:T(8,128)(2,1)S(1)}, u32[]{:S(2)}, u32[]{:S(2)}) collective-permute-start(bf16[768,128]{1,0:T(8,128)(2,1)S(1)} %get-tuple-element.42), channel_id=1, source_target_pairs={{0,4},{1,5},{2,6},{3,7},{4,0},{5,1},{6,2},{7,3},{8,20},{9,21},{10,... | collective-permute-start | bytes 589832 | tf_op jit(solution)/shard_map/ppermute | solution.py:98
  7.2 13.8 %collective-permute-start = (bf16[416,128]{1,0:T(8,128)(2,1)S(1)}, bf16[416,128]{1,0:T(8,128)(2,1)S(1)}, u32[]{:S(2)}, u32[]{:S(2)}) collective-permute-start(bf16[416,128]{1,0:T(8,128)(2,1)S(1)} %get-tuple-element.34), channel_id=1, source_target_pairs={{0,1},{1,2},{2,3},{3,0},{4,5},{5,6},{6,7},{7,4},{8,9},{9,10},{10,1... | collective-permute-start | bytes 319496 | tf_op jit(solution)/shard_map/ppermute | solution.py:98
  8.8 12.2 %collective-permute-start.2 = (bf16[416,128]{1,0:T(8,128)(2,1)S(1)}, bf16[416,128]{1,0:T(8,128)(2,1)S(1)}, u32[]{:S(2)}, u32[]{:S(2)}) collective-permute-start(bf16[416,128]{1,0:T(8,128)(2,1)S(1)} %get-tuple-element.36), channel_id=1, source_target_pairs={{0,3},{1,0},{2,1},{3,2},{4,7},{5,4},{6,5},{7,6},{8,11},{9,8},{10,9... | collective-permute-start | bytes 319496 | tf_op jit(solution)/shard_map/ppermute | solution.py:98
  11.1 10.0 %collective-permute-start.1 = (bf16[384,128]{1,0:T(8,128)(2,1)S(1)}, bf16[384,128]{1,0:T(8,128)(2,1)S(1)}, u32[]{:S(2)}, u32[]{:S(2)}) collective-permute-start(bf16[384,128]{1,0:T(8,128)(2,1)S(1)} %get-tuple-element.35), channel_id=1, source_target_pairs={{0,2},{1,3},{2,0},{3,1},{4,6},{5,7},{6,4},{7,5},{8,10},{9,11},{10,... | collective-permute-start | bytes 294920 | tf_op jit(solution)/shard_map/ppermute | solution.py:98
  21.7 13.3 %collective-permute-start.11 = (bf16[1616,128]{1,0:T(8,128)(2,1)S(1)}, bf16[1616,128]{1,0:T(8,128)(2,1)S(1)}, u32[]{:S(2)}, u32[]{:S(2)}) collective-permute-start(bf16[1616,128]{1,0:T(8,128)(2,1)S(1)} %pair_0.1.g0), channel_id=1, source_target_pairs={{0,3},{1,0},{2,1},{3,2},{4,7},{5,4},{6,5},{7,6},{8,11},{9,8},{10,9... | collective-permute-start | bytes 1241096 | tf_op jit(solution)/shard_map/ppermute | solution.py:98
  23.9 18.7 %collective-permute-start.10 = (bf16[1616,128]{1,0:T(8,128)(2,1)S(1)}, bf16[1616,128]{1,0:T(8,128)(2,1)S(1)}, u32[]{:S(2)}, u32[]{:S(2)}) collective-permute-start(bf16[1616,128]{1,0:T(8,128)(2,1)S(1)} %pair_0.1.g0), channel_id=1, source_target_pairs={{0,1},{1,2},{2,3},{3,0},{4,5},{5,6},{6,7},{7,4},{8,9},{9,10},{10,1... | collective-permute-start | bytes 1241096 | tf_op jit(solution)/shard_map/ppermute | solution.py:98
  23.9 5.6 %collective-permute-start.3 = (bf16[384,128]{1,0:T(8,128)(2,1)S(1)}, bf16[384,128]{1,0:T(8,128)(2,1)S(1)}, u32[]{:S(2)}, u32[]{:S(2)}) collective-permute-start(bf16[384,128]{1,0:T(8,128)(2,1)S(1)} %get-tuple-element.37), channel_id=1, source_target_pairs={{0,4},{1,5},{2,6},{3,7},{4,0},{5,1},{6,2},{7,3},{8,12},{9,13},{10,... | collective-permute-start | bytes 294920 | tf_op jit(solution)/shard_map/ppermute | solution.py:98
  24.5 6.2 %collective-permute-start.4 = (bf16[384,128]{1,0:T(8,128)(2,1)S(1)}, bf16[384,128]{1,0:T(8,128)(2,1)S(1)}, u32[]{:S(2)}, u32[]{:S(2)}) collective-permute-start(bf16[384,128]{1,0:T(8,128)(2,1)S(1)} %get-tuple-element.38), channel_id=1, source_target_pairs={{0,12},{1,13},{2,14},{3,15},{4,8},{5,9},{6,10},{7,11},{8,4},{9,5},... | collective-permute-start | bytes 294920 | tf_op jit(solution)/shard_map/ppermute | solution.py:98
  31.4 18.8 %collective-permute-start.7 = (bf16[1600,128]{1,0:T(8,128)(2,1)S(1)}, bf16[1600,128]{1,0:T(8,128)(2,1)S(1)}, u32[]{:S(2)}, u32[]{:S(2)}) collective-permute-start(bf16[1600,128]{1,0:T(8,128)(2,1)S(1)} %get-tuple-element.39.x_own.own), channel_id=1, source_target_pairs={{0,12},{1,13},{2,14},{3,15},{4,8},{5,9},{6,10},{7,11},{8,4},{9,5},... | collective-permute-start | bytes 1228808 | tf_op jit(solution)/shard_map/ppermute | solution.py:98
  33.0 18.0 %collective-permute-start.5 = (bf16[1600,128]{1,0:T(8,128)(2,1)S(1)}, bf16[1600,128]{1,0:T(8,128)(2,1)S(1)}, u32[]{:S(2)}, u32[]{:S(2)}) collective-permute-start(bf16[1600,128]{1,0:T(8,128)(2,1)S(1)} %get-tuple-element.39.x_own.own), channel_id=1, source_target_pairs={{0,4},{1,5},{2,6},{3,7},{4,0},{5,1},{6,2},{7,3},{8,12},{9,13},{10,... | collective-permute-start | bytes 1228808 | tf_op jit(solution)/shard_map/ppermute | solution.py:98
  34.2 15.9 %collective-permute-start.6 = (bf16[1536,128]{1,0:T(8,128)(2,1)S(1)}, bf16[1536,128]{1,0:T(8,128)(2,1)S(1)}, u32[]{:S(2)}, u32[]{:S(2)}) collective-permute-start(bf16[1536,128]{1,0:T(8,128)(2,1)S(1)} %get-tuple-element.40), channel_id=1, source_target_pairs={{0,8},{1,9},{2,10},{3,11},{4,12},{5,13},{6,14},{7,15},{8,0},{9,1},... | collective-permute-start | bytes 1179656 | tf_op jit(solution)/shard_map/ppermute | solution.py:98
  43.2 12.7 %collective-permute-start.16 = (bf16[768,128]{1,0:T(8,128)(2,1)S(1)}, bf16[768,128]{1,0:T(8,128)(2,1)S(1)}, u32[]{:S(2)}, u32[]{:S(2)}) collective-permute-start(bf16[768,128]{1,0:T(8,128)(2,1)S(1)} %get-tuple-element.45), channel_id=1, source_target_pairs={{0,3},{1,0},{2,1},{3,2},{4,7},{5,4},{6,5},{7,6},{8,11},{9,8},{10,9... | collective-permute-start | bytes 589832 | tf_op jit(solution)/shard_map/ppermute | solution.py:98
  45.1 10.9 %collective-permute-start.15 = (bf16[768,128]{1,0:T(8,128)(2,1)S(1)}, bf16[768,128]{1,0:T(8,128)(2,1)S(1)}, u32[]{:S(2)}, u32[]{:S(2)}) collective-permute-start(bf16[768,128]{1,0:T(8,128)(2,1)S(1)} %get-tuple-element.43.after), channel_id=1, source_target_pairs={{0,1},{1,2},{2,3},{3,0},{4,5},{5,6},{6,7},{7,4},{8,9},{9,10},{10,1... | collective-permute-start | bytes 589832 | tf_op jit(solution)/shard_map/ppermute | solution.py:98
  50.1 8.7 %collective-permute-start.12 = (bf16[1616,128]{1,0:T(8,128)(2,1)S(1)}, bf16[1616,128]{1,0:T(8,128)(2,1)S(1)}, u32[]{:S(2)}, u32[]{:S(2)}) collective-permute-start(bf16[1616,128]{1,0:T(8,128)(2,1)S(1)} %pair_0.1.g0), channel_id=1, source_target_pairs={{0,16},{1,17},{2,18},{3,19},{4,20},{5,21},{6,22},{7,23},{8,24},{9,... | collective-permute-start | bytes 1241096 | tf_op jit(solution)/shard_map/ppermute | solution.py:98
  50.1 8.7 %collective-permute-start.14 = (bf16[1616,128]{1,0:T(8,128)(2,1)S(1)}, bf16[1616,128]{1,0:T(8,128)(2,1)S(1)}, u32[]{:S(2)}, u32[]{:S(2)}) collective-permute-start(bf16[1616,128]{1,0:T(8,128)(2,1)S(1)} %collective-permute-done.11.east.g3), channel_id=1, source_target_pairs={{0,16},{1,17},{2,18},{3,19},{4,20},{5,21},{6,22},{7,23},{8,24},{9,... | collective-permute-start | bytes 1241096 | tf_op jit(solution)/shard_map/ppermute | solution.py:98
  51.0 7.8 %collective-permute-start.13 = (bf16[1616,128]{1,0:T(8,128)(2,1)S(1)}, bf16[1616,128]{1,0:T(8,128)(2,1)S(1)}, u32[]{:S(2)}, u32[]{:S(2)}) collective-permute-start(bf16[1616,128]{1,0:T(8,128)(2,1)S(1)} %collective-permute-done.10.west.g1), channel_id=1, source_target_pairs={{0,16},{1,17},{2,18},{3,19},{4,20},{5,21},{6,22},{7,23},{8,24},{9,... | collective-permute-start | bytes 1241096 | tf_op jit(solution)/shard_map/ppermute | solution.py:98
  56.5 2.4 %collective-permute-start.17 = (bf16[2,768,128]{2,1,0:T(8,128)(2,1)S(1)}, bf16[2,768,128]{2,1,0:T(8,128)(2,1)S(1)}, u32[]{:S(2)}, u32[]{:S(2)}) collective-permute-start(bf16[2,768,128]{2,1,0:T(8,128)(2,1)S(1)} %pair.1.g2), channel_id=1, source_target_pairs={{0,16},{1,17},{2,18},{3,19},{4,20},{5,21},{6,22},{7,23},{8,24},{9,... | collective-permute-start | bytes 1179656 | tf_op jit(solution)/shard_map/ppermute | solution.py:98
  57.1 1.0 copy-start.2
  58.1 16.1 %slice-start = ((s8[7077888]{0:T(1024)(128)(4,1)}), s8[4194304]{0:T(1024)(128)(4,1)S(1)}, s32[]{:S(2)}) async-start(s8[7077888]{0:T(1024)(128)(4,1)} %bitcast.12), calls=%async_computation | async-start | bytes 8388608
  58.8 15.4 %slice-start.1 = ((s8[7077888]{0:T(1024)(128)(4,1)}), s8[2883584]{0:T(1024)(128)(4,1)S(1)}, s32[]{:S(2)}) async-start(s8[7077888]{0:T(1024)(128)(4,1)} %bitcast.12), calls=%async_computation.1 | async-start | bytes 5767168
  58.8 8.7 %collective-permute-start.18 = (bf16[4,6,64,256]{3,2,1,0:T(8,128)(2,1)S(1)}, bf16[4,6,64,256]{3,2,1,0:T(8,128)(2,1)S(1)}, u32[]{:S(2)}, u32[]{:S(2)}) collective-permute-start(bf16[4,6,64,256]{3,2,1,0:T(8,128)(2,1)S(1)} %mine.1), channel_id=1, source_target_pairs={{0,16},{1,17},{2,18},{3,19},{4,20},{5,21},{6,22},{7,23},{8,24},{9,... | collective-permute-start | bytes 2359304 | tf_op jit(solution)/shard_map/ppermute | solution.py:98
  68.4 20.9 %collective-permute-start.28 = (bf16[1552,128]{1,0:T(8,128)(2,1)S(1)}, bf16[1552,128]{1,0:T(8,128)(2,1)S(1)}, u32[]{:S(2)}, u32[]{:S(2)}) collective-permute-start(bf16[1552,128]{1,0:T(8,128)(2,1)S(1)} %get-tuple-element.51), channel_id=1, source_target_pairs={{0,3},{1,0},{2,1},{3,2},{4,7},{5,4},{6,5},{7,6},{8,11},{9,8},{10,9... | collective-permute-start | bytes 1191944 | tf_op jit(solution)/shard_map/ppermute | solution.py:98
  72.3 18.3 %collective-permute-start.27 = (bf16[1552,128]{1,0:T(8,128)(2,1)S(1)}, bf16[1552,128]{1,0:T(8,128)(2,1)S(1)}, u32[]{:S(2)}, u32[]{:S(2)}) collective-permute-start(bf16[1552,128]{1,0:T(8,128)(2,1)S(1)} %get-tuple-element.51), channel_id=1, source_target_pairs={{0,1},{1,2},{2,3},{3,0},{4,5},{5,6},{6,7},{7,4},{8,9},{9,10},{10,1... | collective-permute-start | bytes 1191944 | tf_op jit(solution)/shard_map/ppermute | solution.py:98
  72.3 12.3 %collective-permute-start.20 = (bf16[1744,128]{1,0:T(8,128)(2,1)S(1)}, bf16[1744,128]{1,0:T(8,128)(2,1)S(1)}, u32[]{:S(2)}, u32[]{:S(2)}) collective-permute-start(bf16[1744,128]{1,0:T(8,128)(2,1)S(1)} %get-tuple-element.46.after.after2.own.refs_1_), channel_id=1, source_target_pairs={{0,8},{1,9},{2,10},{3,11},{4,12},{5,13},{6,14},{7,15},{8,0},{9,1},... | collective-permute-start | bytes 1339400 | tf_op jit(solution)/shard_map/ppermute | solution.py:98
  73.6 12.0 %collective-permute-start.19 = (bf16[1744,128]{1,0:T(8,128)(2,1)S(1)}, bf16[1744,128]{1,0:T(8,128)(2,1)S(1)}, u32[]{:S(2)}, u32[]{:S(2)}) collective-permute-start(bf16[1744,128]{1,0:T(8,128)(2,1)S(1)} %get-tuple-element.46.after.after2.own.refs_1_), channel_id=1, source_target_pairs={{0,4},{1,5},{2,6},{3,7},{4,0},{5,1},{6,2},{7,3},{8,12},{9,13},{10,... | collective-permute-start | bytes 1339400 | tf_op jit(solution)/shard_map/ppermute | solution.py:98
  85.6 1.0 copy-start.4
  87.2 6.6 %collective-permute-start.21 = (bf16[896,128]{1,0:T(8,128)(2,1)S(1)}, bf16[896,128]{1,0:T(8,128)(2,1)S(1)}, u32[]{:S(2)}, u32[]{:S(2)}) collective-permute-start(bf16[896,128]{1,0:T(8,128)(2,1)S(1)} %get-tuple-element.47), channel_id=1, source_target_pairs={{0,4},{1,5},{2,6},{3,7},{4,0},{5,1},{6,2},{7,3},{8,12},{9,13},{10,... | collective-permute-start | bytes 688136 | tf_op jit(solution)/shard_map/ppermute | solution.py:98
  87.8 6.0 %collective-permute-start.22 = (bf16[848,128]{1,0:T(8,128)(2,1)S(1)}, bf16[848,128]{1,0:T(8,128)(2,1)S(1)}, u32[]{:S(2)}, u32[]{:S(2)}) collective-permute-start(bf16[848,128]{1,0:T(8,128)(2,1)S(1)} %get-tuple-element.48), channel_id=1, source_target_pairs={{0,8},{1,9},{2,10},{3,11},{4,12},{5,13},{6,14},{7,15},{8,0},{9,1},... | collective-permute-start | bytes 651272 | tf_op jit(solution)/shard_map/ppermute | solution.py:98
  94.5 25.1 %collective-permute-start.36 = (bf16[3104,128]{1,0:T(8,128)(2,1)S(1)}, bf16[3104,128]{1,0:T(8,128)(2,1)S(1)}, u32[]{:S(2)}, u32[]{:S(2)}) collective-permute-start(bf16[3104,128]{1,0:T(8,128)(2,1)S(1)} %get-tuple-element.54.after.after2), channel_id=1, source_target_pairs={{0,8},{1,9},{2,10},{3,11},{4,12},{5,13},{6,14},{7,15},{8,0},{9,1},... | collective-permute-start | bytes 2383880 | tf_op jit(solution)/shard_map/ppermute | solution.py:98
  96.0 23.7 %collective-permute-start.35 = (bf16[3104,128]{1,0:T(8,128)(2,1)S(1)}, bf16[3104,128]{1,0:T(8,128)(2,1)S(1)}, u32[]{:S(2)}, u32[]{:S(2)}) collective-permute-start(bf16[3104,128]{1,0:T(8,128)(2,1)S(1)} %get-tuple-element.54.after.after2), channel_id=1, source_target_pairs={{0,4},{1,5},{2,6},{3,7},{4,0},{5,1},{6,2},{7,3},{8,12},{9,13},{10,... | collective-permute-start | bytes 2383880 | tf_op jit(solution)/shard_map/ppermute | solution.py:98
  96.8 9.6 %collective-permute-start.29 = (bf16[768,128]{1,0:T(8,128)(2,1)S(1)}, bf16[768,128]{1,0:T(8,128)(2,1)S(1)}, u32[]{:S(2)}, u32[]{:S(2)}) collective-permute-start(bf16[768,128]{1,0:T(8,128)(2,1)S(1)} %get-tuple-element.52), channel_id=1, source_target_pairs={{0,1},{1,2},{2,3},{3,0},{4,5},{5,6},{6,7},{7,4},{8,9},{9,10},{10,1... | collective-permute-start | bytes 589832 | tf_op jit(solution)/shard_map/ppermute | solution.py:98
  97.3 17.2 %collective-permute-start.24 = (bf16[832,128]{1,0:T(8,128)(2,1)S(1)}, bf16[832,128]{1,0:T(8,128)(2,1)S(1)}, u32[]{:S(2)}, u32[]{:S(2)}) collective-permute-start(bf16[832,128]{1,0:T(8,128)(2,1)S(1)} %block.1.refs_6_), channel_id=1, source_target_pairs={{0,3},{1,0},{2,1},{3,2},{4,7},{5,4},{6,5},{7,6},{8,11},{9,8},{10,9... | collective-permute-start | bytes 638984 | tf_op jit(solution)/shard_map/ppermute | solution.py:98
  101.2 11.4 %collective-permute-start.30 = (bf16[784,128]{1,0:T(8,128)(2,1)S(1)}, bf16[784,128]{1,0:T(8,128)(2,1)S(1)}, u32[]{:S(2)}, u32[]{:S(2)}) collective-permute-start(bf16[784,128]{1,0:T(8,128)(2,1)S(1)} %get-tuple-element.53), channel_id=1, source_target_pairs={{0,3},{1,0},{2,1},{3,2},{4,7},{5,4},{6,5},{7,6},{8,11},{9,8},{10,9... | collective-permute-start | bytes 602120 | tf_op jit(solution)/shard_map/ppermute | solution.py:98
  106.4 13.2 %collective-permute-start.23 = (bf16[832,128]{1,0:T(8,128)(2,1)S(1)}, bf16[832,128]{1,0:T(8,128)(2,1)S(1)}, u32[]{:S(2)}, u32[]{:S(2)}) collective-permute-start(bf16[832,128]{1,0:T(8,128)(2,1)S(1)} %block.1.refs_6_), channel_id=1, source_target_pairs={{0,1},{1,2},{2,3},{3,0},{4,5},{5,6},{6,7},{7,4},{8,9},{9,10},{10,1... | collective-permute-start | bytes 638984 | tf_op jit(solution)/shard_map/ppermute | solution.py:98
  113.2 12.4 %collective-permute-start.32 = (bf16[1552,128]{1,0:T(8,128)(2,1)S(1)}, bf16[1552,128]{1,0:T(8,128)(2,1)S(1)}, u32[]{:S(2)}, u32[]{:S(2)}) collective-permute-start(bf16[1552,128]{1,0:T(8,128)(2,1)S(1)} %across.1.refs_3_), channel_id=1, source_target_pairs={{0,8},{1,9},{2,10},{3,11},{4,12},{5,13},{6,14},{7,15},{8,0},{9,1},... | collective-permute-start | bytes 1191944 | tf_op jit(solution)/shard_map/ppermute | solution.py:98
  114.5 12.1 %collective-permute-start.31 = (bf16[1552,128]{1,0:T(8,128)(2,1)S(1)}, bf16[1552,128]{1,0:T(8,128)(2,1)S(1)}, u32[]{:S(2)}, u32[]{:S(2)}) collective-permute-start(bf16[1552,128]{1,0:T(8,128)(2,1)S(1)} %across.1.refs_3_), channel_id=1, source_target_pairs={{0,4},{1,5},{2,6},{3,7},{4,0},{5,1},{6,2},{7,3},{8,12},{9,13},{10,... | collective-permute-start | bytes 1191944 | tf_op jit(solution)/shard_map/ppermute | solution.py:98
  119.6 15.4 %copy-start = (bf16[3104,128]{1,0:T(8,128)(2,1)}, bf16[3104,128]{1,0:T(8,128)(2,1)S(1)}, u32[]{:S(2)}) copy-start(bf16[3104,128]{1,0:T(8,128)(2,1)S(1)} %collective-permute-done.36.by_y.refs_4_) | copy-start | bytes 2383876
  120.3 12.9 %collective-permute-start.37 = (bf16[1552,128]{1,0:T(8,128)(2,1)S(1)}, bf16[1552,128]{1,0:T(8,128)(2,1)S(1)}, u32[]{:S(2)}, u32[]{:S(2)}) collective-permute-start(bf16[1552,128]{1,0:T(8,128)(2,1)S(1)} %get-tuple-element.59), channel_id=1, source_target_pairs={{0,4},{1,5},{2,6},{3,7},{4,0},{5,1},{6,2},{7,3},{8,12},{9,13},{10,... | collective-permute-start | bytes 1191944 | tf_op jit(solution)/shard_map/ppermute | solution.py:98
  121.5 13.5 %collective-permute-start.38 = (bf16[1552,128]{1,0:T(8,128)(2,1)S(1)}, bf16[1552,128]{1,0:T(8,128)(2,1)S(1)}, u32[]{:S(2)}, u32[]{:S(2)}) collective-permute-start(bf16[1552,128]{1,0:T(8,128)(2,1)S(1)} %get-tuple-element.60), channel_id=1, source_target_pairs={{0,8},{1,9},{2,10},{3,11},{4,12},{5,13},{6,14},{7,15},{8,0},{9,1},... | collective-permute-start | bytes 1191944 | tf_op jit(solution)/shard_map/ppermute | solution.py:98
  127.2 14.1 %collective-permute-start.34 = (bf16[784,128]{1,0:T(8,128)(2,1)S(1)}, bf16[784,128]{1,0:T(8,128)(2,1)S(1)}, u32[]{:S(2)}, u32[]{:S(2)}) collective-permute-start(bf16[784,128]{1,0:T(8,128)(2,1)S(1)} %get-tuple-element.58), channel_id=1, source_target_pairs={{0,8},{1,9},{2,10},{3,11},{4,12},{5,13},{6,14},{7,15},{8,0},{9,1},... | collective-permute-start | bytes 602120 | tf_op jit(solution)/shard_map/ppermute | solution.py:98
  128.1 13.2 %collective-permute-start.33 = (bf16[768,128]{1,0:T(8,128)(2,1)S(1)}, bf16[768,128]{1,0:T(8,128)(2,1)S(1)}, u32[]{:S(2)}, u32[]{:S(2)}) collective-permute-start(bf16[768,128]{1,0:T(8,128)(2,1)S(1)} %get-tuple-element.57), channel_id=1, source_target_pairs={{0,4},{1,5},{2,6},{3,7},{4,0},{5,1},{6,2},{7,3},{8,12},{9,13},{10,... | collective-permute-start | bytes 589832 | tf_op jit(solution)/shard_map/ppermute | solution.py:98
  129.9 11.4 %collective-permute-start.26 = (bf16[416,128]{1,0:T(8,128)(2,1)S(1)}, bf16[416,128]{1,0:T(8,128)(2,1)S(1)}, u32[]{:S(2)}, u32[]{:S(2)}) collective-permute-start(bf16[416,128]{1,0:T(8,128)(2,1)S(1)} %get-tuple-element.50), channel_id=1, source_target_pairs={{0,3},{1,0},{2,1},{3,2},{4,7},{5,4},{6,5},{7,6},{8,11},{9,8},{10,9... | collective-permute-start | bytes 319496 | tf_op jit(solution)/shard_map/ppermute | solution.py:98
  133.1 8.2 %collective-permute-start.25 = (bf16[416,128]{1,0:T(8,128)(2,1)S(1)}, bf16[416,128]{1,0:T(8,128)(2,1)S(1)}, u32[]{:S(2)}, u32[]{:S(2)}) collective-permute-start(bf16[416,128]{1,0:T(8,128)(2,1)S(1)} %get-tuple-element.49.refs_9_), channel_id=1, source_target_pairs={{0,1},{1,2},{2,3},{3,0},{4,5},{5,6},{6,7},{7,4},{8,9},{9,10},{10,1... | collective-permute-start | bytes 319496 | tf_op jit(solution)/shard_map/ppermute | solution.py:98

commit v19 on v18

--- a/solution.py
+++ b/solution.py
@@ -314,7 +314,7 @@
                 out[(2 - lev_at) * 9 + lat_by * 3 + lon_at] = block[lon_at * span : (lon_at + 1) * span]
 
 
-def code_kernel(pos, held, after, out, late):
+def code_kernel(pos, held, after, out):
     del pos, after
     taps, span, filters = held.shape
     most = jnp.abs(held[0])
@@ -325,16 +325,12 @@
     unit = jnp.broadcast_to(jnp.exp2(power), (16, filters)).astype(out.dtype).astype(jnp.float32)
     shrink = 1.0 / unit[0:1]
     unit = unit.astype(out.dtype)
-    skip = out.shape[0] - late.shape[0]
     for tap in range(taps):
         value = held[tap] * shrink
         square = value * value
         code = (square * value * jnp.abs(value)).astype(out.dtype)
         out[tap * span : (tap + 1) * span, :] = code
-        if tap * span >= skip:
-            late[tap * span - skip : (tap + 1) * span - skip, :] = code
     out[taps * span :, :] = unit
-    late[taps * span - skip :, :] = unit
 
 
 def both_kernel(pos, west, east, after1, after2, both, half_3, half_1):
@@ -358,21 +354,6 @@
     half = half_3.shape[0]
     late[0:half, :] = half_3[...]
     late[half:, :] = half_1[...]
-
-
-def block_kernel(pos, own, x, y, top, bottom, block):
-    del pos
-    rows = block.shape[0] // 4
-    for at, (piece, end) in enumerate(((own, own), (x, x), (y, y), (top, bottom))):
-        block[at * rows : (at + 1) * rows - 16, :] = piece[0 : rows - 16, :]
-        block[(at + 1) * rows - 16 : (at + 1) * rows, :] = end[end.shape[0] - 16 :, :]
-
-
-def hand_kernel(pos, block_3, block_1, first, second):
-    del pos
-    many = first.shape[0]
-    first[...] = block_3[0:many, :]
-    second[...] = block_1[many:, :]
 
 
 def unpack_kernel(pos, *refs, slabs, count, span):
@@ -573,12 +554,10 @@
         pair_kernel, [jax.ShapeDtypeStruct((2, cells, wide), bf16)], (pos, g2a, g2b, xs), [], 0, "pair", 16, held=1
     )
     s2 = move(g2, sibling)
-    early = 3
-    cut, end = early * span, 27 * span
-    size = end + 16 - cut
+    end = 27 * span
+    size = end + 16
     half = size // 32 * 16
-    first_rows = cut + 16
-    own_cut, late_cut = 14 * span, (27 - early) // 2 * span
+    cut = 14 * span
     slab = lambda count: jax.ShapeDtypeStruct((count, wide), bf16)
     (grads,) = call(
         taps_kernel,
@@ -589,7 +568,7 @@
         "taps",
         28,
     )
-    own, late = call(code_kernel, [slab(end + 16), slab(size)], (pos, grads, theirs), [], 0, "code", 16, held=1)
+    (own,) = call(code_kernel, [slab(size)], (pos, grads, theirs), [], 0, "code", 16, held=1)
 
     whole = lambda t: (0, 0, 0, 0)
     field = pl.pallas_call(
@@ -624,10 +603,10 @@
         )
         return move(top, lat_xor(1)), move(bottom, lat_xor(2))
 
-    from_3 = move(late, lon_by(1))
-    from_1 = move(late, lon_by(-1))
+    from_3 = move(own, lon_by(1))
+    from_1 = move(own, lon_by(-1))
     own_x, own_y = to_plane(own)
-    own_top, own_bottom = to_diagonal(own_x, own_y, own_cut, field, own, "cross_1")
+    own_top, own_bottom = to_diagonal(own_x, own_y, cut, field, own, "cross_1")
     pair, half_3, half_1 = call(
         both_kernel,
         [slab(2 * size), slab(half), slab(size - half)],
@@ -641,60 +620,28 @@
     half_3 = move(half_3, lon_by(1))
     half_1 = move(half_1, lon_by(-1))
     pair_x, pair_y = to_plane(pair)
-    (block,) = call(
-        block_kernel, [slab(4 * first_rows)], (pos, own, own_x, own_y, own_top, own_bottom), [], 0, "block", 16
-    )
-    early_3 = move(block, lon_by(1))
-    early_1 = move(block, lon_by(-1))
     (from_2,) = call(across_kernel, [slab(size)], (pos, half_3, half_1, pair), [], 0, "across", 16, held=1)
-    pair_top, pair_bottom = to_diagonal(pair_x, pair_y, size, early_1, early_3, "cross_2")
+    pair_top, pair_bottom = to_diagonal(pair_x, pair_y, size, pair, own, "cross_2")
     from_2x, from_2y = to_plane(from_2)
-    hand_3, hand_1 = call(hand_kernel, [slab(2 * first_rows)] * 2, (pos, early_3, early_1), [], 0, "hand", 16)
-    early_2a = move(hand_3, lon_by(1))
-    early_2b = move(hand_1, lon_by(-1))
-
-    def late_piece(which, row=0):
-        return ((which, row + size - 16), (0, which, row))
-
-    def early_piece(which, row):
-        return ((which, row + cut), (0, which, row))
-
-    pieces = [((which, end), (0, which, 0)) for which in range(3)]
-    pieces.append(((4, end - own_cut), (0, 3, 0), (own_cut // span, 4, 0)))
-    total, token = unpack(
-        pos, total, [own, own_x, own_y, own_top, own_bottom], [block], [(0, 0, 27, pieces)], span, "unpack_1"
-    )
-    from_2top, from_2bottom = to_diagonal(from_2x, from_2y, late_cut, token, pair, "cross_3")
+
+    def piece(which, row=0):
+        return ((which, row + end), (0, which, row))
+
+    def split_piece(top, bottom):
+        return ((bottom, end - cut), (0, top, 0), (cut // span, bottom, 0))
+
+    slabs = [(0, 0, 27, [piece(0), piece(1), piece(2), split_piece(3, 4)])]
+    total, token = unpack(pos, total, [own, own_x, own_y, own_top, own_bottom], [pair], slabs, span, "unpack_1")
+    from_2top, from_2bottom = to_diagonal(from_2x, from_2y, cut, token, pair, "cross_3")
     slabs = [
-        (3, early, 27 - early, [late_piece(0), late_piece(2), late_piece(3), late_piece(4)]),
-        (1, early, 27 - early, [late_piece(1), late_piece(2, size), late_piece(3, size), late_piece(5)]),
-        (3, 0, early, [early_piece(6, tag * first_rows) for tag in range(4)]),
-        (1, 0, early, [early_piece(7, tag * first_rows) for tag in range(4)]),
+        (3, 0, 27, [piece(0), piece(2), piece(3), piece(4)]),
+        (1, 0, 27, [piece(1), piece(2, size), piece(3, size), piece(5)]),
     ]
-    total, _ = unpack(
-        pos,
-        total,
-        [from_3, from_1, pair_x, pair_y, pair_top, pair_bottom, early_3, early_1],
-        [hand_3],
-        slabs,
-        span,
-        "unpack_2",
-    )
-    pieces = [late_piece(2), late_piece(3), late_piece(4)]
-    pieces.append(((6, size - 16 - late_cut), (0, 5, 0), (late_cut // span, 6, 0)))
-    slabs = [
-        (2, 0, early, [early_piece(tag // 2, tag % 2 * first_rows) for tag in range(4)]),
-        (2, early, 27 - early, pieces),
-    ]
-    total, _ = unpack(
-        pos,
-        total,
-        [early_2a, early_2b, from_2, from_2x, from_2y, from_2top, from_2bottom],
-        [],
-        slabs,
-        span,
-        "unpack_3",
-    )
+    sources = [from_3, from_1, pair_x, pair_y, pair_top, pair_bottom]
+    total, _ = unpack(pos, total, sources, [from_2], slabs, span, "unpack_2")
+    slabs = [(2, 0, 27, [piece(0), piece(1), piece(2), split_piece(3, 4)])]
+    sources = [from_2, from_2x, from_2y, from_2top, from_2bottom]
+    total, _ = unpack(pos, total, sources, [], slabs, span, "unpack_3")
     return (jnp.transpose(field, (3, 0, 1, 2)), jnp.transpose(total, (1, 0, 2)))
 
 

time: 146 us -> 150 us (1.027)
  waiting for transfers between devices: 45.7 us -> 57.9 us
  starting transfers between devices: 49.5 us -> 39.7 us
  local copies, waits for them, and re-layouts: 4 us -> 7 us
    ppermute x39 -> x35, waiting for transfers between devices: 45.7 us -> 57.9 us  [move(): return lax.ppermute(x, AXES, pairs)]
    ppermute x39 -> x35, starting transfers between devices: 49.5 us -> 39.7 us  [move(): return lax.ppermute(x, AXES, pairs)]
    unnamed x14, local copies, waits for them, and re-layouts: 4 us -> 7 us
    pallas_call x15 -> x13, Pallas kernels: 17.4 us -> 16.3 us  [call(): pl.pallas_call(kernel, out_shape=outs, in_specs=[pl.BlockSpec(memory_spac...]
  transfers between devices with their start and end apart: 39 -> 35, of which waited for: 14 -> 14; matrix products, arithmetic and copies ran while one was open for 0% -> 0% of each run, Pallas kernels for 26% -> 25%
where the time goes in v19:
time: 150 us
  waiting for transfers between devices  57.9 us (39%)
  Pallas kernels  44 us (29%)
  starting transfers between devices  39.7 us (26%)
  local copies, waits for them, and re-layouts  7 us (5%)
    ppermute x35, waiting for transfers between devices, move(): return lax.ppermute(x, AXES, pairs)  57.9 us
    ppermute x35, starting transfers between devices, move(): return lax.ppermute(x, AXES, pairs)  39.7 us
    pallas_call x13, Pallas kernels, call(): pl.pallas_call(kernel, out_shape=outs, in_specs=[pl.BlockSpec(memory_spac...  16.3 us
    pallas_call x3, Pallas kernels, unpack(): pl.pallas_call(lambda *refs: unpack_kernel(*refs, slabs=slabs, count=len(...  13.4 us
    pallas_call x1, Pallas kernels, blocked_body(): pl.pallas_call(field_kernel, out_shape=jax.ShapeDtypeStruct((levels, heig...  9.5 us
    unnamed x14, local copies, waits for them, and re-layouts  7 us
    pallas_call x1, Pallas kernels, blocked_body(): pl.pallas_call(lines_kernel, out_shape=[jax.ShapeDtypeStruct((levels, row...  4.87 us
  transfers between devices with their start and end apart: 35, of which 14 were waited for; matrix products, arithmetic and copies ran while one was open for 0% of the time, Pallas kernels for 25%

profile of v19, /device:TPU:0, one launch (start us, length us, event | category | flops | bytes accessed | tf_op | source)
XLA Modules:
  0.0 149.8 jit_solution(6236298549124096049)
XLA Ops:
  0.7 1.0 copy-done.2
  1.7 1.0 copy-done.4
  2.7 0.8 pack.1
  3.6 0.7 collective-permute-start.8
  4.2 3.0 %collective-permute-start.9 = (bf16[768,128]{1,0:T(8,128)(2,1)S(1)}, bf16[768,128]{1,0:T(8,128)(2,1)S(1)}, u32[]{:S(2)}, u32[]{:S(2)}) collective-permute-start(bf16[768,128]{1,0:T(8,128)(2,1)S(1)} %get-tuple-element.38), channel_id=1, source_target_pairs={{0,4},{1,5},{2,6},{3,7},{4,0},{5,1},{6,2},{7,3},{8,20},{9,21},{10,... | collective-permute-start | bytes 589832 | tf_op jit(solution)/shard_map/ppermute | solution.py:98
  7.2 1.6 %collective-permute-start = (bf16[416,128]{1,0:T(8,128)(2,1)S(1)}, bf16[416,128]{1,0:T(8,128)(2,1)S(1)}, u32[]{:S(2)}, u32[]{:S(2)}) collective-permute-start(bf16[416,128]{1,0:T(8,128)(2,1)S(1)} %get-tuple-element.30), channel_id=1, source_target_pairs={{0,1},{1,2},{2,3},{3,0},{4,5},{5,6},{6,7},{7,4},{8,9},{9,10},{10,1... | collective-permute-start | bytes 319496 | tf_op jit(solution)/shard_map/ppermute | solution.py:98
  8.8 2.2 %collective-permute-start.2 = (bf16[416,128]{1,0:T(8,128)(2,1)S(1)}, bf16[416,128]{1,0:T(8,128)(2,1)S(1)}, u32[]{:S(2)}, u32[]{:S(2)}) collective-permute-start(bf16[416,128]{1,0:T(8,128)(2,1)S(1)} %get-tuple-element.32), channel_id=1, source_target_pairs={{0,3},{1,0},{2,1},{3,2},{4,7},{5,4},{6,5},{7,6},{8,11},{9,8},{10,9... | collective-permute-start | bytes 319496 | tf_op jit(solution)/shard_map/ppermute | solution.py:98
  11.1 0.8 collective-permute-start.1
  11.9 9.2 %collective-permute-done.1.x2.after2 = bf16[384,128]{1,0:T(8,128)(2,1)S(1)} collective-permute-done((bf16[384,128]{1,0:T(8,128)(2,1)S(1)}, bf16[384,128]{1,0:T(8,128)(2,1)S(1)}, u32[]{:S(2)}, u32[]{:S(2)}) %collective-permute-start.1) | collective-permute-done | bytes 98336 | tf_op jit(solution)/shard_map/ppermute | solution.py:98
  21.7 2.3 %collective-permute-start.11 = (bf16[1616,128]{1,0:T(8,128)(2,1)S(1)}, bf16[1616,128]{1,0:T(8,128)(2,1)S(1)}, u32[]{:S(2)}, u32[]{:S(2)}) collective-permute-start(bf16[1616,128]{1,0:T(8,128)(2,1)S(1)} %pair_0.1.g0), channel_id=1, source_target_pairs={{0,3},{1,0},{2,1},{3,2},{4,7},{5,4},{6,5},{7,6},{8,11},{9,8},{10,9... | collective-permute-start | bytes 1241096 | tf_op jit(solution)/shard_map/ppermute | solution.py:98
  24.5 2.3 %collective-permute-start.4 = (bf16[384,128]{1,0:T(8,128)(2,1)S(1)}, bf16[384,128]{1,0:T(8,128)(2,1)S(1)}, u32[]{:S(2)}, u32[]{:S(2)}) collective-permute-start(bf16[384,128]{1,0:T(8,128)(2,1)S(1)} %get-tuple-element.34), channel_id=1, source_target_pairs={{0,12},{1,13},{2,14},{3,15},{4,8},{5,9},{6,10},{7,11},{8,4},{9,5},... | collective-permute-start | bytes 294920 | tf_op jit(solution)/shard_map/ppermute | solution.py:98
  26.8 2.7 %collective-permute-done.3.after1.by_x = bf16[384,128]{1,0:T(8,128)(2,1)S(1)} collective-permute-done((bf16[384,128]{1,0:T(8,128)(2,1)S(1)}, bf16[384,128]{1,0:T(8,128)(2,1)S(1)}, u32[]{:S(2)}, u32[]{:S(2)}) %collective-permute-start.3) | collective-permute-done | bytes 98336 | tf_op jit(solution)/shard_map/ppermute | solution.py:98
  29.5 1.2 collective-permute-done.4.after2.by_d
  31.4 1.7 %collective-permute-start.7 = (bf16[1600,128]{1,0:T(8,128)(2,1)S(1)}, bf16[1600,128]{1,0:T(8,128)(2,1)S(1)}, u32[]{:S(2)}, u32[]{:S(2)}) collective-permute-start(bf16[1600,128]{1,0:T(8,128)(2,1)S(1)} %get-tuple-element.35.x_own.own), channel_id=1, source_target_pairs={{0,12},{1,13},{2,14},{3,15},{4,8},{5,9},{6,10},{7,11},{8,4},{9,5},... | collective-permute-start | bytes 1228808 | tf_op jit(solution)/shard_map/ppermute | solution.py:98
  33.0 1.2 collective-permute-start.5
  34.2 0.7 collective-permute-start.6
  34.9 7.7 %collective-permute-done.10.west.g1 = bf16[1616,128]{1,0:T(8,128)(2,1)S(1)} collective-permute-done((bf16[1616,128]{1,0:T(8,128)(2,1)S(1)}, bf16[1616,128]{1,0:T(8,128)(2,1)S(1)}, u32[]{:S(2)}, u32[]{:S(2)}) %collective-permute-start.10) | collective-permute-done | bytes 413728 | tf_op jit(solution)/shard_map/ppermute | solution.py:98
  43.2 1.9 %collective-permute-start.16 = (bf16[768,128]{1,0:T(8,128)(2,1)S(1)}, bf16[768,128]{1,0:T(8,128)(2,1)S(1)}, u32[]{:S(2)}, u32[]{:S(2)}) collective-permute-start(bf16[768,128]{1,0:T(8,128)(2,1)S(1)} %get-tuple-element.41), channel_id=1, source_target_pairs={{0,3},{1,0},{2,1},{3,2},{4,7},{5,4},{6,5},{7,6},{8,11},{9,8},{10,9... | collective-permute-start | bytes 589832 | tf_op jit(solution)/shard_map/ppermute | solution.py:98
  45.3 4.9 %collective-permute-done.6.x_y = bf16[1536,128]{1,0:T(8,128)(2,1)S(1)} collective-permute-done((bf16[1536,128]{1,0:T(8,128)(2,1)S(1)}, bf16[1536,128]{1,0:T(8,128)(2,1)S(1)}, u32[]{:S(2)}, u32[]{:S(2)}) %collective-permute-start.6) | collective-permute-done | bytes 393248 | tf_op jit(solution)/shard_map/ppermute | solution.py:98
  51.0 4.9 %lines.1 = (bf16[4,18,192,256]{3,2,1,0:T(8,128)(2,1)S(1)}, f32[27,256,512]{2,1,0:T(8,128)}) custom-call(s32[3]{0:T(128)S(1)} %pad_add_fusion.pos.refs_0_, bf16[1600,128]{1,0:T(8,128)(2,1)S(1)} %get-tuple-element.35.x_own.own, bf16[1600,128]{1,0:T(8,128)(2,1)S(1)} %collective-permute-done.5.x_x, bf16[1536,128]{1,0:T(8,128)(2,1)S(1)} %collective-permute-done.6.x_y, ...), custom_call_target="tpu_custom_call" | custom-call | bytes 1048576 | tf_op jit(solution)/shard_map/lines/pallas_call | solution.py:528
  57.1 1.0 copy-done.3
  58.9 8.6 %taps.1.held = f32[27,64,128]{2,1,0:T(8,128)S(1)} custom-call(s32[3]{0:T(128)S(1)} %pad_add_fusion.pos.refs_0_, bf16[4,18,192,256]{3,2,1,0:T(8,128)(2,1)S(1)} %get-tuple-element.40.after.xs, bf16[1616,128]{1,0:T(8,128)(2,1)S(1)} %pair_0.1.g0, bf16[1616,128]{1,0:T(8,128)(2,1)S(1)} %collective-permute-done.10.west.g1, ...), custom_call_target="tpu_custom_call" | custom-call | flops 5435817984 | bytes 11231232 | tf_op jit(solution)/shard_map/taps/pallas_call | solution.py:116
  67.5 0.9 code.1.after.after2.refs_1_
  68.4 1.7 %collective-permute-start.22 = (bf16[1744,128]{1,0:T(8,128)(2,1)S(1)}, bf16[1744,128]{1,0:T(8,128)(2,1)S(1)}, u32[]{:S(2)}, u32[]{:S(2)}) collective-permute-start(bf16[1744,128]{1,0:T(8,128)(2,1)S(1)} %code.1.after.after2.refs_1_), channel_id=1, source_target_pairs={{0,8},{1,9},{2,10},{3,11},{4,12},{5,13},{6,14},{7,15},{8,0},{9,1},... | collective-permute-start | bytes 1339400 | tf_op jit(solution)/shard_map/ppermute | solution.py:98
  70.1 0.9 collective-permute-start.21
  71.0 3.1 %collective-permute-start.20 = (bf16[1744,128]{1,0:T(8,128)(2,1)S(1)}, bf16[1744,128]{1,0:T(8,128)(2,1)S(1)}, u32[]{:S(2)}, u32[]{:S(2)}) collective-permute-start(bf16[1744,128]{1,0:T(8,128)(2,1)S(1)} %code.1.after.after2.refs_1_), channel_id=1, source_target_pairs={{0,3},{1,0},{2,1},{3,2},{4,7},{5,4},{6,5},{7,6},{8,11},{9,8},{10,9... | collective-permute-start | bytes 1339400 | tf_op jit(solution)/shard_map/ppermute | solution.py:98
  74.1 3.0 %copy-done.6 = bf16[256,27,512]{2,0,1:T(8,128)(2,1)S(1)} copy-done((bf16[256,27,512]{2,0,1:T(8,128)(2,1)S(1)}, bf16[256,27,512]{2,0,1:T(8,128)(2,1)}, u32[]{:S(2)}) %copy-start.6) | copy-done | bytes 7077912
  77.2 9.5 %field.1.after1 = bf16[4,4,48,256]{3,2,1,0:T(8,128)(2,1)} custom-call(s32[3]{0:T(128)S(1)} %pad_add_fusion.pos.refs_0_, bf16[1744,128]{1,0:T(8,128)(2,1)S(1)} %code.1.after.after2.refs_1_, bf16[4,6,64,256]{3,2,1,0:T(8,128)(2,1)S(1)} %mine.1, bf16[4,6,64,256]{3,2,1,0:T(8,128)(2,1)S(1)} %collective-permute-done.18.after.theirs, bf16[27,256,512]{2,1,0:T(8,128)(2,1)S(1)} %bitcast.12), custom_call_target="tpu_custom_call" | custom-call | flops 10871635968 | bytes 7077888 | tf_op jit(solution)/shard_map/field/pallas_call | solution.py:574
  86.7 1.0 copy-done.5
  88.2 1.5 %collective-permute-start.23 = (bf16[896,128]{1,0:T(8,128)(2,1)S(1)}, bf16[896,128]{1,0:T(8,128)(2,1)S(1)}, u32[]{:S(2)}, u32[]{:S(2)}) collective-permute-start(bf16[896,128]{1,0:T(8,128)(2,1)S(1)} %get-tuple-element.42), channel_id=1, source_target_pairs={{0,4},{1,5},{2,6},{3,7},{4,0},{5,1},{6,2},{7,3},{8,12},{9,13},{10,... | collective-permute-start | bytes 688136 | tf_op jit(solution)/shard_map/ppermute | solution.py:98
  89.8 0.8 collective-permute-start.24
  90.5 3.5 %collective-permute-done.19.west.refs_1_ = bf16[1744,128]{1,0:T(8,128)(2,1)S(1)} collective-permute-done((bf16[1744,128]{1,0:T(8,128)(2,1)S(1)}, bf16[1744,128]{1,0:T(8,128)(2,1)S(1)}, u32[]{:S(2)}, u32[]{:S(2)}) %collective-permute-start.19) | collective-permute-done | bytes 446496 | tf_op jit(solution)/shard_map/ppermute | solution.py:98
  94.0 2.3 %collective-permute-done.24.after2.refs_5_ = bf16[848,128]{1,0:T(8,128)(2,1)S(1)} collective-permute-done((bf16[848,128]{1,0:T(8,128)(2,1)S(1)}, bf16[848,128]{1,0:T(8,128)(2,1)S(1)}, u32[]{:S(2)}, u32[]{:S(2)}) %collective-permute-start.24) | collective-permute-done | bytes 217120 | tf_op jit(solution)/shard_map/ppermute | solution.py:98
  97.0 0.8 collective-permute-start.32
  97.8 1.2 collective-permute-start.31
  99.1 3.5 %collective-permute-start.26 = (bf16[880,128]{1,0:T(8,128)(2,1)S(1)}, bf16[880,128]{1,0:T(8,128)(2,1)S(1)}, u32[]{:S(2)}, u32[]{:S(2)}) collective-permute-start(bf16[880,128]{1,0:T(8,128)(2,1)S(1)} %get-tuple-element.45), channel_id=1, source_target_pairs={{0,3},{1,0},{2,1},{3,2},{4,7},{5,4},{6,5},{7,6},{8,11},{9,8},{10,9... | collective-permute-start | bytes 675848 | tf_op jit(solution)/shard_map/ppermute | solution.py:98
  102.6 8.7 %collective-permute-done.25.half_3 = bf16[864,128]{1,0:T(8,128)(2,1)S(1)} collective-permute-done((bf16[864,128]{1,0:T(8,128)(2,1)S(1)}, bf16[864,128]{1,0:T(8,128)(2,1)S(1)}, u32[]{:S(2)}, u32[]{:S(2)}) %collective-permute-start.25) | collective-permute-done | bytes 221216 | tf_op jit(solution)/shard_map/ppermute | solution.py:98
  112.6 1.5 collective-permute-start.27
  114.0 5.8 %collective-permute-done.32.by_y.refs_4_ = bf16[3488,128]{1,0:T(8,128)(2,1)S(1)} collective-permute-done((bf16[3488,128]{1,0:T(8,128)(2,1)S(1)}, bf16[3488,128]{1,0:T(8,128)(2,1)S(1)}, u32[]{:S(2)}, u32[]{:S(2)}) %collective-permute-start.32) | collective-permute-done | bytes 892960 | tf_op jit(solution)/shard_map/ppermute | solution.py:98
  119.8 0.8 collective-permute-done.31.by_x.refs_3_
  121.2 1.3 collective-permute-start.33
  123.1 3.1 %unpack_1.1 = (f32[27,256,512]{2,1,0:T(8,128)}, f32[8,128]{1,0:T(8,128)S(1)}) custom-call(s32[3]{0:T(128)S(1)} %pad_add_fusion.pos.refs_0_, bf16[1744,128]{1,0:T(8,128)(2,1)S(1)} %code.1.after.after2.refs_1_, bf16[1744,128]{1,0:T(8,128)(2,1)S(1)} %collective-permute-done.21.by_x.refs_2_, ...), custom_call_target="tpu_custom_call", output_to_operand_aliasing={{0}: (7, {})} | custom-call | bytes 4194304 | tf_op jit(solution)/shard_map/unpack_1/pallas_call | solution.py:401
  126.2 3.2 %collective-permute-done.28.by_y.refs_3_ = bf16[1744,128]{1,0:T(8,128)(2,1)S(1)} collective-permute-done((bf16[1744,128]{1,0:T(8,128)(2,1)S(1)}, bf16[1744,128]{1,0:T(8,128)(2,1)S(1)}, u32[]{:S(2)}, u32[]{:S(2)}) %collective-permute-start.28) | collective-permute-done | bytes 446496 | tf_op jit(solution)/shard_map/ppermute | solution.py:98
  129.4 0.8 collective-permute-done.27.by_x.refs_2_
  130.8 1.3 collective-permute-start.29
  132.6 6.7 %collective-permute-done.33.refs_5_ = bf16[1744,128]{1,0:T(8,128)(2,1)S(1)} collective-permute-done((bf16[1744,128]{1,0:T(8,128)(2,1)S(1)}, bf16[1744,128]{1,0:T(8,128)(2,1)S(1)}, u32[]{:S(2)}, u32[]{:S(2)}) %collective-permute-start.33) | collective-permute-done | bytes 446496 | tf_op jit(solution)/shard_map/ppermute | solution.py:98
  139.4 6.5 %unpack_2.1 = (f32[27,256,512]{2,1,0:T(8,128)}, f32[8,128]{1,0:T(8,128)}) custom-call(s32[3]{0:T(128)S(1)} %pad_add_fusion.pos.refs_0_, bf16[1744,128]{1,0:T(8,128)(2,1)S(1)} %collective-permute-done.19.west.refs_1_, bf16[1744,128]{1,0:T(8,128)(2,1)S(1)} %collective-permute-done.20.east.refs_2_, ...), custom_call_target="tpu_custom_call", output_to_operand_aliasing={{0}: (8, {})} | custom-call | bytes 4194304 | tf_op jit(solution)/shard_map/unpack_2/pallas_call | solution.py:401
  145.9 3.7 %unpack_3.1 = (f32[27,256,512]{2,1,0:T(8,128)}, f32[8,128]{1,0:T(8,128)}) custom-call(s32[3]{0:T(128)S(1)} %pad_add_fusion.pos.refs_0_, bf16[1744,128]{1,0:T(8,128)(2,1)S(1)} %across.1.refs_7_.refs_1_, bf16[1744,128]{1,0:T(8,128)(2,1)S(1)} %collective-permute-done.27.by_x.refs_2_, ...), custom_call_target="tpu_custom_call", output_to_operand_aliasing={{0}: (6, {})} | custom-call | bytes 4194304 | tf_op jit(solution)/shard_map/unpack_3/pallas_call | solution.py:401
  (55 shorter events, 10.3 us)
Async XLA Ops:
  0.7 1.0 copy-start.2
  1.7 1.0 copy-start.4
  3.6 17.5 %collective-permute-start.8 = (bf16[768,128]{1,0:T(8,128)(2,1)S(1)}, bf16[768,128]{1,0:T(8,128)(2,1)S(1)}, u32[]{:S(2)}, u32[]{:S(2)}) collective-permute-start(bf16[768,128]{1,0:T(8,128)(2,1)S(1)} %get-tuple-element.37), channel_id=1, source_target_pairs={{0,0},{1,1},{2,2},{3,3},{4,4},{5,5},{6,6},{7,7},{8,16},{9,17},{10,... | collective-permute-start | bytes 589832 | tf_op jit(solution)/shard_map/ppermute | solution.py:98
  4.2 16.8 %collective-permute-start.9 = (bf16[768,128]{1,0:T(8,128)(2,1)S(1)}, bf16[768,128]{1,0:T(8,128)(2,1)S(1)}, u32[]{:S(2)}, u32[]{:S(2)}) collective-permute-start(bf16[768,128]{1,0:T(8,128)(2,1)S(1)} %get-tuple-element.38), channel_id=1, source_target_pairs={{0,4},{1,5},{2,6},{3,7},{4,0},{5,1},{6,2},{7,3},{8,20},{9,21},{10,... | collective-permute-start | bytes 589832 | tf_op jit(solution)/shard_map/ppermute | solution.py:98
  7.2 13.8 %collective-permute-start = (bf16[416,128]{1,0:T(8,128)(2,1)S(1)}, bf16[416,128]{1,0:T(8,128)(2,1)S(1)}, u32[]{:S(2)}, u32[]{:S(2)}) collective-permute-start(bf16[416,128]{1,0:T(8,128)(2,1)S(1)} %get-tuple-element.30), channel_id=1, source_target_pairs={{0,1},{1,2},{2,3},{3,0},{4,5},{5,6},{6,7},{7,4},{8,9},{9,10},{10,1... | collective-permute-start | bytes 319496 | tf_op jit(solution)/shard_map/ppermute | solution.py:98
  8.8 12.2 %collective-permute-start.2 = (bf16[416,128]{1,0:T(8,128)(2,1)S(1)}, bf16[416,128]{1,0:T(8,128)(2,1)S(1)}, u32[]{:S(2)}, u32[]{:S(2)}) collective-permute-start(bf16[416,128]{1,0:T(8,128)(2,1)S(1)} %get-tuple-element.32), channel_id=1, source_target_pairs={{0,3},{1,0},{2,1},{3,2},{4,7},{5,4},{6,5},{7,6},{8,11},{9,8},{10,9... | collective-permute-start | bytes 319496 | tf_op jit(solution)/shard_map/ppermute | solution.py:98
  11.1 10.0 %collective-permute-start.1 = (bf16[384,128]{1,0:T(8,128)(2,1)S(1)}, bf16[384,128]{1,0:T(8,128)(2,1)S(1)}, u32[]{:S(2)}, u32[]{:S(2)}) collective-permute-start(bf16[384,128]{1,0:T(8,128)(2,1)S(1)} %get-tuple-element.31), channel_id=1, source_target_pairs={{0,2},{1,3},{2,0},{3,1},{4,6},{5,7},{6,4},{7,5},{8,10},{9,11},{10,... | collective-permute-start | bytes 294920 | tf_op jit(solution)/shard_map/ppermute | solution.py:98
  21.7 13.3 %collective-permute-start.11 = (bf16[1616,128]{1,0:T(8,128)(2,1)S(1)}, bf16[1616,128]{1,0:T(8,128)(2,1)S(1)}, u32[]{:S(2)}, u32[]{:S(2)}) collective-permute-start(bf16[1616,128]{1,0:T(8,128)(2,1)S(1)} %pair_0.1.g0), channel_id=1, source_target_pairs={{0,3},{1,0},{2,1},{3,2},{4,7},{5,4},{6,5},{7,6},{8,11},{9,8},{10,9... | collective-permute-start | bytes 1241096 | tf_op jit(solution)/shard_map/ppermute | solution.py:98
  23.9 18.7 %collective-permute-start.10 = (bf16[1616,128]{1,0:T(8,128)(2,1)S(1)}, bf16[1616,128]{1,0:T(8,128)(2,1)S(1)}, u32[]{:S(2)}, u32[]{:S(2)}) collective-permute-start(bf16[1616,128]{1,0:T(8,128)(2,1)S(1)} %pair_0.1.g0), channel_id=1, source_target_pairs={{0,1},{1,2},{2,3},{3,0},{4,5},{5,6},{6,7},{7,4},{8,9},{9,10},{10,1... | collective-permute-start | bytes 1241096 | tf_op jit(solution)/shard_map/ppermute | solution.py:98
  23.9 5.6 %collective-permute-start.3 = (bf16[384,128]{1,0:T(8,128)(2,1)S(1)}, bf16[384,128]{1,0:T(8,128)(2,1)S(1)}, u32[]{:S(2)}, u32[]{:S(2)}) collective-permute-start(bf16[384,128]{1,0:T(8,128)(2,1)S(1)} %get-tuple-element.33), channel_id=1, source_target_pairs={{0,4},{1,5},{2,6},{3,7},{4,0},{5,1},{6,2},{7,3},{8,12},{9,13},{10,... | collective-permute-start | bytes 294920 | tf_op jit(solution)/shard_map/ppermute | solution.py:98
  24.5 6.2 %collective-permute-start.4 = (bf16[384,128]{1,0:T(8,128)(2,1)S(1)}, bf16[384,128]{1,0:T(8,128)(2,1)S(1)}, u32[]{:S(2)}, u32[]{:S(2)}) collective-permute-start(bf16[384,128]{1,0:T(8,128)(2,1)S(1)} %get-tuple-element.34), channel_id=1, source_target_pairs={{0,12},{1,13},{2,14},{3,15},{4,8},{5,9},{6,10},{7,11},{8,4},{9,5},... | collective-permute-start | bytes 294920 | tf_op jit(solution)/shard_map/ppermute | solution.py:98
  31.4 18.8 %collective-permute-start.7 = (bf16[1600,128]{1,0:T(8,128)(2,1)S(1)}, bf16[1600,128]{1,0:T(8,128)(2,1)S(1)}, u32[]{:S(2)}, u32[]{:S(2)}) collective-permute-start(bf16[1600,128]{1,0:T(8,128)(2,1)S(1)} %get-tuple-element.35.x_own.own), channel_id=1, source_target_pairs={{0,12},{1,13},{2,14},{3,15},{4,8},{5,9},{6,10},{7,11},{8,4},{9,5},... | collective-permute-start | bytes 1228808 | tf_op jit(solution)/shard_map/ppermute | solution.py:98
  33.0 18.0 %collective-permute-start.5 = (bf16[1600,128]{1,0:T(8,128)(2,1)S(1)}, bf16[1600,128]{1,0:T(8,128)(2,1)S(1)}, u32[]{:S(2)}, u32[]{:S(2)}) collective-permute-start(bf16[1600,128]{1,0:T(8,128)(2,1)S(1)} %get-tuple-element.35.x_own.own), channel_id=1, source_target_pairs={{0,4},{1,5},{2,6},{3,7},{4,0},{5,1},{6,2},{7,3},{8,12},{9,13},{10,... | collective-permute-start | bytes 1228808 | tf_op jit(solution)/shard_map/ppermute | solution.py:98
  34.2 15.9 %collective-permute-start.6 = (bf16[1536,128]{1,0:T(8,128)(2,1)S(1)}, bf16[1536,128]{1,0:T(8,128)(2,1)S(1)}, u32[]{:S(2)}, u32[]{:S(2)}) collective-permute-start(bf16[1536,128]{1,0:T(8,128)(2,1)S(1)} %get-tuple-element.36), channel_id=1, source_target_pairs={{0,8},{1,9},{2,10},{3,11},{4,12},{5,13},{6,14},{7,15},{8,0},{9,1},... | collective-permute-start | bytes 1179656 | tf_op jit(solution)/shard_map/ppermute | solution.py:98
  43.2 12.7 %collective-permute-start.16 = (bf16[768,128]{1,0:T(8,128)(2,1)S(1)}, bf16[768,128]{1,0:T(8,128)(2,1)S(1)}, u32[]{:S(2)}, u32[]{:S(2)}) collective-permute-start(bf16[768,128]{1,0:T(8,128)(2,1)S(1)} %get-tuple-element.41), channel_id=1, source_target_pairs={{0,3},{1,0},{2,1},{3,2},{4,7},{5,4},{6,5},{7,6},{8,11},{9,8},{10,9... | collective-permute-start | bytes 589832 | tf_op jit(solution)/shard_map/ppermute | solution.py:98
  45.1 10.9 %collective-permute-start.15 = (bf16[768,128]{1,0:T(8,128)(2,1)S(1)}, bf16[768,128]{1,0:T(8,128)(2,1)S(1)}, u32[]{:S(2)}, u32[]{:S(2)}) collective-permute-start(bf16[768,128]{1,0:T(8,128)(2,1)S(1)} %get-tuple-element.39.after), channel_id=1, source_target_pairs={{0,1},{1,2},{2,3},{3,0},{4,5},{5,6},{6,7},{7,4},{8,9},{9,10},{10,1... | collective-permute-start | bytes 589832 | tf_op jit(solution)/shard_map/ppermute | solution.py:98
  50.1 8.7 %collective-permute-start.12 = (bf16[1616,128]{1,0:T(8,128)(2,1)S(1)}, bf16[1616,128]{1,0:T(8,128)(2,1)S(1)}, u32[]{:S(2)}, u32[]{:S(2)}) collective-permute-start(bf16[1616,128]{1,0:T(8,128)(2,1)S(1)} %pair_0.1.g0), channel_id=1, source_target_pairs={{0,16},{1,17},{2,18},{3,19},{4,20},{5,21},{6,22},{7,23},{8,24},{9,... | collective-permute-start | bytes 1241096 | tf_op jit(solution)/shard_map/ppermute | solution.py:98
  50.1 8.7 %collective-permute-start.14 = (bf16[1616,128]{1,0:T(8,128)(2,1)S(1)}, bf16[1616,128]{1,0:T(8,128)(2,1)S(1)}, u32[]{:S(2)}, u32[]{:S(2)}) collective-permute-start(bf16[1616,128]{1,0:T(8,128)(2,1)S(1)} %collective-permute-done.11.east.g3), channel_id=1, source_target_pairs={{0,16},{1,17},{2,18},{3,19},{4,20},{5,21},{6,22},{7,23},{8,24},{9,... | collective-permute-start | bytes 1241096 | tf_op jit(solution)/shard_map/ppermute | solution.py:98
  51.0 7.8 %collective-permute-start.13 = (bf16[1616,128]{1,0:T(8,128)(2,1)S(1)}, bf16[1616,128]{1,0:T(8,128)(2,1)S(1)}, u32[]{:S(2)}, u32[]{:S(2)}) collective-permute-start(bf16[1616,128]{1,0:T(8,128)(2,1)S(1)} %collective-permute-done.10.west.g1), channel_id=1, source_target_pairs={{0,16},{1,17},{2,18},{3,19},{4,20},{5,21},{6,22},{7,23},{8,24},{9,... | collective-permute-start | bytes 1241096 | tf_op jit(solution)/shard_map/ppermute | solution.py:98
  56.5 2.4 %collective-permute-start.17 = (bf16[2,768,128]{2,1,0:T(8,128)(2,1)S(1)}, bf16[2,768,128]{2,1,0:T(8,128)(2,1)S(1)}, u32[]{:S(2)}, u32[]{:S(2)}) collective-permute-start(bf16[2,768,128]{2,1,0:T(8,128)(2,1)S(1)} %pair.1.g2), channel_id=1, source_target_pairs={{0,16},{1,17},{2,18},{3,19},{4,20},{5,21},{6,22},{7,23},{8,24},{9,... | collective-permute-start | bytes 1179656 | tf_op jit(solution)/shard_map/ppermute | solution.py:98
  57.1 1.0 copy-start.3
  58.8 8.7 %collective-permute-start.18 = (bf16[4,6,64,256]{3,2,1,0:T(8,128)(2,1)S(1)}, bf16[4,6,64,256]{3,2,1,0:T(8,128)(2,1)S(1)}, u32[]{:S(2)}, u32[]{:S(2)}) collective-permute-start(bf16[4,6,64,256]{3,2,1,0:T(8,128)(2,1)S(1)} %mine.1), channel_id=1, source_target_pairs={{0,16},{1,17},{2,18},{3,19},{4,20},{5,21},{6,22},{7,23},{8,24},{9,... | collective-permute-start | bytes 2359304 | tf_op jit(solution)/shard_map/ppermute | solution.py:98
  68.4 18.3 %collective-permute-start.22 = (bf16[1744,128]{1,0:T(8,128)(2,1)S(1)}, bf16[1744,128]{1,0:T(8,128)(2,1)S(1)}, u32[]{:S(2)}, u32[]{:S(2)}) collective-permute-start(bf16[1744,128]{1,0:T(8,128)(2,1)S(1)} %code.1.after.after2.refs_1_), channel_id=1, source_target_pairs={{0,8},{1,9},{2,10},{3,11},{4,12},{5,13},{6,14},{7,15},{8,0},{9,1},... | collective-permute-start | bytes 1339400 | tf_op jit(solution)/shard_map/ppermute | solution.py:98
  70.1 16.6 %collective-permute-start.21 = (bf16[1744,128]{1,0:T(8,128)(2,1)S(1)}, bf16[1744,128]{1,0:T(8,128)(2,1)S(1)}, u32[]{:S(2)}, u32[]{:S(2)}) collective-permute-start(bf16[1744,128]{1,0:T(8,128)(2,1)S(1)} %code.1.after.after2.refs_1_), channel_id=1, source_target_pairs={{0,4},{1,5},{2,6},{3,7},{4,0},{5,1},{6,2},{7,3},{8,12},{9,13},{10,... | collective-permute-start | bytes 1339400 | tf_op jit(solution)/shard_map/ppermute | solution.py:98
  71.0 19.6 %collective-permute-start.20 = (bf16[1744,128]{1,0:T(8,128)(2,1)S(1)}, bf16[1744,128]{1,0:T(8,128)(2,1)S(1)}, u32[]{:S(2)}, u32[]{:S(2)}) collective-permute-start(bf16[1744,128]{1,0:T(8,128)(2,1)S(1)} %code.1.after.after2.refs_1_), channel_id=1, source_target_pairs={{0,3},{1,0},{2,1},{3,2},{4,7},{5,4},{6,5},{7,6},{8,11},{9,8},{10,9... | collective-permute-start | bytes 1339400 | tf_op jit(solution)/shard_map/ppermute | solution.py:98
  74.1 19.9 %collective-permute-start.19 = (bf16[1744,128]{1,0:T(8,128)(2,1)S(1)}, bf16[1744,128]{1,0:T(8,128)(2,1)S(1)}, u32[]{:S(2)}, u32[]{:S(2)}) collective-permute-start(bf16[1744,128]{1,0:T(8,128)(2,1)S(1)} %code.1.after.after2.refs_1_), channel_id=1, source_target_pairs={{0,1},{1,2},{2,3},{3,0},{4,5},{5,6},{6,7},{7,4},{8,9},{9,10},{10,1... | collective-permute-start | bytes 1339400 | tf_op jit(solution)/shard_map/ppermute | solution.py:98
  74.1 3.0 %copy-start.6 = (bf16[256,27,512]{2,0,1:T(8,128)(2,1)S(1)}, bf16[256,27,512]{2,0,1:T(8,128)(2,1)}, u32[]{:S(2)}) copy-start(bf16[256,27,512]{2,0,1:T(8,128)(2,1)} %param.4) | copy-start | bytes 21233668
  86.7 1.0 copy-start.5
  88.2 8.1 %collective-permute-start.23 = (bf16[896,128]{1,0:T(8,128)(2,1)S(1)}, bf16[896,128]{1,0:T(8,128)(2,1)S(1)}, u32[]{:S(2)}, u32[]{:S(2)}) collective-permute-start(bf16[896,128]{1,0:T(8,128)(2,1)S(1)} %get-tuple-element.42), channel_id=1, source_target_pairs={{0,4},{1,5},{2,6},{3,7},{4,0},{5,1},{6,2},{7,3},{8,12},{9,13},{10,... | collective-permute-start | bytes 688136 | tf_op jit(solution)/shard_map/ppermute | solution.py:98
  89.8 6.6 %collective-permute-start.24 = (bf16[848,128]{1,0:T(8,128)(2,1)S(1)}, bf16[848,128]{1,0:T(8,128)(2,1)S(1)}, u32[]{:S(2)}, u32[]{:S(2)}) collective-permute-start(bf16[848,128]{1,0:T(8,128)(2,1)S(1)} %get-tuple-element.43), channel_id=1, source_target_pairs={{0,8},{1,9},{2,10},{3,11},{4,12},{5,13},{6,14},{7,15},{8,0},{9,1},... | collective-permute-start | bytes 651272 | tf_op jit(solution)/shard_map/ppermute | solution.py:98
  97.0 22.8 %collective-permute-start.32 = (bf16[3488,128]{1,0:T(8,128)(2,1)S(1)}, bf16[3488,128]{1,0:T(8,128)(2,1)S(1)}, u32[]{:S(2)}, u32[]{:S(2)}) collective-permute-start(bf16[3488,128]{1,0:T(8,128)(2,1)S(1)} %get-tuple-element.46.after.refs_6_.after2.after1), channel_id=1, source_target_pairs={{0,8},{1,9},{2,10},{3,11},{4,12},{5,13},{6,14},{7,15},{8,0},{9,1},... | collective-permute-start | bytes 2678792 | tf_op jit(solution)/shard_map/ppermute | solution.py:98
  97.8 22.8 %collective-permute-start.31 = (bf16[3488,128]{1,0:T(8,128)(2,1)S(1)}, bf16[3488,128]{1,0:T(8,128)(2,1)S(1)}, u32[]{:S(2)}, u32[]{:S(2)}) collective-permute-start(bf16[3488,128]{1,0:T(8,128)(2,1)S(1)} %get-tuple-element.46.after.refs_6_.after2.after1), channel_id=1, source_target_pairs={{0,4},{1,5},{2,6},{3,7},{4,0},{5,1},{6,2},{7,3},{8,12},{9,13},{10,... | collective-permute-start | bytes 2678792 | tf_op jit(solution)/shard_map/ppermute | solution.py:98
  99.1 12.2 %collective-permute-start.26 = (bf16[880,128]{1,0:T(8,128)(2,1)S(1)}, bf16[880,128]{1,0:T(8,128)(2,1)S(1)}, u32[]{:S(2)}, u32[]{:S(2)}) collective-permute-start(bf16[880,128]{1,0:T(8,128)(2,1)S(1)} %get-tuple-element.45), channel_id=1, source_target_pairs={{0,3},{1,0},{2,1},{3,2},{4,7},{5,4},{6,5},{7,6},{8,11},{9,8},{10,9... | collective-permute-start | bytes 675848 | tf_op jit(solution)/shard_map/ppermute | solution.py:98
  102.6 8.7 %collective-permute-start.25 = (bf16[864,128]{1,0:T(8,128)(2,1)S(1)}, bf16[864,128]{1,0:T(8,128)(2,1)S(1)}, u32[]{:S(2)}, u32[]{:S(2)}) collective-permute-start(bf16[864,128]{1,0:T(8,128)(2,1)S(1)} %get-tuple-element.44), channel_id=1, source_target_pairs={{0,1},{1,2},{2,3},{3,0},{4,5},{5,6},{6,7},{7,4},{8,9},{9,10},{10,1... | collective-permute-start | bytes 663560 | tf_op jit(solution)/shard_map/ppermute | solution.py:98
  111.9 17.5 %collective-permute-start.28 = (bf16[1744,128]{1,0:T(8,128)(2,1)S(1)}, bf16[1744,128]{1,0:T(8,128)(2,1)S(1)}, u32[]{:S(2)}, u32[]{:S(2)}) collective-permute-start(bf16[1744,128]{1,0:T(8,128)(2,1)S(1)} %across.1.refs_7_.refs_1_), channel_id=1, source_target_pairs={{0,8},{1,9},{2,10},{3,11},{4,12},{5,13},{6,14},{7,15},{8,0},{9,1},... | collective-permute-start | bytes 1339400 | tf_op jit(solution)/shard_map/ppermute | solution.py:98
  112.6 17.6 %collective-permute-start.27 = (bf16[1744,128]{1,0:T(8,128)(2,1)S(1)}, bf16[1744,128]{1,0:T(8,128)(2,1)S(1)}, u32[]{:S(2)}, u32[]{:S(2)}) collective-permute-start(bf16[1744,128]{1,0:T(8,128)(2,1)S(1)} %across.1.refs_7_.refs_1_), channel_id=1, source_target_pairs={{0,4},{1,5},{2,6},{3,7},{4,0},{5,1},{6,2},{7,3},{8,12},{9,13},{10,... | collective-permute-start | bytes 1339400 | tf_op jit(solution)/shard_map/ppermute | solution.py:98
  119.8 19.5 %copy-start = (bf16[3488,128]{1,0:T(8,128)(2,1)}, bf16[3488,128]{1,0:T(8,128)(2,1)S(1)}, u32[]{:S(2)}) copy-start(bf16[3488,128]{1,0:T(8,128)(2,1)S(1)} %collective-permute-done.32.by_y.refs_4_) | copy-start | bytes 2678788
  120.6 18.7 %copy-start.1 = (bf16[3488,128]{1,0:T(8,128)(2,1)}, bf16[3488,128]{1,0:T(8,128)(2,1)S(1)}, u32[]{:S(2)}) copy-start(bf16[3488,128]{1,0:T(8,128)(2,1)S(1)} %collective-permute-done.31.by_x.refs_3_) | copy-start | bytes 2678788
  121.2 18.1 %collective-permute-start.33 = (bf16[1744,128]{1,0:T(8,128)(2,1)S(1)}, bf16[1744,128]{1,0:T(8,128)(2,1)S(1)}, u32[]{:S(2)}, u32[]{:S(2)}) collective-permute-start(bf16[1744,128]{1,0:T(8,128)(2,1)S(1)} %get-tuple-element.51), channel_id=1, source_target_pairs={{0,4},{1,5},{2,6},{3,7},{4,0},{5,1},{6,2},{7,3},{8,12},{9,13},{10,... | collective-permute-start | bytes 1339400 | tf_op jit(solution)/shard_map/ppermute | solution.py:98
  122.5 16.8 %collective-permute-start.34 = (bf16[1744,128]{1,0:T(8,128)(2,1)S(1)}, bf16[1744,128]{1,0:T(8,128)(2,1)S(1)}, u32[]{:S(2)}, u32[]{:S(2)}) collective-permute-start(bf16[1744,128]{1,0:T(8,128)(2,1)S(1)} %get-tuple-element.52), channel_id=1, source_target_pairs={{0,8},{1,9},{2,10},{3,11},{4,12},{5,13},{6,14},{7,15},{8,0},{9,1},... | collective-permute-start | bytes 1339400 | tf_op jit(solution)/shard_map/ppermute | solution.py:98
  130.8 15.1 %collective-permute-start.29 = (bf16[896,128]{1,0:T(8,128)(2,1)S(1)}, bf16[896,128]{1,0:T(8,128)(2,1)S(1)}, u32[]{:S(2)}, u32[]{:S(2)}) collective-permute-start(bf16[896,128]{1,0:T(8,128)(2,1)S(1)} %get-tuple-element.49), channel_id=1, source_target_pairs={{0,4},{1,5},{2,6},{3,7},{4,0},{5,1},{6,2},{7,3},{8,12},{9,13},{10,... | collective-permute-start | bytes 688136 | tf_op jit(solution)/shard_map/ppermute | solution.py:98
  132.1 13.8 %collective-permute-start.30 = (bf16[848,128]{1,0:T(8,128)(2,1)S(1)}, bf16[848,128]{1,0:T(8,128)(2,1)S(1)}, u32[]{:S(2)}, u32[]{:S(2)}) collective-permute-start(bf16[848,128]{1,0:T(8,128)(2,1)S(1)} %get-tuple-element.50), channel_id=1, source_target_pairs={{0,8},{1,9},{2,10},{3,11},{4,12},{5,13},{6,14},{7,15},{8,0},{9,1},... | collective-permute-start | bytes 651272 | tf_op jit(solution)/shard_map/ppermute | solution.py:98

commit v20 on v18

--- a/solution.py
+++ b/solution.py
@@ -337,8 +337,8 @@
     late[taps * span - skip :, :] = unit
 
 
-def both_kernel(pos, west, east, after1, after2, both, half_3, half_1):
-    del pos, after1, after2
+def both_kernel(pos, west, east, after1, after2, after3, both, half_3, half_1):
+    del pos, after1, after2, after3
     size, half = west.shape[0], half_3.shape[0]
     both[0:size, :] = west[...]
     both[size:, :] = east[...]
@@ -432,13 +432,15 @@
     )(*ins)
 
 
-def field_kernel(pos, after, mine, theirs, w, out, copies, acc):
+def field_kernel(pos, after, mine, theirs, w, *refs, first, last):
     del after
-    step = pl.program_id(0)
-    levels, height, width, chans = out.shape
+    so_far = refs[0] if first else None
+    out, copies, acc = refs[-3:]
+    step = pl.program_id(0) + first
+    levels, height, width, chans = mine.shape[0], mine.shape[1] - 2, mine.shape[2] - 16, mine.shape[3]
     many = mine.shape[-1]
 
-    @pl.when(step == 0)
+    @pl.when(step == first)
     def _():
         copies[:, 0] = jnp.zeros_like(copies[:, 0])
         copies[:, levels + 1] = jnp.zeros_like(copies[:, levels + 1])
@@ -455,7 +457,7 @@
                     copies[0, lev + 1, row, :, lanes] = later.astype(copies.dtype)
                     copies[1, lev + 1, row, :, lanes] = field[lev, row, 0:width]
                     copies[2, lev + 1, row, :, lanes] = before.astype(copies.dtype)
-        acc[...] = jnp.zeros_like(acc)
+        acc[...] = so_far[...] if first else jnp.zeros_like(acc)
 
     lev_by, lat_by = step // 3, lax.rem(step, 3)
     cells = [
@@ -471,7 +473,7 @@
         preferred_element_type=jnp.float32,
     )
 
-    @pl.when(step == 8)
+    @pl.when(step == last)
     def _():
         out[...] = acc[...].reshape(out.shape).astype(out.dtype)
 
@@ -591,29 +593,36 @@
     )
     own, late = call(code_kernel, [slab(end + 16), slab(size)], (pos, grads, theirs), [], 0, "code", 16, held=1)
 
-    whole = lambda t: (0, 0, 0, 0)
-    field = pl.pallas_call(
-        field_kernel,
-        out_shape=jax.ShapeDtypeStruct((levels, height, width, chans), bf16),
-        grid=(9,),
-        in_specs=[
-            pl.BlockSpec(memory_space=SMEM),
-            pl.BlockSpec(memory_space=pl.ANY),
-            pl.BlockSpec(mine.shape, whole),
-            pl.BlockSpec(mine.shape, whole),
-            pl.BlockSpec((3, chans, filters), lambda t: (t, 0, 0)),
-        ],
-        out_specs=pl.BlockSpec((levels, height, width, chans), whole),
-        scratch_shapes=[
-            VMEM((3, levels + 2, height + 2, width, filters), bf16),
-            VMEM((cells, chans), f32),
-        ],
-        cost_estimate=pl.CostEstimate(
-            flops=4 * 27 * chans * filters * cells, bytes_accessed=27 * chans * filters * 2, transcendentals=0
-        ),
-        compiler_params=pltpu.CompilerParams(vmem_limit_bytes=20 * 1024 * 1024),
-        name="field",
-    )(pos, own, mine, theirs, taps)
+    def part_of_field(after, first, last, so_far, out):
+        whole = lambda t: (0, 0, 0, 0)
+        before = [so_far] if first else []
+        return pl.pallas_call(
+            lambda *refs: field_kernel(*refs, first=first, last=last),
+            out_shape=out,
+            grid=(last - first + 1,),
+            in_specs=[
+                pl.BlockSpec(memory_space=SMEM),
+                pl.BlockSpec(memory_space=pl.ANY),
+                pl.BlockSpec(mine.shape, whole),
+                pl.BlockSpec(mine.shape, whole),
+                pl.BlockSpec((3, chans, filters), lambda t: (t + first, 0, 0)),
+            ]
+            + [pl.BlockSpec(x.shape, lambda t: (0, 0)) for x in before],
+            out_specs=pl.BlockSpec(out.shape, lambda t: (0,) * len(out.shape)),
+            scratch_shapes=[
+                VMEM((3, levels + 2, height + 2, width, filters), bf16),
+                VMEM((cells, chans), f32),
+            ],
+            cost_estimate=pl.CostEstimate(
+                flops=2 * 27 * chans * filters * cells,
+                bytes_accessed=14 * chans * filters * 2,
+                transcendentals=0,
+            ),
+            compiler_params=pltpu.CompilerParams(vmem_limit_bytes=20 * 1024 * 1024),
+            name="field",
+        )(pos, after, mine, theirs, taps, *before)
+
+    so_far = part_of_field(own, 0, 4, None, jax.ShapeDtypeStruct((cells, chans), f32))
 
     def to_plane(share):
         return move(share, lat_xor(1)), move(share, lat_xor(2))
@@ -622,21 +631,22 @@
         top, bottom = call(
             cross_kernel, [slab(cut), slab(by_x.shape[0] - cut)], (pos, by_x, by_y, after1, after2), [], 0, name, 16, held=2
         )
-        return move(top, lat_xor(1)), move(bottom, lat_xor(2))
+        return move(top, lat_xor(1)), move(bottom, lat_xor(2)), top
 
     from_3 = move(late, lon_by(1))
     from_1 = move(late, lon_by(-1))
     own_x, own_y = to_plane(own)
-    own_top, own_bottom = to_diagonal(own_x, own_y, own_cut, field, own, "cross_1")
+    own_top, own_bottom, crossed = to_diagonal(own_x, own_y, own_cut, so_far, own, "cross_1")
+    field = part_of_field(crossed, 5, 8, so_far, jax.ShapeDtypeStruct((levels, height, width, chans), bf16))
     pair, half_3, half_1 = call(
         both_kernel,
         [slab(2 * size), slab(half), slab(size - half)],
-        (pos, from_3, from_1, own_top, own_bottom),
+        (pos, from_3, from_1, own_top, own_bottom, field),
         [],
         0,
         "both",
         16,
-        held=2,
+        held=3,
     )
     half_3 = move(half_3, lon_by(1))
     half_1 = move(half_1, lon_by(-1))
@@ -647,7 +657,7 @@
     early_3 = move(block, lon_by(1))
     early_1 = move(block, lon_by(-1))
     (from_2,) = call(across_kernel, [slab(size)], (pos, half_3, half_1, pair), [], 0, "across", 16, held=1)
-    pair_top, pair_bottom = to_diagonal(pair_x, pair_y, size, early_1, early_3, "cross_2")
+    pair_top, pair_bottom, _ = to_diagonal(pair_x, pair_y, size, early_1, early_3, "cross_2")
     from_2x, from_2y = to_plane(from_2)
     hand_3, hand_1 = call(hand_kernel, [slab(2 * first_rows)] * 2, (pos, early_3, early_1), [], 0, "hand", 16)
     early_2a = move(hand_3, lon_by(1))
@@ -664,7 +674,7 @@
     total, token = unpack(
         pos, total, [own, own_x, own_y, own_top, own_bottom], [block], [(0, 0, 27, pieces)], span, "unpack_1"
     )
-    from_2top, from_2bottom = to_diagonal(from_2x, from_2y, late_cut, token, pair, "cross_3")
+    from_2top, from_2bottom, _ = to_diagonal(from_2x, from_2y, late_cut, token, pair, "cross_3")
     slabs = [
         (3, early, 27 - early, [late_piece(0), late_piece(2), late_piece(3), late_piece(4)]),
         (1, early, 27 - early, [late_piece(1), late_piece(2, size), late_piece(3, size), late_piece(5)]),

time: 146 us -> 147 us (level)
  starting transfers between devices: 49.5 us -> 46.4 us
  waiting for transfers between devices: 45.7 us -> 48.8 us
    ppermute x39, waiting for transfers between devices: 45.7 us -> 48.8 us  [move(): return lax.ppermute(x, AXES, pairs)]
    ppermute x39, starting transfers between devices: 49.5 us -> 46.4 us  [move(): return lax.ppermute(x, AXES, pairs)]
    pallas_call x1 -> x2, Pallas kernels: 9.5 us -> 10.8 us  [part_of_field(): pl.pallas_call(lambda *refs: field_kernel(*refs, first=first, last=last),...]
  transfers between devices with their start and end apart: 39 -> 39, of which waited for: 14 -> 14; matrix products, arithmetic and copies ran while one was open for 0% -> 0% of each run, Pallas kernels for 26% -> 27%
where the time goes in v20:
time: 147 us
  waiting for transfers between devices  48.8 us (33%)
  starting transfers between devices  46.4 us (32%)
  Pallas kernels  46.1 us (31%)
  local copies, waits for them, and re-layouts  3.99 us (3%)
    ppermute x39, waiting for transfers between devices, move(): return lax.ppermute(x, AXES, pairs)  48.8 us
    ppermute x39, starting transfers between devices, move(): return lax.ppermute(x, AXES, pairs)  46.4 us
    pallas_call x15, Pallas kernels, call(): pl.pallas_call(kernel, out_shape=outs, in_specs=[pl.BlockSpec(memory_spac...  17.4 us
    pallas_call x3, Pallas kernels, unpack(): pl.pallas_call(lambda *refs: unpack_kernel(*refs, slabs=slabs, count=len(...  13.1 us
    pallas_call x2, Pallas kernels, part_of_field(): pl.pallas_call(lambda *refs: field_kernel(*refs, first=first, last=last),...  10.8 us
    pallas_call x1, Pallas kernels, blocked_body(): pl.pallas_call(lines_kernel, out_shape=[jax.ShapeDtypeStruct((levels, row...  4.87 us
    unnamed x14, local copies, waits for them, and re-layouts  3.99 us
  transfers between devices with their start and end apart: 39, of which 14 were waited for; matrix products, arithmetic and copies ran while one was open for 0% of the time, Pallas kernels for 27%

profile of v20, /device:TPU:0, one launch (start us, length us, event | category | flops | bytes accessed | tf_op | source)
XLA Modules:
  0.0 146.5 jit_solution(16813672770201647148)
XLA Ops:
  0.7 1.0 copy-done.1
  1.7 1.0 copy-done.3
  2.7 0.8 pack.1
  4.2 3.0 %collective-permute-start.9 = (bf16[768,128]{1,0:T(8,128)(2,1)S(1)}, bf16[768,128]{1,0:T(8,128)(2,1)S(1)}, u32[]{:S(2)}, u32[]{:S(2)}) collective-permute-start(bf16[768,128]{1,0:T(8,128)(2,1)S(1)} %get-tuple-element.42), channel_id=1, source_target_pairs={{0,4},{1,5},{2,6},{3,7},{4,0},{5,1},{6,2},{7,3},{8,20},{9,21},{10,... | collective-permute-start | bytes 589832 | tf_op jit(solution)/shard_map/ppermute | solution.py:98
  7.2 1.6 %collective-permute-start = (bf16[416,128]{1,0:T(8,128)(2,1)S(1)}, bf16[416,128]{1,0:T(8,128)(2,1)S(1)}, u32[]{:S(2)}, u32[]{:S(2)}) collective-permute-start(bf16[416,128]{1,0:T(8,128)(2,1)S(1)} %get-tuple-element.34), channel_id=1, source_target_pairs={{0,1},{1,2},{2,3},{3,0},{4,5},{5,6},{6,7},{7,4},{8,9},{9,10},{10,1... | collective-permute-start | bytes 319496 | tf_op jit(solution)/shard_map/ppermute | solution.py:98
  8.8 2.2 %collective-permute-start.2 = (bf16[416,128]{1,0:T(8,128)(2,1)S(1)}, bf16[416,128]{1,0:T(8,128)(2,1)S(1)}, u32[]{:S(2)}, u32[]{:S(2)}) collective-permute-start(bf16[416,128]{1,0:T(8,128)(2,1)S(1)} %get-tuple-element.36), channel_id=1, source_target_pairs={{0,3},{1,0},{2,1},{3,2},{4,7},{5,4},{6,5},{7,6},{8,11},{9,8},{10,9... | collective-permute-start | bytes 319496 | tf_op jit(solution)/shard_map/ppermute | solution.py:98
  11.9 9.2 %collective-permute-done.1.x2.after2 = bf16[384,128]{1,0:T(8,128)(2,1)S(1)} collective-permute-done((bf16[384,128]{1,0:T(8,128)(2,1)S(1)}, bf16[384,128]{1,0:T(8,128)(2,1)S(1)}, u32[]{:S(2)}, u32[]{:S(2)}) %collective-permute-start.1) | collective-permute-done | bytes 98336 | tf_op jit(solution)/shard_map/ppermute | solution.py:98
  21.7 2.3 %collective-permute-start.11 = (bf16[1616,128]{1,0:T(8,128)(2,1)S(1)}, bf16[1616,128]{1,0:T(8,128)(2,1)S(1)}, u32[]{:S(2)}, u32[]{:S(2)}) collective-permute-start(bf16[1616,128]{1,0:T(8,128)(2,1)S(1)} %pair_0.1.g0), channel_id=1, source_target_pairs={{0,3},{1,0},{2,1},{3,2},{4,7},{5,4},{6,5},{7,6},{8,11},{9,8},{10,9... | collective-permute-start | bytes 1241096 | tf_op jit(solution)/shard_map/ppermute | solution.py:98
  24.5 2.3 %collective-permute-start.4 = (bf16[384,128]{1,0:T(8,128)(2,1)S(1)}, bf16[384,128]{1,0:T(8,128)(2,1)S(1)}, u32[]{:S(2)}, u32[]{:S(2)}) collective-permute-start(bf16[384,128]{1,0:T(8,128)(2,1)S(1)} %get-tuple-element.38), channel_id=1, source_target_pairs={{0,12},{1,13},{2,14},{3,15},{4,8},{5,9},{6,10},{7,11},{8,4},{9,5},... | collective-permute-start | bytes 294920 | tf_op jit(solution)/shard_map/ppermute | solution.py:98
  26.8 2.7 %collective-permute-done.3.after1.by_x = bf16[384,128]{1,0:T(8,128)(2,1)S(1)} collective-permute-done((bf16[384,128]{1,0:T(8,128)(2,1)S(1)}, bf16[384,128]{1,0:T(8,128)(2,1)S(1)}, u32[]{:S(2)}, u32[]{:S(2)}) %collective-permute-start.3) | collective-permute-done | bytes 98336 | tf_op jit(solution)/shard_map/ppermute | solution.py:98
  29.5 1.2 collective-permute-done.4.after2.by_d
  31.4 1.7 %collective-permute-start.7 = (bf16[1600,128]{1,0:T(8,128)(2,1)S(1)}, bf16[1600,128]{1,0:T(8,128)(2,1)S(1)}, u32[]{:S(2)}, u32[]{:S(2)}) collective-permute-start(bf16[1600,128]{1,0:T(8,128)(2,1)S(1)} %get-tuple-element.39.x_own.own), channel_id=1, source_target_pairs={{0,12},{1,13},{2,14},{3,15},{4,8},{5,9},{6,10},{7,11},{8,4},{9,5},... | collective-permute-start | bytes 1228808 | tf_op jit(solution)/shard_map/ppermute | solution.py:98
  33.0 1.2 collective-permute-start.5
  34.9 7.7 %collective-permute-done.10.west.g1 = bf16[1616,128]{1,0:T(8,128)(2,1)S(1)} collective-permute-done((bf16[1616,128]{1,0:T(8,128)(2,1)S(1)}, bf16[1616,128]{1,0:T(8,128)(2,1)S(1)}, u32[]{:S(2)}, u32[]{:S(2)}) %collective-permute-start.10) | collective-permute-done | bytes 413728 | tf_op jit(solution)/shard_map/ppermute | solution.py:98
  43.2 1.9 %collective-permute-start.16 = (bf16[768,128]{1,0:T(8,128)(2,1)S(1)}, bf16[768,128]{1,0:T(8,128)(2,1)S(1)}, u32[]{:S(2)}, u32[]{:S(2)}) collective-permute-start(bf16[768,128]{1,0:T(8,128)(2,1)S(1)} %get-tuple-element.45), channel_id=1, source_target_pairs={{0,3},{1,0},{2,1},{3,2},{4,7},{5,4},{6,5},{7,6},{8,11},{9,8},{10,9... | collective-permute-start | bytes 589832 | tf_op jit(solution)/shard_map/ppermute | solution.py:98
  45.3 4.9 %collective-permute-done.6.x_y = bf16[1536,128]{1,0:T(8,128)(2,1)S(1)} collective-permute-done((bf16[1536,128]{1,0:T(8,128)(2,1)S(1)}, bf16[1536,128]{1,0:T(8,128)(2,1)S(1)}, u32[]{:S(2)}, u32[]{:S(2)}) %collective-permute-start.6) | collective-permute-done | bytes 393248 | tf_op jit(solution)/shard_map/ppermute | solution.py:98
  51.0 4.9 %lines.1 = (bf16[4,18,192,256]{3,2,1,0:T(8,128)(2,1)S(1)}, f32[27,256,512]{2,1,0:T(8,128)}) custom-call(s32[3]{0:T(128)S(1)} %pad_add_fusion.pos.refs_0_, bf16[1600,128]{1,0:T(8,128)(2,1)S(1)} %get-tuple-element.39.x_own.own, bf16[1600,128]{1,0:T(8,128)(2,1)S(1)} %collective-permute-done.5.x_x, bf16[1536,128]{1,0:T(8,128)(2,1)S(1)} %collective-permute-done.6.x_y, ...), custom_call_target="tpu_custom_call" | custom-call | bytes 1048576 | tf_op jit(solution)/shard_map/lines/pallas_call | solution.py:549
  57.1 1.0 copy-done.2
  58.9 8.6 %taps.1.held = f32[27,64,128]{2,1,0:T(8,128)S(1)} custom-call(s32[3]{0:T(128)S(1)} %pad_add_fusion.pos.refs_0_, bf16[4,18,192,256]{3,2,1,0:T(8,128)(2,1)S(1)} %get-tuple-element.44.after.xs, bf16[1616,128]{1,0:T(8,128)(2,1)S(1)} %pair_0.1.g0, bf16[1616,128]{1,0:T(8,128)(2,1)S(1)} %collective-permute-done.10.west.g1, ...), custom_call_target="tpu_custom_call" | custom-call | flops 5435817984 | bytes 11231232 | tf_op jit(solution)/shard_map/taps/pallas_call | solution.py:116
  67.5 0.9 code.1
  68.4 3.9 %collective-permute-start.28 = (bf16[1552,128]{1,0:T(8,128)(2,1)S(1)}, bf16[1552,128]{1,0:T(8,128)(2,1)S(1)}, u32[]{:S(2)}, u32[]{:S(2)}) collective-permute-start(bf16[1552,128]{1,0:T(8,128)(2,1)S(1)} %get-tuple-element.51), channel_id=1, source_target_pairs={{0,3},{1,0},{2,1},{3,2},{4,7},{5,4},{6,5},{7,6},{8,11},{9,8},{10,9... | collective-permute-start | bytes 1191944 | tf_op jit(solution)/shard_map/ppermute | solution.py:98
  72.3 1.3 collective-permute-start.20
  74.2 5.4 %field.2.after1.refs_5_ = f32[768,256]{1,0:T(8,128)S(1)} custom-call(s32[3]{0:T(128)S(1)} %pad_add_fusion.pos.refs_0_, bf16[1744,128]{1,0:T(8,128)(2,1)S(1)} %get-tuple-element.46.refs_1_.after2.own, bf16[4,6,64,256]{3,2,1,0:T(8,128)(2,1)S(1)} %mine.1.refs_2_, bf16[4,6,64,256]{3,2,1,0:T(8,128)(2,1)S(1)} %collective-permute-done.18.after.refs_3_, ...), custom_call_target="tpu_custom_call" | custom-call | flops 5435817984 | bytes 3670016 | tf_op jit(solution)/shard_map/field/pallas_call | solution.py:599
  79.6 5.1 %collective-permute-done.20.by_y.y.refs_3_ = bf16[1744,128]{1,0:T(8,128)(2,1)S(1)} collective-permute-done((bf16[1744,128]{1,0:T(8,128)(2,1)S(1)}, bf16[1744,128]{1,0:T(8,128)(2,1)S(1)}, u32[]{:S(2)}, u32[]{:S(2)}) %collective-permute-start.20) | collective-permute-done | bytes 446496 | tf_op jit(solution)/shard_map/ppermute | solution.py:98
  84.7 1.0 collective-permute-done.19.by_x.x.refs_2_
  86.2 0.8 collective-permute-start.22
  87.0 1.2 collective-permute-start.21
  88.3 5.3 %field.3.after3 = bf16[4,4,48,256]{3,2,1,0:T(8,128)(2,1)} custom-call(s32[3]{0:T(128)S(1)} %pad_add_fusion.pos.refs_0_, bf16[896,128]{1,0:T(8,128)(2,1)S(1)} %get-tuple-element.47.refs_1_, bf16[4,6,64,256]{3,2,1,0:T(8,128)(2,1)S(1)} %mine.1.refs_2_, bf16[4,6,64,256]{3,2,1,0:T(8,128)(2,1)S(1)} %collective-permute-done.18.after.refs_3_, ...), custom_call_target="tpu_custom_call" | custom-call | flops 5435817984 | bytes 3670016 | tf_op jit(solution)/shard_map/field/pallas_call | solution.py:599
  93.6 1.0 copy-done.4
  95.3 1.0 collective-permute-start.36
  96.3 1.1 collective-permute-start.35
  97.9 3.9 %collective-permute-start.24 = (bf16[832,128]{1,0:T(8,128)(2,1)S(1)}, bf16[832,128]{1,0:T(8,128)(2,1)S(1)}, u32[]{:S(2)}, u32[]{:S(2)}) collective-permute-start(bf16[832,128]{1,0:T(8,128)(2,1)S(1)} %block.1.refs_6_), channel_id=1, source_target_pairs={{0,3},{1,0},{2,1},{3,2},{4,7},{5,4},{6,5},{7,6},{8,11},{9,8},{10,9... | collective-permute-start | bytes 638984 | tf_op jit(solution)/shard_map/ppermute | solution.py:98
  101.8 1.8 %collective-permute-start.30 = (bf16[784,128]{1,0:T(8,128)(2,1)S(1)}, bf16[784,128]{1,0:T(8,128)(2,1)S(1)}, u32[]{:S(2)}, u32[]{:S(2)}) collective-permute-start(bf16[784,128]{1,0:T(8,128)(2,1)S(1)} %get-tuple-element.53), channel_id=1, source_target_pairs={{0,3},{1,0},{2,1},{3,2},{4,7},{5,4},{6,5},{7,6},{8,11},{9,8},{10,9... | collective-permute-start | bytes 602120 | tf_op jit(solution)/shard_map/ppermute | solution.py:98
  103.6 3.4 %collective-permute-done.29.half_3 = bf16[768,128]{1,0:T(8,128)(2,1)S(1)} collective-permute-done((bf16[768,128]{1,0:T(8,128)(2,1)S(1)}, bf16[768,128]{1,0:T(8,128)(2,1)S(1)}, u32[]{:S(2)}, u32[]{:S(2)}) %collective-permute-start.29) | collective-permute-done | bytes 196640 | tf_op jit(solution)/shard_map/ppermute | solution.py:98
  107.0 6.5 %collective-permute-done.30.half_1 = bf16[784,128]{1,0:T(8,128)(2,1)S(1)} collective-permute-done((bf16[784,128]{1,0:T(8,128)(2,1)S(1)}, bf16[784,128]{1,0:T(8,128)(2,1)S(1)}, u32[]{:S(2)}, u32[]{:S(2)}) %collective-permute-start.30) | collective-permute-done | bytes 200736 | tf_op jit(solution)/shard_map/ppermute | solution.py:98
  114.1 1.3 collective-permute-start.32
  115.4 0.8 collective-permute-start.31
  116.2 4.1 %collective-permute-done.23.block_3.after2.refs_7_ = bf16[832,128]{1,0:T(8,128)(2,1)S(1)} collective-permute-done((bf16[832,128]{1,0:T(8,128)(2,1)S(1)}, bf16[832,128]{1,0:T(8,128)(2,1)S(1)}, u32[]{:S(2)}, u32[]{:S(2)}) %collective-permute-start.23) | collective-permute-done | bytes 213024 | tf_op jit(solution)/shard_map/ppermute | solution.py:98
  121.7 1.3 collective-permute-start.38
  123.0 3.1 %unpack_1.1 = (f32[27,256,512]{2,1,0:T(8,128)}, f32[8,128]{1,0:T(8,128)S(1)}) custom-call(s32[3]{0:T(128)S(1)} %pad_add_fusion.pos.refs_0_, bf16[1744,128]{1,0:T(8,128)(2,1)S(1)} %get-tuple-element.46.refs_1_.after2.own, bf16[1744,128]{1,0:T(8,128)(2,1)S(1)} %collective-permute-done.19.by_x.x.refs_2_, ...), custom_call_target="tpu_custom_call", output_to_operand_aliasing={{0}: (7, {})} | custom-call | bytes 4194304 | tf_op jit(solution)/shard_map/unpack_1/pallas_call | solution.py:420
  126.3 1.2 collective-permute-done.31.by_x.refs_4_
  128.1 0.8 collective-permute-start.34
  128.9 1.4 collective-permute-start.33
  130.8 2.4 %collective-permute-start.26 = (bf16[416,128]{1,0:T(8,128)(2,1)S(1)}, bf16[416,128]{1,0:T(8,128)(2,1)S(1)}, u32[]{:S(2)}, u32[]{:S(2)}) collective-permute-start(bf16[416,128]{1,0:T(8,128)(2,1)S(1)} %get-tuple-element.50), channel_id=1, source_target_pairs={{0,3},{1,0},{2,1},{3,2},{4,7},{5,4},{6,5},{7,6},{8,11},{9,8},{10,9... | collective-permute-start | bytes 319496 | tf_op jit(solution)/shard_map/ppermute | solution.py:98
  133.2 1.2 collective-permute-done.37.refs_5_
  134.5 1.9 %collective-permute-start.25 = (bf16[416,128]{1,0:T(8,128)(2,1)S(1)}, bf16[416,128]{1,0:T(8,128)(2,1)S(1)}, u32[]{:S(2)}, u32[]{:S(2)}) collective-permute-start(bf16[416,128]{1,0:T(8,128)(2,1)S(1)} %get-tuple-element.49.refs_9_), channel_id=1, source_target_pairs={{0,1},{1,2},{2,3},{3,0},{4,5},{5,6},{6,7},{7,4},{8,9},{9,10},{10,1... | collective-permute-start | bytes 319496 | tf_op jit(solution)/shard_map/ppermute | solution.py:98
  136.4 6.2 %unpack_2.1 = (f32[27,256,512]{2,1,0:T(8,128)}, f32[8,128]{1,0:T(8,128)}) custom-call(s32[3]{0:T(128)S(1)} %pad_add_fusion.pos.refs_0_, bf16[1552,128]{1,0:T(8,128)(2,1)S(1)} %collective-permute-done.27.west.refs_1_, bf16[1552,128]{1,0:T(8,128)(2,1)S(1)} %collective-permute-done.28.east.refs_2_, ...), custom_call_target="tpu_custom_call", output_to_operand_aliasing={{0}: (10, {})} | custom-call | bytes 4194304 | tf_op jit(solution)/shard_map/unpack_2/pallas_call | solution.py:420
  142.6 3.7 %unpack_3.1 = (f32[27,256,512]{2,1,0:T(8,128)}, f32[8,128]{1,0:T(8,128)}) custom-call(s32[3]{0:T(128)S(1)} %pad_add_fusion.pos.refs_0_, bf16[416,128]{1,0:T(8,128)(2,1)S(1)} %collective-permute-done.25.refs_1_, bf16[416,128]{1,0:T(8,128)(2,1)S(1)} %collective-permute-done.26.refs_2_, ...), custom_call_target="tpu_custom_call", output_to_operand_aliasing={{0}: (8, {})} | custom-call | bytes 4194304 | tf_op jit(solution)/shard_map/unpack_3/pallas_call | solution.py:420
  (67 shorter events, 13.2 us)
Async XLA Ops:
  0.7 1.0 copy-start.1
  1.7 1.0 copy-start.3
  3.6 17.5 %collective-permute-start.8 = (bf16[768,128]{1,0:T(8,128)(2,1)S(1)}, bf16[768,128]{1,0:T(8,128)(2,1)S(1)}, u32[]{:S(2)}, u32[]{:S(2)}) collective-permute-start(bf16[768,128]{1,0:T(8,128)(2,1)S(1)} %get-tuple-element.41), channel_id=1, source_target_pairs={{0,0},{1,1},{2,2},{3,3},{4,4},{5,5},{6,6},{7,7},{8,16},{9,17},{10,... | collective-permute-start | bytes 589832 | tf_op jit(solution)/shard_map/ppermute | solution.py:98
  4.2 16.8 %collective-permute-start.9 = (bf16[768,128]{1,0:T(8,128)(2,1)S(1)}, bf16[768,128]{1,0:T(8,128)(2,1)S(1)}, u32[]{:S(2)}, u32[]{:S(2)}) collective-permute-start(bf16[768,128]{1,0:T(8,128)(2,1)S(1)} %get-tuple-element.42), channel_id=1, source_target_pairs={{0,4},{1,5},{2,6},{3,7},{4,0},{5,1},{6,2},{7,3},{8,20},{9,21},{10,... | collective-permute-start | bytes 589832 | tf_op jit(solution)/shard_map/ppermute | solution.py:98
  7.2 13.8 %collective-permute-start = (bf16[416,128]{1,0:T(8,128)(2,1)S(1)}, bf16[416,128]{1,0:T(8,128)(2,1)S(1)}, u32[]{:S(2)}, u32[]{:S(2)}) collective-permute-start(bf16[416,128]{1,0:T(8,128)(2,1)S(1)} %get-tuple-element.34), channel_id=1, source_target_pairs={{0,1},{1,2},{2,3},{3,0},{4,5},{5,6},{6,7},{7,4},{8,9},{9,10},{10,1... | collective-permute-start | bytes 319496 | tf_op jit(solution)/shard_map/ppermute | solution.py:98
  8.8 12.2 %collective-permute-start.2 = (bf16[416,128]{1,0:T(8,128)(2,1)S(1)}, bf16[416,128]{1,0:T(8,128)(2,1)S(1)}, u32[]{:S(2)}, u32[]{:S(2)}) collective-permute-start(bf16[416,128]{1,0:T(8,128)(2,1)S(1)} %get-tuple-element.36), channel_id=1, source_target_pairs={{0,3},{1,0},{2,1},{3,2},{4,7},{5,4},{6,5},{7,6},{8,11},{9,8},{10,9... | collective-permute-start | bytes 319496 | tf_op jit(solution)/shard_map/ppermute | solution.py:98
  11.1 10.0 %collective-permute-start.1 = (bf16[384,128]{1,0:T(8,128)(2,1)S(1)}, bf16[384,128]{1,0:T(8,128)(2,1)S(1)}, u32[]{:S(2)}, u32[]{:S(2)}) collective-permute-start(bf16[384,128]{1,0:T(8,128)(2,1)S(1)} %get-tuple-element.35), channel_id=1, source_target_pairs={{0,2},{1,3},{2,0},{3,1},{4,6},{5,7},{6,4},{7,5},{8,10},{9,11},{10,... | collective-permute-start | bytes 294920 | tf_op jit(solution)/shard_map/ppermute | solution.py:98
  21.7 13.3 %collective-permute-start.11 = (bf16[1616,128]{1,0:T(8,128)(2,1)S(1)}, bf16[1616,128]{1,0:T(8,128)(2,1)S(1)}, u32[]{:S(2)}, u32[]{:S(2)}) collective-permute-start(bf16[1616,128]{1,0:T(8,128)(2,1)S(1)} %pair_0.1.g0), channel_id=1, source_target_pairs={{0,3},{1,0},{2,1},{3,2},{4,7},{5,4},{6,5},{7,6},{8,11},{9,8},{10,9... | collective-permute-start | bytes 1241096 | tf_op jit(solution)/shard_map/ppermute | solution.py:98
  23.9 18.7 %collective-permute-start.10 = (bf16[1616,128]{1,0:T(8,128)(2,1)S(1)}, bf16[1616,128]{1,0:T(8,128)(2,1)S(1)}, u32[]{:S(2)}, u32[]{:S(2)}) collective-permute-start(bf16[1616,128]{1,0:T(8,128)(2,1)S(1)} %pair_0.1.g0), channel_id=1, source_target_pairs={{0,1},{1,2},{2,3},{3,0},{4,5},{5,6},{6,7},{7,4},{8,9},{9,10},{10,1... | collective-permute-start | bytes 1241096 | tf_op jit(solution)/shard_map/ppermute | solution.py:98
  23.9 5.6 %collective-permute-start.3 = (bf16[384,128]{1,0:T(8,128)(2,1)S(1)}, bf16[384,128]{1,0:T(8,128)(2,1)S(1)}, u32[]{:S(2)}, u32[]{:S(2)}) collective-permute-start(bf16[384,128]{1,0:T(8,128)(2,1)S(1)} %get-tuple-element.37), channel_id=1, source_target_pairs={{0,4},{1,5},{2,6},{3,7},{4,0},{5,1},{6,2},{7,3},{8,12},{9,13},{10,... | collective-permute-start | bytes 294920 | tf_op jit(solution)/shard_map/ppermute | solution.py:98
  24.5 6.2 %collective-permute-start.4 = (bf16[384,128]{1,0:T(8,128)(2,1)S(1)}, bf16[384,128]{1,0:T(8,128)(2,1)S(1)}, u32[]{:S(2)}, u32[]{:S(2)}) collective-permute-start(bf16[384,128]{1,0:T(8,128)(2,1)S(1)} %get-tuple-element.38), channel_id=1, source_target_pairs={{0,12},{1,13},{2,14},{3,15},{4,8},{5,9},{6,10},{7,11},{8,4},{9,5},... | collective-permute-start | bytes 294920 | tf_op jit(solution)/shard_map/ppermute | solution.py:98
  31.4 18.8 %collective-permute-start.7 = (bf16[1600,128]{1,0:T(8,128)(2,1)S(1)}, bf16[1600,128]{1,0:T(8,128)(2,1)S(1)}, u32[]{:S(2)}, u32[]{:S(2)}) collective-permute-start(bf16[1600,128]{1,0:T(8,128)(2,1)S(1)} %get-tuple-element.39.x_own.own), channel_id=1, source_target_pairs={{0,12},{1,13},{2,14},{3,15},{4,8},{5,9},{6,10},{7,11},{8,4},{9,5},... | collective-permute-start | bytes 1228808 | tf_op jit(solution)/shard_map/ppermute | solution.py:98
  33.0 18.0 %collective-permute-start.5 = (bf16[1600,128]{1,0:T(8,128)(2,1)S(1)}, bf16[1600,128]{1,0:T(8,128)(2,1)S(1)}, u32[]{:S(2)}, u32[]{:S(2)}) collective-permute-start(bf16[1600,128]{1,0:T(8,128)(2,1)S(1)} %get-tuple-element.39.x_own.own), channel_id=1, source_target_pairs={{0,4},{1,5},{2,6},{3,7},{4,0},{5,1},{6,2},{7,3},{8,12},{9,13},{10,... | collective-permute-start | bytes 1228808 | tf_op jit(solution)/shard_map/ppermute | solution.py:98
  34.2 15.9 %collective-permute-start.6 = (bf16[1536,128]{1,0:T(8,128)(2,1)S(1)}, bf16[1536,128]{1,0:T(8,128)(2,1)S(1)}, u32[]{:S(2)}, u32[]{:S(2)}) collective-permute-start(bf16[1536,128]{1,0:T(8,128)(2,1)S(1)} %get-tuple-element.40), channel_id=1, source_target_pairs={{0,8},{1,9},{2,10},{3,11},{4,12},{5,13},{6,14},{7,15},{8,0},{9,1},... | collective-permute-start | bytes 1179656 | tf_op jit(solution)/shard_map/ppermute | solution.py:98
  43.2 12.7 %collective-permute-start.16 = (bf16[768,128]{1,0:T(8,128)(2,1)S(1)}, bf16[768,128]{1,0:T(8,128)(2,1)S(1)}, u32[]{:S(2)}, u32[]{:S(2)}) collective-permute-start(bf16[768,128]{1,0:T(8,128)(2,1)S(1)} %get-tuple-element.45), channel_id=1, source_target_pairs={{0,3},{1,0},{2,1},{3,2},{4,7},{5,4},{6,5},{7,6},{8,11},{9,8},{10,9... | collective-permute-start | bytes 589832 | tf_op jit(solution)/shard_map/ppermute | solution.py:98
  45.1 10.9 %collective-permute-start.15 = (bf16[768,128]{1,0:T(8,128)(2,1)S(1)}, bf16[768,128]{1,0:T(8,128)(2,1)S(1)}, u32[]{:S(2)}, u32[]{:S(2)}) collective-permute-start(bf16[768,128]{1,0:T(8,128)(2,1)S(1)} %get-tuple-element.43.after), channel_id=1, source_target_pairs={{0,1},{1,2},{2,3},{3,0},{4,5},{5,6},{6,7},{7,4},{8,9},{9,10},{10,1... | collective-permute-start | bytes 589832 | tf_op jit(solution)/shard_map/ppermute | solution.py:98
  50.1 8.7 %collective-permute-start.12 = (bf16[1616,128]{1,0:T(8,128)(2,1)S(1)}, bf16[1616,128]{1,0:T(8,128)(2,1)S(1)}, u32[]{:S(2)}, u32[]{:S(2)}) collective-permute-start(bf16[1616,128]{1,0:T(8,128)(2,1)S(1)} %pair_0.1.g0), channel_id=1, source_target_pairs={{0,16},{1,17},{2,18},{3,19},{4,20},{5,21},{6,22},{7,23},{8,24},{9,... | collective-permute-start | bytes 1241096 | tf_op jit(solution)/shard_map/ppermute | solution.py:98
  50.1 8.7 %collective-permute-start.14 = (bf16[1616,128]{1,0:T(8,128)(2,1)S(1)}, bf16[1616,128]{1,0:T(8,128)(2,1)S(1)}, u32[]{:S(2)}, u32[]{:S(2)}) collective-permute-start(bf16[1616,128]{1,0:T(8,128)(2,1)S(1)} %collective-permute-done.11.east.g3), channel_id=1, source_target_pairs={{0,16},{1,17},{2,18},{3,19},{4,20},{5,21},{6,22},{7,23},{8,24},{9,... | collective-permute-start | bytes 1241096 | tf_op jit(solution)/shard_map/ppermute | solution.py:98
  51.0 7.8 %collective-permute-start.13 = (bf16[1616,128]{1,0:T(8,128)(2,1)S(1)}, bf16[1616,128]{1,0:T(8,128)(2,1)S(1)}, u32[]{:S(2)}, u32[]{:S(2)}) collective-permute-start(bf16[1616,128]{1,0:T(8,128)(2,1)S(1)} %collective-permute-done.10.west.g1), channel_id=1, source_target_pairs={{0,16},{1,17},{2,18},{3,19},{4,20},{5,21},{6,22},{7,23},{8,24},{9,... | collective-permute-start | bytes 1241096 | tf_op jit(solution)/shard_map/ppermute | solution.py:98
  56.5 2.4 %collective-permute-start.17 = (bf16[2,768,128]{2,1,0:T(8,128)(2,1)S(1)}, bf16[2,768,128]{2,1,0:T(8,128)(2,1)S(1)}, u32[]{:S(2)}, u32[]{:S(2)}) collective-permute-start(bf16[2,768,128]{2,1,0:T(8,128)(2,1)S(1)} %pair.1.g2), channel_id=1, source_target_pairs={{0,16},{1,17},{2,18},{3,19},{4,20},{5,21},{6,22},{7,23},{8,24},{9,... | collective-permute-start | bytes 1179656 | tf_op jit(solution)/shard_map/ppermute | solution.py:98
  57.1 1.0 copy-start.2
  58.1 16.1 %slice-start = ((s8[7077888]{0:T(1024)(128)(4,1)}), s8[4194304]{0:T(1024)(128)(4,1)S(1)}, s32[]{:S(2)}) async-start(s8[7077888]{0:T(1024)(128)(4,1)} %bitcast.12), calls=%async_computation | async-start | bytes 8388608
  58.8 15.4 %slice-start.1 = ((s8[7077888]{0:T(1024)(128)(4,1)}), s8[2883584]{0:T(1024)(128)(4,1)S(1)}, s32[]{:S(2)}) async-start(s8[7077888]{0:T(1024)(128)(4,1)} %bitcast.12), calls=%async_computation.1 | async-start | bytes 5767168
  58.8 8.7 %collective-permute-start.18 = (bf16[4,6,64,256]{3,2,1,0:T(8,128)(2,1)S(1)}, bf16[4,6,64,256]{3,2,1,0:T(8,128)(2,1)S(1)}, u32[]{:S(2)}, u32[]{:S(2)}) collective-permute-start(bf16[4,6,64,256]{3,2,1,0:T(8,128)(2,1)S(1)} %mine.1.refs_2_), channel_id=1, source_target_pairs={{0,16},{1,17},{2,18},{3,19},{4,20},{5,21},{6,22},{7,23},{8,24},{9,... | collective-permute-start | bytes 2359304 | tf_op jit(solution)/shard_map/ppermute | solution.py:98
  68.4 25.2 %collective-permute-start.28 = (bf16[1552,128]{1,0:T(8,128)(2,1)S(1)}, bf16[1552,128]{1,0:T(8,128)(2,1)S(1)}, u32[]{:S(2)}, u32[]{:S(2)}) collective-permute-start(bf16[1552,128]{1,0:T(8,128)(2,1)S(1)} %get-tuple-element.51), channel_id=1, source_target_pairs={{0,3},{1,0},{2,1},{3,2},{4,7},{5,4},{6,5},{7,6},{8,11},{9,8},{10,9... | collective-permute-start | bytes 1191944 | tf_op jit(solution)/shard_map/ppermute | solution.py:98
  72.3 21.3 %collective-permute-start.27 = (bf16[1552,128]{1,0:T(8,128)(2,1)S(1)}, bf16[1552,128]{1,0:T(8,128)(2,1)S(1)}, u32[]{:S(2)}, u32[]{:S(2)}) collective-permute-start(bf16[1552,128]{1,0:T(8,128)(2,1)S(1)} %get-tuple-element.51), channel_id=1, source_target_pairs={{0,1},{1,2},{2,3},{3,0},{4,5},{5,6},{6,7},{7,4},{8,9},{9,10},{10,1... | collective-permute-start | bytes 1191944 | tf_op jit(solution)/shard_map/ppermute | solution.py:98
  72.3 12.3 %collective-permute-start.20 = (bf16[1744,128]{1,0:T(8,128)(2,1)S(1)}, bf16[1744,128]{1,0:T(8,128)(2,1)S(1)}, u32[]{:S(2)}, u32[]{:S(2)}) collective-permute-start(bf16[1744,128]{1,0:T(8,128)(2,1)S(1)} %get-tuple-element.46.refs_1_.after2.own), channel_id=1, source_target_pairs={{0,8},{1,9},{2,10},{3,11},{4,12},{5,13},{6,14},{7,15},{8,0},{9,1},... | collective-permute-start | bytes 1339400 | tf_op jit(solution)/shard_map/ppermute | solution.py:98
  73.6 12.0 %collective-permute-start.19 = (bf16[1744,128]{1,0:T(8,128)(2,1)S(1)}, bf16[1744,128]{1,0:T(8,128)(2,1)S(1)}, u32[]{:S(2)}, u32[]{:S(2)}) collective-permute-start(bf16[1744,128]{1,0:T(8,128)(2,1)S(1)} %get-tuple-element.46.refs_1_.after2.own), channel_id=1, source_target_pairs={{0,4},{1,5},{2,6},{3,7},{4,0},{5,1},{6,2},{7,3},{8,12},{9,13},{10,... | collective-permute-start | bytes 1339400 | tf_op jit(solution)/shard_map/ppermute | solution.py:98
  86.2 7.4 %collective-permute-start.22 = (bf16[848,128]{1,0:T(8,128)(2,1)S(1)}, bf16[848,128]{1,0:T(8,128)(2,1)S(1)}, u32[]{:S(2)}, u32[]{:S(2)}) collective-permute-start(bf16[848,128]{1,0:T(8,128)(2,1)S(1)} %get-tuple-element.48), channel_id=1, source_target_pairs={{0,8},{1,9},{2,10},{3,11},{4,12},{5,13},{6,14},{7,15},{8,0},{9,1},... | collective-permute-start | bytes 651272 | tf_op jit(solution)/shard_map/ppermute | solution.py:98
  87.0 6.6 %collective-permute-start.21 = (bf16[896,128]{1,0:T(8,128)(2,1)S(1)}, bf16[896,128]{1,0:T(8,128)(2,1)S(1)}, u32[]{:S(2)}, u32[]{:S(2)}) collective-permute-start(bf16[896,128]{1,0:T(8,128)(2,1)S(1)} %get-tuple-element.47.refs_1_), channel_id=1, source_target_pairs={{0,4},{1,5},{2,6},{3,7},{4,0},{5,1},{6,2},{7,3},{8,12},{9,13},{10,... | collective-permute-start | bytes 688136 | tf_op jit(solution)/shard_map/ppermute | solution.py:98
  93.6 1.0 copy-start.4
  95.3 25.0 %collective-permute-start.36 = (bf16[3104,128]{1,0:T(8,128)(2,1)S(1)}, bf16[3104,128]{1,0:T(8,128)(2,1)S(1)}, u32[]{:S(2)}, u32[]{:S(2)}) collective-permute-start(bf16[3104,128]{1,0:T(8,128)(2,1)S(1)} %get-tuple-element.54.after.after2), channel_id=1, source_target_pairs={{0,8},{1,9},{2,10},{3,11},{4,12},{5,13},{6,14},{7,15},{8,0},{9,1},... | collective-permute-start | bytes 2383880 | tf_op jit(solution)/shard_map/ppermute | solution.py:98
  96.3 24.0 %collective-permute-start.35 = (bf16[3104,128]{1,0:T(8,128)(2,1)S(1)}, bf16[3104,128]{1,0:T(8,128)(2,1)S(1)}, u32[]{:S(2)}, u32[]{:S(2)}) collective-permute-start(bf16[3104,128]{1,0:T(8,128)(2,1)S(1)} %get-tuple-element.54.after.after2), channel_id=1, source_target_pairs={{0,4},{1,5},{2,6},{3,7},{4,0},{5,1},{6,2},{7,3},{8,12},{9,13},{10,... | collective-permute-start | bytes 2383880 | tf_op jit(solution)/shard_map/ppermute | solution.py:98
  97.4 9.6 %collective-permute-start.29 = (bf16[768,128]{1,0:T(8,128)(2,1)S(1)}, bf16[768,128]{1,0:T(8,128)(2,1)S(1)}, u32[]{:S(2)}, u32[]{:S(2)}) collective-permute-start(bf16[768,128]{1,0:T(8,128)(2,1)S(1)} %get-tuple-element.52), channel_id=1, source_target_pairs={{0,1},{1,2},{2,3},{3,0},{4,5},{5,6},{6,7},{7,4},{8,9},{9,10},{10,1... | collective-permute-start | bytes 589832 | tf_op jit(solution)/shard_map/ppermute | solution.py:98
  97.9 17.4 %collective-permute-start.24 = (bf16[832,128]{1,0:T(8,128)(2,1)S(1)}, bf16[832,128]{1,0:T(8,128)(2,1)S(1)}, u32[]{:S(2)}, u32[]{:S(2)}) collective-permute-start(bf16[832,128]{1,0:T(8,128)(2,1)S(1)} %block.1.refs_6_), channel_id=1, source_target_pairs={{0,3},{1,0},{2,1},{3,2},{4,7},{5,4},{6,5},{7,6},{8,11},{9,8},{10,9... | collective-permute-start | bytes 638984 | tf_op jit(solution)/shard_map/ppermute | solution.py:98
  101.8 11.7 %collective-permute-start.30 = (bf16[784,128]{1,0:T(8,128)(2,1)S(1)}, bf16[784,128]{1,0:T(8,128)(2,1)S(1)}, u32[]{:S(2)}, u32[]{:S(2)}) collective-permute-start(bf16[784,128]{1,0:T(8,128)(2,1)S(1)} %get-tuple-element.53), channel_id=1, source_target_pairs={{0,3},{1,0},{2,1},{3,2},{4,7},{5,4},{6,5},{7,6},{8,11},{9,8},{10,9... | collective-permute-start | bytes 602120 | tf_op jit(solution)/shard_map/ppermute | solution.py:98
  107.0 13.3 %collective-permute-start.23 = (bf16[832,128]{1,0:T(8,128)(2,1)S(1)}, bf16[832,128]{1,0:T(8,128)(2,1)S(1)}, u32[]{:S(2)}, u32[]{:S(2)}) collective-permute-start(bf16[832,128]{1,0:T(8,128)(2,1)S(1)} %block.1.refs_6_), channel_id=1, source_target_pairs={{0,1},{1,2},{2,3},{3,0},{4,5},{5,6},{6,7},{7,4},{8,9},{9,10},{10,1... | collective-permute-start | bytes 638984 | tf_op jit(solution)/shard_map/ppermute | solution.py:98
  114.1 12.2 %collective-permute-start.32 = (bf16[1552,128]{1,0:T(8,128)(2,1)S(1)}, bf16[1552,128]{1,0:T(8,128)(2,1)S(1)}, u32[]{:S(2)}, u32[]{:S(2)}) collective-permute-start(bf16[1552,128]{1,0:T(8,128)(2,1)S(1)} %across.1.refs_3_), channel_id=1, source_target_pairs={{0,8},{1,9},{2,10},{3,11},{4,12},{5,13},{6,14},{7,15},{8,0},{9,1},... | collective-permute-start | bytes 1191944 | tf_op jit(solution)/shard_map/ppermute | solution.py:98
  115.4 12.1 %collective-permute-start.31 = (bf16[1552,128]{1,0:T(8,128)(2,1)S(1)}, bf16[1552,128]{1,0:T(8,128)(2,1)S(1)}, u32[]{:S(2)}, u32[]{:S(2)}) collective-permute-start(bf16[1552,128]{1,0:T(8,128)(2,1)S(1)} %across.1.refs_3_), channel_id=1, source_target_pairs={{0,4},{1,5},{2,6},{3,7},{4,0},{5,1},{6,2},{7,3},{8,12},{9,13},{10,... | collective-permute-start | bytes 1191944 | tf_op jit(solution)/shard_map/ppermute | solution.py:98
  120.3 16.1 %copy-start = (bf16[3104,128]{1,0:T(8,128)(2,1)}, bf16[3104,128]{1,0:T(8,128)(2,1)S(1)}, u32[]{:S(2)}) copy-start(bf16[3104,128]{1,0:T(8,128)(2,1)S(1)} %collective-permute-done.36.by_y.refs_4_) | copy-start | bytes 2383876
  120.9 13.6 %collective-permute-start.37 = (bf16[1552,128]{1,0:T(8,128)(2,1)S(1)}, bf16[1552,128]{1,0:T(8,128)(2,1)S(1)}, u32[]{:S(2)}, u32[]{:S(2)}) collective-permute-start(bf16[1552,128]{1,0:T(8,128)(2,1)S(1)} %get-tuple-element.59), channel_id=1, source_target_pairs={{0,4},{1,5},{2,6},{3,7},{4,0},{5,1},{6,2},{7,3},{8,12},{9,13},{10,... | collective-permute-start | bytes 1191944 | tf_op jit(solution)/shard_map/ppermute | solution.py:98
  121.7 14.7 %collective-permute-start.38 = (bf16[1552,128]{1,0:T(8,128)(2,1)S(1)}, bf16[1552,128]{1,0:T(8,128)(2,1)S(1)}, u32[]{:S(2)}, u32[]{:S(2)}) collective-permute-start(bf16[1552,128]{1,0:T(8,128)(2,1)S(1)} %get-tuple-element.60), channel_id=1, source_target_pairs={{0,8},{1,9},{2,10},{3,11},{4,12},{5,13},{6,14},{7,15},{8,0},{9,1},... | collective-permute-start | bytes 1191944 | tf_op jit(solution)/shard_map/ppermute | solution.py:98
  128.1 14.6 %collective-permute-start.34 = (bf16[784,128]{1,0:T(8,128)(2,1)S(1)}, bf16[784,128]{1,0:T(8,128)(2,1)S(1)}, u32[]{:S(2)}, u32[]{:S(2)}) collective-permute-start(bf16[784,128]{1,0:T(8,128)(2,1)S(1)} %get-tuple-element.58), channel_id=1, source_target_pairs={{0,8},{1,9},{2,10},{3,11},{4,12},{5,13},{6,14},{7,15},{8,0},{9,1},... | collective-permute-start | bytes 602120 | tf_op jit(solution)/shard_map/ppermute | solution.py:98
  128.9 13.7 %collective-permute-start.33 = (bf16[768,128]{1,0:T(8,128)(2,1)S(1)}, bf16[768,128]{1,0:T(8,128)(2,1)S(1)}, u32[]{:S(2)}, u32[]{:S(2)}) collective-permute-start(bf16[768,128]{1,0:T(8,128)(2,1)S(1)} %get-tuple-element.57), channel_id=1, source_target_pairs={{0,4},{1,5},{2,6},{3,7},{4,0},{5,1},{6,2},{7,3},{8,12},{9,13},{10,... | collective-permute-start | bytes 589832 | tf_op jit(solution)/shard_map/ppermute | solution.py:98
  130.8 11.8 %collective-permute-start.26 = (bf16[416,128]{1,0:T(8,128)(2,1)S(1)}, bf16[416,128]{1,0:T(8,128)(2,1)S(1)}, u32[]{:S(2)}, u32[]{:S(2)}) collective-permute-start(bf16[416,128]{1,0:T(8,128)(2,1)S(1)} %get-tuple-element.50), channel_id=1, source_target_pairs={{0,3},{1,0},{2,1},{3,2},{4,7},{5,4},{6,5},{7,6},{8,11},{9,8},{10,9... | collective-permute-start | bytes 319496 | tf_op jit(solution)/shard_map/ppermute | solution.py:98
  134.5 8.1 %collective-permute-start.25 = (bf16[416,128]{1,0:T(8,128)(2,1)S(1)}, bf16[416,128]{1,0:T(8,128)(2,1)S(1)}, u32[]{:S(2)}, u32[]{:S(2)}) collective-permute-start(bf16[416,128]{1,0:T(8,128)(2,1)S(1)} %get-tuple-element.49.refs_9_), channel_id=1, source_target_pairs={{0,1},{1,2},{2,3},{3,0},{4,5},{5,6},{6,7},{7,4},{8,9},{9,10},{10,1... | collective-permute-start | bytes 319496 | tf_op jit(solution)/shard_map/ppermute | solution.py:98

commit v21 on v18

--- a/solution.py
+++ b/solution.py
@@ -346,8 +346,8 @@
     half_1[...] = east[half:, :]
 
 
-def cross_kernel(pos, by_x, by_y, after1, after2, top, bottom):
-    del pos, after1, after2
+def cross_kernel(pos, by_x, by_y, after1, after2, after3, top, bottom):
+    del pos, after1, after2, after3
     cut = top.shape[0]
     top[...] = by_y[0:cut, :]
     bottom[...] = by_x[cut:, :]
@@ -618,16 +618,16 @@
     def to_plane(share):
         return move(share, lat_xor(1)), move(share, lat_xor(2))
 
-    def to_diagonal(by_x, by_y, cut, after1, after2, name):
+    def to_diagonal(by_x, by_y, cut, after, name):
         top, bottom = call(
-            cross_kernel, [slab(cut), slab(by_x.shape[0] - cut)], (pos, by_x, by_y, after1, after2), [], 0, name, 16, held=2
+            cross_kernel, [slab(cut), slab(by_x.shape[0] - cut)], (pos, by_x, by_y, *after), [], 0, name, 16, held=3
         )
         return move(top, lat_xor(1)), move(bottom, lat_xor(2))
 
     from_3 = move(late, lon_by(1))
     from_1 = move(late, lon_by(-1))
     own_x, own_y = to_plane(own)
-    own_top, own_bottom = to_diagonal(own_x, own_y, own_cut, field, own, "cross_1")
+    own_top, own_bottom = to_diagonal(own_x, own_y, own_cut, (field, own, own), "cross_1")
     pair, half_3, half_1 = call(
         both_kernel,
         [slab(2 * size), slab(half), slab(size - half)],
@@ -647,7 +647,7 @@
     early_3 = move(block, lon_by(1))
     early_1 = move(block, lon_by(-1))
     (from_2,) = call(across_kernel, [slab(size)], (pos, half_3, half_1, pair), [], 0, "across", 16, held=1)
-    pair_top, pair_bottom = to_diagonal(pair_x, pair_y, size, early_1, early_3, "cross_2")
+    pair_top, pair_bottom = to_diagonal(pair_x, pair_y, size, (early_1, early_3, pair), "cross_2")
     from_2x, from_2y = to_plane(from_2)
     hand_3, hand_1 = call(hand_kernel, [slab(2 * first_rows)] * 2, (pos, early_3, early_1), [], 0, "hand", 16)
     early_2a = move(hand_3, lon_by(1))
@@ -664,7 +664,7 @@
     total, token = unpack(
         pos, total, [own, own_x, own_y, own_top, own_bottom], [block], [(0, 0, 27, pieces)], span, "unpack_1"
     )
-    from_2top, from_2bottom = to_diagonal(from_2x, from_2y, late_cut, token, pair, "cross_3")
+    from_2top, from_2bottom = to_diagonal(from_2x, from_2y, late_cut, (token, early_2a, early_2b), "cross_3")
     slabs = [
         (3, early, 27 - early, [late_piece(0), late_piece(2), late_piece(3), late_piece(4)]),
         (1, early, 27 - early, [late_piece(1), late_piece(2, size), late_piece(3, size), late_piece(5)]),

time: 146 us -> 146 us (level)
  waiting for transfers between devices: 45.7 us -> 49.1 us
  starting transfers between devices: 49.5 us -> 46.4 us
    ppermute x39, waiting for transfers between devices: 45.7 us -> 49.1 us  [move(): return lax.ppermute(x, AXES, pairs)]
    ppermute x39, starting transfers between devices: 49.5 us -> 46.4 us  [move(): return lax.ppermute(x, AXES, pairs)]
where the time goes in v21:
time: 146 us; the launch traced here: 145 us
  waiting for transfers between devices  49.1 us (34%)
  starting transfers between devices  46.4 us (32%)
  Pallas kernels  44.8 us (31%)
  local copies, waits for them, and re-layouts  4 us (3%)
    ppermute x39, waiting for transfers between devices, move(): return lax.ppermute(x, AXES, pairs)  49.1 us
    ppermute x39, starting transfers between devices, move(): return lax.ppermute(x, AXES, pairs)  46.4 us
    pallas_call x15, Pallas kernels, call(): pl.pallas_call(kernel, out_shape=outs, in_specs=[pl.BlockSpec(memory_spac...  17.4 us
    pallas_call x3, Pallas kernels, unpack(): pl.pallas_call(lambda *refs: unpack_kernel(*refs, slabs=slabs, count=len(...  13.1 us
    pallas_call x1, Pallas kernels, blocked_body(): pl.pallas_call(field_kernel, out_shape=jax.ShapeDtypeStruct((levels, heig...  9.5 us
    pallas_call x1, Pallas kernels, blocked_body(): pl.pallas_call(lines_kernel, out_shape=[jax.ShapeDtypeStruct((levels, row...  4.87 us
    unnamed x14, local copies, waits for them, and re-layouts  4 us
  transfers between devices with their start and end apart: 39, of which 14 were waited for; matrix products, arithmetic and copies ran while one was open for 0% of the time, Pallas kernels for 26%

profile of v21, /device:TPU:0, one launch (start us, length us, event | category | flops | bytes accessed | tf_op | source)
XLA Modules:
  0.0 145.5 jit_solution(10295146752675465748)
XLA Ops:
  0.7 1.0 copy-done.1
  1.7 1.0 copy-done.4
  2.7 0.8 pack.1
  4.2 3.0 %collective-permute-start.9 = (bf16[768,128]{1,0:T(8,128)(2,1)S(1)}, bf16[768,128]{1,0:T(8,128)(2,1)S(1)}, u32[]{:S(2)}, u32[]{:S(2)}) collective-permute-start(bf16[768,128]{1,0:T(8,128)(2,1)S(1)} %get-tuple-element.42), channel_id=1, source_target_pairs={{0,4},{1,5},{2,6},{3,7},{4,0},{5,1},{6,2},{7,3},{8,20},{9,21},{10,... | collective-permute-start | bytes 589832 | tf_op jit(solution)/shard_map/ppermute | solution.py:98
  7.2 1.6 %collective-permute-start = (bf16[416,128]{1,0:T(8,128)(2,1)S(1)}, bf16[416,128]{1,0:T(8,128)(2,1)S(1)}, u32[]{:S(2)}, u32[]{:S(2)}) collective-permute-start(bf16[416,128]{1,0:T(8,128)(2,1)S(1)} %get-tuple-element.34), channel_id=1, source_target_pairs={{0,1},{1,2},{2,3},{3,0},{4,5},{5,6},{6,7},{7,4},{8,9},{9,10},{10,1... | collective-permute-start | bytes 319496 | tf_op jit(solution)/shard_map/ppermute | solution.py:98
  8.8 2.2 %collective-permute-start.2 = (bf16[416,128]{1,0:T(8,128)(2,1)S(1)}, bf16[416,128]{1,0:T(8,128)(2,1)S(1)}, u32[]{:S(2)}, u32[]{:S(2)}) collective-permute-start(bf16[416,128]{1,0:T(8,128)(2,1)S(1)} %get-tuple-element.36), channel_id=1, source_target_pairs={{0,3},{1,0},{2,1},{3,2},{4,7},{5,4},{6,5},{7,6},{8,11},{9,8},{10,9... | collective-permute-start | bytes 319496 | tf_op jit(solution)/shard_map/ppermute | solution.py:98
  11.9 9.2 %collective-permute-done.1.x2.after2 = bf16[384,128]{1,0:T(8,128)(2,1)S(1)} collective-permute-done((bf16[384,128]{1,0:T(8,128)(2,1)S(1)}, bf16[384,128]{1,0:T(8,128)(2,1)S(1)}, u32[]{:S(2)}, u32[]{:S(2)}) %collective-permute-start.1) | collective-permute-done | bytes 98336 | tf_op jit(solution)/shard_map/ppermute | solution.py:98
  21.7 2.3 %collective-permute-start.11 = (bf16[1616,128]{1,0:T(8,128)(2,1)S(1)}, bf16[1616,128]{1,0:T(8,128)(2,1)S(1)}, u32[]{:S(2)}, u32[]{:S(2)}) collective-permute-start(bf16[1616,128]{1,0:T(8,128)(2,1)S(1)} %pair_0.1.g0), channel_id=1, source_target_pairs={{0,3},{1,0},{2,1},{3,2},{4,7},{5,4},{6,5},{7,6},{8,11},{9,8},{10,9... | collective-permute-start | bytes 1241096 | tf_op jit(solution)/shard_map/ppermute | solution.py:98
  24.5 2.3 %collective-permute-start.4 = (bf16[384,128]{1,0:T(8,128)(2,1)S(1)}, bf16[384,128]{1,0:T(8,128)(2,1)S(1)}, u32[]{:S(2)}, u32[]{:S(2)}) collective-permute-start(bf16[384,128]{1,0:T(8,128)(2,1)S(1)} %get-tuple-element.38), channel_id=1, source_target_pairs={{0,12},{1,13},{2,14},{3,15},{4,8},{5,9},{6,10},{7,11},{8,4},{9,5},... | collective-permute-start | bytes 294920 | tf_op jit(solution)/shard_map/ppermute | solution.py:98
  26.8 2.7 %collective-permute-done.3.after1.by_x = bf16[384,128]{1,0:T(8,128)(2,1)S(1)} collective-permute-done((bf16[384,128]{1,0:T(8,128)(2,1)S(1)}, bf16[384,128]{1,0:T(8,128)(2,1)S(1)}, u32[]{:S(2)}, u32[]{:S(2)}) %collective-permute-start.3) | collective-permute-done | bytes 98336 | tf_op jit(solution)/shard_map/ppermute | solution.py:98
  29.5 1.2 collective-permute-done.4.after2.by_d
  31.4 1.7 %collective-permute-start.7 = (bf16[1600,128]{1,0:T(8,128)(2,1)S(1)}, bf16[1600,128]{1,0:T(8,128)(2,1)S(1)}, u32[]{:S(2)}, u32[]{:S(2)}) collective-permute-start(bf16[1600,128]{1,0:T(8,128)(2,1)S(1)} %get-tuple-element.39.x_own.own), channel_id=1, source_target_pairs={{0,12},{1,13},{2,14},{3,15},{4,8},{5,9},{6,10},{7,11},{8,4},{9,5},... | collective-permute-start | bytes 1228808 | tf_op jit(solution)/shard_map/ppermute | solution.py:98
  33.0 1.2 collective-permute-start.5
  34.9 7.7 %collective-permute-done.10.west.g1 = bf16[1616,128]{1,0:T(8,128)(2,1)S(1)} collective-permute-done((bf16[1616,128]{1,0:T(8,128)(2,1)S(1)}, bf16[1616,128]{1,0:T(8,128)(2,1)S(1)}, u32[]{:S(2)}, u32[]{:S(2)}) %collective-permute-start.10) | collective-permute-done | bytes 413728 | tf_op jit(solution)/shard_map/ppermute | solution.py:98
  43.2 1.9 %collective-permute-start.16 = (bf16[768,128]{1,0:T(8,128)(2,1)S(1)}, bf16[768,128]{1,0:T(8,128)(2,1)S(1)}, u32[]{:S(2)}, u32[]{:S(2)}) collective-permute-start(bf16[768,128]{1,0:T(8,128)(2,1)S(1)} %get-tuple-element.45), channel_id=1, source_target_pairs={{0,3},{1,0},{2,1},{3,2},{4,7},{5,4},{6,5},{7,6},{8,11},{9,8},{10,9... | collective-permute-start | bytes 589832 | tf_op jit(solution)/shard_map/ppermute | solution.py:98
  45.3 4.9 %collective-permute-done.6.x_y = bf16[1536,128]{1,0:T(8,128)(2,1)S(1)} collective-permute-done((bf16[1536,128]{1,0:T(8,128)(2,1)S(1)}, bf16[1536,128]{1,0:T(8,128)(2,1)S(1)}, u32[]{:S(2)}, u32[]{:S(2)}) %collective-permute-start.6) | collective-permute-done | bytes 393248 | tf_op jit(solution)/shard_map/ppermute | solution.py:98
  51.0 4.9 %lines.1 = (bf16[4,18,192,256]{3,2,1,0:T(8,128)(2,1)S(1)}, f32[27,256,512]{2,1,0:T(8,128)}) custom-call(s32[3]{0:T(128)S(1)} %pad_add_fusion.pos.refs_0_, bf16[1600,128]{1,0:T(8,128)(2,1)S(1)} %get-tuple-element.39.x_own.own, bf16[1600,128]{1,0:T(8,128)(2,1)S(1)} %collective-permute-done.5.x_x, bf16[1536,128]{1,0:T(8,128)(2,1)S(1)} %collective-permute-done.6.x_y, ...), custom_call_target="tpu_custom_call" | custom-call | bytes 1048576 | tf_op jit(solution)/shard_map/lines/pallas_call | solution.py:547
  57.1 1.0 copy-done.2
  58.9 8.6 %taps.1.held = f32[27,64,128]{2,1,0:T(8,128)S(1)} custom-call(s32[3]{0:T(128)S(1)} %pad_add_fusion.pos.refs_0_, bf16[4,18,192,256]{3,2,1,0:T(8,128)(2,1)S(1)} %get-tuple-element.44.after.xs, bf16[1616,128]{1,0:T(8,128)(2,1)S(1)} %pair_0.1.g0, bf16[1616,128]{1,0:T(8,128)(2,1)S(1)} %collective-permute-done.10.west.g1, ...), custom_call_target="tpu_custom_call" | custom-call | flops 5435817984 | bytes 11231232 | tf_op jit(solution)/shard_map/taps/pallas_call | solution.py:116
  67.5 0.9 code.1
  68.4 3.9 %collective-permute-start.28 = (bf16[1552,128]{1,0:T(8,128)(2,1)S(1)}, bf16[1552,128]{1,0:T(8,128)(2,1)S(1)}, u32[]{:S(2)}, u32[]{:S(2)}) collective-permute-start(bf16[1552,128]{1,0:T(8,128)(2,1)S(1)} %get-tuple-element.51), channel_id=1, source_target_pairs={{0,3},{1,0},{2,1},{3,2},{4,7},{5,4},{6,5},{7,6},{8,11},{9,8},{10,9... | collective-permute-start | bytes 1191944 | tf_op jit(solution)/shard_map/ppermute | solution.py:98
  72.3 1.3 collective-permute-start.20
  74.2 9.5 %field.1.after1 = bf16[4,4,48,256]{3,2,1,0:T(8,128)(2,1)} custom-call(s32[3]{0:T(128)S(1)} %pad_add_fusion.pos.refs_0_, bf16[1744,128]{1,0:T(8,128)(2,1)S(1)} %get-tuple-element.46.after.after2.after3.own.refs_1_, bf16[4,6,64,256]{3,2,1,0:T(8,128)(2,1)S(1)} %mine.1, bf16[4,6,64,256]{3,2,1,0:T(8,128)(2,1)S(1)} %collective-permute-done.18.after.theirs, ...), custom_call_target="tpu_custom_call" | custom-call | flops 10871635968 | bytes 7077888 | tf_op jit(solution)/shard_map/field/pallas_call | solution.py:595
  83.7 1.0 collective-permute-done.20.by_y.y.refs_3_
  84.7 1.0 collective-permute-done.19.by_x.x.refs_2_
  85.6 1.0 copy-done.3
  87.8 1.4 collective-permute-start.22
  89.3 1.4 collective-permute-done.27.west.refs_1_
  90.7 3.2 %collective-permute-done.22.bottom.after2.refs_5_ = bf16[848,128]{1,0:T(8,128)(2,1)S(1)} collective-permute-done((bf16[848,128]{1,0:T(8,128)(2,1)S(1)}, bf16[848,128]{1,0:T(8,128)(2,1)S(1)}, u32[]{:S(2)}, u32[]{:S(2)}) %collective-permute-start.22) | collective-permute-done | bytes 217120 | tf_op jit(solution)/shard_map/ppermute | solution.py:98
  94.5 1.5 %collective-permute-start.36 = (bf16[3104,128]{1,0:T(8,128)(2,1)S(1)}, bf16[3104,128]{1,0:T(8,128)(2,1)S(1)}, u32[]{:S(2)}, u32[]{:S(2)}) collective-permute-start(bf16[3104,128]{1,0:T(8,128)(2,1)S(1)} %get-tuple-element.54.after.after3), channel_id=1, source_target_pairs={{0,8},{1,9},{2,10},{3,11},{4,12},{5,13},{6,14},{7,15},{8,0},{9,1},... | collective-permute-start | bytes 2383880 | tf_op jit(solution)/shard_map/ppermute | solution.py:98
  96.0 0.8 collective-permute-start.35
  97.3 3.9 %collective-permute-start.24 = (bf16[832,128]{1,0:T(8,128)(2,1)S(1)}, bf16[832,128]{1,0:T(8,128)(2,1)S(1)}, u32[]{:S(2)}, u32[]{:S(2)}) collective-permute-start(bf16[832,128]{1,0:T(8,128)(2,1)S(1)} %block.1.refs_6_), channel_id=1, source_target_pairs={{0,3},{1,0},{2,1},{3,2},{4,7},{5,4},{6,5},{7,6},{8,11},{9,8},{10,9... | collective-permute-start | bytes 638984 | tf_op jit(solution)/shard_map/ppermute | solution.py:98
  101.2 1.6 %collective-permute-start.30 = (bf16[784,128]{1,0:T(8,128)(2,1)S(1)}, bf16[784,128]{1,0:T(8,128)(2,1)S(1)}, u32[]{:S(2)}, u32[]{:S(2)}) collective-permute-start(bf16[784,128]{1,0:T(8,128)(2,1)S(1)} %get-tuple-element.53), channel_id=1, source_target_pairs={{0,3},{1,0},{2,1},{3,2},{4,7},{5,4},{6,5},{7,6},{8,11},{9,8},{10,9... | collective-permute-start | bytes 602120 | tf_op jit(solution)/shard_map/ppermute | solution.py:98
  102.9 3.6 %collective-permute-done.29.half_3 = bf16[768,128]{1,0:T(8,128)(2,1)S(1)} collective-permute-done((bf16[768,128]{1,0:T(8,128)(2,1)S(1)}, bf16[768,128]{1,0:T(8,128)(2,1)S(1)}, u32[]{:S(2)}, u32[]{:S(2)}) %collective-permute-start.29) | collective-permute-done | bytes 196640 | tf_op jit(solution)/shard_map/ppermute | solution.py:98
  106.4 2.1 %collective-permute-start.23 = (bf16[832,128]{1,0:T(8,128)(2,1)S(1)}, bf16[832,128]{1,0:T(8,128)(2,1)S(1)}, u32[]{:S(2)}, u32[]{:S(2)}) collective-permute-start(bf16[832,128]{1,0:T(8,128)(2,1)S(1)} %block.1.refs_6_), channel_id=1, source_target_pairs={{0,1},{1,2},{2,3},{3,0},{4,5},{5,6},{6,7},{7,4},{8,9},{9,10},{10,1... | collective-permute-start | bytes 638984 | tf_op jit(solution)/shard_map/ppermute | solution.py:98
  108.5 4.1 %collective-permute-done.30.half_1 = bf16[784,128]{1,0:T(8,128)(2,1)S(1)} collective-permute-done((bf16[784,128]{1,0:T(8,128)(2,1)S(1)}, bf16[784,128]{1,0:T(8,128)(2,1)S(1)}, u32[]{:S(2)}, u32[]{:S(2)}) %collective-permute-start.30) | collective-permute-done | bytes 200736 | tf_op jit(solution)/shard_map/ppermute | solution.py:98
  113.2 1.3 collective-permute-start.32
  114.5 0.8 collective-permute-start.31
  115.3 5.5 %collective-permute-done.23.block_3.after2.refs_7_ = bf16[832,128]{1,0:T(8,128)(2,1)S(1)} collective-permute-done((bf16[832,128]{1,0:T(8,128)(2,1)S(1)}, bf16[832,128]{1,0:T(8,128)(2,1)S(1)}, u32[]{:S(2)}, u32[]{:S(2)}) %collective-permute-start.23) | collective-permute-done | bytes 213024 | tf_op jit(solution)/shard_map/ppermute | solution.py:98
  121.3 2.1 %collective-permute-start.26 = (bf16[416,128]{1,0:T(8,128)(2,1)S(1)}, bf16[416,128]{1,0:T(8,128)(2,1)S(1)}, u32[]{:S(2)}, u32[]{:S(2)}) collective-permute-start(bf16[416,128]{1,0:T(8,128)(2,1)S(1)} %get-tuple-element.50), channel_id=1, source_target_pairs={{0,3},{1,0},{2,1},{3,2},{4,7},{5,4},{6,5},{7,6},{8,11},{9,8},{10,9... | collective-permute-start | bytes 319496 | tf_op jit(solution)/shard_map/ppermute | solution.py:98
  124.0 1.3 collective-permute-start.37
  125.3 0.9 collective-permute-start.38
  126.2 3.1 %unpack_1.1 = (f32[27,256,512]{2,1,0:T(8,128)}, f32[8,128]{1,0:T(8,128)S(1)}) custom-call(s32[3]{0:T(128)S(1)} %pad_add_fusion.pos.refs_0_, bf16[1744,128]{1,0:T(8,128)(2,1)S(1)} %get-tuple-element.46.after.after2.after3.own.refs_1_, bf16[1744,128]{1,0:T(8,128)(2,1)S(1)} %collective-permute-done.19.by_x.x.refs_2_, ...), custom_call_target="tpu_custom_call", output_to_operand_aliasing={{0}: (7, {})} | custom-call | bytes 4194304 | tf_op jit(solution)/shard_map/unpack_1/pallas_call | solution.py:420
  129.4 3.3 %collective-permute-done.25.after2.refs_1_ = bf16[416,128]{1,0:T(8,128)(2,1)S(1)} collective-permute-done((bf16[416,128]{1,0:T(8,128)(2,1)S(1)}, bf16[416,128]{1,0:T(8,128)(2,1)S(1)}, u32[]{:S(2)}, u32[]{:S(2)}) %collective-permute-start.25) | collective-permute-done | bytes 106528 | tf_op jit(solution)/shard_map/ppermute | solution.py:98
  133.3 1.2 collective-permute-start.34
  134.5 0.8 collective-permute-start.33
  135.4 6.2 %unpack_2.1 = (f32[27,256,512]{2,1,0:T(8,128)}, f32[8,128]{1,0:T(8,128)}) custom-call(s32[3]{0:T(128)S(1)} %pad_add_fusion.pos.refs_0_, bf16[1552,128]{1,0:T(8,128)(2,1)S(1)} %collective-permute-done.27.west.refs_1_, bf16[1552,128]{1,0:T(8,128)(2,1)S(1)} %collective-permute-done.28.east.refs_2_, ...), custom_call_target="tpu_custom_call", output_to_operand_aliasing={{0}: (10, {})} | custom-call | bytes 4194304 | tf_op jit(solution)/shard_map/unpack_2/pallas_call | solution.py:420
  141.6 3.7 %unpack_3.1 = (f32[27,256,512]{2,1,0:T(8,128)}, f32[8,128]{1,0:T(8,128)}) custom-call(s32[3]{0:T(128)S(1)} %pad_add_fusion.pos.refs_0_, bf16[416,128]{1,0:T(8,128)(2,1)S(1)} %collective-permute-done.25.after2.refs_1_, bf16[416,128]{1,0:T(8,128)(2,1)S(1)} %collective-permute-done.26.after3.refs_2_, ...), custom_call_target="tpu_custom_call", output_to_operand_aliasing={{0}: (8, {})} | custom-call | bytes 4194304 | tf_op jit(solution)/shard_map/unpack_3/pallas_call | solution.py:420
  (66 shorter events, 13.0 us)
Async XLA Ops:
  0.7 1.0 copy-start.1
  1.7 1.0 copy-start.4
  3.6 17.5 %collective-permute-start.8 = (bf16[768,128]{1,0:T(8,128)(2,1)S(1)}, bf16[768,128]{1,0:T(8,128)(2,1)S(1)}, u32[]{:S(2)}, u32[]{:S(2)}) collective-permute-start(bf16[768,128]{1,0:T(8,128)(2,1)S(1)} %get-tuple-element.41), channel_id=1, source_target_pairs={{0,0},{1,1},{2,2},{3,3},{4,4},{5,5},{6,6},{7,7},{8,16},{9,17},{10,... | collective-permute-start | bytes 589832 | tf_op jit(solution)/shard_map/ppermute | solution.py:98
  4.2 16.8 %collective-permute-start.9 = (bf16[768,128]{1,0:T(8,128)(2,1)S(1)}, bf16[768,128]{1,0:T(8,128)(2,1)S(1)}, u32[]{:S(2)}, u32[]{:S(2)}) collective-permute-start(bf16[768,128]{1,0:T(8,128)(2,1)S(1)} %get-tuple-element.42), channel_id=1, source_target_pairs={{0,4},{1,5},{2,6},{3,7},{4,0},{5,1},{6,2},{7,3},{8,20},{9,21},{10,... | collective-permute-start | bytes 589832 | tf_op jit(solution)/shard_map/ppermute | solution.py:98
  7.2 13.8 %collective-permute-start = (bf16[416,128]{1,0:T(8,128)(2,1)S(1)}, bf16[416,128]{1,0:T(8,128)(2,1)S(1)}, u32[]{:S(2)}, u32[]{:S(2)}) collective-permute-start(bf16[416,128]{1,0:T(8,128)(2,1)S(1)} %get-tuple-element.34), channel_id=1, source_target_pairs={{0,1},{1,2},{2,3},{3,0},{4,5},{5,6},{6,7},{7,4},{8,9},{9,10},{10,1... | collective-permute-start | bytes 319496 | tf_op jit(solution)/shard_map/ppermute | solution.py:98
  8.8 12.2 %collective-permute-start.2 = (bf16[416,128]{1,0:T(8,128)(2,1)S(1)}, bf16[416,128]{1,0:T(8,128)(2,1)S(1)}, u32[]{:S(2)}, u32[]{:S(2)}) collective-permute-start(bf16[416,128]{1,0:T(8,128)(2,1)S(1)} %get-tuple-element.36), channel_id=1, source_target_pairs={{0,3},{1,0},{2,1},{3,2},{4,7},{5,4},{6,5},{7,6},{8,11},{9,8},{10,9... | collective-permute-start | bytes 319496 | tf_op jit(solution)/shard_map/ppermute | solution.py:98
  11.1 10.0 %collective-permute-start.1 = (bf16[384,128]{1,0:T(8,128)(2,1)S(1)}, bf16[384,128]{1,0:T(8,128)(2,1)S(1)}, u32[]{:S(2)}, u32[]{:S(2)}) collective-permute-start(bf16[384,128]{1,0:T(8,128)(2,1)S(1)} %get-tuple-element.35), channel_id=1, source_target_pairs={{0,2},{1,3},{2,0},{3,1},{4,6},{5,7},{6,4},{7,5},{8,10},{9,11},{10,... | collective-permute-start | bytes 294920 | tf_op jit(solution)/shard_map/ppermute | solution.py:98
  21.7 13.3 %collective-permute-start.11 = (bf16[1616,128]{1,0:T(8,128)(2,1)S(1)}, bf16[1616,128]{1,0:T(8,128)(2,1)S(1)}, u32[]{:S(2)}, u32[]{:S(2)}) collective-permute-start(bf16[1616,128]{1,0:T(8,128)(2,1)S(1)} %pair_0.1.g0), channel_id=1, source_target_pairs={{0,3},{1,0},{2,1},{3,2},{4,7},{5,4},{6,5},{7,6},{8,11},{9,8},{10,9... | collective-permute-start | bytes 1241096 | tf_op jit(solution)/shard_map/ppermute | solution.py:98
  23.9 18.7 %collective-permute-start.10 = (bf16[1616,128]{1,0:T(8,128)(2,1)S(1)}, bf16[1616,128]{1,0:T(8,128)(2,1)S(1)}, u32[]{:S(2)}, u32[]{:S(2)}) collective-permute-start(bf16[1616,128]{1,0:T(8,128)(2,1)S(1)} %pair_0.1.g0), channel_id=1, source_target_pairs={{0,1},{1,2},{2,3},{3,0},{4,5},{5,6},{6,7},{7,4},{8,9},{9,10},{10,1... | collective-permute-start | bytes 1241096 | tf_op jit(solution)/shard_map/ppermute | solution.py:98
  23.9 5.6 %collective-permute-start.3 = (bf16[384,128]{1,0:T(8,128)(2,1)S(1)}, bf16[384,128]{1,0:T(8,128)(2,1)S(1)}, u32[]{:S(2)}, u32[]{:S(2)}) collective-permute-start(bf16[384,128]{1,0:T(8,128)(2,1)S(1)} %get-tuple-element.37), channel_id=1, source_target_pairs={{0,4},{1,5},{2,6},{3,7},{4,0},{5,1},{6,2},{7,3},{8,12},{9,13},{10,... | collective-permute-start | bytes 294920 | tf_op jit(solution)/shard_map/ppermute | solution.py:98
  24.5 6.2 %collective-permute-start.4 = (bf16[384,128]{1,0:T(8,128)(2,1)S(1)}, bf16[384,128]{1,0:T(8,128)(2,1)S(1)}, u32[]{:S(2)}, u32[]{:S(2)}) collective-permute-start(bf16[384,128]{1,0:T(8,128)(2,1)S(1)} %get-tuple-element.38), channel_id=1, source_target_pairs={{0,12},{1,13},{2,14},{3,15},{4,8},{5,9},{6,10},{7,11},{8,4},{9,5},... | collective-permute-start | bytes 294920 | tf_op jit(solution)/shard_map/ppermute | solution.py:98
  31.4 18.8 %collective-permute-start.7 = (bf16[1600,128]{1,0:T(8,128)(2,1)S(1)}, bf16[1600,128]{1,0:T(8,128)(2,1)S(1)}, u32[]{:S(2)}, u32[]{:S(2)}) collective-permute-start(bf16[1600,128]{1,0:T(8,128)(2,1)S(1)} %get-tuple-element.39.x_own.own), channel_id=1, source_target_pairs={{0,12},{1,13},{2,14},{3,15},{4,8},{5,9},{6,10},{7,11},{8,4},{9,5},... | collective-permute-start | bytes 1228808 | tf_op jit(solution)/shard_map/ppermute | solution.py:98
  33.0 18.0 %collective-permute-start.5 = (bf16[1600,128]{1,0:T(8,128)(2,1)S(1)}, bf16[1600,128]{1,0:T(8,128)(2,1)S(1)}, u32[]{:S(2)}, u32[]{:S(2)}) collective-permute-start(bf16[1600,128]{1,0:T(8,128)(2,1)S(1)} %get-tuple-element.39.x_own.own), channel_id=1, source_target_pairs={{0,4},{1,5},{2,6},{3,7},{4,0},{5,1},{6,2},{7,3},{8,12},{9,13},{10,... | collective-permute-start | bytes 1228808 | tf_op jit(solution)/shard_map/ppermute | solution.py:98
  34.2 15.9 %collective-permute-start.6 = (bf16[1536,128]{1,0:T(8,128)(2,1)S(1)}, bf16[1536,128]{1,0:T(8,128)(2,1)S(1)}, u32[]{:S(2)}, u32[]{:S(2)}) collective-permute-start(bf16[1536,128]{1,0:T(8,128)(2,1)S(1)} %get-tuple-element.40), channel_id=1, source_target_pairs={{0,8},{1,9},{2,10},{3,11},{4,12},{5,13},{6,14},{7,15},{8,0},{9,1},... | collective-permute-start | bytes 1179656 | tf_op jit(solution)/shard_map/ppermute | solution.py:98
  43.2 12.7 %collective-permute-start.16 = (bf16[768,128]{1,0:T(8,128)(2,1)S(1)}, bf16[768,128]{1,0:T(8,128)(2,1)S(1)}, u32[]{:S(2)}, u32[]{:S(2)}) collective-permute-start(bf16[768,128]{1,0:T(8,128)(2,1)S(1)} %get-tuple-element.45), channel_id=1, source_target_pairs={{0,3},{1,0},{2,1},{3,2},{4,7},{5,4},{6,5},{7,6},{8,11},{9,8},{10,9... | collective-permute-start | bytes 589832 | tf_op jit(solution)/shard_map/ppermute | solution.py:98
  45.1 10.9 %collective-permute-start.15 = (bf16[768,128]{1,0:T(8,128)(2,1)S(1)}, bf16[768,128]{1,0:T(8,128)(2,1)S(1)}, u32[]{:S(2)}, u32[]{:S(2)}) collective-permute-start(bf16[768,128]{1,0:T(8,128)(2,1)S(1)} %get-tuple-element.43.after), channel_id=1, source_target_pairs={{0,1},{1,2},{2,3},{3,0},{4,5},{5,6},{6,7},{7,4},{8,9},{9,10},{10,1... | collective-permute-start | bytes 589832 | tf_op jit(solution)/shard_map/ppermute | solution.py:98
  50.1 8.7 %collective-permute-start.12 = (bf16[1616,128]{1,0:T(8,128)(2,1)S(1)}, bf16[1616,128]{1,0:T(8,128)(2,1)S(1)}, u32[]{:S(2)}, u32[]{:S(2)}) collective-permute-start(bf16[1616,128]{1,0:T(8,128)(2,1)S(1)} %pair_0.1.g0), channel_id=1, source_target_pairs={{0,16},{1,17},{2,18},{3,19},{4,20},{5,21},{6,22},{7,23},{8,24},{9,... | collective-permute-start | bytes 1241096 | tf_op jit(solution)/shard_map/ppermute | solution.py:98
  50.1 8.7 %collective-permute-start.14 = (bf16[1616,128]{1,0:T(8,128)(2,1)S(1)}, bf16[1616,128]{1,0:T(8,128)(2,1)S(1)}, u32[]{:S(2)}, u32[]{:S(2)}) collective-permute-start(bf16[1616,128]{1,0:T(8,128)(2,1)S(1)} %collective-permute-done.11.east.g3), channel_id=1, source_target_pairs={{0,16},{1,17},{2,18},{3,19},{4,20},{5,21},{6,22},{7,23},{8,24},{9,... | collective-permute-start | bytes 1241096 | tf_op jit(solution)/shard_map/ppermute | solution.py:98
  51.0 7.8 %collective-permute-start.13 = (bf16[1616,128]{1,0:T(8,128)(2,1)S(1)}, bf16[1616,128]{1,0:T(8,128)(2,1)S(1)}, u32[]{:S(2)}, u32[]{:S(2)}) collective-permute-start(bf16[1616,128]{1,0:T(8,128)(2,1)S(1)} %collective-permute-done.10.west.g1), channel_id=1, source_target_pairs={{0,16},{1,17},{2,18},{3,19},{4,20},{5,21},{6,22},{7,23},{8,24},{9,... | collective-permute-start | bytes 1241096 | tf_op jit(solution)/shard_map/ppermute | solution.py:98
  56.5 2.4 %collective-permute-start.17 = (bf16[2,768,128]{2,1,0:T(8,128)(2,1)S(1)}, bf16[2,768,128]{2,1,0:T(8,128)(2,1)S(1)}, u32[]{:S(2)}, u32[]{:S(2)}) collective-permute-start(bf16[2,768,128]{2,1,0:T(8,128)(2,1)S(1)} %pair.1.g2), channel_id=1, source_target_pairs={{0,16},{1,17},{2,18},{3,19},{4,20},{5,21},{6,22},{7,23},{8,24},{9,... | collective-permute-start | bytes 1179656 | tf_op jit(solution)/shard_map/ppermute | solution.py:98
  57.1 1.0 copy-start.2
  58.1 16.1 %slice-start = ((s8[7077888]{0:T(1024)(128)(4,1)}), s8[4194304]{0:T(1024)(128)(4,1)S(1)}, s32[]{:S(2)}) async-start(s8[7077888]{0:T(1024)(128)(4,1)} %bitcast.12), calls=%async_computation | async-start | bytes 8388608
  58.8 15.4 %slice-start.1 = ((s8[7077888]{0:T(1024)(128)(4,1)}), s8[2883584]{0:T(1024)(128)(4,1)S(1)}, s32[]{:S(2)}) async-start(s8[7077888]{0:T(1024)(128)(4,1)} %bitcast.12), calls=%async_computation.1 | async-start | bytes 5767168
  58.8 8.7 %collective-permute-start.18 = (bf16[4,6,64,256]{3,2,1,0:T(8,128)(2,1)S(1)}, bf16[4,6,64,256]{3,2,1,0:T(8,128)(2,1)S(1)}, u32[]{:S(2)}, u32[]{:S(2)}) collective-permute-start(bf16[4,6,64,256]{3,2,1,0:T(8,128)(2,1)S(1)} %mine.1), channel_id=1, source_target_pairs={{0,16},{1,17},{2,18},{3,19},{4,20},{5,21},{6,22},{7,23},{8,24},{9,... | collective-permute-start | bytes 2359304 | tf_op jit(solution)/shard_map/ppermute | solution.py:98
  68.4 20.9 %collective-permute-start.28 = (bf16[1552,128]{1,0:T(8,128)(2,1)S(1)}, bf16[1552,128]{1,0:T(8,128)(2,1)S(1)}, u32[]{:S(2)}, u32[]{:S(2)}) collective-permute-start(bf16[1552,128]{1,0:T(8,128)(2,1)S(1)} %get-tuple-element.51), channel_id=1, source_target_pairs={{0,3},{1,0},{2,1},{3,2},{4,7},{5,4},{6,5},{7,6},{8,11},{9,8},{10,9... | collective-permute-start | bytes 1191944 | tf_op jit(solution)/shard_map/ppermute | solution.py:98
  72.3 18.3 %collective-permute-start.27 = (bf16[1552,128]{1,0:T(8,128)(2,1)S(1)}, bf16[1552,128]{1,0:T(8,128)(2,1)S(1)}, u32[]{:S(2)}, u32[]{:S(2)}) collective-permute-start(bf16[1552,128]{1,0:T(8,128)(2,1)S(1)} %get-tuple-element.51), channel_id=1, source_target_pairs={{0,1},{1,2},{2,3},{3,0},{4,5},{5,6},{6,7},{7,4},{8,9},{9,10},{10,1... | collective-permute-start | bytes 1191944 | tf_op jit(solution)/shard_map/ppermute | solution.py:98
  72.3 12.3 %collective-permute-start.20 = (bf16[1744,128]{1,0:T(8,128)(2,1)S(1)}, bf16[1744,128]{1,0:T(8,128)(2,1)S(1)}, u32[]{:S(2)}, u32[]{:S(2)}) collective-permute-start(bf16[1744,128]{1,0:T(8,128)(2,1)S(1)} %get-tuple-element.46.after.after2.after3.own.refs_1_), channel_id=1, source_target_pairs={{0,8},{1,9},{2,10},{3,11},{4,12},{5,13},{6,14},{7,15},{8,0},{9,1},... | collective-permute-start | bytes 1339400 | tf_op jit(solution)/shard_map/ppermute | solution.py:98
  73.6 12.0 %collective-permute-start.19 = (bf16[1744,128]{1,0:T(8,128)(2,1)S(1)}, bf16[1744,128]{1,0:T(8,128)(2,1)S(1)}, u32[]{:S(2)}, u32[]{:S(2)}) collective-permute-start(bf16[1744,128]{1,0:T(8,128)(2,1)S(1)} %get-tuple-element.46.after.after2.after3.own.refs_1_), channel_id=1, source_target_pairs={{0,4},{1,5},{2,6},{3,7},{4,0},{5,1},{6,2},{7,3},{8,12},{9,13},{10,... | collective-permute-start | bytes 1339400 | tf_op jit(solution)/shard_map/ppermute | solution.py:98
  85.6 1.0 copy-start.3
  87.2 6.6 %collective-permute-start.21 = (bf16[896,128]{1,0:T(8,128)(2,1)S(1)}, bf16[896,128]{1,0:T(8,128)(2,1)S(1)}, u32[]{:S(2)}, u32[]{:S(2)}) collective-permute-start(bf16[896,128]{1,0:T(8,128)(2,1)S(1)} %get-tuple-element.47), channel_id=1, source_target_pairs={{0,4},{1,5},{2,6},{3,7},{4,0},{5,1},{6,2},{7,3},{8,12},{9,13},{10,... | collective-permute-start | bytes 688136 | tf_op jit(solution)/shard_map/ppermute | solution.py:98
  87.8 6.0 %collective-permute-start.22 = (bf16[848,128]{1,0:T(8,128)(2,1)S(1)}, bf16[848,128]{1,0:T(8,128)(2,1)S(1)}, u32[]{:S(2)}, u32[]{:S(2)}) collective-permute-start(bf16[848,128]{1,0:T(8,128)(2,1)S(1)} %get-tuple-element.48), channel_id=1, source_target_pairs={{0,8},{1,9},{2,10},{3,11},{4,12},{5,13},{6,14},{7,15},{8,0},{9,1},... | collective-permute-start | bytes 651272 | tf_op jit(solution)/shard_map/ppermute | solution.py:98
  94.5 28.9 %collective-permute-start.36 = (bf16[3104,128]{1,0:T(8,128)(2,1)S(1)}, bf16[3104,128]{1,0:T(8,128)(2,1)S(1)}, u32[]{:S(2)}, u32[]{:S(2)}) collective-permute-start(bf16[3104,128]{1,0:T(8,128)(2,1)S(1)} %get-tuple-element.54.after.after3), channel_id=1, source_target_pairs={{0,8},{1,9},{2,10},{3,11},{4,12},{5,13},{6,14},{7,15},{8,0},{9,1},... | collective-permute-start | bytes 2383880 | tf_op jit(solution)/shard_map/ppermute | solution.py:98
  96.0 27.5 %collective-permute-start.35 = (bf16[3104,128]{1,0:T(8,128)(2,1)S(1)}, bf16[3104,128]{1,0:T(8,128)(2,1)S(1)}, u32[]{:S(2)}, u32[]{:S(2)}) collective-permute-start(bf16[3104,128]{1,0:T(8,128)(2,1)S(1)} %get-tuple-element.54.after.after3), channel_id=1, source_target_pairs={{0,4},{1,5},{2,6},{3,7},{4,0},{5,1},{6,2},{7,3},{8,12},{9,13},{10,... | collective-permute-start | bytes 2383880 | tf_op jit(solution)/shard_map/ppermute | solution.py:98
  96.8 9.6 %collective-permute-start.29 = (bf16[768,128]{1,0:T(8,128)(2,1)S(1)}, bf16[768,128]{1,0:T(8,128)(2,1)S(1)}, u32[]{:S(2)}, u32[]{:S(2)}) collective-permute-start(bf16[768,128]{1,0:T(8,128)(2,1)S(1)} %get-tuple-element.52), channel_id=1, source_target_pairs={{0,1},{1,2},{2,3},{3,0},{4,5},{5,6},{6,7},{7,4},{8,9},{9,10},{10,1... | collective-permute-start | bytes 589832 | tf_op jit(solution)/shard_map/ppermute | solution.py:98
  97.3 17.2 %collective-permute-start.24 = (bf16[832,128]{1,0:T(8,128)(2,1)S(1)}, bf16[832,128]{1,0:T(8,128)(2,1)S(1)}, u32[]{:S(2)}, u32[]{:S(2)}) collective-permute-start(bf16[832,128]{1,0:T(8,128)(2,1)S(1)} %block.1.refs_6_), channel_id=1, source_target_pairs={{0,3},{1,0},{2,1},{3,2},{4,7},{5,4},{6,5},{7,6},{8,11},{9,8},{10,9... | collective-permute-start | bytes 638984 | tf_op jit(solution)/shard_map/ppermute | solution.py:98
  101.2 11.4 %collective-permute-start.30 = (bf16[784,128]{1,0:T(8,128)(2,1)S(1)}, bf16[784,128]{1,0:T(8,128)(2,1)S(1)}, u32[]{:S(2)}, u32[]{:S(2)}) collective-permute-start(bf16[784,128]{1,0:T(8,128)(2,1)S(1)} %get-tuple-element.53), channel_id=1, source_target_pairs={{0,3},{1,0},{2,1},{3,2},{4,7},{5,4},{6,5},{7,6},{8,11},{9,8},{10,9... | collective-permute-start | bytes 602120 | tf_op jit(solution)/shard_map/ppermute | solution.py:98
  106.4 14.4 %collective-permute-start.23 = (bf16[832,128]{1,0:T(8,128)(2,1)S(1)}, bf16[832,128]{1,0:T(8,128)(2,1)S(1)}, u32[]{:S(2)}, u32[]{:S(2)}) collective-permute-start(bf16[832,128]{1,0:T(8,128)(2,1)S(1)} %block.1.refs_6_), channel_id=1, source_target_pairs={{0,1},{1,2},{2,3},{3,0},{4,5},{5,6},{6,7},{7,4},{8,9},{9,10},{10,1... | collective-permute-start | bytes 638984 | tf_op jit(solution)/shard_map/ppermute | solution.py:98
  113.2 19.5 %collective-permute-start.32 = (bf16[1552,128]{1,0:T(8,128)(2,1)S(1)}, bf16[1552,128]{1,0:T(8,128)(2,1)S(1)}, u32[]{:S(2)}, u32[]{:S(2)}) collective-permute-start(bf16[1552,128]{1,0:T(8,128)(2,1)S(1)} %across.1.refs_3_), channel_id=1, source_target_pairs={{0,8},{1,9},{2,10},{3,11},{4,12},{5,13},{6,14},{7,15},{8,0},{9,1},... | collective-permute-start | bytes 1191944 | tf_op jit(solution)/shard_map/ppermute | solution.py:98
  114.5 18.2 %collective-permute-start.31 = (bf16[1552,128]{1,0:T(8,128)(2,1)S(1)}, bf16[1552,128]{1,0:T(8,128)(2,1)S(1)}, u32[]{:S(2)}, u32[]{:S(2)}) collective-permute-start(bf16[1552,128]{1,0:T(8,128)(2,1)S(1)} %across.1.refs_3_), channel_id=1, source_target_pairs={{0,4},{1,5},{2,6},{3,7},{4,0},{5,1},{6,2},{7,3},{8,12},{9,13},{10,... | collective-permute-start | bytes 1191944 | tf_op jit(solution)/shard_map/ppermute | solution.py:98
  121.3 4.9 %collective-permute-start.26 = (bf16[416,128]{1,0:T(8,128)(2,1)S(1)}, bf16[416,128]{1,0:T(8,128)(2,1)S(1)}, u32[]{:S(2)}, u32[]{:S(2)}) collective-permute-start(bf16[416,128]{1,0:T(8,128)(2,1)S(1)} %get-tuple-element.50), channel_id=1, source_target_pairs={{0,3},{1,0},{2,1},{3,2},{4,7},{5,4},{6,5},{7,6},{8,11},{9,8},{10,9... | collective-permute-start | bytes 319496 | tf_op jit(solution)/shard_map/ppermute | solution.py:98
  123.4 11.9 %copy-start = (bf16[3104,128]{1,0:T(8,128)(2,1)}, bf16[3104,128]{1,0:T(8,128)(2,1)S(1)}, u32[]{:S(2)}) copy-start(bf16[3104,128]{1,0:T(8,128)(2,1)S(1)} %collective-permute-done.36.by_y.refs_4_) | copy-start | bytes 2383876
  124.0 11.3 %collective-permute-start.37 = (bf16[1552,128]{1,0:T(8,128)(2,1)S(1)}, bf16[1552,128]{1,0:T(8,128)(2,1)S(1)}, u32[]{:S(2)}, u32[]{:S(2)}) collective-permute-start(bf16[1552,128]{1,0:T(8,128)(2,1)S(1)} %get-tuple-element.59), channel_id=1, source_target_pairs={{0,4},{1,5},{2,6},{3,7},{4,0},{5,1},{6,2},{7,3},{8,12},{9,13},{10,... | collective-permute-start | bytes 1191944 | tf_op jit(solution)/shard_map/ppermute | solution.py:98
  125.3 10.0 %collective-permute-start.38 = (bf16[1552,128]{1,0:T(8,128)(2,1)S(1)}, bf16[1552,128]{1,0:T(8,128)(2,1)S(1)}, u32[]{:S(2)}, u32[]{:S(2)}) collective-permute-start(bf16[1552,128]{1,0:T(8,128)(2,1)S(1)} %get-tuple-element.60), channel_id=1, source_target_pairs={{0,8},{1,9},{2,10},{3,11},{4,12},{5,13},{6,14},{7,15},{8,0},{9,1},... | collective-permute-start | bytes 1191944 | tf_op jit(solution)/shard_map/ppermute | solution.py:98
  126.2 6.5 %collective-permute-start.25 = (bf16[416,128]{1,0:T(8,128)(2,1)S(1)}, bf16[416,128]{1,0:T(8,128)(2,1)S(1)}, u32[]{:S(2)}, u32[]{:S(2)}) collective-permute-start(bf16[416,128]{1,0:T(8,128)(2,1)S(1)} %get-tuple-element.49.refs_9_), channel_id=1, source_target_pairs={{0,1},{1,2},{2,3},{3,0},{4,5},{5,6},{6,7},{7,4},{8,9},{9,10},{10,1... | collective-permute-start | bytes 319496 | tf_op jit(solution)/shard_map/ppermute | solution.py:98
  133.3 8.3 %collective-permute-start.34 = (bf16[784,128]{1,0:T(8,128)(2,1)S(1)}, bf16[784,128]{1,0:T(8,128)(2,1)S(1)}, u32[]{:S(2)}, u32[]{:S(2)}) collective-permute-start(bf16[784,128]{1,0:T(8,128)(2,1)S(1)} %get-tuple-element.58), channel_id=1, source_target_pairs={{0,8},{1,9},{2,10},{3,11},{4,12},{5,13},{6,14},{7,15},{8,0},{9,1},... | collective-permute-start | bytes 602120 | tf_op jit(solution)/shard_map/ppermute | solution.py:98
  134.5 7.1 %collective-permute-start.33 = (bf16[768,128]{1,0:T(8,128)(2,1)S(1)}, bf16[768,128]{1,0:T(8,128)(2,1)S(1)}, u32[]{:S(2)}, u32[]{:S(2)}) collective-permute-start(bf16[768,128]{1,0:T(8,128)(2,1)S(1)} %get-tuple-element.57), channel_id=1, source_target_pairs={{0,4},{1,5},{2,6},{3,7},{4,0},{5,1},{6,2},{7,3},{8,12},{9,13},{10,... | collective-permute-start | bytes 589832 | tf_op jit(solution)/shard_map/ppermute | solution.py:98

commit v22 on v12

--- a/solution.py
+++ b/solution.py
@@ -155,8 +155,8 @@
             out[at * line : (at + 1) * line, :] = facing[:, at * wide : (at + 1) * wide]
 
 
-def spread_kernel(pos, x0, x1, x2, x3, own, own_y):
-    del pos
+def spread_kernel(pos, x0, x1, x2, x3, after1, after2, own, own_y):
+    del pos, after1, after2
     many = x0.shape[0]
     for at, piece in enumerate((x0, x1, x2, x3)):
         own[at * many : (at + 1) * many, :] = piece[0:many, :]
@@ -166,15 +166,15 @@
     own[4 * many + extra :, :] = x3[many:, :]
 
 
-def split_kernel(
-    pos, here, west, east, g, own, x_x, x_d, by_x, by_d, after, first, second, near, mine
-):
+def split_kernel(pos, west, east, first, second):
+    del pos
+    many = first.shape[0]
+    first[...] = west[0:many, :]
+    second[...] = east[many : 2 * many, :]
+
+
+def mine_kernel(pos, g, own, x_x, x_d, by_x, by_d, after, mine):
     del after
-    first[...] = west[0]
-    second[...] = east[1]
-    for at, part in enumerate((here, west, east)):
-        near[2 * at : 2 * at + 2] = part[...]
-
     levels, height, width, chans = g.shape
     edge, line, wide = levels * height, levels * width, chans // 2
     inner = own.shape[0] - 4 * edge
@@ -225,6 +225,14 @@
     del pos, after
     both[0] = one[...]
     both[1] = two[...]
+
+
+def first_pair_kernel(pos, one, two, after1, after2, after3, both):
+    del pos, after1, after2, after3
+    many = one.shape[0]
+    both[0:many, :] = one[...]
+    both[many : 2 * many, :] = two[...]
+    both[2 * many :, :] = jnp.zeros((both.shape[0] - 2 * many, both.shape[1]), both.dtype)
 
 
 def lines_kernel(pos, x_own, x_x, x_y, x_d, after, xs, blank):
@@ -268,15 +276,19 @@
         ] = block.T
 
 
-def taps_kernel(pos, xs, g, s, g2, s2, out, gt, acc):
+def taps_kernel(pos, xs, g0, g1, g3, s0, s1, s3, g2, s2, out, gt, acc):
     levels, rows, circle, lanes = xs.shape
     rows, width, span = rows - 2, circle // 4, lanes // 4
     filters = gt.shape[0] // levels
     deep = rows * width
     right = lax.rem(pos[1], 2)
-    for core, parts, last in ((pos[0], g, g2), (1 - pos[0], s, s2)):
-        for slot, (ref, at) in enumerate(((parts, 0), (parts, 4), (last, 0), (parts, 2))):
-            turn(gt, slot, core, ref[at + right], ref[at + 1 - right], levels)
+    many = g2.shape[1]
+    for core, parts, last in ((pos[0], (g0, g3, g1), g2), (1 - pos[0], (s0, s3, s1), s2)):
+        for slot, part in zip((0, 1, 3), parts):
+            first = part[pl.ds(pl.multiple_of(right * many, many), many), :]
+            second = part[pl.ds(pl.multiple_of((1 - right) * many, many), many), :]
+            turn(gt, slot, core, first, second, levels)
+        turn(gt, 2, core, last[right], last[1 - right], levels)
     acc[...] = jnp.zeros_like(acc)
 
     @pl.loop(0, 3)
@@ -494,41 +506,34 @@
 
     inner = 4 * many
     (g0,) = call(
-        pair_kernel, [jax.ShapeDtypeStruct((2, cells, wide), bf16)], (pos, g_s, g_o, x0), [], 0, "pair_0", 16, held=1
+        first_pair_kernel,
+        [jax.ShapeDtypeStruct((2 * cells + 80, wide), bf16)],
+        (pos, g_s, g_o, x_r1, x_r2, x_r3),
+        [],
+        0,
+        "pair_0",
+        16,
+        held=3,
     )
     x_own, x_own_y = call(
         spread_kernel,
         [jax.ShapeDtypeStruct((count, 2 * span), bf16) for count in (inner + 4 * edge, inner)],
-        (pos, x0, x_r1, x_r2, x_r3),
+        (pos, x0, x_r1, x_r2, x_r3, by_x, by_d),
         [],
         0,
         "spread",
         16,
+        held=2,
     )
     x_x = move(x_own, lat_xor(1))
     x_d = move(x_own, lat_xor(3))
     x_y = move(x_own_y, lat_xor(2))
     g1 = move(g0, lon_by(1))
     g3 = move(g0, lon_by(-1))
-    far_a, far_b, g_near, mine = call(
-        split_kernel,
-        [
-            block,
-            block,
-            jax.ShapeDtypeStruct((6, cells, wide), bf16),
-            jax.ShapeDtypeStruct((levels, height + 2, width + 16, chans), bf16),
-        ],
-        (pos, g0, g1, g3, g_cells, x_own, x_x, x_d, by_x, by_d, x_y),
-        [],
-        0,
-        "split",
-        16,
-        held=1,
-    )
+    far_a, far_b = call(split_kernel, [block, block], (pos, g1, g3), [], 0, "split", 16)
     g2a = move(far_a, lon_by(1))
     g2b = move(far_b, lon_by(-1))
-    s_near = move(g_near, sibling)
-    theirs = move(mine, sibling)
+    s0, s1, s3 = move(g0, sibling), move(g1, sibling), move(g3, sibling)
     xs, total = pl.pallas_call(
         lines_kernel,
         out_shape=[
@@ -543,6 +548,17 @@
         compiler_params=pltpu.CompilerParams(vmem_limit_bytes=24 * 1024 * 1024),
         name="lines",
     )(pos, x_own, x_x, x_y, x_d, far_a)
+    (mine,) = call(
+        mine_kernel,
+        [jax.ShapeDtypeStruct((levels, height + 2, width + 16, chans), bf16)],
+        (pos, g_cells, x_own, x_x, x_d, by_x, by_d, xs),
+        [],
+        0,
+        "mine",
+        16,
+        held=1,
+    )
+    theirs = move(mine, sibling)
     (g2,) = call(
         pair_kernel, [jax.ShapeDtypeStruct((2, cells, wide), bf16)], (pos, g2a, g2b, xs), [], 0, "pair", 16, held=1
     )
@@ -557,7 +573,7 @@
     (grads,) = call(
         taps_kernel,
         [jax.ShapeDtypeStruct((27, span, wide), f32)],
-        (pos, xs, g_near, s_near, g2, s2),
+        (pos, xs, g0, g1, g3, s0, s1, s3, g2, s2),
         [VMEM((levels * wide, rows * circle), bf16), VMEM((3, 3 * wide, 4 * span), f32)],
         2 * 27 * span * wide * rows * circle * levels,
         "taps",

time: 147 us -> 148 us (level)
  waiting for transfers between devices: 51 us -> 52.5 us
    ppermute x34 -> x36, waiting for transfers between devices: 51 us -> 52.5 us  [move(): return lax.ppermute(x, AXES, pairs)]
    ppermute x34 -> x36, starting transfers between devices: 47.7 us -> 47 us  [move(): return lax.ppermute(x, AXES, pairs)]
    pallas_call x10 -> x11, Pallas kernels: 14.6 us -> 15.1 us  [call(): pl.pallas_call(kernel, out_shape=outs, in_specs=[pl.BlockSpec(memory_spac...]
  transfers between devices with their start and end apart: 34 -> 36, of which waited for: 13 -> 10; matrix products, arithmetic and copies ran while one was open for 0% -> 0% of each run, Pallas kernels for 25% -> 25%
where the time goes in v22:
time: 148 us
  waiting for transfers between devices  52.5 us (35%)
  starting transfers between devices  47 us (32%)
  Pallas kernels  43.4 us (29%)
  local copies, waits for them, and re-layouts  4.01 us (3%)
    ppermute x36, waiting for transfers between devices, move(): return lax.ppermute(x, AXES, pairs)  52.5 us
    ppermute x36, starting transfers between devices, move(): return lax.ppermute(x, AXES, pairs)  47 us
    pallas_call x11, Pallas kernels, call(): pl.pallas_call(kernel, out_shape=outs, in_specs=[pl.BlockSpec(memory_spac...  15.1 us
    pallas_call x3, Pallas kernels, unpack(): pl.pallas_call(lambda *refs: unpack_kernel(*refs, slabs=slabs, count=len(...  13.9 us
    pallas_call x1, Pallas kernels, blocked_body(): pl.pallas_call(field_kernel, out_shape=jax.ShapeDtypeStruct((levels, heig...  9.5 us
    pallas_call x1, Pallas kernels, blocked_body(): pl.pallas_call(lines_kernel, out_shape=[jax.ShapeDtypeStruct((levels, row...  4.86 us
    unnamed x20, local copies, waits for them, and re-layouts  4.01 us
  transfers between devices with their start and end apart: 36, of which 10 were waited for; matrix products, arithmetic and copies ran while one was open for 0% of the time, Pallas kernels for 25%

profile of v22, /device:TPU:0, one launch (start us, length us, event | category | flops | bytes accessed | tf_op | source)
XLA Modules:
  0.0 148.0 jit_solution(11350991724149395521)
XLA Ops:
  0.7 1.0 copy-done.1
  1.7 1.0 copy-done.3
  2.7 0.8 pack.1
  3.6 0.7 collective-permute-start.8
  4.2 3.0 %collective-permute-start.9 = (bf16[768,128]{1,0:T(8,128)(2,1)S(1)}, bf16[768,128]{1,0:T(8,128)(2,1)S(1)}, u32[]{:S(2)}, u32[]{:S(2)}) collective-permute-start(bf16[768,128]{1,0:T(8,128)(2,1)S(1)} %get-tuple-element.39), channel_id=1, source_target_pairs={{0,4},{1,5},{2,6},{3,7},{4,0},{5,1},{6,2},{7,3},{8,20},{9,21},{10,... | collective-permute-start | bytes 589832 | tf_op jit(solution)/shard_map/ppermute | solution.py:98
  7.2 1.6 %collective-permute-start = (bf16[416,128]{1,0:T(8,128)(2,1)S(1)}, bf16[416,128]{1,0:T(8,128)(2,1)S(1)}, u32[]{:S(2)}, u32[]{:S(2)}) collective-permute-start(bf16[416,128]{1,0:T(8,128)(2,1)S(1)} %get-tuple-element.31), channel_id=1, source_target_pairs={{0,1},{1,2},{2,3},{3,0},{4,5},{5,6},{6,7},{7,4},{8,9},{9,10},{10,1... | collective-permute-start | bytes 319496 | tf_op jit(solution)/shard_map/ppermute | solution.py:98
  8.8 2.2 %collective-permute-start.2 = (bf16[416,128]{1,0:T(8,128)(2,1)S(1)}, bf16[416,128]{1,0:T(8,128)(2,1)S(1)}, u32[]{:S(2)}, u32[]{:S(2)}) collective-permute-start(bf16[416,128]{1,0:T(8,128)(2,1)S(1)} %get-tuple-element.33), channel_id=1, source_target_pairs={{0,3},{1,0},{2,1},{3,2},{4,7},{5,4},{6,5},{7,6},{8,11},{9,8},{10,9... | collective-permute-start | bytes 319496 | tf_op jit(solution)/shard_map/ppermute | solution.py:98
  11.1 0.8 collective-permute-start.1
  11.9 9.2 %collective-permute-done.1.x2.after2 = bf16[384,128]{1,0:T(8,128)(2,1)S(1)} collective-permute-done((bf16[384,128]{1,0:T(8,128)(2,1)S(1)}, bf16[384,128]{1,0:T(8,128)(2,1)S(1)}, u32[]{:S(2)}, u32[]{:S(2)}) %collective-permute-start.1) | collective-permute-done | bytes 98336 | tf_op jit(solution)/shard_map/ppermute | solution.py:98
  21.7 3.8 %collective-permute-start.11 = (bf16[1616,128]{1,0:T(8,128)(2,1)S(1)}, bf16[1616,128]{1,0:T(8,128)(2,1)S(1)}, u32[]{:S(2)}, u32[]{:S(2)}) collective-permute-start(bf16[1616,128]{1,0:T(8,128)(2,1)S(1)} %pair_0.1.g0), channel_id=1, source_target_pairs={{0,3},{1,0},{2,1},{3,2},{4,7},{5,4},{6,5},{7,6},{8,11},{9,8},{10,9... | collective-permute-start | bytes 1241096 | tf_op jit(solution)/shard_map/ppermute | solution.py:98
  25.6 2.0 %collective-permute-start.4 = (bf16[384,128]{1,0:T(8,128)(2,1)S(1)}, bf16[384,128]{1,0:T(8,128)(2,1)S(1)}, u32[]{:S(2)}, u32[]{:S(2)}) collective-permute-start(bf16[384,128]{1,0:T(8,128)(2,1)S(1)} %get-tuple-element.35), channel_id=1, source_target_pairs={{0,12},{1,13},{2,14},{3,15},{4,8},{5,9},{6,10},{7,11},{8,4},{9,5},... | collective-permute-start | bytes 294920 | tf_op jit(solution)/shard_map/ppermute | solution.py:98
  27.6 3.3 %collective-permute-done.3.after1.by_x = bf16[384,128]{1,0:T(8,128)(2,1)S(1)} collective-permute-done((bf16[384,128]{1,0:T(8,128)(2,1)S(1)}, bf16[384,128]{1,0:T(8,128)(2,1)S(1)}, u32[]{:S(2)}, u32[]{:S(2)}) %collective-permute-start.3) | collective-permute-done | bytes 98336 | tf_op jit(solution)/shard_map/ppermute | solution.py:98
  30.9 1.0 collective-permute-done.4.after2.by_d
  31.9 0.6 spread.1
  32.5 1.3 collective-permute-start.5
  33.8 1.8 %collective-permute-start.7 = (bf16[1600,128]{1,0:T(8,128)(2,1)S(1)}, bf16[1600,128]{1,0:T(8,128)(2,1)S(1)}, u32[]{:S(2)}, u32[]{:S(2)}) collective-permute-start(bf16[1600,128]{1,0:T(8,128)(2,1)S(1)} %get-tuple-element.36.x_own.own), channel_id=1, source_target_pairs={{0,12},{1,13},{2,14},{3,15},{4,8},{5,9},{6,10},{7,11},{8,4},{9,5},... | collective-permute-start | bytes 1228808 | tf_op jit(solution)/shard_map/ppermute | solution.py:98
  36.1 6.2 %collective-permute-done.11.east.g3 = bf16[1616,128]{1,0:T(8,128)(2,1)S(1)} collective-permute-done((bf16[1616,128]{1,0:T(8,128)(2,1)S(1)}, bf16[1616,128]{1,0:T(8,128)(2,1)S(1)}, u32[]{:S(2)}, u32[]{:S(2)}) %collective-permute-start.11) | collective-permute-done | bytes 413728 | tf_op jit(solution)/shard_map/ppermute | solution.py:98
  42.8 1.3 collective-permute-start.15
  44.1 2.6 %collective-permute-start.16 = (bf16[768,128]{1,0:T(8,128)(2,1)S(1)}, bf16[768,128]{1,0:T(8,128)(2,1)S(1)}, u32[]{:S(2)}, u32[]{:S(2)}) collective-permute-start(bf16[768,128]{1,0:T(8,128)(2,1)S(1)} %get-tuple-element.42), channel_id=1, source_target_pairs={{0,3},{1,0},{2,1},{3,2},{4,7},{5,4},{6,5},{7,6},{8,11},{9,8},{10,9... | collective-permute-start | bytes 589832 | tf_op jit(solution)/shard_map/ppermute | solution.py:98
  46.7 6.8 %collective-permute-done.6.x_y = bf16[1536,128]{1,0:T(8,128)(2,1)S(1)} collective-permute-done((bf16[1536,128]{1,0:T(8,128)(2,1)S(1)}, bf16[1536,128]{1,0:T(8,128)(2,1)S(1)}, u32[]{:S(2)}, u32[]{:S(2)}) %collective-permute-start.6) | collective-permute-done | bytes 393248 | tf_op jit(solution)/shard_map/ppermute | solution.py:98
  54.1 4.9 %lines.1 = (bf16[4,18,192,256]{3,2,1,0:T(8,128)(2,1)S(1)}, f32[27,256,512]{2,1,0:T(8,128)}) custom-call(s32[3]{0:T(128)S(1)} %pad_add_fusion.pos.refs_0_, bf16[1600,128]{1,0:T(8,128)(2,1)S(1)} %get-tuple-element.36.x_own.own, bf16[1600,128]{1,0:T(8,128)(2,1)S(1)} %collective-permute-done.5.x_x, bf16[1536,128]{1,0:T(8,128)(2,1)S(1)} %collective-permute-done.6.x_y, ...), custom_call_target="tpu_custom_call" | custom-call | bytes 1048576 | tf_op jit(solution)/shard_map/lines/pallas_call | solution.py:537
  60.0 1.0 copy-done.2
  61.0 0.7 mine.1
  61.9 8.6 %taps.1.held = f32[27,64,128]{2,1,0:T(8,128)S(1)} custom-call(s32[3]{0:T(128)S(1)} %pad_add_fusion.pos.refs_0_, bf16[4,18,192,256]{3,2,1,0:T(8,128)(2,1)S(1)} %get-tuple-element.41.after.xs, bf16[1616,128]{1,0:T(8,128)(2,1)S(1)} %pair_0.1.g0, bf16[1616,128]{1,0:T(8,128)(2,1)S(1)} %collective-permute-done.10.west.g1, ...), custom_call_target="tpu_custom_call" | custom-call | flops 5435817984 | bytes 11231232 | tf_op jit(solution)/shard_map/taps/pallas_call | solution.py:116
  70.5 0.9 code.1
  71.5 3.8 %collective-permute-start.20 = (bf16[1296,128]{1,0:T(8,128)(2,1)S(1)}, bf16[1296,128]{1,0:T(8,128)(2,1)S(1)}, u32[]{:S(2)}, u32[]{:S(2)}) collective-permute-start(bf16[1296,128]{1,0:T(8,128)(2,1)S(1)} %get-tuple-element.44), channel_id=1, source_target_pairs={{0,3},{1,0},{2,1},{3,2},{4,7},{5,4},{6,5},{7,6},{8,11},{9,8},{10,9... | collective-permute-start | bytes 995336 | tf_op jit(solution)/shard_map/ppermute | solution.py:98
  75.3 0.7 collective-permute-start.23
  75.9 1.2 collective-permute-start.24
  77.1 1.6 %collective-permute-start.25 = (bf16[1232,128]{1,0:T(8,128)(2,1)S(1)}, bf16[1232,128]{1,0:T(8,128)(2,1)S(1)}, u32[]{:S(2)}, u32[]{:S(2)}) collective-permute-start(bf16[1232,128]{1,0:T(8,128)(2,1)S(1)} %get-tuple-element.43.after.own.refs_1_.refs_9_), channel_id=1, source_target_pairs={{0,12},{1,13},{2,14},{3,15},{4,8},{5,9},{6,10},{7,11},{8,4},{9,5},... | collective-permute-start | bytes 946184 | tf_op jit(solution)/shard_map/ppermute | solution.py:98
  78.8 9.5 %field.1.after = bf16[4,4,48,256]{3,2,1,0:T(8,128)(2,1)} custom-call(s32[3]{0:T(128)S(1)} %pad_add_fusion.pos.refs_0_, bf16[1232,128]{1,0:T(8,128)(2,1)S(1)} %get-tuple-element.43.after.own.refs_1_.refs_9_, bf16[4,6,64,256]{3,2,1,0:T(8,128)(2,1)S(1)} %mine.1, bf16[4,6,64,256]{3,2,1,0:T(8,128)(2,1)S(1)} %collective-permute-done.18.after.theirs, ...), custom_call_target="tpu_custom_call" | custom-call | flops 10871635968 | bytes 7077888 | tf_op jit(solution)/shard_map/field/pallas_call | solution.py:594
  88.8 1.0 copy-done.4
  89.8 0.6 both.1
  90.4 0.8 collective-permute-start.33
  91.2 1.2 collective-permute-start.34
  92.3 1.6 %collective-permute-start.35 = (bf16[3104,128]{1,0:T(8,128)(2,1)S(1)}, bf16[3104,128]{1,0:T(8,128)(2,1)S(1)}, u32[]{:S(2)}, u32[]{:S(2)}) collective-permute-start(bf16[3104,128]{1,0:T(8,128)(2,1)S(1)} %get-tuple-element.54), channel_id=1, source_target_pairs={{0,12},{1,13},{2,14},{3,15},{4,8},{5,9},{6,10},{7,11},{8,4},{9,5},... | collective-permute-start | bytes 2383880 | tf_op jit(solution)/shard_map/ppermute | solution.py:98
  94.0 2.0 %collective-permute-start.22 = (bf16[656,128]{1,0:T(8,128)(2,1)S(1)}, bf16[656,128]{1,0:T(8,128)(2,1)S(1)}, u32[]{:S(2)}, u32[]{:S(2)}) collective-permute-start(bf16[656,128]{1,0:T(8,128)(2,1)S(1)} %get-tuple-element.47), channel_id=1, source_target_pairs={{0,3},{1,0},{2,1},{3,2},{4,7},{5,4},{6,5},{7,6},{8,11},{9,8},{10,9... | collective-permute-start | bytes 503816 | tf_op jit(solution)/shard_map/ppermute | solution.py:98
  96.0 8.4 %collective-permute-done.21.half_3 = bf16[640,128]{1,0:T(8,128)(2,1)S(1)} collective-permute-done((bf16[640,128]{1,0:T(8,128)(2,1)S(1)}, bf16[640,128]{1,0:T(8,128)(2,1)S(1)}, u32[]{:S(2)}, u32[]{:S(2)}) %collective-permute-start.21) | collective-permute-done | bytes 163872 | tf_op jit(solution)/shard_map/ppermute | solution.py:98
  104.4 0.6 across.1
  105.4 3.5 %collective-permute-start.27 = (bf16[1856,128]{1,0:T(8,128)(2,1)S(1)}, bf16[1856,128]{1,0:T(8,128)(2,1)S(1)}, u32[]{:S(2)}, u32[]{:S(2)}) collective-permute-start(bf16[1856,128]{1,0:T(8,128)(2,1)S(1)} %get-tuple-element.48.refs_5_), channel_id=1, source_target_pairs={{0,3},{1,0},{2,1},{3,2},{4,7},{5,4},{6,5},{7,6},{8,11},{9,8},{10,9... | collective-permute-start | bytes 1425416 | tf_op jit(solution)/shard_map/ppermute | solution.py:98
  108.9 11.8 %collective-permute-done.26.block_3.refs_4_ = bf16[1856,128]{1,0:T(8,128)(2,1)S(1)} collective-permute-done((bf16[1856,128]{1,0:T(8,128)(2,1)S(1)}, bf16[1856,128]{1,0:T(8,128)(2,1)S(1)}, u32[]{:S(2)}, u32[]{:S(2)}) %collective-permute-start.26) | collective-permute-done | bytes 475168 | tf_op jit(solution)/shard_map/ppermute | solution.py:98
  120.7 0.7 collective-permute-start.30
  121.4 4.8 %collective-permute-done.27.block_1.refs_5_ = bf16[1856,128]{1,0:T(8,128)(2,1)S(1)} collective-permute-done((bf16[1856,128]{1,0:T(8,128)(2,1)S(1)}, bf16[1856,128]{1,0:T(8,128)(2,1)S(1)}, u32[]{:S(2)}, u32[]{:S(2)}) %collective-permute-start.27) | collective-permute-done | bytes 475168 | tf_op jit(solution)/shard_map/ppermute | solution.py:98
  126.7 1.7 %collective-permute-start.32 = (bf16[1296,128]{1,0:T(8,128)(2,1)S(1)}, bf16[1296,128]{1,0:T(8,128)(2,1)S(1)}, u32[]{:S(2)}, u32[]{:S(2)}) collective-permute-start(bf16[1296,128]{1,0:T(8,128)(2,1)S(1)} %get-tuple-element.53.refs_3_), channel_id=1, source_target_pairs={{0,12},{1,13},{2,14},{3,15},{4,8},{5,9},{6,10},{7,11},{8,4},{9,5},... | collective-permute-start | bytes 995336 | tf_op jit(solution)/shard_map/ppermute | solution.py:98
  128.4 2.5 %unpack_1.1 = (f32[27,256,512]{2,1,0:T(8,128)}, f32[8,128]{1,0:T(8,128)S(1)}) custom-call(s32[3]{0:T(128)S(1)} %pad_add_fusion.pos.refs_0_, bf16[1232,128]{1,0:T(8,128)(2,1)S(1)} %get-tuple-element.43.after.own.refs_1_.refs_9_, bf16[1232,128]{1,0:T(8,128)(2,1)S(1)} %collective-permute-done.23.x.refs_2_.refs_10_, ...), custom_call_target="tpu_custom_call", output_to_operand_aliasing={{0}: (6, {})} | custom-call | bytes 4194304 | tf_op jit(solution)/shard_map/unpack_1/pallas_call | solution.py:410
  131.5 1.9 %collective-permute-start.28 = (bf16[928,128]{1,0:T(8,128)(2,1)S(1)}, bf16[928,128]{1,0:T(8,128)(2,1)S(1)}, u32[]{:S(2)}, u32[]{:S(2)}) collective-permute-start(bf16[928,128]{1,0:T(8,128)(2,1)S(1)} %get-tuple-element.51.refs_13_), channel_id=1, source_target_pairs={{0,1},{1,2},{2,3},{3,0},{4,5},{5,6},{6,7},{7,4},{8,9},{9,10},{10,1... | collective-permute-start | bytes 712712 | tf_op jit(solution)/shard_map/ppermute | solution.py:98
  133.4 2.5 %collective-permute-start.29 = (bf16[928,128]{1,0:T(8,128)(2,1)S(1)}, bf16[928,128]{1,0:T(8,128)(2,1)S(1)}, u32[]{:S(2)}, u32[]{:S(2)}) collective-permute-start(bf16[928,128]{1,0:T(8,128)(2,1)S(1)} %get-tuple-element.52), channel_id=1, source_target_pairs={{0,3},{1,0},{2,1},{3,2},{4,7},{5,4},{6,5},{7,6},{8,11},{9,8},{10,9... | collective-permute-start | bytes 712712 | tf_op jit(solution)/shard_map/ppermute | solution.py:98
  135.9 7.6 %unpack_2.1 = (f32[27,256,512]{2,1,0:T(8,128)}, f32[8,128]{1,0:T(8,128)}) custom-call(s32[3]{0:T(128)S(1)} %pad_add_fusion.pos.refs_0_, bf16[3104,128]{1,0:T(8,128)(2,1)} %copy-done.5, bf16[3104,128]{1,0:T(8,128)(2,1)} %copy-done.6, bf16[3104,128]{1,0:T(8,128)(2,1)} %copy-done.7, ...), custom_call_target="tpu_custom_call", output_to_operand_aliasing={{0}: (14, {})} | custom-call | bytes 4194304 | tf_op jit(solution)/shard_map/unpack_2/pallas_call | solution.py:410
  144.0 3.8 %unpack_3.1 = (f32[27,256,512]{2,1,0:T(8,128)}, f32[8,128]{1,0:T(8,128)}) custom-call(s32[3]{0:T(128)S(1)} %pad_add_fusion.pos.refs_0_, bf16[928,128]{1,0:T(8,128)(2,1)S(1)} %collective-permute-done.28.refs_1_, bf16[928,128]{1,0:T(8,128)(2,1)S(1)} %collective-permute-done.29.refs_2_, ...), custom_call_target="tpu_custom_call", output_to_operand_aliasing={{0}: (7, {})} | custom-call | bytes 4194304 | tf_op jit(solution)/shard_map/unpack_3/pallas_call | solution.py:410
  (62 shorter events, 6.2 us)
Async XLA Ops:
  0.7 1.0 copy-start.1
  1.7 1.0 copy-start.3
  3.6 17.5 %collective-permute-start.8 = (bf16[768,128]{1,0:T(8,128)(2,1)S(1)}, bf16[768,128]{1,0:T(8,128)(2,1)S(1)}, u32[]{:S(2)}, u32[]{:S(2)}) collective-permute-start(bf16[768,128]{1,0:T(8,128)(2,1)S(1)} %get-tuple-element.38), channel_id=1, source_target_pairs={{0,0},{1,1},{2,2},{3,3},{4,4},{5,5},{6,6},{7,7},{8,16},{9,17},{10,... | collective-permute-start | bytes 589832 | tf_op jit(solution)/shard_map/ppermute | solution.py:98
  4.2 16.8 %collective-permute-start.9 = (bf16[768,128]{1,0:T(8,128)(2,1)S(1)}, bf16[768,128]{1,0:T(8,128)(2,1)S(1)}, u32[]{:S(2)}, u32[]{:S(2)}) collective-permute-start(bf16[768,128]{1,0:T(8,128)(2,1)S(1)} %get-tuple-element.39), channel_id=1, source_target_pairs={{0,4},{1,5},{2,6},{3,7},{4,0},{5,1},{6,2},{7,3},{8,20},{9,21},{10,... | collective-permute-start | bytes 589832 | tf_op jit(solution)/shard_map/ppermute | solution.py:98
  7.2 13.8 %collective-permute-start = (bf16[416,128]{1,0:T(8,128)(2,1)S(1)}, bf16[416,128]{1,0:T(8,128)(2,1)S(1)}, u32[]{:S(2)}, u32[]{:S(2)}) collective-permute-start(bf16[416,128]{1,0:T(8,128)(2,1)S(1)} %get-tuple-element.31), channel_id=1, source_target_pairs={{0,1},{1,2},{2,3},{3,0},{4,5},{5,6},{6,7},{7,4},{8,9},{9,10},{10,1... | collective-permute-start | bytes 319496 | tf_op jit(solution)/shard_map/ppermute | solution.py:98
  8.8 12.2 %collective-permute-start.2 = (bf16[416,128]{1,0:T(8,128)(2,1)S(1)}, bf16[416,128]{1,0:T(8,128)(2,1)S(1)}, u32[]{:S(2)}, u32[]{:S(2)}) collective-permute-start(bf16[416,128]{1,0:T(8,128)(2,1)S(1)} %get-tuple-element.33), channel_id=1, source_target_pairs={{0,3},{1,0},{2,1},{3,2},{4,7},{5,4},{6,5},{7,6},{8,11},{9,8},{10,9... | collective-permute-start | bytes 319496 | tf_op jit(solution)/shard_map/ppermute | solution.py:98
  11.1 10.0 %collective-permute-start.1 = (bf16[384,128]{1,0:T(8,128)(2,1)S(1)}, bf16[384,128]{1,0:T(8,128)(2,1)S(1)}, u32[]{:S(2)}, u32[]{:S(2)}) collective-permute-start(bf16[384,128]{1,0:T(8,128)(2,1)S(1)} %get-tuple-element.32), channel_id=1, source_target_pairs={{0,2},{1,3},{2,0},{3,1},{4,6},{5,7},{6,4},{7,5},{8,10},{9,11},{10,... | collective-permute-start | bytes 294920 | tf_op jit(solution)/shard_map/ppermute | solution.py:98
  21.7 14.4 %collective-permute-start.10 = (bf16[1616,128]{1,0:T(8,128)(2,1)S(1)}, bf16[1616,128]{1,0:T(8,128)(2,1)S(1)}, u32[]{:S(2)}, u32[]{:S(2)}) collective-permute-start(bf16[1616,128]{1,0:T(8,128)(2,1)S(1)} %pair_0.1.g0), channel_id=1, source_target_pairs={{0,1},{1,2},{2,3},{3,0},{4,5},{5,6},{6,7},{7,4},{8,9},{9,10},{10,1... | collective-permute-start | bytes 1241096 | tf_op jit(solution)/shard_map/ppermute | solution.py:98
  21.7 20.5 %collective-permute-start.11 = (bf16[1616,128]{1,0:T(8,128)(2,1)S(1)}, bf16[1616,128]{1,0:T(8,128)(2,1)S(1)}, u32[]{:S(2)}, u32[]{:S(2)}) collective-permute-start(bf16[1616,128]{1,0:T(8,128)(2,1)S(1)} %pair_0.1.g0), channel_id=1, source_target_pairs={{0,3},{1,0},{2,1},{3,2},{4,7},{5,4},{6,5},{7,6},{8,11},{9,8},{10,9... | collective-permute-start | bytes 1241096 | tf_op jit(solution)/shard_map/ppermute | solution.py:98
  25.5 5.3 %collective-permute-start.3 = (bf16[384,128]{1,0:T(8,128)(2,1)S(1)}, bf16[384,128]{1,0:T(8,128)(2,1)S(1)}, u32[]{:S(2)}, u32[]{:S(2)}) collective-permute-start(bf16[384,128]{1,0:T(8,128)(2,1)S(1)} %get-tuple-element.34), channel_id=1, source_target_pairs={{0,4},{1,5},{2,6},{3,7},{4,0},{5,1},{6,2},{7,3},{8,12},{9,13},{10,... | collective-permute-start | bytes 294920 | tf_op jit(solution)/shard_map/ppermute | solution.py:98
  25.6 6.2 %collective-permute-start.4 = (bf16[384,128]{1,0:T(8,128)(2,1)S(1)}, bf16[384,128]{1,0:T(8,128)(2,1)S(1)}, u32[]{:S(2)}, u32[]{:S(2)}) collective-permute-start(bf16[384,128]{1,0:T(8,128)(2,1)S(1)} %get-tuple-element.35), channel_id=1, source_target_pairs={{0,12},{1,13},{2,14},{3,15},{4,8},{5,9},{6,10},{7,11},{8,4},{9,5},... | collective-permute-start | bytes 294920 | tf_op jit(solution)/shard_map/ppermute | solution.py:98
  32.5 21.0 %collective-permute-start.5 = (bf16[1600,128]{1,0:T(8,128)(2,1)S(1)}, bf16[1600,128]{1,0:T(8,128)(2,1)S(1)}, u32[]{:S(2)}, u32[]{:S(2)}) collective-permute-start(bf16[1600,128]{1,0:T(8,128)(2,1)S(1)} %get-tuple-element.36.x_own.own), channel_id=1, source_target_pairs={{0,4},{1,5},{2,6},{3,7},{4,0},{5,1},{6,2},{7,3},{8,12},{9,13},{10,... | collective-permute-start | bytes 1228808 | tf_op jit(solution)/shard_map/ppermute | solution.py:98
  33.8 20.2 %collective-permute-start.7 = (bf16[1600,128]{1,0:T(8,128)(2,1)S(1)}, bf16[1600,128]{1,0:T(8,128)(2,1)S(1)}, u32[]{:S(2)}, u32[]{:S(2)}) collective-permute-start(bf16[1600,128]{1,0:T(8,128)(2,1)S(1)} %get-tuple-element.36.x_own.own), channel_id=1, source_target_pairs={{0,12},{1,13},{2,14},{3,15},{4,8},{5,9},{6,10},{7,11},{8,4},{9,5},... | collective-permute-start | bytes 1228808 | tf_op jit(solution)/shard_map/ppermute | solution.py:98
  35.6 17.9 %collective-permute-start.6 = (bf16[1536,128]{1,0:T(8,128)(2,1)S(1)}, bf16[1536,128]{1,0:T(8,128)(2,1)S(1)}, u32[]{:S(2)}, u32[]{:S(2)}) collective-permute-start(bf16[1536,128]{1,0:T(8,128)(2,1)S(1)} %get-tuple-element.37), channel_id=1, source_target_pairs={{0,8},{1,9},{2,10},{3,11},{4,12},{5,13},{6,14},{7,15},{8,0},{9,1},... | collective-permute-start | bytes 1179656 | tf_op jit(solution)/shard_map/ppermute | solution.py:98
  42.8 16.1 %collective-permute-start.15 = (bf16[768,128]{1,0:T(8,128)(2,1)S(1)}, bf16[768,128]{1,0:T(8,128)(2,1)S(1)}, u32[]{:S(2)}, u32[]{:S(2)}) collective-permute-start(bf16[768,128]{1,0:T(8,128)(2,1)S(1)} %get-tuple-element.40.after), channel_id=1, source_target_pairs={{0,1},{1,2},{2,3},{3,0},{4,5},{5,6},{6,7},{7,4},{8,9},{9,10},{10,1... | collective-permute-start | bytes 589832 | tf_op jit(solution)/shard_map/ppermute | solution.py:98
  44.1 14.9 %collective-permute-start.16 = (bf16[768,128]{1,0:T(8,128)(2,1)S(1)}, bf16[768,128]{1,0:T(8,128)(2,1)S(1)}, u32[]{:S(2)}, u32[]{:S(2)}) collective-permute-start(bf16[768,128]{1,0:T(8,128)(2,1)S(1)} %get-tuple-element.42), channel_id=1, source_target_pairs={{0,3},{1,0},{2,1},{3,2},{4,7},{5,4},{6,5},{7,6},{8,11},{9,8},{10,9... | collective-permute-start | bytes 589832 | tf_op jit(solution)/shard_map/ppermute | solution.py:98
  53.5 8.4 %collective-permute-start.12 = (bf16[1616,128]{1,0:T(8,128)(2,1)S(1)}, bf16[1616,128]{1,0:T(8,128)(2,1)S(1)}, u32[]{:S(2)}, u32[]{:S(2)}) collective-permute-start(bf16[1616,128]{1,0:T(8,128)(2,1)S(1)} %pair_0.1.g0), channel_id=1, source_target_pairs={{0,16},{1,17},{2,18},{3,19},{4,20},{5,21},{6,22},{7,23},{8,24},{9,... | collective-permute-start | bytes 1241096 | tf_op jit(solution)/shard_map/ppermute | solution.py:98
  53.5 8.4 %collective-permute-start.13 = (bf16[1616,128]{1,0:T(8,128)(2,1)S(1)}, bf16[1616,128]{1,0:T(8,128)(2,1)S(1)}, u32[]{:S(2)}, u32[]{:S(2)}) collective-permute-start(bf16[1616,128]{1,0:T(8,128)(2,1)S(1)} %collective-permute-done.10.west.g1), channel_id=1, source_target_pairs={{0,16},{1,17},{2,18},{3,19},{4,20},{5,21},{6,22},{7,23},{8,24},{9,... | collective-permute-start | bytes 1241096 | tf_op jit(solution)/shard_map/ppermute | solution.py:98
  54.0 7.9 %collective-permute-start.14 = (bf16[1616,128]{1,0:T(8,128)(2,1)S(1)}, bf16[1616,128]{1,0:T(8,128)(2,1)S(1)}, u32[]{:S(2)}, u32[]{:S(2)}) collective-permute-start(bf16[1616,128]{1,0:T(8,128)(2,1)S(1)} %collective-permute-done.11.east.g3), channel_id=1, source_target_pairs={{0,16},{1,17},{2,18},{3,19},{4,20},{5,21},{6,22},{7,23},{8,24},{9,... | collective-permute-start | bytes 1241096 | tf_op jit(solution)/shard_map/ppermute | solution.py:98
  59.5 2.3 %collective-permute-start.17 = (bf16[2,768,128]{2,1,0:T(8,128)(2,1)S(1)}, bf16[2,768,128]{2,1,0:T(8,128)(2,1)S(1)}, u32[]{:S(2)}, u32[]{:S(2)}) collective-permute-start(bf16[2,768,128]{2,1,0:T(8,128)(2,1)S(1)} %pair.1.g2), channel_id=1, source_target_pairs={{0,16},{1,17},{2,18},{3,19},{4,20},{5,21},{6,22},{7,23},{8,24},{9,... | collective-permute-start | bytes 1179656 | tf_op jit(solution)/shard_map/ppermute | solution.py:98
  60.0 1.0 copy-start.2
  61.0 17.7 %slice-start = ((s8[7077888]{0:T(1024)(128)(4,1)}), s8[4194304]{0:T(1024)(128)(4,1)S(1)}, s32[]{:S(2)}) async-start(s8[7077888]{0:T(1024)(128)(4,1)} %bitcast.12), calls=%async_computation | async-start | bytes 8388608
  61.7 17.0 %slice-start.1 = ((s8[7077888]{0:T(1024)(128)(4,1)}), s8[2883584]{0:T(1024)(128)(4,1)S(1)}, s32[]{:S(2)}) async-start(s8[7077888]{0:T(1024)(128)(4,1)} %bitcast.12), calls=%async_computation.1 | async-start | bytes 5767168
  61.7 8.7 %collective-permute-start.18 = (bf16[4,6,64,256]{3,2,1,0:T(8,128)(2,1)S(1)}, bf16[4,6,64,256]{3,2,1,0:T(8,128)(2,1)S(1)}, u32[]{:S(2)}, u32[]{:S(2)}) collective-permute-start(bf16[4,6,64,256]{3,2,1,0:T(8,128)(2,1)S(1)} %mine.1), channel_id=1, source_target_pairs={{0,16},{1,17},{2,18},{3,19},{4,20},{5,21},{6,22},{7,23},{8,24},{9,... | collective-permute-start | bytes 2359304 | tf_op jit(solution)/shard_map/ppermute | solution.py:98
  71.4 16.9 %collective-permute-start.19 = (bf16[1296,128]{1,0:T(8,128)(2,1)S(1)}, bf16[1296,128]{1,0:T(8,128)(2,1)S(1)}, u32[]{:S(2)}, u32[]{:S(2)}) collective-permute-start(bf16[1296,128]{1,0:T(8,128)(2,1)S(1)} %get-tuple-element.44), channel_id=1, source_target_pairs={{0,1},{1,2},{2,3},{3,0},{4,5},{5,6},{6,7},{7,4},{8,9},{9,10},{10,1... | collective-permute-start | bytes 995336 | tf_op jit(solution)/shard_map/ppermute | solution.py:98
  71.5 17.3 %collective-permute-start.20 = (bf16[1296,128]{1,0:T(8,128)(2,1)S(1)}, bf16[1296,128]{1,0:T(8,128)(2,1)S(1)}, u32[]{:S(2)}, u32[]{:S(2)}) collective-permute-start(bf16[1296,128]{1,0:T(8,128)(2,1)S(1)} %get-tuple-element.44), channel_id=1, source_target_pairs={{0,3},{1,0},{2,1},{3,2},{4,7},{5,4},{6,5},{7,6},{8,11},{9,8},{10,9... | collective-permute-start | bytes 995336 | tf_op jit(solution)/shard_map/ppermute | solution.py:98
  75.3 17.1 %collective-permute-start.23 = (bf16[1232,128]{1,0:T(8,128)(2,1)S(1)}, bf16[1232,128]{1,0:T(8,128)(2,1)S(1)}, u32[]{:S(2)}, u32[]{:S(2)}) collective-permute-start(bf16[1232,128]{1,0:T(8,128)(2,1)S(1)} %get-tuple-element.43.after.own.refs_1_.refs_9_), channel_id=1, source_target_pairs={{0,4},{1,5},{2,6},{3,7},{4,0},{5,1},{6,2},{7,3},{8,12},{9,13},{10,... | collective-permute-start | bytes 946184 | tf_op jit(solution)/shard_map/ppermute | solution.py:98
  75.9 18.0 %collective-permute-start.24 = (bf16[1232,128]{1,0:T(8,128)(2,1)S(1)}, bf16[1232,128]{1,0:T(8,128)(2,1)S(1)}, u32[]{:S(2)}, u32[]{:S(2)}) collective-permute-start(bf16[1232,128]{1,0:T(8,128)(2,1)S(1)} %get-tuple-element.43.after.own.refs_1_.refs_9_), channel_id=1, source_target_pairs={{0,8},{1,9},{2,10},{3,11},{4,12},{5,13},{6,14},{7,15},{8,0},{9,1},... | collective-permute-start | bytes 946184 | tf_op jit(solution)/shard_map/ppermute | solution.py:98
  77.1 18.8 %collective-permute-start.25 = (bf16[1232,128]{1,0:T(8,128)(2,1)S(1)}, bf16[1232,128]{1,0:T(8,128)(2,1)S(1)}, u32[]{:S(2)}, u32[]{:S(2)}) collective-permute-start(bf16[1232,128]{1,0:T(8,128)(2,1)S(1)} %get-tuple-element.43.after.own.refs_1_.refs_9_), channel_id=1, source_target_pairs={{0,12},{1,13},{2,14},{3,15},{4,8},{5,9},{6,10},{7,11},{8,4},{9,5},... | collective-permute-start | bytes 946184 | tf_op jit(solution)/shard_map/ppermute | solution.py:98
  88.8 1.0 copy-start.4
  90.4 36.3 %collective-permute-start.33 = (bf16[3104,128]{1,0:T(8,128)(2,1)S(1)}, bf16[3104,128]{1,0:T(8,128)(2,1)S(1)}, u32[]{:S(2)}, u32[]{:S(2)}) collective-permute-start(bf16[3104,128]{1,0:T(8,128)(2,1)S(1)} %get-tuple-element.54), channel_id=1, source_target_pairs={{0,4},{1,5},{2,6},{3,7},{4,0},{5,1},{6,2},{7,3},{8,12},{9,13},{10,... | collective-permute-start | bytes 2383880 | tf_op jit(solution)/shard_map/ppermute | solution.py:98
  91.2 40.3 %collective-permute-start.34 = (bf16[3104,128]{1,0:T(8,128)(2,1)S(1)}, bf16[3104,128]{1,0:T(8,128)(2,1)S(1)}, u32[]{:S(2)}, u32[]{:S(2)}) collective-permute-start(bf16[3104,128]{1,0:T(8,128)(2,1)S(1)} %get-tuple-element.54), channel_id=1, source_target_pairs={{0,8},{1,9},{2,10},{3,11},{4,12},{5,13},{6,14},{7,15},{8,0},{9,1},... | collective-permute-start | bytes 2383880 | tf_op jit(solution)/shard_map/ppermute | solution.py:98
  92.3 41.1 %collective-permute-start.35 = (bf16[3104,128]{1,0:T(8,128)(2,1)S(1)}, bf16[3104,128]{1,0:T(8,128)(2,1)S(1)}, u32[]{:S(2)}, u32[]{:S(2)}) collective-permute-start(bf16[3104,128]{1,0:T(8,128)(2,1)S(1)} %get-tuple-element.54), channel_id=1, source_target_pairs={{0,12},{1,13},{2,14},{3,15},{4,8},{5,9},{6,10},{7,11},{8,4},{9,5},... | collective-permute-start | bytes 2383880 | tf_op jit(solution)/shard_map/ppermute | solution.py:98
  94.0 10.5 %collective-permute-start.22 = (bf16[656,128]{1,0:T(8,128)(2,1)S(1)}, bf16[656,128]{1,0:T(8,128)(2,1)S(1)}, u32[]{:S(2)}, u32[]{:S(2)}) collective-permute-start(bf16[656,128]{1,0:T(8,128)(2,1)S(1)} %get-tuple-element.47), channel_id=1, source_target_pairs={{0,3},{1,0},{2,1},{3,2},{4,7},{5,4},{6,5},{7,6},{8,11},{9,8},{10,9... | collective-permute-start | bytes 503816 | tf_op jit(solution)/shard_map/ppermute | solution.py:98
  96.0 8.4 %collective-permute-start.21 = (bf16[640,128]{1,0:T(8,128)(2,1)S(1)}, bf16[640,128]{1,0:T(8,128)(2,1)S(1)}, u32[]{:S(2)}, u32[]{:S(2)}) collective-permute-start(bf16[640,128]{1,0:T(8,128)(2,1)S(1)} %get-tuple-element.46), channel_id=1, source_target_pairs={{0,1},{1,2},{2,3},{3,0},{4,5},{5,6},{6,7},{7,4},{8,9},{9,10},{10,1... | collective-permute-start | bytes 491528 | tf_op jit(solution)/shard_map/ppermute | solution.py:98
  105.0 15.7 %collective-permute-start.26 = (bf16[1856,128]{1,0:T(8,128)(2,1)S(1)}, bf16[1856,128]{1,0:T(8,128)(2,1)S(1)}, u32[]{:S(2)}, u32[]{:S(2)}) collective-permute-start(bf16[1856,128]{1,0:T(8,128)(2,1)S(1)} %get-tuple-element.48.refs_5_), channel_id=1, source_target_pairs={{0,1},{1,2},{2,3},{3,0},{4,5},{5,6},{6,7},{7,4},{8,9},{9,10},{10,1... | collective-permute-start | bytes 1425416 | tf_op jit(solution)/shard_map/ppermute | solution.py:98
  105.4 20.8 %collective-permute-start.27 = (bf16[1856,128]{1,0:T(8,128)(2,1)S(1)}, bf16[1856,128]{1,0:T(8,128)(2,1)S(1)}, u32[]{:S(2)}, u32[]{:S(2)}) collective-permute-start(bf16[1856,128]{1,0:T(8,128)(2,1)S(1)} %get-tuple-element.48.refs_5_), channel_id=1, source_target_pairs={{0,3},{1,0},{2,1},{3,2},{4,7},{5,4},{6,5},{7,6},{8,11},{9,8},{10,9... | collective-permute-start | bytes 1425416 | tf_op jit(solution)/shard_map/ppermute | solution.py:98
  120.7 22.9 %collective-permute-start.30 = (bf16[1296,128]{1,0:T(8,128)(2,1)S(1)}, bf16[1296,128]{1,0:T(8,128)(2,1)S(1)}, u32[]{:S(2)}, u32[]{:S(2)}) collective-permute-start(bf16[1296,128]{1,0:T(8,128)(2,1)S(1)} %get-tuple-element.53.refs_3_), channel_id=1, source_target_pairs={{0,4},{1,5},{2,6},{3,7},{4,0},{5,1},{6,2},{7,3},{8,12},{9,13},{10,... | collective-permute-start | bytes 995336 | tf_op jit(solution)/shard_map/ppermute | solution.py:98
  126.2 9.7 %copy-start = (bf16[1856,128]{1,0:T(8,128)(2,1)}, bf16[1856,128]{1,0:T(8,128)(2,1)S(1)}, u32[]{:S(2)}) copy-start(bf16[1856,128]{1,0:T(8,128)(2,1)S(1)} %collective-permute-done.27.block_1.refs_5_) | copy-start | bytes 1425412
  126.2 17.3 %collective-permute-start.31 = (bf16[1296,128]{1,0:T(8,128)(2,1)S(1)}, bf16[1296,128]{1,0:T(8,128)(2,1)S(1)}, u32[]{:S(2)}, u32[]{:S(2)}) collective-permute-start(bf16[1296,128]{1,0:T(8,128)(2,1)S(1)} %get-tuple-element.53.refs_3_), channel_id=1, source_target_pairs={{0,8},{1,9},{2,10},{3,11},{4,12},{5,13},{6,14},{7,15},{8,0},{9,1},... | collective-permute-start | bytes 995336 | tf_op jit(solution)/shard_map/ppermute | solution.py:98
  126.7 9.2 %copy-start.5 = (bf16[3104,128]{1,0:T(8,128)(2,1)}, bf16[3104,128]{1,0:T(8,128)(2,1)S(1)}, u32[]{:S(2)}) copy-start(bf16[3104,128]{1,0:T(8,128)(2,1)S(1)} %collective-permute-done.33.refs_1_) | copy-start | bytes 2383876
  126.7 16.8 %collective-permute-start.32 = (bf16[1296,128]{1,0:T(8,128)(2,1)S(1)}, bf16[1296,128]{1,0:T(8,128)(2,1)S(1)}, u32[]{:S(2)}, u32[]{:S(2)}) collective-permute-start(bf16[1296,128]{1,0:T(8,128)(2,1)S(1)} %get-tuple-element.53.refs_3_), channel_id=1, source_target_pairs={{0,12},{1,13},{2,14},{3,15},{4,8},{5,9},{6,10},{7,11},{8,4},{9,5},... | collective-permute-start | bytes 995336 | tf_op jit(solution)/shard_map/ppermute | solution.py:98
  131.5 4.4 %copy-start.6 = (bf16[3104,128]{1,0:T(8,128)(2,1)}, bf16[3104,128]{1,0:T(8,128)(2,1)S(1)}, u32[]{:S(2)}) copy-start(bf16[3104,128]{1,0:T(8,128)(2,1)S(1)} %collective-permute-done.34.refs_2_) | copy-start | bytes 2383876
  131.5 12.1 %collective-permute-start.28 = (bf16[928,128]{1,0:T(8,128)(2,1)S(1)}, bf16[928,128]{1,0:T(8,128)(2,1)S(1)}, u32[]{:S(2)}, u32[]{:S(2)}) collective-permute-start(bf16[928,128]{1,0:T(8,128)(2,1)S(1)} %get-tuple-element.51.refs_13_), channel_id=1, source_target_pairs={{0,1},{1,2},{2,3},{3,0},{4,5},{5,6},{6,7},{7,4},{8,9},{9,10},{10,1... | collective-permute-start | bytes 712712 | tf_op jit(solution)/shard_map/ppermute | solution.py:98
  133.4 2.5 %copy-start.7 = (bf16[3104,128]{1,0:T(8,128)(2,1)}, bf16[3104,128]{1,0:T(8,128)(2,1)S(1)}, u32[]{:S(2)}) copy-start(bf16[3104,128]{1,0:T(8,128)(2,1)S(1)} %collective-permute-done.35.refs_3_) | copy-start | bytes 2383876
  133.4 10.6 %collective-permute-start.29 = (bf16[928,128]{1,0:T(8,128)(2,1)S(1)}, bf16[928,128]{1,0:T(8,128)(2,1)S(1)}, u32[]{:S(2)}, u32[]{:S(2)}) collective-permute-start(bf16[928,128]{1,0:T(8,128)(2,1)S(1)} %get-tuple-element.52), channel_id=1, source_target_pairs={{0,3},{1,0},{2,1},{3,2},{4,7},{5,4},{6,5},{7,6},{8,11},{9,8},{10,9... | collective-permute-start | bytes 712712 | tf_op jit(solution)/shard_map/ppermute | solution.py:98

commit v23 on v21

--- a/solution.py
+++ b/solution.py
@@ -573,7 +573,7 @@
         pair_kernel, [jax.ShapeDtypeStruct((2, cells, wide), bf16)], (pos, g2a, g2b, xs), [], 0, "pair", 16, held=1
     )
     s2 = move(g2, sibling)
-    early = 3
+    early = 2
     cut, end = early * span, 27 * span
     size = end + 16 - cut
     half = size // 32 * 16

time: 146 us -> 146 us (level)
  no operation moved by 1% of the time
where the time goes in v23:
time: 146 us
  waiting for transfers between devices  49.8 us (34%)
  starting transfers between devices  46 us (32%)
  Pallas kernels  45 us (31%)
  local copies, waits for them, and re-layouts  4 us (3%)
    ppermute x39, waiting for transfers between devices, move(): return lax.ppermute(x, AXES, pairs)  49.8 us
    ppermute x39, starting transfers between devices, move(): return lax.ppermute(x, AXES, pairs)  46 us
    pallas_call x15, Pallas kernels, call(): pl.pallas_call(kernel, out_shape=outs, in_specs=[pl.BlockSpec(memory_spac...  17.4 us
    pallas_call x3, Pallas kernels, unpack(): pl.pallas_call(lambda *refs: unpack_kernel(*refs, slabs=slabs, count=len(...  13.2 us
    pallas_call x1, Pallas kernels, blocked_body(): pl.pallas_call(field_kernel, out_shape=jax.ShapeDtypeStruct((levels, heig...  9.5 us
    pallas_call x1, Pallas kernels, blocked_body(): pl.pallas_call(lines_kernel, out_shape=[jax.ShapeDtypeStruct((levels, row...  4.87 us
    unnamed x14, local copies, waits for them, and re-layouts  4 us
  transfers between devices with their start and end apart: 39, of which 14 were waited for; matrix products, arithmetic and copies ran while one was open for 0% of the time, Pallas kernels for 26%

profile of v23, /device:TPU:0, one launch (start us, length us, event | category | flops | bytes accessed | tf_op | source)
XLA Modules:
  0.0 145.9 jit_solution(12698976203619902461)
XLA Ops:
  0.7 1.0 copy-done.1
  1.7 1.0 copy-done.4
  2.7 0.8 pack.1
  4.2 3.0 %collective-permute-start.9 = (bf16[768,128]{1,0:T(8,128)(2,1)S(1)}, bf16[768,128]{1,0:T(8,128)(2,1)S(1)}, u32[]{:S(2)}, u32[]{:S(2)}) collective-permute-start(bf16[768,128]{1,0:T(8,128)(2,1)S(1)} %get-tuple-element.42), channel_id=1, source_target_pairs={{0,4},{1,5},{2,6},{3,7},{4,0},{5,1},{6,2},{7,3},{8,20},{9,21},{10,... | collective-permute-start | bytes 589832 | tf_op jit(solution)/shard_map/ppermute | solution.py:98
  7.2 1.6 %collective-permute-start = (bf16[416,128]{1,0:T(8,128)(2,1)S(1)}, bf16[416,128]{1,0:T(8,128)(2,1)S(1)}, u32[]{:S(2)}, u32[]{:S(2)}) collective-permute-start(bf16[416,128]{1,0:T(8,128)(2,1)S(1)} %get-tuple-element.34), channel_id=1, source_target_pairs={{0,1},{1,2},{2,3},{3,0},{4,5},{5,6},{6,7},{7,4},{8,9},{9,10},{10,1... | collective-permute-start | bytes 319496 | tf_op jit(solution)/shard_map/ppermute | solution.py:98
  8.8 2.2 %collective-permute-start.2 = (bf16[416,128]{1,0:T(8,128)(2,1)S(1)}, bf16[416,128]{1,0:T(8,128)(2,1)S(1)}, u32[]{:S(2)}, u32[]{:S(2)}) collective-permute-start(bf16[416,128]{1,0:T(8,128)(2,1)S(1)} %get-tuple-element.36), channel_id=1, source_target_pairs={{0,3},{1,0},{2,1},{3,2},{4,7},{5,4},{6,5},{7,6},{8,11},{9,8},{10,9... | collective-permute-start | bytes 319496 | tf_op jit(solution)/shard_map/ppermute | solution.py:98
  11.1 0.8 collective-permute-start.1
  11.9 9.2 %collective-permute-done.1.x2.after2 = bf16[384,128]{1,0:T(8,128)(2,1)S(1)} collective-permute-done((bf16[384,128]{1,0:T(8,128)(2,1)S(1)}, bf16[384,128]{1,0:T(8,128)(2,1)S(1)}, u32[]{:S(2)}, u32[]{:S(2)}) %collective-permute-start.1) | collective-permute-done | bytes 98336 | tf_op jit(solution)/shard_map/ppermute | solution.py:98
  21.7 2.3 %collective-permute-start.11 = (bf16[1616,128]{1,0:T(8,128)(2,1)S(1)}, bf16[1616,128]{1,0:T(8,128)(2,1)S(1)}, u32[]{:S(2)}, u32[]{:S(2)}) collective-permute-start(bf16[1616,128]{1,0:T(8,128)(2,1)S(1)} %pair_0.1.g0), channel_id=1, source_target_pairs={{0,3},{1,0},{2,1},{3,2},{4,7},{5,4},{6,5},{7,6},{8,11},{9,8},{10,9... | collective-permute-start | bytes 1241096 | tf_op jit(solution)/shard_map/ppermute | solution.py:98
  24.5 2.3 %collective-permute-start.4 = (bf16[384,128]{1,0:T(8,128)(2,1)S(1)}, bf16[384,128]{1,0:T(8,128)(2,1)S(1)}, u32[]{:S(2)}, u32[]{:S(2)}) collective-permute-start(bf16[384,128]{1,0:T(8,128)(2,1)S(1)} %get-tuple-element.38), channel_id=1, source_target_pairs={{0,12},{1,13},{2,14},{3,15},{4,8},{5,9},{6,10},{7,11},{8,4},{9,5},... | collective-permute-start | bytes 294920 | tf_op jit(solution)/shard_map/ppermute | solution.py:98
  26.8 2.7 %collective-permute-done.3.after1.by_x = bf16[384,128]{1,0:T(8,128)(2,1)S(1)} collective-permute-done((bf16[384,128]{1,0:T(8,128)(2,1)S(1)}, bf16[384,128]{1,0:T(8,128)(2,1)S(1)}, u32[]{:S(2)}, u32[]{:S(2)}) %collective-permute-start.3) | collective-permute-done | bytes 98336 | tf_op jit(solution)/shard_map/ppermute | solution.py:98
  29.5 1.2 collective-permute-done.4.after2.by_d
  31.4 1.7 %collective-permute-start.7 = (bf16[1600,128]{1,0:T(8,128)(2,1)S(1)}, bf16[1600,128]{1,0:T(8,128)(2,1)S(1)}, u32[]{:S(2)}, u32[]{:S(2)}) collective-permute-start(bf16[1600,128]{1,0:T(8,128)(2,1)S(1)} %get-tuple-element.39.x_own.own), channel_id=1, source_target_pairs={{0,12},{1,13},{2,14},{3,15},{4,8},{5,9},{6,10},{7,11},{8,4},{9,5},... | collective-permute-start | bytes 1228808 | tf_op jit(solution)/shard_map/ppermute | solution.py:98
  33.0 1.2 collective-permute-start.5
  34.2 0.7 collective-permute-start.6
  34.9 7.7 %collective-permute-done.10.west.g1 = bf16[1616,128]{1,0:T(8,128)(2,1)S(1)} collective-permute-done((bf16[1616,128]{1,0:T(8,128)(2,1)S(1)}, bf16[1616,128]{1,0:T(8,128)(2,1)S(1)}, u32[]{:S(2)}, u32[]{:S(2)}) %collective-permute-start.10) | collective-permute-done | bytes 413728 | tf_op jit(solution)/shard_map/ppermute | solution.py:98
  43.2 1.9 %collective-permute-start.16 = (bf16[768,128]{1,0:T(8,128)(2,1)S(1)}, bf16[768,128]{1,0:T(8,128)(2,1)S(1)}, u32[]{:S(2)}, u32[]{:S(2)}) collective-permute-start(bf16[768,128]{1,0:T(8,128)(2,1)S(1)} %get-tuple-element.45), channel_id=1, source_target_pairs={{0,3},{1,0},{2,1},{3,2},{4,7},{5,4},{6,5},{7,6},{8,11},{9,8},{10,9... | collective-permute-start | bytes 589832 | tf_op jit(solution)/shard_map/ppermute | solution.py:98
  45.3 4.9 %collective-permute-done.6.x_y = bf16[1536,128]{1,0:T(8,128)(2,1)S(1)} collective-permute-done((bf16[1536,128]{1,0:T(8,128)(2,1)S(1)}, bf16[1536,128]{1,0:T(8,128)(2,1)S(1)}, u32[]{:S(2)}, u32[]{:S(2)}) %collective-permute-start.6) | collective-permute-done | bytes 393248 | tf_op jit(solution)/shard_map/ppermute | solution.py:98
  51.0 4.9 %lines.1 = (bf16[4,18,192,256]{3,2,1,0:T(8,128)(2,1)S(1)}, f32[27,256,512]{2,1,0:T(8,128)}) custom-call(s32[3]{0:T(128)S(1)} %pad_add_fusion.pos.refs_0_, bf16[1600,128]{1,0:T(8,128)(2,1)S(1)} %get-tuple-element.39.x_own.own, bf16[1600,128]{1,0:T(8,128)(2,1)S(1)} %collective-permute-done.5.x_x, bf16[1536,128]{1,0:T(8,128)(2,1)S(1)} %collective-permute-done.6.x_y, ...), custom_call_target="tpu_custom_call" | custom-call | bytes 1048576 | tf_op jit(solution)/shard_map/lines/pallas_call | solution.py:547
  57.1 1.0 copy-done.2
  58.9 8.6 %taps.1.held = f32[27,64,128]{2,1,0:T(8,128)S(1)} custom-call(s32[3]{0:T(128)S(1)} %pad_add_fusion.pos.refs_0_, bf16[4,18,192,256]{3,2,1,0:T(8,128)(2,1)S(1)} %get-tuple-element.44.after.xs, bf16[1616,128]{1,0:T(8,128)(2,1)S(1)} %pair_0.1.g0, bf16[1616,128]{1,0:T(8,128)(2,1)S(1)} %collective-permute-done.10.west.g1, ...), custom_call_target="tpu_custom_call" | custom-call | flops 5435817984 | bytes 11231232 | tf_op jit(solution)/shard_map/taps/pallas_call | solution.py:116
  67.5 0.9 code.1
  68.4 3.9 %collective-permute-start.28 = (bf16[1616,128]{1,0:T(8,128)(2,1)S(1)}, bf16[1616,128]{1,0:T(8,128)(2,1)S(1)}, u32[]{:S(2)}, u32[]{:S(2)}) collective-permute-start(bf16[1616,128]{1,0:T(8,128)(2,1)S(1)} %get-tuple-element.51), channel_id=1, source_target_pairs={{0,3},{1,0},{2,1},{3,2},{4,7},{5,4},{6,5},{7,6},{8,11},{9,8},{10,9... | collective-permute-start | bytes 1241096 | tf_op jit(solution)/shard_map/ppermute | solution.py:98
  72.3 1.3 collective-permute-start.20
  74.2 9.5 %field.1.after1 = bf16[4,4,48,256]{3,2,1,0:T(8,128)(2,1)} custom-call(s32[3]{0:T(128)S(1)} %pad_add_fusion.pos.refs_0_, bf16[1744,128]{1,0:T(8,128)(2,1)S(1)} %get-tuple-element.46.after.after2.after3.own.refs_1_, bf16[4,6,64,256]{3,2,1,0:T(8,128)(2,1)S(1)} %mine.1, bf16[4,6,64,256]{3,2,1,0:T(8,128)(2,1)S(1)} %collective-permute-done.18.after.theirs, ...), custom_call_target="tpu_custom_call" | custom-call | flops 10871635968 | bytes 7077888 | tf_op jit(solution)/shard_map/field/pallas_call | solution.py:595
  83.7 1.0 collective-permute-done.20.by_y.y.refs_3_
  84.7 1.0 collective-permute-done.19.by_x.x.refs_2_
  85.6 1.0 copy-done.3
  87.8 1.4 collective-permute-start.22
  89.3 2.1 %collective-permute-done.27.west.refs_1_ = bf16[1616,128]{1,0:T(8,128)(2,1)S(1)} collective-permute-done((bf16[1616,128]{1,0:T(8,128)(2,1)S(1)}, bf16[1616,128]{1,0:T(8,128)(2,1)S(1)}, u32[]{:S(2)}, u32[]{:S(2)}) %collective-permute-start.27) | collective-permute-done | bytes 413728 | tf_op jit(solution)/shard_map/ppermute | solution.py:98
  91.4 2.5 %collective-permute-done.22.bottom.after2.refs_5_ = bf16[848,128]{1,0:T(8,128)(2,1)S(1)} collective-permute-done((bf16[848,128]{1,0:T(8,128)(2,1)S(1)}, bf16[848,128]{1,0:T(8,128)(2,1)S(1)}, u32[]{:S(2)}, u32[]{:S(2)}) %collective-permute-start.22) | collective-permute-done | bytes 217120 | tf_op jit(solution)/shard_map/ppermute | solution.py:98
  94.5 1.5 collective-permute-start.36
  96.0 0.8 collective-permute-start.35
  96.8 3.4 %collective-permute-start.30 = (bf16[816,128]{1,0:T(8,128)(2,1)S(1)}, bf16[816,128]{1,0:T(8,128)(2,1)S(1)}, u32[]{:S(2)}, u32[]{:S(2)}) collective-permute-start(bf16[816,128]{1,0:T(8,128)(2,1)S(1)} %get-tuple-element.53), channel_id=1, source_target_pairs={{0,3},{1,0},{2,1},{3,2},{4,7},{5,4},{6,5},{7,6},{8,11},{9,8},{10,9... | collective-permute-start | bytes 626696 | tf_op jit(solution)/shard_map/ppermute | solution.py:98
  100.8 3.9 %collective-permute-start.24 = (bf16[576,128]{1,0:T(8,128)(2,1)S(1)}, bf16[576,128]{1,0:T(8,128)(2,1)S(1)}, u32[]{:S(2)}, u32[]{:S(2)}) collective-permute-start(bf16[576,128]{1,0:T(8,128)(2,1)S(1)} %block.1.refs_6_), channel_id=1, source_target_pairs={{0,3},{1,0},{2,1},{3,2},{4,7},{5,4},{6,5},{7,6},{8,11},{9,8},{10,9... | collective-permute-start | bytes 442376 | tf_op jit(solution)/shard_map/ppermute | solution.py:98
  104.7 5.0 %collective-permute-done.29.half_3 = bf16[800,128]{1,0:T(8,128)(2,1)S(1)} collective-permute-done((bf16[800,128]{1,0:T(8,128)(2,1)S(1)}, bf16[800,128]{1,0:T(8,128)(2,1)S(1)}, u32[]{:S(2)}, u32[]{:S(2)}) %collective-permute-start.29) | collective-permute-done | bytes 204832 | tf_op jit(solution)/shard_map/ppermute | solution.py:98
  110.2 1.4 collective-permute-start.32
  112.1 0.8 collective-permute-start.23
  112.9 6.3 %collective-permute-done.23.block_3.after2.refs_7_ = bf16[576,128]{1,0:T(8,128)(2,1)S(1)} collective-permute-done((bf16[576,128]{1,0:T(8,128)(2,1)S(1)}, bf16[576,128]{1,0:T(8,128)(2,1)S(1)}, u32[]{:S(2)}, u32[]{:S(2)}) %collective-permute-start.23) | collective-permute-done | bytes 147488 | tf_op jit(solution)/shard_map/ppermute | solution.py:98
  119.7 1.6 %collective-permute-start.37 = (bf16[1616,128]{1,0:T(8,128)(2,1)S(1)}, bf16[1616,128]{1,0:T(8,128)(2,1)S(1)}, u32[]{:S(2)}, u32[]{:S(2)}) collective-permute-start(bf16[1616,128]{1,0:T(8,128)(2,1)S(1)} %get-tuple-element.59), channel_id=1, source_target_pairs={{0,4},{1,5},{2,6},{3,7},{4,0},{5,1},{6,2},{7,3},{8,12},{9,13},{10,... | collective-permute-start | bytes 1241096 | tf_op jit(solution)/shard_map/ppermute | solution.py:98
  121.3 0.7 collective-permute-start.38
  122.6 1.5 %collective-permute-start.26 = (bf16[288,128]{1,0:T(8,128)(2,1)S(1)}, bf16[288,128]{1,0:T(8,128)(2,1)S(1)}, u32[]{:S(2)}, u32[]{:S(2)}) collective-permute-start(bf16[288,128]{1,0:T(8,128)(2,1)S(1)} %get-tuple-element.50), channel_id=1, source_target_pairs={{0,3},{1,0},{2,1},{3,2},{4,7},{5,4},{6,5},{7,6},{8,11},{9,8},{10,9... | collective-permute-start | bytes 221192 | tf_op jit(solution)/shard_map/ppermute | solution.py:98
  124.1 2.9 %collective-permute-done.26.after3.refs_2_ = bf16[288,128]{1,0:T(8,128)(2,1)S(1)} collective-permute-done((bf16[288,128]{1,0:T(8,128)(2,1)S(1)}, bf16[288,128]{1,0:T(8,128)(2,1)S(1)}, u32[]{:S(2)}, u32[]{:S(2)}) %collective-permute-start.26) | collective-permute-done | bytes 73760 | tf_op jit(solution)/shard_map/ppermute | solution.py:98
  127.0 3.1 %unpack_1.1 = (f32[27,256,512]{2,1,0:T(8,128)}, f32[8,128]{1,0:T(8,128)S(1)}) custom-call(s32[3]{0:T(128)S(1)} %pad_add_fusion.pos.refs_0_, bf16[1744,128]{1,0:T(8,128)(2,1)S(1)} %get-tuple-element.46.after.after2.after3.own.refs_1_, bf16[1744,128]{1,0:T(8,128)(2,1)S(1)} %collective-permute-done.19.by_x.x.refs_2_, ...), custom_call_target="tpu_custom_call", output_to_operand_aliasing={{0}: (7, {})} | custom-call | bytes 4194304 | tf_op jit(solution)/shard_map/unpack_1/pallas_call | solution.py:420
  130.2 3.0 %collective-permute-done.25.after2.refs_1_ = bf16[288,128]{1,0:T(8,128)(2,1)S(1)} collective-permute-done((bf16[288,128]{1,0:T(8,128)(2,1)S(1)}, bf16[288,128]{1,0:T(8,128)(2,1)S(1)}, u32[]{:S(2)}, u32[]{:S(2)}) %collective-permute-start.25) | collective-permute-done | bytes 73760 | tf_op jit(solution)/shard_map/ppermute | solution.py:98
  133.7 1.4 collective-permute-start.34
  135.6 6.4 %unpack_2.1 = (f32[27,256,512]{2,1,0:T(8,128)}, f32[8,128]{1,0:T(8,128)}) custom-call(s32[3]{0:T(128)S(1)} %pad_add_fusion.pos.refs_0_, bf16[1616,128]{1,0:T(8,128)(2,1)S(1)} %collective-permute-done.27.west.refs_1_, bf16[1616,128]{1,0:T(8,128)(2,1)S(1)} %collective-permute-done.28.east.refs_2_, ...), custom_call_target="tpu_custom_call", output_to_operand_aliasing={{0}: (10, {})} | custom-call | bytes 4194304 | tf_op jit(solution)/shard_map/unpack_2/pallas_call | solution.py:420
  142.0 3.7 %unpack_3.1 = (f32[27,256,512]{2,1,0:T(8,128)}, f32[8,128]{1,0:T(8,128)}) custom-call(s32[3]{0:T(128)S(1)} %pad_add_fusion.pos.refs_0_, bf16[288,128]{1,0:T(8,128)(2,1)S(1)} %collective-permute-done.25.after2.refs_1_, bf16[288,128]{1,0:T(8,128)(2,1)S(1)} %collective-permute-done.26.after3.refs_2_, ...), custom_call_target="tpu_custom_call", output_to_operand_aliasing={{0}: (8, {})} | custom-call | bytes 4194304 | tf_op jit(solution)/shard_map/unpack_3/pallas_call | solution.py:420
  (66 shorter events, 12.5 us)
Async XLA Ops:
  0.7 1.0 copy-start.1
  1.7 1.0 copy-start.4
  3.6 17.5 %collective-permute-start.8 = (bf16[768,128]{1,0:T(8,128)(2,1)S(1)}, bf16[768,128]{1,0:T(8,128)(2,1)S(1)}, u32[]{:S(2)}, u32[]{:S(2)}) collective-permute-start(bf16[768,128]{1,0:T(8,128)(2,1)S(1)} %get-tuple-element.41), channel_id=1, source_target_pairs={{0,0},{1,1},{2,2},{3,3},{4,4},{5,5},{6,6},{7,7},{8,16},{9,17},{10,... | collective-permute-start | bytes 589832 | tf_op jit(solution)/shard_map/ppermute | solution.py:98
  4.2 16.8 %collective-permute-start.9 = (bf16[768,128]{1,0:T(8,128)(2,1)S(1)}, bf16[768,128]{1,0:T(8,128)(2,1)S(1)}, u32[]{:S(2)}, u32[]{:S(2)}) collective-permute-start(bf16[768,128]{1,0:T(8,128)(2,1)S(1)} %get-tuple-element.42), channel_id=1, source_target_pairs={{0,4},{1,5},{2,6},{3,7},{4,0},{5,1},{6,2},{7,3},{8,20},{9,21},{10,... | collective-permute-start | bytes 589832 | tf_op jit(solution)/shard_map/ppermute | solution.py:98
  7.2 13.8 %collective-permute-start = (bf16[416,128]{1,0:T(8,128)(2,1)S(1)}, bf16[416,128]{1,0:T(8,128)(2,1)S(1)}, u32[]{:S(2)}, u32[]{:S(2)}) collective-permute-start(bf16[416,128]{1,0:T(8,128)(2,1)S(1)} %get-tuple-element.34), channel_id=1, source_target_pairs={{0,1},{1,2},{2,3},{3,0},{4,5},{5,6},{6,7},{7,4},{8,9},{9,10},{10,1... | collective-permute-start | bytes 319496 | tf_op jit(solution)/shard_map/ppermute | solution.py:98
  8.8 12.2 %collective-permute-start.2 = (bf16[416,128]{1,0:T(8,128)(2,1)S(1)}, bf16[416,128]{1,0:T(8,128)(2,1)S(1)}, u32[]{:S(2)}, u32[]{:S(2)}) collective-permute-start(bf16[416,128]{1,0:T(8,128)(2,1)S(1)} %get-tuple-element.36), channel_id=1, source_target_pairs={{0,3},{1,0},{2,1},{3,2},{4,7},{5,4},{6,5},{7,6},{8,11},{9,8},{10,9... | collective-permute-start | bytes 319496 | tf_op jit(solution)/shard_map/ppermute | solution.py:98
  11.1 10.0 %collective-permute-start.1 = (bf16[384,128]{1,0:T(8,128)(2,1)S(1)}, bf16[384,128]{1,0:T(8,128)(2,1)S(1)}, u32[]{:S(2)}, u32[]{:S(2)}) collective-permute-start(bf16[384,128]{1,0:T(8,128)(2,1)S(1)} %get-tuple-element.35), channel_id=1, source_target_pairs={{0,2},{1,3},{2,0},{3,1},{4,6},{5,7},{6,4},{7,5},{8,10},{9,11},{10,... | collective-permute-start | bytes 294920 | tf_op jit(solution)/shard_map/ppermute | solution.py:98
  21.7 13.3 %collective-permute-start.11 = (bf16[1616,128]{1,0:T(8,128)(2,1)S(1)}, bf16[1616,128]{1,0:T(8,128)(2,1)S(1)}, u32[]{:S(2)}, u32[]{:S(2)}) collective-permute-start(bf16[1616,128]{1,0:T(8,128)(2,1)S(1)} %pair_0.1.g0), channel_id=1, source_target_pairs={{0,3},{1,0},{2,1},{3,2},{4,7},{5,4},{6,5},{7,6},{8,11},{9,8},{10,9... | collective-permute-start | bytes 1241096 | tf_op jit(solution)/shard_map/ppermute | solution.py:98
  23.9 18.7 %collective-permute-start.10 = (bf16[1616,128]{1,0:T(8,128)(2,1)S(1)}, bf16[1616,128]{1,0:T(8,128)(2,1)S(1)}, u32[]{:S(2)}, u32[]{:S(2)}) collective-permute-start(bf16[1616,128]{1,0:T(8,128)(2,1)S(1)} %pair_0.1.g0), channel_id=1, source_target_pairs={{0,1},{1,2},{2,3},{3,0},{4,5},{5,6},{6,7},{7,4},{8,9},{9,10},{10,1... | collective-permute-start | bytes 1241096 | tf_op jit(solution)/shard_map/ppermute | solution.py:98
  23.9 5.6 %collective-permute-start.3 = (bf16[384,128]{1,0:T(8,128)(2,1)S(1)}, bf16[384,128]{1,0:T(8,128)(2,1)S(1)}, u32[]{:S(2)}, u32[]{:S(2)}) collective-permute-start(bf16[384,128]{1,0:T(8,128)(2,1)S(1)} %get-tuple-element.37), channel_id=1, source_target_pairs={{0,4},{1,5},{2,6},{3,7},{4,0},{5,1},{6,2},{7,3},{8,12},{9,13},{10,... | collective-permute-start | bytes 294920 | tf_op jit(solution)/shard_map/ppermute | solution.py:98
  24.5 6.2 %collective-permute-start.4 = (bf16[384,128]{1,0:T(8,128)(2,1)S(1)}, bf16[384,128]{1,0:T(8,128)(2,1)S(1)}, u32[]{:S(2)}, u32[]{:S(2)}) collective-permute-start(bf16[384,128]{1,0:T(8,128)(2,1)S(1)} %get-tuple-element.38), channel_id=1, source_target_pairs={{0,12},{1,13},{2,14},{3,15},{4,8},{5,9},{6,10},{7,11},{8,4},{9,5},... | collective-permute-start | bytes 294920 | tf_op jit(solution)/shard_map/ppermute | solution.py:98
  31.4 18.8 %collective-permute-start.7 = (bf16[1600,128]{1,0:T(8,128)(2,1)S(1)}, bf16[1600,128]{1,0:T(8,128)(2,1)S(1)}, u32[]{:S(2)}, u32[]{:S(2)}) collective-permute-start(bf16[1600,128]{1,0:T(8,128)(2,1)S(1)} %get-tuple-element.39.x_own.own), channel_id=1, source_target_pairs={{0,12},{1,13},{2,14},{3,15},{4,8},{5,9},{6,10},{7,11},{8,4},{9,5},... | collective-permute-start | bytes 1228808 | tf_op jit(solution)/shard_map/ppermute | solution.py:98
  33.0 18.0 %collective-permute-start.5 = (bf16[1600,128]{1,0:T(8,128)(2,1)S(1)}, bf16[1600,128]{1,0:T(8,128)(2,1)S(1)}, u32[]{:S(2)}, u32[]{:S(2)}) collective-permute-start(bf16[1600,128]{1,0:T(8,128)(2,1)S(1)} %get-tuple-element.39.x_own.own), channel_id=1, source_target_pairs={{0,4},{1,5},{2,6},{3,7},{4,0},{5,1},{6,2},{7,3},{8,12},{9,13},{10,... | collective-permute-start | bytes 1228808 | tf_op jit(solution)/shard_map/ppermute | solution.py:98
  34.2 15.9 %collective-permute-start.6 = (bf16[1536,128]{1,0:T(8,128)(2,1)S(1)}, bf16[1536,128]{1,0:T(8,128)(2,1)S(1)}, u32[]{:S(2)}, u32[]{:S(2)}) collective-permute-start(bf16[1536,128]{1,0:T(8,128)(2,1)S(1)} %get-tuple-element.40), channel_id=1, source_target_pairs={{0,8},{1,9},{2,10},{3,11},{4,12},{5,13},{6,14},{7,15},{8,0},{9,1},... | collective-permute-start | bytes 1179656 | tf_op jit(solution)/shard_map/ppermute | solution.py:98
  43.2 12.7 %collective-permute-start.16 = (bf16[768,128]{1,0:T(8,128)(2,1)S(1)}, bf16[768,128]{1,0:T(8,128)(2,1)S(1)}, u32[]{:S(2)}, u32[]{:S(2)}) collective-permute-start(bf16[768,128]{1,0:T(8,128)(2,1)S(1)} %get-tuple-element.45), channel_id=1, source_target_pairs={{0,3},{1,0},{2,1},{3,2},{4,7},{5,4},{6,5},{7,6},{8,11},{9,8},{10,9... | collective-permute-start | bytes 589832 | tf_op jit(solution)/shard_map/ppermute | solution.py:98
  45.1 10.9 %collective-permute-start.15 = (bf16[768,128]{1,0:T(8,128)(2,1)S(1)}, bf16[768,128]{1,0:T(8,128)(2,1)S(1)}, u32[]{:S(2)}, u32[]{:S(2)}) collective-permute-start(bf16[768,128]{1,0:T(8,128)(2,1)S(1)} %get-tuple-element.43.after), channel_id=1, source_target_pairs={{0,1},{1,2},{2,3},{3,0},{4,5},{5,6},{6,7},{7,4},{8,9},{9,10},{10,1... | collective-permute-start | bytes 589832 | tf_op jit(solution)/shard_map/ppermute | solution.py:98
  50.1 8.7 %collective-permute-start.12 = (bf16[1616,128]{1,0:T(8,128)(2,1)S(1)}, bf16[1616,128]{1,0:T(8,128)(2,1)S(1)}, u32[]{:S(2)}, u32[]{:S(2)}) collective-permute-start(bf16[1616,128]{1,0:T(8,128)(2,1)S(1)} %pair_0.1.g0), channel_id=1, source_target_pairs={{0,16},{1,17},{2,18},{3,19},{4,20},{5,21},{6,22},{7,23},{8,24},{9,... | collective-permute-start | bytes 1241096 | tf_op jit(solution)/shard_map/ppermute | solution.py:98
  50.1 8.7 %collective-permute-start.14 = (bf16[1616,128]{1,0:T(8,128)(2,1)S(1)}, bf16[1616,128]{1,0:T(8,128)(2,1)S(1)}, u32[]{:S(2)}, u32[]{:S(2)}) collective-permute-start(bf16[1616,128]{1,0:T(8,128)(2,1)S(1)} %collective-permute-done.11.east.g3), channel_id=1, source_target_pairs={{0,16},{1,17},{2,18},{3,19},{4,20},{5,21},{6,22},{7,23},{8,24},{9,... | collective-permute-start | bytes 1241096 | tf_op jit(solution)/shard_map/ppermute | solution.py:98
  51.0 7.8 %collective-permute-start.13 = (bf16[1616,128]{1,0:T(8,128)(2,1)S(1)}, bf16[1616,128]{1,0:T(8,128)(2,1)S(1)}, u32[]{:S(2)}, u32[]{:S(2)}) collective-permute-start(bf16[1616,128]{1,0:T(8,128)(2,1)S(1)} %collective-permute-done.10.west.g1), channel_id=1, source_target_pairs={{0,16},{1,17},{2,18},{3,19},{4,20},{5,21},{6,22},{7,23},{8,24},{9,... | collective-permute-start | bytes 1241096 | tf_op jit(solution)/shard_map/ppermute | solution.py:98
  56.5 2.4 %collective-permute-start.17 = (bf16[2,768,128]{2,1,0:T(8,128)(2,1)S(1)}, bf16[2,768,128]{2,1,0:T(8,128)(2,1)S(1)}, u32[]{:S(2)}, u32[]{:S(2)}) collective-permute-start(bf16[2,768,128]{2,1,0:T(8,128)(2,1)S(1)} %pair.1.g2), channel_id=1, source_target_pairs={{0,16},{1,17},{2,18},{3,19},{4,20},{5,21},{6,22},{7,23},{8,24},{9,... | collective-permute-start | bytes 1179656 | tf_op jit(solution)/shard_map/ppermute | solution.py:98
  57.1 1.0 copy-start.2
  58.1 16.1 %slice-start = ((s8[7077888]{0:T(1024)(128)(4,1)}), s8[4194304]{0:T(1024)(128)(4,1)S(1)}, s32[]{:S(2)}) async-start(s8[7077888]{0:T(1024)(128)(4,1)} %bitcast.12), calls=%async_computation | async-start | bytes 8388608
  58.8 15.4 %slice-start.1 = ((s8[7077888]{0:T(1024)(128)(4,1)}), s8[2883584]{0:T(1024)(128)(4,1)S(1)}, s32[]{:S(2)}) async-start(s8[7077888]{0:T(1024)(128)(4,1)} %bitcast.12), calls=%async_computation.1 | async-start | bytes 5767168
  58.8 8.7 %collective-permute-start.18 = (bf16[4,6,64,256]{3,2,1,0:T(8,128)(2,1)S(1)}, bf16[4,6,64,256]{3,2,1,0:T(8,128)(2,1)S(1)}, u32[]{:S(2)}, u32[]{:S(2)}) collective-permute-start(bf16[4,6,64,256]{3,2,1,0:T(8,128)(2,1)S(1)} %mine.1), channel_id=1, source_target_pairs={{0,16},{1,17},{2,18},{3,19},{4,20},{5,21},{6,22},{7,23},{8,24},{9,... | collective-permute-start | bytes 2359304 | tf_op jit(solution)/shard_map/ppermute | solution.py:98
  68.4 20.9 %collective-permute-start.28 = (bf16[1616,128]{1,0:T(8,128)(2,1)S(1)}, bf16[1616,128]{1,0:T(8,128)(2,1)S(1)}, u32[]{:S(2)}, u32[]{:S(2)}) collective-permute-start(bf16[1616,128]{1,0:T(8,128)(2,1)S(1)} %get-tuple-element.51), channel_id=1, source_target_pairs={{0,3},{1,0},{2,1},{3,2},{4,7},{5,4},{6,5},{7,6},{8,11},{9,8},{10,9... | collective-permute-start | bytes 1241096 | tf_op jit(solution)/shard_map/ppermute | solution.py:98
  72.3 19.0 %collective-permute-start.27 = (bf16[1616,128]{1,0:T(8,128)(2,1)S(1)}, bf16[1616,128]{1,0:T(8,128)(2,1)S(1)}, u32[]{:S(2)}, u32[]{:S(2)}) collective-permute-start(bf16[1616,128]{1,0:T(8,128)(2,1)S(1)} %get-tuple-element.51), channel_id=1, source_target_pairs={{0,1},{1,2},{2,3},{3,0},{4,5},{5,6},{6,7},{7,4},{8,9},{9,10},{10,1... | collective-permute-start | bytes 1241096 | tf_op jit(solution)/shard_map/ppermute | solution.py:98
  72.3 12.3 %collective-permute-start.20 = (bf16[1744,128]{1,0:T(8,128)(2,1)S(1)}, bf16[1744,128]{1,0:T(8,128)(2,1)S(1)}, u32[]{:S(2)}, u32[]{:S(2)}) collective-permute-start(bf16[1744,128]{1,0:T(8,128)(2,1)S(1)} %get-tuple-element.46.after.after2.after3.own.refs_1_), channel_id=1, source_target_pairs={{0,8},{1,9},{2,10},{3,11},{4,12},{5,13},{6,14},{7,15},{8,0},{9,1},... | collective-permute-start | bytes 1339400 | tf_op jit(solution)/shard_map/ppermute | solution.py:98
  73.6 12.0 %collective-permute-start.19 = (bf16[1744,128]{1,0:T(8,128)(2,1)S(1)}, bf16[1744,128]{1,0:T(8,128)(2,1)S(1)}, u32[]{:S(2)}, u32[]{:S(2)}) collective-permute-start(bf16[1744,128]{1,0:T(8,128)(2,1)S(1)} %get-tuple-element.46.after.after2.after3.own.refs_1_), channel_id=1, source_target_pairs={{0,4},{1,5},{2,6},{3,7},{4,0},{5,1},{6,2},{7,3},{8,12},{9,13},{10,... | collective-permute-start | bytes 1339400 | tf_op jit(solution)/shard_map/ppermute | solution.py:98
  85.6 1.0 copy-start.3
  87.2 6.6 %collective-permute-start.21 = (bf16[896,128]{1,0:T(8,128)(2,1)S(1)}, bf16[896,128]{1,0:T(8,128)(2,1)S(1)}, u32[]{:S(2)}, u32[]{:S(2)}) collective-permute-start(bf16[896,128]{1,0:T(8,128)(2,1)S(1)} %get-tuple-element.47), channel_id=1, source_target_pairs={{0,4},{1,5},{2,6},{3,7},{4,0},{5,1},{6,2},{7,3},{8,12},{9,13},{10,... | collective-permute-start | bytes 688136 | tf_op jit(solution)/shard_map/ppermute | solution.py:98
  87.8 6.0 %collective-permute-start.22 = (bf16[848,128]{1,0:T(8,128)(2,1)S(1)}, bf16[848,128]{1,0:T(8,128)(2,1)S(1)}, u32[]{:S(2)}, u32[]{:S(2)}) collective-permute-start(bf16[848,128]{1,0:T(8,128)(2,1)S(1)} %get-tuple-element.48), channel_id=1, source_target_pairs={{0,8},{1,9},{2,10},{3,11},{4,12},{5,13},{6,14},{7,15},{8,0},{9,1},... | collective-permute-start | bytes 651272 | tf_op jit(solution)/shard_map/ppermute | solution.py:98
  94.5 24.6 %collective-permute-start.36 = (bf16[3232,128]{1,0:T(8,128)(2,1)S(1)}, bf16[3232,128]{1,0:T(8,128)(2,1)S(1)}, u32[]{:S(2)}, u32[]{:S(2)}) collective-permute-start(bf16[3232,128]{1,0:T(8,128)(2,1)S(1)} %get-tuple-element.54.after.after3), channel_id=1, source_target_pairs={{0,8},{1,9},{2,10},{3,11},{4,12},{5,13},{6,14},{7,15},{8,0},{9,1},... | collective-permute-start | bytes 2482184 | tf_op jit(solution)/shard_map/ppermute | solution.py:98
  96.0 23.2 %collective-permute-start.35 = (bf16[3232,128]{1,0:T(8,128)(2,1)S(1)}, bf16[3232,128]{1,0:T(8,128)(2,1)S(1)}, u32[]{:S(2)}, u32[]{:S(2)}) collective-permute-start(bf16[3232,128]{1,0:T(8,128)(2,1)S(1)} %get-tuple-element.54.after.after3), channel_id=1, source_target_pairs={{0,4},{1,5},{2,6},{3,7},{4,0},{5,1},{6,2},{7,3},{8,12},{9,13},{10,... | collective-permute-start | bytes 2482184 | tf_op jit(solution)/shard_map/ppermute | solution.py:98
  96.8 12.8 %collective-permute-start.30 = (bf16[816,128]{1,0:T(8,128)(2,1)S(1)}, bf16[816,128]{1,0:T(8,128)(2,1)S(1)}, u32[]{:S(2)}, u32[]{:S(2)}) collective-permute-start(bf16[816,128]{1,0:T(8,128)(2,1)S(1)} %get-tuple-element.53), channel_id=1, source_target_pairs={{0,3},{1,0},{2,1},{3,2},{4,7},{5,4},{6,5},{7,6},{8,11},{9,8},{10,9... | collective-permute-start | bytes 626696 | tf_op jit(solution)/shard_map/ppermute | solution.py:98
  100.2 9.4 %collective-permute-start.29 = (bf16[800,128]{1,0:T(8,128)(2,1)S(1)}, bf16[800,128]{1,0:T(8,128)(2,1)S(1)}, u32[]{:S(2)}, u32[]{:S(2)}) collective-permute-start(bf16[800,128]{1,0:T(8,128)(2,1)S(1)} %get-tuple-element.52), channel_id=1, source_target_pairs={{0,1},{1,2},{2,3},{3,0},{4,5},{5,6},{6,7},{7,4},{8,9},{9,10},{10,1... | collective-permute-start | bytes 614408 | tf_op jit(solution)/shard_map/ppermute | solution.py:98
  100.8 11.3 %collective-permute-start.24 = (bf16[576,128]{1,0:T(8,128)(2,1)S(1)}, bf16[576,128]{1,0:T(8,128)(2,1)S(1)}, u32[]{:S(2)}, u32[]{:S(2)}) collective-permute-start(bf16[576,128]{1,0:T(8,128)(2,1)S(1)} %block.1.refs_6_), channel_id=1, source_target_pairs={{0,3},{1,0},{2,1},{3,2},{4,7},{5,4},{6,5},{7,6},{8,11},{9,8},{10,9... | collective-permute-start | bytes 442376 | tf_op jit(solution)/shard_map/ppermute | solution.py:98
  110.2 23.0 %collective-permute-start.32 = (bf16[1616,128]{1,0:T(8,128)(2,1)S(1)}, bf16[1616,128]{1,0:T(8,128)(2,1)S(1)}, u32[]{:S(2)}, u32[]{:S(2)}) collective-permute-start(bf16[1616,128]{1,0:T(8,128)(2,1)S(1)} %across.1.refs_3_), channel_id=1, source_target_pairs={{0,8},{1,9},{2,10},{3,11},{4,12},{5,13},{6,14},{7,15},{8,0},{9,1},... | collective-permute-start | bytes 1241096 | tf_op jit(solution)/shard_map/ppermute | solution.py:98
  111.6 21.6 %collective-permute-start.31 = (bf16[1616,128]{1,0:T(8,128)(2,1)S(1)}, bf16[1616,128]{1,0:T(8,128)(2,1)S(1)}, u32[]{:S(2)}, u32[]{:S(2)}) collective-permute-start(bf16[1616,128]{1,0:T(8,128)(2,1)S(1)} %across.1.refs_3_), channel_id=1, source_target_pairs={{0,4},{1,5},{2,6},{3,7},{4,0},{5,1},{6,2},{7,3},{8,12},{9,13},{10,... | collective-permute-start | bytes 1241096 | tf_op jit(solution)/shard_map/ppermute | solution.py:98
  112.1 7.0 %collective-permute-start.23 = (bf16[576,128]{1,0:T(8,128)(2,1)S(1)}, bf16[576,128]{1,0:T(8,128)(2,1)S(1)}, u32[]{:S(2)}, u32[]{:S(2)}) collective-permute-start(bf16[576,128]{1,0:T(8,128)(2,1)S(1)} %block.1.refs_6_), channel_id=1, source_target_pairs={{0,1},{1,2},{2,3},{3,0},{4,5},{5,6},{6,7},{7,4},{8,9},{9,10},{10,1... | collective-permute-start | bytes 442376 | tf_op jit(solution)/shard_map/ppermute | solution.py:98
  119.1 16.5 %copy-start = (bf16[3232,128]{1,0:T(8,128)(2,1)}, bf16[3232,128]{1,0:T(8,128)(2,1)S(1)}, u32[]{:S(2)}) copy-start(bf16[3232,128]{1,0:T(8,128)(2,1)S(1)} %collective-permute-done.36.by_y.refs_4_) | copy-start | bytes 2482180
  119.7 15.9 %collective-permute-start.37 = (bf16[1616,128]{1,0:T(8,128)(2,1)S(1)}, bf16[1616,128]{1,0:T(8,128)(2,1)S(1)}, u32[]{:S(2)}, u32[]{:S(2)}) collective-permute-start(bf16[1616,128]{1,0:T(8,128)(2,1)S(1)} %get-tuple-element.59), channel_id=1, source_target_pairs={{0,4},{1,5},{2,6},{3,7},{4,0},{5,1},{6,2},{7,3},{8,12},{9,13},{10,... | collective-permute-start | bytes 1241096 | tf_op jit(solution)/shard_map/ppermute | solution.py:98
  121.3 14.3 %collective-permute-start.38 = (bf16[1616,128]{1,0:T(8,128)(2,1)S(1)}, bf16[1616,128]{1,0:T(8,128)(2,1)S(1)}, u32[]{:S(2)}, u32[]{:S(2)}) collective-permute-start(bf16[1616,128]{1,0:T(8,128)(2,1)S(1)} %get-tuple-element.60), channel_id=1, source_target_pairs={{0,8},{1,9},{2,10},{3,11},{4,12},{5,13},{6,14},{7,15},{8,0},{9,1},... | collective-permute-start | bytes 1241096 | tf_op jit(solution)/shard_map/ppermute | solution.py:98
  122.6 4.4 %collective-permute-start.26 = (bf16[288,128]{1,0:T(8,128)(2,1)S(1)}, bf16[288,128]{1,0:T(8,128)(2,1)S(1)}, u32[]{:S(2)}, u32[]{:S(2)}) collective-permute-start(bf16[288,128]{1,0:T(8,128)(2,1)S(1)} %get-tuple-element.50), channel_id=1, source_target_pairs={{0,3},{1,0},{2,1},{3,2},{4,7},{5,4},{6,5},{7,6},{8,11},{9,8},{10,9... | collective-permute-start | bytes 221192 | tf_op jit(solution)/shard_map/ppermute | solution.py:98
  127.0 6.2 %collective-permute-start.25 = (bf16[288,128]{1,0:T(8,128)(2,1)S(1)}, bf16[288,128]{1,0:T(8,128)(2,1)S(1)}, u32[]{:S(2)}, u32[]{:S(2)}) collective-permute-start(bf16[288,128]{1,0:T(8,128)(2,1)S(1)} %get-tuple-element.49.refs_9_), channel_id=1, source_target_pairs={{0,1},{1,2},{2,3},{3,0},{4,5},{5,6},{6,7},{7,4},{8,9},{9,10},{10,1... | collective-permute-start | bytes 221192 | tf_op jit(solution)/shard_map/ppermute | solution.py:98
  133.7 8.3 %collective-permute-start.34 = (bf16[848,128]{1,0:T(8,128)(2,1)S(1)}, bf16[848,128]{1,0:T(8,128)(2,1)S(1)}, u32[]{:S(2)}, u32[]{:S(2)}) collective-permute-start(bf16[848,128]{1,0:T(8,128)(2,1)S(1)} %get-tuple-element.58), channel_id=1, source_target_pairs={{0,8},{1,9},{2,10},{3,11},{4,12},{5,13},{6,14},{7,15},{8,0},{9,1},... | collective-permute-start | bytes 651272 | tf_op jit(solution)/shard_map/ppermute | solution.py:98
  135.1 6.9 %collective-permute-start.33 = (bf16[768,128]{1,0:T(8,128)(2,1)S(1)}, bf16[768,128]{1,0:T(8,128)(2,1)S(1)}, u32[]{:S(2)}, u32[]{:S(2)}) collective-permute-start(bf16[768,128]{1,0:T(8,128)(2,1)S(1)} %get-tuple-element.57), channel_id=1, source_target_pairs={{0,4},{1,5},{2,6},{3,7},{4,0},{5,1},{6,2},{7,3},{8,12},{9,13},{10,... | collective-permute-start | bytes 589832 | tf_op jit(solution)/shard_map/ppermute | solution.py:98
